TPU v7x, 32 devices: a whole 2x2x4 slice. The times are simulated.
32 devices in a mesh: dom: 2 (over x), vocab: 16 (over z, y, core).
Axes of the slice: x: 2, y: 2, z: 4, core: 2. Of those that a mesh axis runs over, the one named last changes fastest.
Arguments:
- hidden_states: bfloat16 [128, 5120], P('dom', 'vocab'), parts along dimension 0
- head: bfloat16 [19456, 5120], P('vocab'), may hold values from -0.078125 to 0.078125
- teacher_values: bfloat16 [128, 19456], P(('dom', 'vocab')), parts along dimension 0
- teacher_scales: float32 [128, 608], P(('dom', 'vocab')), parts along dimension 0, as said below
- token_ids: int32 [128], P('dom'), parts along dimension 0, may hold values from 0 to 19455
- lengths: int32 [4], P('dom'), parts along dimension 0, may hold values from 1 to 32, as said below
- row_map: int32 [128], P('dom'), parts along dimension 0, may hold values from -1 to 63, as said below
- loss_scale: float32 [1], replicated, may hold values from 65536 to 262144
Outputs:
- grad_hidden: bfloat16 [128, 5120], P('dom', 'vocab'), parts along dimension 0
- loss: float32 [2], P('dom'), parts along dimension 0
There are 2 independent parts, one for each index of `dom`. A program takes and returns all parts, laid end to end along the dimension named above; an argument that names none is the same for every part. Nothing has to cross between parts.
Inputs may be any that keep to these rules, and one draw needn't show every extreme that they name: `lengths`: every response has at least one live position, and some response has all 32 positions live. `row_map`: each live position t (t % 32 < lengths[t // 32]) is named by exactly one slot; no other position is named; slots naming no position hold -1. How many live rows a device's slots hold varies. `teacher_scales`: every scale is a power of two.
All inputs are finite; a program needn't handle non-finite values.
Results may differ from a plain program's by a relative error of at most 0.0054.
Values may be sent and summed in bfloat16 or wider, within the bound.
No kernel may reach another device: no remote copies, remote signals or barrier semaphores. Data moves between devices by JAX's collectives and lax.ppermute only.
A program may use at most 64 MiB of HBM per device.

v0:
```python
import jax
import jax.numpy as jnp
from jax import lax
from jax.sharding import PartitionSpec as P

BLOCK = 32


sample_weight = 0.5


def shards(
    hidden_states, head, teacher_values, teacher_scales, token_ids, lengths, row_map, loss_scale
):
    parts_count = lax.axis_size("vocab")
    own_index = lax.axis_index("vocab")
    tok_count = hidden_states.shape[0]
    shard_rows = head.shape[0]
    seq_length = tok_count // lengths.shape[0]
    contract_last = (((1,), (1,)), ((), ()))
    gathered = lax.all_gather(hidden_states, "vocab", axis=1, tiled=True)
    logits = lax.dot_general(gathered, head, contract_last, preferred_element_type=jnp.float32)
    slot_rows = teacher_values.shape[0]
    block_count = shard_rows // BLOCK
    values_split = teacher_values.reshape(slot_rows, parts_count, shard_rows)
    scales_split = teacher_scales.reshape(slot_rows, parts_count, block_count)
    arrived_values, arrived_scales = (
        lax.all_to_all(values_split, "vocab", split_axis=1, concat_axis=0, tiled=True),
        lax.all_to_all(
            scales_split.astype(jnp.bfloat16), "vocab", split_axis=1, concat_axis=0, tiled=True
        ).astype(scales_split.dtype),
    )
    positions = jnp.arange(tok_count, dtype=jnp.int32)
    owner = row_map[None, :] == positions[:, None]
    slot_of = jnp.sum(jnp.where(owner, positions[None, :], 0), axis=1)
    placed_values = jnp.take(arrived_values.reshape(tok_count, shard_rows), slot_of, axis=0)
    placed_scales = jnp.take(arrived_scales.reshape(tok_count, block_count), slot_of, axis=0)
    teacher_logits = (
        placed_values.astype(jnp.float32).reshape(tok_count, block_count, BLOCK)
        * placed_scales[:, :, None]
    ).reshape(tok_count, shard_rows)
    seq_ids = jnp.arange(lengths.shape[0], dtype=jnp.int32)
    own_length = jnp.sum(
        jnp.where((positions // seq_length)[:, None] == seq_ids[None, :], lengths[None, :], 0),
        axis=1,
    )
    live_mask = (positions % seq_length < own_length).astype(jnp.float32)
    live_count = jnp.sum(live_mask)
    local_ids = token_ids - own_index * shard_rows
    target_hit = local_ids[:, None] == jnp.arange(shard_rows, dtype=jnp.int32)[None, :]
    target_part = jnp.sum(jnp.where(target_hit, logits, 0.0), axis=1)
    student_max, teacher_max = lax.pmax(
        (jnp.max(logits, axis=1), jnp.max(teacher_logits, axis=1)), "vocab"
    )
    student_total, teacher_total = lax.psum(
        (
            jnp.sum(jnp.exp(logits - student_max[:, None]), axis=1),
            jnp.sum(jnp.exp(teacher_logits - teacher_max[:, None]), axis=1),
        ),
        "vocab",
    )
    student_lse = student_max + jnp.log(student_total)
    teacher_lse = teacher_max + jnp.log(teacher_total)
    log_student = logits - student_lse[:, None]
    log_teacher = teacher_logits - teacher_lse[:, None]
    student_prob = jnp.exp(log_student)
    divergence, target = lax.psum(
        (jnp.sum(student_prob * (log_student - log_teacher), axis=1), target_part), "vocab"
    )
    per_token = divergence + sample_weight * (student_lse - target)
    loss = jnp.reshape(jnp.sum(live_mask * per_token) / live_count, (1,))
    token_weight = live_mask * loss_scale[0] / live_count
    grad_logits = (
        token_weight[:, None]
        * (
            student_prob * (log_student - log_teacher - divergence[:, None])
            + sample_weight * (student_prob - target_hit.astype(jnp.float32))
        )
    ).astype(jnp.bfloat16)
    terms = jnp.dot(grad_logits, head, preferred_element_type=jnp.float32)
    grad_hidden = lax.psum_scatter(terms, "vocab", scatter_dimension=1, tiled=True)
    return (grad_hidden.astype(jnp.bfloat16), loss)


def solution(mesh):
    in_specs = (
        P("dom", "vocab"),
        P("vocab", None),
        P(("dom", "vocab"), None),
        P(("dom", "vocab"), None),
        P("dom"),
        P("dom"),
        P("dom"),
        P(),
    )
    out_specs = (P("dom", "vocab"), P("dom"))
    return jax.shard_map(shards, mesh=mesh, in_specs=in_specs, out_specs=out_specs, check_vma=False)
```

profile of v0, /device:TPU:0, one launch (start us, length us, event | category | flops | bytes accessed | tf_op | source)
XLA Modules:
  0.0 240.1 jit_solution(12170332636485097766)
XLA Ops:
  7.2 0.7 convert_element_type.48
  8.0 0.6 copy.24
  8.6 7.4 %all-to-all-start.1 = ((bf16[4,16,38]{2,0,1:T(4,128)(2,1)}), bf16[4,16,38]{2,0,1:T(4,128)(2,1)S(1)}, u32[]{:S(2)}, u32[]{:S(2)}) async-start(bf16[4,16,38]{2,0,1:T(4,128)(2,1)} %copy.24), calls=%async_computation.1 | async-start | bytes 32768 | tf_op jit(solution)/shard_map/all_to_all | solution.py:29
  16.0 0.8 select_reduce_fusion.1
  16.8 24.3 %all-gather = bf16[16,320,64]{1,2,0:T(8,128)(2,1)S(1)} all-gather(bf16[1,320,64]{1,2,0:T(8,128)(2,1)} %bitcast.34), channel_id=1, replica_groups=mesh['dom'=2,'vocab'=16] {'vocab'}, dimensions={0}, use_global_device_ids=true | all-gather | bytes 696320 | tf_op jit(solution)/shard_map/all_gather | solution.py:21
  41.1 0.5 copy.22
  41.6 0.6 reshape.150
  42.2 0.7 broadcast_subtract_fusion
  42.9 0.7 fusion.6
  43.6 8.4 %fusion.12 = (f32[64]{0:T(128)S(1)}, f32[64,1216]{1,0:T(8,128)S(1)}) fusion(bf16[5120,64]{0,1:T(8,128)(2,1)S(1)} %reshape.150, bf16[1216,5120]{1,0:T(8,128)(2,1)} %param.9), kind=kOutput, calls=%fused_computation.42 | convolution fusion | flops 796995520 | bytes 13418752 | tf_op jit(solution)/shard_map/dot_general | solution.py:22
  53.0 0.7 copy.23
  53.7 3.5 %all-to-all-start = ((bf16[4,16,1216]{2,0,1:T(4,128)(2,1)}), bf16[4,16,1216]{2,0,1:T(4,128)(2,1)S(1)}, u32[]{:S(2)}, u32[]{:S(2)}) async-start(bf16[4,16,1216]{2,0,1:T(4,128)(2,1)} %copy.23), calls=%async_computation | async-start | bytes 327680 | tf_op jit(solution)/shard_map/all_to_all | solution.py:28
  57.3 0.6 gather_fusion.1
  58.3 7.3 %all-to-all-done = bf16[4,16,1216]{2,0,1:T(4,128)(2,1)S(1)} async-done(((bf16[4,16,1216]{2,0,1:T(4,128)(2,1)}), bf16[4,16,1216]{2,0,1:T(4,128)(2,1)S(1)}, u32[]{:S(2)}, u32[]{:S(2)}) %all-to-all-start) | async-done | bytes 155680 | tf_op jit(solution)/shard_map/all_to_all | solution.py:28
  65.7 0.7 gather_fusion
  66.7 30.3 %all-reduce.2 = (f32[64]{0:T(128)S(1)}, f32[64]{0:T(128)S(1)}) all-reduce(f32[64]{0:T(128)S(1)} %fusion.10, f32[64]{0:T(128)S(1)} %get-tuple-element.13), channel_id=1, replica_groups=mesh['dom'=2,'vocab'=16] {'vocab'}, use_global_device_ids=true, to_apply=%region_8.9 | all-reduce | flops 128 | bytes 1024 | tf_op jit(solution)/shard_map/pmax | solution.py:52
  97.3 29.5 %all-reduce.1 = (f32[64]{0:T(128)S(1)}, f32[64]{0:T(128)S(1)}) all-reduce(f32[64]{0:T(128)S(1)} %get-tuple-element.15, f32[64]{0:T(128)S(1)} %get-tuple-element.16), channel_id=1, replica_groups=mesh['dom'=2,'vocab'=16] {'vocab'}, use_global_device_ids=true, to_apply=%region_10.11 | all-reduce | flops 128 | bytes 1024 | tf_op jit(solution)/shard_map/psum | solution.py:55
  126.8 0.3 select_reduce_fusion
  127.1 29.5 %all-reduce = (f32[64]{0:T(128)S(1)}, f32[64]{0:T(128)S(1)}) all-reduce(f32[64]{0:T(128)S(1)} %get-tuple-element.3, f32[64]{0:T(128)S(1)} %get-tuple-element.2), channel_id=1, replica_groups=mesh['dom'=2,'vocab'=16] {'vocab'}, use_global_device_ids=true, to_apply=%region_12.13 | all-reduce | flops 128 | bytes 1024 | tf_op jit(solution)/shard_map/psum | solution.py:67
  156.6 0.6 select_reduce_fusion.2
  157.2 0.6 select_divide_fusion
  157.9 11.3 %convolution_bitcast_fusion = f32[5120,64]{1,0:T(8,128)} fusion(bf16[1216,5120]{1,0:T(8,128)(2,1)} %param.9, f32[64,1216]{1,0:T(8,128)S(1)} %get-tuple-element.14, s32[64]{0:T(128)S(1)} %broadcast_subtract_fusion, f32[64]{0:T(128)S(1)} %get-tuple-element.6, f32[64]{0:T(128)S(1)} %log_add_fusion, f32[64]{0:T(128)S(1)} %log_add_fusion.1, ...), kind=kOutput, calls=%fused_computation.2 | convolution fusion | flops 798085120 | bytes 14542144
  170.6 60.0 %reduce-scatter.4.cloned.1.call-done = f32[320,64]{1,0:T(8,128)} async-done(((f32[5120,64]{1,0:T(8,128)}), f32[320,64]{1,0:T(8,128)}) %reduce-scatter.4.cloned.1.call-update) | async-done | bytes 81936
  230.5 1.6 copy.28
  (21 shorter events, 1.4 us)
Async XLA Ops:
  7.2 45.6 %copy-start = (bf16[4,19456]{1,0:T(4,128)(2,1)S(1)}, bf16[4,19456]{1,0:T(4,128)(2,1)}, u32[]{:S(2)}) copy-start(bf16[4,19456]{1,0:T(4,128)(2,1)} %param.10) | copy-start | bytes 466948
  8.6 45.1 %all-to-all-start.1 = ((bf16[4,16,38]{2,0,1:T(4,128)(2,1)}), bf16[4,16,38]{2,0,1:T(4,128)(2,1)S(1)}, u32[]{:S(2)}, u32[]{:S(2)}) async-start(bf16[4,16,38]{2,0,1:T(4,128)(2,1)} %copy.24), calls=%async_computation.1 | async-start | bytes 32768 | tf_op jit(solution)/shard_map/all_to_all | solution.py:29
  53.7 11.9 %all-to-all-start = ((bf16[4,16,1216]{2,0,1:T(4,128)(2,1)}), bf16[4,16,1216]{2,0,1:T(4,128)(2,1)S(1)}, u32[]{:S(2)}, u32[]{:S(2)}) async-start(bf16[4,16,1216]{2,0,1:T(4,128)(2,1)} %copy.23), calls=%async_computation | async-start | bytes 327680 | tf_op jit(solution)/shard_map/all_to_all | solution.py:28
  57.2 173.3 %reduce-scatter.4.cloned.1.call-start = ((), (), s32[]{:S(2)}) async-start(), calls=%async_computation.3 | async-start | bytes 2785280
Sparse Core Ops, SparseCore 0:
  169.3 61.1 reduce-scatter.3
where the time goes:
time: 241 us; the launch traced here: 240 us
  blocking collectives  114 us (47%)
  waiting for transfers between devices  67.3 us (28%)
  matrix products  19.8 us (8%)
  between operations  17.3 us (7%)
  starting transfers between devices  10.9 us (5%)
  local copies, waits for them, and re-layouts  6.06 us (3%)
  other arithmetic  5.11 us (2%)
    unnamed x2, waiting for transfers between devices  60 us
    pmax x1, blocking collectives, shards(): lax.pmax((jnp.max(logits, axis=1), jnp.max(teacher_logits, axis=1)), 'voc...  30.3 us
    psum x1, blocking collectives, shards(): lax.psum((jnp.sum(student_prob * (log_student - log_teacher), axis=1), ta...  29.5 us
    psum x1, blocking collectives, shards(): lax.psum((jnp.sum(jnp.exp(logits - student_max[:, None]), axis=1), jnp.su...  29.5 us
    all_gather x1, blocking collectives, shards(): gathered = lax.all_gather(hidden_states, 'vocab', axis=1, tiled=True)  24.3 us
    unnamed x1, matrix products  11.3 us
    dot_general x1, matrix products, shards(): lax.dot_general(gathered, head, contract_last, preferred_element_type=jnp...  8.45 us
    all_to_all x1, starting transfers between devices, shards(): lax.all_to_all(scales_split.astype(jnp.bfloat16), 'vocab', split_axis=1,...  7.39 us
  transfers between devices with their start and end apart: 3, of which 2 were waited for; matrix products, arithmetic and copies ran while one was open for 6% of the time, Pallas kernels for 0%

commit v1 on v0

v1 whole, which is shorter than its diff:
```python
import jax
import jax.numpy as jnp
from jax import lax
from jax.sharding import PartitionSpec as P

BLOCK = 32


sample_weight = 0.5


def to_all(piece, count):
    copies = jnp.broadcast_to(piece[None], (count,) + piece.shape)
    return lax.all_to_all(copies, "vocab", split_axis=0, concat_axis=0, tiled=True)


def shards(
    hidden_states, head, teacher_values, teacher_scales, token_ids, lengths, row_map, loss_scale
):
    count = lax.axis_size("vocab")
    own_index = lax.axis_index("vocab")
    tokens = hidden_states.shape[0]
    own_features = hidden_states.shape[1]
    shard_rows = head.shape[0]
    seq_length = tokens // lengths.shape[0]
    slot_rows = teacher_values.shape[0]
    contract_last = (((1,), (1,)), ((), ()))

    scaled = (
        teacher_values.astype(jnp.float32).reshape(slot_rows, -1, BLOCK) * teacher_scales[:, :, None]
    ).astype(jnp.bfloat16)
    scaled = scaled.reshape(slot_rows, count, shard_rows).transpose(1, 0, 2)
    arrived = lax.all_to_all(scaled, "vocab", split_axis=0, concat_axis=0, tiled=True)
    arrived = arrived.reshape(tokens, shard_rows)

    gathered = to_all(hidden_states, count).transpose(1, 0, 2).reshape(tokens, -1)
    logits = lax.dot_general(gathered, head, contract_last, preferred_element_type=jnp.float32)

    positions = jnp.arange(tokens, dtype=jnp.int32)
    owner = row_map[None, :] == positions[:, None]
    slot_of = jnp.sum(jnp.where(owner, positions[None, :], 0), axis=1)
    teacher = jnp.take(arrived, slot_of, axis=0).astype(jnp.float32)

    seq_ids = jnp.arange(lengths.shape[0], dtype=jnp.int32)
    own_length = jnp.sum(
        jnp.where((positions // seq_length)[:, None] == seq_ids[None, :], lengths[None, :], 0),
        axis=1,
    )
    live_mask = (positions % seq_length < own_length).astype(jnp.float32)
    live_count = jnp.sum(live_mask)

    local_ids = token_ids - own_index * shard_rows
    target_hit = local_ids[:, None] == jnp.arange(shard_rows, dtype=jnp.int32)[None, :]
    target_part = jnp.sum(jnp.where(target_hit, logits, 0.0), axis=1)
    student_top = jnp.max(logits, axis=1)
    teacher_top = jnp.max(teacher, axis=1)
    student_off = logits - student_top[:, None]
    teacher_off = teacher - teacher_top[:, None]
    student_exp = jnp.exp(student_off)
    student_sum = jnp.sum(student_exp, axis=1)
    teacher_sum = jnp.sum(jnp.exp(teacher_off), axis=1)
    cross_sum = jnp.sum(student_exp * (student_off - teacher_off), axis=1)

    stats = to_all(
        jnp.stack(
            [student_top, student_sum, teacher_top, teacher_sum, cross_sum, target_part]
        ),
        count,
    )
    tops, sums, teacher_tops, teacher_sums, crosses, targets = [stats[:, i] for i in range(6)]
    student_max = jnp.max(tops, axis=0)
    teacher_max = jnp.max(teacher_tops, axis=0)
    student_shift = tops - student_max[None, :]
    teacher_shift = teacher_tops - teacher_max[None, :]
    weight = jnp.exp(student_shift)
    student_total = jnp.sum(sums * weight, axis=0)
    teacher_total = jnp.sum(teacher_sums * jnp.exp(teacher_shift), axis=0)
    cross_total = jnp.sum(weight * (crosses + sums * (student_shift - teacher_shift)), axis=0)
    student_log = jnp.log(student_total)
    teacher_log = jnp.log(teacher_total)
    student_lse = student_max + student_log
    teacher_lse = teacher_max + teacher_log
    divergence = cross_total / student_total - (student_log - teacher_log)
    target = jnp.sum(targets, axis=0)

    per_token = divergence + sample_weight * (student_lse - target)
    loss = jnp.reshape(jnp.sum(live_mask * per_token) / live_count, (1,))
    token_weight = live_mask * loss_scale[0] / live_count
    log_student = logits - student_lse[:, None]
    log_teacher = teacher - teacher_lse[:, None]
    student_prob = jnp.exp(log_student)
    grad_logits = (
        token_weight[:, None]
        * (
            student_prob * (log_student - log_teacher - divergence[:, None])
            + sample_weight * (student_prob - target_hit.astype(jnp.float32))
        )
    ).astype(jnp.bfloat16)
    terms = jnp.dot(grad_logits, head, preferred_element_type=jnp.float32).astype(jnp.bfloat16)
    terms = terms.reshape(tokens, count, own_features).transpose(1, 0, 2)
    shares = lax.all_to_all(terms, "vocab", split_axis=0, concat_axis=0, tiled=True)
    grad_hidden = jnp.sum(shares.astype(jnp.float32), axis=0)
    return (grad_hidden.astype(jnp.bfloat16), loss)


def solution(mesh):
    in_specs = (
        P("dom", "vocab"),
        P("vocab", None),
        P(("dom", "vocab"), None),
        P(("dom", "vocab"), None),
        P("dom"),
        P("dom"),
        P("dom"),
        P(),
    )
    out_specs = (P("dom", "vocab"), P("dom"))
    return jax.shard_map(shards, mesh=mesh, in_specs=in_specs, out_specs=out_specs, check_vma=False)
```

time: 241 us -> 103 us (0.43)
  blocking collectives: 114 us -> 0 us
  waiting for transfers between devices: 67.3 us -> 47.8 us
  between operations: 17.3 us -> 3.93 us
  starting transfers between devices: 10.9 us -> 20 us
  matrix products: 19.8 us -> 15.5 us
  local copies, waits for them, and re-layouts: 6.06 us -> 9.91 us
    unnamed x2 -> x0, waiting for transfers between devices: 60 us -> none
    psum x2 -> x0, blocking collectives: 59 us -> none  [the longest x1 29.5 us: shards(): lax.psum((jnp.sum(student_prob * (log_student - log_teacher), axis=1), ta...]
    all_to_all x2 -> x4, waiting for transfers between devices: 7.33 us -> 47.8 us  [the longest x2 22.8 us: to_all(): lax.all_to_all(copies, 'vocab', split_axis=0, concat_axis=0, tiled=True)]
    pmax x1 -> x0, blocking collectives: 30.3 us -> none  [shards(): lax.pmax((jnp.max(logits, axis=1), jnp.max(teacher_logits, axis=1)), 'voc...]
    all_gather x1 -> x0, blocking collectives: 24.3 us -> none  [shards(): gathered = lax.all_gather(hidden_states, 'vocab', axis=1, tiled=True)]
    unnamed x1 -> x0, matrix products: 11.3 us -> none
    all_to_all x2 -> x4, starting transfers between devices: 10.9 us -> 20 us  [the longest x2 9.04 us: to_all(): lax.all_to_all(copies, 'vocab', split_axis=0, concat_axis=0, tiled=True)]
    dot_general x0 -> x1, matrix products: none -> 7.02 us  [shards(): jnp.dot(grad_logits, head, preferred_element_type=jnp.float32)]
  transfers between devices with their start and end apart: 3 -> 4, of which waited for: 2 -> 4; matrix products, arithmetic and copies ran while one was open for 6% -> 2% of each run, Pallas kernels for 0% -> 0%
where the time goes in v1:
time: 103 us; the launch traced here: 102 us
  waiting for transfers between devices  47.8 us (46%)
  starting transfers between devices  20 us (19%)
  matrix products  15.5 us (15%)
  local copies, waits for them, and re-layouts  9.91 us (10%)
  other arithmetic  4.93 us (5%)
  between operations  3.93 us (4%)
    all_to_all x2, waiting for transfers between devices, to_all(): lax.all_to_all(copies, 'vocab', split_axis=0, concat_axis=0, tiled=True)  22.8 us
    all_to_all x1, waiting for transfers between devices, shards(): lax.all_to_all(terms, 'vocab', split_axis=0, concat_axis=0, tiled=True)  17.3 us
    all_to_all x2, starting transfers between devices, to_all(): lax.all_to_all(copies, 'vocab', split_axis=0, concat_axis=0, tiled=True)  9.04 us
    dot_general x1, matrix products, shards(): lax.dot_general(gathered, head, contract_last, preferred_element_type=jnp...  8.45 us
    all_to_all x1, waiting for transfers between devices, shards(): lax.all_to_all(scaled, 'vocab', split_axis=0, concat_axis=0, tiled=True)  7.69 us
    all_to_all x1, starting transfers between devices, shards(): lax.all_to_all(scaled, 'vocab', split_axis=0, concat_axis=0, tiled=True)  7.39 us
    dot_general x1, matrix products, shards(): jnp.dot(grad_logits, head, preferred_element_type=jnp.float32)  7.02 us
    all_to_all x1, starting transfers between devices, shards(): lax.all_to_all(terms, 'vocab', split_axis=0, concat_axis=0, tiled=True)  3.61 us
  transfers between devices with their start and end apart: 4, of which 4 were waited for; matrix products, arithmetic and copies ran while one was open for 2% of the time, Pallas kernels for 0%

profile of v1, /device:TPU:0, one launch (start us, length us, event | category | flops | bytes accessed | tf_op | source)
XLA Modules:
  0.0 102.1 jit_solution(4470044252407005946)
XLA Ops:
  0.6 1.1 %mul.64 = f32[4,608,32]{2,1,0:T(8,128)S(1)} broadcast(f32[4,608]{1,0:T(4,128)} %param.11), dimensions={0,1} | broadcast | bytes 321024 | tf_op jit(solution)/shard_map/mul | solution.py:30
  2.1 1.1 %reshape.119 = f32[4,16,1216]{2,1,0:T(8,128)S(1)} reshape(bf16[4,19456]{1,0:T(4,128)(2,1)} %param.10) | data formatting | bytes 466944 | tf_op jit(solution)/shard_map/reshape | solution.py:30
  3.2 0.7 copy.31
  3.9 7.4 %all-to-all-start.1 = ((bf16[16,4,1216]{2,1,0:T(4,128)(2,1)}), bf16[16,4,1216]{2,1,0:T(4,128)(2,1)S(1)}, u32[]{:S(2)}, u32[]{:S(2)}) async-start(bf16[16,4,1216]{2,1,0:T(4,128)(2,1)} %copy.31), calls=%async_computation.1 | async-start | bytes 327680 | tf_op jit(solution)/shard_map/all_to_all | solution.py:33
  11.3 0.8 select_reduce_fusion.1
  12.1 7.7 %all-to-all-done.1 = bf16[16,4,1216]{2,1,0:T(4,128)(2,1)S(1)} async-done(((bf16[16,4,1216]{2,1,0:T(4,128)(2,1)}), bf16[16,4,1216]{2,1,0:T(4,128)(2,1)S(1)}, u32[]{:S(2)}, u32[]{:S(2)}) %all-to-all-start.1) | async-done | bytes 155680 | tf_op jit(solution)/shard_map/all_to_all | solution.py:33
  19.8 1.8 %broadcast_in_dim.44 = bf16[16,64,320]{2,1,0:T(8,128)(2,1)} broadcast(bf16[64,320]{1,0:T(8,128)(2,1)} %param.8), dimensions={1,2} | broadcast | bytes 696320 | tf_op jit(solution)/shard_map/broadcast_in_dim | solution.py:13
  21.6 3.6 %all-to-all-start = ((bf16[16,64,320]{2,1,0:T(8,128)(2,1)}), bf16[16,64,320]{2,1,0:T(8,128)(2,1)S(1)}, u32[]{:S(2)}, u32[]{:S(2)}) async-start(bf16[16,64,320]{2,1,0:T(8,128)(2,1)} %broadcast_in_dim.44), calls=%async_computation | async-start | bytes 1572864 | tf_op jit(solution)/shard_map/all_to_all | solution.py:14
  25.2 0.7 broadcast_subtract_fusion
  26.0 0.7 gather_fusion
  26.9 17.0 %all-to-all-done = bf16[16,64,320]{2,1,0:T(8,128)(2,1)S(1)} async-done(((bf16[16,64,320]{2,1,0:T(8,128)(2,1)}), bf16[16,64,320]{2,1,0:T(8,128)(2,1)S(1)}, u32[]{:S(2)}, u32[]{:S(2)}) %all-to-all-start) | async-done | bytes 655392 | tf_op jit(solution)/shard_map/all_to_all | solution.py:14
  44.3 0.6 reshape.112
  44.9 8.4 %fusion.26 = (f32[64]{0:T(128)S(1)}, f32[64,1216]{1,0:T(8,128)S(1)}) fusion(bf16[64,5120]{1,0:T(8,128)(2,1)S(1)} %reshape.112, bf16[1216,5120]{1,0:T(8,128)(2,1)} %param.9), kind=kOutput, calls=%fused_computation.57 | convolution fusion | flops 796995520 | bytes 13418752 | tf_op jit(solution)/shard_map/dot_general | solution.py:37
  53.8 0.7 reshape.129
  54.5 5.4 %all-to-all-start.2 = ((f32[16,1,384]{2,1,0:T(1,128)}), f32[16,1,384]{2,1,0:T(1,128)S(1)}, u32[]{:S(2)}, u32[]{:S(2)}) async-start(f32[16,1,384]{2,1,0:T(1,128)} %reshape.129), calls=%async_computation.2 | async-start | bytes 49152 | tf_op jit(solution)/shard_map/all_to_all | solution.py:14
  60.7 5.8 %all-to-all-done.2 = f32[16,1,384]{2,1,0:T(1,128)S(1)} async-done(((f32[16,1,384]{2,1,0:T(1,128)}), f32[16,1,384]{2,1,0:T(1,128)S(1)}, u32[]{:S(2)}, u32[]{:S(2)}) %all-to-all-start.2) | async-done | bytes 24608 | tf_op jit(solution)/shard_map/all_to_all | solution.py:14
  67.0 0.7 reduce.5
  68.5 0.6 select_divide_fusion
  69.2 7.0 %convolution_convert_fusion = bf16[64,5120]{1,0:T(8,128)(2,1)S(1)} fusion(bf16[1216,5120]{1,0:T(8,128)(2,1)} %param.9, f32[64,1216]{1,0:T(8,128)S(1)} %get-tuple-element.24, f32[64]{0:T(128)S(1)} %get-tuple-element.13, f32[64]{0:T(128)S(1)} %get-tuple-element.20, f32[64]{0:T(128)S(1)} %get-tuple-element.12, s32[64]{0:T(128)S(1)} %broadcast_subtract_fusion, ...), kind=kOutput, calls=%fused_computation.1 | convolution fusion | flops 798334976 | bytes 13575488 | tf_op jit(solution)/shard_map/dot_general | solution.py:99
  76.2 0.6 reshape.116
  76.9 1.1 %copy.43 = bf16[64,16,320]{2,0,1:T(8,128)(2,1)} copy(bf16[64,16,320]{2,1,0:T(8,128)(2,1)S(1)} %reshape.116) | data formatting | bytes 1310720 | tf_op jit(solution)/shard_map/reshape | solution.py:100
  77.9 3.6 %all-to-all-start.3 = ((bf16[16,64,320]{2,1,0:T(8,128)(2,1)}), bf16[16,64,320]{2,1,0:T(8,128)(2,1)S(1)}, u32[]{:S(2)}, u32[]{:S(2)}) async-start(bf16[16,64,320]{2,1,0:T(8,128)(2,1)} %bitcast.35), calls=%async_computation.3 | async-start | bytes 1572864 | tf_op jit(solution)/shard_map/all_to_all | solution.py:101
  82.9 17.3 %all-to-all-done.3 = bf16[16,64,320]{2,1,0:T(8,128)(2,1)S(1)} async-done(((bf16[16,64,320]{2,1,0:T(8,128)(2,1)}), bf16[16,64,320]{2,1,0:T(8,128)(2,1)S(1)}, u32[]{:S(2)}, u32[]{:S(2)}) %all-to-all-start.3) | async-done | bytes 655392 | tf_op jit(solution)/shard_map/all_to_all | solution.py:101
  100.2 0.7 reduce_sum.133
  (24 shorter events, 2.9 us)
Async XLA Ops:
  1.7 58.2 %copy-start = (s32[2]{0:T(128)S(1)}, s32[2]{0:T(128)}, u32[]{:S(2)}) copy-start(s32[2]{0:T(128)} %param.13) | copy-start | bytes 28
  3.9 15.9 %all-to-all-start.1 = ((bf16[16,4,1216]{2,1,0:T(4,128)(2,1)}), bf16[16,4,1216]{2,1,0:T(4,128)(2,1)S(1)}, u32[]{:S(2)}, u32[]{:S(2)}) async-start(bf16[16,4,1216]{2,1,0:T(4,128)(2,1)} %copy.31), calls=%async_computation.1 | async-start | bytes 327680 | tf_op jit(solution)/shard_map/all_to_all | solution.py:33
  21.6 22.3 %all-to-all-start = ((bf16[16,64,320]{2,1,0:T(8,128)(2,1)}), bf16[16,64,320]{2,1,0:T(8,128)(2,1)S(1)}, u32[]{:S(2)}, u32[]{:S(2)}) async-start(bf16[16,64,320]{2,1,0:T(8,128)(2,1)} %broadcast_in_dim.44), calls=%async_computation | async-start | bytes 1572864 | tf_op jit(solution)/shard_map/all_to_all | solution.py:14
  54.5 12.0 %all-to-all-start.2 = ((f32[16,1,384]{2,1,0:T(1,128)}), f32[16,1,384]{2,1,0:T(1,128)S(1)}, u32[]{:S(2)}, u32[]{:S(2)}) async-start(f32[16,1,384]{2,1,0:T(1,128)} %reshape.129), calls=%async_computation.2 | async-start | bytes 49152 | tf_op jit(solution)/shard_map/all_to_all | solution.py:14
  77.9 22.3 %all-to-all-start.3 = ((bf16[16,64,320]{2,1,0:T(8,128)(2,1)}), bf16[16,64,320]{2,1,0:T(8,128)(2,1)S(1)}, u32[]{:S(2)}, u32[]{:S(2)}) async-start(bf16[16,64,320]{2,1,0:T(8,128)(2,1)} %bitcast.35), calls=%async_computation.3 | async-start | bytes 1572864 | tf_op jit(solution)/shard_map/all_to_all | solution.py:101

commit v2 on v1

--- a/solution.py
+++ b/solution.py
@@ -1,9 +1,15 @@
+import functools
+
 import jax
 import jax.numpy as jnp
 from jax import lax
+from jax.experimental import pallas as pl
+from jax.experimental.pallas import tpu as pltpu
 from jax.sharding import PartitionSpec as P
 
 BLOCK = 32
+LANES = 128
+STATS = 8
 
 
 sample_weight = 0.5
@@ -12,6 +18,256 @@
 def to_all(piece, count):
     copies = jnp.broadcast_to(piece[None], (count,) + piece.shape)
     return lax.all_to_all(copies, "vocab", split_axis=0, concat_axis=0, tiled=True)
+
+
+def scaled_teacher(teacher_values, teacher_scales, count, shard_rows):
+    slot_rows = teacher_values.shape[0]
+    scaled = (
+        teacher_values.astype(jnp.float32).reshape(slot_rows, -1, BLOCK) * teacher_scales[:, :, None]
+    ).astype(jnp.bfloat16)
+    scaled = scaled.reshape(slot_rows, count, shard_rows).transpose(1, 0, 2)
+    arrived = lax.all_to_all(scaled, "vocab", split_axis=0, concat_axis=0, tiled=True)
+    return arrived.reshape(count * slot_rows, shard_rows)
+
+
+def merge_stats(tops, sums, teacher_tops, teacher_sums, crosses):
+    top = jnp.max(tops, axis=0)
+    teacher_top = jnp.max(teacher_tops, axis=0)
+    shift = tops - top[None]
+    teacher_shift = teacher_tops - teacher_top[None]
+    weight = jnp.exp(shift)
+    total = jnp.sum(sums * weight, axis=0)
+    teacher_total = jnp.sum(teacher_sums * jnp.exp(teacher_shift), axis=0)
+    cross = jnp.sum(weight * (crosses + sums * (shift - teacher_shift)), axis=0)
+    return top, total, teacher_top, teacher_total, cross
+
+
+def swap_cores(count):
+    return [(i, i ^ 1) for i in range(count)]
+
+
+def next_chips(count, step):
+    return [(i, (i + 2 * step) % count) for i in range(count)]
+
+
+def gather_chips(piece, count):
+    return [piece] + [
+        lax.ppermute(piece, "vocab", next_chips(count, step)) for step in range(1, count // 2)
+    ]
+
+
+def all_stats(stats, count):
+    own_index = lax.axis_index("vocab")
+    reach = 1
+    while reach < count:
+        other = lax.ppermute(stats, "vocab", [(i, i ^ reach) for i in range(count)])
+        upper = (own_index & reach) > 0
+        low = jnp.where(upper, other, stats)
+        high = jnp.where(upper, stats, other)
+        pair = jnp.stack([low, high])
+        top, total, teacher_top, teacher_total, cross = merge_stats(
+            *[pair[:, i : i + 1] for i in range(5)]
+        )
+        target = low[5:6] + high[5:6]
+        stats = jnp.concatenate(
+            [top, total, teacher_top, teacher_total, cross, target, target, target]
+        )
+        reach *= 2
+    return stats
+
+
+def logits_kernel(
+    place_ref,
+    *refs,
+    chips,
+    width,
+):
+    near = refs[:chips]
+    far = refs[chips : 2 * chips]
+    head_ref, arrived_ref, map_ref, ids_ref, logits_ref, teacher_ref, stats_ref, hidden = refs[
+        2 * chips :
+    ]
+    own_index = place_ref[0]
+    chip, core = own_index // 2, own_index % 2
+    tokens, shard_rows = logits_ref.shape
+    for step in range(chips):
+        mine, other = near[step][...], far[step][...]
+        hidden[step] = jnp.where(
+            core == 0,
+            jnp.concatenate([mine, other], axis=1),
+            jnp.concatenate([other, mine], axis=1),
+        )
+
+    def add(step, _):
+        source = lax.rem(chip - step + chips, chips)
+        columns = pl.ds(pl.multiple_of(source * width, LANES), width)
+        logits_ref[...] += lax.dot_general(
+            hidden[step],
+            head_ref[:, columns],
+            (((1,), (1,)), ((), ())),
+            preferred_element_type=jnp.float32,
+        )
+
+    logits_ref[...] = jnp.zeros_like(logits_ref)
+    lax.fori_loop(0, chips, add, None)
+
+    token = lax.broadcasted_iota(jnp.int32, (tokens, tokens), 0)
+    slot = lax.broadcasted_iota(jnp.int32, (tokens, tokens), 1)
+    owner = (map_ref[...] == token).astype(jnp.float32)
+    named = jnp.max(owner, axis=1, keepdims=True)
+    owner = jnp.where((slot == 0) & (named == 0.0), 1.0, owner)
+    teacher = jnp.dot(
+        owner.astype(jnp.bfloat16), arrived_ref[...], preferred_element_type=jnp.float32
+    )
+    teacher_ref[...] = teacher
+
+    logits = logits_ref[...]
+    top = jnp.max(logits, axis=1, keepdims=True)
+    teacher_top = jnp.max(teacher, axis=1, keepdims=True)
+    off = logits - top
+    teacher_off = teacher - teacher_top
+    exps = jnp.exp(off)
+    total = jnp.sum(exps, axis=1, keepdims=True)
+    teacher_total = jnp.sum(jnp.exp(teacher_off), axis=1, keepdims=True)
+    cross = jnp.sum(exps * (off - teacher_off), axis=1, keepdims=True)
+    entry = lax.broadcasted_iota(jnp.int32, (tokens, shard_rows), 1)
+    hit = entry == ids_ref[...] - own_index * shard_rows
+    target = jnp.sum(jnp.where(hit, logits, 0.0), axis=1, keepdims=True)
+    lane = lax.broadcasted_iota(jnp.int32, (tokens, LANES), 1)
+    table = jnp.zeros((tokens, LANES), jnp.float32)
+    for place, column in enumerate((top, total, teacher_top, teacher_total, cross, target)):
+        table = jnp.where(lane == place, column, table)
+    stats_ref[...] = table.T[:STATS]
+
+
+def grads_kernel(
+    place_ref,
+    lengths_ref,
+    scale_ref,
+    logits_ref,
+    teacher_ref,
+    stats_ref,
+    ids_ref,
+    head_ref,
+    keep_ref,
+    give_ref,
+    loss_ref,
+    grads,
+    *,
+    chips,
+    width,
+):
+    own_index = place_ref[0]
+    chip, core = own_index // 2, own_index % 2
+    tokens, shard_rows = logits_ref.shape
+    half = width // 2
+    seqs = lengths_ref.shape[0]
+    seq_length = tokens // seqs
+    stats = jnp.concatenate(
+        [stats_ref[...], jnp.zeros((LANES - STATS, tokens), jnp.float32)], axis=0
+    ).T
+    top, total, teacher_top, teacher_total, cross, target = [stats[:, i : i + 1] for i in range(6)]
+    student_log = jnp.log(total)
+    teacher_log = jnp.log(teacher_total)
+    student_lse = top + student_log
+    teacher_lse = teacher_top + teacher_log
+    divergence = cross / total - (student_log - teacher_log)
+
+    position = lax.broadcasted_iota(jnp.int32, (tokens, 1), 0)
+    own_length = jnp.zeros((tokens, 1), jnp.int32)
+    for seq in range(seqs):
+        inside = (position >= seq * seq_length) & (position < (seq + 1) * seq_length)
+        own_length = jnp.where(inside, lengths_ref[seq] + seq * seq_length, own_length)
+    live = (position < own_length).astype(jnp.float32)
+    live_count = jnp.sum(live, axis=0, keepdims=True)
+    per_token = divergence + sample_weight * (student_lse - target)
+    loss_ref[...] = jnp.sum(live * per_token, axis=0, keepdims=True) / live_count
+    token_weight = live * scale_ref[0] / live_count
+
+    log_student = logits_ref[...] - student_lse
+    log_teacher = teacher_ref[...] - teacher_lse
+    prob = jnp.exp(log_student)
+    entry = lax.broadcasted_iota(jnp.int32, (tokens, shard_rows), 1)
+    hit = (entry == ids_ref[...] - own_index * shard_rows).astype(jnp.float32)
+    grads[...] = (
+        token_weight
+        * (prob * (log_student - log_teacher - divergence) + sample_weight * (prob - hit))
+    ).astype(jnp.bfloat16)
+
+    def put(step, _):
+        to = lax.rem(chip + step, chips)
+        columns = pl.ds(pl.multiple_of(to * width, LANES), width)
+        terms = jnp.dot(grads[...], head_ref[:, columns], preferred_element_type=jnp.float32)
+        first, second = terms[:, :half], terms[:, half:]
+        keep_ref[step] = jnp.where(core == 0, first, second)
+        give_ref[step] = jnp.where(core == 0, second, first).astype(jnp.bfloat16)
+
+    lax.fori_loop(0, chips, put, None)
+
+
+def paired_shards(
+    hidden_states, head, teacher_values, teacher_scales, token_ids, lengths, row_map, loss_scale
+):
+    count = lax.axis_size("vocab")
+    own_index = lax.axis_index("vocab")
+    chips = count // 2
+    tokens, half = hidden_states.shape
+    width = 2 * half
+    shard_rows = head.shape[0]
+    place = jnp.reshape(own_index, (1,))
+    vmem = pl.BlockSpec(memory_space=pltpu.VMEM)
+    smem = pl.BlockSpec(memory_space=pltpu.SMEM)
+
+    near = gather_chips(hidden_states, count)
+    far = [lax.ppermute(piece, "vocab", swap_cores(count)) for piece in near]
+    arrived = scaled_teacher(teacher_values, teacher_scales, count, shard_rows)
+    ids = token_ids[:, None]
+    logits, teacher, stats = pl.pallas_call(
+        functools.partial(logits_kernel, chips=chips, width=width),
+        out_shape=(
+            jax.ShapeDtypeStruct((tokens, shard_rows), jnp.float32),
+            jax.ShapeDtypeStruct((tokens, shard_rows), jnp.float32),
+            jax.ShapeDtypeStruct((STATS, tokens), jnp.float32),
+        ),
+        in_specs=[smem] + [vmem] * (2 * chips + 4),
+        out_specs=[vmem] * 3,
+        scratch_shapes=[pltpu.VMEM((chips, tokens, width), jnp.bfloat16)],
+        compiler_params=pltpu.CompilerParams(vmem_limit_bytes=VMEM_LIMIT),
+        name="logits",
+    )(place, *near, *far, in_vmem(head), arrived, row_map[None, :], ids)
+
+    stats = all_stats(stats, count)
+
+    keep, give, loss = pl.pallas_call(
+        functools.partial(grads_kernel, chips=chips, width=width),
+        out_shape=(
+            jax.ShapeDtypeStruct((chips, tokens, half), jnp.float32),
+            jax.ShapeDtypeStruct((chips, tokens, half), jnp.bfloat16),
+            jax.ShapeDtypeStruct((1, 1), jnp.float32),
+        ),
+        in_specs=[smem] * 3 + [vmem] * 5,
+        out_specs=[vmem] * 3,
+        scratch_shapes=[pltpu.VMEM((tokens, shard_rows), jnp.bfloat16)],
+        compiler_params=pltpu.CompilerParams(vmem_limit_bytes=VMEM_LIMIT),
+        name="grads",
+    )(place, lengths, loss_scale, logits, teacher, stats, ids, in_vmem(head))
+
+    taken = lax.ppermute(give, "vocab", swap_cores(count))
+    sums = keep + taken.astype(jnp.float32)
+    total = sums[0]
+    for step in range(1, chips):
+        share = lax.ppermute(
+            sums[step].astype(jnp.bfloat16), "vocab", next_chips(count, step)
+        )
+        total = total + share.astype(jnp.float32)
+    return total.astype(jnp.bfloat16), jnp.reshape(loss, (1,))
+
+
+VMEM_LIMIT = 40 * 1024 * 1024
+
+
+def in_vmem(array):
+    return pltpu.with_memory_space_constraint(array, pltpu.VMEM)
 
 
 def shards(
@@ -23,16 +279,9 @@
     own_features = hidden_states.shape[1]
     shard_rows = head.shape[0]
     seq_length = tokens // lengths.shape[0]
-    slot_rows = teacher_values.shape[0]
     contract_last = (((1,), (1,)), ((), ()))
 
-    scaled = (
-        teacher_values.astype(jnp.float32).reshape(slot_rows, -1, BLOCK) * teacher_scales[:, :, None]
-    ).astype(jnp.bfloat16)
-    scaled = scaled.reshape(slot_rows, count, shard_rows).transpose(1, 0, 2)
-    arrived = lax.all_to_all(scaled, "vocab", split_axis=0, concat_axis=0, tiled=True)
-    arrived = arrived.reshape(tokens, shard_rows)
-
+    arrived = scaled_teacher(teacher_values, teacher_scales, count, shard_rows)
     gathered = to_all(hidden_states, count).transpose(1, 0, 2).reshape(tokens, -1)
     logits = lax.dot_general(gathered, head, contract_last, preferred_element_type=jnp.float32)
 
@@ -68,14 +317,9 @@
         count,
     )
     tops, sums, teacher_tops, teacher_sums, crosses, targets = [stats[:, i] for i in range(6)]
-    student_max = jnp.max(tops, axis=0)
-    teacher_max = jnp.max(teacher_tops, axis=0)
-    student_shift = tops - student_max[None, :]
-    teacher_shift = teacher_tops - teacher_max[None, :]
-    weight = jnp.exp(student_shift)
-    student_total = jnp.sum(sums * weight, axis=0)
-    teacher_total = jnp.sum(teacher_sums * jnp.exp(teacher_shift), axis=0)
-    cross_total = jnp.sum(weight * (crosses + sums * (student_shift - teacher_shift)), axis=0)
+    student_max, student_total, teacher_max, teacher_total, cross_total = merge_stats(
+        tops, sums, teacher_tops, teacher_sums, crosses
+    )
     student_log = jnp.log(student_total)
     teacher_log = jnp.log(teacher_total)
     student_lse = student_max + student_log
@@ -103,6 +347,13 @@
     return (grad_hidden.astype(jnp.bfloat16), loss)
 
 
+def any_shards(*arrays):
+    pair_width = 2 * arrays[0].shape[1]
+    if lax.axis_size("vocab") > 2 and pair_width % LANES == 0:
+        return paired_shards(*arrays)
+    return shards(*arrays)
+
+
 def solution(mesh):
     in_specs = (
         P("dom", "vocab"),
@@ -115,4 +366,6 @@
         P(),
     )
     out_specs = (P("dom", "vocab"), P("dom"))
-    return jax.shard_map(shards, mesh=mesh, in_specs=in_specs, out_specs=out_specs, check_vma=False)
+    return jax.shard_map(
+        any_shards, mesh=mesh, in_specs=in_specs, out_specs=out_specs, check_vma=False
+    )

time: 103 us -> 83.7 us (0.81)
  waiting for transfers between devices: 47.8 us -> 25.2 us
  matrix products: 15.5 us -> 0 us
  Pallas kernels: 0 us -> 10.8 us
  starting transfers between devices: 20 us -> 30 us
  local copies, waits for them, and re-layouts: 9.91 us -> 14.7 us
  other arithmetic: 4.93 us -> 1.12 us
  between operations: 3.93 us -> 1.46 us
    all_to_all x4 -> x1, waiting for transfers between devices: 47.8 us -> 0.01 us  [scaled_teacher(): lax.all_to_all(scaled, 'vocab', split_axis=0, concat_axis=0, tiled=True)]
    ppermute x0 -> x27, waiting for transfers between devices: none -> 25.2 us  [the longest x4 11.1 us: all_stats(): other = lax.ppermute(stats, 'vocab', [(i, i ^ reach) for i in range(count)])]
    ppermute x0 -> x27, starting transfers between devices: none -> 22.7 us  [the longest x7 10.5 us: gather_chips(): lax.ppermute(piece, 'vocab', next_chips(count, step))]
    dot_general x2 -> x0, matrix products: 15.5 us -> none  [the longest x1 8.45 us: shards(): lax.dot_general(gathered, head, contract_last, preferred_element_type=jnp...]
    all_to_all x4 -> x1, starting transfers between devices: 20 us -> 7.39 us  [scaled_teacher(): lax.all_to_all(scaled, 'vocab', split_axis=0, concat_axis=0, tiled=True)]
    pallas_call x0 -> x2, Pallas kernels: none -> 10.8 us  [the longest x1 5.66 us: paired_shards(): pl.pallas_call(functools.partial(logits_kernel, chips=chips, width=width)...]
    unnamed x4 -> x10, local copies, waits for them, and re-layouts: 0.79 us -> 10.5 us
    reduce_sum x7 -> x4, other arithmetic: 2.61 us -> 0.14 us  [merge_stats(): cross = jnp.sum(weight * (crosses + sums * (shift - teacher_shift)), axis=0)]
  transfers between devices with their start and end apart: 4 -> 28, of which waited for: 4 -> 14; matrix products, arithmetic and copies ran while one was open for 2% -> 1% of each run, Pallas kernels for 0% -> 0%
where the time goes in v2:
time: 83.7 us; the launch traced here: 83.3 us
  starting transfers between devices  30 us (36%)
  waiting for transfers between devices  25.2 us (30%)
  local copies, waits for them, and re-layouts  14.7 us (18%)
  Pallas kernels  10.8 us (13%)
  between operations  1.46 us (2%)
  other arithmetic  1.12 us (1%)
    ppermute x4, waiting for transfers between devices, all_stats(): other = lax.ppermute(stats, 'vocab', [(i, i ^ reach) for i in range(count)])  11.1 us
    unnamed x10, local copies, waits for them, and re-layouts  10.5 us
    ppermute x7, starting transfers between devices, gather_chips(): lax.ppermute(piece, 'vocab', next_chips(count, step))  10.5 us
    ppermute x7, starting transfers between devices, paired_shards(): lax.ppermute(sums[step].astype(jnp.bfloat16), 'vocab', next_chips(count,...  9.15 us
    ppermute x7, waiting for transfers between devices, gather_chips(): lax.ppermute(piece, 'vocab', next_chips(count, step))  8.08 us
    all_to_all x1, starting transfers between devices, scaled_teacher(): lax.all_to_all(scaled, 'vocab', split_axis=0, concat_axis=0, tiled=True)  7.39 us
    pallas_call x1, Pallas kernels, paired_shards(): pl.pallas_call(functools.partial(logits_kernel, chips=chips, width=width)...  5.66 us
    pallas_call x1, Pallas kernels, paired_shards(): pl.pallas_call(functools.partial(grads_kernel, chips=chips, width=width),...  5.12 us
  transfers between devices with their start and end apart: 28, of which 14 were waited for; matrix products, arithmetic and copies ran while one was open for 1% of the time, Pallas kernels for 0%

profile of v2, /device:TPU:0, one launch (start us, length us, event | category | flops | bytes accessed | tf_op | source)
XLA Modules:
  0.0 83.3 jit_solution(4165141420150633570)
XLA Ops:
  0.6 1.1 %mul.59 = f32[4,608,32]{2,1,0:T(8,128)S(1)} broadcast(f32[4,608]{1,0:T(4,128)} %param.11), dimensions={0,1} | broadcast | bytes 321024 | tf_op jit(solution)/shard_map/mul | solution.py:26
  2.1 1.1 %reshape.88 = f32[4,16,1216]{2,1,0:T(8,128)S(1)} reshape(bf16[4,19456]{1,0:T(4,128)(2,1)} %param.10) | data formatting | bytes 466944 | tf_op jit(solution)/shard_map/reshape | solution.py:26
  3.9 7.4 %all-to-all-start = ((bf16[16,4,1216]{2,1,0:T(4,128)(2,1)}), bf16[16,4,1216]{2,1,0:T(4,128)(2,1)S(1)}, u32[]{:S(2)}, u32[]{:S(2)}) async-start(bf16[16,4,1216]{2,1,0:T(4,128)(2,1)} %copy.16), calls=%async_computation | async-start | bytes 327680 | tf_op jit(solution)/shard_map/all_to_all | solution.py:29
  11.3 2.8 %collective-permute-start.2 = (bf16[64,320]{1,0:T(8,128)(2,1)}, bf16[64,320]{1,0:T(8,128)(2,1)S(1)}, u32[]{:S(2)}, u32[]{:S(2)}) collective-permute-start(bf16[64,320]{1,0:T(8,128)(2,1)} %refs_0_.1), channel_id=1, source_target_pairs={{0,6},{1,7},{2,8},{3,9},{4,10},{5,11},{6,12},{7,13},{8,14},{9,15},... | collective-permute-start | bytes 122888 | tf_op jit(solution)/shard_map/ppermute | solution.py:55
  14.2 2.4 %collective-permute-start.3 = (bf16[64,320]{1,0:T(8,128)(2,1)}, bf16[64,320]{1,0:T(8,128)(2,1)S(1)}, u32[]{:S(2)}, u32[]{:S(2)}) collective-permute-start(bf16[64,320]{1,0:T(8,128)(2,1)} %refs_0_.1), channel_id=1, source_target_pairs={{0,8},{1,9},{2,10},{3,11},{4,12},{5,13},{6,14},{7,15},{8,0},{9,1},... | collective-permute-start | bytes 122888 | tf_op jit(solution)/shard_map/ppermute | solution.py:55
  16.5 1.5 %collective-permute-start.4 = (bf16[64,320]{1,0:T(8,128)(2,1)}, bf16[64,320]{1,0:T(8,128)(2,1)S(1)}, u32[]{:S(2)}, u32[]{:S(2)}) collective-permute-start(bf16[64,320]{1,0:T(8,128)(2,1)} %refs_0_.1), channel_id=1, source_target_pairs={{0,10},{1,11},{2,12},{3,13},{4,14},{5,15},{6,0},{7,1},{8,2},{9,3},... | collective-permute-start | bytes 122888 | tf_op jit(solution)/shard_map/ppermute | solution.py:55
  18.0 1.5 %collective-permute-start.5 = (bf16[64,320]{1,0:T(8,128)(2,1)}, bf16[64,320]{1,0:T(8,128)(2,1)S(1)}, u32[]{:S(2)}, u32[]{:S(2)}) collective-permute-start(bf16[64,320]{1,0:T(8,128)(2,1)} %refs_0_.1), channel_id=1, source_target_pairs={{0,12},{1,13},{2,14},{3,15},{4,0},{5,1},{6,2},{7,3},{8,4},{9,5},{1... | collective-permute-start | bytes 122888 | tf_op jit(solution)/shard_map/ppermute | solution.py:55
  19.4 1.5 %collective-permute-start.6 = (bf16[64,320]{1,0:T(8,128)(2,1)}, bf16[64,320]{1,0:T(8,128)(2,1)S(1)}, u32[]{:S(2)}, u32[]{:S(2)}) collective-permute-start(bf16[64,320]{1,0:T(8,128)(2,1)} %refs_0_.1), channel_id=1, source_target_pairs={{0,14},{1,15},{2,0},{3,1},{4,2},{5,3},{6,4},{7,5},{8,6},{9,7},{10,... | collective-permute-start | bytes 122888 | tf_op jit(solution)/shard_map/ppermute | solution.py:55
  20.9 2.6 %collective-permute-done.2.refs_3_ = bf16[64,320]{1,0:T(8,128)(2,1)S(1)} collective-permute-done((bf16[64,320]{1,0:T(8,128)(2,1)}, bf16[64,320]{1,0:T(8,128)(2,1)S(1)}, u32[]{:S(2)}, u32[]{:S(2)}) %collective-permute-start.2) | collective-permute-done | bytes 40992 | tf_op jit(solution)/shard_map/ppermute | solution.py:55
  25.2 5.3 %collective-permute-done.refs_1_ = bf16[64,320]{1,0:T(8,128)(2,1)S(1)} collective-permute-done((bf16[64,320]{1,0:T(8,128)(2,1)}, bf16[64,320]{1,0:T(8,128)(2,1)S(1)}, u32[]{:S(2)}, u32[]{:S(2)}) %collective-permute-start) | collective-permute-done | bytes 40992 | tf_op jit(solution)/shard_map/ppermute | solution.py:55
  32.8 4.5 %copy-done = bf16[1216,5120]{1,0:T(8,128)(2,1)S(1)} copy-done((bf16[1216,5120]{1,0:T(8,128)(2,1)S(1)}, bf16[1216,5120]{1,0:T(8,128)(2,1)}, u32[]{:S(2)}) %copy-start) | copy-done | bytes 12451864
  38.7 5.7 %logits.1 = (f32[64,1216]{1,0:T(8,128)S(1)}, f32[64,1216]{1,0:T(8,128)S(1)}, f32[8,64]{1,0:T(8,128)S(1)}) custom-call(s32[1]{0:T(128)} %bitcast.place_ref, bf16[64,320]{1,0:T(8,128)(2,1)S(1)} %copy-done.2, bf16[64,320]{1,0:T(8,128)(2,1)S(1)} %collective-permute-done.refs_1_, bf16[64,320]{1,0:T(8,128)(2,1)S(1)} %collective-permute-done.1.refs_2_, ...), custom_call_target="tpu_custom_call" | custom-call | tf_op jit(solution)/shard_map/logits/pallas_call | solution.py:225
  44.6 1.0 %collective-permute-done.15 = f32[8,64]{1,0:T(8,128)S(1)} collective-permute-done((f32[8,64]{1,0:T(8,128)S(1)}, f32[8,64]{1,0:T(8,128)S(1)}, u32[]{:S(2)}, u32[]{:S(2)}) %collective-permute-start.15) | collective-permute-done | bytes 2080 | tf_op jit(solution)/shard_map/ppermute | solution.py:63
  46.5 2.9 %collective-permute-done.16 = f32[8,64]{1,0:T(8,128)S(1)} collective-permute-done((f32[8,64]{1,0:T(8,128)S(1)}, f32[8,64]{1,0:T(8,128)S(1)}, u32[]{:S(2)}, u32[]{:S(2)}) %collective-permute-start.16) | collective-permute-done | bytes 2080 | tf_op jit(solution)/shard_map/ppermute | solution.py:63
  49.6 3.6 %collective-permute-done.17 = f32[8,64]{1,0:T(8,128)S(1)} collective-permute-done((f32[8,64]{1,0:T(8,128)S(1)}, f32[8,64]{1,0:T(8,128)S(1)}, u32[]{:S(2)}, u32[]{:S(2)}) %collective-permute-start.17) | collective-permute-done | bytes 2080 | tf_op jit(solution)/shard_map/ppermute | solution.py:63
  54.1 3.7 %collective-permute-done.18 = f32[8,64]{1,0:T(8,128)S(1)} collective-permute-done((f32[8,64]{1,0:T(8,128)S(1)}, f32[8,64]{1,0:T(8,128)S(1)}, u32[]{:S(2)}, u32[]{:S(2)}) %collective-permute-start.18) | collective-permute-done | bytes 2080 | tf_op jit(solution)/shard_map/ppermute | solution.py:63
  57.9 4.5 %copy-done.1 = bf16[1216,5120]{1,0:T(8,128)(2,1)S(1)} copy-done((bf16[1216,5120]{1,0:T(8,128)(2,1)S(1)}, bf16[1216,5120]{1,0:T(8,128)(2,1)}, u32[]{:S(2)}) %copy-start.1) | copy-done | bytes 12451864
  62.5 5.1 %grads.1 = (f32[8,64,320]{2,1,0:T(8,128)S(1)}, bf16[8,64,320]{2,1,0:T(8,128)(2,1)S(1)}, f32[1,1]{1,0:T(1,128)}) custom-call(s32[1]{0:T(128)} %bitcast.place_ref, s32[2]{0:T(128)S(1)} %copy-done.4, f32[1]{0:T(128)S(6)} %copy.19.scale_ref, f32[64,1216]{1,0:T(8,128)S(1)} %get-tuple-element.8.logits_ref, f32[64,1216]{1,0:T(8,128)S(1)} %get-tuple-element.9.teacher_ref, ...), custom_call_target="tpu_custom_call" | custom-call | tf_op jit(solution)/shard_map/grads/pallas_call | solution.py:241
  67.6 1.7 %collective-permute-done.19 = bf16[8,64,320]{2,1,0:T(8,128)(2,1)S(1)} collective-permute-done((bf16[8,64,320]{2,1,0:T(8,128)(2,1)S(1)}, bf16[8,64,320]{2,1,0:T(8,128)(2,1)S(1)}, u32[]{:S(2)}, u32[]{:S(2)}) %collective-permute-start.19) | collective-permute-done | bytes 327712 | tf_op jit(solution)/shard_map/ppermute | solution.py:255
  70.3 2.7 %collective-permute-start.22 = (bf16[64,320]{1,0:T(8,128)(2,1)S(1)}, bf16[64,320]{1,0:T(8,128)(2,1)S(1)}, u32[]{:S(2)}, u32[]{:S(2)}) collective-permute-start(bf16[64,320]{1,0:T(8,128)(2,1)S(1)} %get-tuple-element.41), channel_id=1, source_target_pairs={{0,6},{1,7},{2,8},{3,9},{4,10},{5,11},{6,12},{7,13},{8,14},{9,15},... | collective-permute-start | bytes 122888 | tf_op jit(solution)/shard_map/ppermute | solution.py:259
  73.0 1.8 %collective-permute-start.23 = (bf16[64,320]{1,0:T(8,128)(2,1)S(1)}, bf16[64,320]{1,0:T(8,128)(2,1)S(1)}, u32[]{:S(2)}, u32[]{:S(2)}) collective-permute-start(bf16[64,320]{1,0:T(8,128)(2,1)S(1)} %get-tuple-element.40), channel_id=1, source_target_pairs={{0,8},{1,9},{2,10},{3,11},{4,12},{5,13},{6,14},{7,15},{8,0},{9,1},... | collective-permute-start | bytes 122888 | tf_op jit(solution)/shard_map/ppermute | solution.py:259
  74.9 1.3 %collective-permute-start.24 = (bf16[64,320]{1,0:T(8,128)(2,1)S(1)}, bf16[64,320]{1,0:T(8,128)(2,1)S(1)}, u32[]{:S(2)}, u32[]{:S(2)}) collective-permute-start(bf16[64,320]{1,0:T(8,128)(2,1)S(1)} %get-tuple-element.39), channel_id=1, source_target_pairs={{0,10},{1,11},{2,12},{3,13},{4,14},{5,15},{6,0},{7,1},{8,2},{9,3},... | collective-permute-start | bytes 122888 | tf_op jit(solution)/shard_map/ppermute | solution.py:259
  77.0 1.6 %collective-permute-start.25 = (bf16[64,320]{1,0:T(8,128)(2,1)S(1)}, bf16[64,320]{1,0:T(8,128)(2,1)S(1)}, u32[]{:S(2)}, u32[]{:S(2)}) collective-permute-start(bf16[64,320]{1,0:T(8,128)(2,1)S(1)} %get-tuple-element.38), channel_id=1, source_target_pairs={{0,12},{1,13},{2,14},{3,15},{4,0},{5,1},{6,2},{7,3},{8,4},{9,5},{1... | collective-permute-start | bytes 122888 | tf_op jit(solution)/shard_map/ppermute | solution.py:259
  80.1 1.5 %collective-permute-done.24 = bf16[64,320]{1,0:T(8,128)(2,1)S(1)} collective-permute-done((bf16[64,320]{1,0:T(8,128)(2,1)S(1)}, bf16[64,320]{1,0:T(8,128)(2,1)S(1)}, u32[]{:S(2)}, u32[]{:S(2)}) %collective-permute-start.24) | collective-permute-done | bytes 40992 | tf_op jit(solution)/shard_map/ppermute | solution.py:259
  (74 shorter events, 13.1 us)
Async XLA Ops:
  3.9 28.4 %all-to-all-start = ((bf16[16,4,1216]{2,1,0:T(4,128)(2,1)}), bf16[16,4,1216]{2,1,0:T(4,128)(2,1)S(1)}, u32[]{:S(2)}, u32[]{:S(2)}) async-start(bf16[16,4,1216]{2,1,0:T(4,128)(2,1)} %copy.16), calls=%async_computation | async-start | bytes 327680 | tf_op jit(solution)/shard_map/all_to_all | solution.py:29
  11.3 12.2 %collective-permute-start.2 = (bf16[64,320]{1,0:T(8,128)(2,1)}, bf16[64,320]{1,0:T(8,128)(2,1)S(1)}, u32[]{:S(2)}, u32[]{:S(2)}) collective-permute-start(bf16[64,320]{1,0:T(8,128)(2,1)} %refs_0_.1), channel_id=1, source_target_pairs={{0,6},{1,7},{2,8},{3,9},{4,10},{5,11},{6,12},{7,13},{8,14},{9,15},... | collective-permute-start | bytes 122888 | tf_op jit(solution)/shard_map/ppermute | solution.py:55
  14.2 9.5 %collective-permute-start.3 = (bf16[64,320]{1,0:T(8,128)(2,1)}, bf16[64,320]{1,0:T(8,128)(2,1)S(1)}, u32[]{:S(2)}, u32[]{:S(2)}) collective-permute-start(bf16[64,320]{1,0:T(8,128)(2,1)} %refs_0_.1), channel_id=1, source_target_pairs={{0,8},{1,9},{2,10},{3,11},{4,12},{5,13},{6,14},{7,15},{8,0},{9,1},... | collective-permute-start | bytes 122888 | tf_op jit(solution)/shard_map/ppermute | solution.py:55
  16.5 8.0 %collective-permute-start.4 = (bf16[64,320]{1,0:T(8,128)(2,1)}, bf16[64,320]{1,0:T(8,128)(2,1)S(1)}, u32[]{:S(2)}, u32[]{:S(2)}) collective-permute-start(bf16[64,320]{1,0:T(8,128)(2,1)} %refs_0_.1), channel_id=1, source_target_pairs={{0,10},{1,11},{2,12},{3,13},{4,14},{5,15},{6,0},{7,1},{8,2},{9,3},... | collective-permute-start | bytes 122888 | tf_op jit(solution)/shard_map/ppermute | solution.py:55
  18.0 6.6 %collective-permute-start.5 = (bf16[64,320]{1,0:T(8,128)(2,1)}, bf16[64,320]{1,0:T(8,128)(2,1)S(1)}, u32[]{:S(2)}, u32[]{:S(2)}) collective-permute-start(bf16[64,320]{1,0:T(8,128)(2,1)} %refs_0_.1), channel_id=1, source_target_pairs={{0,12},{1,13},{2,14},{3,15},{4,0},{5,1},{6,2},{7,3},{8,4},{9,5},{1... | collective-permute-start | bytes 122888 | tf_op jit(solution)/shard_map/ppermute | solution.py:55
  19.4 5.6 %collective-permute-start.6 = (bf16[64,320]{1,0:T(8,128)(2,1)}, bf16[64,320]{1,0:T(8,128)(2,1)S(1)}, u32[]{:S(2)}, u32[]{:S(2)}) collective-permute-start(bf16[64,320]{1,0:T(8,128)(2,1)} %refs_0_.1), channel_id=1, source_target_pairs={{0,14},{1,15},{2,0},{3,1},{4,2},{5,3},{6,4},{7,5},{8,6},{9,7},{10,... | collective-permute-start | bytes 122888 | tf_op jit(solution)/shard_map/ppermute | solution.py:55
  23.5 7.0 %collective-permute-start = (bf16[64,320]{1,0:T(8,128)(2,1)}, bf16[64,320]{1,0:T(8,128)(2,1)S(1)}, u32[]{:S(2)}, u32[]{:S(2)}) collective-permute-start(bf16[64,320]{1,0:T(8,128)(2,1)} %refs_0_.1), channel_id=1, source_target_pairs={{0,2},{1,3},{2,4},{3,5},{4,6},{5,7},{6,8},{7,9},{8,10},{9,11},{10,... | collective-permute-start | bytes 122888 | tf_op jit(solution)/shard_map/ppermute | solution.py:55
  23.7 6.8 %collective-permute-start.1 = (bf16[64,320]{1,0:T(8,128)(2,1)}, bf16[64,320]{1,0:T(8,128)(2,1)S(1)}, u32[]{:S(2)}, u32[]{:S(2)}) collective-permute-start(bf16[64,320]{1,0:T(8,128)(2,1)} %refs_0_.1), channel_id=1, source_target_pairs={{0,4},{1,5},{2,6},{3,7},{4,8},{5,9},{6,10},{7,11},{8,12},{9,13},{1... | collective-permute-start | bytes 122888 | tf_op jit(solution)/shard_map/ppermute | solution.py:55
  24.6 6.4 %collective-permute-start.7 = (bf16[64,320]{1,0:T(8,128)(2,1)}, bf16[64,320]{1,0:T(8,128)(2,1)S(1)}, u32[]{:S(2)}, u32[]{:S(2)}) collective-permute-start(bf16[64,320]{1,0:T(8,128)(2,1)} %refs_0_.1), channel_id=1, source_target_pairs={{0,1},{1,0},{2,3},{3,2},{4,5},{5,4},{6,7},{7,6},{8,9},{9,8},{10,11... | collective-permute-start | bytes 122888 | tf_op jit(solution)/shard_map/ppermute | solution.py:222
  24.6 6.5 %collective-permute-start.10 = (bf16[64,320]{1,0:T(8,128)(2,1)S(1)}, bf16[64,320]{1,0:T(8,128)(2,1)S(1)}, u32[]{:S(2)}, u32[]{:S(2)}) collective-permute-start(bf16[64,320]{1,0:T(8,128)(2,1)S(1)} %collective-permute-done.2.refs_3_), channel_id=1, source_target_pairs={{0,1},{1,0},{2,3},{3,2},{4,5},{5,4},{6,7},{7,6},{8,9},{9,8},{10,11... | collective-permute-start | bytes 122888 | tf_op jit(solution)/shard_map/ppermute | solution.py:222
  25.1 6.4 %collective-permute-start.11 = (bf16[64,320]{1,0:T(8,128)(2,1)S(1)}, bf16[64,320]{1,0:T(8,128)(2,1)S(1)}, u32[]{:S(2)}, u32[]{:S(2)}) collective-permute-start(bf16[64,320]{1,0:T(8,128)(2,1)S(1)} %collective-permute-done.3.refs_4_), channel_id=1, source_target_pairs={{0,1},{1,0},{2,3},{3,2},{4,5},{5,4},{6,7},{7,6},{8,9},{9,8},{10,11... | collective-permute-start | bytes 122888 | tf_op jit(solution)/shard_map/ppermute | solution.py:222
  30.5 1.9 %collective-permute-start.12 = (bf16[64,320]{1,0:T(8,128)(2,1)S(1)}, bf16[64,320]{1,0:T(8,128)(2,1)S(1)}, u32[]{:S(2)}, u32[]{:S(2)}) collective-permute-start(bf16[64,320]{1,0:T(8,128)(2,1)S(1)} %collective-permute-done.4.refs_5_), channel_id=1, source_target_pairs={{0,1},{1,0},{2,3},{3,2},{4,5},{5,4},{6,7},{7,6},{8,9},{9,8},{10,11... | collective-permute-start | bytes 122888 | tf_op jit(solution)/shard_map/ppermute | solution.py:222
  30.5 1.9 %collective-permute-start.13 = (bf16[64,320]{1,0:T(8,128)(2,1)S(1)}, bf16[64,320]{1,0:T(8,128)(2,1)S(1)}, u32[]{:S(2)}, u32[]{:S(2)}) collective-permute-start(bf16[64,320]{1,0:T(8,128)(2,1)S(1)} %collective-permute-done.5.refs_6_), channel_id=1, source_target_pairs={{0,1},{1,0},{2,3},{3,2},{4,5},{5,4},{6,7},{7,6},{8,9},{9,8},{10,11... | collective-permute-start | bytes 122888 | tf_op jit(solution)/shard_map/ppermute | solution.py:222
  45.7 3.7 %collective-permute-start.16 = (f32[8,64]{1,0:T(8,128)S(1)}, f32[8,64]{1,0:T(8,128)S(1)}, u32[]{:S(2)}, u32[]{:S(2)}) collective-permute-start(f32[8,64]{1,0:T(8,128)S(1)} %concatenate.12), channel_id=1, source_target_pairs={{0,2},{1,3},{2,0},{3,1},{4,6},{5,7},{6,4},{7,5},{8,10},{9,11},{10,... | collective-permute-start | bytes 6152 | tf_op jit(solution)/shard_map/ppermute | solution.py:63
  49.5 3.7 %collective-permute-start.17 = (f32[8,64]{1,0:T(8,128)S(1)}, f32[8,64]{1,0:T(8,128)S(1)}, u32[]{:S(2)}, u32[]{:S(2)}) collective-permute-start(f32[8,64]{1,0:T(8,128)S(1)} %concatenate.13), channel_id=1, source_target_pairs={{0,4},{1,5},{2,6},{3,7},{4,0},{5,1},{6,2},{7,3},{8,12},{9,13},{10,... | collective-permute-start | bytes 6152 | tf_op jit(solution)/shard_map/ppermute | solution.py:63
  53.2 4.6 %collective-permute-start.18 = (f32[8,64]{1,0:T(8,128)S(1)}, f32[8,64]{1,0:T(8,128)S(1)}, u32[]{:S(2)}, u32[]{:S(2)}) collective-permute-start(f32[8,64]{1,0:T(8,128)S(1)} %concatenate.14), channel_id=1, source_target_pairs={{0,8},{1,9},{2,10},{3,11},{4,12},{5,13},{6,14},{7,15},{8,0},{9,1},... | collective-permute-start | bytes 6152 | tf_op jit(solution)/shard_map/ppermute | solution.py:63
  67.6 1.8 %collective-permute-start.19 = (bf16[8,64,320]{2,1,0:T(8,128)(2,1)S(1)}, bf16[8,64,320]{2,1,0:T(8,128)(2,1)S(1)}, u32[]{:S(2)}, u32[]{:S(2)}) collective-permute-start(bf16[8,64,320]{2,1,0:T(8,128)(2,1)S(1)} %get-tuple-element.12), channel_id=1, source_target_pairs={{0,1},{1,0},{2,3},{3,2},{4,5},{5,4},{6,7},{7,6},{8,9},{9,8},{10,11... | collective-permute-start | bytes 983048 | tf_op jit(solution)/shard_map/ppermute | solution.py:255
  69.5 7.4 %collective-permute-start.20 = (bf16[64,320]{1,0:T(8,128)(2,1)S(1)}, bf16[64,320]{1,0:T(8,128)(2,1)S(1)}, u32[]{:S(2)}, u32[]{:S(2)}) collective-permute-start(bf16[64,320]{1,0:T(8,128)(2,1)S(1)} %get-tuple-element.36), channel_id=1, source_target_pairs={{0,2},{1,3},{2,4},{3,5},{4,6},{5,7},{6,8},{7,9},{8,10},{9,11},{10,... | collective-permute-start | bytes 122888 | tf_op jit(solution)/shard_map/ppermute | solution.py:259
  70.3 8.2 %collective-permute-start.21 = (bf16[64,320]{1,0:T(8,128)(2,1)S(1)}, bf16[64,320]{1,0:T(8,128)(2,1)S(1)}, u32[]{:S(2)}, u32[]{:S(2)}) collective-permute-start(bf16[64,320]{1,0:T(8,128)(2,1)S(1)} %get-tuple-element.42), channel_id=1, source_target_pairs={{0,4},{1,5},{2,6},{3,7},{4,8},{5,9},{6,10},{7,11},{8,12},{9,13},{1... | collective-permute-start | bytes 122888 | tf_op jit(solution)/shard_map/ppermute | solution.py:259
  70.3 9.8 %collective-permute-start.22 = (bf16[64,320]{1,0:T(8,128)(2,1)S(1)}, bf16[64,320]{1,0:T(8,128)(2,1)S(1)}, u32[]{:S(2)}, u32[]{:S(2)}) collective-permute-start(bf16[64,320]{1,0:T(8,128)(2,1)S(1)} %get-tuple-element.41), channel_id=1, source_target_pairs={{0,6},{1,7},{2,8},{3,9},{4,10},{5,11},{6,12},{7,13},{8,14},{9,15},... | collective-permute-start | bytes 122888 | tf_op jit(solution)/shard_map/ppermute | solution.py:259
  73.0 7.1 %collective-permute-start.23 = (bf16[64,320]{1,0:T(8,128)(2,1)S(1)}, bf16[64,320]{1,0:T(8,128)(2,1)S(1)}, u32[]{:S(2)}, u32[]{:S(2)}) collective-permute-start(bf16[64,320]{1,0:T(8,128)(2,1)S(1)} %get-tuple-element.40), channel_id=1, source_target_pairs={{0,8},{1,9},{2,10},{3,11},{4,12},{5,13},{6,14},{7,15},{8,0},{9,1},... | collective-permute-start | bytes 122888 | tf_op jit(solution)/shard_map/ppermute | solution.py:259
  74.9 6.7 %collective-permute-start.24 = (bf16[64,320]{1,0:T(8,128)(2,1)S(1)}, bf16[64,320]{1,0:T(8,128)(2,1)S(1)}, u32[]{:S(2)}, u32[]{:S(2)}) collective-permute-start(bf16[64,320]{1,0:T(8,128)(2,1)S(1)} %get-tuple-element.39), channel_id=1, source_target_pairs={{0,10},{1,11},{2,12},{3,13},{4,14},{5,15},{6,0},{7,1},{8,2},{9,3},... | collective-permute-start | bytes 122888 | tf_op jit(solution)/shard_map/ppermute | solution.py:259
  77.0 4.7 %collective-permute-start.25 = (bf16[64,320]{1,0:T(8,128)(2,1)S(1)}, bf16[64,320]{1,0:T(8,128)(2,1)S(1)}, u32[]{:S(2)}, u32[]{:S(2)}) collective-permute-start(bf16[64,320]{1,0:T(8,128)(2,1)S(1)} %get-tuple-element.38), channel_id=1, source_target_pairs={{0,12},{1,13},{2,14},{3,15},{4,0},{5,1},{6,2},{7,3},{8,4},{9,5},{1... | collective-permute-start | bytes 122888 | tf_op jit(solution)/shard_map/ppermute | solution.py:259
  78.6 4.1 %collective-permute-start.26 = (bf16[64,320]{1,0:T(8,128)(2,1)S(1)}, bf16[64,320]{1,0:T(8,128)(2,1)S(1)}, u32[]{:S(2)}, u32[]{:S(2)}) collective-permute-start(bf16[64,320]{1,0:T(8,128)(2,1)S(1)} %get-tuple-element.37), channel_id=1, source_target_pairs={{0,14},{1,15},{2,0},{3,1},{4,2},{5,3},{6,4},{7,5},{8,6},{9,7},{10,... | collective-permute-start | bytes 122888 | tf_op jit(solution)/shard_map/ppermute | solution.py:259
  (9 other events, 73.0 us)

commit v3 on v1

--- a/solution.py
+++ b/solution.py
@@ -1,9 +1,15 @@
+import functools
+
 import jax
 import jax.numpy as jnp
 from jax import lax
+from jax.experimental import pallas as pl
+from jax.experimental.pallas import tpu as pltpu
 from jax.sharding import PartitionSpec as P
 
 BLOCK = 32
+LANES = 128
+STATS = 8
 
 
 sample_weight = 0.5
@@ -12,6 +18,300 @@
 def to_all(piece, count):
     copies = jnp.broadcast_to(piece[None], (count,) + piece.shape)
     return lax.all_to_all(copies, "vocab", split_axis=0, concat_axis=0, tiled=True)
+
+
+def scaled_teacher(teacher_values, teacher_scales, count, shard_rows):
+    slot_rows = teacher_values.shape[0]
+    scaled = (
+        teacher_values.astype(jnp.float32).reshape(slot_rows, -1, BLOCK) * teacher_scales[:, :, None]
+    ).astype(jnp.bfloat16)
+    scaled = scaled.reshape(slot_rows, count, shard_rows).transpose(1, 0, 2)
+    arrived = lax.all_to_all(scaled, "vocab", split_axis=0, concat_axis=0, tiled=True)
+    return arrived.reshape(count * slot_rows, shard_rows)
+
+
+def merge_stats(tops, sums, teacher_tops, teacher_sums, crosses):
+    top = jnp.max(tops, axis=0)
+    teacher_top = jnp.max(teacher_tops, axis=0)
+    shift = tops - top[None]
+    teacher_shift = teacher_tops - teacher_top[None]
+    weight = jnp.exp(shift)
+    total = jnp.sum(sums * weight, axis=0)
+    teacher_total = jnp.sum(teacher_sums * jnp.exp(teacher_shift), axis=0)
+    cross = jnp.sum(weight * (crosses + sums * (shift - teacher_shift)), axis=0)
+    return top, total, teacher_top, teacher_total, cross
+
+
+def swap_cores(array):
+    count = lax.axis_size("vocab")
+    return lax.ppermute(array, "vocab", [(i, i ^ 1) for i in range(count)])
+
+
+def across_chips(blocks):
+    count = lax.axis_size("vocab")
+    groups = [list(range(core, count, 2)) for core in range(2)]
+    return lax.all_to_all(
+        blocks, "vocab", split_axis=0, concat_axis=0, axis_index_groups=groups, tiled=True
+    )
+
+
+def vmem_array(shape, dtype):
+    return pltpu.VMEM(shape, dtype)
+
+
+def in_vmem(array):
+    return pltpu.with_memory_space_constraint(array, pltpu.VMEM)
+
+
+def in_hbm(array):
+    return pltpu.with_memory_space_constraint(array, pltpu.HBM)
+
+
+def column_of(row):
+    size = row.shape[1]
+    down = lax.broadcasted_iota(jnp.int32, (size, size), 0)
+    along = lax.broadcasted_iota(jnp.int32, (size, size), 1)
+    return jnp.sum(jnp.where(down == along, row, jnp.zeros_like(row)), axis=1, keepdims=True)
+
+
+def prepare_kernel(
+    place_ref, lengths_ref, scale_ref, ids_ref, map_ref, head_ref, held_ref, owner_ref, tokens_ref, sem
+):
+    copy = pltpu.make_async_copy(head_ref, held_ref, sem)
+    copy.start()
+    tokens = map_ref.shape[1]
+    shard_rows = head_ref.shape[0]
+    token = lax.broadcasted_iota(jnp.int32, (tokens, tokens), 0)
+    slot = lax.broadcasted_iota(jnp.int32, (tokens, tokens), 1)
+    owner = (map_ref[...] == token).astype(jnp.float32)
+    named = jnp.max(owner, axis=1, keepdims=True)
+    owner = jnp.where((slot == 0) & (named == 0.0), 1.0, owner)
+    owner_ref[...] = owner.astype(jnp.bfloat16)
+
+    seqs = lengths_ref.shape[0]
+    seq_length = tokens // seqs
+    position = lax.broadcasted_iota(jnp.int32, (tokens, 1), 0)
+    live_until = jnp.zeros((tokens, 1), jnp.int32)
+    for seq in range(seqs):
+        inside = (position >= seq * seq_length) & (position < (seq + 1) * seq_length)
+        live_until = jnp.where(inside, lengths_ref[seq] + seq * seq_length, live_until)
+    live = (position < live_until).astype(jnp.float32)
+    share = live / jnp.sum(live, axis=0, keepdims=True)
+    weight = live * scale_ref[0] / jnp.sum(live, axis=0, keepdims=True)
+    entry = (column_of(ids_ref[...]) - place_ref[0] * shard_rows).astype(jnp.float32)
+    lane = lax.broadcasted_iota(jnp.int32, (tokens, LANES), 1)
+    table = jnp.where(lane == 0, entry, jnp.where(lane == 1, share, weight))
+    tokens_ref[...] = table
+    copy.wait()
+
+
+def logits_kernel(
+    place_ref,
+    own_ref,
+    other_ref,
+    head_ref,
+    arrived_ref,
+    owner_ref,
+    tokens_ref,
+    rows_ref,
+    stats_ref,
+):
+    core = place_ref[0] % 2
+    chips, tokens, half = own_ref.shape
+    shard_rows = head_ref.shape[0]
+    logits = jnp.zeros((tokens, shard_rows), jnp.float32)
+    for chip in range(chips):
+        own, other = own_ref[chip], other_ref[chip]
+        block = jnp.where(
+            core == 0,
+            jnp.concatenate([own, other], axis=1),
+            jnp.concatenate([other, own], axis=1),
+        )
+        logits += lax.dot_general(
+            block,
+            head_ref[:, 2 * half * chip : 2 * half * (chip + 1)],
+            (((1,), (1,)), ((), ())),
+            preferred_element_type=jnp.float32,
+        )
+    teacher = jnp.dot(owner_ref[...], arrived_ref[...], preferred_element_type=jnp.float32)
+
+    top = jnp.max(logits, axis=1, keepdims=True)
+    teacher_top = jnp.max(teacher, axis=1, keepdims=True)
+    off = logits - top
+    teacher_off = teacher - teacher_top
+    exps = jnp.exp(off)
+    total = jnp.sum(exps, axis=1, keepdims=True)
+    teacher_total = jnp.sum(jnp.exp(teacher_off), axis=1, keepdims=True)
+    gap = off - teacher_off
+    cross = jnp.sum(exps * gap, axis=1, keepdims=True)
+    centre = cross / total
+    entry = lax.broadcasted_iota(jnp.int32, (tokens, shard_rows), 1)
+    hit = entry == tokens_ref[:, :1].astype(jnp.int32)
+    target = jnp.sum(jnp.where(hit, logits, 0.0), axis=1, keepdims=True)
+    rows_ref[:tokens] = (exps * (gap - centre)).astype(jnp.bfloat16)
+    rows_ref[tokens : 2 * tokens] = exps.astype(jnp.bfloat16)
+    rows_ref[2 * tokens :] = hit.astype(jnp.bfloat16)
+
+    lane = lax.broadcasted_iota(jnp.int32, (tokens, LANES), 1)
+    table = jnp.zeros((tokens, LANES), jnp.float32)
+    for place, column in enumerate(
+        (top, total, teacher_top, teacher_total, cross, target, centre)
+    ):
+        table = jnp.where(lane == place, column, table)
+    stats = jnp.concatenate([table, jnp.zeros((stats_ref.shape[2] - tokens, LANES), jnp.float32)])
+    stats_ref[...] = jnp.broadcast_to(stats.T[None, :STATS], stats_ref.shape)
+
+
+def products_kernel(rows_ref, head_ref, terms_ref):
+    chips, _, width = terms_ref.shape
+
+    def multiply(chip, _):
+        columns = pl.ds(pl.multiple_of(chip * width, LANES), width)
+        terms_ref[chip] = jnp.dot(
+            rows_ref[...], head_ref[:, columns], preferred_element_type=jnp.float32
+        )
+
+    lax.fori_loop(0, chips, multiply, None)
+
+
+def combine_kernel(
+    place_ref, stats_ref, own_ref, tokens_ref, terms_ref, keep_ref, give_ref, loss_ref
+):
+    core = place_ref[0] % 2
+    chips, _, width = terms_ref.shape
+    tokens = tokens_ref.shape[0]
+    half = width // 2
+    tops, sums, teacher_tops, teacher_sums, crosses, targets = [
+        stats_ref[:, i, :tokens] for i in range(6)
+    ]
+    top, total, teacher_top, teacher_total, cross = [
+        part[None] for part in merge_stats(tops, sums, teacher_tops, teacher_sums, crosses)
+    ]
+    target = jnp.sum(targets, axis=0, keepdims=True)
+    student_log = jnp.log(total)
+    teacher_log = jnp.log(teacher_total)
+    divergence = cross / total - (student_log - teacher_log)
+    student_lse = top + student_log
+    per_token = divergence + sample_weight * (student_lse - target)
+    student_shift = own_ref[0, 0:1, :tokens] - top - student_log
+    teacher_shift = own_ref[0, 2:3, :tokens] - teacher_top - teacher_log
+    factor = jnp.exp(student_shift)
+    level = own_ref[0, 6:7, :tokens] + student_shift - teacher_shift - divergence + sample_weight
+    zeros = jnp.zeros((LANES - 3, tokens), jnp.float32)
+    columns = jnp.concatenate([factor, level, per_token, zeros], axis=0).T
+    share, weight = tokens_ref[:, 1:2], tokens_ref[:, 2:3]
+    loss_ref[...] = jnp.sum(share * columns[:, 2:3], axis=0, keepdims=True)
+    factor = weight * columns[:, 0:1]
+    level = columns[:, 1:2]
+    weight = sample_weight * weight
+    for chip in range(chips):
+        block = (
+            factor * (terms_ref[chip, :tokens] + level * terms_ref[chip, tokens : 2 * tokens])
+            - weight * terms_ref[chip, 2 * tokens :]
+        )
+        first, second = block[:, :half], block[:, half:]
+        keep_ref[chip] = jnp.where(core == 0, first, second)
+        give_ref[chip] = jnp.where(core == 0, second, first).astype(jnp.bfloat16)
+
+
+def sum_kernel(shares_ref, total_ref):
+    total = shares_ref[0].astype(jnp.float32)
+    for chip in range(1, shares_ref.shape[0]):
+        total += shares_ref[chip].astype(jnp.float32)
+    total_ref[...] = total.astype(total_ref.dtype)
+
+
+def paired_shards(
+    hidden_states, head, teacher_values, teacher_scales, token_ids, lengths, row_map, loss_scale
+):
+    count = lax.axis_size("vocab")
+    own_index = lax.axis_index("vocab")
+    chips = count // 2
+    tokens, half = hidden_states.shape
+    width = 2 * half
+    shard_rows = head.shape[0]
+    place = jnp.reshape(own_index, (1,))
+    vmem = pl.BlockSpec(memory_space=pltpu.VMEM)
+    smem = pl.BlockSpec(memory_space=pltpu.SMEM)
+    params = pltpu.CompilerParams(vmem_limit_bytes=VMEM_LIMIT)
+
+    gathered = across_chips(jnp.broadcast_to(hidden_states[None], (chips, tokens, half)))
+    other = swap_cores(gathered)
+
+    held, owner, table = pl.pallas_call(
+        prepare_kernel,
+        out_shape=(
+            vmem_array(head.shape, head.dtype),
+            vmem_array((tokens, tokens), jnp.bfloat16),
+            vmem_array((tokens, LANES), jnp.float32),
+        ),
+        in_specs=[smem] * 3 + [vmem] * 2 + [pl.BlockSpec(memory_space=pl.ANY)],
+        out_specs=[vmem] * 3,
+        scratch_shapes=[pltpu.SemaphoreType.DMA],
+        compiler_params=params,
+        cost_estimate=pl.CostEstimate(
+            flops=0, bytes_accessed=2 * head.size * 2, transcendentals=0
+        ),
+        name="prepare",
+    )(place, lengths, loss_scale, token_ids[None, :], row_map[None, :], in_hbm(head))
+
+    arrived = scaled_teacher(teacher_values, teacher_scales, count, shard_rows)
+    rows, stats = pl.pallas_call(
+        logits_kernel,
+        out_shape=(
+            vmem_array((3 * tokens, shard_rows), jnp.bfloat16),
+            vmem_array((count, STATS, pl.cdiv(tokens, LANES) * LANES), jnp.float32),
+        ),
+        in_specs=[smem] + [vmem] * 6,
+        out_specs=[vmem] * 2,
+        compiler_params=params,
+        cost_estimate=pl.CostEstimate(
+            flops=2 * tokens * head.size, bytes_accessed=2 * head.size, transcendentals=0
+        ),
+        name="logits",
+    )(place, in_vmem(gathered), in_vmem(other), in_vmem(held), in_vmem(arrived), in_vmem(owner), in_vmem(table))
+
+    all_stats = lax.all_to_all(stats, "vocab", split_axis=0, concat_axis=0, tiled=True)
+
+    terms = pl.pallas_call(
+        products_kernel,
+        out_shape=vmem_array((chips, 3 * tokens, width), jnp.float32),
+        in_specs=[vmem] * 2,
+        out_specs=vmem,
+        compiler_params=params,
+        cost_estimate=pl.CostEstimate(
+            flops=6 * tokens * head.size, bytes_accessed=2 * head.size, transcendentals=0
+        ),
+        name="products",
+    )(in_vmem(rows), in_vmem(held))
+
+    keep, give, loss = pl.pallas_call(
+        combine_kernel,
+        out_shape=(
+            vmem_array((chips, tokens, half), jnp.float32),
+            vmem_array((chips, tokens, half), jnp.bfloat16),
+            jax.ShapeDtypeStruct((1, 1), jnp.float32),
+        ),
+        in_specs=[smem] + [vmem] * 4,
+        out_specs=[vmem] * 3,
+        compiler_params=params,
+        name="combine",
+    )(place, in_vmem(all_stats), in_vmem(stats), in_vmem(table), in_vmem(terms))
+
+    sums = keep + swap_cores(give).astype(jnp.float32)
+    shares = across_chips(sums.astype(jnp.bfloat16))
+    total = pl.pallas_call(
+        sum_kernel,
+        out_shape=jax.ShapeDtypeStruct((tokens, half), jnp.bfloat16),
+        in_specs=[vmem],
+        out_specs=vmem,
+        compiler_params=params,
+        name="total",
+    )(in_vmem(shares))
+    return total, jnp.reshape(loss, (1,))
+
+
+VMEM_LIMIT = 12 * 1024 * 1024
 
 
 def shards(
@@ -23,16 +323,9 @@
     own_features = hidden_states.shape[1]
     shard_rows = head.shape[0]
     seq_length = tokens // lengths.shape[0]
-    slot_rows = teacher_values.shape[0]
     contract_last = (((1,), (1,)), ((), ()))
 
-    scaled = (
-        teacher_values.astype(jnp.float32).reshape(slot_rows, -1, BLOCK) * teacher_scales[:, :, None]
-    ).astype(jnp.bfloat16)
-    scaled = scaled.reshape(slot_rows, count, shard_rows).transpose(1, 0, 2)
-    arrived = lax.all_to_all(scaled, "vocab", split_axis=0, concat_axis=0, tiled=True)
-    arrived = arrived.reshape(tokens, shard_rows)
-
+    arrived = scaled_teacher(teacher_values, teacher_scales, count, shard_rows)
     gathered = to_all(hidden_states, count).transpose(1, 0, 2).reshape(tokens, -1)
     logits = lax.dot_general(gathered, head, contract_last, preferred_element_type=jnp.float32)
 
@@ -68,14 +361,9 @@
         count,
     )
     tops, sums, teacher_tops, teacher_sums, crosses, targets = [stats[:, i] for i in range(6)]
-    student_max = jnp.max(tops, axis=0)
-    teacher_max = jnp.max(teacher_tops, axis=0)
-    student_shift = tops - student_max[None, :]
-    teacher_shift = teacher_tops - teacher_max[None, :]
-    weight = jnp.exp(student_shift)
-    student_total = jnp.sum(sums * weight, axis=0)
-    teacher_total = jnp.sum(teacher_sums * jnp.exp(teacher_shift), axis=0)
-    cross_total = jnp.sum(weight * (crosses + sums * (student_shift - teacher_shift)), axis=0)
+    student_max, student_total, teacher_max, teacher_total, cross_total = merge_stats(
+        tops, sums, teacher_tops, teacher_sums, crosses
+    )
     student_log = jnp.log(student_total)
     teacher_log = jnp.log(teacher_total)
     student_lse = student_max + student_log
@@ -103,6 +391,13 @@
     return (grad_hidden.astype(jnp.bfloat16), loss)
 
 
+def any_shards(*arrays):
+    pair_width = 2 * arrays[0].shape[1]
+    if lax.axis_size("vocab") > 2 and pair_width % LANES == 0:
+        return paired_shards(*arrays)
+    return shards(*arrays)
+
+
 def solution(mesh):
     in_specs = (
         P("dom", "vocab"),
@@ -115,4 +410,6 @@
         P(),
     )
     out_specs = (P("dom", "vocab"), P("dom"))
-    return jax.shard_map(shards, mesh=mesh, in_specs=in_specs, out_specs=out_specs, check_vma=False)
+    return jax.shard_map(
+        any_shards, mesh=mesh, in_specs=in_specs, out_specs=out_specs, check_vma=False
+    )

time: 103 us -> 89.9 us (0.87)
  waiting for transfers between devices: 47.8 us -> 10.5 us
  blocking collectives: 0 us -> 18 us
  Pallas kernels: 0 us -> 17.1 us
  matrix products: 15.5 us -> 0 us
  local copies, waits for them, and re-layouts: 9.91 us -> 24.4 us
  other arithmetic: 4.93 us -> 0.14 us
  between operations: 3.93 us -> 1.41 us
  starting transfers between devices: 20 us -> 17.6 us
    all_to_all x4 -> x3, waiting for transfers between devices: 47.8 us -> 9.18 us  [the longest x1 9.18 us: across_chips(): lax.all_to_all(blocks, 'vocab', split_axis=0, concat_axis=0, axis_index_g...]
    unnamed x4 -> x16, local copies, waits for them, and re-layouts: 0.79 us -> 19.5 us
    all_to_all x0 -> x1, blocking collectives: none -> 18 us  [across_chips(): lax.all_to_all(blocks, 'vocab', split_axis=0, concat_axis=0, axis_index_g...]
    pallas_call x0 -> x5, Pallas kernels: none -> 17.1 us  [the longest x1 5.09 us: paired_shards(): pl.pallas_call(prepare_kernel, out_shape=(vmem_array(head.shape, head.dty...]
    dot_general x2 -> x0, matrix products: 15.5 us -> none  [the longest x1 8.45 us: shards(): lax.dot_general(gathered, head, contract_last, preferred_element_type=jnp...]
    all_to_all x4 -> x3, starting transfers between devices: 20 us -> 17.1 us  [the longest x1 7.28 us: across_chips(): lax.all_to_all(blocks, 'vocab', split_axis=0, concat_axis=0, axis_index_g...]
    reduce_sum x7 -> x0, other arithmetic: 2.61 us -> none  [the longest x1 0.76 us: shards(): slot_of = jnp.sum(jnp.where(owner, positions[None, :], 0), axis=1)]
    reshape x5 -> x2, local copies, waits for them, and re-layouts: 3.44 us -> 1.13 us  [the longest x1 1.08 us: scaled_teacher(): teacher_values.astype(jnp.float32).reshape(slot_rows, -1, BLOCK)]
  transfers between devices with their start and end apart: 4 -> 5, of which waited for: 4 -> 2; matrix products, arithmetic and copies ran while one was open for 2% -> 4% of each run, Pallas kernels for 0% -> 11%
where the time goes in v3:
time: 89.9 us; the launch traced here: 89.1 us
  local copies, waits for them, and re-layouts  24.4 us (27%)
  blocking collectives  18 us (20%)
  starting transfers between devices  17.6 us (20%)
  Pallas kernels  17.1 us (19%)
  waiting for transfers between devices  10.5 us (12%)
  between operations  1.41 us (2%)
    unnamed x16, local copies, waits for them, and re-layouts  19.5 us
    all_to_all x1, blocking collectives, across_chips(): lax.all_to_all(blocks, 'vocab', split_axis=0, concat_axis=0, axis_index_g...  18 us
    all_to_all x1, waiting for transfers between devices, across_chips(): lax.all_to_all(blocks, 'vocab', split_axis=0, concat_axis=0, axis_index_g...  9.18 us
    all_to_all x1, starting transfers between devices, across_chips(): lax.all_to_all(blocks, 'vocab', split_axis=0, concat_axis=0, axis_index_g...  7.28 us
    all_to_all x1, starting transfers between devices, paired_shards(): lax.all_to_all(stats, 'vocab', split_axis=0, concat_axis=0, tiled=True)  6.02 us
    pallas_call x1, Pallas kernels, paired_shards(): pl.pallas_call(prepare_kernel, out_shape=(vmem_array(head.shape, head.dty...  5.09 us
    pallas_call x1, Pallas kernels, paired_shards(): pl.pallas_call(logits_kernel, out_shape=(vmem_array((3 * tokens, shard_ro...  4.91 us
    pallas_call x1, Pallas kernels, paired_shards(): pl.pallas_call(products_kernel, out_shape=vmem_array((chips, 3 * tokens,...  4.58 us
  transfers between devices with their start and end apart: 5, of which 2 were waited for; matrix products, arithmetic and copies ran while one was open for 4% of the time, Pallas kernels for 11%

profile of v3, /device:TPU:0, one launch (start us, length us, event | category | flops | bytes accessed | tf_op | source)
XLA Modules:
  0.0 89.1 jit_solution(15362940720781407101)
XLA Ops:
  0.6 1.6 %broadcast_in_dim.6 = bf16[8,64,320]{2,1,0:T(8,128)(2,1)} broadcast(bf16[64,320]{1,0:T(8,128)(2,1)} %param.8), dimensions={1,2} | broadcast | bytes 368640 | tf_op jit(solution)/shard_map/broadcast_in_dim | solution.py:238
  2.2 7.3 %all-to-all-start = ((bf16[8,64,320]{2,1,0:T(8,128)(2,1)}), bf16[8,64,320]{2,1,0:T(8,128)(2,1)S(1)}, u32[]{:S(2)}, u32[]{:S(2)}) async-start(bf16[8,64,320]{2,1,0:T(8,128)(2,1)} %broadcast_in_dim.6), calls=%async_computation | async-start | bytes 786432 | tf_op jit(solution)/shard_map/all_to_all | solution.py:53
  9.5 1.1 %reshape.30 = f32[4,16,1216]{2,1,0:T(8,128)S(1)} reshape(bf16[4,19456]{1,0:T(4,128)(2,1)} %param.10) | data formatting | bytes 466944 | tf_op jit(solution)/shard_map/reshape | solution.py:26
  10.6 1.1 %mul.11 = f32[4,608,32]{2,1,0:T(8,128)S(1)} broadcast(f32[4,608]{1,0:T(4,128)} %param.11), dimensions={0,1} | broadcast | bytes 321024 | tf_op jit(solution)/shard_map/mul | solution.py:26
  12.0 9.2 %all-to-all-done.own_ref = bf16[8,64,320]{2,1,0:T(8,128)(2,1)S(1)} async-done(((bf16[8,64,320]{2,1,0:T(8,128)(2,1)}), bf16[8,64,320]{2,1,0:T(8,128)(2,1)S(1)}, u32[]{:S(2)}, u32[]{:S(2)}) %all-to-all-start) | async-done | bytes 327712 | tf_op jit(solution)/shard_map/all_to_all | solution.py:53
  21.2 0.8 copy.12
  22.0 3.8 %all-to-all-start.1 = ((bf16[16,4,1216]{2,1,0:T(4,128)(2,1)}), bf16[16,4,1216]{2,1,0:T(4,128)(2,1)S(1)}, u32[]{:S(2)}, u32[]{:S(2)}) async-start(bf16[16,4,1216]{2,1,0:T(4,128)(2,1)} %copy.12), calls=%async_computation.1 | async-start | bytes 327680 | tf_op jit(solution)/shard_map/all_to_all | solution.py:29
  26.5 0.6 copy-done.5
  27.1 0.7 copy-done.6
  27.8 0.7 copy-done.7
  28.4 5.1 %prepare.1 = (bf16[1216,5120]{1,0:T(8,128)(2,1)S(1)}, bf16[64,64]{1,0:T(8,128)(2,1)S(1)}, f32[64,128]{1,0:T(8,128)S(1)}) custom-call(s32[1]{0:T(128)} %bitcast.place_ref, s32[2]{0:T(128)S(1)} %copy-done.5, f32[1]{0:T(128)S(6)} %copy.13.scale_ref, s32[1,64]{1,0:T(1,128)S(1)} %bitcast.6, s32[1,64]{1,0:T(1,128)S(1)} %bitcast.7, bf16[1216,5120]{1,0:T(8,128)(2,1)} %head_ref.1), custom_call_target="tpu_custom_call" | custom-call | bytes 24903680 | tf_op jit(solution)/shard_map/prepare/pallas_call | solution.py:241
  33.6 4.5 %copy-done = bf16[1216,5120]{1,0:T(8,128)(2,1)} copy-done((bf16[1216,5120]{1,0:T(8,128)(2,1)}, bf16[1216,5120]{1,0:T(8,128)(2,1)S(1)}, u32[]{:S(2)}) %copy-start) | copy-done | bytes 12451864
  38.1 4.5 %copy-done.1 = bf16[1216,5120]{1,0:T(8,128)(2,1)S(1)} copy-done((bf16[1216,5120]{1,0:T(8,128)(2,1)S(1)}, bf16[1216,5120]{1,0:T(8,128)(2,1)}, u32[]{:S(2)}) %copy-start.1) | copy-done | bytes 12451864
  42.6 4.9 %logits.1 = (bf16[192,1216]{1,0:T(8,128)(2,1)S(1)}, f32[16,8,128]{2,1,0:T(8,128)}) custom-call(s32[1]{0:T(128)} %bitcast.place_ref, bf16[8,64,320]{2,1,0:T(8,128)(2,1)S(1)} %all-to-all-done.own_ref, bf16[8,64,320]{2,1,0:T(8,128)(2,1)S(1)} %collective-permute-done.other_ref, bf16[1216,5120]{1,0:T(8,128)(2,1)S(1)} %copy-done.1, ...), custom_call_target="tpu_custom_call" | custom-call | flops 796917760 | bytes 12451840 | tf_op jit(solution)/shard_map/logits/pallas_call | solution.py:259
  47.6 6.0 %all-to-all-start.2 = ((f32[16,8,128]{2,1,0:T(8,128)}), f32[16,8,128]{2,1,0:T(8,128)S(1)}, u32[]{:S(2)}, u32[]{:S(2)}) async-start(f32[16,8,128]{2,1,0:T(8,128)} %get-tuple-element.13.own_ref), calls=%async_computation.2 | async-start | bytes 131072 | tf_op jit(solution)/shard_map/all_to_all | solution.py:274
  53.6 4.5 %copy-done.2 = bf16[1216,5120]{1,0:T(8,128)(2,1)S(1)} copy-done((bf16[1216,5120]{1,0:T(8,128)(2,1)S(1)}, bf16[1216,5120]{1,0:T(8,128)(2,1)}, u32[]{:S(2)}) %copy-start.2) | copy-done | bytes 12451864
  58.1 4.6 %products.1.terms_ref = f32[8,192,640]{2,1,0:T(8,128)S(1)} custom-call(bf16[192,1216]{1,0:T(8,128)(2,1)S(1)} %get-tuple-element.14.rows_ref, bf16[1216,5120]{1,0:T(8,128)(2,1)S(1)} %copy-done.2), custom_call_target="tpu_custom_call" | custom-call | flops 2390753280 | bytes 12451840 | tf_op jit(solution)/shard_map/products/pallas_call | solution.py:276
  62.7 1.8 %copy-done.3 = f32[8,192,640]{2,1,0:T(8,128)} copy-done((f32[8,192,640]{2,1,0:T(8,128)}, f32[8,192,640]{2,1,0:T(8,128)S(1)}, u32[]{:S(2)}) %copy-start.3) | copy-done | bytes 3932184
  64.6 2.1 %copy-done.4 = f32[8,192,640]{2,1,0:T(8,128)S(1)} copy-done((f32[8,192,640]{2,1,0:T(8,128)S(1)}, f32[8,192,640]{2,1,0:T(8,128)}, u32[]{:S(2)}) %copy-start.4) | copy-done | bytes 3932184
  66.7 1.8 %combine.1 = (f32[8,64,320]{2,1,0:T(8,128)S(1)}, bf16[8,64,320]{2,1,0:T(8,128)(2,1)S(1)}, f32[1,1]{1,0:T(1,128)}) custom-call(s32[1]{0:T(128)} %bitcast.place_ref, f32[16,8,128]{2,1,0:T(8,128)S(1)} %all-to-all-done.2.stats_ref, f32[16,8,128]{2,1,0:T(8,128)} %get-tuple-element.13.own_ref, f32[64,128]{1,0:T(8,128)S(1)} %get-tuple-element.12.tokens_ref, ...), custom_call_target="tpu_custom_call" | custom-call | tf_op jit(solution)/shard_map/combine/pallas_call | solution.py:288
  68.5 0.4 collective-permute-start.1
  68.9 1.3 %collective-permute-done.1 = bf16[8,64,320]{2,1,0:T(8,128)(2,1)S(1)} collective-permute-done((bf16[8,64,320]{2,1,0:T(8,128)(2,1)S(1)}, bf16[8,64,320]{2,1,0:T(8,128)(2,1)S(1)}, u32[]{:S(2)}, u32[]{:S(2)}) %collective-permute-start.1) | collective-permute-done | bytes 327712 | tf_op jit(solution)/shard_map/ppermute | solution.py:47
  70.4 18.0 %all_to_all.20.shares_ref = bf16[8,64,320]{2,1,0:T(8,128)(2,1)S(1)} all-to-all(bf16[8,64,320]{2,1,0:T(8,128)(2,1)S(1)} %add_convert_fusion), channel_id=1, replica_groups={{0,2,4,6,8,10,12,14},{1,3,5,7,9,11,13,15},{16,18,20,22,24,26,28,30},{17..., dimensions={0} | all-to-all | bytes 655360 | tf_op jit(solution)/shard_map/all_to_all | solution.py:53
  88.5 0.7 total.1
  (16 shorter events, 0.6 us)
Async XLA Ops:
  2.2 19.0 %all-to-all-start = ((bf16[8,64,320]{2,1,0:T(8,128)(2,1)}), bf16[8,64,320]{2,1,0:T(8,128)(2,1)S(1)}, u32[]{:S(2)}, u32[]{:S(2)}) async-start(bf16[8,64,320]{2,1,0:T(8,128)(2,1)} %broadcast_in_dim.6), calls=%async_computation | async-start | bytes 786432 | tf_op jit(solution)/shard_map/all_to_all | solution.py:53
  21.2 16.9 %collective-permute-start = (bf16[8,64,320]{2,1,0:T(8,128)(2,1)S(1)}, bf16[8,64,320]{2,1,0:T(8,128)(2,1)S(1)}, u32[]{:S(2)}, u32[]{:S(2)}) collective-permute-start(bf16[8,64,320]{2,1,0:T(8,128)(2,1)S(1)} %all-to-all-done.own_ref), channel_id=1, source_target_pairs={{0,1},{1,0},{2,3},{3,2},{4,5},{5,4},{6,7},{7,6},{8,9},{9,8},{10,11... | collective-permute-start | bytes 983048 | tf_op jit(solution)/shard_map/ppermute | solution.py:47
  22.0 16.1 %all-to-all-start.1 = ((bf16[16,4,1216]{2,1,0:T(4,128)(2,1)}), bf16[16,4,1216]{2,1,0:T(4,128)(2,1)S(1)}, u32[]{:S(2)}, u32[]{:S(2)}) async-start(bf16[16,4,1216]{2,1,0:T(4,128)(2,1)} %copy.12), calls=%async_computation.1 | async-start | bytes 327680 | tf_op jit(solution)/shard_map/all_to_all | solution.py:29
  26.5 0.7 copy-start.5
  27.1 0.7 copy-start.6
  27.8 0.7 copy-start.7
  33.5 4.5 %copy-start = (bf16[1216,5120]{1,0:T(8,128)(2,1)}, bf16[1216,5120]{1,0:T(8,128)(2,1)S(1)}, u32[]{:S(2)}) copy-start(bf16[1216,5120]{1,0:T(8,128)(2,1)S(1)} %get-tuple-element.10.head_ref) | copy-start | bytes 37355524
  38.1 4.5 %copy-start.1 = (bf16[1216,5120]{1,0:T(8,128)(2,1)S(1)}, bf16[1216,5120]{1,0:T(8,128)(2,1)}, u32[]{:S(2)}) copy-start(bf16[1216,5120]{1,0:T(8,128)(2,1)} %copy-done) | copy-start | bytes 37355524
  47.6 17.0 %all-to-all-start.2 = ((f32[16,8,128]{2,1,0:T(8,128)}), f32[16,8,128]{2,1,0:T(8,128)S(1)}, u32[]{:S(2)}, u32[]{:S(2)}) async-start(f32[16,8,128]{2,1,0:T(8,128)} %get-tuple-element.13.own_ref), calls=%async_computation.2 | async-start | bytes 131072 | tf_op jit(solution)/shard_map/all_to_all | solution.py:274
  53.6 4.5 %copy-start.2 = (bf16[1216,5120]{1,0:T(8,128)(2,1)S(1)}, bf16[1216,5120]{1,0:T(8,128)(2,1)}, u32[]{:S(2)}) copy-start(bf16[1216,5120]{1,0:T(8,128)(2,1)} %copy-done) | copy-start | bytes 37355524
  62.7 1.9 %copy-start.3 = (f32[8,192,640]{2,1,0:T(8,128)}, f32[8,192,640]{2,1,0:T(8,128)S(1)}, u32[]{:S(2)}) copy-start(f32[8,192,640]{2,1,0:T(8,128)S(1)} %products.1.terms_ref) | copy-start | bytes 11796484
  64.6 2.1 %copy-start.4 = (f32[8,192,640]{2,1,0:T(8,128)S(1)}, f32[8,192,640]{2,1,0:T(8,128)}, u32[]{:S(2)}) copy-start(f32[8,192,640]{2,1,0:T(8,128)} %copy-done.3) | copy-start | bytes 11796484
  68.5 1.8 %collective-permute-start.1 = (bf16[8,64,320]{2,1,0:T(8,128)(2,1)S(1)}, bf16[8,64,320]{2,1,0:T(8,128)(2,1)S(1)}, u32[]{:S(2)}, u32[]{:S(2)}) collective-permute-start(bf16[8,64,320]{2,1,0:T(8,128)(2,1)S(1)} %get-tuple-element.16), channel_id=1, source_target_pairs={{0,1},{1,0},{2,3},{3,2},{4,5},{5,4},{6,7},{7,6},{8,9},{9,8},{10,11... | collective-permute-start | bytes 983048 | tf_op jit(solution)/shard_map/ppermute | solution.py:47

commit v4 on v3

--- a/solution.py
+++ b/solution.py
@@ -25,9 +25,7 @@
     scaled = (
         teacher_values.astype(jnp.float32).reshape(slot_rows, -1, BLOCK) * teacher_scales[:, :, None]
     ).astype(jnp.bfloat16)
-    scaled = scaled.reshape(slot_rows, count, shard_rows).transpose(1, 0, 2)
-    arrived = lax.all_to_all(scaled, "vocab", split_axis=0, concat_axis=0, tiled=True)
-    return arrived.reshape(count * slot_rows, shard_rows)
+    return scaled.reshape(slot_rows, count, shard_rows).transpose(1, 0, 2)
 
 
 def merge_stats(tops, sums, teacher_tops, teacher_sums, crosses):
@@ -47,12 +45,9 @@
     return lax.ppermute(array, "vocab", [(i, i ^ 1) for i in range(count)])
 
 
-def across_chips(blocks):
+def across_chips(array, step):
     count = lax.axis_size("vocab")
-    groups = [list(range(core, count, 2)) for core in range(2)]
-    return lax.all_to_all(
-        blocks, "vocab", split_axis=0, concat_axis=0, axis_index_groups=groups, tiled=True
-    )
+    return lax.ppermute(array, "vocab", [(i, i ^ (2 * step)) for i in range(count)])
 
 
 def vmem_array(shape, dtype):
@@ -75,12 +70,9 @@
 
 
 def prepare_kernel(
-    place_ref, lengths_ref, scale_ref, ids_ref, map_ref, head_ref, held_ref, owner_ref, tokens_ref, sem
+    place_ref, lengths_ref, scale_ref, ids_ref, map_ref, owner_ref, tokens_ref, *, shard_rows
 ):
-    copy = pltpu.make_async_copy(head_ref, held_ref, sem)
-    copy.start()
     tokens = map_ref.shape[1]
-    shard_rows = head_ref.shape[0]
     token = lax.broadcasted_iota(jnp.int32, (tokens, tokens), 0)
     slot = lax.broadcasted_iota(jnp.int32, (tokens, tokens), 1)
     owner = (map_ref[...] == token).astype(jnp.float32)
@@ -100,41 +92,47 @@
     weight = live * scale_ref[0] / jnp.sum(live, axis=0, keepdims=True)
     entry = (column_of(ids_ref[...]) - place_ref[0] * shard_rows).astype(jnp.float32)
     lane = lax.broadcasted_iota(jnp.int32, (tokens, LANES), 1)
-    table = jnp.where(lane == 0, entry, jnp.where(lane == 1, share, weight))
-    tokens_ref[...] = table
-    copy.wait()
-
-
-def logits_kernel(
-    place_ref,
-    own_ref,
-    other_ref,
-    head_ref,
-    arrived_ref,
-    owner_ref,
-    tokens_ref,
-    rows_ref,
-    stats_ref,
-):
+    tokens_ref[...] = jnp.where(lane == 0, entry, jnp.where(lane == 1, share, weight))
+
+
+def head_copies(place_ref, head_ref, held_ref, sems):
+    chips, _, width = held_ref.shape
+    chip = place_ref[0] // 2
+    copies = []
+    for step in range(chips):
+        columns = pl.ds(pl.multiple_of(jnp.bitwise_xor(chip, step) * width, LANES), width)
+        copies.append(
+            pltpu.make_async_copy(head_ref.at[:, columns], held_ref.at[step], sems.at[step])
+        )
+    return copies
+
+
+def logits_kernel(place_ref, *refs, chips):
+    near, far = refs[:chips], refs[chips : 2 * chips]
+    head_ref, logits_ref, held_ref, sems = refs[2 * chips :]
+    copies = head_copies(place_ref, head_ref, held_ref, sems)
+    for copy in copies:
+        copy.start()
     core = place_ref[0] % 2
-    chips, tokens, half = own_ref.shape
-    shard_rows = head_ref.shape[0]
-    logits = jnp.zeros((tokens, shard_rows), jnp.float32)
-    for chip in range(chips):
-        own, other = own_ref[chip], other_ref[chip]
+    logits = jnp.zeros(logits_ref.shape, jnp.float32)
+    for step in range(chips):
+        own, other = near[step][...], far[step][...]
         block = jnp.where(
             core == 0,
             jnp.concatenate([own, other], axis=1),
             jnp.concatenate([other, own], axis=1),
         )
+        copies[step].wait()
         logits += lax.dot_general(
-            block,
-            head_ref[:, 2 * half * chip : 2 * half * (chip + 1)],
-            (((1,), (1,)), ((), ())),
-            preferred_element_type=jnp.float32,
+            block, held_ref[step], (((1,), (1,)), ((), ())), preferred_element_type=jnp.float32
         )
+    logits_ref[...] = logits
+
+
+def softmax_kernel(logits_ref, arrived_ref, owner_ref, tokens_ref, rows_ref, stats_ref):
+    tokens, shard_rows = logits_ref.shape
+    logits = logits_ref[...]
     teacher = jnp.dot(owner_ref[...], arrived_ref[...], preferred_element_type=jnp.float32)
-
     top = jnp.max(logits, axis=1, keepdims=True)
     teacher_top = jnp.max(teacher, axis=1, keepdims=True)
     off = logits - top
@@ -162,20 +160,20 @@
     stats_ref[...] = jnp.broadcast_to(stats.T[None, :STATS], stats_ref.shape)
 
 
-def products_kernel(rows_ref, head_ref, terms_ref):
-    chips, _, width = terms_ref.shape
-
-    def multiply(chip, _):
-        columns = pl.ds(pl.multiple_of(chip * width, LANES), width)
-        terms_ref[chip] = jnp.dot(
-            rows_ref[...], head_ref[:, columns], preferred_element_type=jnp.float32
-        )
-
-    lax.fori_loop(0, chips, multiply, None)
+def products_kernel(place_ref, rows_ref, head_ref, terms_ref, picks_ref, held_ref, sems):
+    copies = head_copies(place_ref, head_ref, held_ref, sems)
+    for copy in copies:
+        copy.start()
+    sums_rows = terms_ref.shape[1]
+    for step, copy in enumerate(copies):
+        copy.wait()
+        products = jnp.dot(rows_ref[...], held_ref[step], preferred_element_type=jnp.float32)
+        terms_ref[step] = products[:sums_rows]
+        picks_ref[step] = products[sums_rows:].astype(jnp.bfloat16)
 
 
 def combine_kernel(
-    place_ref, stats_ref, own_ref, tokens_ref, terms_ref, keep_ref, give_ref, loss_ref
+    place_ref, stats_ref, own_ref, tokens_ref, terms_ref, picks_ref, keep_ref, give_ref, loss_ref
 ):
     core = place_ref[0] % 2
     chips, _, width = terms_ref.shape
@@ -196,7 +194,9 @@
     student_shift = own_ref[0, 0:1, :tokens] - top - student_log
     teacher_shift = own_ref[0, 2:3, :tokens] - teacher_top - teacher_log
     factor = jnp.exp(student_shift)
-    level = own_ref[0, 6:7, :tokens] + student_shift - teacher_shift - divergence + sample_weight
+    level = (
+        own_ref[0, 6:7, :tokens] + student_shift - teacher_shift - divergence + sample_weight
+    )
     zeros = jnp.zeros((LANES - 3, tokens), jnp.float32)
     columns = jnp.concatenate([factor, level, per_token, zeros], axis=0).T
     share, weight = tokens_ref[:, 1:2], tokens_ref[:, 2:3]
@@ -204,21 +204,21 @@
     factor = weight * columns[:, 0:1]
     level = columns[:, 1:2]
     weight = sample_weight * weight
-    for chip in range(chips):
+    for step in range(chips):
         block = (
-            factor * (terms_ref[chip, :tokens] + level * terms_ref[chip, tokens : 2 * tokens])
-            - weight * terms_ref[chip, 2 * tokens :]
+            factor * (terms_ref[step, :tokens] + level * terms_ref[step, tokens:])
+            - weight * picks_ref[step].astype(jnp.float32)
         )
         first, second = block[:, :half], block[:, half:]
-        keep_ref[chip] = jnp.where(core == 0, first, second)
-        give_ref[chip] = jnp.where(core == 0, second, first).astype(jnp.bfloat16)
-
-
-def sum_kernel(shares_ref, total_ref):
-    total = shares_ref[0].astype(jnp.float32)
-    for chip in range(1, shares_ref.shape[0]):
-        total += shares_ref[chip].astype(jnp.float32)
-    total_ref[...] = total.astype(total_ref.dtype)
+        keep_ref[step] = jnp.where(core == 0, first, second)
+        give_ref[step] = jnp.where(core == 0, second, first).astype(jnp.bfloat16)
+
+
+def sum_kernel(own_ref, *refs):
+    total = own_ref[...]
+    for share_ref in refs[:-1]:
+        total += share_ref[...].astype(jnp.float32)
+    refs[-1][...] = total.astype(refs[-1].dtype)
 
 
 def paired_shards(
@@ -233,57 +233,77 @@
     place = jnp.reshape(own_index, (1,))
     vmem = pl.BlockSpec(memory_space=pltpu.VMEM)
     smem = pl.BlockSpec(memory_space=pltpu.SMEM)
+    hbm = pl.BlockSpec(memory_space=pl.ANY)
     params = pltpu.CompilerParams(vmem_limit_bytes=VMEM_LIMIT)
-
-    gathered = across_chips(jnp.broadcast_to(hidden_states[None], (chips, tokens, half)))
-    other = swap_cores(gathered)
-
-    held, owner, table = pl.pallas_call(
-        prepare_kernel,
+    head = in_hbm(head)
+    head_scratch = [
+        pltpu.VMEM((chips, shard_rows, width), head.dtype),
+        pltpu.SemaphoreType.DMA((chips,)),
+    ]
+
+    steps = list(range(chips - 1, 0, -1))
+    near = [across_chips(hidden_states, step) for step in steps]
+    scaled = scaled_teacher(teacher_values, teacher_scales, count, shard_rows)
+    near, scaled = lax.optimization_barrier((near, scaled))
+    near = [hidden_states] + near[::-1]
+    far = [swap_cores(piece) for piece in near]
+    arrived = lax.all_to_all(scaled, "vocab", split_axis=0, concat_axis=0, tiled=True)
+    arrived = arrived.reshape(tokens, shard_rows)
+
+    owner, table = pl.pallas_call(
+        functools.partial(prepare_kernel, shard_rows=shard_rows),
         out_shape=(
-            vmem_array(head.shape, head.dtype),
             vmem_array((tokens, tokens), jnp.bfloat16),
             vmem_array((tokens, LANES), jnp.float32),
         ),
-        in_specs=[smem] * 3 + [vmem] * 2 + [pl.BlockSpec(memory_space=pl.ANY)],
-        out_specs=[vmem] * 3,
-        scratch_shapes=[pltpu.SemaphoreType.DMA],
+        in_specs=[smem] * 3 + [vmem] * 2,
+        out_specs=[vmem] * 2,
+        compiler_params=params,
+        name="prepare",
+    )(place, lengths, loss_scale, token_ids[None, :], row_map[None, :])
+
+    logits = pl.pallas_call(
+        functools.partial(logits_kernel, chips=chips),
+        out_shape=vmem_array((tokens, shard_rows), jnp.float32),
+        in_specs=[smem] + [vmem] * (2 * chips) + [hbm],
+        out_specs=vmem,
+        scratch_shapes=head_scratch,
         compiler_params=params,
         cost_estimate=pl.CostEstimate(
-            flops=0, bytes_accessed=2 * head.size * 2, transcendentals=0
-        ),
-        name="prepare",
-    )(place, lengths, loss_scale, token_ids[None, :], row_map[None, :], in_hbm(head))
-
-    arrived = scaled_teacher(teacher_values, teacher_scales, count, shard_rows)
+            flops=2 * tokens * head.size, bytes_accessed=2 * head.size, transcendentals=0
+        ),
+        name="logits",
+    )(place, *near, *far, head)
+
     rows, stats = pl.pallas_call(
-        logits_kernel,
+        softmax_kernel,
         out_shape=(
             vmem_array((3 * tokens, shard_rows), jnp.bfloat16),
             vmem_array((count, STATS, pl.cdiv(tokens, LANES) * LANES), jnp.float32),
         ),
-        in_specs=[smem] + [vmem] * 6,
+        in_specs=[vmem] * 4,
         out_specs=[vmem] * 2,
         compiler_params=params,
-        cost_estimate=pl.CostEstimate(
-            flops=2 * tokens * head.size, bytes_accessed=2 * head.size, transcendentals=0
-        ),
-        name="logits",
-    )(place, in_vmem(gathered), in_vmem(other), in_vmem(held), in_vmem(arrived), in_vmem(owner), in_vmem(table))
+        name="softmax",
+    )(in_vmem(logits), in_vmem(arrived), in_vmem(owner), in_vmem(table))
 
     all_stats = lax.all_to_all(stats, "vocab", split_axis=0, concat_axis=0, tiled=True)
 
-    terms = pl.pallas_call(
+    terms, picks = pl.pallas_call(
         products_kernel,
-        out_shape=vmem_array((chips, 3 * tokens, width), jnp.float32),
-        in_specs=[vmem] * 2,
-        out_specs=vmem,
+        out_shape=(
+            vmem_array((chips, 2 * tokens, width), jnp.float32),
+            vmem_array((chips, tokens, width), jnp.bfloat16),
+        ),
+        in_specs=[smem, vmem, hbm],
+        out_specs=[vmem] * 2,
+        scratch_shapes=head_scratch,
         compiler_params=params,
         cost_estimate=pl.CostEstimate(
             flops=6 * tokens * head.size, bytes_accessed=2 * head.size, transcendentals=0
         ),
         name="products",
-    )(in_vmem(rows), in_vmem(held))
+    )(place, in_vmem(rows), head)
 
     keep, give, loss = pl.pallas_call(
         combine_kernel,
@@ -292,26 +312,33 @@
             vmem_array((chips, tokens, half), jnp.bfloat16),
             jax.ShapeDtypeStruct((1, 1), jnp.float32),
         ),
-        in_specs=[smem] + [vmem] * 4,
+        in_specs=[smem] + [vmem] * 5,
         out_specs=[vmem] * 3,
         compiler_params=params,
         name="combine",
-    )(place, in_vmem(all_stats), in_vmem(stats), in_vmem(table), in_vmem(terms))
+    )(
+        place,
+        in_vmem(all_stats),
+        in_vmem(stats),
+        in_vmem(table),
+        in_vmem(terms),
+        in_vmem(picks),
+    )
 
     sums = keep + swap_cores(give).astype(jnp.float32)
-    shares = across_chips(sums.astype(jnp.bfloat16))
+    shares = [across_chips(sums[step].astype(jnp.bfloat16), step) for step in steps]
     total = pl.pallas_call(
         sum_kernel,
         out_shape=jax.ShapeDtypeStruct((tokens, half), jnp.bfloat16),
-        in_specs=[vmem],
+        in_specs=[vmem] * chips,
         out_specs=vmem,
         compiler_params=params,
         name="total",
-    )(in_vmem(shares))
+    )(sums[0], *shares)
     return total, jnp.reshape(loss, (1,))
 
 
-VMEM_LIMIT = 12 * 1024 * 1024
+VMEM_LIMIT = 24 * 1024 * 1024
 
 
 def shards(
@@ -325,7 +352,9 @@
     seq_length = tokens // lengths.shape[0]
     contract_last = (((1,), (1,)), ((), ()))
 
-    arrived = scaled_teacher(teacher_values, teacher_scales, count, shard_rows)
+    scaled = scaled_teacher(teacher_values, teacher_scales, count, shard_rows)
+    arrived = lax.all_to_all(scaled, "vocab", split_axis=0, concat_axis=0, tiled=True)
+    arrived = arrived.reshape(tokens, shard_rows)
     gathered = to_all(hidden_states, count).transpose(1, 0, 2).reshape(tokens, -1)
     logits = lax.dot_general(gathered, head, contract_last, preferred_element_type=jnp.float32)
 
@@ -392,8 +421,9 @@
 
 
 def any_shards(*arrays):
+    count = lax.axis_size("vocab")
     pair_width = 2 * arrays[0].shape[1]
-    if lax.axis_size("vocab") > 2 and pair_width % LANES == 0:
+    if count > 2 and count & (count - 1) == 0 and pair_width % LANES == 0:
         return paired_shards(*arrays)
     return shards(*arrays)
 

time: 89.9 us -> 74.9 us (0.83)
  local copies, waits for them, and re-layouts: 24.4 us -> 5.17 us
  starting transfers between devices: 17.6 us -> 35.7 us
  blocking collectives: 18 us -> 0 us
  waiting for transfers between devices: 10.5 us -> 14.7 us
    ppermute x0 -> x14, starting transfers between devices: none -> 23.8 us  [across_chips(): lax.ppermute(array, 'vocab', [(i, i ^ 2 * step) for i in range(count)])]
    all_to_all x1 -> x0, blocking collectives: 18 us -> none  [across_chips(): lax.all_to_all(blocks, 'vocab', split_axis=0, concat_axis=0, axis_index_g...]
    unnamed x16 -> x12, local copies, waits for them, and re-layouts: 19.5 us -> 1.83 us
    ppermute x0 -> x14, waiting for transfers between devices: none -> 13.3 us  [across_chips(): lax.ppermute(array, 'vocab', [(i, i ^ 2 * step) for i in range(count)])]
    all_to_all x2 -> x1, waiting for transfers between devices: 9.18 us -> 0.01 us  [paired_shards(): lax.all_to_all(scaled, 'vocab', split_axis=0, concat_axis=0, tiled=True)]
    all_to_all x2 -> x1, starting transfers between devices: 11.1 us -> 3.52 us  [paired_shards(): lax.all_to_all(scaled, 'vocab', split_axis=0, concat_axis=0, tiled=True)]
    ppermute x2 -> x9, starting transfers between devices: 0.42 us -> 2.52 us  [swap_cores(): return lax.ppermute(array, 'vocab', [(i, i ^ 1) for i in range(count)])]
    broadcast_in_dim x1 -> x0, local copies, waits for them, and re-layouts: 1.59 us -> none  [paired_shards(): jnp.broadcast_to(hidden_states[None], (chips, tokens, half))]
  transfers between devices with their start and end apart: 5 -> 25, of which waited for: 2 -> 5; matrix products, arithmetic and copies ran while one was open for 4% -> 3% of each run, Pallas kernels for 11% -> 18%
where the time goes in v4:
time: 74.9 us; the launch traced here: 74.5 us
  starting transfers between devices  35.7 us (48%)
  Pallas kernels  17.2 us (23%)
  waiting for transfers between devices  14.7 us (20%)
  local copies, waits for them, and re-layouts  5.17 us (7%)
  between operations  1.56 us (2%)
    ppermute x14, starting transfers between devices, across_chips(): lax.ppermute(array, 'vocab', [(i, i ^ 2 * step) for i in range(count)])  23.8 us
    ppermute x14, waiting for transfers between devices, across_chips(): lax.ppermute(array, 'vocab', [(i, i ^ 2 * step) for i in range(count)])  13.3 us
    pallas_call x1, Pallas kernels, paired_shards(): pl.pallas_call(functools.partial(logits_kernel, chips=chips), out_shape=v...  6.57 us
    pallas_call x1, Pallas kernels, paired_shards(): pl.pallas_call(products_kernel, out_shape=(vmem_array((chips, 2 * tokens,...  6.28 us
    all_to_all x1, starting transfers between devices, paired_shards(): lax.all_to_all(stats, 'vocab', split_axis=0, concat_axis=0, tiled=True)  5.91 us
    all_to_all x1, starting transfers between devices, paired_shards(): lax.all_to_all(scaled, 'vocab', split_axis=0, concat_axis=0, tiled=True)  3.52 us
    ppermute x9, starting transfers between devices, swap_cores(): return lax.ppermute(array, 'vocab', [(i, i ^ 1) for i in range(count)])  2.52 us
    pallas_call x1, Pallas kernels, paired_shards(): pl.pallas_call(combine_kernel, out_shape=(vmem_array((chips, tokens, half...  1.84 us
  transfers between devices with their start and end apart: 25, of which 5 were waited for; matrix products, arithmetic and copies ran while one was open for 3% of the time, Pallas kernels for 18%

profile of v4, /device:TPU:0, one launch (start us, length us, event | category | flops | bytes accessed | tf_op | source)
XLA Modules:
  0.0 74.5 jit_solution(7490785542139378161)
XLA Ops:
  0.7 3.0 %collective-permute-start.6 = (bf16[64,320]{1,0:T(8,128)(2,1)}, bf16[64,320]{1,0:T(8,128)(2,1)S(1)}, u32[]{:S(2)}, u32[]{:S(2)}) collective-permute-start(bf16[64,320]{1,0:T(8,128)(2,1)} %refs_0_.1), channel_id=1, source_target_pairs={{0,2},{1,3},{2,0},{3,1},{4,6},{5,7},{6,4},{7,5},{8,10},{9,11},{10,... | collective-permute-start | bytes 122888 | tf_op jit(solution)/shard_map/ppermute | solution.py:50
  3.7 1.6 %collective-permute-start.5 = (bf16[64,320]{1,0:T(8,128)(2,1)}, bf16[64,320]{1,0:T(8,128)(2,1)S(1)}, u32[]{:S(2)}, u32[]{:S(2)}) collective-permute-start(bf16[64,320]{1,0:T(8,128)(2,1)} %refs_0_.1), channel_id=1, source_target_pairs={{0,4},{1,5},{2,6},{3,7},{4,0},{5,1},{6,2},{7,3},{8,12},{9,13},{10,... | collective-permute-start | bytes 122888 | tf_op jit(solution)/shard_map/ppermute | solution.py:50
  5.3 3.0 %collective-permute-start.3 = (bf16[64,320]{1,0:T(8,128)(2,1)}, bf16[64,320]{1,0:T(8,128)(2,1)S(1)}, u32[]{:S(2)}, u32[]{:S(2)}) collective-permute-start(bf16[64,320]{1,0:T(8,128)(2,1)} %refs_0_.1), channel_id=1, source_target_pairs={{0,8},{1,9},{2,10},{3,11},{4,12},{5,13},{6,14},{7,15},{8,0},{9,1},... | collective-permute-start | bytes 122888 | tf_op jit(solution)/shard_map/ppermute | solution.py:50
  8.3 1.3 %collective-permute-start.2 = (bf16[64,320]{1,0:T(8,128)(2,1)}, bf16[64,320]{1,0:T(8,128)(2,1)S(1)}, u32[]{:S(2)}, u32[]{:S(2)}) collective-permute-start(bf16[64,320]{1,0:T(8,128)(2,1)} %refs_0_.1), channel_id=1, source_target_pairs={{0,10},{1,11},{2,8},{3,9},{4,14},{5,15},{6,12},{7,13},{8,2},{9,3},... | collective-permute-start | bytes 122888 | tf_op jit(solution)/shard_map/ppermute | solution.py:50
  9.6 1.1 %reshape.36 = f32[4,16,1216]{2,1,0:T(8,128)S(1)} reshape(bf16[4,19456]{1,0:T(4,128)(2,1)} %param.10) | data formatting | bytes 466944 | tf_op jit(solution)/shard_map/reshape | solution.py:26
  10.6 1.1 %mul.11 = f32[4,608,32]{2,1,0:T(8,128)S(1)} broadcast(f32[4,608]{1,0:T(4,128)} %param.11), dimensions={0,1} | broadcast | bytes 321024 | tf_op jit(solution)/shard_map/mul | solution.py:26
  12.1 3.7 %collective-permute-start.1 = (bf16[64,320]{1,0:T(8,128)(2,1)S(1)}, bf16[64,320]{1,0:T(8,128)(2,1)S(1)}, u32[]{:S(2)}, u32[]{:S(2)}) collective-permute-start(bf16[64,320]{1,0:T(8,128)(2,1)S(1)} %copy-done.2), channel_id=1, source_target_pairs={{0,12},{1,13},{2,14},{3,15},{4,8},{5,9},{6,10},{7,11},{8,4},{9,5},... | collective-permute-start | bytes 122888 | tf_op jit(solution)/shard_map/ppermute | solution.py:50
  15.9 2.2 %collective-permute-done.1.refs_6_ = bf16[64,320]{1,0:T(8,128)(2,1)S(1)} collective-permute-done((bf16[64,320]{1,0:T(8,128)(2,1)S(1)}, bf16[64,320]{1,0:T(8,128)(2,1)S(1)}, u32[]{:S(2)}, u32[]{:S(2)}) %collective-permute-start.1) | collective-permute-done | bytes 40992 | tf_op jit(solution)/shard_map/ppermute | solution.py:50
  18.0 4.5 %collective-permute-done.refs_7_ = bf16[64,320]{1,0:T(8,128)(2,1)S(1)} collective-permute-done((bf16[64,320]{1,0:T(8,128)(2,1)S(1)}, bf16[64,320]{1,0:T(8,128)(2,1)S(1)}, u32[]{:S(2)}, u32[]{:S(2)}) %collective-permute-start) | collective-permute-done | bytes 40992 | tf_op jit(solution)/shard_map/ppermute | solution.py:50
  23.3 3.5 %all-to-all-start = ((bf16[16,4,1216]{2,1,0:T(4,128)(2,1)}), bf16[16,4,1216]{2,1,0:T(4,128)(2,1)S(1)}, u32[]{:S(2)}, u32[]{:S(2)}) async-start(bf16[16,4,1216]{2,1,0:T(4,128)(2,1)} %copy.12), calls=%async_computation | async-start | bytes 327680 | tf_op jit(solution)/shard_map/all_to_all | solution.py:250
  30.3 6.6 %logits.1.logits_ref = f32[64,1216]{1,0:T(8,128)S(1)} custom-call(s32[1]{0:T(128)} %bitcast.place_ref, bf16[64,320]{1,0:T(8,128)(2,1)S(1)} %copy-done.2, bf16[64,320]{1,0:T(8,128)(2,1)S(1)} %collective-permute-done.6.refs_1_, bf16[64,320]{1,0:T(8,128)(2,1)S(1)} %collective-permute-done.5.refs_2_, bf16[64,320]{1,0:T(8,128)(2,1)S(1)} %collective-permute-done.4.refs_3_, ...), custom_call_target="tpu_custom_call" | custom-call | flops 796917760 | bytes 12451840 | tf_op jit(solution)/shard_map/logits/pallas_call | solution.py:265
  37.0 1.2 %softmax.1 = (bf16[192,1216]{1,0:T(8,128)(2,1)S(1)}, f32[16,8,128]{2,1,0:T(8,128)}) custom-call(f32[64,1216]{1,0:T(8,128)S(1)} %logits.1.logits_ref, bf16[64,1216]{1,0:T(8,128)(2,1)S(1)} %reshape.33.arrived_ref, bf16[64,64]{1,0:T(8,128)(2,1)S(1)} %get-tuple-element.27.owner_ref, f32[64,128]{1,0:T(8,128)S(1)} %get-tuple-element.28.tokens_ref), custom_call_target="tpu_custom_call" | custom-call | tf_op jit(solution)/shard_map/softmax/pallas_call | solution.py:278
  38.9 5.9 %all-to-all-start.1 = ((f32[16,8,128]{2,1,0:T(8,128)}), f32[16,8,128]{2,1,0:T(8,128)S(1)}, u32[]{:S(2)}, u32[]{:S(2)}) async-start(f32[16,8,128]{2,1,0:T(8,128)} %get-tuple-element.29.own_ref), calls=%async_computation.1 | async-start | bytes 131072 | tf_op jit(solution)/shard_map/all_to_all | solution.py:290
  44.8 1.0 %copy-done.1 = bf16[192,1216]{1,0:T(8,128)(2,1)S(1)} copy-done((bf16[192,1216]{1,0:T(8,128)(2,1)S(1)}, bf16[192,1216]{1,0:T(8,128)(2,1)}, u32[]{:S(2)}) %copy-start.1) | copy-done | bytes 466968
  45.9 6.3 %products.1 = (f32[8,128,640]{2,1,0:T(8,128)S(1)}, bf16[8,64,640]{2,1,0:T(8,128)(2,1)S(1)}) custom-call(s32[1]{0:T(128)} %bitcast.place_ref, bf16[192,1216]{1,0:T(8,128)(2,1)S(1)} %copy-done.1, bf16[1216,5120]{1,0:T(8,128)(2,1)} %head_ref.1), custom_call_target="tpu_custom_call" | custom-call | flops 2390753280 | bytes 12451840 | tf_op jit(solution)/shard_map/products/pallas_call | solution.py:292
  52.2 1.8 %combine.1 = (f32[8,64,320]{2,1,0:T(8,128)S(1)}, bf16[8,64,320]{2,1,0:T(8,128)(2,1)S(1)}, f32[1,1]{1,0:T(1,128)}) custom-call(s32[1]{0:T(128)} %bitcast.place_ref, f32[16,8,128]{2,1,0:T(8,128)S(1)} %all-to-all-done.1.stats_ref, f32[16,8,128]{2,1,0:T(8,128)} %get-tuple-element.29.own_ref, f32[64,128]{1,0:T(8,128)S(1)} %get-tuple-element.28.tokens_ref, ...), custom_call_target="tpu_custom_call" | custom-call | tf_op jit(solution)/shard_map/combine/pallas_call | solution.py:308
  54.4 1.3 %collective-permute-done.15 = bf16[8,64,320]{2,1,0:T(8,128)(2,1)S(1)} collective-permute-done((bf16[8,64,320]{2,1,0:T(8,128)(2,1)S(1)}, bf16[8,64,320]{2,1,0:T(8,128)(2,1)S(1)}, u32[]{:S(2)}, u32[]{:S(2)}) %collective-permute-start.15) | collective-permute-done | bytes 327712 | tf_op jit(solution)/shard_map/ppermute | solution.py:45
  56.0 2.0 %collective-permute-start.22 = (bf16[64,320]{1,0:T(8,128)(2,1)S(1)}, bf16[64,320]{1,0:T(8,128)(2,1)S(1)}, u32[]{:S(2)}, u32[]{:S(2)}) collective-permute-start(bf16[64,320]{1,0:T(8,128)(2,1)S(1)} %get-tuple-element.38), channel_id=1, source_target_pairs={{0,2},{1,3},{2,0},{3,1},{4,6},{5,7},{6,4},{7,5},{8,10},{9,11},{10,... | collective-permute-start | bytes 122888 | tf_op jit(solution)/shard_map/ppermute | solution.py:50
  57.9 1.4 %collective-permute-start.21 = (bf16[64,320]{1,0:T(8,128)(2,1)S(1)}, bf16[64,320]{1,0:T(8,128)(2,1)S(1)}, u32[]{:S(2)}, u32[]{:S(2)}) collective-permute-start(bf16[64,320]{1,0:T(8,128)(2,1)S(1)} %get-tuple-element.39), channel_id=1, source_target_pairs={{0,4},{1,5},{2,6},{3,7},{4,0},{5,1},{6,2},{7,3},{8,12},{9,13},{10,... | collective-permute-start | bytes 122888 | tf_op jit(solution)/shard_map/ppermute | solution.py:50
  59.5 2.8 %collective-permute-start.19 = (bf16[64,320]{1,0:T(8,128)(2,1)S(1)}, bf16[64,320]{1,0:T(8,128)(2,1)S(1)}, u32[]{:S(2)}, u32[]{:S(2)}) collective-permute-start(bf16[64,320]{1,0:T(8,128)(2,1)S(1)} %get-tuple-element.41), channel_id=1, source_target_pairs={{0,8},{1,9},{2,10},{3,11},{4,12},{5,13},{6,14},{7,15},{8,0},{9,1},... | collective-permute-start | bytes 122888 | tf_op jit(solution)/shard_map/ppermute | solution.py:50
  62.3 1.5 %collective-permute-start.18 = (bf16[64,320]{1,0:T(8,128)(2,1)S(1)}, bf16[64,320]{1,0:T(8,128)(2,1)S(1)}, u32[]{:S(2)}, u32[]{:S(2)}) collective-permute-start(bf16[64,320]{1,0:T(8,128)(2,1)S(1)} %get-tuple-element.42), channel_id=1, source_target_pairs={{0,10},{1,11},{2,8},{3,9},{4,14},{5,15},{6,12},{7,13},{8,2},{9,3},... | collective-permute-start | bytes 122888 | tf_op jit(solution)/shard_map/ppermute | solution.py:50
  63.8 3.3 %collective-permute-start.17 = (bf16[64,320]{1,0:T(8,128)(2,1)S(1)}, bf16[64,320]{1,0:T(8,128)(2,1)S(1)}, u32[]{:S(2)}, u32[]{:S(2)}) collective-permute-start(bf16[64,320]{1,0:T(8,128)(2,1)S(1)} %get-tuple-element.43), channel_id=1, source_target_pairs={{0,12},{1,13},{2,14},{3,15},{4,8},{5,9},{6,10},{7,11},{8,4},{9,5},... | collective-permute-start | bytes 122888 | tf_op jit(solution)/shard_map/ppermute | solution.py:50
  67.2 2.8 %collective-permute-done.18.refs_2_ = bf16[64,320]{1,0:T(8,128)(2,1)S(1)} collective-permute-done((bf16[64,320]{1,0:T(8,128)(2,1)S(1)}, bf16[64,320]{1,0:T(8,128)(2,1)S(1)}, u32[]{:S(2)}, u32[]{:S(2)}) %collective-permute-start.18) | collective-permute-done | bytes 40992 | tf_op jit(solution)/shard_map/ppermute | solution.py:50
  70.0 3.8 %collective-permute-done.16.refs_0_ = bf16[64,320]{1,0:T(8,128)(2,1)S(1)} collective-permute-done((bf16[64,320]{1,0:T(8,128)(2,1)S(1)}, bf16[64,320]{1,0:T(8,128)(2,1)S(1)}, u32[]{:S(2)}, u32[]{:S(2)}) %collective-permute-start.16) | collective-permute-done | bytes 40992 | tf_op jit(solution)/shard_map/ppermute | solution.py:50
  (53 shorter events, 6.4 us)
Async XLA Ops:
  0.7 11.4 %collective-permute-start.6 = (bf16[64,320]{1,0:T(8,128)(2,1)}, bf16[64,320]{1,0:T(8,128)(2,1)S(1)}, u32[]{:S(2)}, u32[]{:S(2)}) collective-permute-start(bf16[64,320]{1,0:T(8,128)(2,1)} %refs_0_.1), channel_id=1, source_target_pairs={{0,2},{1,3},{2,0},{3,1},{4,6},{5,7},{6,4},{7,5},{8,10},{9,11},{10,... | collective-permute-start | bytes 122888 | tf_op jit(solution)/shard_map/ppermute | solution.py:50
  3.7 12.1 %collective-permute-start.5 = (bf16[64,320]{1,0:T(8,128)(2,1)}, bf16[64,320]{1,0:T(8,128)(2,1)S(1)}, u32[]{:S(2)}, u32[]{:S(2)}) collective-permute-start(bf16[64,320]{1,0:T(8,128)(2,1)} %refs_0_.1), channel_id=1, source_target_pairs={{0,4},{1,5},{2,6},{3,7},{4,0},{5,1},{6,2},{7,3},{8,12},{9,13},{10,... | collective-permute-start | bytes 122888 | tf_op jit(solution)/shard_map/ppermute | solution.py:50
  5.3 10.5 %collective-permute-start.4 = (bf16[64,320]{1,0:T(8,128)(2,1)}, bf16[64,320]{1,0:T(8,128)(2,1)S(1)}, u32[]{:S(2)}, u32[]{:S(2)}) collective-permute-start(bf16[64,320]{1,0:T(8,128)(2,1)} %refs_0_.1), channel_id=1, source_target_pairs={{0,6},{1,7},{2,4},{3,5},{4,2},{5,3},{6,0},{7,1},{8,14},{9,15},{10,... | collective-permute-start | bytes 122888 | tf_op jit(solution)/shard_map/ppermute | solution.py:50
  5.3 10.6 %collective-permute-start.3 = (bf16[64,320]{1,0:T(8,128)(2,1)}, bf16[64,320]{1,0:T(8,128)(2,1)S(1)}, u32[]{:S(2)}, u32[]{:S(2)}) collective-permute-start(bf16[64,320]{1,0:T(8,128)(2,1)} %refs_0_.1), channel_id=1, source_target_pairs={{0,8},{1,9},{2,10},{3,11},{4,12},{5,13},{6,14},{7,15},{8,0},{9,1},... | collective-permute-start | bytes 122888 | tf_op jit(solution)/shard_map/ppermute | solution.py:50
  8.3 7.6 %collective-permute-start.2 = (bf16[64,320]{1,0:T(8,128)(2,1)}, bf16[64,320]{1,0:T(8,128)(2,1)S(1)}, u32[]{:S(2)}, u32[]{:S(2)}) collective-permute-start(bf16[64,320]{1,0:T(8,128)(2,1)} %refs_0_.1), channel_id=1, source_target_pairs={{0,10},{1,11},{2,8},{3,9},{4,14},{5,15},{6,12},{7,13},{8,2},{9,3},... | collective-permute-start | bytes 122888 | tf_op jit(solution)/shard_map/ppermute | solution.py:50
  12.1 6.0 %collective-permute-start.1 = (bf16[64,320]{1,0:T(8,128)(2,1)S(1)}, bf16[64,320]{1,0:T(8,128)(2,1)S(1)}, u32[]{:S(2)}, u32[]{:S(2)}) collective-permute-start(bf16[64,320]{1,0:T(8,128)(2,1)S(1)} %copy-done.2), channel_id=1, source_target_pairs={{0,12},{1,13},{2,14},{3,15},{4,8},{5,9},{6,10},{7,11},{8,4},{9,5},... | collective-permute-start | bytes 122888 | tf_op jit(solution)/shard_map/ppermute | solution.py:50
  15.8 6.8 %collective-permute-start = (bf16[64,320]{1,0:T(8,128)(2,1)S(1)}, bf16[64,320]{1,0:T(8,128)(2,1)S(1)}, u32[]{:S(2)}, u32[]{:S(2)}) collective-permute-start(bf16[64,320]{1,0:T(8,128)(2,1)S(1)} %copy-done.2), channel_id=1, source_target_pairs={{0,14},{1,15},{2,12},{3,13},{4,10},{5,11},{6,8},{7,9},{8,6},{9,7},... | collective-permute-start | bytes 122888 | tf_op jit(solution)/shard_map/ppermute | solution.py:50
  23.3 13.6 %all-to-all-start = ((bf16[16,4,1216]{2,1,0:T(4,128)(2,1)}), bf16[16,4,1216]{2,1,0:T(4,128)(2,1)S(1)}, u32[]{:S(2)}, u32[]{:S(2)}) async-start(bf16[16,4,1216]{2,1,0:T(4,128)(2,1)} %copy.12), calls=%async_computation | async-start | bytes 327680 | tf_op jit(solution)/shard_map/all_to_all | solution.py:250
  26.8 1.3 %collective-permute-start.7 = (bf16[64,320]{1,0:T(8,128)(2,1)S(1)}, bf16[64,320]{1,0:T(8,128)(2,1)S(1)}, u32[]{:S(2)}, u32[]{:S(2)}) collective-permute-start(bf16[64,320]{1,0:T(8,128)(2,1)S(1)} %copy-done.2), channel_id=1, source_target_pairs={{0,1},{1,0},{2,3},{3,2},{4,5},{5,4},{6,7},{7,6},{8,9},{9,8},{10,11... | collective-permute-start | bytes 122888 | tf_op jit(solution)/shard_map/ppermute | solution.py:45
  27.1 1.3 %collective-permute-start.8 = (bf16[64,320]{1,0:T(8,128)(2,1)S(1)}, bf16[64,320]{1,0:T(8,128)(2,1)S(1)}, u32[]{:S(2)}, u32[]{:S(2)}) collective-permute-start(bf16[64,320]{1,0:T(8,128)(2,1)S(1)} %collective-permute-done.6.refs_1_), channel_id=1, source_target_pairs={{0,1},{1,0},{2,3},{3,2},{4,5},{5,4},{6,7},{7,6},{8,9},{9,8},{10,11... | collective-permute-start | bytes 122888 | tf_op jit(solution)/shard_map/ppermute | solution.py:45
  27.6 2.7 %collective-permute-start.10 = (bf16[64,320]{1,0:T(8,128)(2,1)S(1)}, bf16[64,320]{1,0:T(8,128)(2,1)S(1)}, u32[]{:S(2)}, u32[]{:S(2)}) collective-permute-start(bf16[64,320]{1,0:T(8,128)(2,1)S(1)} %collective-permute-done.4.refs_3_), channel_id=1, source_target_pairs={{0,1},{1,0},{2,3},{3,2},{4,5},{5,4},{6,7},{7,6},{8,9},{9,8},{10,11... | collective-permute-start | bytes 122888 | tf_op jit(solution)/shard_map/ppermute | solution.py:45
  27.9 2.4 %collective-permute-start.11 = (bf16[64,320]{1,0:T(8,128)(2,1)S(1)}, bf16[64,320]{1,0:T(8,128)(2,1)S(1)}, u32[]{:S(2)}, u32[]{:S(2)}) collective-permute-start(bf16[64,320]{1,0:T(8,128)(2,1)S(1)} %collective-permute-done.3.refs_4_), channel_id=1, source_target_pairs={{0,1},{1,0},{2,3},{3,2},{4,5},{5,4},{6,7},{7,6},{8,9},{9,8},{10,11... | collective-permute-start | bytes 122888 | tf_op jit(solution)/shard_map/ppermute | solution.py:45
  28.1 2.2 %collective-permute-start.12 = (bf16[64,320]{1,0:T(8,128)(2,1)S(1)}, bf16[64,320]{1,0:T(8,128)(2,1)S(1)}, u32[]{:S(2)}, u32[]{:S(2)}) collective-permute-start(bf16[64,320]{1,0:T(8,128)(2,1)S(1)} %collective-permute-done.2.refs_5_), channel_id=1, source_target_pairs={{0,1},{1,0},{2,3},{3,2},{4,5},{5,4},{6,7},{7,6},{8,9},{9,8},{10,11... | collective-permute-start | bytes 122888 | tf_op jit(solution)/shard_map/ppermute | solution.py:45
  28.4 1.9 %collective-permute-start.13 = (bf16[64,320]{1,0:T(8,128)(2,1)S(1)}, bf16[64,320]{1,0:T(8,128)(2,1)S(1)}, u32[]{:S(2)}, u32[]{:S(2)}) collective-permute-start(bf16[64,320]{1,0:T(8,128)(2,1)S(1)} %collective-permute-done.1.refs_6_), channel_id=1, source_target_pairs={{0,1},{1,0},{2,3},{3,2},{4,5},{5,4},{6,7},{7,6},{8,9},{9,8},{10,11... | collective-permute-start | bytes 122888 | tf_op jit(solution)/shard_map/ppermute | solution.py:45
  28.7 1.7 %collective-permute-start.14 = (bf16[64,320]{1,0:T(8,128)(2,1)S(1)}, bf16[64,320]{1,0:T(8,128)(2,1)S(1)}, u32[]{:S(2)}, u32[]{:S(2)}) collective-permute-start(bf16[64,320]{1,0:T(8,128)(2,1)S(1)} %collective-permute-done.refs_7_), channel_id=1, source_target_pairs={{0,1},{1,0},{2,3},{3,2},{4,5},{5,4},{6,7},{7,6},{8,9},{9,8},{10,11... | collective-permute-start | bytes 122888 | tf_op jit(solution)/shard_map/ppermute | solution.py:45
  38.9 13.2 %all-to-all-start.1 = ((f32[16,8,128]{2,1,0:T(8,128)}), f32[16,8,128]{2,1,0:T(8,128)S(1)}, u32[]{:S(2)}, u32[]{:S(2)}) async-start(f32[16,8,128]{2,1,0:T(8,128)} %get-tuple-element.29.own_ref), calls=%async_computation.1 | async-start | bytes 131072 | tf_op jit(solution)/shard_map/all_to_all | solution.py:290
  54.0 1.8 %collective-permute-start.15 = (bf16[8,64,320]{2,1,0:T(8,128)(2,1)S(1)}, bf16[8,64,320]{2,1,0:T(8,128)(2,1)S(1)}, u32[]{:S(2)}, u32[]{:S(2)}) collective-permute-start(bf16[8,64,320]{2,1,0:T(8,128)(2,1)S(1)} %get-tuple-element.34), channel_id=1, source_target_pairs={{0,1},{1,0},{2,3},{3,2},{4,5},{5,4},{6,7},{7,6},{8,9},{9,8},{10,11... | collective-permute-start | bytes 983048 | tf_op jit(solution)/shard_map/ppermute | solution.py:45
  56.0 7.8 %collective-permute-start.22 = (bf16[64,320]{1,0:T(8,128)(2,1)S(1)}, bf16[64,320]{1,0:T(8,128)(2,1)S(1)}, u32[]{:S(2)}, u32[]{:S(2)}) collective-permute-start(bf16[64,320]{1,0:T(8,128)(2,1)S(1)} %get-tuple-element.38), channel_id=1, source_target_pairs={{0,2},{1,3},{2,0},{3,1},{4,6},{5,7},{6,4},{7,5},{8,10},{9,11},{10,... | collective-permute-start | bytes 122888 | tf_op jit(solution)/shard_map/ppermute | solution.py:50
  57.9 9.1 %collective-permute-start.21 = (bf16[64,320]{1,0:T(8,128)(2,1)S(1)}, bf16[64,320]{1,0:T(8,128)(2,1)S(1)}, u32[]{:S(2)}, u32[]{:S(2)}) collective-permute-start(bf16[64,320]{1,0:T(8,128)(2,1)S(1)} %get-tuple-element.39), channel_id=1, source_target_pairs={{0,4},{1,5},{2,6},{3,7},{4,0},{5,1},{6,2},{7,3},{8,12},{9,13},{10,... | collective-permute-start | bytes 122888 | tf_op jit(solution)/shard_map/ppermute | solution.py:50
  59.4 7.8 %collective-permute-start.20 = (bf16[64,320]{1,0:T(8,128)(2,1)S(1)}, bf16[64,320]{1,0:T(8,128)(2,1)S(1)}, u32[]{:S(2)}, u32[]{:S(2)}) collective-permute-start(bf16[64,320]{1,0:T(8,128)(2,1)S(1)} %get-tuple-element.40), channel_id=1, source_target_pairs={{0,6},{1,7},{2,4},{3,5},{4,2},{5,3},{6,0},{7,1},{8,14},{9,15},{10,... | collective-permute-start | bytes 122888 | tf_op jit(solution)/shard_map/ppermute | solution.py:50
  59.5 7.7 %collective-permute-start.19 = (bf16[64,320]{1,0:T(8,128)(2,1)S(1)}, bf16[64,320]{1,0:T(8,128)(2,1)S(1)}, u32[]{:S(2)}, u32[]{:S(2)}) collective-permute-start(bf16[64,320]{1,0:T(8,128)(2,1)S(1)} %get-tuple-element.41), channel_id=1, source_target_pairs={{0,8},{1,9},{2,10},{3,11},{4,12},{5,13},{6,14},{7,15},{8,0},{9,1},... | collective-permute-start | bytes 122888 | tf_op jit(solution)/shard_map/ppermute | solution.py:50
  62.3 7.7 %collective-permute-start.18 = (bf16[64,320]{1,0:T(8,128)(2,1)S(1)}, bf16[64,320]{1,0:T(8,128)(2,1)S(1)}, u32[]{:S(2)}, u32[]{:S(2)}) collective-permute-start(bf16[64,320]{1,0:T(8,128)(2,1)S(1)} %get-tuple-element.42), channel_id=1, source_target_pairs={{0,10},{1,11},{2,8},{3,9},{4,14},{5,15},{6,12},{7,13},{8,2},{9,3},... | collective-permute-start | bytes 122888 | tf_op jit(solution)/shard_map/ppermute | solution.py:50
  63.8 6.3 %collective-permute-start.17 = (bf16[64,320]{1,0:T(8,128)(2,1)S(1)}, bf16[64,320]{1,0:T(8,128)(2,1)S(1)}, u32[]{:S(2)}, u32[]{:S(2)}) collective-permute-start(bf16[64,320]{1,0:T(8,128)(2,1)S(1)} %get-tuple-element.43), channel_id=1, source_target_pairs={{0,12},{1,13},{2,14},{3,15},{4,8},{5,9},{6,10},{7,11},{8,4},{9,5},... | collective-permute-start | bytes 122888 | tf_op jit(solution)/shard_map/ppermute | solution.py:50
  67.0 6.8 %collective-permute-start.16 = (bf16[64,320]{1,0:T(8,128)(2,1)S(1)}, bf16[64,320]{1,0:T(8,128)(2,1)S(1)}, u32[]{:S(2)}, u32[]{:S(2)}) collective-permute-start(bf16[64,320]{1,0:T(8,128)(2,1)S(1)} %get-tuple-element.44), channel_id=1, source_target_pairs={{0,14},{1,15},{2,12},{3,13},{4,10},{5,11},{6,8},{7,9},{8,6},{9,7},... | collective-permute-start | bytes 122888 | tf_op jit(solution)/shard_map/ppermute | solution.py:50
  (7 other events, 101.4 us)

commit v5 on v4

--- a/solution.py
+++ b/solution.py
@@ -45,9 +45,17 @@
     return lax.ppermute(array, "vocab", [(i, i ^ 1) for i in range(count)])
 
 
-def across_chips(array, step):
-    count = lax.axis_size("vocab")
-    return lax.ppermute(array, "vocab", [(i, i ^ (2 * step)) for i in range(count)])
+def across_chips(blocks):
+    count = lax.axis_size("vocab")
+    groups = [list(range(core, count, 2)) for core in range(2)]
+    return lax.all_to_all(
+        blocks, "vocab", split_axis=0, concat_axis=0, axis_index_groups=groups, tiled=True
+    )
+
+
+def along_chips(array, step):
+    count = lax.axis_size("vocab")
+    return lax.ppermute(array, "vocab", [(i, (i + 2 * step) % count) for i in range(count)])
 
 
 def vmem_array(shape, dtype):
@@ -95,36 +103,33 @@
     tokens_ref[...] = jnp.where(lane == 0, entry, jnp.where(lane == 1, share, weight))
 
 
-def head_copies(place_ref, head_ref, held_ref, sems):
+def head_copies(head_ref, held_ref, sems, first):
     chips, _, width = held_ref.shape
-    chip = place_ref[0] // 2
     copies = []
     for step in range(chips):
-        columns = pl.ds(pl.multiple_of(jnp.bitwise_xor(chip, step) * width, LANES), width)
+        columns = pl.ds(pl.multiple_of(lax.rem(first + step, chips) * width, LANES), width)
         copies.append(
             pltpu.make_async_copy(head_ref.at[:, columns], held_ref.at[step], sems.at[step])
         )
     return copies
 
 
-def logits_kernel(place_ref, *refs, chips):
-    near, far = refs[:chips], refs[chips : 2 * chips]
-    head_ref, logits_ref, held_ref, sems = refs[2 * chips :]
-    copies = head_copies(place_ref, head_ref, held_ref, sems)
+def logits_kernel(place_ref, own_ref, other_ref, head_ref, logits_ref, held_ref, sems):
+    copies = head_copies(head_ref, held_ref, sems, 0)
     for copy in copies:
         copy.start()
     core = place_ref[0] % 2
     logits = jnp.zeros(logits_ref.shape, jnp.float32)
-    for step in range(chips):
-        own, other = near[step][...], far[step][...]
+    for chip, copy in enumerate(copies):
+        own, other = own_ref[chip], other_ref[chip]
         block = jnp.where(
             core == 0,
             jnp.concatenate([own, other], axis=1),
             jnp.concatenate([other, own], axis=1),
         )
-        copies[step].wait()
+        copy.wait()
         logits += lax.dot_general(
-            block, held_ref[step], (((1,), (1,)), ((), ())), preferred_element_type=jnp.float32
+            block, held_ref[chip], (((1,), (1,)), ((), ())), preferred_element_type=jnp.float32
         )
     logits_ref[...] = logits
 
@@ -161,7 +166,7 @@
 
 
 def products_kernel(place_ref, rows_ref, head_ref, terms_ref, picks_ref, held_ref, sems):
-    copies = head_copies(place_ref, head_ref, held_ref, sems)
+    copies = head_copies(head_ref, held_ref, sems, place_ref[0] // 2)
     for copy in copies:
         copy.start()
     sums_rows = terms_ref.shape[1]
@@ -241,12 +246,10 @@
         pltpu.SemaphoreType.DMA((chips,)),
     ]
 
-    steps = list(range(chips - 1, 0, -1))
-    near = [across_chips(hidden_states, step) for step in steps]
+    gathered = across_chips(jnp.broadcast_to(hidden_states[None], (chips, tokens, half)))
     scaled = scaled_teacher(teacher_values, teacher_scales, count, shard_rows)
-    near, scaled = lax.optimization_barrier((near, scaled))
-    near = [hidden_states] + near[::-1]
-    far = [swap_cores(piece) for piece in near]
+    gathered, scaled = lax.optimization_barrier((gathered, scaled))
+    other = swap_cores(gathered)
     arrived = lax.all_to_all(scaled, "vocab", split_axis=0, concat_axis=0, tiled=True)
     arrived = arrived.reshape(tokens, shard_rows)
 
@@ -263,9 +266,9 @@
     )(place, lengths, loss_scale, token_ids[None, :], row_map[None, :])
 
     logits = pl.pallas_call(
-        functools.partial(logits_kernel, chips=chips),
+        logits_kernel,
         out_shape=vmem_array((tokens, shard_rows), jnp.float32),
-        in_specs=[smem] + [vmem] * (2 * chips) + [hbm],
+        in_specs=[smem] + [vmem] * 2 + [hbm],
         out_specs=vmem,
         scratch_shapes=head_scratch,
         compiler_params=params,
@@ -273,19 +276,19 @@
             flops=2 * tokens * head.size, bytes_accessed=2 * head.size, transcendentals=0
         ),
         name="logits",
-    )(place, *near, *far, head)
+    )(place, gathered, other, head)
 
     rows, stats = pl.pallas_call(
         softmax_kernel,
         out_shape=(
-            vmem_array((3 * tokens, shard_rows), jnp.bfloat16),
-            vmem_array((count, STATS, pl.cdiv(tokens, LANES) * LANES), jnp.float32),
+            jax.ShapeDtypeStruct((3 * tokens, shard_rows), jnp.bfloat16),
+            jax.ShapeDtypeStruct((count, STATS, pl.cdiv(tokens, LANES) * LANES), jnp.float32),
         ),
         in_specs=[vmem] * 4,
         out_specs=[vmem] * 2,
         compiler_params=params,
         name="softmax",
-    )(in_vmem(logits), in_vmem(arrived), in_vmem(owner), in_vmem(table))
+    )(in_vmem(logits), arrived, in_vmem(owner), in_vmem(table))
 
     all_stats = lax.all_to_all(stats, "vocab", split_axis=0, concat_axis=0, tiled=True)
 
@@ -303,7 +306,7 @@
             flops=6 * tokens * head.size, bytes_accessed=2 * head.size, transcendentals=0
         ),
         name="products",
-    )(place, in_vmem(rows), head)
+    )(place, rows, head)
 
     keep, give, loss = pl.pallas_call(
         combine_kernel,
@@ -318,15 +321,15 @@
         name="combine",
     )(
         place,
-        in_vmem(all_stats),
-        in_vmem(stats),
+        all_stats,
+        stats,
         in_vmem(table),
         in_vmem(terms),
         in_vmem(picks),
     )
 
     sums = keep + swap_cores(give).astype(jnp.float32)
-    shares = [across_chips(sums[step].astype(jnp.bfloat16), step) for step in steps]
+    shares = [along_chips(sums[step].astype(jnp.bfloat16), step) for step in range(1, chips)]
     total = pl.pallas_call(
         sum_kernel,
         out_shape=jax.ShapeDtypeStruct((tokens, half), jnp.bfloat16),

time: 74.9 us -> 75.7 us (1.011)
  starting transfers between devices: 35.7 us -> 26.1 us
  waiting for transfers between devices: 14.7 us -> 23.5 us
  local copies, waits for them, and re-layouts: 5.17 us -> 6.74 us
    ppermute x14 -> x7, starting transfers between devices: 23.8 us -> 11 us  [along_chips(): lax.ppermute(array, 'vocab', [(i, (i + 2 * step) % count) for i in range(...]
    all_to_all x0 -> x1, waiting for transfers between devices: none -> 9.13 us  [across_chips(): lax.all_to_all(blocks, 'vocab', split_axis=0, concat_axis=0, axis_index_g...]
    ppermute x14 -> x7, waiting for transfers between devices: 13.3 us -> 5.82 us  [along_chips(): lax.ppermute(array, 'vocab', [(i, (i + 2 * step) % count) for i in range(...]
    all_to_all x0 -> x1, starting transfers between devices: none -> 7.41 us  [across_chips(): lax.all_to_all(blocks, 'vocab', split_axis=0, concat_axis=0, axis_index_g...]
    all_to_all x1, waiting for transfers between devices: 0.01 us -> 7.13 us  [paired_shards(): lax.all_to_all(scaled, 'vocab', split_axis=0, concat_axis=0, tiled=True)]
    all_to_all x1, starting transfers between devices: 5.91 us -> 3.48 us  [paired_shards(): lax.all_to_all(stats, 'vocab', split_axis=0, concat_axis=0, tiled=True)]
    ppermute x9 -> x2, starting transfers between devices: 2.52 us -> 0.29 us  [swap_cores(): return lax.ppermute(array, 'vocab', [(i, i ^ 1) for i in range(count)])]
    broadcast_in_dim x0 -> x1, local copies, waits for them, and re-layouts: none -> 1.57 us  [paired_shards(): jnp.broadcast_to(hidden_states[None], (chips, tokens, half))]
  transfers between devices with their start and end apart: 25 -> 12, of which waited for: 5 -> 6; matrix products, arithmetic and copies ran while one was open for 3% -> 4% of each run, Pallas kernels for 18% -> 9%
where the time goes in v5:
time: 75.7 us; the launch traced here: 75.1 us
  starting transfers between devices  26.1 us (34%)
  waiting for transfers between devices  23.5 us (31%)
  Pallas kernels  17.1 us (23%)
  local copies, waits for them, and re-layouts  6.74 us (9%)
  between operations  1.44 us (2%)
    ppermute x7, starting transfers between devices, along_chips(): lax.ppermute(array, 'vocab', [(i, (i + 2 * step) % count) for i in range(...  11 us
    all_to_all x1, waiting for transfers between devices, across_chips(): lax.all_to_all(blocks, 'vocab', split_axis=0, concat_axis=0, axis_index_g...  9.13 us
    all_to_all x1, starting transfers between devices, across_chips(): lax.all_to_all(blocks, 'vocab', split_axis=0, concat_axis=0, axis_index_g...  7.41 us
    all_to_all x1, waiting for transfers between devices, paired_shards(): lax.all_to_all(scaled, 'vocab', split_axis=0, concat_axis=0, tiled=True)  7.13 us
    pallas_call x1, Pallas kernels, paired_shards(): pl.pallas_call(logits_kernel, out_shape=vmem_array((tokens, shard_rows),...  6.55 us
    pallas_call x1, Pallas kernels, paired_shards(): pl.pallas_call(products_kernel, out_shape=(vmem_array((chips, 2 * tokens,...  6.28 us
    ppermute x7, waiting for transfers between devices, along_chips(): lax.ppermute(array, 'vocab', [(i, (i + 2 * step) % count) for i in range(...  5.82 us
    all_to_all x1, starting transfers between devices, paired_shards(): lax.all_to_all(scaled, 'vocab', split_axis=0, concat_axis=0, tiled=True)  3.84 us
  transfers between devices with their start and end apart: 12, of which 6 were waited for; matrix products, arithmetic and copies ran while one was open for 4% of the time, Pallas kernels for 9%

profile of v5, /device:TPU:0, one launch (start us, length us, event | category | flops | bytes accessed | tf_op | source)
XLA Modules:
  0.0 75.1 jit_solution(4094983295679785095)
XLA Ops:
  0.6 1.6 %broadcast_in_dim.6 = bf16[8,64,320]{2,1,0:T(8,128)(2,1)} broadcast(bf16[64,320]{1,0:T(8,128)(2,1)} %param.8), dimensions={1,2} | broadcast | bytes 368640 | tf_op jit(solution)/shard_map/broadcast_in_dim | solution.py:249
  2.2 7.4 %all-to-all-start = ((bf16[8,64,320]{2,1,0:T(8,128)(2,1)}), bf16[8,64,320]{2,1,0:T(8,128)(2,1)S(1)}, u32[]{:S(2)}, u32[]{:S(2)}) async-start(bf16[8,64,320]{2,1,0:T(8,128)(2,1)} %broadcast_in_dim.6), calls=%async_computation | async-start | bytes 786432 | tf_op jit(solution)/shard_map/all_to_all | solution.py:51
  9.6 1.1 %reshape.37 = f32[4,16,1216]{2,1,0:T(8,128)S(1)} reshape(bf16[4,19456]{1,0:T(4,128)(2,1)} %param.10) | data formatting | bytes 466944 | tf_op jit(solution)/shard_map/reshape | solution.py:26
  10.7 1.1 %mul.11 = f32[4,608,32]{2,1,0:T(8,128)S(1)} broadcast(f32[4,608]{1,0:T(4,128)} %param.11), dimensions={0,1} | broadcast | bytes 321024 | tf_op jit(solution)/shard_map/mul | solution.py:26
  12.2 9.1 %all-to-all-done.own_ref = bf16[8,64,320]{2,1,0:T(8,128)(2,1)S(1)} async-done(((bf16[8,64,320]{2,1,0:T(8,128)(2,1)}), bf16[8,64,320]{2,1,0:T(8,128)(2,1)S(1)}, u32[]{:S(2)}, u32[]{:S(2)}) %all-to-all-start) | async-done | bytes 327712 | tf_op jit(solution)/shard_map/all_to_all | solution.py:51
  21.3 0.7 copy.12
  22.1 3.8 %all-to-all-start.1 = ((bf16[16,4,1216]{2,1,0:T(4,128)(2,1)}), bf16[16,4,1216]{2,1,0:T(4,128)(2,1)S(1)}, u32[]{:S(2)}, u32[]{:S(2)}) async-start(bf16[16,4,1216]{2,1,0:T(4,128)(2,1)} %copy.12), calls=%async_computation.1 | async-start | bytes 327680 | tf_op jit(solution)/shard_map/all_to_all | solution.py:253
  27.2 7.1 %all-to-all-done.1 = bf16[16,4,1216]{2,1,0:T(4,128)(2,1)S(1)} async-done(((bf16[16,4,1216]{2,1,0:T(4,128)(2,1)}), bf16[16,4,1216]{2,1,0:T(4,128)(2,1)S(1)}, u32[]{:S(2)}, u32[]{:S(2)}) %all-to-all-start.1) | async-done | bytes 155680 | tf_op jit(solution)/shard_map/all_to_all | solution.py:253
  34.4 6.6 %logits.1.logits_ref = f32[64,1216]{1,0:T(8,128)S(1)} custom-call(s32[1]{0:T(128)} %bitcast.place_ref, bf16[8,64,320]{2,1,0:T(8,128)(2,1)S(1)} %all-to-all-done.own_ref, bf16[8,64,320]{2,1,0:T(8,128)(2,1)S(1)} %collective-permute-done.other_ref, bf16[1216,5120]{1,0:T(8,128)(2,1)} %head_ref.3), custom_call_target="tpu_custom_call" | custom-call | flops 796917760 | bytes 12451840 | tf_op jit(solution)/shard_map/logits/pallas_call | solution.py:268
  41.0 1.2 %softmax.1 = (bf16[192,1216]{1,0:T(8,128)(2,1)S(1)}, f32[16,8,128]{2,1,0:T(8,128)}) custom-call(f32[64,1216]{1,0:T(8,128)S(1)} %logits.1.logits_ref, bf16[64,1216]{1,0:T(8,128)(2,1)S(1)} %reshape.34.arrived_ref, bf16[64,64]{1,0:T(8,128)(2,1)S(1)} %get-tuple-element.15.owner_ref, f32[64,128]{1,0:T(8,128)S(1)} %get-tuple-element.16.tokens_ref), custom_call_target="tpu_custom_call" | custom-call | tf_op jit(solution)/shard_map/softmax/pallas_call | solution.py:281
  42.2 0.8 %copy-done = bf16[192,1216]{1,0:T(8,128)(2,1)} copy-done((bf16[192,1216]{1,0:T(8,128)(2,1)}, bf16[192,1216]{1,0:T(8,128)(2,1)S(1)}, u32[]{:S(2)}) %copy-start) | copy-done | bytes 466968
  42.9 3.5 %all-to-all-start.2 = ((f32[16,8,128]{2,1,0:T(8,128)}), f32[16,8,128]{2,1,0:T(8,128)S(1)}, u32[]{:S(2)}, u32[]{:S(2)}) async-start(f32[16,8,128]{2,1,0:T(8,128)} %get-tuple-element.17.own_ref), calls=%async_computation.2 | async-start | bytes 131072 | tf_op jit(solution)/shard_map/all_to_all | solution.py:293
  46.4 1.0 %copy-done.1 = bf16[192,1216]{1,0:T(8,128)(2,1)S(1)} copy-done((bf16[192,1216]{1,0:T(8,128)(2,1)S(1)}, bf16[192,1216]{1,0:T(8,128)(2,1)}, u32[]{:S(2)}) %copy-start.1) | copy-done | bytes 466968
  47.5 6.3 %products.1 = (f32[8,128,640]{2,1,0:T(8,128)S(1)}, bf16[8,64,640]{2,1,0:T(8,128)(2,1)S(1)}) custom-call(s32[1]{0:T(128)} %bitcast.place_ref, bf16[192,1216]{1,0:T(8,128)(2,1)S(1)} %copy-done.1, bf16[1216,5120]{1,0:T(8,128)(2,1)} %head_ref.3), custom_call_target="tpu_custom_call" | custom-call | flops 2390753280 | bytes 12451840 | tf_op jit(solution)/shard_map/products/pallas_call | solution.py:295
  53.8 1.8 %combine.1 = (f32[8,64,320]{2,1,0:T(8,128)S(1)}, bf16[8,64,320]{2,1,0:T(8,128)(2,1)S(1)}, f32[1,1]{1,0:T(1,128)}) custom-call(s32[1]{0:T(128)} %bitcast.place_ref, f32[16,8,128]{2,1,0:T(8,128)S(1)} %all-to-all-done.2.stats_ref, f32[16,8,128]{2,1,0:T(8,128)} %get-tuple-element.17.own_ref, f32[64,128]{1,0:T(8,128)S(1)} %get-tuple-element.16.tokens_ref, ...), custom_call_target="tpu_custom_call" | custom-call | tf_op jit(solution)/shard_map/combine/pallas_call | solution.py:311
  55.9 1.4 %collective-permute-done.1 = bf16[8,64,320]{2,1,0:T(8,128)(2,1)S(1)} collective-permute-done((bf16[8,64,320]{2,1,0:T(8,128)(2,1)S(1)}, bf16[8,64,320]{2,1,0:T(8,128)(2,1)S(1)}, u32[]{:S(2)}, u32[]{:S(2)}) %collective-permute-start.1) | collective-permute-done | bytes 327712 | tf_op jit(solution)/shard_map/ppermute | solution.py:45
  57.5 4.6 %collective-permute-start.8 = (bf16[64,320]{1,0:T(8,128)(2,1)S(1)}, bf16[64,320]{1,0:T(8,128)(2,1)S(1)}, u32[]{:S(2)}, u32[]{:S(2)}) collective-permute-start(bf16[64,320]{1,0:T(8,128)(2,1)S(1)} %get-tuple-element.26), channel_id=1, source_target_pairs={{0,14},{1,15},{2,0},{3,1},{4,2},{5,3},{6,4},{7,5},{8,6},{9,7},{10,... | collective-permute-start | bytes 122888 | tf_op jit(solution)/shard_map/ppermute | solution.py:58
  62.7 2.9 %collective-permute-start.5 = (bf16[64,320]{1,0:T(8,128)(2,1)S(1)}, bf16[64,320]{1,0:T(8,128)(2,1)S(1)}, u32[]{:S(2)}, u32[]{:S(2)}) collective-permute-start(bf16[64,320]{1,0:T(8,128)(2,1)S(1)} %get-tuple-element.29), channel_id=1, source_target_pairs={{0,8},{1,9},{2,10},{3,11},{4,12},{5,13},{6,14},{7,15},{8,0},{9,1},... | collective-permute-start | bytes 122888 | tf_op jit(solution)/shard_map/ppermute | solution.py:58
  65.6 2.0 %collective-permute-start.3 = (bf16[64,320]{1,0:T(8,128)(2,1)S(1)}, bf16[64,320]{1,0:T(8,128)(2,1)S(1)}, u32[]{:S(2)}, u32[]{:S(2)}) collective-permute-start(bf16[64,320]{1,0:T(8,128)(2,1)S(1)} %get-tuple-element.31), channel_id=1, source_target_pairs={{0,4},{1,5},{2,6},{3,7},{4,8},{5,9},{6,10},{7,11},{8,12},{9,13},{1... | collective-permute-start | bytes 122888 | tf_op jit(solution)/shard_map/ppermute | solution.py:58
  67.6 1.0 %collective-permute-start.2 = (bf16[64,320]{1,0:T(8,128)(2,1)S(1)}, bf16[64,320]{1,0:T(8,128)(2,1)S(1)}, u32[]{:S(2)}, u32[]{:S(2)}) collective-permute-start(bf16[64,320]{1,0:T(8,128)(2,1)S(1)} %get-tuple-element.32), channel_id=1, source_target_pairs={{0,2},{1,3},{2,4},{3,5},{4,6},{5,7},{6,8},{7,9},{8,10},{9,11},{10,... | collective-permute-start | bytes 122888 | tf_op jit(solution)/shard_map/ppermute | solution.py:58
  68.6 0.9 %collective-permute-done.5.refs_3_ = bf16[64,320]{1,0:T(8,128)(2,1)S(1)} collective-permute-done((bf16[64,320]{1,0:T(8,128)(2,1)S(1)}, bf16[64,320]{1,0:T(8,128)(2,1)S(1)}, u32[]{:S(2)}, u32[]{:S(2)}) %collective-permute-start.5) | collective-permute-done | bytes 40992 | tf_op jit(solution)/shard_map/ppermute | solution.py:58
  69.5 4.2 %collective-permute-done.4.refs_2_ = bf16[64,320]{1,0:T(8,128)(2,1)S(1)} collective-permute-done((bf16[64,320]{1,0:T(8,128)(2,1)S(1)}, bf16[64,320]{1,0:T(8,128)(2,1)S(1)}, u32[]{:S(2)}, u32[]{:S(2)}) %collective-permute-start.4) | collective-permute-done | bytes 40992 | tf_op jit(solution)/shard_map/ppermute | solution.py:58
  73.7 0.7 collective-permute-done.2.refs_0_
  74.4 0.7 total.1
  (26 shorter events, 2.1 us)
Async XLA Ops:
  2.2 24.4 %copy-start.2 = (s32[2]{0:T(128)S(1)}, s32[2]{0:T(128)}, u32[]{:S(2)}) copy-start(s32[2]{0:T(128)} %lengths_ref.1) | copy-start | bytes 28
  2.2 24.4 %copy-start.3 = (s32[64]{0:T(128)S(1)}, s32[64]{0:T(128)}, u32[]{:S(2)}) copy-start(s32[64]{0:T(128)} %param.12) | copy-start | bytes 772
  2.2 24.4 %copy-start.4 = (s32[64]{0:T(128)S(1)}, s32[64]{0:T(128)}, u32[]{:S(2)}) copy-start(s32[64]{0:T(128)} %param.14) | copy-start | bytes 772
  2.2 19.1 %all-to-all-start = ((bf16[8,64,320]{2,1,0:T(8,128)(2,1)}), bf16[8,64,320]{2,1,0:T(8,128)(2,1)S(1)}, u32[]{:S(2)}, u32[]{:S(2)}) async-start(bf16[8,64,320]{2,1,0:T(8,128)(2,1)} %broadcast_in_dim.6), calls=%async_computation | async-start | bytes 786432 | tf_op jit(solution)/shard_map/all_to_all | solution.py:51
  21.3 13.1 %collective-permute-start = (bf16[8,64,320]{2,1,0:T(8,128)(2,1)S(1)}, bf16[8,64,320]{2,1,0:T(8,128)(2,1)S(1)}, u32[]{:S(2)}, u32[]{:S(2)}) collective-permute-start(bf16[8,64,320]{2,1,0:T(8,128)(2,1)S(1)} %all-to-all-done.own_ref), channel_id=1, source_target_pairs={{0,1},{1,0},{2,3},{3,2},{4,5},{5,4},{6,7},{7,6},{8,9},{9,8},{10,11... | collective-permute-start | bytes 983048 | tf_op jit(solution)/shard_map/ppermute | solution.py:45
  22.1 12.3 %all-to-all-start.1 = ((bf16[16,4,1216]{2,1,0:T(4,128)(2,1)}), bf16[16,4,1216]{2,1,0:T(4,128)(2,1)S(1)}, u32[]{:S(2)}, u32[]{:S(2)}) async-start(bf16[16,4,1216]{2,1,0:T(4,128)(2,1)} %copy.12), calls=%async_computation.1 | async-start | bytes 327680 | tf_op jit(solution)/shard_map/all_to_all | solution.py:253
  42.1 0.8 %copy-start = (bf16[192,1216]{1,0:T(8,128)(2,1)}, bf16[192,1216]{1,0:T(8,128)(2,1)S(1)}, u32[]{:S(2)}) copy-start(bf16[192,1216]{1,0:T(8,128)(2,1)S(1)} %get-tuple-element.18.rows_ref) | copy-start | bytes 1400836
  42.9 10.8 %all-to-all-start.2 = ((f32[16,8,128]{2,1,0:T(8,128)}), f32[16,8,128]{2,1,0:T(8,128)S(1)}, u32[]{:S(2)}, u32[]{:S(2)}) async-start(f32[16,8,128]{2,1,0:T(8,128)} %get-tuple-element.17.own_ref), calls=%async_computation.2 | async-start | bytes 131072 | tf_op jit(solution)/shard_map/all_to_all | solution.py:293
  46.4 1.0 %copy-start.1 = (bf16[192,1216]{1,0:T(8,128)(2,1)S(1)}, bf16[192,1216]{1,0:T(8,128)(2,1)}, u32[]{:S(2)}) copy-start(bf16[192,1216]{1,0:T(8,128)(2,1)} %copy-done) | copy-start | bytes 1400836
  55.6 1.7 %collective-permute-start.1 = (bf16[8,64,320]{2,1,0:T(8,128)(2,1)S(1)}, bf16[8,64,320]{2,1,0:T(8,128)(2,1)S(1)}, u32[]{:S(2)}, u32[]{:S(2)}) collective-permute-start(bf16[8,64,320]{2,1,0:T(8,128)(2,1)S(1)} %get-tuple-element.22), channel_id=1, source_target_pairs={{0,1},{1,0},{2,3},{3,2},{4,5},{5,4},{6,7},{7,6},{8,9},{9,8},{10,11... | collective-permute-start | bytes 983048 | tf_op jit(solution)/shard_map/ppermute | solution.py:45
  57.5 8.1 %collective-permute-start.8 = (bf16[64,320]{1,0:T(8,128)(2,1)S(1)}, bf16[64,320]{1,0:T(8,128)(2,1)S(1)}, u32[]{:S(2)}, u32[]{:S(2)}) collective-permute-start(bf16[64,320]{1,0:T(8,128)(2,1)S(1)} %get-tuple-element.26), channel_id=1, source_target_pairs={{0,14},{1,15},{2,0},{3,1},{4,2},{5,3},{6,4},{7,5},{8,6},{9,7},{10,... | collective-permute-start | bytes 122888 | tf_op jit(solution)/shard_map/ppermute | solution.py:58
  62.1 5.5 %collective-permute-start.7 = (bf16[64,320]{1,0:T(8,128)(2,1)S(1)}, bf16[64,320]{1,0:T(8,128)(2,1)S(1)}, u32[]{:S(2)}, u32[]{:S(2)}) collective-permute-start(bf16[64,320]{1,0:T(8,128)(2,1)S(1)} %get-tuple-element.27), channel_id=1, source_target_pairs={{0,12},{1,13},{2,14},{3,15},{4,0},{5,1},{6,2},{7,3},{8,4},{9,5},{1... | collective-permute-start | bytes 122888 | tf_op jit(solution)/shard_map/ppermute | solution.py:58
  62.7 5.9 %collective-permute-start.6 = (bf16[64,320]{1,0:T(8,128)(2,1)S(1)}, bf16[64,320]{1,0:T(8,128)(2,1)S(1)}, u32[]{:S(2)}, u32[]{:S(2)}) collective-permute-start(bf16[64,320]{1,0:T(8,128)(2,1)S(1)} %get-tuple-element.28), channel_id=1, source_target_pairs={{0,10},{1,11},{2,12},{3,13},{4,14},{5,15},{6,0},{7,1},{8,2},{9,3},... | collective-permute-start | bytes 122888 | tf_op jit(solution)/shard_map/ppermute | solution.py:58
  62.7 6.8 %collective-permute-start.5 = (bf16[64,320]{1,0:T(8,128)(2,1)S(1)}, bf16[64,320]{1,0:T(8,128)(2,1)S(1)}, u32[]{:S(2)}, u32[]{:S(2)}) collective-permute-start(bf16[64,320]{1,0:T(8,128)(2,1)S(1)} %get-tuple-element.29), channel_id=1, source_target_pairs={{0,8},{1,9},{2,10},{3,11},{4,12},{5,13},{6,14},{7,15},{8,0},{9,1},... | collective-permute-start | bytes 122888 | tf_op jit(solution)/shard_map/ppermute | solution.py:58
  65.6 8.0 %collective-permute-start.4 = (bf16[64,320]{1,0:T(8,128)(2,1)S(1)}, bf16[64,320]{1,0:T(8,128)(2,1)S(1)}, u32[]{:S(2)}, u32[]{:S(2)}) collective-permute-start(bf16[64,320]{1,0:T(8,128)(2,1)S(1)} %get-tuple-element.30), channel_id=1, source_target_pairs={{0,6},{1,7},{2,8},{3,9},{4,10},{5,11},{6,12},{7,13},{8,14},{9,15},... | collective-permute-start | bytes 122888 | tf_op jit(solution)/shard_map/ppermute | solution.py:58
  65.6 8.0 %collective-permute-start.3 = (bf16[64,320]{1,0:T(8,128)(2,1)S(1)}, bf16[64,320]{1,0:T(8,128)(2,1)S(1)}, u32[]{:S(2)}, u32[]{:S(2)}) collective-permute-start(bf16[64,320]{1,0:T(8,128)(2,1)S(1)} %get-tuple-element.31), channel_id=1, source_target_pairs={{0,4},{1,5},{2,6},{3,7},{4,8},{5,9},{6,10},{7,11},{8,12},{9,13},{1... | collective-permute-start | bytes 122888 | tf_op jit(solution)/shard_map/ppermute | solution.py:58
  67.6 6.8 %collective-permute-start.2 = (bf16[64,320]{1,0:T(8,128)(2,1)S(1)}, bf16[64,320]{1,0:T(8,128)(2,1)S(1)}, u32[]{:S(2)}, u32[]{:S(2)}) collective-permute-start(bf16[64,320]{1,0:T(8,128)(2,1)S(1)} %get-tuple-element.32), channel_id=1, source_target_pairs={{0,2},{1,3},{2,4},{3,5},{4,6},{5,7},{6,8},{7,9},{8,10},{9,11},{10,... | collective-permute-start | bytes 122888 | tf_op jit(solution)/shard_map/ppermute | solution.py:58

commit v6 on v5

--- a/solution.py
+++ b/solution.py
@@ -70,11 +70,117 @@
     return pltpu.with_memory_space_constraint(array, pltpu.HBM)
 
 
+def hbm_array(shape, dtype):
+    return pltpu.HBM(shape, dtype)
+
+
+def low_lanes(shape):
+    return lax.broadcasted_iota(jnp.int32, shape, len(shape) - 1) < LANES // 2
+
+
+def low_rows(shape, count):
+    return lax.broadcasted_iota(jnp.int32, shape, 0) < count
+
+
+def turned(array):
+    return pltpu.roll(array, LANES // 2, 1)
+
+
+def packed_half(tiles):
+    rows = tiles[2].shape[0] // 2
+    upper, lower = tiles[2][:rows], tiles[2][rows:]
+    rest = jnp.where(low_lanes(upper.shape), upper, turned(lower))
+    return jnp.concatenate([tiles[0], tiles[1], rest], axis=0)
+
+
+def unpacked_half(packed, tokens):
+    rest = packed[2 * tokens :]
+    return [packed[:tokens], packed[tokens : 2 * tokens], jnp.concatenate([rest, turned(rest)])]
+
+
+def joined(first, second):
+    low = low_lanes(first[0].shape)
+    turns = [turned(tile) for tile in second]
+    return [
+        first[0],
+        first[1],
+        jnp.where(low, first[2], turns[0]),
+        jnp.where(low, turns[0], turns[1]),
+        jnp.where(low, turns[1], turns[2]),
+    ]
+
+
+def parted(tiles):
+    low = low_lanes(tiles[0].shape)
+    turns = [turned(tile) for tile in tiles[2:]]
+    return tiles[:3], [
+        jnp.where(low, turns[0], turns[1]),
+        jnp.where(low, turns[1], turns[2]),
+        turns[2],
+    ]
+
+
 def column_of(row):
     size = row.shape[1]
     down = lax.broadcasted_iota(jnp.int32, (size, size), 0)
     along = lax.broadcasted_iota(jnp.int32, (size, size), 1)
     return jnp.sum(jnp.where(down == along, row, jnp.zeros_like(row)), axis=1, keepdims=True)
+
+
+def pack_kernel(hidden_ref, values_ref, scales_ref, packed_ref, wide_ref):
+    chips = packed_ref.shape[0]
+    tokens, half = hidden_ref.shape
+    slots, entries = values_ref.shape
+    pair = entries // chips
+    shard = pair // 2
+    blocks = pair // BLOCK
+    scales = jnp.concatenate([scales_ref[...]] * 2, axis=0)
+    stacked = jnp.concatenate(
+        [scales[:, blocks * chip : blocks * (chip + 1)] for chip in range(chips)], axis=0
+    )
+    block = lax.broadcasted_iota(jnp.int32, (blocks, pair), 0)
+    entry = lax.broadcasted_iota(jnp.int32, (blocks, pair), 1)
+    inside = (entry >= block * BLOCK) & (entry < block * BLOCK + BLOCK)
+    spread = jnp.dot(
+        stacked.astype(jnp.bfloat16),
+        inside.astype(jnp.bfloat16),
+        preferred_element_type=jnp.float32,
+    )
+    values = values_ref[...].astype(jnp.float32)
+    values = jnp.concatenate([values, values], axis=0)
+    for chip in range(chips):
+        wide_ref[:, pair * chip : pair * (chip + 1)] = (
+            values[:, pair * chip : pair * (chip + 1)]
+            * spread[2 * slots * chip : 2 * slots * (chip + 1)]
+        )
+    wide_ref[:, entries:] = jnp.zeros((2 * slots, LANES), jnp.float32)
+
+    hidden = hidden_ref[...].astype(jnp.float32)
+    hidden = jnp.concatenate([hidden, jnp.zeros((tokens, LANES // 2), jnp.float32)], axis=1)
+    hidden = packed_half([hidden[:, LANES * i : LANES * (i + 1)] for i in range(3)])
+    hidden = hidden.astype(jnp.bfloat16)
+    hidden_rows = hidden.shape[0]
+    upper = low_rows((2 * slots, LANES), slots)
+    low = low_lanes((2 * slots, LANES))
+    tile_pairs = (shard + LANES // 2) // LANES // 2
+    for chip in range(chips):
+        rows = []
+        for core in range(2):
+            start = pair * chip + (shard - LANES // 2) * core
+            tiles = [
+                wide_ref[:, start + LANES * i : start + LANES * (i + 1)]
+                for i in range(2 * tile_pairs + core)
+            ]
+            if core == 1:
+                tiles = [turned(tile) for tile in tiles]
+                tiles = [
+                    jnp.where(low, tiles[i], tiles[i + 1]) for i in range(2 * tile_pairs)
+                ]
+            rows += [
+                jnp.where(upper, tiles[2 * i], tiles[2 * i + 1]) for i in range(tile_pairs)
+            ]
+        packed_ref[chip, :hidden_rows] = hidden
+        packed_ref[chip, hidden_rows:] = jnp.concatenate(rows, axis=0).astype(jnp.bfloat16)
 
 
 def prepare_kernel(
@@ -114,30 +220,65 @@
     return copies
 
 
-def logits_kernel(place_ref, own_ref, other_ref, head_ref, logits_ref, held_ref, sems):
+def logits_kernel(
+    place_ref,
+    own_ref,
+    other_ref,
+    owner_ref,
+    tokens_ref,
+    head_ref,
+    rows_ref,
+    stats_ref,
+    held_ref,
+    made_ref,
+    hidden_ref,
+    arrived_ref,
+    sems,
+    made_sem,
+):
     copies = head_copies(head_ref, held_ref, sems, 0)
     for copy in copies:
         copy.start()
     core = place_ref[0] % 2
-    logits = jnp.zeros(logits_ref.shape, jnp.float32)
+    chips, tokens, width = hidden_ref.shape
+    shard_rows = head_ref.shape[0]
+    hidden_rows = tokens * width // 2 // LANES
+    slots = tokens // (2 * chips)
+    upper = low_rows((2 * slots, LANES), slots)
+    for chip in range(chips):
+        own, other = own_ref[chip].astype(jnp.float32), other_ref[chip].astype(jnp.float32)
+        first = jnp.where(core == 0, own, other)
+        second = jnp.where(core == 0, other, own)
+        tiles = joined(
+            unpacked_half(first[:hidden_rows], tokens),
+            unpacked_half(second[:hidden_rows], tokens),
+        )
+        hidden_ref[chip] = jnp.concatenate(tiles, axis=1).astype(jnp.bfloat16)
+        first, second = first[hidden_rows:], second[hidden_rows:]
+        share = first.shape[0] // 2
+        first = jnp.where(core == 0, first[:share], first[share:])
+        second = jnp.where(core == 0, second[:share], second[share:])
+        tiles = []
+        for row in range(0, share, 2 * slots):
+            one, two = first[row : row + 2 * slots], second[row : row + 2 * slots]
+            tiles.append(jnp.where(upper, one, pltpu.roll(two, slots, 0)))
+            tiles.append(jnp.where(upper, pltpu.roll(one, slots, 0), two))
+        arrived_ref[2 * slots * chip : 2 * slots * (chip + 1)] = jnp.concatenate(tiles, axis=1)
+    teacher = jnp.dot(
+        owner_ref[...],
+        arrived_ref[:, :shard_rows].astype(jnp.bfloat16),
+        preferred_element_type=jnp.float32,
+    )
+    logits = jnp.zeros((tokens, shard_rows), jnp.float32)
     for chip, copy in enumerate(copies):
-        own, other = own_ref[chip], other_ref[chip]
-        block = jnp.where(
-            core == 0,
-            jnp.concatenate([own, other], axis=1),
-            jnp.concatenate([other, own], axis=1),
-        )
         copy.wait()
         logits += lax.dot_general(
-            block, held_ref[chip], (((1,), (1,)), ((), ())), preferred_element_type=jnp.float32
+            hidden_ref[chip],
+            held_ref[chip],
+            (((1,), (1,)), ((), ())),
+            preferred_element_type=jnp.float32,
         )
-    logits_ref[...] = logits
-
-
-def softmax_kernel(logits_ref, arrived_ref, owner_ref, tokens_ref, rows_ref, stats_ref):
-    tokens, shard_rows = logits_ref.shape
-    logits = logits_ref[...]
-    teacher = jnp.dot(owner_ref[...], arrived_ref[...], preferred_element_type=jnp.float32)
+
     top = jnp.max(logits, axis=1, keepdims=True)
     teacher_top = jnp.max(teacher, axis=1, keepdims=True)
     off = logits - top
@@ -151,9 +292,11 @@
     entry = lax.broadcasted_iota(jnp.int32, (tokens, shard_rows), 1)
     hit = entry == tokens_ref[:, :1].astype(jnp.int32)
     target = jnp.sum(jnp.where(hit, logits, 0.0), axis=1, keepdims=True)
-    rows_ref[:tokens] = (exps * (gap - centre)).astype(jnp.bfloat16)
-    rows_ref[tokens : 2 * tokens] = exps.astype(jnp.bfloat16)
-    rows_ref[2 * tokens :] = hit.astype(jnp.bfloat16)
+    made_ref[:tokens] = (exps * (gap - centre)).astype(jnp.bfloat16)
+    made_ref[tokens : 2 * tokens] = exps.astype(jnp.bfloat16)
+    made_ref[2 * tokens :] = hit.astype(jnp.bfloat16)
+    out = pltpu.make_async_copy(made_ref, rows_ref, made_sem)
+    out.start()
 
     lane = lax.broadcasted_iota(jnp.int32, (tokens, LANES), 1)
     table = jnp.zeros((tokens, LANES), jnp.float32)
@@ -163,16 +306,22 @@
         table = jnp.where(lane == place, column, table)
     stats = jnp.concatenate([table, jnp.zeros((stats_ref.shape[2] - tokens, LANES), jnp.float32)])
     stats_ref[...] = jnp.broadcast_to(stats.T[None, :STATS], stats_ref.shape)
-
-
-def products_kernel(place_ref, rows_ref, head_ref, terms_ref, picks_ref, held_ref, sems):
+    out.wait()
+
+
+def products_kernel(
+    place_ref, rows_ref, head_ref, terms_ref, picks_ref, held_ref, made_ref, sems, made_sem
+):
+    into = pltpu.make_async_copy(rows_ref, made_ref, made_sem)
+    into.start()
     copies = head_copies(head_ref, held_ref, sems, place_ref[0] // 2)
     for copy in copies:
         copy.start()
+    into.wait()
     sums_rows = terms_ref.shape[1]
     for step, copy in enumerate(copies):
         copy.wait()
-        products = jnp.dot(rows_ref[...], held_ref[step], preferred_element_type=jnp.float32)
+        products = jnp.dot(made_ref[...], held_ref[step], preferred_element_type=jnp.float32)
         terms_ref[step] = products[:sums_rows]
         picks_ref[step] = products[sums_rows:].astype(jnp.bfloat16)
 
@@ -183,7 +332,6 @@
     core = place_ref[0] % 2
     chips, _, width = terms_ref.shape
     tokens = tokens_ref.shape[0]
-    half = width // 2
     tops, sums, teacher_tops, teacher_sums, crosses, targets = [
         stats_ref[:, i, :tokens] for i in range(6)
     ]
@@ -214,16 +362,19 @@
             factor * (terms_ref[step, :tokens] + level * terms_ref[step, tokens:])
             - weight * picks_ref[step].astype(jnp.float32)
         )
-        first, second = block[:, :half], block[:, half:]
+        first, second = parted([block[:, i : i + LANES] for i in range(0, width, LANES)])
+        first, second = packed_half(first), packed_half(second)
         keep_ref[step] = jnp.where(core == 0, first, second)
         give_ref[step] = jnp.where(core == 0, second, first).astype(jnp.bfloat16)
 
 
 def sum_kernel(own_ref, *refs):
+    tokens, half = refs[-1].shape
     total = own_ref[...]
     for share_ref in refs[:-1]:
         total += share_ref[...].astype(jnp.float32)
-    refs[-1][...] = total.astype(refs[-1].dtype)
+    tiles = jnp.concatenate(unpacked_half(total, tokens), axis=1)
+    refs[-1][...] = tiles[:, :half].astype(refs[-1].dtype)
 
 
 def paired_shards(
@@ -241,17 +392,25 @@
     hbm = pl.BlockSpec(memory_space=pl.ANY)
     params = pltpu.CompilerParams(vmem_limit_bytes=VMEM_LIMIT)
     head = in_hbm(head)
-    head_scratch = [
-        pltpu.VMEM((chips, shard_rows, width), head.dtype),
-        pltpu.SemaphoreType.DMA((chips,)),
-    ]
-
-    gathered = across_chips(jnp.broadcast_to(hidden_states[None], (chips, tokens, half)))
-    scaled = scaled_teacher(teacher_values, teacher_scales, count, shard_rows)
-    gathered, scaled = lax.optimization_barrier((gathered, scaled))
+    head_scratch = pltpu.VMEM((chips, shard_rows, width), head.dtype)
+    head_sems = pltpu.SemaphoreType.DMA((chips,))
+    rows_scratch = pltpu.VMEM((3 * tokens, shard_rows), jnp.bfloat16)
+    rows_sem = pltpu.SemaphoreType.DMA
+    slots, entries = teacher_values.shape
+    hidden_rows = tokens * half // LANES
+    teacher_rows = 2 * slots * (shard_rows + LANES // 2) // LANES
+
+    packed = pl.pallas_call(
+        pack_kernel,
+        out_shape=jax.ShapeDtypeStruct((chips, hidden_rows + teacher_rows, LANES), jnp.bfloat16),
+        in_specs=[vmem] * 3,
+        out_specs=vmem,
+        scratch_shapes=[pltpu.VMEM((2 * slots, entries + LANES), jnp.float32)],
+        compiler_params=params,
+        name="pack",
+    )(hidden_states, teacher_values, teacher_scales)
+    gathered = across_chips(packed)
     other = swap_cores(gathered)
-    arrived = lax.all_to_all(scaled, "vocab", split_axis=0, concat_axis=0, tiled=True)
-    arrived = arrived.reshape(tokens, shard_rows)
 
     owner, table = pl.pallas_call(
         functools.partial(prepare_kernel, shard_rows=shard_rows),
@@ -265,30 +424,28 @@
         name="prepare",
     )(place, lengths, loss_scale, token_ids[None, :], row_map[None, :])
 
-    logits = pl.pallas_call(
+    rows, stats = pl.pallas_call(
         logits_kernel,
-        out_shape=vmem_array((tokens, shard_rows), jnp.float32),
-        in_specs=[smem] + [vmem] * 2 + [hbm],
-        out_specs=vmem,
-        scratch_shapes=head_scratch,
+        out_shape=(
+            hbm_array((3 * tokens, shard_rows), jnp.bfloat16),
+            jax.ShapeDtypeStruct((count, STATS, pl.cdiv(tokens, LANES) * LANES), jnp.float32),
+        ),
+        in_specs=[smem] + [vmem] * 4 + [hbm],
+        out_specs=[hbm, vmem],
+        scratch_shapes=[
+            head_scratch,
+            rows_scratch,
+            pltpu.VMEM((chips, tokens, width), jnp.bfloat16),
+            pltpu.VMEM((tokens, shard_rows + LANES // 2), jnp.float32),
+            head_sems,
+            rows_sem,
+        ],
         compiler_params=params,
         cost_estimate=pl.CostEstimate(
             flops=2 * tokens * head.size, bytes_accessed=2 * head.size, transcendentals=0
         ),
         name="logits",
-    )(place, gathered, other, head)
-
-    rows, stats = pl.pallas_call(
-        softmax_kernel,
-        out_shape=(
-            jax.ShapeDtypeStruct((3 * tokens, shard_rows), jnp.bfloat16),
-            jax.ShapeDtypeStruct((count, STATS, pl.cdiv(tokens, LANES) * LANES), jnp.float32),
-        ),
-        in_specs=[vmem] * 4,
-        out_specs=[vmem] * 2,
-        compiler_params=params,
-        name="softmax",
-    )(in_vmem(logits), arrived, in_vmem(owner), in_vmem(table))
+    )(place, gathered, other, in_vmem(owner), in_vmem(table), head)
 
     all_stats = lax.all_to_all(stats, "vocab", split_axis=0, concat_axis=0, tiled=True)
 
@@ -298,21 +455,21 @@
             vmem_array((chips, 2 * tokens, width), jnp.float32),
             vmem_array((chips, tokens, width), jnp.bfloat16),
         ),
-        in_specs=[smem, vmem, hbm],
+        in_specs=[smem, hbm, hbm],
         out_specs=[vmem] * 2,
-        scratch_shapes=head_scratch,
+        scratch_shapes=[head_scratch, rows_scratch, head_sems, rows_sem],
         compiler_params=params,
         cost_estimate=pl.CostEstimate(
             flops=6 * tokens * head.size, bytes_accessed=2 * head.size, transcendentals=0
         ),
         name="products",
-    )(place, rows, head)
+    )(place, in_hbm(rows), head)
 
     keep, give, loss = pl.pallas_call(
         combine_kernel,
         out_shape=(
-            vmem_array((chips, tokens, half), jnp.float32),
-            vmem_array((chips, tokens, half), jnp.bfloat16),
+            vmem_array((chips, hidden_rows, LANES), jnp.float32),
+            vmem_array((chips, hidden_rows, LANES), jnp.bfloat16),
             jax.ShapeDtypeStruct((1, 1), jnp.float32),
         ),
         in_specs=[smem] + [vmem] * 5,
@@ -329,7 +486,8 @@
     )
 
     sums = keep + swap_cores(give).astype(jnp.float32)
-    shares = [along_chips(sums[step].astype(jnp.bfloat16), step) for step in range(1, chips)]
+    steps = range(chips - 1, 0, -1)
+    shares = [along_chips(sums[step].astype(jnp.bfloat16), step) for step in steps]
     total = pl.pallas_call(
         sum_kernel,
         out_shape=jax.ShapeDtypeStruct((tokens, half), jnp.bfloat16),
@@ -424,11 +582,17 @@
 
 
 def any_shards(*arrays):
+    hidden_states, head, teacher_values = arrays[:3]
     count = lax.axis_size("vocab")
-    pair_width = 2 * arrays[0].shape[1]
-    if count > 2 and count & (count - 1) == 0 and pair_width % LANES == 0:
-        return paired_shards(*arrays)
-    return shards(*arrays)
+    fits = (
+        count % 2 == 0
+        and hidden_states.shape[1] == 5 * LANES // 2
+        and hidden_states.shape[0] % 32 == 0
+        and head.shape[0] % LANES == LANES // 2
+        and (head.shape[0] + LANES // 2) // LANES % 2 == 0
+        and teacher_values.shape[0] == 4
+    )
+    return paired_shards(*arrays) if fits else shards(*arrays)
 
 
 def solution(mesh):

time: 75.7 us -> 69.1 us (0.913)
  blocking collectives: 0 us -> 20.9 us
  waiting for transfers between devices: 23.5 us -> 3.81 us
  starting transfers between devices: 26.1 us -> 16.7 us
  Pallas kernels: 17.1 us -> 21.4 us
  local copies, waits for them, and re-layouts: 6.74 us -> 4.39 us
    all_to_all x0 -> x1, blocking collectives: none -> 20.9 us  [across_chips(): lax.all_to_all(blocks, 'vocab', split_axis=0, concat_axis=0, axis_index_g...]
    all_to_all x2 -> x0, waiting for transfers between devices: 16.3 us -> none  [the longest x1 9.13 us: across_chips(): lax.all_to_all(blocks, 'vocab', split_axis=0, concat_axis=0, axis_index_g...]
    all_to_all x2 -> x0, starting transfers between devices: 11.2 us -> none  [the longest x1 7.41 us: across_chips(): lax.all_to_all(blocks, 'vocab', split_axis=0, concat_axis=0, axis_index_g...]
    ppermute x7, waiting for transfers between devices: 5.82 us -> 2.54 us  [along_chips(): lax.ppermute(array, 'vocab', [(i, (i + 2 * step) % count) for i in range(...]
    pallas_call x1, Pallas kernels: 6.28 us -> 9.09 us  [paired_shards(): pl.pallas_call(products_kernel, out_shape=(vmem_array((chips, 2 * tokens,...]
    unnamed x10 -> x12, local copies, waits for them, and re-layouts: 1.83 us -> 4.37 us
    broadcast_in_dim x1 -> x0, local copies, waits for them, and re-layouts: 1.57 us -> none  [paired_shards(): jnp.broadcast_to(hidden_states[None], (chips, tokens, half))]
    ppermute x7, starting transfers between devices: 11 us -> 12.5 us  [along_chips(): lax.ppermute(array, 'vocab', [(i, (i + 2 * step) % count) for i in range(...]
  transfers between devices with their start and end apart: 12 -> 10, of which waited for: 6 -> 4; matrix products, arithmetic and copies ran while one was open for 4% -> 0% of each run, Pallas kernels for 9% -> 14%
where the time goes in v6:
time: 69.1 us; the launch traced here: 68.7 us
  Pallas kernels  21.4 us (31%)
  blocking collectives  20.9 us (30%)
  starting transfers between devices  16.7 us (24%)
  local copies, waits for them, and re-layouts  4.39 us (6%)
  waiting for transfers between devices  3.81 us (6%)
  between operations  1.39 us (2%)
    all_to_all x1, blocking collectives, across_chips(): lax.all_to_all(blocks, 'vocab', split_axis=0, concat_axis=0, axis_index_g...  20.9 us
    ppermute x7, starting transfers between devices, along_chips(): lax.ppermute(array, 'vocab', [(i, (i + 2 * step) % count) for i in range(...  12.5 us
    pallas_call x1, Pallas kernels, paired_shards(): pl.pallas_call(products_kernel, out_shape=(vmem_array((chips, 2 * tokens,...  9.09 us
    pallas_call x1, Pallas kernels, paired_shards(): pl.pallas_call(logits_kernel, out_shape=(hbm_array((3 * tokens, shard_row...  8.67 us
    unnamed x12, local copies, waits for them, and re-layouts  4.37 us
    all_to_all x1, starting transfers between devices, paired_shards(): lax.all_to_all(stats, 'vocab', split_axis=0, concat_axis=0, tiled=True)  3.82 us
    ppermute x7, waiting for transfers between devices, along_chips(): lax.ppermute(array, 'vocab', [(i, (i + 2 * step) % count) for i in range(...  2.54 us
    pallas_call x1, Pallas kernels, paired_shards(): pl.pallas_call(combine_kernel, out_shape=(vmem_array((chips, hidden_rows,...  1.85 us
  transfers between devices with their start and end apart: 10, of which 4 were waited for; matrix products, arithmetic and copies ran while one was open for 0% of the time, Pallas kernels for 14%

profile of v6, /device:TPU:0, one launch (start us, length us, event | category | flops | bytes accessed | tf_op | source)
XLA Modules:
  0.0 68.7 jit_solution(853473647401815493)
XLA Ops:
  0.6 0.9 %copy-done = bf16[4,19456]{1,0:T(4,128)(2,1)S(1)} copy-done((bf16[4,19456]{1,0:T(4,128)(2,1)S(1)}, bf16[4,19456]{1,0:T(4,128)(2,1)}, u32[]{:S(2)}) %copy-start) | copy-done | bytes 155672
  1.5 0.8 %copy-done.1 = bf16[64,320]{1,0:T(8,128)(2,1)S(1)} copy-done((bf16[64,320]{1,0:T(8,128)(2,1)S(1)}, bf16[64,320]{1,0:T(8,128)(2,1)}, u32[]{:S(2)}) %copy-start.1) | copy-done | bytes 40984
  2.3 0.7 %copy-done.2 = f32[4,608]{1,0:T(4,128)S(1)} copy-done((f32[4,608]{1,0:T(4,128)S(1)}, f32[4,608]{1,0:T(4,128)}, u32[]{:S(2)}) %copy-start.2) | copy-done | bytes 9752
  3.0 0.4 pack.1
  3.5 20.9 %all_to_all.10.own_ref = bf16[8,240,128]{2,1,0:T(8,128)(2,1)S(1)} all-to-all(bf16[8,240,128]{2,1,0:T(8,128)(2,1)S(1)} %pack.1), channel_id=1, replica_groups={{0,2,4,6,8,10,12,14},{1,3,5,7,9,11,13,15},{16,18,20,22,24,26,28,30},{17..., dimensions={0} | all-to-all | bytes 983040 | tf_op jit(solution)/shard_map/all_to_all | solution.py:51
  25.1 0.6 copy-done.3
  25.7 0.7 copy-done.4
  26.4 0.7 copy-done.5
  27.0 0.6 prepare.1
  27.7 8.7 %logits.1 = (bf16[192,1216]{1,0:T(8,128)(2,1)}, f32[16,8,128]{2,1,0:T(8,128)}) custom-call(s32[1]{0:T(128)} %bitcast.place_ref, bf16[8,240,128]{2,1,0:T(8,128)(2,1)S(1)} %all_to_all.10.own_ref, bf16[8,240,128]{2,1,0:T(8,128)(2,1)S(1)} %collective-permute-done.other_ref, bf16[64,64]{1,0:T(8,128)(2,1)S(1)} %get-tuple-element.11.owner_ref, ...), custom_call_target="tpu_custom_call" | custom-call | flops 796917760 | bytes 12451840 | tf_op jit(solution)/shard_map/logits/pallas_call | solution.py:427
  36.4 3.8 %all-to-all-start.1 = ((f32[16,8,128]{2,1,0:T(8,128)}), f32[16,8,128]{2,1,0:T(8,128)S(1)}, u32[]{:S(2)}, u32[]{:S(2)}) async-start(f32[16,8,128]{2,1,0:T(8,128)} %get-tuple-element.13.own_ref), calls=%async_computation.1 | async-start | bytes 131072 | tf_op jit(solution)/shard_map/all_to_all | solution.py:450
  40.2 9.1 %products.1 = (f32[8,128,640]{2,1,0:T(8,128)S(1)}, bf16[8,64,640]{2,1,0:T(8,128)(2,1)S(1)}) custom-call(s32[1]{0:T(128)} %bitcast.place_ref, bf16[192,1216]{1,0:T(8,128)(2,1)} %get-tuple-element.14.rows_ref, bf16[1216,5120]{1,0:T(8,128)(2,1)} %head_ref.3), custom_call_target="tpu_custom_call" | custom-call | flops 2390753280 | bytes 12451840 | tf_op jit(solution)/shard_map/products/pallas_call | solution.py:452
  49.3 1.8 %combine.1 = (f32[8,160,128]{2,1,0:T(8,128)S(1)}, bf16[8,160,128]{2,1,0:T(8,128)(2,1)S(1)}, f32[1,1]{1,0:T(1,128)}) custom-call(s32[1]{0:T(128)} %bitcast.place_ref, f32[16,8,128]{2,1,0:T(8,128)S(1)} %all-to-all-done.1.stats_ref, f32[16,8,128]{2,1,0:T(8,128)} %get-tuple-element.13.own_ref, f32[64,128]{1,0:T(8,128)S(1)} %get-tuple-element.12.tokens_ref, ...), custom_call_target="tpu_custom_call" | custom-call | tf_op jit(solution)/shard_map/combine/pallas_call | solution.py:468
  51.5 1.3 %collective-permute-done.1 = bf16[8,160,128]{2,1,0:T(8,128)(2,1)S(1)} collective-permute-done((bf16[8,160,128]{2,1,0:T(8,128)(2,1)S(1)}, bf16[8,160,128]{2,1,0:T(8,128)(2,1)S(1)}, u32[]{:S(2)}, u32[]{:S(2)}) %collective-permute-start.1) | collective-permute-done | bytes 327712 | tf_op jit(solution)/shard_map/ppermute | solution.py:45
  52.9 2.0 %collective-permute-start.8 = (bf16[160,128]{1,0:T(8,128)(2,1)S(1)}, bf16[160,128]{1,0:T(8,128)(2,1)S(1)}, u32[]{:S(2)}, u32[]{:S(2)}) collective-permute-start(bf16[160,128]{1,0:T(8,128)(2,1)S(1)} %get-tuple-element.22), channel_id=1, source_target_pairs={{0,2},{1,3},{2,4},{3,5},{4,6},{5,7},{6,8},{7,9},{8,10},{9,11},{10,... | collective-permute-start | bytes 122888 | tf_op jit(solution)/shard_map/ppermute | solution.py:58
  54.9 1.4 %collective-permute-start.7 = (bf16[160,128]{1,0:T(8,128)(2,1)S(1)}, bf16[160,128]{1,0:T(8,128)(2,1)S(1)}, u32[]{:S(2)}, u32[]{:S(2)}) collective-permute-start(bf16[160,128]{1,0:T(8,128)(2,1)S(1)} %get-tuple-element.23), channel_id=1, source_target_pairs={{0,4},{1,5},{2,6},{3,7},{4,8},{5,9},{6,10},{7,11},{8,12},{9,13},{1... | collective-permute-start | bytes 122888 | tf_op jit(solution)/shard_map/ppermute | solution.py:58
  56.3 2.4 %collective-permute-start.6 = (bf16[160,128]{1,0:T(8,128)(2,1)S(1)}, bf16[160,128]{1,0:T(8,128)(2,1)S(1)}, u32[]{:S(2)}, u32[]{:S(2)}) collective-permute-start(bf16[160,128]{1,0:T(8,128)(2,1)S(1)} %get-tuple-element.24), channel_id=1, source_target_pairs={{0,6},{1,7},{2,8},{3,9},{4,10},{5,11},{6,12},{7,13},{8,14},{9,15},... | collective-permute-start | bytes 122888 | tf_op jit(solution)/shard_map/ppermute | solution.py:58
  58.7 1.4 %collective-permute-start.5 = (bf16[160,128]{1,0:T(8,128)(2,1)S(1)}, bf16[160,128]{1,0:T(8,128)(2,1)S(1)}, u32[]{:S(2)}, u32[]{:S(2)}) collective-permute-start(bf16[160,128]{1,0:T(8,128)(2,1)S(1)} %get-tuple-element.25), channel_id=1, source_target_pairs={{0,8},{1,9},{2,10},{3,11},{4,12},{5,13},{6,14},{7,15},{8,0},{9,1},... | collective-permute-start | bytes 122888 | tf_op jit(solution)/shard_map/ppermute | solution.py:58
  60.1 2.4 %collective-permute-start.4 = (bf16[160,128]{1,0:T(8,128)(2,1)S(1)}, bf16[160,128]{1,0:T(8,128)(2,1)S(1)}, u32[]{:S(2)}, u32[]{:S(2)}) collective-permute-start(bf16[160,128]{1,0:T(8,128)(2,1)S(1)} %get-tuple-element.26), channel_id=1, source_target_pairs={{0,10},{1,11},{2,12},{3,13},{4,14},{5,15},{6,0},{7,1},{8,2},{9,3},... | collective-permute-start | bytes 122888 | tf_op jit(solution)/shard_map/ppermute | solution.py:58
  62.5 1.5 %collective-permute-start.3 = (bf16[160,128]{1,0:T(8,128)(2,1)S(1)}, bf16[160,128]{1,0:T(8,128)(2,1)S(1)}, u32[]{:S(2)}, u32[]{:S(2)}) collective-permute-start(bf16[160,128]{1,0:T(8,128)(2,1)S(1)} %get-tuple-element.27), channel_id=1, source_target_pairs={{0,12},{1,13},{2,14},{3,15},{4,0},{5,1},{6,2},{7,3},{8,4},{9,5},{1... | collective-permute-start | bytes 122888 | tf_op jit(solution)/shard_map/ppermute | solution.py:58
  64.0 1.4 %collective-permute-start.2 = (bf16[160,128]{1,0:T(8,128)(2,1)S(1)}, bf16[160,128]{1,0:T(8,128)(2,1)S(1)}, u32[]{:S(2)}, u32[]{:S(2)}) collective-permute-start(bf16[160,128]{1,0:T(8,128)(2,1)S(1)} %get-tuple-element.28), channel_id=1, source_target_pairs={{0,14},{1,15},{2,0},{3,1},{4,2},{5,3},{6,4},{7,5},{8,6},{9,7},{10,... | collective-permute-start | bytes 122888 | tf_op jit(solution)/shard_map/ppermute | solution.py:58
  65.5 1.0 %collective-permute-done.3.refs_1_ = bf16[160,128]{1,0:T(8,128)(2,1)S(1)} collective-permute-done((bf16[160,128]{1,0:T(8,128)(2,1)S(1)}, bf16[160,128]{1,0:T(8,128)(2,1)S(1)}, u32[]{:S(2)}, u32[]{:S(2)}) %collective-permute-start.3) | collective-permute-done | bytes 40992 | tf_op jit(solution)/shard_map/ppermute | solution.py:58
  66.5 1.5 %collective-permute-done.2.refs_0_ = bf16[160,128]{1,0:T(8,128)(2,1)S(1)} collective-permute-done((bf16[160,128]{1,0:T(8,128)(2,1)S(1)}, bf16[160,128]{1,0:T(8,128)(2,1)S(1)}, u32[]{:S(2)}, u32[]{:S(2)}) %collective-permute-start.2) | collective-permute-done | bytes 40992 | tf_op jit(solution)/shard_map/ppermute | solution.py:58
  68.0 0.7 %total.1 = bf16[64,320]{1,0:T(8,128)(2,1)} custom-call(f32[160,128]{1,0:T(8,128)S(1)} %slice_bitcast_fusion.own_ref, bf16[160,128]{1,0:T(8,128)(2,1)S(1)} %collective-permute-done.2.refs_0_, bf16[160,128]{1,0:T(8,128)(2,1)S(1)} %collective-permute-done.3.refs_1_, bf16[160,128]{1,0:T(8,128)(2,1)S(1)} %collective-permute-done.4.refs_2_, ...), custom_call_target="tpu_custom_call" | custom-call | tf_op jit(solution)/shard_map/total/pallas_call | solution.py:491
  (18 shorter events, 0.6 us)
Async XLA Ops:
  0.6 0.9 %copy-start = (bf16[4,19456]{1,0:T(4,128)(2,1)S(1)}, bf16[4,19456]{1,0:T(4,128)(2,1)}, u32[]{:S(2)}) copy-start(bf16[4,19456]{1,0:T(4,128)(2,1)} %values_ref.1) | copy-start | bytes 466948
  1.5 0.8 %copy-start.1 = (bf16[64,320]{1,0:T(8,128)(2,1)S(1)}, bf16[64,320]{1,0:T(8,128)(2,1)}, u32[]{:S(2)}) copy-start(bf16[64,320]{1,0:T(8,128)(2,1)} %hidden_ref.1) | copy-start | bytes 122884
  2.3 0.7 %copy-start.2 = (f32[4,608]{1,0:T(4,128)S(1)}, f32[4,608]{1,0:T(4,128)}, u32[]{:S(2)}) copy-start(f32[4,608]{1,0:T(4,128)} %scales_ref.1) | copy-start | bytes 29188
  24.4 3.3 %collective-permute-start = (bf16[8,240,128]{2,1,0:T(8,128)(2,1)S(1)}, bf16[8,240,128]{2,1,0:T(8,128)(2,1)S(1)}, u32[]{:S(2)}, u32[]{:S(2)}) collective-permute-start(bf16[8,240,128]{2,1,0:T(8,128)(2,1)S(1)} %all_to_all.10.own_ref), channel_id=1, source_target_pairs={{0,1},{1,0},{2,3},{3,2},{4,5},{5,4},{6,7},{7,6},{8,9},{9,8},{10,11... | collective-permute-start | bytes 1474568 | tf_op jit(solution)/shard_map/ppermute | solution.py:45
  25.0 0.7 copy-start.3
  25.7 0.7 copy-start.4
  26.4 0.7 copy-start.5
  36.4 12.9 %all-to-all-start.1 = ((f32[16,8,128]{2,1,0:T(8,128)}), f32[16,8,128]{2,1,0:T(8,128)S(1)}, u32[]{:S(2)}, u32[]{:S(2)}) async-start(f32[16,8,128]{2,1,0:T(8,128)} %get-tuple-element.13.own_ref), calls=%async_computation.1 | async-start | bytes 131072 | tf_op jit(solution)/shard_map/all_to_all | solution.py:450
  51.1 1.6 %collective-permute-start.1 = (bf16[8,160,128]{2,1,0:T(8,128)(2,1)S(1)}, bf16[8,160,128]{2,1,0:T(8,128)(2,1)S(1)}, u32[]{:S(2)}, u32[]{:S(2)}) collective-permute-start(bf16[8,160,128]{2,1,0:T(8,128)(2,1)S(1)} %get-tuple-element.18), channel_id=1, source_target_pairs={{0,1},{1,0},{2,3},{3,2},{4,5},{5,4},{6,7},{7,6},{8,9},{9,8},{10,11... | collective-permute-start | bytes 983048 | tf_op jit(solution)/shard_map/ppermute | solution.py:45
  52.9 9.6 %collective-permute-start.8 = (bf16[160,128]{1,0:T(8,128)(2,1)S(1)}, bf16[160,128]{1,0:T(8,128)(2,1)S(1)}, u32[]{:S(2)}, u32[]{:S(2)}) collective-permute-start(bf16[160,128]{1,0:T(8,128)(2,1)S(1)} %get-tuple-element.22), channel_id=1, source_target_pairs={{0,2},{1,3},{2,4},{3,5},{4,6},{5,7},{6,8},{7,9},{8,10},{9,11},{10,... | collective-permute-start | bytes 122888 | tf_op jit(solution)/shard_map/ppermute | solution.py:58
  54.9 9.1 %collective-permute-start.7 = (bf16[160,128]{1,0:T(8,128)(2,1)S(1)}, bf16[160,128]{1,0:T(8,128)(2,1)S(1)}, u32[]{:S(2)}, u32[]{:S(2)}) collective-permute-start(bf16[160,128]{1,0:T(8,128)(2,1)S(1)} %get-tuple-element.23), channel_id=1, source_target_pairs={{0,4},{1,5},{2,6},{3,7},{4,8},{5,9},{6,10},{7,11},{8,12},{9,13},{1... | collective-permute-start | bytes 122888 | tf_op jit(solution)/shard_map/ppermute | solution.py:58
  56.3 9.1 %collective-permute-start.6 = (bf16[160,128]{1,0:T(8,128)(2,1)S(1)}, bf16[160,128]{1,0:T(8,128)(2,1)S(1)}, u32[]{:S(2)}, u32[]{:S(2)}) collective-permute-start(bf16[160,128]{1,0:T(8,128)(2,1)S(1)} %get-tuple-element.24), channel_id=1, source_target_pairs={{0,6},{1,7},{2,8},{3,9},{4,10},{5,11},{6,12},{7,13},{8,14},{9,15},... | collective-permute-start | bytes 122888 | tf_op jit(solution)/shard_map/ppermute | solution.py:58
  58.7 6.8 %collective-permute-start.5 = (bf16[160,128]{1,0:T(8,128)(2,1)S(1)}, bf16[160,128]{1,0:T(8,128)(2,1)S(1)}, u32[]{:S(2)}, u32[]{:S(2)}) collective-permute-start(bf16[160,128]{1,0:T(8,128)(2,1)S(1)} %get-tuple-element.25), channel_id=1, source_target_pairs={{0,8},{1,9},{2,10},{3,11},{4,12},{5,13},{6,14},{7,15},{8,0},{9,1},... | collective-permute-start | bytes 122888 | tf_op jit(solution)/shard_map/ppermute | solution.py:58
  60.1 5.4 %collective-permute-start.4 = (bf16[160,128]{1,0:T(8,128)(2,1)S(1)}, bf16[160,128]{1,0:T(8,128)(2,1)S(1)}, u32[]{:S(2)}, u32[]{:S(2)}) collective-permute-start(bf16[160,128]{1,0:T(8,128)(2,1)S(1)} %get-tuple-element.26), channel_id=1, source_target_pairs={{0,10},{1,11},{2,12},{3,13},{4,14},{5,15},{6,0},{7,1},{8,2},{9,3},... | collective-permute-start | bytes 122888 | tf_op jit(solution)/shard_map/ppermute | solution.py:58
  62.5 4.0 %collective-permute-start.3 = (bf16[160,128]{1,0:T(8,128)(2,1)S(1)}, bf16[160,128]{1,0:T(8,128)(2,1)S(1)}, u32[]{:S(2)}, u32[]{:S(2)}) collective-permute-start(bf16[160,128]{1,0:T(8,128)(2,1)S(1)} %get-tuple-element.27), channel_id=1, source_target_pairs={{0,12},{1,13},{2,14},{3,15},{4,0},{5,1},{6,2},{7,3},{8,4},{9,5},{1... | collective-permute-start | bytes 122888 | tf_op jit(solution)/shard_map/ppermute | solution.py:58
  64.0 4.0 %collective-permute-start.2 = (bf16[160,128]{1,0:T(8,128)(2,1)S(1)}, bf16[160,128]{1,0:T(8,128)(2,1)S(1)}, u32[]{:S(2)}, u32[]{:S(2)}) collective-permute-start(bf16[160,128]{1,0:T(8,128)(2,1)S(1)} %get-tuple-element.28), channel_id=1, source_target_pairs={{0,14},{1,15},{2,0},{3,1},{4,2},{5,3},{6,4},{7,5},{8,6},{9,7},{10,... | collective-permute-start | bytes 122888 | tf_op jit(solution)/shard_map/ppermute | solution.py:58

commit v7 on v6

--- a/solution.py
+++ b/solution.py
@@ -10,6 +10,7 @@
 BLOCK = 32
 LANES = 128
 STATS = 8
+AHEAD = 3
 
 
 sample_weight = 0.5
@@ -127,7 +128,48 @@
     return jnp.sum(jnp.where(down == along, row, jnp.zeros_like(row)), axis=1, keepdims=True)
 
 
-def pack_kernel(hidden_ref, values_ref, scales_ref, packed_ref, wide_ref):
+def token_facts(ids, row_map, lengths, loss_scale, first_entry):
+    tokens = row_map.shape[1]
+    token = lax.broadcasted_iota(jnp.int32, (tokens, tokens), 0)
+    slot = lax.broadcasted_iota(jnp.int32, (tokens, tokens), 1)
+    owner = (row_map == token).astype(jnp.float32)
+    named = jnp.max(owner, axis=1, keepdims=True)
+    owner = jnp.where((slot == 0) & (named == 0.0), 1.0, owner)
+
+    seqs = lengths.shape[1]
+    seq_length = tokens // seqs
+    position = lax.broadcasted_iota(jnp.int32, (tokens, 1), 0)
+    live_until = jnp.zeros((tokens, 1), jnp.int32)
+    for seq in range(seqs):
+        inside = (position >= seq * seq_length) & (position < (seq + 1) * seq_length)
+        until = lengths[:, seq : seq + 1] + seq * seq_length
+        live_until = jnp.where(inside, until, live_until)
+    live = (position < live_until).astype(jnp.float32)
+    count = jnp.sum(live, axis=0, keepdims=True)
+    entry = (column_of(ids) - first_entry).astype(jnp.float32)
+    lane = lax.broadcasted_iota(jnp.int32, (tokens, LANES), 1)
+    table = jnp.where(
+        lane == 0, entry, jnp.where(lane == 1, live / count, live * loss_scale / count)
+    )
+    return owner.astype(jnp.bfloat16), table
+
+
+def pack_kernel(place_ref, scale_ref, *refs, shard_rows):
+    outside, refs = refs[:6], refs[6:]
+    packed_ref, owner_ref, table_ref = refs[:3]
+    inside, wide_ref, sems = refs[3:9], refs[9], refs[10]
+    copies = [
+        pltpu.make_async_copy(source, target, sems.at[i])
+        for i, (source, target) in enumerate(zip(outside, inside))
+    ]
+    for copy in copies:
+        copy.start()
+    for copy in copies:
+        copy.wait()
+    hidden_ref, values_ref, scales_ref, ids_ref, map_ref, lengths_ref = inside
+    owner_ref[...], table_ref[...] = token_facts(
+        ids_ref[...], map_ref[...], lengths_ref[...], scale_ref[0], place_ref[0] * shard_rows
+    )
     chips = packed_ref.shape[0]
     tokens, half = hidden_ref.shape
     slots, entries = values_ref.shape
@@ -183,32 +225,6 @@
         packed_ref[chip, hidden_rows:] = jnp.concatenate(rows, axis=0).astype(jnp.bfloat16)
 
 
-def prepare_kernel(
-    place_ref, lengths_ref, scale_ref, ids_ref, map_ref, owner_ref, tokens_ref, *, shard_rows
-):
-    tokens = map_ref.shape[1]
-    token = lax.broadcasted_iota(jnp.int32, (tokens, tokens), 0)
-    slot = lax.broadcasted_iota(jnp.int32, (tokens, tokens), 1)
-    owner = (map_ref[...] == token).astype(jnp.float32)
-    named = jnp.max(owner, axis=1, keepdims=True)
-    owner = jnp.where((slot == 0) & (named == 0.0), 1.0, owner)
-    owner_ref[...] = owner.astype(jnp.bfloat16)
-
-    seqs = lengths_ref.shape[0]
-    seq_length = tokens // seqs
-    position = lax.broadcasted_iota(jnp.int32, (tokens, 1), 0)
-    live_until = jnp.zeros((tokens, 1), jnp.int32)
-    for seq in range(seqs):
-        inside = (position >= seq * seq_length) & (position < (seq + 1) * seq_length)
-        live_until = jnp.where(inside, lengths_ref[seq] + seq * seq_length, live_until)
-    live = (position < live_until).astype(jnp.float32)
-    share = live / jnp.sum(live, axis=0, keepdims=True)
-    weight = live * scale_ref[0] / jnp.sum(live, axis=0, keepdims=True)
-    entry = (column_of(ids_ref[...]) - place_ref[0] * shard_rows).astype(jnp.float32)
-    lane = lax.broadcasted_iota(jnp.int32, (tokens, LANES), 1)
-    tokens_ref[...] = jnp.where(lane == 0, entry, jnp.where(lane == 1, share, weight))
-
-
 def head_copies(head_ref, held_ref, sems, first):
     chips, _, width = held_ref.shape
     copies = []
@@ -237,7 +253,7 @@
     made_sem,
 ):
     copies = head_copies(head_ref, held_ref, sems, 0)
-    for copy in copies:
+    for copy in copies[:AHEAD]:
         copy.start()
     core = place_ref[0] % 2
     chips, tokens, width = hidden_ref.shape
@@ -272,6 +288,8 @@
     logits = jnp.zeros((tokens, shard_rows), jnp.float32)
     for chip, copy in enumerate(copies):
         copy.wait()
+        if chip + AHEAD < chips:
+            copies[chip + AHEAD].start()
         logits += lax.dot_general(
             hidden_ref[chip],
             held_ref[chip],
@@ -315,12 +333,14 @@
     into = pltpu.make_async_copy(rows_ref, made_ref, made_sem)
     into.start()
     copies = head_copies(head_ref, held_ref, sems, place_ref[0] // 2)
-    for copy in copies:
+    for copy in copies[:AHEAD]:
         copy.start()
     into.wait()
     sums_rows = terms_ref.shape[1]
     for step, copy in enumerate(copies):
         copy.wait()
+        if step + AHEAD < len(copies):
+            copies[step + AHEAD].start()
         products = jnp.dot(made_ref[...], held_ref[step], preferred_element_type=jnp.float32)
         terms_ref[step] = products[:sums_rows]
         picks_ref[step] = products[sums_rows:].astype(jnp.bfloat16)
@@ -400,29 +420,33 @@
     hidden_rows = tokens * half // LANES
     teacher_rows = 2 * slots * (shard_rows + LANES // 2) // LANES
 
-    packed = pl.pallas_call(
-        pack_kernel,
-        out_shape=jax.ShapeDtypeStruct((chips, hidden_rows + teacher_rows, LANES), jnp.bfloat16),
-        in_specs=[vmem] * 3,
-        out_specs=vmem,
-        scratch_shapes=[pltpu.VMEM((2 * slots, entries + LANES), jnp.float32)],
-        compiler_params=params,
-        name="pack",
-    )(hidden_states, teacher_values, teacher_scales)
-    gathered = across_chips(packed)
-    other = swap_cores(gathered)
-
-    owner, table = pl.pallas_call(
-        functools.partial(prepare_kernel, shard_rows=shard_rows),
+    operands = (
+        hidden_states,
+        teacher_values,
+        teacher_scales,
+        token_ids[None, :],
+        row_map[None, :],
+        lengths[None, :],
+    )
+    packed, owner, table = pl.pallas_call(
+        functools.partial(pack_kernel, shard_rows=shard_rows),
         out_shape=(
+            jax.ShapeDtypeStruct((chips, hidden_rows + teacher_rows, LANES), jnp.bfloat16),
             vmem_array((tokens, tokens), jnp.bfloat16),
             vmem_array((tokens, LANES), jnp.float32),
         ),
-        in_specs=[smem] * 3 + [vmem] * 2,
-        out_specs=[vmem] * 2,
+        in_specs=[smem] * 2 + [hbm] * len(operands),
+        out_specs=[vmem] * 3,
+        scratch_shapes=[pltpu.VMEM(operand.shape, operand.dtype) for operand in operands]
+        + [
+            pltpu.VMEM((2 * slots, entries + LANES), jnp.float32),
+            pltpu.SemaphoreType.DMA((len(operands),)),
+        ],
         compiler_params=params,
-        name="prepare",
-    )(place, lengths, loss_scale, token_ids[None, :], row_map[None, :])
+        name="pack",
+    )(place, loss_scale, *[in_hbm(operand) for operand in operands])
+    gathered = across_chips(packed)
+    other = swap_cores(gathered)
 
     rows, stats = pl.pallas_call(
         logits_kernel,

time: 69.1 us -> 64 us (0.926)
  local copies, waits for them, and re-layouts: 4.39 us -> 0.03 us
  waiting for transfers between devices: 3.81 us -> 6.65 us
  Pallas kernels: 21.4 us -> 19 us
  starting transfers between devices: 16.7 us -> 15.6 us
    unnamed x12 -> x0, local copies, waits for them, and re-layouts: 4.37 us -> none
    pallas_call x1, Pallas kernels: 9.09 us -> 6.29 us  [paired_shards(): pl.pallas_call(products_kernel, out_shape=(vmem_array((chips, 2 * tokens,...]
    ppermute x2, waiting for transfers between devices: 1.26 us -> 3.49 us  [swap_cores(): return lax.ppermute(array, 'vocab', [(i, i ^ 1) for i in range(count)])]
    pallas_call x2 -> x1, Pallas kernels: 1.07 us -> 1.48 us  [paired_shards(): pl.pallas_call(functools.partial(pack_kernel, shard_rows=shard_rows), out...]
  transfers between devices with their start and end apart: 10 -> 10, of which waited for: 4 -> 6; matrix products, arithmetic and copies ran while one was open for 0% -> 0% of each run, Pallas kernels for 14% -> 10%
where the time goes in v7:
time: 64 us; the launch traced here: 63.7 us
  blocking collectives  20.9 us (33%)
  Pallas kernels  19 us (30%)
  starting transfers between devices  15.6 us (24%)
  waiting for transfers between devices  6.65 us (10%)
  between operations  1.35 us (2%)
    all_to_all x1, blocking collectives, across_chips(): lax.all_to_all(blocks, 'vocab', split_axis=0, concat_axis=0, axis_index_g...  20.9 us
    ppermute x7, starting transfers between devices, along_chips(): lax.ppermute(array, 'vocab', [(i, (i + 2 * step) % count) for i in range(...  11.9 us
    pallas_call x1, Pallas kernels, paired_shards(): pl.pallas_call(logits_kernel, out_shape=(hbm_array((3 * tokens, shard_row...  8.67 us
    pallas_call x1, Pallas kernels, paired_shards(): pl.pallas_call(products_kernel, out_shape=(vmem_array((chips, 2 * tokens,...  6.29 us
    all_to_all x1, starting transfers between devices, paired_shards(): lax.all_to_all(stats, 'vocab', split_axis=0, concat_axis=0, tiled=True)  3.71 us
    ppermute x2, waiting for transfers between devices, swap_cores(): return lax.ppermute(array, 'vocab', [(i, i ^ 1) for i in range(count)])  3.49 us
    ppermute x7, waiting for transfers between devices, along_chips(): lax.ppermute(array, 'vocab', [(i, (i + 2 * step) % count) for i in range(...  2.56 us
    pallas_call x1, Pallas kernels, paired_shards(): pl.pallas_call(combine_kernel, out_shape=(vmem_array((chips, hidden_rows,...  1.84 us
  transfers between devices with their start and end apart: 10, of which 6 were waited for; matrix products, arithmetic and copies ran while one was open for 0% of the time, Pallas kernels for 10%

profile of v7, /device:TPU:0, one launch (start us, length us, event | category | flops | bytes accessed | tf_op | source)
XLA Modules:
  0.0 63.7 jit_solution(10592233666353299607)
XLA Ops:
  1.3 1.5 %pack.1 = (bf16[8,240,128]{2,1,0:T(8,128)(2,1)S(1)}, bf16[64,64]{1,0:T(8,128)(2,1)S(1)}, f32[64,128]{1,0:T(8,128)S(1)}) custom-call(s32[1]{0:T(128)} %bitcast.place_ref, f32[1]{0:T(128)S(6)} %copy.10.scale_ref, bf16[64,320]{1,0:T(8,128)(2,1)} %refs_0_.1, bf16[4,19456]{1,0:T(4,128)(2,1)} %refs_1_.1, f32[4,608]{1,0:T(4,128)} %refs_2_.1, s32[1,64]{1,0:T(1,128)} %bitcast.21, ...), custom_call_target="tpu_custom_call" | custom-call | tf_op jit(solution)/shard_map/pack/pallas_call | solution.py:431
  2.8 20.9 %all_to_all.10.own_ref = bf16[8,240,128]{2,1,0:T(8,128)(2,1)S(1)} all-to-all(bf16[8,240,128]{2,1,0:T(8,128)(2,1)S(1)} %get-tuple-element.12), channel_id=1, replica_groups={{0,2,4,6,8,10,12,14},{1,3,5,7,9,11,13,15},{16,18,20,22,24,26,28,30},{17..., dimensions={0} | all-to-all | bytes 983040 | tf_op jit(solution)/shard_map/all_to_all | solution.py:52
  23.7 0.0 collective-permute-start
  23.7 1.9 %collective-permute-done.other_ref = bf16[8,240,128]{2,1,0:T(8,128)(2,1)S(1)} collective-permute-done((bf16[8,240,128]{2,1,0:T(8,128)(2,1)S(1)}, bf16[8,240,128]{2,1,0:T(8,128)(2,1)S(1)}, u32[]{:S(2)}, u32[]{:S(2)}) %collective-permute-start) | collective-permute-done | bytes 491552 | tf_op jit(solution)/shard_map/ppermute | solution.py:46
  25.5 8.7 %logits.1 = (bf16[192,1216]{1,0:T(8,128)(2,1)}, f32[16,8,128]{2,1,0:T(8,128)}) custom-call(s32[1]{0:T(128)} %bitcast.place_ref, bf16[8,240,128]{2,1,0:T(8,128)(2,1)S(1)} %all_to_all.10.own_ref, bf16[8,240,128]{2,1,0:T(8,128)(2,1)S(1)} %collective-permute-done.other_ref, bf16[64,64]{1,0:T(8,128)(2,1)S(1)} %get-tuple-element.13.owner_ref, ...), custom_call_target="tpu_custom_call" | custom-call | flops 796917760 | bytes 12451840 | tf_op jit(solution)/shard_map/logits/pallas_call | solution.py:451
  34.2 3.7 %all-to-all-start.1 = ((f32[16,8,128]{2,1,0:T(8,128)}), f32[16,8,128]{2,1,0:T(8,128)S(1)}, u32[]{:S(2)}, u32[]{:S(2)}) async-start(f32[16,8,128]{2,1,0:T(8,128)} %get-tuple-element.15.own_ref), calls=%async_computation.1 | async-start | bytes 131072 | tf_op jit(solution)/shard_map/all_to_all | solution.py:474
  37.9 6.3 %products.1 = (f32[8,128,640]{2,1,0:T(8,128)S(1)}, bf16[8,64,640]{2,1,0:T(8,128)(2,1)S(1)}) custom-call(s32[1]{0:T(128)} %bitcast.place_ref, bf16[192,1216]{1,0:T(8,128)(2,1)} %get-tuple-element.16.rows_ref, bf16[1216,5120]{1,0:T(8,128)(2,1)} %head_ref.3), custom_call_target="tpu_custom_call" | custom-call | flops 2390753280 | bytes 12451840 | tf_op jit(solution)/shard_map/products/pallas_call | solution.py:476
  44.2 0.6 all-to-all-done.1.stats_ref
  44.8 1.8 %combine.1 = (f32[8,160,128]{2,1,0:T(8,128)S(1)}, bf16[8,160,128]{2,1,0:T(8,128)(2,1)S(1)}, f32[1,1]{1,0:T(1,128)}) custom-call(s32[1]{0:T(128)} %bitcast.place_ref, f32[16,8,128]{2,1,0:T(8,128)S(1)} %all-to-all-done.1.stats_ref, f32[16,8,128]{2,1,0:T(8,128)} %get-tuple-element.15.own_ref, f32[64,128]{1,0:T(8,128)S(1)} %get-tuple-element.14.tokens_ref, ...), custom_call_target="tpu_custom_call" | custom-call | tf_op jit(solution)/shard_map/combine/pallas_call | solution.py:492
  46.7 0.0 collective-permute-start.1
  46.7 1.6 %collective-permute-done.1 = bf16[8,160,128]{2,1,0:T(8,128)(2,1)S(1)} collective-permute-done((bf16[8,160,128]{2,1,0:T(8,128)(2,1)S(1)}, bf16[8,160,128]{2,1,0:T(8,128)(2,1)S(1)}, u32[]{:S(2)}, u32[]{:S(2)}) %collective-permute-start.1) | collective-permute-done | bytes 327712 | tf_op jit(solution)/shard_map/ppermute | solution.py:46
  48.3 0.1 fusion
  48.4 1.4 %collective-permute-start.8 = (bf16[160,128]{1,0:T(8,128)(2,1)S(1)}, bf16[160,128]{1,0:T(8,128)(2,1)S(1)}, u32[]{:S(2)}, u32[]{:S(2)}) collective-permute-start(bf16[160,128]{1,0:T(8,128)(2,1)S(1)} %get-tuple-element.24), channel_id=1, source_target_pairs={{0,2},{1,3},{2,4},{3,5},{4,6},{5,7},{6,8},{7,9},{8,10},{9,11},{10,... | collective-permute-start | bytes 122888 | tf_op jit(solution)/shard_map/ppermute | solution.py:59
  49.8 1.5 %collective-permute-start.7 = (bf16[160,128]{1,0:T(8,128)(2,1)S(1)}, bf16[160,128]{1,0:T(8,128)(2,1)S(1)}, u32[]{:S(2)}, u32[]{:S(2)}) collective-permute-start(bf16[160,128]{1,0:T(8,128)(2,1)S(1)} %get-tuple-element.25), channel_id=1, source_target_pairs={{0,4},{1,5},{2,6},{3,7},{4,8},{5,9},{6,10},{7,11},{8,12},{9,13},{1... | collective-permute-start | bytes 122888 | tf_op jit(solution)/shard_map/ppermute | solution.py:59
  51.4 2.3 %collective-permute-start.6 = (bf16[160,128]{1,0:T(8,128)(2,1)S(1)}, bf16[160,128]{1,0:T(8,128)(2,1)S(1)}, u32[]{:S(2)}, u32[]{:S(2)}) collective-permute-start(bf16[160,128]{1,0:T(8,128)(2,1)S(1)} %get-tuple-element.26), channel_id=1, source_target_pairs={{0,6},{1,7},{2,8},{3,9},{4,10},{5,11},{6,12},{7,13},{8,14},{9,15},... | collective-permute-start | bytes 122888 | tf_op jit(solution)/shard_map/ppermute | solution.py:59
  53.6 1.5 %collective-permute-start.5 = (bf16[160,128]{1,0:T(8,128)(2,1)S(1)}, bf16[160,128]{1,0:T(8,128)(2,1)S(1)}, u32[]{:S(2)}, u32[]{:S(2)}) collective-permute-start(bf16[160,128]{1,0:T(8,128)(2,1)S(1)} %get-tuple-element.27), channel_id=1, source_target_pairs={{0,8},{1,9},{2,10},{3,11},{4,12},{5,13},{6,14},{7,15},{8,0},{9,1},... | collective-permute-start | bytes 122888 | tf_op jit(solution)/shard_map/ppermute | solution.py:59
  55.1 2.4 %collective-permute-start.4 = (bf16[160,128]{1,0:T(8,128)(2,1)S(1)}, bf16[160,128]{1,0:T(8,128)(2,1)S(1)}, u32[]{:S(2)}, u32[]{:S(2)}) collective-permute-start(bf16[160,128]{1,0:T(8,128)(2,1)S(1)} %get-tuple-element.28), channel_id=1, source_target_pairs={{0,10},{1,11},{2,12},{3,13},{4,14},{5,15},{6,0},{7,1},{8,2},{9,3},... | collective-permute-start | bytes 122888 | tf_op jit(solution)/shard_map/ppermute | solution.py:59
  57.5 1.5 %collective-permute-start.3 = (bf16[160,128]{1,0:T(8,128)(2,1)S(1)}, bf16[160,128]{1,0:T(8,128)(2,1)S(1)}, u32[]{:S(2)}, u32[]{:S(2)}) collective-permute-start(bf16[160,128]{1,0:T(8,128)(2,1)S(1)} %get-tuple-element.29), channel_id=1, source_target_pairs={{0,12},{1,13},{2,14},{3,15},{4,0},{5,1},{6,2},{7,3},{8,4},{9,5},{1... | collective-permute-start | bytes 122888 | tf_op jit(solution)/shard_map/ppermute | solution.py:59
  59.0 0.0 collective-permute-done.7.refs_5_
  59.0 1.4 %collective-permute-start.2 = (bf16[160,128]{1,0:T(8,128)(2,1)S(1)}, bf16[160,128]{1,0:T(8,128)(2,1)S(1)}, u32[]{:S(2)}, u32[]{:S(2)}) collective-permute-start(bf16[160,128]{1,0:T(8,128)(2,1)S(1)} %get-tuple-element.30), channel_id=1, source_target_pairs={{0,14},{1,15},{2,0},{3,1},{4,2},{5,3},{6,4},{7,5},{8,6},{9,7},{10,... | collective-permute-start | bytes 122888 | tf_op jit(solution)/shard_map/ppermute | solution.py:59
  60.4 0.1 collective-permute-done.4.refs_2_
  60.5 1.0 %collective-permute-done.3.refs_1_ = bf16[160,128]{1,0:T(8,128)(2,1)S(1)} collective-permute-done((bf16[160,128]{1,0:T(8,128)(2,1)S(1)}, bf16[160,128]{1,0:T(8,128)(2,1)S(1)}, u32[]{:S(2)}, u32[]{:S(2)}) %collective-permute-start.3) | collective-permute-done | bytes 40992 | tf_op jit(solution)/shard_map/ppermute | solution.py:59
  61.5 1.4 %collective-permute-done.2.refs_0_ = bf16[160,128]{1,0:T(8,128)(2,1)S(1)} collective-permute-done((bf16[160,128]{1,0:T(8,128)(2,1)S(1)}, bf16[160,128]{1,0:T(8,128)(2,1)S(1)}, u32[]{:S(2)}, u32[]{:S(2)}) %collective-permute-start.2) | collective-permute-done | bytes 40992 | tf_op jit(solution)/shard_map/ppermute | solution.py:59
  63.0 0.7 %total.1 = bf16[64,320]{1,0:T(8,128)(2,1)} custom-call(f32[160,128]{1,0:T(8,128)S(1)} %slice_bitcast_fusion.own_ref, bf16[160,128]{1,0:T(8,128)(2,1)S(1)} %collective-permute-done.2.refs_0_, bf16[160,128]{1,0:T(8,128)(2,1)S(1)} %collective-permute-done.3.refs_1_, bf16[160,128]{1,0:T(8,128)(2,1)S(1)} %collective-permute-done.4.refs_2_, ...), custom_call_target="tpu_custom_call" | custom-call | tf_op jit(solution)/shard_map/total/pallas_call | solution.py:515
  (5 shorter events, 0.0 us)
Async XLA Ops:
  23.7 1.9 %collective-permute-start = (bf16[8,240,128]{2,1,0:T(8,128)(2,1)S(1)}, bf16[8,240,128]{2,1,0:T(8,128)(2,1)S(1)}, u32[]{:S(2)}, u32[]{:S(2)}) collective-permute-start(bf16[8,240,128]{2,1,0:T(8,128)(2,1)S(1)} %all_to_all.10.own_ref), channel_id=1, source_target_pairs={{0,1},{1,0},{2,3},{3,2},{4,5},{5,4},{6,7},{7,6},{8,9},{9,8},{10,11... | collective-permute-start | bytes 1474568 | tf_op jit(solution)/shard_map/ppermute | solution.py:46
  34.2 10.6 %all-to-all-start.1 = ((f32[16,8,128]{2,1,0:T(8,128)}), f32[16,8,128]{2,1,0:T(8,128)S(1)}, u32[]{:S(2)}, u32[]{:S(2)}) async-start(f32[16,8,128]{2,1,0:T(8,128)} %get-tuple-element.15.own_ref), calls=%async_computation.1 | async-start | bytes 131072 | tf_op jit(solution)/shard_map/all_to_all | solution.py:474
  46.7 1.6 %collective-permute-start.1 = (bf16[8,160,128]{2,1,0:T(8,128)(2,1)S(1)}, bf16[8,160,128]{2,1,0:T(8,128)(2,1)S(1)}, u32[]{:S(2)}, u32[]{:S(2)}) collective-permute-start(bf16[8,160,128]{2,1,0:T(8,128)(2,1)S(1)} %get-tuple-element.20), channel_id=1, source_target_pairs={{0,1},{1,0},{2,3},{3,2},{4,5},{5,4},{6,7},{7,6},{8,9},{9,8},{10,11... | collective-permute-start | bytes 983048 | tf_op jit(solution)/shard_map/ppermute | solution.py:46
  48.4 9.0 %collective-permute-start.8 = (bf16[160,128]{1,0:T(8,128)(2,1)S(1)}, bf16[160,128]{1,0:T(8,128)(2,1)S(1)}, u32[]{:S(2)}, u32[]{:S(2)}) collective-permute-start(bf16[160,128]{1,0:T(8,128)(2,1)S(1)} %get-tuple-element.24), channel_id=1, source_target_pairs={{0,2},{1,3},{2,4},{3,5},{4,6},{5,7},{6,8},{7,9},{8,10},{9,11},{10,... | collective-permute-start | bytes 122888 | tf_op jit(solution)/shard_map/ppermute | solution.py:59
  49.8 9.1 %collective-permute-start.7 = (bf16[160,128]{1,0:T(8,128)(2,1)S(1)}, bf16[160,128]{1,0:T(8,128)(2,1)S(1)}, u32[]{:S(2)}, u32[]{:S(2)}) collective-permute-start(bf16[160,128]{1,0:T(8,128)(2,1)S(1)} %get-tuple-element.25), channel_id=1, source_target_pairs={{0,4},{1,5},{2,6},{3,7},{4,8},{5,9},{6,10},{7,11},{8,12},{9,13},{1... | collective-permute-start | bytes 122888 | tf_op jit(solution)/shard_map/ppermute | solution.py:59
  51.4 9.0 %collective-permute-start.6 = (bf16[160,128]{1,0:T(8,128)(2,1)S(1)}, bf16[160,128]{1,0:T(8,128)(2,1)S(1)}, u32[]{:S(2)}, u32[]{:S(2)}) collective-permute-start(bf16[160,128]{1,0:T(8,128)(2,1)S(1)} %get-tuple-element.26), channel_id=1, source_target_pairs={{0,6},{1,7},{2,8},{3,9},{4,10},{5,11},{6,12},{7,13},{8,14},{9,15},... | collective-permute-start | bytes 122888 | tf_op jit(solution)/shard_map/ppermute | solution.py:59
  53.6 6.8 %collective-permute-start.5 = (bf16[160,128]{1,0:T(8,128)(2,1)S(1)}, bf16[160,128]{1,0:T(8,128)(2,1)S(1)}, u32[]{:S(2)}, u32[]{:S(2)}) collective-permute-start(bf16[160,128]{1,0:T(8,128)(2,1)S(1)} %get-tuple-element.27), channel_id=1, source_target_pairs={{0,8},{1,9},{2,10},{3,11},{4,12},{5,13},{6,14},{7,15},{8,0},{9,1},... | collective-permute-start | bytes 122888 | tf_op jit(solution)/shard_map/ppermute | solution.py:59
  55.1 5.4 %collective-permute-start.4 = (bf16[160,128]{1,0:T(8,128)(2,1)S(1)}, bf16[160,128]{1,0:T(8,128)(2,1)S(1)}, u32[]{:S(2)}, u32[]{:S(2)}) collective-permute-start(bf16[160,128]{1,0:T(8,128)(2,1)S(1)} %get-tuple-element.28), channel_id=1, source_target_pairs={{0,10},{1,11},{2,12},{3,13},{4,14},{5,15},{6,0},{7,1},{8,2},{9,3},... | collective-permute-start | bytes 122888 | tf_op jit(solution)/shard_map/ppermute | solution.py:59
  57.5 4.1 %collective-permute-start.3 = (bf16[160,128]{1,0:T(8,128)(2,1)S(1)}, bf16[160,128]{1,0:T(8,128)(2,1)S(1)}, u32[]{:S(2)}, u32[]{:S(2)}) collective-permute-start(bf16[160,128]{1,0:T(8,128)(2,1)S(1)} %get-tuple-element.29), channel_id=1, source_target_pairs={{0,12},{1,13},{2,14},{3,15},{4,0},{5,1},{6,2},{7,3},{8,4},{9,5},{1... | collective-permute-start | bytes 122888 | tf_op jit(solution)/shard_map/ppermute | solution.py:59
  59.0 4.0 %collective-permute-start.2 = (bf16[160,128]{1,0:T(8,128)(2,1)S(1)}, bf16[160,128]{1,0:T(8,128)(2,1)S(1)}, u32[]{:S(2)}, u32[]{:S(2)}) collective-permute-start(bf16[160,128]{1,0:T(8,128)(2,1)S(1)} %get-tuple-element.30), channel_id=1, source_target_pairs={{0,14},{1,15},{2,0},{3,1},{4,2},{5,3},{6,4},{7,5},{8,6},{9,7},{10,... | collective-permute-start | bytes 122888 | tf_op jit(solution)/shard_map/ppermute | solution.py:59

commit v8 on v7

--- a/solution.py
+++ b/solution.py
@@ -111,16 +111,6 @@
     ]
 
 
-def parted(tiles):
-    low = low_lanes(tiles[0].shape)
-    turns = [turned(tile) for tile in tiles[2:]]
-    return tiles[:3], [
-        jnp.where(low, turns[0], turns[1]),
-        jnp.where(low, turns[1], turns[2]),
-        turns[2],
-    ]
-
-
 def column_of(row):
     size = row.shape[1]
     down = lax.broadcasted_iota(jnp.int32, (size, size), 0)
@@ -128,7 +118,7 @@
     return jnp.sum(jnp.where(down == along, row, jnp.zeros_like(row)), axis=1, keepdims=True)
 
 
-def token_facts(ids, row_map, lengths, loss_scale, first_entry):
+def token_facts(ids, row_map, lengths, first_entry):
     tokens = row_map.shape[1]
     token = lax.broadcasted_iota(jnp.int32, (tokens, tokens), 0)
     slot = lax.broadcasted_iota(jnp.int32, (tokens, tokens), 1)
@@ -148,13 +138,10 @@
     count = jnp.sum(live, axis=0, keepdims=True)
     entry = (column_of(ids) - first_entry).astype(jnp.float32)
     lane = lax.broadcasted_iota(jnp.int32, (tokens, LANES), 1)
-    table = jnp.where(
-        lane == 0, entry, jnp.where(lane == 1, live / count, live * loss_scale / count)
-    )
-    return owner.astype(jnp.bfloat16), table
-
-
-def pack_kernel(place_ref, scale_ref, *refs, shard_rows):
+    return owner.astype(jnp.bfloat16), jnp.where(lane == 0, entry, live / count)
+
+
+def pack_kernel(place_ref, *refs, shard_rows):
     outside, refs = refs[:6], refs[6:]
     packed_ref, owner_ref, table_ref = refs[:3]
     inside, wide_ref, sems = refs[3:9], refs[9], refs[10]
@@ -168,7 +155,7 @@
         copy.wait()
     hidden_ref, values_ref, scales_ref, ids_ref, map_ref, lengths_ref = inside
     owner_ref[...], table_ref[...] = token_facts(
-        ids_ref[...], map_ref[...], lengths_ref[...], scale_ref[0], place_ref[0] * shard_rows
+        ids_ref[...], map_ref[...], lengths_ref[...], place_ref[0] * shard_rows
     )
     chips = packed_ref.shape[0]
     tokens, half = hidden_ref.shape
@@ -249,6 +236,7 @@
     made_ref,
     hidden_ref,
     arrived_ref,
+    teacher_ref,
     sems,
     made_sem,
 ):
@@ -261,16 +249,19 @@
     hidden_rows = tokens * width // 2 // LANES
     slots = tokens // (2 * chips)
     upper = low_rows((2 * slots, LANES), slots)
-    for chip in range(chips):
-        own, other = own_ref[chip].astype(jnp.float32), other_ref[chip].astype(jnp.float32)
-        first = jnp.where(core == 0, own, other)
-        second = jnp.where(core == 0, other, own)
-        tiles = joined(
-            unpacked_half(first[:hidden_rows], tokens),
-            unpacked_half(second[:hidden_rows], tokens),
-        )
+
+    def both(chip, rows):
+        own = own_ref[chip, rows].astype(jnp.float32)
+        other = other_ref[chip, rows].astype(jnp.float32)
+        return jnp.where(core == 0, own, other), jnp.where(core == 0, other, own)
+
+    def unpack_hidden(chip):
+        first, second = both(chip, slice(0, hidden_rows))
+        tiles = joined(unpacked_half(first, tokens), unpacked_half(second, tokens))
         hidden_ref[chip] = jnp.concatenate(tiles, axis=1).astype(jnp.bfloat16)
-        first, second = first[hidden_rows:], second[hidden_rows:]
+
+    def unpack_teacher(chip):
+        first, second = both(chip, slice(hidden_rows, own_ref.shape[1]))
         share = first.shape[0] // 2
         first = jnp.where(core == 0, first[:share], first[share:])
         second = jnp.where(core == 0, second[:share], second[share:])
@@ -280,16 +271,28 @@
             tiles.append(jnp.where(upper, one, pltpu.roll(two, slots, 0)))
             tiles.append(jnp.where(upper, pltpu.roll(one, slots, 0), two))
         arrived_ref[2 * slots * chip : 2 * slots * (chip + 1)] = jnp.concatenate(tiles, axis=1)
-    teacher = jnp.dot(
-        owner_ref[...],
-        arrived_ref[:, :shard_rows].astype(jnp.bfloat16),
-        preferred_element_type=jnp.float32,
-    )
+
+    unpack_hidden(0)
     logits = jnp.zeros((tokens, shard_rows), jnp.float32)
     for chip, copy in enumerate(copies):
         copy.wait()
         if chip + AHEAD < chips:
             copies[chip + AHEAD].start()
+        if chip + 1 < chips:
+            unpack_hidden(chip + 1)
+        if chip < chips // 2:
+            unpack_teacher(2 * chip)
+            unpack_teacher(2 * chip + 1)
+        if chip == chips // 2:
+            teacher = jnp.dot(
+                owner_ref[...],
+                arrived_ref[:, :shard_rows].astype(jnp.bfloat16),
+                preferred_element_type=jnp.float32,
+            )
+            teacher_top = jnp.max(teacher, axis=1, keepdims=True)
+            teacher_off = teacher - teacher_top
+            teacher_total = jnp.sum(jnp.exp(teacher_off), axis=1, keepdims=True)
+            teacher_ref[...] = teacher_off
         logits += lax.dot_general(
             hidden_ref[chip],
             held_ref[chip],
@@ -298,13 +301,10 @@
         )
 
     top = jnp.max(logits, axis=1, keepdims=True)
-    teacher_top = jnp.max(teacher, axis=1, keepdims=True)
     off = logits - top
-    teacher_off = teacher - teacher_top
     exps = jnp.exp(off)
     total = jnp.sum(exps, axis=1, keepdims=True)
-    teacher_total = jnp.sum(jnp.exp(teacher_off), axis=1, keepdims=True)
-    gap = off - teacher_off
+    gap = off - teacher_ref[...]
     cross = jnp.sum(exps * gap, axis=1, keepdims=True)
     centre = cross / total
     entry = lax.broadcasted_iota(jnp.int32, (tokens, shard_rows), 1)
@@ -346,11 +346,38 @@
         picks_ref[step] = products[sums_rows:].astype(jnp.bfloat16)
 
 
-def combine_kernel(
-    place_ref, stats_ref, own_ref, tokens_ref, terms_ref, picks_ref, keep_ref, give_ref, loss_ref
+def parity_half(parity, step, factors_ref, terms_ref, picks_ref):
+    tokens = picks_ref.shape[1]
+    lanes = pl.ds(pl.multiple_of(parity * 2 * LANES, LANES), 3 * LANES)
+    factor, level, weight = [factors_ref[:, i : i + 1] for i in range(3)]
+    block = (
+        factor * (terms_ref[step, :tokens, lanes] + level * terms_ref[step, tokens:, lanes])
+        - weight * picks_ref[step, :, lanes].astype(jnp.float32)
+    )
+    tiles = [block[:, i : i + LANES] for i in range(0, 3 * LANES, LANES)]
+    turns = [turned(tile) for tile in tiles]
+    low = low_lanes(tiles[0].shape)
+    first = parity == 0
+    return packed_half(
+        [
+            jnp.where(first, tiles[0], jnp.where(low, turns[0], turns[1])),
+            jnp.where(first, tiles[1], jnp.where(low, turns[1], turns[2])),
+            jnp.where(first, tiles[2], turns[2]),
+        ]
+    )
+
+
+def give_kernel(
+    place_ref,
+    stats_ref,
+    own_ref,
+    tokens_ref,
+    terms_ref,
+    picks_ref,
+    give_ref,
+    factors_ref,
+    loss_ref,
 ):
-    core = place_ref[0] % 2
-    chips, _, width = terms_ref.shape
     tokens = tokens_ref.shape[0]
     tops, sums, teacher_tops, teacher_sums, crosses, targets = [
         stats_ref[:, i, :tokens] for i in range(6)
@@ -372,28 +399,33 @@
     )
     zeros = jnp.zeros((LANES - 3, tokens), jnp.float32)
     columns = jnp.concatenate([factor, level, per_token, zeros], axis=0).T
-    share, weight = tokens_ref[:, 1:2], tokens_ref[:, 2:3]
+    share = tokens_ref[:, 1:2]
     loss_ref[...] = jnp.sum(share * columns[:, 2:3], axis=0, keepdims=True)
-    factor = weight * columns[:, 0:1]
-    level = columns[:, 1:2]
-    weight = sample_weight * weight
-    for step in range(chips):
-        block = (
-            factor * (terms_ref[step, :tokens] + level * terms_ref[step, tokens:])
-            - weight * picks_ref[step].astype(jnp.float32)
+    lane = lax.broadcasted_iota(jnp.int32, (tokens, LANES), 1)
+    factors_ref[...] = jnp.where(
+        lane == 0,
+        share * columns[:, 0:1],
+        jnp.where(lane == 1, columns[:, 1:2], sample_weight * share),
+    )
+    parity = 1 - place_ref[0] % 2
+    for step in range(terms_ref.shape[0]):
+        give_ref[step] = parity_half(parity, step, factors_ref, terms_ref, picks_ref).astype(
+            jnp.bfloat16
         )
-        first, second = parted([block[:, i : i + LANES] for i in range(0, width, LANES)])
-        first, second = packed_half(first), packed_half(second)
-        keep_ref[step] = jnp.where(core == 0, first, second)
-        give_ref[step] = jnp.where(core == 0, second, first).astype(jnp.bfloat16)
-
-
-def sum_kernel(own_ref, *refs):
+
+
+def keep_kernel(place_ref, factors_ref, terms_ref, picks_ref, keep_ref):
+    parity = place_ref[0] % 2
+    for step in range(terms_ref.shape[0]):
+        keep_ref[step] = parity_half(parity, step, factors_ref, terms_ref, picks_ref)
+
+
+def sum_kernel(scale_ref, own_ref, *refs):
     tokens, half = refs[-1].shape
     total = own_ref[...]
     for share_ref in refs[:-1]:
         total += share_ref[...].astype(jnp.float32)
-    tiles = jnp.concatenate(unpacked_half(total, tokens), axis=1)
+    tiles = jnp.concatenate(unpacked_half(total * scale_ref[0], tokens), axis=1)
     refs[-1][...] = tiles[:, :half].astype(refs[-1].dtype)
 
 
@@ -435,7 +467,7 @@
             vmem_array((tokens, tokens), jnp.bfloat16),
             vmem_array((tokens, LANES), jnp.float32),
         ),
-        in_specs=[smem] * 2 + [hbm] * len(operands),
+        in_specs=[smem] + [hbm] * len(operands),
         out_specs=[vmem] * 3,
         scratch_shapes=[pltpu.VMEM(operand.shape, operand.dtype) for operand in operands]
         + [
@@ -444,7 +476,7 @@
         ],
         compiler_params=params,
         name="pack",
-    )(place, loss_scale, *[in_hbm(operand) for operand in operands])
+    )(place, *[in_hbm(operand) for operand in operands])
     gathered = across_chips(packed)
     other = swap_cores(gathered)
 
@@ -461,6 +493,7 @@
             rows_scratch,
             pltpu.VMEM((chips, tokens, width), jnp.bfloat16),
             pltpu.VMEM((tokens, shard_rows + LANES // 2), jnp.float32),
+            pltpu.VMEM((tokens, shard_rows), jnp.float32),
             head_sems,
             rows_sem,
         ],
@@ -489,37 +522,42 @@
         name="products",
     )(place, in_hbm(rows), head)
 
-    keep, give, loss = pl.pallas_call(
-        combine_kernel,
+    terms, picks = in_vmem(terms), in_vmem(picks)
+    give, factors, loss = pl.pallas_call(
+        give_kernel,
         out_shape=(
-            vmem_array((chips, hidden_rows, LANES), jnp.float32),
             vmem_array((chips, hidden_rows, LANES), jnp.bfloat16),
+            vmem_array((tokens, LANES), jnp.float32),
             jax.ShapeDtypeStruct((1, 1), jnp.float32),
         ),
         in_specs=[smem] + [vmem] * 5,
         out_specs=[vmem] * 3,
         compiler_params=params,
-        name="combine",
-    )(
-        place,
-        all_stats,
-        stats,
-        in_vmem(table),
-        in_vmem(terms),
-        in_vmem(picks),
-    )
-
-    sums = keep + swap_cores(give).astype(jnp.float32)
+        name="give",
+    )(place, all_stats, stats, in_vmem(table), terms, picks)
+    taken = swap_cores(give)
+    keep = pl.pallas_call(
+        keep_kernel,
+        out_shape=vmem_array((chips, hidden_rows, LANES), jnp.float32),
+        in_specs=[smem] + [vmem] * 3,
+        out_specs=vmem,
+        compiler_params=params,
+        cost_estimate=pl.CostEstimate(
+            flops=8 * terms.size, bytes_accessed=8 * terms.size, transcendentals=0
+        ),
+        name="keep",
+    )(place, in_vmem(factors), terms, picks)
+    sums = keep + taken.astype(jnp.float32)
     steps = range(chips - 1, 0, -1)
     shares = [along_chips(sums[step].astype(jnp.bfloat16), step) for step in steps]
     total = pl.pallas_call(
         sum_kernel,
         out_shape=jax.ShapeDtypeStruct((tokens, half), jnp.bfloat16),
-        in_specs=[vmem] * chips,
+        in_specs=[smem] + [vmem] * chips,
         out_specs=vmem,
         compiler_params=params,
         name="total",
-    )(sums[0], *shares)
+    )(loss_scale, sums[0], *shares)
     return total, jnp.reshape(loss, (1,))
 
 

time: 64 us -> 65.7 us (1.027)
  waiting for transfers between devices: 6.65 us -> 8.47 us
  starting transfers between devices: 15.6 us -> 14.4 us
  Pallas kernels: 19 us -> 20.1 us
    ppermute x7, waiting for transfers between devices: 2.56 us -> 5.78 us  [along_chips(): lax.ppermute(array, 'vocab', [(i, (i + 2 * step) % count) for i in range(...]
    ppermute x2, waiting for transfers between devices: 3.49 us -> 2.11 us  [swap_cores(): return lax.ppermute(array, 'vocab', [(i, i ^ 1) for i in range(count)])]
    pallas_call x1 -> x2, Pallas kernels: 1.84 us -> 3.18 us  [the longest x1 1.82 us: paired_shards(): pl.pallas_call(give_kernel, out_shape=(vmem_array((chips, hidden_rows, LA...]
    ppermute x7, starting transfers between devices: 11.9 us -> 10.6 us  [along_chips(): lax.ppermute(array, 'vocab', [(i, (i + 2 * step) % count) for i in range(...]
  transfers between devices with their start and end apart: 10 -> 10, of which waited for: 6 -> 5; matrix products, arithmetic and copies ran while one was open for 0% -> 0% of each run, Pallas kernels for 10% -> 12%
where the time goes in v8:
time: 65.7 us; the launch traced here: 65.4 us
  blocking collectives  20.9 us (32%)
  Pallas kernels  20.1 us (31%)
  starting transfers between devices  14.4 us (22%)
  waiting for transfers between devices  8.47 us (13%)
  between operations  1.38 us (2%)
    all_to_all x1, blocking collectives, across_chips(): lax.all_to_all(blocks, 'vocab', split_axis=0, concat_axis=0, axis_index_g...  20.9 us
    ppermute x7, starting transfers between devices, along_chips(): lax.ppermute(array, 'vocab', [(i, (i + 2 * step) % count) for i in range(...  10.6 us
    pallas_call x1, Pallas kernels, paired_shards(): pl.pallas_call(logits_kernel, out_shape=(hbm_array((3 * tokens, shard_row...  8.39 us
    pallas_call x1, Pallas kernels, paired_shards(): pl.pallas_call(products_kernel, out_shape=(vmem_array((chips, 2 * tokens,...  6.31 us
    ppermute x7, waiting for transfers between devices, along_chips(): lax.ppermute(array, 'vocab', [(i, (i + 2 * step) % count) for i in range(...  5.78 us
    all_to_all x1, starting transfers between devices, paired_shards(): lax.all_to_all(stats, 'vocab', split_axis=0, concat_axis=0, tiled=True)  3.7 us
    ppermute x2, waiting for transfers between devices, swap_cores(): return lax.ppermute(array, 'vocab', [(i, i ^ 1) for i in range(count)])  2.11 us
    pallas_call x1, Pallas kernels, paired_shards(): pl.pallas_call(give_kernel, out_shape=(vmem_array((chips, hidden_rows, LA...  1.82 us
  transfers between devices with their start and end apart: 10, of which 5 were waited for; matrix products, arithmetic and copies ran while one was open for 0% of the time, Pallas kernels for 12%

profile of v8, /device:TPU:0, one launch (start us, length us, event | category | flops | bytes accessed | tf_op | source)
XLA Modules:
  0.0 65.4 jit_solution(8732752748794913082)
XLA Ops:
  0.6 1.5 %pack.1 = (bf16[8,240,128]{2,1,0:T(8,128)(2,1)S(1)}, bf16[64,64]{1,0:T(8,128)(2,1)S(1)}, f32[64,128]{1,0:T(8,128)S(1)}) custom-call(s32[1]{0:T(128)} %bitcast.place_ref, bf16[64,320]{1,0:T(8,128)(2,1)} %refs_0_.1, bf16[4,19456]{1,0:T(4,128)(2,1)} %refs_1_.1, f32[4,608]{1,0:T(4,128)} %refs_2_.1, s32[1,64]{1,0:T(1,128)} %bitcast.21, s32[1,64]{1,0:T(1,128)} %bitcast.22, ...), custom_call_target="tpu_custom_call" | custom-call | tf_op jit(solution)/shard_map/pack/pallas_call | solution.py:463
  2.1 20.9 %all_to_all.10.own_ref = bf16[8,240,128]{2,1,0:T(8,128)(2,1)S(1)} all-to-all(bf16[8,240,128]{2,1,0:T(8,128)(2,1)S(1)} %get-tuple-element.12), channel_id=1, replica_groups={{0,2,4,6,8,10,12,14},{1,3,5,7,9,11,13,15},{16,18,20,22,24,26,28,30},{17..., dimensions={0} | all-to-all | bytes 983040 | tf_op jit(solution)/shard_map/all_to_all | solution.py:52
  23.1 0.0 collective-permute-start
  23.1 1.9 %collective-permute-done.other_ref = bf16[8,240,128]{2,1,0:T(8,128)(2,1)S(1)} collective-permute-done((bf16[8,240,128]{2,1,0:T(8,128)(2,1)S(1)}, bf16[8,240,128]{2,1,0:T(8,128)(2,1)S(1)}, u32[]{:S(2)}, u32[]{:S(2)}) %collective-permute-start) | collective-permute-done | bytes 491552 | tf_op jit(solution)/shard_map/ppermute | solution.py:46
  24.9 8.4 %logits.1 = (bf16[192,1216]{1,0:T(8,128)(2,1)}, f32[16,8,128]{2,1,0:T(8,128)}) custom-call(s32[1]{0:T(128)} %bitcast.place_ref, bf16[8,240,128]{2,1,0:T(8,128)(2,1)S(1)} %all_to_all.10.own_ref, bf16[8,240,128]{2,1,0:T(8,128)(2,1)S(1)} %collective-permute-done.other_ref, bf16[64,64]{1,0:T(8,128)(2,1)S(1)} %get-tuple-element.13.owner_ref, ...), custom_call_target="tpu_custom_call" | custom-call | flops 796917760 | bytes 12451840 | tf_op jit(solution)/shard_map/logits/pallas_call | solution.py:483
  33.3 3.7 %all-to-all-start.1 = ((f32[16,8,128]{2,1,0:T(8,128)}), f32[16,8,128]{2,1,0:T(8,128)S(1)}, u32[]{:S(2)}, u32[]{:S(2)}) async-start(f32[16,8,128]{2,1,0:T(8,128)} %get-tuple-element.15.own_ref), calls=%async_computation.1 | async-start | bytes 131072 | tf_op jit(solution)/shard_map/all_to_all | solution.py:507
  37.0 6.3 %products.1 = (f32[8,128,640]{2,1,0:T(8,128)S(1)}, bf16[8,64,640]{2,1,0:T(8,128)(2,1)S(1)}) custom-call(s32[1]{0:T(128)} %bitcast.place_ref, bf16[192,1216]{1,0:T(8,128)(2,1)} %get-tuple-element.16.rows_ref, bf16[1216,5120]{1,0:T(8,128)(2,1)} %head_ref.3), custom_call_target="tpu_custom_call" | custom-call | flops 2390753280 | bytes 12451840 | tf_op jit(solution)/shard_map/products/pallas_call | solution.py:509
  43.4 0.6 all-to-all-done.1.stats_ref
  43.9 1.8 %give.1 = (bf16[8,160,128]{2,1,0:T(8,128)(2,1)S(1)}, f32[64,128]{1,0:T(8,128)S(1)}, f32[1,1]{1,0:T(1,128)}) custom-call(s32[1]{0:T(128)} %bitcast.place_ref, f32[16,8,128]{2,1,0:T(8,128)S(1)} %all-to-all-done.1.stats_ref, f32[16,8,128]{2,1,0:T(8,128)} %get-tuple-element.15.own_ref, f32[64,128]{1,0:T(8,128)S(1)} %get-tuple-element.14.tokens_ref, ...), custom_call_target="tpu_custom_call" | custom-call | tf_op jit(solution)/shard_map/give/pallas_call | solution.py:526
  45.8 0.1 collective-permute-start.1
  45.8 1.4 %keep.1 = f32[8,160,128]{2,1,0:T(8,128)S(1)} custom-call(s32[1]{0:T(128)} %bitcast.place_ref, f32[64,128]{1,0:T(8,128)S(1)} %get-tuple-element.19.factors_ref, f32[8,128,640]{2,1,0:T(8,128)S(1)} %get-tuple-element.17.terms_ref, bf16[8,64,640]{2,1,0:T(8,128)(2,1)S(1)} %get-tuple-element.18.picks_ref), custom_call_target="tpu_custom_call" | custom-call | flops 5242880 | bytes 5242880 | tf_op jit(solution)/shard_map/keep/pallas_call | solution.py:539
  47.2 0.3 collective-permute-done.1
  47.5 0.1 fusion
  47.6 4.1 %collective-permute-start.2 = (bf16[160,128]{1,0:T(8,128)(2,1)S(1)}, bf16[160,128]{1,0:T(8,128)(2,1)S(1)}, u32[]{:S(2)}, u32[]{:S(2)}) collective-permute-start(bf16[160,128]{1,0:T(8,128)(2,1)S(1)} %get-tuple-element.30), channel_id=1, source_target_pairs={{0,14},{1,15},{2,0},{3,1},{4,2},{5,3},{6,4},{7,5},{8,6},{9,7},{10,... | collective-permute-start | bytes 122888 | tf_op jit(solution)/shard_map/ppermute | solution.py:59
  51.7 0.6 collective-permute-start.3
  52.9 0.1 collective-permute-start.4
  53.0 2.9 %collective-permute-start.5 = (bf16[160,128]{1,0:T(8,128)(2,1)S(1)}, bf16[160,128]{1,0:T(8,128)(2,1)S(1)}, u32[]{:S(2)}, u32[]{:S(2)}) collective-permute-start(bf16[160,128]{1,0:T(8,128)(2,1)S(1)} %get-tuple-element.27), channel_id=1, source_target_pairs={{0,8},{1,9},{2,10},{3,11},{4,12},{5,13},{6,14},{7,15},{8,0},{9,1},... | collective-permute-start | bytes 122888 | tf_op jit(solution)/shard_map/ppermute | solution.py:59
  55.9 0.0 collective-permute-start.6
  55.9 0.0 collective-permute-done.2.refs_0_
  55.9 2.1 %collective-permute-start.7 = (bf16[160,128]{1,0:T(8,128)(2,1)S(1)}, bf16[160,128]{1,0:T(8,128)(2,1)S(1)}, u32[]{:S(2)}, u32[]{:S(2)}) collective-permute-start(bf16[160,128]{1,0:T(8,128)(2,1)S(1)} %get-tuple-element.25), channel_id=1, source_target_pairs={{0,4},{1,5},{2,6},{3,7},{4,8},{5,9},{6,10},{7,11},{8,12},{9,13},{1... | collective-permute-start | bytes 122888 | tf_op jit(solution)/shard_map/ppermute | solution.py:59
  58.0 0.9 %collective-permute-start.8 = (bf16[160,128]{1,0:T(8,128)(2,1)S(1)}, bf16[160,128]{1,0:T(8,128)(2,1)S(1)}, u32[]{:S(2)}, u32[]{:S(2)}) collective-permute-start(bf16[160,128]{1,0:T(8,128)(2,1)S(1)} %get-tuple-element.24), channel_id=1, source_target_pairs={{0,2},{1,3},{2,4},{3,5},{4,6},{5,7},{6,8},{7,9},{8,10},{9,11},{10,... | collective-permute-start | bytes 122888 | tf_op jit(solution)/shard_map/ppermute | solution.py:59
  58.9 4.2 %collective-permute-done.6.refs_4_ = bf16[160,128]{1,0:T(8,128)(2,1)S(1)} collective-permute-done((bf16[160,128]{1,0:T(8,128)(2,1)S(1)}, bf16[160,128]{1,0:T(8,128)(2,1)S(1)}, u32[]{:S(2)}, u32[]{:S(2)}) %collective-permute-start.6) | collective-permute-done | bytes 40992 | tf_op jit(solution)/shard_map/ppermute | solution.py:59
  63.1 1.6 %collective-permute-done.8.refs_6_ = bf16[160,128]{1,0:T(8,128)(2,1)S(1)} collective-permute-done((bf16[160,128]{1,0:T(8,128)(2,1)S(1)}, bf16[160,128]{1,0:T(8,128)(2,1)S(1)}, u32[]{:S(2)}, u32[]{:S(2)}) %collective-permute-start.8) | collective-permute-done | bytes 40992 | tf_op jit(solution)/shard_map/ppermute | solution.py:59
  64.7 0.7 %total.1 = bf16[64,320]{1,0:T(8,128)(2,1)} custom-call(f32[1]{0:T(128)S(6)} %copy.10.scale_ref, f32[160,128]{1,0:T(8,128)S(1)} %slice_bitcast_fusion.own_ref, bf16[160,128]{1,0:T(8,128)(2,1)S(1)} %collective-permute-done.2.refs_0_, bf16[160,128]{1,0:T(8,128)(2,1)S(1)} %collective-permute-done.3.refs_1_, bf16[160,128]{1,0:T(8,128)(2,1)S(1)} %collective-permute-done.4.refs_2_, ...), custom_call_target="tpu_custom_call" | custom-call | tf_op jit(solution)/shard_map/total/pallas_call | solution.py:553
  (6 shorter events, 0.0 us)
Async XLA Ops:
  23.1 1.9 %collective-permute-start = (bf16[8,240,128]{2,1,0:T(8,128)(2,1)S(1)}, bf16[8,240,128]{2,1,0:T(8,128)(2,1)S(1)}, u32[]{:S(2)}, u32[]{:S(2)}) collective-permute-start(bf16[8,240,128]{2,1,0:T(8,128)(2,1)S(1)} %all_to_all.10.own_ref), channel_id=1, source_target_pairs={{0,1},{1,0},{2,3},{3,2},{4,5},{5,4},{6,7},{7,6},{8,9},{9,8},{10,11... | collective-permute-start | bytes 1474568 | tf_op jit(solution)/shard_map/ppermute | solution.py:46
  33.3 10.6 %all-to-all-start.1 = ((f32[16,8,128]{2,1,0:T(8,128)}), f32[16,8,128]{2,1,0:T(8,128)S(1)}, u32[]{:S(2)}, u32[]{:S(2)}) async-start(f32[16,8,128]{2,1,0:T(8,128)} %get-tuple-element.15.own_ref), calls=%async_computation.1 | async-start | bytes 131072 | tf_op jit(solution)/shard_map/all_to_all | solution.py:507
  45.8 1.7 %collective-permute-start.1 = (bf16[8,160,128]{2,1,0:T(8,128)(2,1)S(1)}, bf16[8,160,128]{2,1,0:T(8,128)(2,1)S(1)}, u32[]{:S(2)}, u32[]{:S(2)}) collective-permute-start(bf16[8,160,128]{2,1,0:T(8,128)(2,1)S(1)} %get-tuple-element.20), channel_id=1, source_target_pairs={{0,1},{1,0},{2,3},{3,2},{4,5},{5,4},{6,7},{7,6},{8,9},{9,8},{10,11... | collective-permute-start | bytes 983048 | tf_op jit(solution)/shard_map/ppermute | solution.py:46
  47.6 8.3 %collective-permute-start.2 = (bf16[160,128]{1,0:T(8,128)(2,1)S(1)}, bf16[160,128]{1,0:T(8,128)(2,1)S(1)}, u32[]{:S(2)}, u32[]{:S(2)}) collective-permute-start(bf16[160,128]{1,0:T(8,128)(2,1)S(1)} %get-tuple-element.30), channel_id=1, source_target_pairs={{0,14},{1,15},{2,0},{3,1},{4,2},{5,3},{6,4},{7,5},{8,6},{9,7},{10,... | collective-permute-start | bytes 122888 | tf_op jit(solution)/shard_map/ppermute | solution.py:59
  51.7 6.3 %collective-permute-start.3 = (bf16[160,128]{1,0:T(8,128)(2,1)S(1)}, bf16[160,128]{1,0:T(8,128)(2,1)S(1)}, u32[]{:S(2)}, u32[]{:S(2)}) collective-permute-start(bf16[160,128]{1,0:T(8,128)(2,1)S(1)} %get-tuple-element.29), channel_id=1, source_target_pairs={{0,12},{1,13},{2,14},{3,15},{4,0},{5,1},{6,2},{7,3},{8,4},{9,5},{1... | collective-permute-start | bytes 122888 | tf_op jit(solution)/shard_map/ppermute | solution.py:59
  52.9 6.0 %collective-permute-start.4 = (bf16[160,128]{1,0:T(8,128)(2,1)S(1)}, bf16[160,128]{1,0:T(8,128)(2,1)S(1)}, u32[]{:S(2)}, u32[]{:S(2)}) collective-permute-start(bf16[160,128]{1,0:T(8,128)(2,1)S(1)} %get-tuple-element.28), channel_id=1, source_target_pairs={{0,10},{1,11},{2,12},{3,13},{4,14},{5,15},{6,0},{7,1},{8,2},{9,3},... | collective-permute-start | bytes 122888 | tf_op jit(solution)/shard_map/ppermute | solution.py:59
  53.0 5.9 %collective-permute-start.5 = (bf16[160,128]{1,0:T(8,128)(2,1)S(1)}, bf16[160,128]{1,0:T(8,128)(2,1)S(1)}, u32[]{:S(2)}, u32[]{:S(2)}) collective-permute-start(bf16[160,128]{1,0:T(8,128)(2,1)S(1)} %get-tuple-element.27), channel_id=1, source_target_pairs={{0,8},{1,9},{2,10},{3,11},{4,12},{5,13},{6,14},{7,15},{8,0},{9,1},... | collective-permute-start | bytes 122888 | tf_op jit(solution)/shard_map/ppermute | solution.py:59
  55.9 7.2 %collective-permute-start.6 = (bf16[160,128]{1,0:T(8,128)(2,1)S(1)}, bf16[160,128]{1,0:T(8,128)(2,1)S(1)}, u32[]{:S(2)}, u32[]{:S(2)}) collective-permute-start(bf16[160,128]{1,0:T(8,128)(2,1)S(1)} %get-tuple-element.26), channel_id=1, source_target_pairs={{0,6},{1,7},{2,8},{3,9},{4,10},{5,11},{6,12},{7,13},{8,14},{9,15},... | collective-permute-start | bytes 122888 | tf_op jit(solution)/shard_map/ppermute | solution.py:59
  55.9 7.2 %collective-permute-start.7 = (bf16[160,128]{1,0:T(8,128)(2,1)S(1)}, bf16[160,128]{1,0:T(8,128)(2,1)S(1)}, u32[]{:S(2)}, u32[]{:S(2)}) collective-permute-start(bf16[160,128]{1,0:T(8,128)(2,1)S(1)} %get-tuple-element.25), channel_id=1, source_target_pairs={{0,4},{1,5},{2,6},{3,7},{4,8},{5,9},{6,10},{7,11},{8,12},{9,13},{1... | collective-permute-start | bytes 122888 | tf_op jit(solution)/shard_map/ppermute | solution.py:59
  58.0 6.7 %collective-permute-start.8 = (bf16[160,128]{1,0:T(8,128)(2,1)S(1)}, bf16[160,128]{1,0:T(8,128)(2,1)S(1)}, u32[]{:S(2)}, u32[]{:S(2)}) collective-permute-start(bf16[160,128]{1,0:T(8,128)(2,1)S(1)} %get-tuple-element.24), channel_id=1, source_target_pairs={{0,2},{1,3},{2,4},{3,5},{4,6},{5,7},{6,8},{7,9},{8,10},{9,11},{10,... | collective-permute-start | bytes 122888 | tf_op jit(solution)/shard_map/ppermute | solution.py:59

commit v9 on v8

--- a/solution.py
+++ b/solution.py
@@ -108,6 +108,16 @@
         jnp.where(low, first[2], turns[0]),
         jnp.where(low, turns[0], turns[1]),
         jnp.where(low, turns[1], turns[2]),
+    ]
+
+
+def parted(tiles):
+    low = low_lanes(tiles[0].shape)
+    turns = [turned(tile) for tile in tiles[2:]]
+    return tiles[:3], [
+        jnp.where(low, turns[0], turns[1]),
+        jnp.where(low, turns[1], turns[2]),
+        turns[2],
     ]
 
 
@@ -233,12 +243,10 @@
     rows_ref,
     stats_ref,
     held_ref,
-    made_ref,
     hidden_ref,
     arrived_ref,
     teacher_ref,
     sems,
-    made_sem,
 ):
     copies = head_copies(head_ref, held_ref, sems, 0)
     for copy in copies[:AHEAD]:
@@ -310,11 +318,9 @@
     entry = lax.broadcasted_iota(jnp.int32, (tokens, shard_rows), 1)
     hit = entry == tokens_ref[:, :1].astype(jnp.int32)
     target = jnp.sum(jnp.where(hit, logits, 0.0), axis=1, keepdims=True)
-    made_ref[:tokens] = (exps * (gap - centre)).astype(jnp.bfloat16)
-    made_ref[tokens : 2 * tokens] = exps.astype(jnp.bfloat16)
-    made_ref[2 * tokens :] = hit.astype(jnp.bfloat16)
-    out = pltpu.make_async_copy(made_ref, rows_ref, made_sem)
-    out.start()
+    rows_ref[:tokens] = (exps * (gap - centre)).astype(jnp.bfloat16)
+    rows_ref[tokens : 2 * tokens] = exps.astype(jnp.bfloat16)
+    rows_ref[2 * tokens :] = hit.astype(jnp.bfloat16)
 
     lane = lax.broadcasted_iota(jnp.int32, (tokens, LANES), 1)
     table = jnp.zeros((tokens, LANES), jnp.float32)
@@ -324,60 +330,51 @@
         table = jnp.where(lane == place, column, table)
     stats = jnp.concatenate([table, jnp.zeros((stats_ref.shape[2] - tokens, LANES), jnp.float32)])
     stats_ref[...] = jnp.broadcast_to(stats.T[None, :STATS], stats_ref.shape)
-    out.wait()
 
 
 def products_kernel(
-    place_ref, rows_ref, head_ref, terms_ref, picks_ref, held_ref, made_ref, sems, made_sem
+    place_ref, rows_ref, head_ref, terms_ref, picks_ref, held_ref, made_ref, sems, made_sems
 ):
-    into = pltpu.make_async_copy(rows_ref, made_ref, made_sem)
-    into.start()
     copies = head_copies(head_ref, held_ref, sems, place_ref[0] // 2)
     for copy in copies[:AHEAD]:
         copy.start()
-    into.wait()
     sums_rows = terms_ref.shape[1]
+    outs = []
     for step, copy in enumerate(copies):
         copy.wait()
         if step + AHEAD < len(copies):
             copies[step + AHEAD].start()
-        products = jnp.dot(made_ref[...], held_ref[step], preferred_element_type=jnp.float32)
-        terms_ref[step] = products[:sums_rows]
-        picks_ref[step] = products[sums_rows:].astype(jnp.bfloat16)
-
-
-def parity_half(parity, step, factors_ref, terms_ref, picks_ref):
-    tokens = picks_ref.shape[1]
-    lanes = pl.ds(pl.multiple_of(parity * 2 * LANES, LANES), 3 * LANES)
-    factor, level, weight = [factors_ref[:, i : i + 1] for i in range(3)]
-    block = (
-        factor * (terms_ref[step, :tokens, lanes] + level * terms_ref[step, tokens:, lanes])
-        - weight * picks_ref[step, :, lanes].astype(jnp.float32)
-    )
-    tiles = [block[:, i : i + LANES] for i in range(0, 3 * LANES, LANES)]
-    turns = [turned(tile) for tile in tiles]
-    low = low_lanes(tiles[0].shape)
-    first = parity == 0
-    return packed_half(
-        [
-            jnp.where(first, tiles[0], jnp.where(low, turns[0], turns[1])),
-            jnp.where(first, tiles[1], jnp.where(low, turns[1], turns[2])),
-            jnp.where(first, tiles[2], turns[2]),
-        ]
-    )
-
-
-def give_kernel(
+        made_ref[step] = jnp.dot(
+            rows_ref[sums_rows:], held_ref[step], preferred_element_type=jnp.float32
+        ).astype(jnp.bfloat16)
+        outs.append(
+            pltpu.make_async_copy(made_ref.at[step], picks_ref.at[step], made_sems.at[step])
+        )
+        outs[-1].start()
+        terms_ref[step] = jnp.dot(
+            rows_ref[:sums_rows], held_ref[step], preferred_element_type=jnp.float32
+        )
+    for out in outs:
+        out.wait()
+
+
+def combine_kernel(
     place_ref,
     stats_ref,
     own_ref,
     tokens_ref,
     terms_ref,
     picks_ref,
+    keep_ref,
     give_ref,
-    factors_ref,
     loss_ref,
+    got_ref,
+    sem,
 ):
+    into = pltpu.make_async_copy(picks_ref, got_ref, sem)
+    into.start()
+    core = place_ref[0] % 2
+    chips, _, width = terms_ref.shape
     tokens = tokens_ref.shape[0]
     tops, sums, teacher_tops, teacher_sums, crosses, targets = [
         stats_ref[:, i, :tokens] for i in range(6)
@@ -401,23 +398,19 @@
     columns = jnp.concatenate([factor, level, per_token, zeros], axis=0).T
     share = tokens_ref[:, 1:2]
     loss_ref[...] = jnp.sum(share * columns[:, 2:3], axis=0, keepdims=True)
-    lane = lax.broadcasted_iota(jnp.int32, (tokens, LANES), 1)
-    factors_ref[...] = jnp.where(
-        lane == 0,
-        share * columns[:, 0:1],
-        jnp.where(lane == 1, columns[:, 1:2], sample_weight * share),
-    )
-    parity = 1 - place_ref[0] % 2
-    for step in range(terms_ref.shape[0]):
-        give_ref[step] = parity_half(parity, step, factors_ref, terms_ref, picks_ref).astype(
-            jnp.bfloat16
+    factor = share * columns[:, 0:1]
+    level = columns[:, 1:2]
+    weight = sample_weight * share
+    into.wait()
+    for step in range(chips):
+        block = (
+            factor * (terms_ref[step, :tokens] + level * terms_ref[step, tokens:])
+            - weight * got_ref[step].astype(jnp.float32)
         )
-
-
-def keep_kernel(place_ref, factors_ref, terms_ref, picks_ref, keep_ref):
-    parity = place_ref[0] % 2
-    for step in range(terms_ref.shape[0]):
-        keep_ref[step] = parity_half(parity, step, factors_ref, terms_ref, picks_ref)
+        first, second = parted([block[:, i : i + LANES] for i in range(0, width, LANES)])
+        first, second = packed_half(first), packed_half(second)
+        keep_ref[step] = jnp.where(core == 0, first, second)
+        give_ref[step] = jnp.where(core == 0, second, first).astype(jnp.bfloat16)
 
 
 def sum_kernel(scale_ref, own_ref, *refs):
@@ -446,8 +439,7 @@
     head = in_hbm(head)
     head_scratch = pltpu.VMEM((chips, shard_rows, width), head.dtype)
     head_sems = pltpu.SemaphoreType.DMA((chips,))
-    rows_scratch = pltpu.VMEM((3 * tokens, shard_rows), jnp.bfloat16)
-    rows_sem = pltpu.SemaphoreType.DMA
+    picks_scratch = pltpu.VMEM((chips, tokens, width), jnp.bfloat16)
     slots, entries = teacher_values.shape
     hidden_rows = tokens * half // LANES
     teacher_rows = 2 * slots * (shard_rows + LANES // 2) // LANES
@@ -483,19 +475,17 @@
     rows, stats = pl.pallas_call(
         logits_kernel,
         out_shape=(
-            hbm_array((3 * tokens, shard_rows), jnp.bfloat16),
+            vmem_array((3 * tokens, shard_rows), jnp.bfloat16),
             jax.ShapeDtypeStruct((count, STATS, pl.cdiv(tokens, LANES) * LANES), jnp.float32),
         ),
         in_specs=[smem] + [vmem] * 4 + [hbm],
-        out_specs=[hbm, vmem],
+        out_specs=[vmem] * 2,
         scratch_shapes=[
             head_scratch,
-            rows_scratch,
             pltpu.VMEM((chips, tokens, width), jnp.bfloat16),
             pltpu.VMEM((tokens, shard_rows + LANES // 2), jnp.float32),
             pltpu.VMEM((tokens, shard_rows), jnp.float32),
             head_sems,
-            rows_sem,
         ],
         compiler_params=params,
         cost_estimate=pl.CostEstimate(
@@ -510,45 +500,34 @@
         products_kernel,
         out_shape=(
             vmem_array((chips, 2 * tokens, width), jnp.float32),
-            vmem_array((chips, tokens, width), jnp.bfloat16),
+            hbm_array((chips, tokens, width), jnp.bfloat16),
         ),
-        in_specs=[smem, hbm, hbm],
-        out_specs=[vmem] * 2,
-        scratch_shapes=[head_scratch, rows_scratch, head_sems, rows_sem],
+        in_specs=[smem, vmem, hbm],
+        out_specs=[vmem, hbm],
+        scratch_shapes=[head_scratch, picks_scratch, head_sems, head_sems],
         compiler_params=params,
         cost_estimate=pl.CostEstimate(
             flops=6 * tokens * head.size, bytes_accessed=2 * head.size, transcendentals=0
         ),
         name="products",
-    )(place, in_hbm(rows), head)
-
-    terms, picks = in_vmem(terms), in_vmem(picks)
-    give, factors, loss = pl.pallas_call(
-        give_kernel,
+    )(place, in_vmem(rows), head)
+
+    keep, give, loss = pl.pallas_call(
+        combine_kernel,
         out_shape=(
+            vmem_array((chips, hidden_rows, LANES), jnp.float32),
             vmem_array((chips, hidden_rows, LANES), jnp.bfloat16),
-            vmem_array((tokens, LANES), jnp.float32),
             jax.ShapeDtypeStruct((1, 1), jnp.float32),
         ),
-        in_specs=[smem] + [vmem] * 5,
+        in_specs=[smem] + [vmem] * 4 + [hbm],
         out_specs=[vmem] * 3,
+        scratch_shapes=[picks_scratch, pltpu.SemaphoreType.DMA],
         compiler_params=params,
-        name="give",
-    )(place, all_stats, stats, in_vmem(table), terms, picks)
-    taken = swap_cores(give)
-    keep = pl.pallas_call(
-        keep_kernel,
-        out_shape=vmem_array((chips, hidden_rows, LANES), jnp.float32),
-        in_specs=[smem] + [vmem] * 3,
-        out_specs=vmem,
-        compiler_params=params,
-        cost_estimate=pl.CostEstimate(
-            flops=8 * terms.size, bytes_accessed=8 * terms.size, transcendentals=0
-        ),
-        name="keep",
-    )(place, in_vmem(factors), terms, picks)
-    sums = keep + taken.astype(jnp.float32)
-    steps = range(chips - 1, 0, -1)
+        name="combine",
+    )(place, all_stats, stats, in_vmem(table), in_vmem(terms), in_hbm(picks))
+
+    sums = keep + swap_cores(give).astype(jnp.float32)
+    steps = range(1, chips)
     shares = [along_chips(sums[step].astype(jnp.bfloat16), step) for step in steps]
     total = pl.pallas_call(
         sum_kernel,

time: 65.7 us -> 65.3 us (level)
  waiting for transfers between devices: 8.47 us -> 5.63 us
  starting transfers between devices: 14.4 us -> 16.7 us
    ppermute x7, waiting for transfers between devices: 5.78 us -> 2.51 us  [along_chips(): lax.ppermute(array, 'vocab', [(i, (i + 2 * step) % count) for i in range(...]
    ppermute x7, starting transfers between devices: 10.6 us -> 12.6 us  [along_chips(): lax.ppermute(array, 'vocab', [(i, (i + 2 * step) % count) for i in range(...]
    pallas_call x1, Pallas kernels: 6.31 us -> 7.77 us  [paired_shards(): pl.pallas_call(products_kernel, out_shape=(vmem_array((chips, 2 * tokens,...]
    pallas_call x3 -> x2, Pallas kernels: 11.6 us -> 10.2 us  [the longest x1 7.67 us: paired_shards(): pl.pallas_call(logits_kernel, out_shape=(vmem_array((3 * tokens, shard_ro...]
    ppermute x2, waiting for transfers between devices: 2.11 us -> 3.12 us  [swap_cores(): return lax.ppermute(array, 'vocab', [(i, i ^ 1) for i in range(count)])]
where the time goes in v9:
time: 65.3 us; the launch traced here: 64.9 us
  blocking collectives  20.9 us (32%)
  Pallas kernels  20.2 us (31%)
  starting transfers between devices  16.7 us (26%)
  waiting for transfers between devices  5.63 us (9%)
  between operations  1.37 us (2%)
    all_to_all x1, blocking collectives, across_chips(): lax.all_to_all(blocks, 'vocab', split_axis=0, concat_axis=0, axis_index_g...  20.9 us
    ppermute x7, starting transfers between devices, along_chips(): lax.ppermute(array, 'vocab', [(i, (i + 2 * step) % count) for i in range(...  12.6 us
    pallas_call x1, Pallas kernels, paired_shards(): pl.pallas_call(products_kernel, out_shape=(vmem_array((chips, 2 * tokens,...  7.77 us
    pallas_call x1, Pallas kernels, paired_shards(): pl.pallas_call(logits_kernel, out_shape=(vmem_array((3 * tokens, shard_ro...  7.67 us
    all_to_all x1, starting transfers between devices, paired_shards(): lax.all_to_all(stats, 'vocab', split_axis=0, concat_axis=0, tiled=True)  3.7 us
    ppermute x2, waiting for transfers between devices, swap_cores(): return lax.ppermute(array, 'vocab', [(i, i ^ 1) for i in range(count)])  3.12 us
    ppermute x7, waiting for transfers between devices, along_chips(): lax.ppermute(array, 'vocab', [(i, (i + 2 * step) % count) for i in range(...  2.51 us
    pallas_call x1, Pallas kernels, paired_shards(): pl.pallas_call(combine_kernel, out_shape=(vmem_array((chips, hidden_rows,...  2.51 us
  transfers between devices with their start and end apart: 10, of which 5 were waited for; matrix products, arithmetic and copies ran while one was open for 0% of the time, Pallas kernels for 12%

profile of v9, /device:TPU:0, one launch (start us, length us, event | category | flops | bytes accessed | tf_op | source)
XLA Modules:
  0.0 64.9 jit_solution(8280034178618300107)
XLA Ops:
  0.6 1.5 %pack.1 = (bf16[8,240,128]{2,1,0:T(8,128)(2,1)S(1)}, bf16[64,64]{1,0:T(8,128)(2,1)S(1)}, f32[64,128]{1,0:T(8,128)S(1)}) custom-call(s32[1]{0:T(128)} %bitcast.place_ref, bf16[64,320]{1,0:T(8,128)(2,1)} %refs_0_.1, bf16[4,19456]{1,0:T(4,128)(2,1)} %refs_1_.1, f32[4,608]{1,0:T(4,128)} %refs_2_.1, s32[1,64]{1,0:T(1,128)} %bitcast.21, s32[1,64]{1,0:T(1,128)} %bitcast.22, ...), custom_call_target="tpu_custom_call" | custom-call | tf_op jit(solution)/shard_map/pack/pallas_call | solution.py:455
  2.1 20.9 %all_to_all.10.own_ref = bf16[8,240,128]{2,1,0:T(8,128)(2,1)S(1)} all-to-all(bf16[8,240,128]{2,1,0:T(8,128)(2,1)S(1)} %get-tuple-element.12), channel_id=1, replica_groups={{0,2,4,6,8,10,12,14},{1,3,5,7,9,11,13,15},{16,18,20,22,24,26,28,30},{17..., dimensions={0} | all-to-all | bytes 983040 | tf_op jit(solution)/shard_map/all_to_all | solution.py:52
  23.1 0.0 collective-permute-start
  23.1 1.9 %collective-permute-done.other_ref = bf16[8,240,128]{2,1,0:T(8,128)(2,1)S(1)} collective-permute-done((bf16[8,240,128]{2,1,0:T(8,128)(2,1)S(1)}, bf16[8,240,128]{2,1,0:T(8,128)(2,1)S(1)}, u32[]{:S(2)}, u32[]{:S(2)}) %collective-permute-start) | collective-permute-done | bytes 491552 | tf_op jit(solution)/shard_map/ppermute | solution.py:46
  24.9 7.7 %logits.1 = (bf16[192,1216]{1,0:T(8,128)(2,1)S(1)}, f32[16,8,128]{2,1,0:T(8,128)}) custom-call(s32[1]{0:T(128)} %bitcast.place_ref, bf16[8,240,128]{2,1,0:T(8,128)(2,1)S(1)} %all_to_all.10.own_ref, bf16[8,240,128]{2,1,0:T(8,128)(2,1)S(1)} %collective-permute-done.other_ref, bf16[64,64]{1,0:T(8,128)(2,1)S(1)} %get-tuple-element.13.owner_ref, ...), custom_call_target="tpu_custom_call" | custom-call | flops 796917760 | bytes 12451840 | tf_op jit(solution)/shard_map/logits/pallas_call | solution.py:475
  32.6 3.7 %all-to-all-start.1 = ((f32[16,8,128]{2,1,0:T(8,128)}), f32[16,8,128]{2,1,0:T(8,128)S(1)}, u32[]{:S(2)}, u32[]{:S(2)}) async-start(f32[16,8,128]{2,1,0:T(8,128)} %get-tuple-element.15.own_ref), calls=%async_computation.1 | async-start | bytes 131072 | tf_op jit(solution)/shard_map/all_to_all | solution.py:497
  36.3 7.8 %products.1 = (f32[8,128,640]{2,1,0:T(8,128)S(1)}, bf16[8,64,640]{2,1,0:T(8,128)(2,1)}) custom-call(s32[1]{0:T(128)} %bitcast.place_ref, bf16[192,1216]{1,0:T(8,128)(2,1)S(1)} %get-tuple-element.16.rows_ref, bf16[1216,5120]{1,0:T(8,128)(2,1)} %head_ref.3), custom_call_target="tpu_custom_call" | custom-call | flops 2390753280 | bytes 12451840 | tf_op jit(solution)/shard_map/products/pallas_call | solution.py:499
  44.1 2.5 %combine.1 = (f32[8,160,128]{2,1,0:T(8,128)S(1)}, bf16[8,160,128]{2,1,0:T(8,128)(2,1)S(1)}, f32[1,1]{1,0:T(1,128)}) custom-call(s32[1]{0:T(128)} %bitcast.place_ref, f32[16,8,128]{2,1,0:T(8,128)S(1)} %all-to-all-done.1.stats_ref, f32[16,8,128]{2,1,0:T(8,128)} %get-tuple-element.15.own_ref, f32[64,128]{1,0:T(8,128)S(1)} %get-tuple-element.14.tokens_ref, ...), custom_call_target="tpu_custom_call" | custom-call | tf_op jit(solution)/shard_map/combine/pallas_call | solution.py:515
  46.6 0.5 collective-permute-start.1
  47.1 1.3 %collective-permute-done.1 = bf16[8,160,128]{2,1,0:T(8,128)(2,1)S(1)} collective-permute-done((bf16[8,160,128]{2,1,0:T(8,128)(2,1)S(1)}, bf16[8,160,128]{2,1,0:T(8,128)(2,1)S(1)}, u32[]{:S(2)}, u32[]{:S(2)}) %collective-permute-start.1) | collective-permute-done | bytes 327712 | tf_op jit(solution)/shard_map/ppermute | solution.py:46
  48.3 0.1 fusion
  48.5 1.9 %collective-permute-start.2 = (bf16[160,128]{1,0:T(8,128)(2,1)S(1)}, bf16[160,128]{1,0:T(8,128)(2,1)S(1)}, u32[]{:S(2)}, u32[]{:S(2)}) collective-permute-start(bf16[160,128]{1,0:T(8,128)(2,1)S(1)} %get-tuple-element.30), channel_id=1, source_target_pairs={{0,2},{1,3},{2,4},{3,5},{4,6},{5,7},{6,8},{7,9},{8,10},{9,11},{10,... | collective-permute-start | bytes 122888 | tf_op jit(solution)/shard_map/ppermute | solution.py:59
  50.4 1.5 %collective-permute-start.3 = (bf16[160,128]{1,0:T(8,128)(2,1)S(1)}, bf16[160,128]{1,0:T(8,128)(2,1)S(1)}, u32[]{:S(2)}, u32[]{:S(2)}) collective-permute-start(bf16[160,128]{1,0:T(8,128)(2,1)S(1)} %get-tuple-element.29), channel_id=1, source_target_pairs={{0,4},{1,5},{2,6},{3,7},{4,8},{5,9},{6,10},{7,11},{8,12},{9,13},{1... | collective-permute-start | bytes 122888 | tf_op jit(solution)/shard_map/ppermute | solution.py:59
  52.5 2.4 %collective-permute-start.4 = (bf16[160,128]{1,0:T(8,128)(2,1)S(1)}, bf16[160,128]{1,0:T(8,128)(2,1)S(1)}, u32[]{:S(2)}, u32[]{:S(2)}) collective-permute-start(bf16[160,128]{1,0:T(8,128)(2,1)S(1)} %get-tuple-element.28), channel_id=1, source_target_pairs={{0,6},{1,7},{2,8},{3,9},{4,10},{5,11},{6,12},{7,13},{8,14},{9,15},... | collective-permute-start | bytes 122888 | tf_op jit(solution)/shard_map/ppermute | solution.py:59
  54.9 1.5 %collective-permute-start.5 = (bf16[160,128]{1,0:T(8,128)(2,1)S(1)}, bf16[160,128]{1,0:T(8,128)(2,1)S(1)}, u32[]{:S(2)}, u32[]{:S(2)}) collective-permute-start(bf16[160,128]{1,0:T(8,128)(2,1)S(1)} %get-tuple-element.27), channel_id=1, source_target_pairs={{0,8},{1,9},{2,10},{3,11},{4,12},{5,13},{6,14},{7,15},{8,0},{9,1},... | collective-permute-start | bytes 122888 | tf_op jit(solution)/shard_map/ppermute | solution.py:59
  56.4 2.4 %collective-permute-start.6 = (bf16[160,128]{1,0:T(8,128)(2,1)S(1)}, bf16[160,128]{1,0:T(8,128)(2,1)S(1)}, u32[]{:S(2)}, u32[]{:S(2)}) collective-permute-start(bf16[160,128]{1,0:T(8,128)(2,1)S(1)} %get-tuple-element.26), channel_id=1, source_target_pairs={{0,10},{1,11},{2,12},{3,13},{4,14},{5,15},{6,0},{7,1},{8,2},{9,3},... | collective-permute-start | bytes 122888 | tf_op jit(solution)/shard_map/ppermute | solution.py:59
  58.8 1.5 %collective-permute-start.7 = (bf16[160,128]{1,0:T(8,128)(2,1)S(1)}, bf16[160,128]{1,0:T(8,128)(2,1)S(1)}, u32[]{:S(2)}, u32[]{:S(2)}) collective-permute-start(bf16[160,128]{1,0:T(8,128)(2,1)S(1)} %get-tuple-element.25), channel_id=1, source_target_pairs={{0,12},{1,13},{2,14},{3,15},{4,0},{5,1},{6,2},{7,3},{8,4},{9,5},{1... | collective-permute-start | bytes 122888 | tf_op jit(solution)/shard_map/ppermute | solution.py:59
  60.2 0.0 collective-permute-done.3.refs_1_
  60.2 1.5 %collective-permute-start.8 = (bf16[160,128]{1,0:T(8,128)(2,1)S(1)}, bf16[160,128]{1,0:T(8,128)(2,1)S(1)}, u32[]{:S(2)}, u32[]{:S(2)}) collective-permute-start(bf16[160,128]{1,0:T(8,128)(2,1)S(1)} %get-tuple-element.24), channel_id=1, source_target_pairs={{0,14},{1,15},{2,0},{3,1},{4,2},{5,3},{6,4},{7,5},{8,6},{9,7},{10,... | collective-permute-start | bytes 122888 | tf_op jit(solution)/shard_map/ppermute | solution.py:59
  61.7 0.0 collective-permute-done.4.refs_2_
  61.7 0.1 collective-permute-done.6.refs_4_
  61.8 1.0 %collective-permute-done.7.refs_5_ = bf16[160,128]{1,0:T(8,128)(2,1)S(1)} collective-permute-done((bf16[160,128]{1,0:T(8,128)(2,1)S(1)}, bf16[160,128]{1,0:T(8,128)(2,1)S(1)}, u32[]{:S(2)}, u32[]{:S(2)}) %collective-permute-start.7) | collective-permute-done | bytes 40992 | tf_op jit(solution)/shard_map/ppermute | solution.py:59
  62.8 1.4 %collective-permute-done.8.refs_6_ = bf16[160,128]{1,0:T(8,128)(2,1)S(1)} collective-permute-done((bf16[160,128]{1,0:T(8,128)(2,1)S(1)}, bf16[160,128]{1,0:T(8,128)(2,1)S(1)}, u32[]{:S(2)}, u32[]{:S(2)}) %collective-permute-start.8) | collective-permute-done | bytes 40992 | tf_op jit(solution)/shard_map/ppermute | solution.py:59
  64.2 0.7 %total.1 = bf16[64,320]{1,0:T(8,128)(2,1)} custom-call(f32[1]{0:T(128)S(6)} %copy.10.scale_ref, f32[160,128]{1,0:T(8,128)S(1)} %slice_bitcast_fusion.own_ref, bf16[160,128]{1,0:T(8,128)(2,1)S(1)} %collective-permute-done.2.refs_0_, bf16[160,128]{1,0:T(8,128)(2,1)S(1)} %collective-permute-done.3.refs_1_, bf16[160,128]{1,0:T(8,128)(2,1)S(1)} %collective-permute-done.4.refs_2_, ...), custom_call_target="tpu_custom_call" | custom-call | tf_op jit(solution)/shard_map/total/pallas_call | solution.py:532
  (5 shorter events, 0.0 us)
Async XLA Ops:
  23.1 1.9 %collective-permute-start = (bf16[8,240,128]{2,1,0:T(8,128)(2,1)S(1)}, bf16[8,240,128]{2,1,0:T(8,128)(2,1)S(1)}, u32[]{:S(2)}, u32[]{:S(2)}) collective-permute-start(bf16[8,240,128]{2,1,0:T(8,128)(2,1)S(1)} %all_to_all.10.own_ref), channel_id=1, source_target_pairs={{0,1},{1,0},{2,3},{3,2},{4,5},{5,4},{6,7},{7,6},{8,9},{9,8},{10,11... | collective-permute-start | bytes 1474568 | tf_op jit(solution)/shard_map/ppermute | solution.py:46
  32.6 11.5 %all-to-all-start.1 = ((f32[16,8,128]{2,1,0:T(8,128)}), f32[16,8,128]{2,1,0:T(8,128)S(1)}, u32[]{:S(2)}, u32[]{:S(2)}) async-start(f32[16,8,128]{2,1,0:T(8,128)} %get-tuple-element.15.own_ref), calls=%async_computation.1 | async-start | bytes 131072 | tf_op jit(solution)/shard_map/all_to_all | solution.py:497
  46.6 1.7 %collective-permute-start.1 = (bf16[8,160,128]{2,1,0:T(8,128)(2,1)S(1)}, bf16[8,160,128]{2,1,0:T(8,128)(2,1)S(1)}, u32[]{:S(2)}, u32[]{:S(2)}) collective-permute-start(bf16[8,160,128]{2,1,0:T(8,128)(2,1)S(1)} %get-tuple-element.20), channel_id=1, source_target_pairs={{0,1},{1,0},{2,3},{3,2},{4,5},{5,4},{6,7},{7,6},{8,9},{9,8},{10,11... | collective-permute-start | bytes 983048 | tf_op jit(solution)/shard_map/ppermute | solution.py:46
  48.5 10.3 %collective-permute-start.2 = (bf16[160,128]{1,0:T(8,128)(2,1)S(1)}, bf16[160,128]{1,0:T(8,128)(2,1)S(1)}, u32[]{:S(2)}, u32[]{:S(2)}) collective-permute-start(bf16[160,128]{1,0:T(8,128)(2,1)S(1)} %get-tuple-element.30), channel_id=1, source_target_pairs={{0,2},{1,3},{2,4},{3,5},{4,6},{5,7},{6,8},{7,9},{8,10},{9,11},{10,... | collective-permute-start | bytes 122888 | tf_op jit(solution)/shard_map/ppermute | solution.py:59
  50.4 9.8 %collective-permute-start.3 = (bf16[160,128]{1,0:T(8,128)(2,1)S(1)}, bf16[160,128]{1,0:T(8,128)(2,1)S(1)}, u32[]{:S(2)}, u32[]{:S(2)}) collective-permute-start(bf16[160,128]{1,0:T(8,128)(2,1)S(1)} %get-tuple-element.29), channel_id=1, source_target_pairs={{0,4},{1,5},{2,6},{3,7},{4,8},{5,9},{6,10},{7,11},{8,12},{9,13},{1... | collective-permute-start | bytes 122888 | tf_op jit(solution)/shard_map/ppermute | solution.py:59
  52.5 9.2 %collective-permute-start.4 = (bf16[160,128]{1,0:T(8,128)(2,1)S(1)}, bf16[160,128]{1,0:T(8,128)(2,1)S(1)}, u32[]{:S(2)}, u32[]{:S(2)}) collective-permute-start(bf16[160,128]{1,0:T(8,128)(2,1)S(1)} %get-tuple-element.28), channel_id=1, source_target_pairs={{0,6},{1,7},{2,8},{3,9},{4,10},{5,11},{6,12},{7,13},{8,14},{9,15},... | collective-permute-start | bytes 122888 | tf_op jit(solution)/shard_map/ppermute | solution.py:59
  54.9 6.8 %collective-permute-start.5 = (bf16[160,128]{1,0:T(8,128)(2,1)S(1)}, bf16[160,128]{1,0:T(8,128)(2,1)S(1)}, u32[]{:S(2)}, u32[]{:S(2)}) collective-permute-start(bf16[160,128]{1,0:T(8,128)(2,1)S(1)} %get-tuple-element.27), channel_id=1, source_target_pairs={{0,8},{1,9},{2,10},{3,11},{4,12},{5,13},{6,14},{7,15},{8,0},{9,1},... | collective-permute-start | bytes 122888 | tf_op jit(solution)/shard_map/ppermute | solution.py:59
  56.4 5.4 %collective-permute-start.6 = (bf16[160,128]{1,0:T(8,128)(2,1)S(1)}, bf16[160,128]{1,0:T(8,128)(2,1)S(1)}, u32[]{:S(2)}, u32[]{:S(2)}) collective-permute-start(bf16[160,128]{1,0:T(8,128)(2,1)S(1)} %get-tuple-element.26), channel_id=1, source_target_pairs={{0,10},{1,11},{2,12},{3,13},{4,14},{5,15},{6,0},{7,1},{8,2},{9,3},... | collective-permute-start | bytes 122888 | tf_op jit(solution)/shard_map/ppermute | solution.py:59
  58.8 4.0 %collective-permute-start.7 = (bf16[160,128]{1,0:T(8,128)(2,1)S(1)}, bf16[160,128]{1,0:T(8,128)(2,1)S(1)}, u32[]{:S(2)}, u32[]{:S(2)}) collective-permute-start(bf16[160,128]{1,0:T(8,128)(2,1)S(1)} %get-tuple-element.25), channel_id=1, source_target_pairs={{0,12},{1,13},{2,14},{3,15},{4,0},{5,1},{6,2},{7,3},{8,4},{9,5},{1... | collective-permute-start | bytes 122888 | tf_op jit(solution)/shard_map/ppermute | solution.py:59
  60.2 4.0 %collective-permute-start.8 = (bf16[160,128]{1,0:T(8,128)(2,1)S(1)}, bf16[160,128]{1,0:T(8,128)(2,1)S(1)}, u32[]{:S(2)}, u32[]{:S(2)}) collective-permute-start(bf16[160,128]{1,0:T(8,128)(2,1)S(1)} %get-tuple-element.24), channel_id=1, source_target_pairs={{0,14},{1,15},{2,0},{3,1},{4,2},{5,3},{6,4},{7,5},{8,6},{9,7},{10,... | collective-permute-start | bytes 122888 | tf_op jit(solution)/shard_map/ppermute | solution.py:59

commit v10 on v9

--- a/solution.py
+++ b/solution.py
@@ -44,14 +44,6 @@
 def swap_cores(array):
     count = lax.axis_size("vocab")
     return lax.ppermute(array, "vocab", [(i, i ^ 1) for i in range(count)])
-
-
-def across_chips(blocks):
-    count = lax.axis_size("vocab")
-    groups = [list(range(core, count, 2)) for core in range(2)]
-    return lax.all_to_all(
-        blocks, "vocab", split_axis=0, concat_axis=0, axis_index_groups=groups, tiled=True
-    )
 
 
 def along_chips(array, step):
@@ -218,58 +210,51 @@
             rows += [
                 jnp.where(upper, tiles[2 * i], tiles[2 * i + 1]) for i in range(tile_pairs)
             ]
-        packed_ref[chip, :hidden_rows] = hidden
-        packed_ref[chip, hidden_rows:] = jnp.concatenate(rows, axis=0).astype(jnp.bfloat16)
-
-
-def head_copies(head_ref, held_ref, sems, first):
-    chips, _, width = held_ref.shape
+        step = lax.rem(chip - place_ref[0] // 2 + chips, chips)
+        packed_ref[step, :hidden_rows] = hidden
+        packed_ref[step, hidden_rows:] = jnp.concatenate(rows, axis=0).astype(jnp.bfloat16)
+
+
+def head_copies(head_ref, held_ref, sems, chips):
+    width = held_ref.shape[2]
     copies = []
-    for step in range(chips):
-        columns = pl.ds(pl.multiple_of(lax.rem(first + step, chips) * width, LANES), width)
+    for step, chip in enumerate(chips):
+        columns = pl.ds(pl.multiple_of(chip * width, LANES), width)
         copies.append(
             pltpu.make_async_copy(head_ref.at[:, columns], held_ref.at[step], sems.at[step])
         )
     return copies
 
 
-def logits_kernel(
-    place_ref,
-    own_ref,
-    other_ref,
-    owner_ref,
-    tokens_ref,
-    head_ref,
-    rows_ref,
-    stats_ref,
-    held_ref,
-    hidden_ref,
-    arrived_ref,
-    teacher_ref,
-    sems,
-):
-    copies = head_copies(head_ref, held_ref, sems, 0)
+def logits_kernel(place_ref, *refs, chips):
+    near, far, refs = refs[:chips], refs[chips : chips + 2], refs[chips + 2 :]
+    owner_ref, tokens_ref, head_ref, rows_ref, stats_ref = refs[:5]
+    held_ref, made_ref, hidden_ref, arrived_ref, teacher_ref, sems, made_sem = refs[5:]
+    place = place_ref[0] // 2
+    core = place_ref[0] % 2
+    sources = [lax.rem(place - step + chips, chips) for step in range(chips)]
+    copies = head_copies(head_ref, held_ref, sems, sources)
     for copy in copies[:AHEAD]:
         copy.start()
-    core = place_ref[0] % 2
-    chips, tokens, width = hidden_ref.shape
+    _, tokens, width = hidden_ref.shape
     shard_rows = head_ref.shape[0]
     hidden_rows = tokens * width // 2 // LANES
     slots = tokens // (2 * chips)
     upper = low_rows((2 * slots, LANES), slots)
 
-    def both(chip, rows):
-        own = own_ref[chip, rows].astype(jnp.float32)
-        other = other_ref[chip, rows].astype(jnp.float32)
+    def both(step, rows):
+        own = near[step][rows].astype(jnp.float32)
+        group = far[step // (chips // 2)]
+        other = group[step % (chips // 2), rows].astype(jnp.float32)
         return jnp.where(core == 0, own, other), jnp.where(core == 0, other, own)
 
-    def unpack_hidden(chip):
-        first, second = both(chip, slice(0, hidden_rows))
+    def unpack_hidden(step):
+        first, second = both(step, slice(0, hidden_rows))
         tiles = joined(unpacked_half(first, tokens), unpacked_half(second, tokens))
-        hidden_ref[chip] = jnp.concatenate(tiles, axis=1).astype(jnp.bfloat16)
-
-    def unpack_teacher(chip):
-        first, second = both(chip, slice(hidden_rows, own_ref.shape[1]))
+        hidden_ref[step] = jnp.concatenate(tiles, axis=1).astype(jnp.bfloat16)
+
+    def unpack_teacher(step):
+        first, second = both(step, slice(hidden_rows, near[0].shape[0]))
         share = first.shape[0] // 2
         first = jnp.where(core == 0, first[:share], first[share:])
         second = jnp.where(core == 0, second[:share], second[share:])
@@ -278,7 +263,8 @@
             one, two = first[row : row + 2 * slots], second[row : row + 2 * slots]
             tiles.append(jnp.where(upper, one, pltpu.roll(two, slots, 0)))
             tiles.append(jnp.where(upper, pltpu.roll(one, slots, 0), two))
-        arrived_ref[2 * slots * chip : 2 * slots * (chip + 1)] = jnp.concatenate(tiles, axis=1)
+        rows = pl.ds(pl.multiple_of(2 * slots * sources[step], 2 * slots), 2 * slots)
+        arrived_ref[rows] = jnp.concatenate(tiles, axis=1)
 
     unpack_hidden(0)
     logits = jnp.zeros((tokens, shard_rows), jnp.float32)
@@ -318,9 +304,11 @@
     entry = lax.broadcasted_iota(jnp.int32, (tokens, shard_rows), 1)
     hit = entry == tokens_ref[:, :1].astype(jnp.int32)
     target = jnp.sum(jnp.where(hit, logits, 0.0), axis=1, keepdims=True)
-    rows_ref[:tokens] = (exps * (gap - centre)).astype(jnp.bfloat16)
-    rows_ref[tokens : 2 * tokens] = exps.astype(jnp.bfloat16)
-    rows_ref[2 * tokens :] = hit.astype(jnp.bfloat16)
+    made_ref[:tokens] = (exps * (gap - centre)).astype(jnp.bfloat16)
+    made_ref[tokens : 2 * tokens] = exps.astype(jnp.bfloat16)
+    made_ref[2 * tokens :] = hit.astype(jnp.bfloat16)
+    out = pltpu.make_async_copy(made_ref, rows_ref, made_sem)
+    out.start()
 
     lane = lax.broadcasted_iota(jnp.int32, (tokens, LANES), 1)
     table = jnp.zeros((tokens, LANES), jnp.float32)
@@ -330,32 +318,28 @@
         table = jnp.where(lane == place, column, table)
     stats = jnp.concatenate([table, jnp.zeros((stats_ref.shape[2] - tokens, LANES), jnp.float32)])
     stats_ref[...] = jnp.broadcast_to(stats.T[None, :STATS], stats_ref.shape)
+    out.wait()
 
 
 def products_kernel(
-    place_ref, rows_ref, head_ref, terms_ref, picks_ref, held_ref, made_ref, sems, made_sems
+    place_ref, rows_ref, head_ref, terms_ref, picks_ref, held_ref, made_ref, sems, made_sem
 ):
-    copies = head_copies(head_ref, held_ref, sems, place_ref[0] // 2)
+    into = pltpu.make_async_copy(rows_ref, made_ref, made_sem)
+    into.start()
+    chips = held_ref.shape[0]
+    targets = [lax.rem(place_ref[0] // 2 + step, chips) for step in range(chips)]
+    copies = head_copies(head_ref, held_ref, sems, targets)
     for copy in copies[:AHEAD]:
         copy.start()
+    into.wait()
     sums_rows = terms_ref.shape[1]
-    outs = []
     for step, copy in enumerate(copies):
         copy.wait()
         if step + AHEAD < len(copies):
             copies[step + AHEAD].start()
-        made_ref[step] = jnp.dot(
-            rows_ref[sums_rows:], held_ref[step], preferred_element_type=jnp.float32
-        ).astype(jnp.bfloat16)
-        outs.append(
-            pltpu.make_async_copy(made_ref.at[step], picks_ref.at[step], made_sems.at[step])
-        )
-        outs[-1].start()
-        terms_ref[step] = jnp.dot(
-            rows_ref[:sums_rows], held_ref[step], preferred_element_type=jnp.float32
-        )
-    for out in outs:
-        out.wait()
+        products = jnp.dot(made_ref[...], held_ref[step], preferred_element_type=jnp.float32)
+        terms_ref[step] = products[:sums_rows]
+        picks_ref[step] = products[sums_rows:].astype(jnp.bfloat16)
 
 
 def combine_kernel(
@@ -368,11 +352,7 @@
     keep_ref,
     give_ref,
     loss_ref,
-    got_ref,
-    sem,
 ):
-    into = pltpu.make_async_copy(picks_ref, got_ref, sem)
-    into.start()
     core = place_ref[0] % 2
     chips, _, width = terms_ref.shape
     tokens = tokens_ref.shape[0]
@@ -401,11 +381,10 @@
     factor = share * columns[:, 0:1]
     level = columns[:, 1:2]
     weight = sample_weight * share
-    into.wait()
     for step in range(chips):
         block = (
             factor * (terms_ref[step, :tokens] + level * terms_ref[step, tokens:])
-            - weight * got_ref[step].astype(jnp.float32)
+            - weight * picks_ref[step].astype(jnp.float32)
         )
         first, second = parted([block[:, i : i + LANES] for i in range(0, width, LANES)])
         first, second = packed_half(first), packed_half(second)
@@ -418,7 +397,7 @@
     total = own_ref[...]
     for share_ref in refs[:-1]:
         total += share_ref[...].astype(jnp.float32)
-    tiles = jnp.concatenate(unpacked_half(total * scale_ref[0], tokens), axis=1)
+    tiles = jnp.concatenate(unpacked_half(total * scale_ref[...], tokens), axis=1)
     refs[-1][...] = tiles[:, :half].astype(refs[-1].dtype)
 
 
@@ -439,7 +418,8 @@
     head = in_hbm(head)
     head_scratch = pltpu.VMEM((chips, shard_rows, width), head.dtype)
     head_sems = pltpu.SemaphoreType.DMA((chips,))
-    picks_scratch = pltpu.VMEM((chips, tokens, width), jnp.bfloat16)
+    rows_scratch = pltpu.VMEM((3 * tokens, shard_rows), jnp.bfloat16)
+    rows_sem = pltpu.SemaphoreType.DMA
     slots, entries = teacher_values.shape
     hidden_rows = tokens * half // LANES
     teacher_rows = 2 * slots * (shard_rows + LANES // 2) // LANES
@@ -469,30 +449,36 @@
         compiler_params=params,
         name="pack",
     )(place, *[in_hbm(operand) for operand in operands])
-    gathered = across_chips(packed)
-    other = swap_cores(gathered)
+    steps = range(1, chips)
+    near = [packed[0]] + [along_chips(packed[step], step) for step in steps]
+    far = [
+        swap_cores(jnp.stack(near[: chips // 2])),
+        swap_cores(jnp.stack(near[chips // 2 :])),
+    ]
 
     rows, stats = pl.pallas_call(
-        logits_kernel,
+        functools.partial(logits_kernel, chips=chips),
         out_shape=(
-            vmem_array((3 * tokens, shard_rows), jnp.bfloat16),
+            hbm_array((3 * tokens, shard_rows), jnp.bfloat16),
             jax.ShapeDtypeStruct((count, STATS, pl.cdiv(tokens, LANES) * LANES), jnp.float32),
         ),
-        in_specs=[smem] + [vmem] * 4 + [hbm],
-        out_specs=[vmem] * 2,
+        in_specs=[smem] + [vmem] * (chips + 4) + [hbm],
+        out_specs=[hbm, vmem],
         scratch_shapes=[
             head_scratch,
+            rows_scratch,
             pltpu.VMEM((chips, tokens, width), jnp.bfloat16),
             pltpu.VMEM((tokens, shard_rows + LANES // 2), jnp.float32),
             pltpu.VMEM((tokens, shard_rows), jnp.float32),
             head_sems,
+            rows_sem,
         ],
         compiler_params=params,
         cost_estimate=pl.CostEstimate(
             flops=2 * tokens * head.size, bytes_accessed=2 * head.size, transcendentals=0
         ),
         name="logits",
-    )(place, gathered, other, in_vmem(owner), in_vmem(table), head)
+    )(place, *near, *far, in_vmem(owner), in_vmem(table), head)
 
     all_stats = lax.all_to_all(stats, "vocab", split_axis=0, concat_axis=0, tiled=True)
 
@@ -500,17 +486,17 @@
         products_kernel,
         out_shape=(
             vmem_array((chips, 2 * tokens, width), jnp.float32),
-            hbm_array((chips, tokens, width), jnp.bfloat16),
+            vmem_array((chips, tokens, width), jnp.bfloat16),
         ),
-        in_specs=[smem, vmem, hbm],
-        out_specs=[vmem, hbm],
-        scratch_shapes=[head_scratch, picks_scratch, head_sems, head_sems],
+        in_specs=[smem, hbm, hbm],
+        out_specs=[vmem] * 2,
+        scratch_shapes=[head_scratch, rows_scratch, head_sems, rows_sem],
         compiler_params=params,
         cost_estimate=pl.CostEstimate(
             flops=6 * tokens * head.size, bytes_accessed=2 * head.size, transcendentals=0
         ),
         name="products",
-    )(place, in_vmem(rows), head)
+    )(place, in_hbm(rows), head)
 
     keep, give, loss = pl.pallas_call(
         combine_kernel,
@@ -519,24 +505,22 @@
             vmem_array((chips, hidden_rows, LANES), jnp.bfloat16),
             jax.ShapeDtypeStruct((1, 1), jnp.float32),
         ),
-        in_specs=[smem] + [vmem] * 4 + [hbm],
+        in_specs=[smem] + [vmem] * 5,
         out_specs=[vmem] * 3,
-        scratch_shapes=[picks_scratch, pltpu.SemaphoreType.DMA],
         compiler_params=params,
         name="combine",
-    )(place, all_stats, stats, in_vmem(table), in_vmem(terms), in_hbm(picks))
+    )(place, all_stats, stats, in_vmem(table), in_vmem(terms), in_vmem(picks))
 
     sums = keep + swap_cores(give).astype(jnp.float32)
-    steps = range(1, chips)
     shares = [along_chips(sums[step].astype(jnp.bfloat16), step) for step in steps]
     total = pl.pallas_call(
         sum_kernel,
         out_shape=jax.ShapeDtypeStruct((tokens, half), jnp.bfloat16),
-        in_specs=[smem] + [vmem] * chips,
+        in_specs=[vmem] * (chips + 1),
         out_specs=vmem,
         compiler_params=params,
         name="total",
-    )(loss_scale, sums[0], *shares)
+    )(loss_scale[None, :], sums[0], *shares)
     return total, jnp.reshape(loss, (1,))
 
 

time: 65.3 us -> 63.1 us (0.966)
  blocking collectives: 20.9 us -> 0 us
  starting transfers between devices: 16.7 us -> 30.3 us
  waiting for transfers between devices: 5.63 us -> 11.9 us
  Pallas kernels: 20.2 us -> 18.9 us
    all_to_all x1 -> x0, blocking collectives: 20.9 us -> none  [across_chips(): lax.all_to_all(blocks, 'vocab', split_axis=0, concat_axis=0, axis_index_g...]
    ppermute x7 -> x14, starting transfers between devices: 12.6 us -> 25.3 us  [along_chips(): lax.ppermute(array, 'vocab', [(i, (i + 2 * step) % count) for i in range(...]
    ppermute x7 -> x14, waiting for transfers between devices: 2.51 us -> 8.2 us  [along_chips(): lax.ppermute(array, 'vocab', [(i, (i + 2 * step) % count) for i in range(...]
    pallas_call x1, Pallas kernels: 7.77 us -> 6.28 us  [paired_shards(): pl.pallas_call(products_kernel, out_shape=(vmem_array((chips, 2 * tokens,...]
    all_to_all x1, starting transfers between devices: 3.7 us -> 4.88 us  [paired_shards(): lax.all_to_all(stats, 'vocab', split_axis=0, concat_axis=0, tiled=True)]
    pallas_call x1, Pallas kernels: 7.67 us -> 8.45 us  [paired_shards(): pl.pallas_call(functools.partial(logits_kernel, chips=chips), out_shape=(...]
    pallas_call x1, Pallas kernels: 2.51 us -> 1.84 us  [paired_shards(): pl.pallas_call(combine_kernel, out_shape=(vmem_array((chips, hidden_rows,...]
    ppermute x2 -> x3, waiting for transfers between devices: 3.12 us -> 3.12 us  [swap_cores(): return lax.ppermute(array, 'vocab', [(i, i ^ 1) for i in range(count)])]
  transfers between devices with their start and end apart: 10 -> 18, of which waited for: 5 -> 8; matrix products, arithmetic and copies ran while one was open for 0% -> 0% of each run, Pallas kernels for 12% -> 10%
where the time goes in v10:
time: 63.1 us; the launch traced here: 62.8 us
  starting transfers between devices  30.3 us (48%)
  Pallas kernels  18.9 us (30%)
  waiting for transfers between devices  11.9 us (19%)
  between operations  1.41 us (2%)
    ppermute x14, starting transfers between devices, along_chips(): lax.ppermute(array, 'vocab', [(i, (i + 2 * step) % count) for i in range(...  25.3 us
    pallas_call x1, Pallas kernels, paired_shards(): pl.pallas_call(functools.partial(logits_kernel, chips=chips), out_shape=(...  8.45 us
    ppermute x14, waiting for transfers between devices, along_chips(): lax.ppermute(array, 'vocab', [(i, (i + 2 * step) % count) for i in range(...  8.2 us
    pallas_call x1, Pallas kernels, paired_shards(): pl.pallas_call(products_kernel, out_shape=(vmem_array((chips, 2 * tokens,...  6.28 us
    all_to_all x1, starting transfers between devices, paired_shards(): lax.all_to_all(stats, 'vocab', split_axis=0, concat_axis=0, tiled=True)  4.88 us
    ppermute x3, waiting for transfers between devices, swap_cores(): return lax.ppermute(array, 'vocab', [(i, i ^ 1) for i in range(count)])  3.12 us
    pallas_call x1, Pallas kernels, paired_shards(): pl.pallas_call(combine_kernel, out_shape=(vmem_array((chips, hidden_rows,...  1.84 us
    pallas_call x1, Pallas kernels, paired_shards(): pl.pallas_call(functools.partial(pack_kernel, shard_rows=shard_rows), out...  1.52 us
  transfers between devices with their start and end apart: 18, of which 8 were waited for; matrix products, arithmetic and copies ran while one was open for 0% of the time, Pallas kernels for 10%

profile of v10, /device:TPU:0, one launch (start us, length us, event | category | flops | bytes accessed | tf_op | source)
XLA Modules:
  0.0 62.8 jit_solution(16549922631015939227)
XLA Ops:
  0.6 1.5 %pack.1 = (bf16[8,240,128]{2,1,0:T(8,128)(2,1)S(1)}, bf16[64,64]{1,0:T(8,128)(2,1)S(1)}, f32[64,128]{1,0:T(8,128)S(1)}) custom-call(s32[1]{0:T(128)} %bitcast.1.place_ref, bf16[64,320]{1,0:T(8,128)(2,1)} %refs_0_.1, bf16[4,19456]{1,0:T(4,128)(2,1)} %refs_1_.1, f32[4,608]{1,0:T(4,128)} %refs_2_.1, s32[1,64]{1,0:T(1,128)} %bitcast.53, s32[1,64]{1,0:T(1,128)} %bitcast.54, ...), custom_call_target="tpu_custom_call" | custom-call | tf_op jit(solution)/shard_map/pack/pallas_call | solution.py:435
  2.2 4.1 %collective-permute-start.3 = (bf16[240,128]{1,0:T(8,128)(2,1)S(1)}, bf16[240,128]{1,0:T(8,128)(2,1)S(1)}, u32[]{:S(2)}, u32[]{:S(2)}) collective-permute-start(bf16[240,128]{1,0:T(8,128)(2,1)S(1)} %get-tuple-element.29), channel_id=1, source_target_pairs={{0,8},{1,9},{2,10},{3,11},{4,12},{5,13},{6,14},{7,15},{8,0},{9,1},... | collective-permute-start | bytes 184328 | tf_op jit(solution)/shard_map/ppermute | solution.py:51
  6.3 1.3 %collective-permute-start.4 = (bf16[240,128]{1,0:T(8,128)(2,1)S(1)}, bf16[240,128]{1,0:T(8,128)(2,1)S(1)}, u32[]{:S(2)}, u32[]{:S(2)}) collective-permute-start(bf16[240,128]{1,0:T(8,128)(2,1)S(1)} %get-tuple-element.28), channel_id=1, source_target_pairs={{0,10},{1,11},{2,12},{3,13},{4,14},{5,15},{6,0},{7,1},{8,2},{9,3},... | collective-permute-start | bytes 184328 | tf_op jit(solution)/shard_map/ppermute | solution.py:51
  7.6 3.6 %collective-permute-start.5 = (bf16[240,128]{1,0:T(8,128)(2,1)S(1)}, bf16[240,128]{1,0:T(8,128)(2,1)S(1)}, u32[]{:S(2)}, u32[]{:S(2)}) collective-permute-start(bf16[240,128]{1,0:T(8,128)(2,1)S(1)} %get-tuple-element.27), channel_id=1, source_target_pairs={{0,12},{1,13},{2,14},{3,15},{4,0},{5,1},{6,2},{7,3},{8,4},{9,5},{1... | collective-permute-start | bytes 184328 | tf_op jit(solution)/shard_map/ppermute | solution.py:51
  11.7 1.5 %collective-permute-start = (bf16[240,128]{1,0:T(8,128)(2,1)S(1)}, bf16[240,128]{1,0:T(8,128)(2,1)S(1)}, u32[]{:S(2)}, u32[]{:S(2)}) collective-permute-start(bf16[240,128]{1,0:T(8,128)(2,1)S(1)} %get-tuple-element.32), channel_id=1, source_target_pairs={{0,2},{1,3},{2,4},{3,5},{4,6},{5,7},{6,8},{7,9},{8,10},{9,11},{10,... | collective-permute-start | bytes 184328 | tf_op jit(solution)/shard_map/ppermute | solution.py:51
  13.3 2.3 %collective-permute-start.2 = (bf16[240,128]{1,0:T(8,128)(2,1)S(1)}, bf16[240,128]{1,0:T(8,128)(2,1)S(1)}, u32[]{:S(2)}, u32[]{:S(2)}) collective-permute-start(bf16[240,128]{1,0:T(8,128)(2,1)S(1)} %get-tuple-element.30), channel_id=1, source_target_pairs={{0,6},{1,7},{2,8},{3,9},{4,10},{5,11},{6,12},{7,13},{8,14},{9,15},... | collective-permute-start | bytes 184328 | tf_op jit(solution)/shard_map/ppermute | solution.py:51
  15.7 3.1 %collective-permute-done.refs_1_ = bf16[240,128]{1,0:T(8,128)(2,1)S(1)} collective-permute-done((bf16[240,128]{1,0:T(8,128)(2,1)S(1)}, bf16[240,128]{1,0:T(8,128)(2,1)S(1)}, u32[]{:S(2)}, u32[]{:S(2)}) %collective-permute-start) | collective-permute-done | bytes 61472 | tf_op jit(solution)/shard_map/ppermute | solution.py:51
  19.3 2.1 %collective-permute-done.2.refs_3_ = bf16[240,128]{1,0:T(8,128)(2,1)S(1)} collective-permute-done((bf16[240,128]{1,0:T(8,128)(2,1)S(1)}, bf16[240,128]{1,0:T(8,128)(2,1)S(1)}, u32[]{:S(2)}, u32[]{:S(2)}) %collective-permute-start.2) | collective-permute-done | bytes 61472 | tf_op jit(solution)/shard_map/ppermute | solution.py:51
  21.5 1.5 %collective-permute-done.7.refs_8_ = bf16[4,240,128]{2,1,0:T(8,128)(2,1)S(1)} collective-permute-done((bf16[4,240,128]{2,1,0:T(8,128)(2,1)S(1)}, bf16[4,240,128]{2,1,0:T(8,128)(2,1)S(1)}, u32[]{:S(2)}, u32[]{:S(2)}) %collective-permute-start.7) | collective-permute-done | bytes 245792 | tf_op jit(solution)/shard_map/ppermute | solution.py:46
  23.0 8.4 %logits.1 = (bf16[192,1216]{1,0:T(8,128)(2,1)}, f32[16,8,128]{2,1,0:T(8,128)}) custom-call(s32[1]{0:T(128)} %bitcast.1.place_ref, bf16[240,128]{1,0:T(8,128)(2,1)S(1)} %get-tuple-element.25.refs_0_, bf16[240,128]{1,0:T(8,128)(2,1)S(1)} %collective-permute-done.refs_1_, bf16[240,128]{1,0:T(8,128)(2,1)S(1)} %collective-permute-done.1.refs_2_, ...), custom_call_target="tpu_custom_call" | custom-call | flops 796917760 | bytes 12451840 | tf_op jit(solution)/shard_map/logits/pallas_call | solution.py:459
  31.4 4.9 %all-to-all-start = ((f32[16,8,128]{2,1,0:T(8,128)}), f32[16,8,128]{2,1,0:T(8,128)S(1)}, u32[]{:S(2)}, u32[]{:S(2)}) async-start(f32[16,8,128]{2,1,0:T(8,128)} %get-tuple-element.15.own_ref), calls=%async_computation | async-start | bytes 131072 | tf_op jit(solution)/shard_map/all_to_all | solution.py:483
  36.3 6.3 %products.1 = (f32[8,128,640]{2,1,0:T(8,128)S(1)}, bf16[8,64,640]{2,1,0:T(8,128)(2,1)S(1)}) custom-call(s32[1]{0:T(128)} %bitcast.1.place_ref, bf16[192,1216]{1,0:T(8,128)(2,1)} %get-tuple-element.16.rows_ref, bf16[1216,5120]{1,0:T(8,128)(2,1)} %head_ref.1), custom_call_target="tpu_custom_call" | custom-call | flops 2390753280 | bytes 12451840 | tf_op jit(solution)/shard_map/products/pallas_call | solution.py:485
  43.2 1.8 %combine.1 = (f32[8,160,128]{2,1,0:T(8,128)S(1)}, bf16[8,160,128]{2,1,0:T(8,128)(2,1)S(1)}, f32[1,1]{1,0:T(1,128)}) custom-call(s32[1]{0:T(128)} %bitcast.1.place_ref, f32[16,8,128]{2,1,0:T(8,128)S(1)} %all-to-all-done.stats_ref, f32[16,8,128]{2,1,0:T(8,128)} %get-tuple-element.15.own_ref, f32[64,128]{1,0:T(8,128)S(1)} %get-tuple-element.14.refs_11_.tokens_ref, ...), custom_call_target="tpu_custom_call" | custom-call | tf_op jit(solution)/shard_map/combine/pallas_call | solution.py:501
  45.1 1.6 %collective-permute-done.9 = bf16[8,160,128]{2,1,0:T(8,128)(2,1)S(1)} collective-permute-done((bf16[8,160,128]{2,1,0:T(8,128)(2,1)S(1)}, bf16[8,160,128]{2,1,0:T(8,128)(2,1)S(1)}, u32[]{:S(2)}, u32[]{:S(2)}) %collective-permute-start.9) | collective-permute-done | bytes 327712 | tf_op jit(solution)/shard_map/ppermute | solution.py:46
  46.8 1.4 %collective-permute-start.10 = (bf16[160,128]{1,0:T(8,128)(2,1)S(1)}, bf16[160,128]{1,0:T(8,128)(2,1)S(1)}, u32[]{:S(2)}, u32[]{:S(2)}) collective-permute-start(bf16[160,128]{1,0:T(8,128)(2,1)S(1)} %get-tuple-element.39), channel_id=1, source_target_pairs={{0,2},{1,3},{2,4},{3,5},{4,6},{5,7},{6,8},{7,9},{8,10},{9,11},{10,... | collective-permute-start | bytes 122888 | tf_op jit(solution)/shard_map/ppermute | solution.py:51
  48.2 1.5 %collective-permute-start.11 = (bf16[160,128]{1,0:T(8,128)(2,1)S(1)}, bf16[160,128]{1,0:T(8,128)(2,1)S(1)}, u32[]{:S(2)}, u32[]{:S(2)}) collective-permute-start(bf16[160,128]{1,0:T(8,128)(2,1)S(1)} %get-tuple-element.38), channel_id=1, source_target_pairs={{0,4},{1,5},{2,6},{3,7},{4,8},{5,9},{6,10},{7,11},{8,12},{9,13},{1... | collective-permute-start | bytes 122888 | tf_op jit(solution)/shard_map/ppermute | solution.py:51
  50.3 2.4 %collective-permute-start.12 = (bf16[160,128]{1,0:T(8,128)(2,1)S(1)}, bf16[160,128]{1,0:T(8,128)(2,1)S(1)}, u32[]{:S(2)}, u32[]{:S(2)}) collective-permute-start(bf16[160,128]{1,0:T(8,128)(2,1)S(1)} %get-tuple-element.37), channel_id=1, source_target_pairs={{0,6},{1,7},{2,8},{3,9},{4,10},{5,11},{6,12},{7,13},{8,14},{9,15},... | collective-permute-start | bytes 122888 | tf_op jit(solution)/shard_map/ppermute | solution.py:51
  52.7 1.5 %collective-permute-start.13 = (bf16[160,128]{1,0:T(8,128)(2,1)S(1)}, bf16[160,128]{1,0:T(8,128)(2,1)S(1)}, u32[]{:S(2)}, u32[]{:S(2)}) collective-permute-start(bf16[160,128]{1,0:T(8,128)(2,1)S(1)} %get-tuple-element.36), channel_id=1, source_target_pairs={{0,8},{1,9},{2,10},{3,11},{4,12},{5,13},{6,14},{7,15},{8,0},{9,1},... | collective-permute-start | bytes 122888 | tf_op jit(solution)/shard_map/ppermute | solution.py:51
  54.2 2.4 %collective-permute-start.14 = (bf16[160,128]{1,0:T(8,128)(2,1)S(1)}, bf16[160,128]{1,0:T(8,128)(2,1)S(1)}, u32[]{:S(2)}, u32[]{:S(2)}) collective-permute-start(bf16[160,128]{1,0:T(8,128)(2,1)S(1)} %get-tuple-element.35), channel_id=1, source_target_pairs={{0,10},{1,11},{2,12},{3,13},{4,14},{5,15},{6,0},{7,1},{8,2},{9,3},... | collective-permute-start | bytes 122888 | tf_op jit(solution)/shard_map/ppermute | solution.py:51
  56.6 1.4 %collective-permute-start.15 = (bf16[160,128]{1,0:T(8,128)(2,1)S(1)}, bf16[160,128]{1,0:T(8,128)(2,1)S(1)}, u32[]{:S(2)}, u32[]{:S(2)}) collective-permute-start(bf16[160,128]{1,0:T(8,128)(2,1)S(1)} %get-tuple-element.34), channel_id=1, source_target_pairs={{0,12},{1,13},{2,14},{3,15},{4,0},{5,1},{6,2},{7,3},{8,4},{9,5},{1... | collective-permute-start | bytes 122888 | tf_op jit(solution)/shard_map/ppermute | solution.py:51
  58.0 1.5 %collective-permute-start.16 = (bf16[160,128]{1,0:T(8,128)(2,1)S(1)}, bf16[160,128]{1,0:T(8,128)(2,1)S(1)}, u32[]{:S(2)}, u32[]{:S(2)}) collective-permute-start(bf16[160,128]{1,0:T(8,128)(2,1)S(1)} %get-tuple-element.33), channel_id=1, source_target_pairs={{0,14},{1,15},{2,0},{3,1},{4,2},{5,3},{6,4},{7,5},{8,6},{9,7},{10,... | collective-permute-start | bytes 122888 | tf_op jit(solution)/shard_map/ppermute | solution.py:51
  59.5 1.1 %collective-permute-done.15.refs_5_ = bf16[160,128]{1,0:T(8,128)(2,1)S(1)} collective-permute-done((bf16[160,128]{1,0:T(8,128)(2,1)S(1)}, bf16[160,128]{1,0:T(8,128)(2,1)S(1)}, u32[]{:S(2)}, u32[]{:S(2)}) %collective-permute-start.15) | collective-permute-done | bytes 40992 | tf_op jit(solution)/shard_map/ppermute | solution.py:51
  60.6 1.4 %collective-permute-done.16.refs_6_ = bf16[160,128]{1,0:T(8,128)(2,1)S(1)} collective-permute-done((bf16[160,128]{1,0:T(8,128)(2,1)S(1)}, bf16[160,128]{1,0:T(8,128)(2,1)S(1)}, u32[]{:S(2)}, u32[]{:S(2)}) %collective-permute-start.16) | collective-permute-done | bytes 40992 | tf_op jit(solution)/shard_map/ppermute | solution.py:51
  62.0 0.8 %total.1 = bf16[64,320]{1,0:T(8,128)(2,1)} custom-call(f32[1,1]{1,0:T(1,128)} %bitcast.45.scale_ref, f32[160,128]{1,0:T(8,128)S(1)} %slice_bitcast_fusion.own_ref, bf16[160,128]{1,0:T(8,128)(2,1)S(1)} %collective-permute-done.10.refs_0_, bf16[160,128]{1,0:T(8,128)(2,1)S(1)} %collective-permute-done.11.refs_1_, ...), custom_call_target="tpu_custom_call" | custom-call | tf_op jit(solution)/shard_map/total/pallas_call | solution.py:516
  (23 shorter events, 2.0 us)
Async XLA Ops:
  2.2 11.0 %collective-permute-start.3 = (bf16[240,128]{1,0:T(8,128)(2,1)S(1)}, bf16[240,128]{1,0:T(8,128)(2,1)S(1)}, u32[]{:S(2)}, u32[]{:S(2)}) collective-permute-start(bf16[240,128]{1,0:T(8,128)(2,1)S(1)} %get-tuple-element.29), channel_id=1, source_target_pairs={{0,8},{1,9},{2,10},{3,11},{4,12},{5,13},{6,14},{7,15},{8,0},{9,1},... | collective-permute-start | bytes 184328 | tf_op jit(solution)/shard_map/ppermute | solution.py:51
  6.3 6.9 %collective-permute-start.4 = (bf16[240,128]{1,0:T(8,128)(2,1)S(1)}, bf16[240,128]{1,0:T(8,128)(2,1)S(1)}, u32[]{:S(2)}, u32[]{:S(2)}) collective-permute-start(bf16[240,128]{1,0:T(8,128)(2,1)S(1)} %get-tuple-element.28), channel_id=1, source_target_pairs={{0,10},{1,11},{2,12},{3,13},{4,14},{5,15},{6,0},{7,1},{8,2},{9,3},... | collective-permute-start | bytes 184328 | tf_op jit(solution)/shard_map/ppermute | solution.py:51
  7.6 7.9 %collective-permute-start.5 = (bf16[240,128]{1,0:T(8,128)(2,1)S(1)}, bf16[240,128]{1,0:T(8,128)(2,1)S(1)}, u32[]{:S(2)}, u32[]{:S(2)}) collective-permute-start(bf16[240,128]{1,0:T(8,128)(2,1)S(1)} %get-tuple-element.27), channel_id=1, source_target_pairs={{0,12},{1,13},{2,14},{3,15},{4,0},{5,1},{6,2},{7,3},{8,4},{9,5},{1... | collective-permute-start | bytes 184328 | tf_op jit(solution)/shard_map/ppermute | solution.py:51
  11.2 4.3 %collective-permute-start.6 = (bf16[240,128]{1,0:T(8,128)(2,1)S(1)}, bf16[240,128]{1,0:T(8,128)(2,1)S(1)}, u32[]{:S(2)}, u32[]{:S(2)}) collective-permute-start(bf16[240,128]{1,0:T(8,128)(2,1)S(1)} %get-tuple-element.26), channel_id=1, source_target_pairs={{0,14},{1,15},{2,0},{3,1},{4,2},{5,3},{6,4},{7,5},{8,6},{9,7},{10,... | collective-permute-start | bytes 184328 | tf_op jit(solution)/shard_map/ppermute | solution.py:51
  11.7 7.1 %collective-permute-start = (bf16[240,128]{1,0:T(8,128)(2,1)S(1)}, bf16[240,128]{1,0:T(8,128)(2,1)S(1)}, u32[]{:S(2)}, u32[]{:S(2)}) collective-permute-start(bf16[240,128]{1,0:T(8,128)(2,1)S(1)} %get-tuple-element.32), channel_id=1, source_target_pairs={{0,2},{1,3},{2,4},{3,5},{4,6},{5,7},{6,8},{7,9},{8,10},{9,11},{10,... | collective-permute-start | bytes 184328 | tf_op jit(solution)/shard_map/ppermute | solution.py:51
  13.2 6.0 %collective-permute-start.1 = (bf16[240,128]{1,0:T(8,128)(2,1)S(1)}, bf16[240,128]{1,0:T(8,128)(2,1)S(1)}, u32[]{:S(2)}, u32[]{:S(2)}) collective-permute-start(bf16[240,128]{1,0:T(8,128)(2,1)S(1)} %get-tuple-element.31), channel_id=1, source_target_pairs={{0,4},{1,5},{2,6},{3,7},{4,8},{5,9},{6,10},{7,11},{8,12},{9,13},{1... | collective-permute-start | bytes 184328 | tf_op jit(solution)/shard_map/ppermute | solution.py:51
  13.3 8.1 %collective-permute-start.2 = (bf16[240,128]{1,0:T(8,128)(2,1)S(1)}, bf16[240,128]{1,0:T(8,128)(2,1)S(1)}, u32[]{:S(2)}, u32[]{:S(2)}) collective-permute-start(bf16[240,128]{1,0:T(8,128)(2,1)S(1)} %get-tuple-element.30), channel_id=1, source_target_pairs={{0,6},{1,7},{2,8},{3,9},{4,10},{5,11},{6,12},{7,13},{8,14},{9,15},... | collective-permute-start | bytes 184328 | tf_op jit(solution)/shard_map/ppermute | solution.py:51
  15.6 5.9 %collective-permute-start.8 = (bf16[4,240,128]{2,1,0:T(8,128)(2,1)S(1)}, bf16[4,240,128]{2,1,0:T(8,128)(2,1)S(1)}, u32[]{:S(2)}, u32[]{:S(2)}) collective-permute-start(bf16[4,240,128]{2,1,0:T(8,128)(2,1)S(1)} %pad_maximum_fusion.1), channel_id=1, source_target_pairs={{0,1},{1,0},{2,3},{3,2},{4,5},{5,4},{6,7},{7,6},{8,9},{9,8},{10,11... | collective-permute-start | bytes 737288 | tf_op jit(solution)/shard_map/ppermute | solution.py:46
  21.4 1.6 %collective-permute-start.7 = (bf16[4,240,128]{2,1,0:T(8,128)(2,1)S(1)}, bf16[4,240,128]{2,1,0:T(8,128)(2,1)S(1)}, u32[]{:S(2)}, u32[]{:S(2)}) collective-permute-start(bf16[4,240,128]{2,1,0:T(8,128)(2,1)S(1)} %pad_maximum_fusion), channel_id=1, source_target_pairs={{0,1},{1,0},{2,3},{3,2},{4,5},{5,4},{6,7},{7,6},{8,9},{9,8},{10,11... | collective-permute-start | bytes 737288 | tf_op jit(solution)/shard_map/ppermute | solution.py:46
  31.4 11.8 %all-to-all-start = ((f32[16,8,128]{2,1,0:T(8,128)}), f32[16,8,128]{2,1,0:T(8,128)S(1)}, u32[]{:S(2)}, u32[]{:S(2)}) async-start(f32[16,8,128]{2,1,0:T(8,128)} %get-tuple-element.15.own_ref), calls=%async_computation | async-start | bytes 131072 | tf_op jit(solution)/shard_map/all_to_all | solution.py:483
  45.1 1.6 %collective-permute-start.9 = (bf16[8,160,128]{2,1,0:T(8,128)(2,1)S(1)}, bf16[8,160,128]{2,1,0:T(8,128)(2,1)S(1)}, u32[]{:S(2)}, u32[]{:S(2)}) collective-permute-start(bf16[8,160,128]{2,1,0:T(8,128)(2,1)S(1)} %get-tuple-element.20), channel_id=1, source_target_pairs={{0,1},{1,0},{2,3},{3,2},{4,5},{5,4},{6,7},{7,6},{8,9},{9,8},{10,11... | collective-permute-start | bytes 983048 | tf_op jit(solution)/shard_map/ppermute | solution.py:46
  46.8 9.8 %collective-permute-start.10 = (bf16[160,128]{1,0:T(8,128)(2,1)S(1)}, bf16[160,128]{1,0:T(8,128)(2,1)S(1)}, u32[]{:S(2)}, u32[]{:S(2)}) collective-permute-start(bf16[160,128]{1,0:T(8,128)(2,1)S(1)} %get-tuple-element.39), channel_id=1, source_target_pairs={{0,2},{1,3},{2,4},{3,5},{4,6},{5,7},{6,8},{7,9},{8,10},{9,11},{10,... | collective-permute-start | bytes 122888 | tf_op jit(solution)/shard_map/ppermute | solution.py:51
  48.2 9.8 %collective-permute-start.11 = (bf16[160,128]{1,0:T(8,128)(2,1)S(1)}, bf16[160,128]{1,0:T(8,128)(2,1)S(1)}, u32[]{:S(2)}, u32[]{:S(2)}) collective-permute-start(bf16[160,128]{1,0:T(8,128)(2,1)S(1)} %get-tuple-element.38), channel_id=1, source_target_pairs={{0,4},{1,5},{2,6},{3,7},{4,8},{5,9},{6,10},{7,11},{8,12},{9,13},{1... | collective-permute-start | bytes 122888 | tf_op jit(solution)/shard_map/ppermute | solution.py:51
  50.3 9.2 %collective-permute-start.12 = (bf16[160,128]{1,0:T(8,128)(2,1)S(1)}, bf16[160,128]{1,0:T(8,128)(2,1)S(1)}, u32[]{:S(2)}, u32[]{:S(2)}) collective-permute-start(bf16[160,128]{1,0:T(8,128)(2,1)S(1)} %get-tuple-element.37), channel_id=1, source_target_pairs={{0,6},{1,7},{2,8},{3,9},{4,10},{5,11},{6,12},{7,13},{8,14},{9,15},... | collective-permute-start | bytes 122888 | tf_op jit(solution)/shard_map/ppermute | solution.py:51
  52.7 6.8 %collective-permute-start.13 = (bf16[160,128]{1,0:T(8,128)(2,1)S(1)}, bf16[160,128]{1,0:T(8,128)(2,1)S(1)}, u32[]{:S(2)}, u32[]{:S(2)}) collective-permute-start(bf16[160,128]{1,0:T(8,128)(2,1)S(1)} %get-tuple-element.36), channel_id=1, source_target_pairs={{0,8},{1,9},{2,10},{3,11},{4,12},{5,13},{6,14},{7,15},{8,0},{9,1},... | collective-permute-start | bytes 122888 | tf_op jit(solution)/shard_map/ppermute | solution.py:51
  54.2 5.3 %collective-permute-start.14 = (bf16[160,128]{1,0:T(8,128)(2,1)S(1)}, bf16[160,128]{1,0:T(8,128)(2,1)S(1)}, u32[]{:S(2)}, u32[]{:S(2)}) collective-permute-start(bf16[160,128]{1,0:T(8,128)(2,1)S(1)} %get-tuple-element.35), channel_id=1, source_target_pairs={{0,10},{1,11},{2,12},{3,13},{4,14},{5,15},{6,0},{7,1},{8,2},{9,3},... | collective-permute-start | bytes 122888 | tf_op jit(solution)/shard_map/ppermute | solution.py:51
  56.6 4.1 %collective-permute-start.15 = (bf16[160,128]{1,0:T(8,128)(2,1)S(1)}, bf16[160,128]{1,0:T(8,128)(2,1)S(1)}, u32[]{:S(2)}, u32[]{:S(2)}) collective-permute-start(bf16[160,128]{1,0:T(8,128)(2,1)S(1)} %get-tuple-element.34), channel_id=1, source_target_pairs={{0,12},{1,13},{2,14},{3,15},{4,0},{5,1},{6,2},{7,3},{8,4},{9,5},{1... | collective-permute-start | bytes 122888 | tf_op jit(solution)/shard_map/ppermute | solution.py:51
  58.0 4.0 %collective-permute-start.16 = (bf16[160,128]{1,0:T(8,128)(2,1)S(1)}, bf16[160,128]{1,0:T(8,128)(2,1)S(1)}, u32[]{:S(2)}, u32[]{:S(2)}) collective-permute-start(bf16[160,128]{1,0:T(8,128)(2,1)S(1)} %get-tuple-element.33), channel_id=1, source_target_pairs={{0,14},{1,15},{2,0},{3,1},{4,2},{5,3},{6,4},{7,5},{8,6},{9,7},{10,... | collective-permute-start | bytes 122888 | tf_op jit(solution)/shard_map/ppermute | solution.py:51

commit v11 on v10

--- a/solution.py
+++ b/solution.py
@@ -227,7 +227,7 @@
 
 
 def logits_kernel(place_ref, *refs, chips):
-    near, far, refs = refs[:chips], refs[chips : chips + 2], refs[chips + 2 :]
+    near, far, refs = refs[:chips][::-1], refs[chips : chips + 2], refs[chips + 2 :]
     owner_ref, tokens_ref, head_ref, rows_ref, stats_ref = refs[:5]
     held_ref, made_ref, hidden_ref, arrived_ref, teacher_ref, sems, made_sem = refs[5:]
     place = place_ref[0] // 2
@@ -244,8 +244,9 @@
 
     def both(step, rows):
         own = near[step][rows].astype(jnp.float32)
-        group = far[step // (chips // 2)]
-        other = group[step % (chips // 2), rows].astype(jnp.float32)
+        late = step > chips // 2
+        group = far[0] if late else far[1]
+        other = group[step - chips // 2 - 1 if late else step, rows].astype(jnp.float32)
         return jnp.where(core == 0, own, other), jnp.where(core == 0, other, own)
 
     def unpack_hidden(step):
@@ -344,6 +345,7 @@
 
 def combine_kernel(
     place_ref,
+    scale_ref,
     stats_ref,
     own_ref,
     tokens_ref,
@@ -377,10 +379,11 @@
     zeros = jnp.zeros((LANES - 3, tokens), jnp.float32)
     columns = jnp.concatenate([factor, level, per_token, zeros], axis=0).T
     share = tokens_ref[:, 1:2]
+    weight = share * scale_ref[0]
     loss_ref[...] = jnp.sum(share * columns[:, 2:3], axis=0, keepdims=True)
-    factor = share * columns[:, 0:1]
+    factor = weight * columns[:, 0:1]
     level = columns[:, 1:2]
-    weight = sample_weight * share
+    weight = sample_weight * weight
     for step in range(chips):
         block = (
             factor * (terms_ref[step, :tokens] + level * terms_ref[step, tokens:])
@@ -392,12 +395,12 @@
         give_ref[step] = jnp.where(core == 0, second, first).astype(jnp.bfloat16)
 
 
-def sum_kernel(scale_ref, own_ref, *refs):
+def sum_kernel(own_ref, *refs):
     tokens, half = refs[-1].shape
     total = own_ref[...]
     for share_ref in refs[:-1]:
         total += share_ref[...].astype(jnp.float32)
-    tiles = jnp.concatenate(unpacked_half(total * scale_ref[...], tokens), axis=1)
+    tiles = jnp.concatenate(unpacked_half(total, tokens), axis=1)
     refs[-1][...] = tiles[:, :half].astype(refs[-1].dtype)
 
 
@@ -452,8 +455,8 @@
     steps = range(1, chips)
     near = [packed[0]] + [along_chips(packed[step], step) for step in steps]
     far = [
-        swap_cores(jnp.stack(near[: chips // 2])),
-        swap_cores(jnp.stack(near[chips // 2 :])),
+        swap_cores(jnp.stack(near[chips // 2 + 1 :])),
+        swap_cores(jnp.stack(near[: chips // 2 + 1])),
     ]
 
     rows, stats = pl.pallas_call(
@@ -478,7 +481,7 @@
             flops=2 * tokens * head.size, bytes_accessed=2 * head.size, transcendentals=0
         ),
         name="logits",
-    )(place, *near, *far, in_vmem(owner), in_vmem(table), head)
+    )(place, *near[::-1], *far, in_vmem(owner), in_vmem(table), head)
 
     all_stats = lax.all_to_all(stats, "vocab", split_axis=0, concat_axis=0, tiled=True)
 
@@ -505,22 +508,22 @@
             vmem_array((chips, hidden_rows, LANES), jnp.bfloat16),
             jax.ShapeDtypeStruct((1, 1), jnp.float32),
         ),
-        in_specs=[smem] + [vmem] * 5,
+        in_specs=[smem] * 2 + [vmem] * 5,
         out_specs=[vmem] * 3,
         compiler_params=params,
         name="combine",
-    )(place, all_stats, stats, in_vmem(table), in_vmem(terms), in_vmem(picks))
+    )(place, loss_scale, all_stats, stats, in_vmem(table), in_vmem(terms), in_vmem(picks))
 
     sums = keep + swap_cores(give).astype(jnp.float32)
-    shares = [along_chips(sums[step].astype(jnp.bfloat16), step) for step in steps]
+    shares = [along_chips(sums[step].astype(jnp.bfloat16), step) for step in steps[::-1]]
     total = pl.pallas_call(
         sum_kernel,
         out_shape=jax.ShapeDtypeStruct((tokens, half), jnp.bfloat16),
-        in_specs=[vmem] * (chips + 1),
+        in_specs=[vmem] * chips,
         out_specs=vmem,
         compiler_params=params,
         name="total",
-    )(loss_scale[None, :], sums[0], *shares)
+    )(sums[0], *shares)
     return total, jnp.reshape(loss, (1,))
 
 

time: 63.1 us -> 60.8 us (0.964)
  waiting for transfers between devices: 11.9 us -> 8.22 us
  starting transfers between devices: 30.3 us -> 31.8 us
    ppermute x14, waiting for transfers between devices: 8.2 us -> 5.26 us  [along_chips(): lax.ppermute(array, 'vocab', [(i, (i + 2 * step) % count) for i in range(...]
    all_to_all x1, starting transfers between devices: 4.88 us -> 5.89 us  [paired_shards(): lax.all_to_all(stats, 'vocab', split_axis=0, concat_axis=0, tiled=True)]
    ppermute x3, waiting for transfers between devices: 3.12 us -> 2.39 us  [swap_cores(): return lax.ppermute(array, 'vocab', [(i, i ^ 1) for i in range(count)])]
  transfers between devices with their start and end apart: 18 -> 18, of which waited for: 8 -> 11; matrix products, arithmetic and copies ran while one was open for 0% -> 0% of each run, Pallas kernels for 10% -> 10%
where the time goes in v11:
time: 60.8 us; the launch traced here: 60.5 us
  starting transfers between devices  31.8 us (52%)
  Pallas kernels  18.8 us (31%)
  waiting for transfers between devices  8.22 us (14%)
  between operations  1.4 us (2%)
    ppermute x14, starting transfers between devices, along_chips(): lax.ppermute(array, 'vocab', [(i, (i + 2 * step) % count) for i in range(...  25.8 us
    pallas_call x1, Pallas kernels, paired_shards(): pl.pallas_call(functools.partial(logits_kernel, chips=chips), out_shape=(...  8.44 us
    pallas_call x1, Pallas kernels, paired_shards(): pl.pallas_call(products_kernel, out_shape=(vmem_array((chips, 2 * tokens,...  6.32 us
    all_to_all x1, starting transfers between devices, paired_shards(): lax.all_to_all(stats, 'vocab', split_axis=0, concat_axis=0, tiled=True)  5.89 us
    ppermute x14, waiting for transfers between devices, along_chips(): lax.ppermute(array, 'vocab', [(i, (i + 2 * step) % count) for i in range(...  5.26 us
    ppermute x3, waiting for transfers between devices, swap_cores(): return lax.ppermute(array, 'vocab', [(i, i ^ 1) for i in range(count)])  2.39 us
    pallas_call x1, Pallas kernels, paired_shards(): pl.pallas_call(combine_kernel, out_shape=(vmem_array((chips, hidden_rows,...  1.84 us
    pallas_call x1, Pallas kernels, paired_shards(): pl.pallas_call(functools.partial(pack_kernel, shard_rows=shard_rows), out...  1.52 us
  transfers between devices with their start and end apart: 18, of which 11 were waited for; matrix products, arithmetic and copies ran while one was open for 0% of the time, Pallas kernels for 10%

profile of v11, /device:TPU:0, one launch (start us, length us, event | category | flops | bytes accessed | tf_op | source)
XLA Modules:
  0.0 60.5 jit_solution(11338160873514885840)
XLA Ops:
  0.6 1.5 %pack.1 = (bf16[8,240,128]{2,1,0:T(8,128)(2,1)S(1)}, bf16[64,64]{1,0:T(8,128)(2,1)S(1)}, f32[64,128]{1,0:T(8,128)S(1)}) custom-call(s32[1]{0:T(128)} %bitcast.place_ref, bf16[64,320]{1,0:T(8,128)(2,1)} %refs_0_.1, bf16[4,19456]{1,0:T(4,128)(2,1)} %refs_1_.1, f32[4,608]{1,0:T(4,128)} %refs_2_.1, s32[1,64]{1,0:T(1,128)} %bitcast.51, s32[1,64]{1,0:T(1,128)} %bitcast.52, ...), custom_call_target="tpu_custom_call" | custom-call | tf_op jit(solution)/shard_map/pack/pallas_call | solution.py:438
  2.2 3.0 %collective-permute-start.6 = (bf16[240,128]{1,0:T(8,128)(2,1)S(1)}, bf16[240,128]{1,0:T(8,128)(2,1)S(1)}, u32[]{:S(2)}, u32[]{:S(2)}) collective-permute-start(bf16[240,128]{1,0:T(8,128)(2,1)S(1)} %get-tuple-element.26), channel_id=1, source_target_pairs={{0,2},{1,3},{2,4},{3,5},{4,6},{5,7},{6,8},{7,9},{8,10},{9,11},{10,... | collective-permute-start | bytes 184328 | tf_op jit(solution)/shard_map/ppermute | solution.py:51
  5.2 1.6 %collective-permute-start.5 = (bf16[240,128]{1,0:T(8,128)(2,1)S(1)}, bf16[240,128]{1,0:T(8,128)(2,1)S(1)}, u32[]{:S(2)}, u32[]{:S(2)}) collective-permute-start(bf16[240,128]{1,0:T(8,128)(2,1)S(1)} %get-tuple-element.27), channel_id=1, source_target_pairs={{0,4},{1,5},{2,6},{3,7},{4,8},{5,9},{6,10},{7,11},{8,12},{9,13},{1... | collective-permute-start | bytes 184328 | tf_op jit(solution)/shard_map/ppermute | solution.py:51
  6.8 2.5 %collective-permute-start.4 = (bf16[240,128]{1,0:T(8,128)(2,1)S(1)}, bf16[240,128]{1,0:T(8,128)(2,1)S(1)}, u32[]{:S(2)}, u32[]{:S(2)}) collective-permute-start(bf16[240,128]{1,0:T(8,128)(2,1)S(1)} %get-tuple-element.28), channel_id=1, source_target_pairs={{0,6},{1,7},{2,8},{3,9},{4,10},{5,11},{6,12},{7,13},{8,14},{9,15},... | collective-permute-start | bytes 184328 | tf_op jit(solution)/shard_map/ppermute | solution.py:51
  9.3 1.2 %collective-permute-start.3 = (bf16[240,128]{1,0:T(8,128)(2,1)S(1)}, bf16[240,128]{1,0:T(8,128)(2,1)S(1)}, u32[]{:S(2)}, u32[]{:S(2)}) collective-permute-start(bf16[240,128]{1,0:T(8,128)(2,1)S(1)} %get-tuple-element.29), channel_id=1, source_target_pairs={{0,8},{1,9},{2,10},{3,11},{4,12},{5,13},{6,14},{7,15},{8,0},{9,1},... | collective-permute-start | bytes 184328 | tf_op jit(solution)/shard_map/ppermute | solution.py:51
  10.6 2.6 %collective-permute-start.2 = (bf16[240,128]{1,0:T(8,128)(2,1)S(1)}, bf16[240,128]{1,0:T(8,128)(2,1)S(1)}, u32[]{:S(2)}, u32[]{:S(2)}) collective-permute-start(bf16[240,128]{1,0:T(8,128)(2,1)S(1)} %get-tuple-element.30), channel_id=1, source_target_pairs={{0,10},{1,11},{2,12},{3,13},{4,14},{5,15},{6,0},{7,1},{8,2},{9,3},... | collective-permute-start | bytes 184328 | tf_op jit(solution)/shard_map/ppermute | solution.py:51
  13.2 1.3 %collective-permute-start.1 = (bf16[240,128]{1,0:T(8,128)(2,1)S(1)}, bf16[240,128]{1,0:T(8,128)(2,1)S(1)}, u32[]{:S(2)}, u32[]{:S(2)}) collective-permute-start(bf16[240,128]{1,0:T(8,128)(2,1)S(1)} %get-tuple-element.31), channel_id=1, source_target_pairs={{0,12},{1,13},{2,14},{3,15},{4,0},{5,1},{6,2},{7,3},{8,4},{9,5},{1... | collective-permute-start | bytes 184328 | tf_op jit(solution)/shard_map/ppermute | solution.py:51
  14.6 1.5 %collective-permute-start = (bf16[240,128]{1,0:T(8,128)(2,1)S(1)}, bf16[240,128]{1,0:T(8,128)(2,1)S(1)}, u32[]{:S(2)}, u32[]{:S(2)}) collective-permute-start(bf16[240,128]{1,0:T(8,128)(2,1)S(1)} %get-tuple-element.32), channel_id=1, source_target_pairs={{0,14},{1,15},{2,0},{3,1},{4,2},{5,3},{6,4},{7,5},{8,6},{9,7},{10,... | collective-permute-start | bytes 184328 | tf_op jit(solution)/shard_map/ppermute | solution.py:51
  17.5 1.1 %collective-permute-done.1.refs_1_ = bf16[240,128]{1,0:T(8,128)(2,1)S(1)} collective-permute-done((bf16[240,128]{1,0:T(8,128)(2,1)S(1)}, bf16[240,128]{1,0:T(8,128)(2,1)S(1)}, u32[]{:S(2)}, u32[]{:S(2)}) %collective-permute-start.1) | collective-permute-done | bytes 61472 | tf_op jit(solution)/shard_map/ppermute | solution.py:51
  19.6 0.8 %collective-permute-done.7.refs_8_ = bf16[3,240,128]{2,1,0:T(8,128)(2,1)S(1)} collective-permute-done((bf16[3,240,128]{2,1,0:T(8,128)(2,1)S(1)}, bf16[3,240,128]{2,1,0:T(8,128)(2,1)S(1)}, u32[]{:S(2)}, u32[]{:S(2)}) %collective-permute-start.7) | collective-permute-done | bytes 184352 | tf_op jit(solution)/shard_map/ppermute | solution.py:46
  20.4 8.4 %logits.1 = (bf16[192,1216]{1,0:T(8,128)(2,1)}, f32[16,8,128]{2,1,0:T(8,128)}) custom-call(s32[1]{0:T(128)} %bitcast.place_ref, bf16[240,128]{1,0:T(8,128)(2,1)S(1)} %collective-permute-done.refs_0_, bf16[240,128]{1,0:T(8,128)(2,1)S(1)} %collective-permute-done.1.refs_1_, bf16[240,128]{1,0:T(8,128)(2,1)S(1)} %collective-permute-done.2.refs_2_, ...), custom_call_target="tpu_custom_call" | custom-call | flops 796917760 | bytes 12451840 | tf_op jit(solution)/shard_map/logits/pallas_call | solution.py:462
  28.8 5.9 %all-to-all-start = ((f32[16,8,128]{2,1,0:T(8,128)}), f32[16,8,128]{2,1,0:T(8,128)S(1)}, u32[]{:S(2)}, u32[]{:S(2)}) async-start(f32[16,8,128]{2,1,0:T(8,128)} %get-tuple-element.15.own_ref), calls=%async_computation | async-start | bytes 131072 | tf_op jit(solution)/shard_map/all_to_all | solution.py:486
  34.7 6.3 %products.1 = (f32[8,128,640]{2,1,0:T(8,128)S(1)}, bf16[8,64,640]{2,1,0:T(8,128)(2,1)S(1)}) custom-call(s32[1]{0:T(128)} %bitcast.place_ref, bf16[192,1216]{1,0:T(8,128)(2,1)} %get-tuple-element.16.rows_ref, bf16[1216,5120]{1,0:T(8,128)(2,1)} %head_ref.1), custom_call_target="tpu_custom_call" | custom-call | flops 2390753280 | bytes 12451840 | tf_op jit(solution)/shard_map/products/pallas_call | solution.py:488
  41.6 1.8 %combine.1 = (f32[8,160,128]{2,1,0:T(8,128)S(1)}, bf16[8,160,128]{2,1,0:T(8,128)(2,1)S(1)}, f32[1,1]{1,0:T(1,128)}) custom-call(s32[1]{0:T(128)} %bitcast.place_ref, f32[1]{0:T(128)S(6)} %copy.14.scale_ref, f32[16,8,128]{2,1,0:T(8,128)S(1)} %all-to-all-done.stats_ref, f32[16,8,128]{2,1,0:T(8,128)} %get-tuple-element.15.own_ref, ...), custom_call_target="tpu_custom_call" | custom-call | tf_op jit(solution)/shard_map/combine/pallas_call | solution.py:504
  43.5 1.6 %collective-permute-done.9 = bf16[8,160,128]{2,1,0:T(8,128)(2,1)S(1)} collective-permute-done((bf16[8,160,128]{2,1,0:T(8,128)(2,1)S(1)}, bf16[8,160,128]{2,1,0:T(8,128)(2,1)S(1)}, u32[]{:S(2)}, u32[]{:S(2)}) %collective-permute-start.9) | collective-permute-done | bytes 327712 | tf_op jit(solution)/shard_map/ppermute | solution.py:46
  45.3 1.4 %collective-permute-start.16 = (bf16[160,128]{1,0:T(8,128)(2,1)S(1)}, bf16[160,128]{1,0:T(8,128)(2,1)S(1)}, u32[]{:S(2)}, u32[]{:S(2)}) collective-permute-start(bf16[160,128]{1,0:T(8,128)(2,1)S(1)} %get-tuple-element.33), channel_id=1, source_target_pairs={{0,2},{1,3},{2,4},{3,5},{4,6},{5,7},{6,8},{7,9},{8,10},{9,11},{10,... | collective-permute-start | bytes 122888 | tf_op jit(solution)/shard_map/ppermute | solution.py:51
  46.7 1.4 %collective-permute-start.15 = (bf16[160,128]{1,0:T(8,128)(2,1)S(1)}, bf16[160,128]{1,0:T(8,128)(2,1)S(1)}, u32[]{:S(2)}, u32[]{:S(2)}) collective-permute-start(bf16[160,128]{1,0:T(8,128)(2,1)S(1)} %get-tuple-element.34), channel_id=1, source_target_pairs={{0,4},{1,5},{2,6},{3,7},{4,8},{5,9},{6,10},{7,11},{8,12},{9,13},{1... | collective-permute-start | bytes 122888 | tf_op jit(solution)/shard_map/ppermute | solution.py:51
  48.1 2.4 %collective-permute-start.14 = (bf16[160,128]{1,0:T(8,128)(2,1)S(1)}, bf16[160,128]{1,0:T(8,128)(2,1)S(1)}, u32[]{:S(2)}, u32[]{:S(2)}) collective-permute-start(bf16[160,128]{1,0:T(8,128)(2,1)S(1)} %get-tuple-element.35), channel_id=1, source_target_pairs={{0,6},{1,7},{2,8},{3,9},{4,10},{5,11},{6,12},{7,13},{8,14},{9,15},... | collective-permute-start | bytes 122888 | tf_op jit(solution)/shard_map/ppermute | solution.py:51
  50.5 1.4 %collective-permute-start.13 = (bf16[160,128]{1,0:T(8,128)(2,1)S(1)}, bf16[160,128]{1,0:T(8,128)(2,1)S(1)}, u32[]{:S(2)}, u32[]{:S(2)}) collective-permute-start(bf16[160,128]{1,0:T(8,128)(2,1)S(1)} %get-tuple-element.36), channel_id=1, source_target_pairs={{0,8},{1,9},{2,10},{3,11},{4,12},{5,13},{6,14},{7,15},{8,0},{9,1},... | collective-permute-start | bytes 122888 | tf_op jit(solution)/shard_map/ppermute | solution.py:51
  51.9 2.4 %collective-permute-start.12 = (bf16[160,128]{1,0:T(8,128)(2,1)S(1)}, bf16[160,128]{1,0:T(8,128)(2,1)S(1)}, u32[]{:S(2)}, u32[]{:S(2)}) collective-permute-start(bf16[160,128]{1,0:T(8,128)(2,1)S(1)} %get-tuple-element.37), channel_id=1, source_target_pairs={{0,10},{1,11},{2,12},{3,13},{4,14},{5,15},{6,0},{7,1},{8,2},{9,3},... | collective-permute-start | bytes 122888 | tf_op jit(solution)/shard_map/ppermute | solution.py:51
  54.3 1.5 %collective-permute-start.11 = (bf16[160,128]{1,0:T(8,128)(2,1)S(1)}, bf16[160,128]{1,0:T(8,128)(2,1)S(1)}, u32[]{:S(2)}, u32[]{:S(2)}) collective-permute-start(bf16[160,128]{1,0:T(8,128)(2,1)S(1)} %get-tuple-element.38), channel_id=1, source_target_pairs={{0,12},{1,13},{2,14},{3,15},{4,0},{5,1},{6,2},{7,3},{8,4},{9,5},{1... | collective-permute-start | bytes 122888 | tf_op jit(solution)/shard_map/ppermute | solution.py:51
  55.8 1.4 %collective-permute-start.10 = (bf16[160,128]{1,0:T(8,128)(2,1)S(1)}, bf16[160,128]{1,0:T(8,128)(2,1)S(1)}, u32[]{:S(2)}, u32[]{:S(2)}) collective-permute-start(bf16[160,128]{1,0:T(8,128)(2,1)S(1)} %get-tuple-element.39), channel_id=1, source_target_pairs={{0,14},{1,15},{2,0},{3,1},{4,2},{5,3},{6,4},{7,5},{8,6},{9,7},{10,... | collective-permute-start | bytes 122888 | tf_op jit(solution)/shard_map/ppermute | solution.py:51
  57.3 1.0 %collective-permute-done.11.refs_1_ = bf16[160,128]{1,0:T(8,128)(2,1)S(1)} collective-permute-done((bf16[160,128]{1,0:T(8,128)(2,1)S(1)}, bf16[160,128]{1,0:T(8,128)(2,1)S(1)}, u32[]{:S(2)}, u32[]{:S(2)}) %collective-permute-start.11) | collective-permute-done | bytes 40992 | tf_op jit(solution)/shard_map/ppermute | solution.py:51
  58.4 1.4 %collective-permute-done.10.refs_0_ = bf16[160,128]{1,0:T(8,128)(2,1)S(1)} collective-permute-done((bf16[160,128]{1,0:T(8,128)(2,1)S(1)}, bf16[160,128]{1,0:T(8,128)(2,1)S(1)}, u32[]{:S(2)}, u32[]{:S(2)}) %collective-permute-start.10) | collective-permute-done | bytes 40992 | tf_op jit(solution)/shard_map/ppermute | solution.py:51
  (26 shorter events, 3.4 us)
Async XLA Ops:
  2.2 11.0 %collective-permute-start.6 = (bf16[240,128]{1,0:T(8,128)(2,1)S(1)}, bf16[240,128]{1,0:T(8,128)(2,1)S(1)}, u32[]{:S(2)}, u32[]{:S(2)}) collective-permute-start(bf16[240,128]{1,0:T(8,128)(2,1)S(1)} %get-tuple-element.26), channel_id=1, source_target_pairs={{0,2},{1,3},{2,4},{3,5},{4,6},{5,7},{6,8},{7,9},{8,10},{9,11},{10,... | collective-permute-start | bytes 184328 | tf_op jit(solution)/shard_map/ppermute | solution.py:51
  5.2 9.4 %collective-permute-start.5 = (bf16[240,128]{1,0:T(8,128)(2,1)S(1)}, bf16[240,128]{1,0:T(8,128)(2,1)S(1)}, u32[]{:S(2)}, u32[]{:S(2)}) collective-permute-start(bf16[240,128]{1,0:T(8,128)(2,1)S(1)} %get-tuple-element.27), channel_id=1, source_target_pairs={{0,4},{1,5},{2,6},{3,7},{4,8},{5,9},{6,10},{7,11},{8,12},{9,13},{1... | collective-permute-start | bytes 184328 | tf_op jit(solution)/shard_map/ppermute | solution.py:51
  6.8 9.4 %collective-permute-start.4 = (bf16[240,128]{1,0:T(8,128)(2,1)S(1)}, bf16[240,128]{1,0:T(8,128)(2,1)S(1)}, u32[]{:S(2)}, u32[]{:S(2)}) collective-permute-start(bf16[240,128]{1,0:T(8,128)(2,1)S(1)} %get-tuple-element.28), channel_id=1, source_target_pairs={{0,6},{1,7},{2,8},{3,9},{4,10},{5,11},{6,12},{7,13},{8,14},{9,15},... | collective-permute-start | bytes 184328 | tf_op jit(solution)/shard_map/ppermute | solution.py:51
  9.3 7.4 %collective-permute-start.3 = (bf16[240,128]{1,0:T(8,128)(2,1)S(1)}, bf16[240,128]{1,0:T(8,128)(2,1)S(1)}, u32[]{:S(2)}, u32[]{:S(2)}) collective-permute-start(bf16[240,128]{1,0:T(8,128)(2,1)S(1)} %get-tuple-element.29), channel_id=1, source_target_pairs={{0,8},{1,9},{2,10},{3,11},{4,12},{5,13},{6,14},{7,15},{8,0},{9,1},... | collective-permute-start | bytes 184328 | tf_op jit(solution)/shard_map/ppermute | solution.py:51
  10.6 7.0 %collective-permute-start.2 = (bf16[240,128]{1,0:T(8,128)(2,1)S(1)}, bf16[240,128]{1,0:T(8,128)(2,1)S(1)}, u32[]{:S(2)}, u32[]{:S(2)}) collective-permute-start(bf16[240,128]{1,0:T(8,128)(2,1)S(1)} %get-tuple-element.30), channel_id=1, source_target_pairs={{0,10},{1,11},{2,12},{3,13},{4,14},{5,15},{6,0},{7,1},{8,2},{9,3},... | collective-permute-start | bytes 184328 | tf_op jit(solution)/shard_map/ppermute | solution.py:51
  13.2 5.4 %collective-permute-start.1 = (bf16[240,128]{1,0:T(8,128)(2,1)S(1)}, bf16[240,128]{1,0:T(8,128)(2,1)S(1)}, u32[]{:S(2)}, u32[]{:S(2)}) collective-permute-start(bf16[240,128]{1,0:T(8,128)(2,1)S(1)} %get-tuple-element.31), channel_id=1, source_target_pairs={{0,12},{1,13},{2,14},{3,15},{4,0},{5,1},{6,2},{7,3},{8,4},{9,5},{1... | collective-permute-start | bytes 184328 | tf_op jit(solution)/shard_map/ppermute | solution.py:51
  14.6 4.3 %collective-permute-start = (bf16[240,128]{1,0:T(8,128)(2,1)S(1)}, bf16[240,128]{1,0:T(8,128)(2,1)S(1)}, u32[]{:S(2)}, u32[]{:S(2)}) collective-permute-start(bf16[240,128]{1,0:T(8,128)(2,1)S(1)} %get-tuple-element.32), channel_id=1, source_target_pairs={{0,14},{1,15},{2,0},{3,1},{4,2},{5,3},{6,4},{7,5},{8,6},{9,7},{10,... | collective-permute-start | bytes 184328 | tf_op jit(solution)/shard_map/ppermute | solution.py:51
  16.8 3.6 %collective-permute-start.8 = (bf16[5,240,128]{2,1,0:T(8,128)(2,1)S(1)}, bf16[5,240,128]{2,1,0:T(8,128)(2,1)S(1)}, u32[]{:S(2)}, u32[]{:S(2)}) collective-permute-start(bf16[5,240,128]{2,1,0:T(8,128)(2,1)S(1)} %bitcast_dynamic-update-slice_fusion), channel_id=1, source_target_pairs={{0,1},{1,0},{2,3},{3,2},{4,5},{5,4},{6,7},{7,6},{8,9},{9,8},{10,11... | collective-permute-start | bytes 921608 | tf_op jit(solution)/shard_map/ppermute | solution.py:46
  18.9 1.5 %collective-permute-start.7 = (bf16[3,240,128]{2,1,0:T(8,128)(2,1)S(1)}, bf16[3,240,128]{2,1,0:T(8,128)(2,1)S(1)}, u32[]{:S(2)}, u32[]{:S(2)}) collective-permute-start(bf16[3,240,128]{2,1,0:T(8,128)(2,1)S(1)} %pad_maximum_fusion), channel_id=1, source_target_pairs={{0,1},{1,0},{2,3},{3,2},{4,5},{5,4},{6,7},{7,6},{8,9},{9,8},{10,11... | collective-permute-start | bytes 552968 | tf_op jit(solution)/shard_map/ppermute | solution.py:46
  28.8 12.8 %all-to-all-start = ((f32[16,8,128]{2,1,0:T(8,128)}), f32[16,8,128]{2,1,0:T(8,128)S(1)}, u32[]{:S(2)}, u32[]{:S(2)}) async-start(f32[16,8,128]{2,1,0:T(8,128)} %get-tuple-element.15.own_ref), calls=%async_computation | async-start | bytes 131072 | tf_op jit(solution)/shard_map/all_to_all | solution.py:486
  43.5 1.6 %collective-permute-start.9 = (bf16[8,160,128]{2,1,0:T(8,128)(2,1)S(1)}, bf16[8,160,128]{2,1,0:T(8,128)(2,1)S(1)}, u32[]{:S(2)}, u32[]{:S(2)}) collective-permute-start(bf16[8,160,128]{2,1,0:T(8,128)(2,1)S(1)} %get-tuple-element.20), channel_id=1, source_target_pairs={{0,1},{1,0},{2,3},{3,2},{4,5},{5,4},{6,7},{7,6},{8,9},{9,8},{10,11... | collective-permute-start | bytes 983048 | tf_op jit(solution)/shard_map/ppermute | solution.py:46
  45.3 9.0 %collective-permute-start.16 = (bf16[160,128]{1,0:T(8,128)(2,1)S(1)}, bf16[160,128]{1,0:T(8,128)(2,1)S(1)}, u32[]{:S(2)}, u32[]{:S(2)}) collective-permute-start(bf16[160,128]{1,0:T(8,128)(2,1)S(1)} %get-tuple-element.33), channel_id=1, source_target_pairs={{0,2},{1,3},{2,4},{3,5},{4,6},{5,7},{6,8},{7,9},{8,10},{9,11},{10,... | collective-permute-start | bytes 122888 | tf_op jit(solution)/shard_map/ppermute | solution.py:51
  46.7 9.1 %collective-permute-start.15 = (bf16[160,128]{1,0:T(8,128)(2,1)S(1)}, bf16[160,128]{1,0:T(8,128)(2,1)S(1)}, u32[]{:S(2)}, u32[]{:S(2)}) collective-permute-start(bf16[160,128]{1,0:T(8,128)(2,1)S(1)} %get-tuple-element.34), channel_id=1, source_target_pairs={{0,4},{1,5},{2,6},{3,7},{4,8},{5,9},{6,10},{7,11},{8,12},{9,13},{1... | collective-permute-start | bytes 122888 | tf_op jit(solution)/shard_map/ppermute | solution.py:51
  48.1 9.1 %collective-permute-start.14 = (bf16[160,128]{1,0:T(8,128)(2,1)S(1)}, bf16[160,128]{1,0:T(8,128)(2,1)S(1)}, u32[]{:S(2)}, u32[]{:S(2)}) collective-permute-start(bf16[160,128]{1,0:T(8,128)(2,1)S(1)} %get-tuple-element.35), channel_id=1, source_target_pairs={{0,6},{1,7},{2,8},{3,9},{4,10},{5,11},{6,12},{7,13},{8,14},{9,15},... | collective-permute-start | bytes 122888 | tf_op jit(solution)/shard_map/ppermute | solution.py:51
  50.5 6.7 %collective-permute-start.13 = (bf16[160,128]{1,0:T(8,128)(2,1)S(1)}, bf16[160,128]{1,0:T(8,128)(2,1)S(1)}, u32[]{:S(2)}, u32[]{:S(2)}) collective-permute-start(bf16[160,128]{1,0:T(8,128)(2,1)S(1)} %get-tuple-element.36), channel_id=1, source_target_pairs={{0,8},{1,9},{2,10},{3,11},{4,12},{5,13},{6,14},{7,15},{8,0},{9,1},... | collective-permute-start | bytes 122888 | tf_op jit(solution)/shard_map/ppermute | solution.py:51
  51.9 5.4 %collective-permute-start.12 = (bf16[160,128]{1,0:T(8,128)(2,1)S(1)}, bf16[160,128]{1,0:T(8,128)(2,1)S(1)}, u32[]{:S(2)}, u32[]{:S(2)}) collective-permute-start(bf16[160,128]{1,0:T(8,128)(2,1)S(1)} %get-tuple-element.37), channel_id=1, source_target_pairs={{0,10},{1,11},{2,12},{3,13},{4,14},{5,15},{6,0},{7,1},{8,2},{9,3},... | collective-permute-start | bytes 122888 | tf_op jit(solution)/shard_map/ppermute | solution.py:51
  54.3 4.1 %collective-permute-start.11 = (bf16[160,128]{1,0:T(8,128)(2,1)S(1)}, bf16[160,128]{1,0:T(8,128)(2,1)S(1)}, u32[]{:S(2)}, u32[]{:S(2)}) collective-permute-start(bf16[160,128]{1,0:T(8,128)(2,1)S(1)} %get-tuple-element.38), channel_id=1, source_target_pairs={{0,12},{1,13},{2,14},{3,15},{4,0},{5,1},{6,2},{7,3},{8,4},{9,5},{1... | collective-permute-start | bytes 122888 | tf_op jit(solution)/shard_map/ppermute | solution.py:51
  55.8 4.0 %collective-permute-start.10 = (bf16[160,128]{1,0:T(8,128)(2,1)S(1)}, bf16[160,128]{1,0:T(8,128)(2,1)S(1)}, u32[]{:S(2)}, u32[]{:S(2)}) collective-permute-start(bf16[160,128]{1,0:T(8,128)(2,1)S(1)} %get-tuple-element.39), channel_id=1, source_target_pairs={{0,14},{1,15},{2,0},{3,1},{4,2},{5,3},{6,4},{7,5},{8,6},{9,7},{10,... | collective-permute-start | bytes 122888 | tf_op jit(solution)/shard_map/ppermute | solution.py:51

commit v12 on v11

--- a/solution.py
+++ b/solution.py
@@ -46,9 +46,9 @@
     return lax.ppermute(array, "vocab", [(i, i ^ 1) for i in range(count)])
 
 
-def along_chips(array, step):
+def across_chips(array, step):
     count = lax.axis_size("vocab")
-    return lax.ppermute(array, "vocab", [(i, (i + 2 * step) % count) for i in range(count)])
+    return lax.ppermute(array, "vocab", [(i, i ^ (2 * step)) for i in range(count)])
 
 
 def vmem_array(shape, dtype):
@@ -210,7 +210,7 @@
             rows += [
                 jnp.where(upper, tiles[2 * i], tiles[2 * i + 1]) for i in range(tile_pairs)
             ]
-        step = lax.rem(chip - place_ref[0] // 2 + chips, chips)
+        step = jnp.bitwise_xor(place_ref[0] // 2, chip)
         packed_ref[step, :hidden_rows] = hidden
         packed_ref[step, hidden_rows:] = jnp.concatenate(rows, axis=0).astype(jnp.bfloat16)
 
@@ -232,7 +232,7 @@
     held_ref, made_ref, hidden_ref, arrived_ref, teacher_ref, sems, made_sem = refs[5:]
     place = place_ref[0] // 2
     core = place_ref[0] % 2
-    sources = [lax.rem(place - step + chips, chips) for step in range(chips)]
+    sources = [jnp.bitwise_xor(place, step) for step in range(chips)]
     copies = head_copies(head_ref, held_ref, sems, sources)
     for copy in copies[:AHEAD]:
         copy.start()
@@ -328,7 +328,7 @@
     into = pltpu.make_async_copy(rows_ref, made_ref, made_sem)
     into.start()
     chips = held_ref.shape[0]
-    targets = [lax.rem(place_ref[0] // 2 + step, chips) for step in range(chips)]
+    targets = [jnp.bitwise_xor(place_ref[0] // 2, step) for step in range(chips)]
     copies = head_copies(head_ref, held_ref, sems, targets)
     for copy in copies[:AHEAD]:
         copy.start()
@@ -453,7 +453,7 @@
         name="pack",
     )(place, *[in_hbm(operand) for operand in operands])
     steps = range(1, chips)
-    near = [packed[0]] + [along_chips(packed[step], step) for step in steps]
+    near = [packed[0]] + [across_chips(packed[step], step) for step in steps]
     far = [
         swap_cores(jnp.stack(near[chips // 2 + 1 :])),
         swap_cores(jnp.stack(near[: chips // 2 + 1])),
@@ -515,7 +515,7 @@
     )(place, loss_scale, all_stats, stats, in_vmem(table), in_vmem(terms), in_vmem(picks))
 
     sums = keep + swap_cores(give).astype(jnp.float32)
-    shares = [along_chips(sums[step].astype(jnp.bfloat16), step) for step in steps[::-1]]
+    shares = [across_chips(sums[step].astype(jnp.bfloat16), step) for step in steps[::-1]]
     total = pl.pallas_call(
         sum_kernel,
         out_shape=jax.ShapeDtypeStruct((tokens, half), jnp.bfloat16),
@@ -613,7 +613,8 @@
     hidden_states, head, teacher_values = arrays[:3]
     count = lax.axis_size("vocab")
     fits = (
-        count % 2 == 0
+        count > 1
+        and count & (count - 1) == 0
         and hidden_states.shape[1] == 5 * LANES // 2
         and hidden_states.shape[0] % 32 == 0
         and head.shape[0] % LANES == LANES // 2

time: 60.8 us -> 64 us (1.053)
  waiting for transfers between devices: 8.22 us -> 15.8 us
  starting transfers between devices: 31.8 us -> 27.4 us
    ppermute x14, waiting for transfers between devices: 5.26 us -> 12.9 us  [across_chips(): lax.ppermute(array, 'vocab', [(i, i ^ 2 * step) for i in range(count)])]
    all_to_all x1, starting transfers between devices: 5.89 us -> 3.5 us  [paired_shards(): lax.all_to_all(stats, 'vocab', split_axis=0, concat_axis=0, tiled=True)]
    ppermute x14, starting transfers between devices: 25.8 us -> 23.8 us  [across_chips(): lax.ppermute(array, 'vocab', [(i, i ^ 2 * step) for i in range(count)])]
  transfers between devices with their start and end apart: 18 -> 18, of which waited for: 11 -> 8; matrix products, arithmetic and copies ran while one was open for 0% -> 0% of each run, Pallas kernels for 10% -> 10%
where the time goes in v12:
time: 64 us; the launch traced here: 63.7 us
  starting transfers between devices  27.4 us (43%)
  Pallas kernels  18.8 us (29%)
  waiting for transfers between devices  15.8 us (25%)
  between operations  1.43 us (2%)
    ppermute x14, starting transfers between devices, across_chips(): lax.ppermute(array, 'vocab', [(i, i ^ 2 * step) for i in range(count)])  23.8 us
    ppermute x14, waiting for transfers between devices, across_chips(): lax.ppermute(array, 'vocab', [(i, i ^ 2 * step) for i in range(count)])  12.9 us
    pallas_call x1, Pallas kernels, paired_shards(): pl.pallas_call(functools.partial(logits_kernel, chips=chips), out_shape=(...  8.43 us
    pallas_call x1, Pallas kernels, paired_shards(): pl.pallas_call(products_kernel, out_shape=(vmem_array((chips, 2 * tokens,...  6.3 us
    all_to_all x1, starting transfers between devices, paired_shards(): lax.all_to_all(stats, 'vocab', split_axis=0, concat_axis=0, tiled=True)  3.5 us
    ppermute x3, waiting for transfers between devices, swap_cores(): return lax.ppermute(array, 'vocab', [(i, i ^ 1) for i in range(count)])  2.39 us
    pallas_call x1, Pallas kernels, paired_shards(): pl.pallas_call(combine_kernel, out_shape=(vmem_array((chips, hidden_rows,...  1.84 us
    pallas_call x1, Pallas kernels, paired_shards(): pl.pallas_call(functools.partial(pack_kernel, shard_rows=shard_rows), out...  1.52 us
  transfers between devices with their start and end apart: 18, of which 8 were waited for; matrix products, arithmetic and copies ran while one was open for 0% of the time, Pallas kernels for 10%

profile of v12, /device:TPU:0, one launch (start us, length us, event | category | flops | bytes accessed | tf_op | source)
XLA Modules:
  0.0 63.7 jit_solution(16337339214136754645)
XLA Ops:
  0.6 1.5 %pack.1 = (bf16[8,240,128]{2,1,0:T(8,128)(2,1)S(1)}, bf16[64,64]{1,0:T(8,128)(2,1)S(1)}, f32[64,128]{1,0:T(8,128)S(1)}) custom-call(s32[1]{0:T(128)} %bitcast.place_ref, bf16[64,320]{1,0:T(8,128)(2,1)} %refs_0_.1, bf16[4,19456]{1,0:T(4,128)(2,1)} %refs_1_.1, f32[4,608]{1,0:T(4,128)} %refs_2_.1, s32[1,64]{1,0:T(1,128)} %bitcast.51, s32[1,64]{1,0:T(1,128)} %bitcast.52, ...), custom_call_target="tpu_custom_call" | custom-call | tf_op jit(solution)/shard_map/pack/pallas_call | solution.py:438
  2.2 3.0 %collective-permute-start.6 = (bf16[240,128]{1,0:T(8,128)(2,1)S(1)}, bf16[240,128]{1,0:T(8,128)(2,1)S(1)}, u32[]{:S(2)}, u32[]{:S(2)}) collective-permute-start(bf16[240,128]{1,0:T(8,128)(2,1)S(1)} %get-tuple-element.26), channel_id=1, source_target_pairs={{0,2},{1,3},{2,0},{3,1},{4,6},{5,7},{6,4},{7,5},{8,10},{9,11},{10,... | collective-permute-start | bytes 184328 | tf_op jit(solution)/shard_map/ppermute | solution.py:51
  5.2 1.6 %collective-permute-start.5 = (bf16[240,128]{1,0:T(8,128)(2,1)S(1)}, bf16[240,128]{1,0:T(8,128)(2,1)S(1)}, u32[]{:S(2)}, u32[]{:S(2)}) collective-permute-start(bf16[240,128]{1,0:T(8,128)(2,1)S(1)} %get-tuple-element.27), channel_id=1, source_target_pairs={{0,4},{1,5},{2,6},{3,7},{4,0},{5,1},{6,2},{7,3},{8,12},{9,13},{10,... | collective-permute-start | bytes 184328 | tf_op jit(solution)/shard_map/ppermute | solution.py:51
  6.8 3.0 %collective-permute-start.3 = (bf16[240,128]{1,0:T(8,128)(2,1)S(1)}, bf16[240,128]{1,0:T(8,128)(2,1)S(1)}, u32[]{:S(2)}, u32[]{:S(2)}) collective-permute-start(bf16[240,128]{1,0:T(8,128)(2,1)S(1)} %get-tuple-element.29), channel_id=1, source_target_pairs={{0,8},{1,9},{2,10},{3,11},{4,12},{5,13},{6,14},{7,15},{8,0},{9,1},... | collective-permute-start | bytes 184328 | tf_op jit(solution)/shard_map/ppermute | solution.py:51
  9.8 1.3 %collective-permute-start.2 = (bf16[240,128]{1,0:T(8,128)(2,1)S(1)}, bf16[240,128]{1,0:T(8,128)(2,1)S(1)}, u32[]{:S(2)}, u32[]{:S(2)}) collective-permute-start(bf16[240,128]{1,0:T(8,128)(2,1)S(1)} %get-tuple-element.30), channel_id=1, source_target_pairs={{0,10},{1,11},{2,8},{3,9},{4,14},{5,15},{6,12},{7,13},{8,2},{9,3},... | collective-permute-start | bytes 184328 | tf_op jit(solution)/shard_map/ppermute | solution.py:51
  11.1 3.6 %collective-permute-start.1 = (bf16[240,128]{1,0:T(8,128)(2,1)S(1)}, bf16[240,128]{1,0:T(8,128)(2,1)S(1)}, u32[]{:S(2)}, u32[]{:S(2)}) collective-permute-start(bf16[240,128]{1,0:T(8,128)(2,1)S(1)} %get-tuple-element.31), channel_id=1, source_target_pairs={{0,12},{1,13},{2,14},{3,15},{4,8},{5,9},{6,10},{7,11},{8,4},{9,5},... | collective-permute-start | bytes 184328 | tf_op jit(solution)/shard_map/ppermute | solution.py:51
  15.0 4.5 %collective-permute-done.2.refs_2_ = bf16[240,128]{1,0:T(8,128)(2,1)S(1)} collective-permute-done((bf16[240,128]{1,0:T(8,128)(2,1)S(1)}, bf16[240,128]{1,0:T(8,128)(2,1)S(1)}, u32[]{:S(2)}, u32[]{:S(2)}) %collective-permute-start.2) | collective-permute-done | bytes 61472 | tf_op jit(solution)/shard_map/ppermute | solution.py:51
  19.5 2.3 %collective-permute-done.refs_0_ = bf16[240,128]{1,0:T(8,128)(2,1)S(1)} collective-permute-done((bf16[240,128]{1,0:T(8,128)(2,1)S(1)}, bf16[240,128]{1,0:T(8,128)(2,1)S(1)}, u32[]{:S(2)}, u32[]{:S(2)}) %collective-permute-start) | collective-permute-done | bytes 61472 | tf_op jit(solution)/shard_map/ppermute | solution.py:51
  22.6 0.8 %collective-permute-done.7.refs_8_ = bf16[3,240,128]{2,1,0:T(8,128)(2,1)S(1)} collective-permute-done((bf16[3,240,128]{2,1,0:T(8,128)(2,1)S(1)}, bf16[3,240,128]{2,1,0:T(8,128)(2,1)S(1)}, u32[]{:S(2)}, u32[]{:S(2)}) %collective-permute-start.7) | collective-permute-done | bytes 184352 | tf_op jit(solution)/shard_map/ppermute | solution.py:46
  23.3 8.4 %logits.1 = (bf16[192,1216]{1,0:T(8,128)(2,1)}, f32[16,8,128]{2,1,0:T(8,128)}) custom-call(s32[1]{0:T(128)} %bitcast.place_ref, bf16[240,128]{1,0:T(8,128)(2,1)S(1)} %collective-permute-done.refs_0_, bf16[240,128]{1,0:T(8,128)(2,1)S(1)} %collective-permute-done.1.refs_1_, bf16[240,128]{1,0:T(8,128)(2,1)S(1)} %collective-permute-done.2.refs_2_, ...), custom_call_target="tpu_custom_call" | custom-call | flops 796917760 | bytes 12451840 | tf_op jit(solution)/shard_map/logits/pallas_call | solution.py:462
  31.8 3.5 %all-to-all-start = ((f32[16,8,128]{2,1,0:T(8,128)}), f32[16,8,128]{2,1,0:T(8,128)S(1)}, u32[]{:S(2)}, u32[]{:S(2)}) async-start(f32[16,8,128]{2,1,0:T(8,128)} %get-tuple-element.15.own_ref), calls=%async_computation | async-start | bytes 131072 | tf_op jit(solution)/shard_map/all_to_all | solution.py:486
  35.3 6.3 %products.1 = (f32[8,128,640]{2,1,0:T(8,128)S(1)}, bf16[8,64,640]{2,1,0:T(8,128)(2,1)S(1)}) custom-call(s32[1]{0:T(128)} %bitcast.place_ref, bf16[192,1216]{1,0:T(8,128)(2,1)} %get-tuple-element.16.rows_ref, bf16[1216,5120]{1,0:T(8,128)(2,1)} %head_ref.1), custom_call_target="tpu_custom_call" | custom-call | flops 2390753280 | bytes 12451840 | tf_op jit(solution)/shard_map/products/pallas_call | solution.py:488
  42.1 1.8 %combine.1 = (f32[8,160,128]{2,1,0:T(8,128)S(1)}, bf16[8,160,128]{2,1,0:T(8,128)(2,1)S(1)}, f32[1,1]{1,0:T(1,128)}) custom-call(s32[1]{0:T(128)} %bitcast.place_ref, f32[1]{0:T(128)S(6)} %copy.14.scale_ref, f32[16,8,128]{2,1,0:T(8,128)S(1)} %all-to-all-done.stats_ref, f32[16,8,128]{2,1,0:T(8,128)} %get-tuple-element.15.own_ref, ...), custom_call_target="tpu_custom_call" | custom-call | tf_op jit(solution)/shard_map/combine/pallas_call | solution.py:504
  44.0 1.6 %collective-permute-done.9 = bf16[8,160,128]{2,1,0:T(8,128)(2,1)S(1)} collective-permute-done((bf16[8,160,128]{2,1,0:T(8,128)(2,1)S(1)}, bf16[8,160,128]{2,1,0:T(8,128)(2,1)S(1)}, u32[]{:S(2)}, u32[]{:S(2)}) %collective-permute-start.9) | collective-permute-done | bytes 327712 | tf_op jit(solution)/shard_map/ppermute | solution.py:46
  45.7 1.3 %collective-permute-start.16 = (bf16[160,128]{1,0:T(8,128)(2,1)S(1)}, bf16[160,128]{1,0:T(8,128)(2,1)S(1)}, u32[]{:S(2)}, u32[]{:S(2)}) collective-permute-start(bf16[160,128]{1,0:T(8,128)(2,1)S(1)} %get-tuple-element.33), channel_id=1, source_target_pairs={{0,2},{1,3},{2,0},{3,1},{4,6},{5,7},{6,4},{7,5},{8,10},{9,11},{10,... | collective-permute-start | bytes 122888 | tf_op jit(solution)/shard_map/ppermute | solution.py:51
  47.1 1.5 %collective-permute-start.15 = (bf16[160,128]{1,0:T(8,128)(2,1)S(1)}, bf16[160,128]{1,0:T(8,128)(2,1)S(1)}, u32[]{:S(2)}, u32[]{:S(2)}) collective-permute-start(bf16[160,128]{1,0:T(8,128)(2,1)S(1)} %get-tuple-element.34), channel_id=1, source_target_pairs={{0,4},{1,5},{2,6},{3,7},{4,0},{5,1},{6,2},{7,3},{8,12},{9,13},{10,... | collective-permute-start | bytes 122888 | tf_op jit(solution)/shard_map/ppermute | solution.py:51
  48.6 0.8 %collective-permute-start.14 = (bf16[160,128]{1,0:T(8,128)(2,1)S(1)}, bf16[160,128]{1,0:T(8,128)(2,1)S(1)}, u32[]{:S(2)}, u32[]{:S(2)}) collective-permute-start(bf16[160,128]{1,0:T(8,128)(2,1)S(1)} %get-tuple-element.35), channel_id=1, source_target_pairs={{0,6},{1,7},{2,4},{3,5},{4,2},{5,3},{6,0},{7,1},{8,14},{9,15},{10,... | collective-permute-start | bytes 122888 | tf_op jit(solution)/shard_map/ppermute | solution.py:51
  49.3 2.2 %collective-permute-start.13 = (bf16[160,128]{1,0:T(8,128)(2,1)S(1)}, bf16[160,128]{1,0:T(8,128)(2,1)S(1)}, u32[]{:S(2)}, u32[]{:S(2)}) collective-permute-start(bf16[160,128]{1,0:T(8,128)(2,1)S(1)} %get-tuple-element.36), channel_id=1, source_target_pairs={{0,8},{1,9},{2,10},{3,11},{4,12},{5,13},{6,14},{7,15},{8,0},{9,1},... | collective-permute-start | bytes 122888 | tf_op jit(solution)/shard_map/ppermute | solution.py:51
  51.5 1.4 %collective-permute-start.12 = (bf16[160,128]{1,0:T(8,128)(2,1)S(1)}, bf16[160,128]{1,0:T(8,128)(2,1)S(1)}, u32[]{:S(2)}, u32[]{:S(2)}) collective-permute-start(bf16[160,128]{1,0:T(8,128)(2,1)S(1)} %get-tuple-element.37), channel_id=1, source_target_pairs={{0,10},{1,11},{2,8},{3,9},{4,14},{5,15},{6,12},{7,13},{8,2},{9,3},... | collective-permute-start | bytes 122888 | tf_op jit(solution)/shard_map/ppermute | solution.py:51
  52.9 3.4 %collective-permute-start.11 = (bf16[160,128]{1,0:T(8,128)(2,1)S(1)}, bf16[160,128]{1,0:T(8,128)(2,1)S(1)}, u32[]{:S(2)}, u32[]{:S(2)}) collective-permute-start(bf16[160,128]{1,0:T(8,128)(2,1)S(1)} %get-tuple-element.38), channel_id=1, source_target_pairs={{0,12},{1,13},{2,14},{3,15},{4,8},{5,9},{6,10},{7,11},{8,4},{9,5},... | collective-permute-start | bytes 122888 | tf_op jit(solution)/shard_map/ppermute | solution.py:51
  57.0 0.8 %collective-permute-done.12.refs_2_ = bf16[160,128]{1,0:T(8,128)(2,1)S(1)} collective-permute-done((bf16[160,128]{1,0:T(8,128)(2,1)S(1)}, bf16[160,128]{1,0:T(8,128)(2,1)S(1)}, u32[]{:S(2)}, u32[]{:S(2)}) %collective-permute-start.12) | collective-permute-done | bytes 40992 | tf_op jit(solution)/shard_map/ppermute | solution.py:51
  57.8 1.0 %collective-permute-done.11.refs_1_ = bf16[160,128]{1,0:T(8,128)(2,1)S(1)} collective-permute-done((bf16[160,128]{1,0:T(8,128)(2,1)S(1)}, bf16[160,128]{1,0:T(8,128)(2,1)S(1)}, u32[]{:S(2)}, u32[]{:S(2)}) %collective-permute-start.11) | collective-permute-done | bytes 40992 | tf_op jit(solution)/shard_map/ppermute | solution.py:51
  58.8 4.2 %collective-permute-done.10.refs_0_ = bf16[160,128]{1,0:T(8,128)(2,1)S(1)} collective-permute-done((bf16[160,128]{1,0:T(8,128)(2,1)S(1)}, bf16[160,128]{1,0:T(8,128)(2,1)S(1)}, u32[]{:S(2)}, u32[]{:S(2)}) %collective-permute-start.10) | collective-permute-done | bytes 40992 | tf_op jit(solution)/shard_map/ppermute | solution.py:51
  63.0 0.7 %total.1 = bf16[64,320]{1,0:T(8,128)(2,1)} custom-call(f32[160,128]{1,0:T(8,128)S(1)} %slice_bitcast_fusion.own_ref, bf16[160,128]{1,0:T(8,128)(2,1)S(1)} %collective-permute-done.10.refs_0_, bf16[160,128]{1,0:T(8,128)(2,1)S(1)} %collective-permute-done.11.refs_1_, bf16[160,128]{1,0:T(8,128)(2,1)S(1)} %collective-permute-done.12.refs_2_, ...), custom_call_target="tpu_custom_call" | custom-call | tf_op jit(solution)/shard_map/total/pallas_call | solution.py:519
  (26 shorter events, 1.7 us)
Async XLA Ops:
  2.2 8.9 %collective-permute-start.6 = (bf16[240,128]{1,0:T(8,128)(2,1)S(1)}, bf16[240,128]{1,0:T(8,128)(2,1)S(1)}, u32[]{:S(2)}, u32[]{:S(2)}) collective-permute-start(bf16[240,128]{1,0:T(8,128)(2,1)S(1)} %get-tuple-element.26), channel_id=1, source_target_pairs={{0,2},{1,3},{2,0},{3,1},{4,6},{5,7},{6,4},{7,5},{8,10},{9,11},{10,... | collective-permute-start | bytes 184328 | tf_op jit(solution)/shard_map/ppermute | solution.py:51
  5.2 9.5 %collective-permute-start.5 = (bf16[240,128]{1,0:T(8,128)(2,1)S(1)}, bf16[240,128]{1,0:T(8,128)(2,1)S(1)}, u32[]{:S(2)}, u32[]{:S(2)}) collective-permute-start(bf16[240,128]{1,0:T(8,128)(2,1)S(1)} %get-tuple-element.27), channel_id=1, source_target_pairs={{0,4},{1,5},{2,6},{3,7},{4,0},{5,1},{6,2},{7,3},{8,12},{9,13},{10,... | collective-permute-start | bytes 184328 | tf_op jit(solution)/shard_map/ppermute | solution.py:51
  6.8 8.0 %collective-permute-start.4 = (bf16[240,128]{1,0:T(8,128)(2,1)S(1)}, bf16[240,128]{1,0:T(8,128)(2,1)S(1)}, u32[]{:S(2)}, u32[]{:S(2)}) collective-permute-start(bf16[240,128]{1,0:T(8,128)(2,1)S(1)} %get-tuple-element.28), channel_id=1, source_target_pairs={{0,6},{1,7},{2,4},{3,5},{4,2},{5,3},{6,0},{7,1},{8,14},{9,15},{10,... | collective-permute-start | bytes 184328 | tf_op jit(solution)/shard_map/ppermute | solution.py:51
  6.8 8.0 %collective-permute-start.3 = (bf16[240,128]{1,0:T(8,128)(2,1)S(1)}, bf16[240,128]{1,0:T(8,128)(2,1)S(1)}, u32[]{:S(2)}, u32[]{:S(2)}) collective-permute-start(bf16[240,128]{1,0:T(8,128)(2,1)S(1)} %get-tuple-element.29), channel_id=1, source_target_pairs={{0,8},{1,9},{2,10},{3,11},{4,12},{5,13},{6,14},{7,15},{8,0},{9,1},... | collective-permute-start | bytes 184328 | tf_op jit(solution)/shard_map/ppermute | solution.py:51
  9.8 9.7 %collective-permute-start.2 = (bf16[240,128]{1,0:T(8,128)(2,1)S(1)}, bf16[240,128]{1,0:T(8,128)(2,1)S(1)}, u32[]{:S(2)}, u32[]{:S(2)}) collective-permute-start(bf16[240,128]{1,0:T(8,128)(2,1)S(1)} %get-tuple-element.30), channel_id=1, source_target_pairs={{0,10},{1,11},{2,8},{3,9},{4,14},{5,15},{6,12},{7,13},{8,2},{9,3},... | collective-permute-start | bytes 184328 | tf_op jit(solution)/shard_map/ppermute | solution.py:51
  11.1 8.4 %collective-permute-start.1 = (bf16[240,128]{1,0:T(8,128)(2,1)S(1)}, bf16[240,128]{1,0:T(8,128)(2,1)S(1)}, u32[]{:S(2)}, u32[]{:S(2)}) collective-permute-start(bf16[240,128]{1,0:T(8,128)(2,1)S(1)} %get-tuple-element.31), channel_id=1, source_target_pairs={{0,12},{1,13},{2,14},{3,15},{4,8},{5,9},{6,10},{7,11},{8,4},{9,5},... | collective-permute-start | bytes 184328 | tf_op jit(solution)/shard_map/ppermute | solution.py:51
  14.7 7.1 %collective-permute-start = (bf16[240,128]{1,0:T(8,128)(2,1)S(1)}, bf16[240,128]{1,0:T(8,128)(2,1)S(1)}, u32[]{:S(2)}, u32[]{:S(2)}) collective-permute-start(bf16[240,128]{1,0:T(8,128)(2,1)S(1)} %get-tuple-element.32), channel_id=1, source_target_pairs={{0,14},{1,15},{2,12},{3,13},{4,10},{5,11},{6,8},{7,9},{8,6},{9,7},... | collective-permute-start | bytes 184328 | tf_op jit(solution)/shard_map/ppermute | solution.py:51
  14.9 8.5 %collective-permute-start.8 = (bf16[5,240,128]{2,1,0:T(8,128)(2,1)S(1)}, bf16[5,240,128]{2,1,0:T(8,128)(2,1)S(1)}, u32[]{:S(2)}, u32[]{:S(2)}) collective-permute-start(bf16[5,240,128]{2,1,0:T(8,128)(2,1)S(1)} %bitcast_dynamic-update-slice_fusion), channel_id=1, source_target_pairs={{0,1},{1,0},{2,3},{3,2},{4,5},{5,4},{6,7},{7,6},{8,9},{9,8},{10,11... | collective-permute-start | bytes 921608 | tf_op jit(solution)/shard_map/ppermute | solution.py:46
  21.8 1.5 %collective-permute-start.7 = (bf16[3,240,128]{2,1,0:T(8,128)(2,1)S(1)}, bf16[3,240,128]{2,1,0:T(8,128)(2,1)S(1)}, u32[]{:S(2)}, u32[]{:S(2)}) collective-permute-start(bf16[3,240,128]{2,1,0:T(8,128)(2,1)S(1)} %pad_maximum_fusion), channel_id=1, source_target_pairs={{0,1},{1,0},{2,3},{3,2},{4,5},{5,4},{6,7},{7,6},{8,9},{9,8},{10,11... | collective-permute-start | bytes 552968 | tf_op jit(solution)/shard_map/ppermute | solution.py:46
  31.8 10.4 %all-to-all-start = ((f32[16,8,128]{2,1,0:T(8,128)}), f32[16,8,128]{2,1,0:T(8,128)S(1)}, u32[]{:S(2)}, u32[]{:S(2)}) async-start(f32[16,8,128]{2,1,0:T(8,128)} %get-tuple-element.15.own_ref), calls=%async_computation | async-start | bytes 131072 | tf_op jit(solution)/shard_map/all_to_all | solution.py:486
  44.0 1.6 %collective-permute-start.9 = (bf16[8,160,128]{2,1,0:T(8,128)(2,1)S(1)}, bf16[8,160,128]{2,1,0:T(8,128)(2,1)S(1)}, u32[]{:S(2)}, u32[]{:S(2)}) collective-permute-start(bf16[8,160,128]{2,1,0:T(8,128)(2,1)S(1)} %get-tuple-element.20), channel_id=1, source_target_pairs={{0,1},{1,0},{2,3},{3,2},{4,5},{5,4},{6,7},{7,6},{8,9},{9,8},{10,11... | collective-permute-start | bytes 983048 | tf_op jit(solution)/shard_map/ppermute | solution.py:46
  45.7 7.2 %collective-permute-start.16 = (bf16[160,128]{1,0:T(8,128)(2,1)S(1)}, bf16[160,128]{1,0:T(8,128)(2,1)S(1)}, u32[]{:S(2)}, u32[]{:S(2)}) collective-permute-start(bf16[160,128]{1,0:T(8,128)(2,1)S(1)} %get-tuple-element.33), channel_id=1, source_target_pairs={{0,2},{1,3},{2,0},{3,1},{4,6},{5,7},{6,4},{7,5},{8,10},{9,11},{10,... | collective-permute-start | bytes 122888 | tf_op jit(solution)/shard_map/ppermute | solution.py:51
  47.1 9.2 %collective-permute-start.15 = (bf16[160,128]{1,0:T(8,128)(2,1)S(1)}, bf16[160,128]{1,0:T(8,128)(2,1)S(1)}, u32[]{:S(2)}, u32[]{:S(2)}) collective-permute-start(bf16[160,128]{1,0:T(8,128)(2,1)S(1)} %get-tuple-element.34), channel_id=1, source_target_pairs={{0,4},{1,5},{2,6},{3,7},{4,0},{5,1},{6,2},{7,3},{8,12},{9,13},{10,... | collective-permute-start | bytes 122888 | tf_op jit(solution)/shard_map/ppermute | solution.py:51
  48.6 8.4 %collective-permute-start.14 = (bf16[160,128]{1,0:T(8,128)(2,1)S(1)}, bf16[160,128]{1,0:T(8,128)(2,1)S(1)}, u32[]{:S(2)}, u32[]{:S(2)}) collective-permute-start(bf16[160,128]{1,0:T(8,128)(2,1)S(1)} %get-tuple-element.35), channel_id=1, source_target_pairs={{0,6},{1,7},{2,4},{3,5},{4,2},{5,3},{6,0},{7,1},{8,14},{9,15},{10,... | collective-permute-start | bytes 122888 | tf_op jit(solution)/shard_map/ppermute | solution.py:51
  49.3 7.7 %collective-permute-start.13 = (bf16[160,128]{1,0:T(8,128)(2,1)S(1)}, bf16[160,128]{1,0:T(8,128)(2,1)S(1)}, u32[]{:S(2)}, u32[]{:S(2)}) collective-permute-start(bf16[160,128]{1,0:T(8,128)(2,1)S(1)} %get-tuple-element.36), channel_id=1, source_target_pairs={{0,8},{1,9},{2,10},{3,11},{4,12},{5,13},{6,14},{7,15},{8,0},{9,1},... | collective-permute-start | bytes 122888 | tf_op jit(solution)/shard_map/ppermute | solution.py:51
  51.5 6.3 %collective-permute-start.12 = (bf16[160,128]{1,0:T(8,128)(2,1)S(1)}, bf16[160,128]{1,0:T(8,128)(2,1)S(1)}, u32[]{:S(2)}, u32[]{:S(2)}) collective-permute-start(bf16[160,128]{1,0:T(8,128)(2,1)S(1)} %get-tuple-element.37), channel_id=1, source_target_pairs={{0,10},{1,11},{2,8},{3,9},{4,14},{5,15},{6,12},{7,13},{8,2},{9,3},... | collective-permute-start | bytes 122888 | tf_op jit(solution)/shard_map/ppermute | solution.py:51
  52.9 5.9 %collective-permute-start.11 = (bf16[160,128]{1,0:T(8,128)(2,1)S(1)}, bf16[160,128]{1,0:T(8,128)(2,1)S(1)}, u32[]{:S(2)}, u32[]{:S(2)}) collective-permute-start(bf16[160,128]{1,0:T(8,128)(2,1)S(1)} %get-tuple-element.38), channel_id=1, source_target_pairs={{0,12},{1,13},{2,14},{3,15},{4,8},{5,9},{6,10},{7,11},{8,4},{9,5},... | collective-permute-start | bytes 122888 | tf_op jit(solution)/shard_map/ppermute | solution.py:51
  56.3 6.7 %collective-permute-start.10 = (bf16[160,128]{1,0:T(8,128)(2,1)S(1)}, bf16[160,128]{1,0:T(8,128)(2,1)S(1)}, u32[]{:S(2)}, u32[]{:S(2)}) collective-permute-start(bf16[160,128]{1,0:T(8,128)(2,1)S(1)} %get-tuple-element.39), channel_id=1, source_target_pairs={{0,14},{1,15},{2,12},{3,13},{4,10},{5,11},{6,8},{7,9},{8,6},{9,7},... | collective-permute-start | bytes 122888 | tf_op jit(solution)/shard_map/ppermute | solution.py:51

commit v13 on v11

--- a/solution.py
+++ b/solution.py
@@ -11,6 +11,7 @@
 LANES = 128
 STATS = 8
 AHEAD = 3
+EARLY = 3
 
 
 sample_weight = 0.5
@@ -226,14 +227,27 @@
     return copies
 
 
+def source_chips(place_ref, chips):
+    return [lax.rem(place_ref[0] // 2 - step + chips, chips) for step in range(chips)]
+
+
+def preload_kernel(place_ref, head_ref, _, early_ref, sems, *, chips):
+    sources = source_chips(place_ref, chips)[: early_ref.shape[0]]
+    copies = head_copies(head_ref, early_ref, sems, sources)
+    for copy in copies:
+        copy.start()
+    for copy in copies:
+        copy.wait()
+
+
 def logits_kernel(place_ref, *refs, chips):
     near, far, refs = refs[:chips][::-1], refs[chips : chips + 2], refs[chips + 2 :]
-    owner_ref, tokens_ref, head_ref, rows_ref, stats_ref = refs[:5]
-    held_ref, made_ref, hidden_ref, arrived_ref, teacher_ref, sems, made_sem = refs[5:]
-    place = place_ref[0] // 2
+    owner_ref, tokens_ref, early_ref, head_ref, rows_ref, stats_ref = refs[:6]
+    held_ref, made_ref, hidden_ref, arrived_ref, teacher_ref, sems, made_sem = refs[6:]
     core = place_ref[0] % 2
-    sources = [lax.rem(place - step + chips, chips) for step in range(chips)]
-    copies = head_copies(head_ref, held_ref, sems, sources)
+    sources = source_chips(place_ref, chips)
+    early = early_ref.shape[0]
+    copies = head_copies(head_ref, held_ref, sems, sources[early:])
     for copy in copies[:AHEAD]:
         copy.start()
     _, tokens, width = hidden_ref.shape
@@ -269,10 +283,11 @@
 
     unpack_hidden(0)
     logits = jnp.zeros((tokens, shard_rows), jnp.float32)
-    for chip, copy in enumerate(copies):
-        copy.wait()
-        if chip + AHEAD < chips:
-            copies[chip + AHEAD].start()
+    for chip in range(chips):
+        if chip >= early:
+            copies[chip - early].wait()
+        if 0 < chip + 1 - early and chip + AHEAD - early < len(copies):
+            copies[chip + AHEAD - early].start()
         if chip + 1 < chips:
             unpack_hidden(chip + 1)
         if chip < chips // 2:
@@ -290,7 +305,7 @@
             teacher_ref[...] = teacher_off
         logits += lax.dot_general(
             hidden_ref[chip],
-            held_ref[chip],
+            early_ref[chip] if chip < early else held_ref[chip - early],
             (((1,), (1,)), ((), ())),
             preferred_element_type=jnp.float32,
         )
@@ -333,17 +348,30 @@
     for copy in copies[:AHEAD]:
         copy.start()
     into.wait()
-    sums_rows = terms_ref.shape[1]
+    tokens = made_ref.shape[0] // 3
+    width = held_ref.shape[2]
     for step, copy in enumerate(copies):
         copy.wait()
         if step + AHEAD < len(copies):
             copies[step + AHEAD].start()
         products = jnp.dot(made_ref[...], held_ref[step], preferred_element_type=jnp.float32)
-        terms_ref[step] = products[:sums_rows]
-        picks_ref[step] = products[sums_rows:].astype(jnp.bfloat16)
-
-
-def combine_kernel(
+        for part in range(3):
+            rows = products[tokens * part : tokens * (part + 1)]
+            halves = parted([rows[:, i : i + LANES] for i in range(0, width, LANES)])
+            for parity, tiles in enumerate(halves):
+                packed = packed_half(tiles)
+                if part < 2:
+                    terms_ref[step, parity, part] = packed
+                else:
+                    picks_ref[step, parity] = packed.astype(jnp.bfloat16)
+
+
+def gradient_share(step, parity, factors_ref, terms_ref, picks_ref):
+    sums = terms_ref[step, parity, 0] + factors_ref[1] * terms_ref[step, parity, 1]
+    return factors_ref[0] * sums - factors_ref[2] * picks_ref[step, parity].astype(jnp.float32)
+
+
+def give_kernel(
     place_ref,
     scale_ref,
     stats_ref,
@@ -351,12 +379,10 @@
     tokens_ref,
     terms_ref,
     picks_ref,
-    keep_ref,
     give_ref,
+    factors_ref,
     loss_ref,
 ):
-    core = place_ref[0] % 2
-    chips, _, width = terms_ref.shape
     tokens = tokens_ref.shape[0]
     tops, sums, teacher_tops, teacher_sums, crosses, targets = [
         stats_ref[:, i, :tokens] for i in range(6)
@@ -381,18 +407,20 @@
     share = tokens_ref[:, 1:2]
     weight = share * scale_ref[0]
     loss_ref[...] = jnp.sum(share * columns[:, 2:3], axis=0, keepdims=True)
-    factor = weight * columns[:, 0:1]
-    level = columns[:, 1:2]
-    weight = sample_weight * weight
-    for step in range(chips):
-        block = (
-            factor * (terms_ref[step, :tokens] + level * terms_ref[step, tokens:])
-            - weight * picks_ref[step].astype(jnp.float32)
-        )
-        first, second = parted([block[:, i : i + LANES] for i in range(0, width, LANES)])
-        first, second = packed_half(first), packed_half(second)
-        keep_ref[step] = jnp.where(core == 0, first, second)
-        give_ref[step] = jnp.where(core == 0, second, first).astype(jnp.bfloat16)
+    for i, column in enumerate(
+        (weight * columns[:, 0:1], columns[:, 1:2], sample_weight * weight)
+    ):
+        factors_ref[i] = packed_half([jnp.broadcast_to(column, (tokens, LANES))] * 3)
+    parity = 1 - place_ref[0] % 2
+    for step in range(terms_ref.shape[0]):
+        share = gradient_share(step, parity, factors_ref, terms_ref, picks_ref)
+        give_ref[step] = share.astype(jnp.bfloat16)
+
+
+def keep_kernel(place_ref, factors_ref, terms_ref, picks_ref, keep_ref):
+    parity = place_ref[0] % 2
+    for step in range(terms_ref.shape[0]):
+        keep_ref[step] = gradient_share(step, parity, factors_ref, terms_ref, picks_ref)
 
 
 def sum_kernel(own_ref, *refs):
@@ -454,10 +482,21 @@
     )(place, *[in_hbm(operand) for operand in operands])
     steps = range(1, chips)
     near = [packed[0]] + [along_chips(packed[step], step) for step in steps]
-    far = [
-        swap_cores(jnp.stack(near[chips // 2 + 1 :])),
-        swap_cores(jnp.stack(near[: chips // 2 + 1])),
-    ]
+    first, last = jnp.stack(near[: chips // 2 + 1]), jnp.stack(near[chips // 2 + 1 :])
+    early = pl.pallas_call(
+        functools.partial(preload_kernel, chips=chips),
+        out_shape=vmem_array((EARLY, shard_rows, width), head.dtype),
+        in_specs=[smem] + [hbm] * 2,
+        out_specs=vmem,
+        scratch_shapes=[pltpu.SemaphoreType.DMA((EARLY,))],
+        compiler_params=params,
+        cost_estimate=pl.CostEstimate(
+            flops=0, bytes_accessed=4 * EARLY * shard_rows * width, transcendentals=0
+        ),
+        name="preload",
+    )(place, head, near[3])
+    last, early = lax.optimization_barrier((last, early))
+    far = [swap_cores(last), swap_cores(first)]
 
     rows, stats = pl.pallas_call(
         functools.partial(logits_kernel, chips=chips),
@@ -465,15 +504,15 @@
             hbm_array((3 * tokens, shard_rows), jnp.bfloat16),
             jax.ShapeDtypeStruct((count, STATS, pl.cdiv(tokens, LANES) * LANES), jnp.float32),
         ),
-        in_specs=[smem] + [vmem] * (chips + 4) + [hbm],
+        in_specs=[smem] + [vmem] * (chips + 5) + [hbm],
         out_specs=[hbm, vmem],
         scratch_shapes=[
-            head_scratch,
+            pltpu.VMEM((chips - EARLY, shard_rows, width), head.dtype),
             rows_scratch,
             pltpu.VMEM((chips, tokens, width), jnp.bfloat16),
             pltpu.VMEM((tokens, shard_rows + LANES // 2), jnp.float32),
             pltpu.VMEM((tokens, shard_rows), jnp.float32),
-            head_sems,
+            pltpu.SemaphoreType.DMA((chips - EARLY,)),
             rows_sem,
         ],
         compiler_params=params,
@@ -481,15 +520,15 @@
             flops=2 * tokens * head.size, bytes_accessed=2 * head.size, transcendentals=0
         ),
         name="logits",
-    )(place, *near[::-1], *far, in_vmem(owner), in_vmem(table), head)
+    )(place, *near[::-1], *far, in_vmem(owner), in_vmem(table), in_vmem(early), head)
 
     all_stats = lax.all_to_all(stats, "vocab", split_axis=0, concat_axis=0, tiled=True)
 
     terms, picks = pl.pallas_call(
         products_kernel,
         out_shape=(
-            vmem_array((chips, 2 * tokens, width), jnp.float32),
-            vmem_array((chips, tokens, width), jnp.bfloat16),
+            vmem_array((chips, 2, 2, hidden_rows, LANES), jnp.float32),
+            vmem_array((chips, 2, hidden_rows, LANES), jnp.bfloat16),
         ),
         in_specs=[smem, hbm, hbm],
         out_specs=[vmem] * 2,
@@ -501,21 +540,33 @@
         name="products",
     )(place, in_hbm(rows), head)
 
-    keep, give, loss = pl.pallas_call(
-        combine_kernel,
+    terms, picks = in_vmem(terms), in_vmem(picks)
+    give, factors, loss = pl.pallas_call(
+        give_kernel,
         out_shape=(
-            vmem_array((chips, hidden_rows, LANES), jnp.float32),
             vmem_array((chips, hidden_rows, LANES), jnp.bfloat16),
+            vmem_array((3, hidden_rows, LANES), jnp.float32),
             jax.ShapeDtypeStruct((1, 1), jnp.float32),
         ),
         in_specs=[smem] * 2 + [vmem] * 5,
         out_specs=[vmem] * 3,
         compiler_params=params,
-        name="combine",
-    )(place, loss_scale, all_stats, stats, in_vmem(table), in_vmem(terms), in_vmem(picks))
-
-    sums = keep + swap_cores(give).astype(jnp.float32)
-    shares = [along_chips(sums[step].astype(jnp.bfloat16), step) for step in steps[::-1]]
+        name="give",
+    )(place, loss_scale, all_stats, stats, in_vmem(table), terms, picks)
+    taken = swap_cores(give)
+    keep = pl.pallas_call(
+        keep_kernel,
+        out_shape=vmem_array((chips, hidden_rows, LANES), jnp.float32),
+        in_specs=[smem] + [vmem] * 3,
+        out_specs=vmem,
+        compiler_params=params,
+        cost_estimate=pl.CostEstimate(
+            flops=4 * terms.size, bytes_accessed=4 * terms.size, transcendentals=0
+        ),
+        name="keep",
+    )(place, in_vmem(factors), terms, picks)
+    sums = keep + taken.astype(jnp.float32)
+    shares = [along_chips(sums[step].astype(jnp.bfloat16), step) for step in steps]
     total = pl.pallas_call(
         sum_kernel,
         out_shape=jax.ShapeDtypeStruct((tokens, half), jnp.bfloat16),

time: 60.8 us -> 61.9 us (1.018)
  waiting for transfers between devices: 8.22 us -> 4.67 us
  Pallas kernels: 18.8 us -> 21.7 us
  starting transfers between devices: 31.8 us -> 33.6 us
    pallas_call x2 -> x4, Pallas kernels: 8.16 us -> 11.8 us  [the longest x1 7.38 us: paired_shards(): pl.pallas_call(products_kernel, out_shape=(vmem_array((chips, 2, 2, hidde...]
    ppermute x14, waiting for transfers between devices: 5.26 us -> 3.19 us  [along_chips(): lax.ppermute(array, 'vocab', [(i, (i + 2 * step) % count) for i in range(...]
    ppermute x3, waiting for transfers between devices: 2.39 us -> 1.48 us  [swap_cores(): return lax.ppermute(array, 'vocab', [(i, i ^ 1) for i in range(count)])]
    ppermute x3, starting transfers between devices: 0.14 us -> 1.01 us  [swap_cores(): return lax.ppermute(array, 'vocab', [(i, i ^ 1) for i in range(count)])]
    pallas_call x1, Pallas kernels: 8.44 us -> 7.7 us  [paired_shards(): pl.pallas_call(functools.partial(logits_kernel, chips=chips), out_shape=(...]
  transfers between devices with their start and end apart: 18 -> 18, of which waited for: 11 -> 7; matrix products, arithmetic and copies ran while one was open for 0% -> 0% of each run, Pallas kernels for 10% -> 16%
where the time goes in v13:
time: 61.9 us; the launch traced here: 61.6 us
  starting transfers between devices  33.6 us (54%)
  Pallas kernels  21.7 us (35%)
  waiting for transfers between devices  4.67 us (8%)
  between operations  1.44 us (2%)
    ppermute x14, starting transfers between devices, along_chips(): lax.ppermute(array, 'vocab', [(i, (i + 2 * step) % count) for i in range(...  26.3 us
    pallas_call x1, Pallas kernels, paired_shards(): pl.pallas_call(functools.partial(logits_kernel, chips=chips), out_shape=(...  7.7 us
    pallas_call x1, Pallas kernels, paired_shards(): pl.pallas_call(products_kernel, out_shape=(vmem_array((chips, 2, 2, hidde...  7.38 us
    all_to_all x1, starting transfers between devices, paired_shards(): lax.all_to_all(stats, 'vocab', split_axis=0, concat_axis=0, tiled=True)  6.21 us
    ppermute x14, waiting for transfers between devices, along_chips(): lax.ppermute(array, 'vocab', [(i, (i + 2 * step) % count) for i in range(...  3.19 us
    pallas_call x1, Pallas kernels, paired_shards(): pl.pallas_call(functools.partial(preload_kernel, chips=chips), out_shape=...  2.4 us
    pallas_call x1, Pallas kernels, paired_shards(): pl.pallas_call(give_kernel, out_shape=(vmem_array((chips, hidden_rows, LA...  1.79 us
    pallas_call x1, Pallas kernels, paired_shards(): pl.pallas_call(functools.partial(pack_kernel, shard_rows=shard_rows), out...  1.52 us
  transfers between devices with their start and end apart: 18, of which 7 were waited for; matrix products, arithmetic and copies ran while one was open for 0% of the time, Pallas kernels for 16%

profile of v13, /device:TPU:0, one launch (start us, length us, event | category | flops | bytes accessed | tf_op | source)
XLA Modules:
  0.0 61.6 jit_solution(12065953939496528307)
XLA Ops:
  0.6 1.5 %pack.1 = (bf16[8,240,128]{2,1,0:T(8,128)(2,1)S(1)}, bf16[64,64]{1,0:T(8,128)(2,1)S(1)}, f32[64,128]{1,0:T(8,128)S(1)}) custom-call(s32[1]{0:T(128)} %bitcast.place_ref, bf16[64,320]{1,0:T(8,128)(2,1)} %refs_0_.1, bf16[4,19456]{1,0:T(4,128)(2,1)} %refs_1_.1, f32[4,608]{1,0:T(4,128)} %refs_2_.1, s32[1,64]{1,0:T(1,128)} %bitcast.51, s32[1,64]{1,0:T(1,128)} %bitcast.52, ...), custom_call_target="tpu_custom_call" | custom-call | tf_op jit(solution)/shard_map/pack/pallas_call | solution.py:466
  2.2 3.0 %collective-permute-start.6 = (bf16[240,128]{1,0:T(8,128)(2,1)S(1)}, bf16[240,128]{1,0:T(8,128)(2,1)S(1)}, u32[]{:S(2)}, u32[]{:S(2)}) collective-permute-start(bf16[240,128]{1,0:T(8,128)(2,1)S(1)} %get-tuple-element.30), channel_id=1, source_target_pairs={{0,2},{1,3},{2,4},{3,5},{4,6},{5,7},{6,8},{7,9},{8,10},{9,11},{10,... | collective-permute-start | bytes 184328 | tf_op jit(solution)/shard_map/ppermute | solution.py:52
  5.2 1.6 %collective-permute-start.5 = (bf16[240,128]{1,0:T(8,128)(2,1)S(1)}, bf16[240,128]{1,0:T(8,128)(2,1)S(1)}, u32[]{:S(2)}, u32[]{:S(2)}) collective-permute-start(bf16[240,128]{1,0:T(8,128)(2,1)S(1)} %get-tuple-element.31), channel_id=1, source_target_pairs={{0,4},{1,5},{2,6},{3,7},{4,8},{5,9},{6,10},{7,11},{8,12},{9,13},{1... | collective-permute-start | bytes 184328 | tf_op jit(solution)/shard_map/ppermute | solution.py:52
  6.8 2.5 %collective-permute-start.4 = (bf16[240,128]{1,0:T(8,128)(2,1)S(1)}, bf16[240,128]{1,0:T(8,128)(2,1)S(1)}, u32[]{:S(2)}, u32[]{:S(2)}) collective-permute-start(bf16[240,128]{1,0:T(8,128)(2,1)S(1)} %get-tuple-element.32), channel_id=1, source_target_pairs={{0,6},{1,7},{2,8},{3,9},{4,10},{5,11},{6,12},{7,13},{8,14},{9,15},... | collective-permute-start | bytes 184328 | tf_op jit(solution)/shard_map/ppermute | solution.py:52
  9.3 1.2 %collective-permute-start.3 = (bf16[240,128]{1,0:T(8,128)(2,1)S(1)}, bf16[240,128]{1,0:T(8,128)(2,1)S(1)}, u32[]{:S(2)}, u32[]{:S(2)}) collective-permute-start(bf16[240,128]{1,0:T(8,128)(2,1)S(1)} %get-tuple-element.33), channel_id=1, source_target_pairs={{0,8},{1,9},{2,10},{3,11},{4,12},{5,13},{6,14},{7,15},{8,0},{9,1},... | collective-permute-start | bytes 184328 | tf_op jit(solution)/shard_map/ppermute | solution.py:52
  10.6 2.6 %collective-permute-start.2 = (bf16[240,128]{1,0:T(8,128)(2,1)S(1)}, bf16[240,128]{1,0:T(8,128)(2,1)S(1)}, u32[]{:S(2)}, u32[]{:S(2)}) collective-permute-start(bf16[240,128]{1,0:T(8,128)(2,1)S(1)} %get-tuple-element.34), channel_id=1, source_target_pairs={{0,10},{1,11},{2,12},{3,13},{4,14},{5,15},{6,0},{7,1},{8,2},{9,3},... | collective-permute-start | bytes 184328 | tf_op jit(solution)/shard_map/ppermute | solution.py:52
  13.2 1.3 %collective-permute-start.1 = (bf16[240,128]{1,0:T(8,128)(2,1)S(1)}, bf16[240,128]{1,0:T(8,128)(2,1)S(1)}, u32[]{:S(2)}, u32[]{:S(2)}) collective-permute-start(bf16[240,128]{1,0:T(8,128)(2,1)S(1)} %get-tuple-element.35), channel_id=1, source_target_pairs={{0,12},{1,13},{2,14},{3,15},{4,0},{5,1},{6,2},{7,3},{8,4},{9,5},{1... | collective-permute-start | bytes 184328 | tf_op jit(solution)/shard_map/ppermute | solution.py:52
  14.6 1.5 %collective-permute-start = (bf16[240,128]{1,0:T(8,128)(2,1)S(1)}, bf16[240,128]{1,0:T(8,128)(2,1)S(1)}, u32[]{:S(2)}, u32[]{:S(2)}) collective-permute-start(bf16[240,128]{1,0:T(8,128)(2,1)S(1)} %get-tuple-element.36), channel_id=1, source_target_pairs={{0,14},{1,15},{2,0},{3,1},{4,2},{5,3},{6,4},{7,5},{8,6},{9,7},{10,... | collective-permute-start | bytes 184328 | tf_op jit(solution)/shard_map/ppermute | solution.py:52
  16.8 2.4 %preload.1.refs_12_ = bf16[3,1216,640]{2,1,0:T(8,128)(2,1)S(1)} custom-call(s32[1]{0:T(128)} %bitcast.place_ref, bf16[1216,5120]{1,0:T(8,128)(2,1)} %head_ref.3, bf16[240,128]{1,0:T(8,128)(2,1)S(1)} %collective-permute-done.4._.refs_4_), custom_call_target="tpu_custom_call" | custom-call | bytes 9338880 | tf_op jit(solution)/shard_map/preload/pallas_call | solution.py:486
  20.9 7.7 %logits.1 = (bf16[192,1216]{1,0:T(8,128)(2,1)}, f32[16,8,128]{2,1,0:T(8,128)}) custom-call(s32[1]{0:T(128)} %bitcast.place_ref, bf16[240,128]{1,0:T(8,128)(2,1)S(1)} %collective-permute-done.refs_0_, bf16[240,128]{1,0:T(8,128)(2,1)S(1)} %collective-permute-done.1.refs_1_, bf16[240,128]{1,0:T(8,128)(2,1)S(1)} %collective-permute-done.2.refs_2_, ...), custom_call_target="tpu_custom_call" | custom-call | flops 796917760 | bytes 12451840 | tf_op jit(solution)/shard_map/logits/pallas_call | solution.py:501
  28.6 6.2 %all-to-all-start = ((f32[16,8,128]{2,1,0:T(8,128)}), f32[16,8,128]{2,1,0:T(8,128)S(1)}, u32[]{:S(2)}, u32[]{:S(2)}) async-start(f32[16,8,128]{2,1,0:T(8,128)} %get-tuple-element.19.own_ref), calls=%async_computation | async-start | bytes 131072 | tf_op jit(solution)/shard_map/all_to_all | solution.py:525
  34.8 7.4 %products.1 = (f32[8,2,2,160,128]{4,3,2,1,0:T(8,128)S(1)}, bf16[8,2,160,128]{3,2,1,0:T(8,128)(2,1)S(1)}) custom-call(s32[1]{0:T(128)} %bitcast.place_ref, bf16[192,1216]{1,0:T(8,128)(2,1)} %get-tuple-element.20.rows_ref, bf16[1216,5120]{1,0:T(8,128)(2,1)} %head_ref.3), custom_call_target="tpu_custom_call" | custom-call | flops 2390753280 | bytes 12451840 | tf_op jit(solution)/shard_map/products/pallas_call | solution.py:527
  42.2 1.8 %give.1 = (bf16[8,160,128]{2,1,0:T(8,128)(2,1)S(1)}, f32[3,160,128]{2,1,0:T(8,128)S(1)}, f32[1,1]{1,0:T(1,128)}) custom-call(s32[1]{0:T(128)} %bitcast.place_ref, f32[1]{0:T(128)S(6)} %copy.14.scale_ref, f32[16,8,128]{2,1,0:T(8,128)S(1)} %all-to-all-done.stats_ref, f32[16,8,128]{2,1,0:T(8,128)} %get-tuple-element.19.own_ref, ...), custom_call_target="tpu_custom_call" | custom-call | tf_op jit(solution)/shard_map/give/pallas_call | solution.py:544
  44.6 1.1 %collective-permute-done.9 = bf16[8,160,128]{2,1,0:T(8,128)(2,1)S(1)} collective-permute-done((bf16[8,160,128]{2,1,0:T(8,128)(2,1)S(1)}, bf16[8,160,128]{2,1,0:T(8,128)(2,1)S(1)}, u32[]{:S(2)}, u32[]{:S(2)}) %collective-permute-start.9) | collective-permute-done | bytes 327712 | tf_op jit(solution)/shard_map/ppermute | solution.py:47
  45.8 2.0 %collective-permute-start.10 = (bf16[160,128]{1,0:T(8,128)(2,1)S(1)}, bf16[160,128]{1,0:T(8,128)(2,1)S(1)}, u32[]{:S(2)}, u32[]{:S(2)}) collective-permute-start(bf16[160,128]{1,0:T(8,128)(2,1)S(1)} %get-tuple-element.43), channel_id=1, source_target_pairs={{0,2},{1,3},{2,4},{3,5},{4,6},{5,7},{6,8},{7,9},{8,10},{9,11},{10,... | collective-permute-start | bytes 122888 | tf_op jit(solution)/shard_map/ppermute | solution.py:52
  47.8 1.5 %collective-permute-start.11 = (bf16[160,128]{1,0:T(8,128)(2,1)S(1)}, bf16[160,128]{1,0:T(8,128)(2,1)S(1)}, u32[]{:S(2)}, u32[]{:S(2)}) collective-permute-start(bf16[160,128]{1,0:T(8,128)(2,1)S(1)} %get-tuple-element.42), channel_id=1, source_target_pairs={{0,4},{1,5},{2,6},{3,7},{4,8},{5,9},{6,10},{7,11},{8,12},{9,13},{1... | collective-permute-start | bytes 122888 | tf_op jit(solution)/shard_map/ppermute | solution.py:52
  49.2 2.3 %collective-permute-start.12 = (bf16[160,128]{1,0:T(8,128)(2,1)S(1)}, bf16[160,128]{1,0:T(8,128)(2,1)S(1)}, u32[]{:S(2)}, u32[]{:S(2)}) collective-permute-start(bf16[160,128]{1,0:T(8,128)(2,1)S(1)} %get-tuple-element.41), channel_id=1, source_target_pairs={{0,6},{1,7},{2,8},{3,9},{4,10},{5,11},{6,12},{7,13},{8,14},{9,15},... | collective-permute-start | bytes 122888 | tf_op jit(solution)/shard_map/ppermute | solution.py:52
  51.6 1.5 %collective-permute-start.13 = (bf16[160,128]{1,0:T(8,128)(2,1)S(1)}, bf16[160,128]{1,0:T(8,128)(2,1)S(1)}, u32[]{:S(2)}, u32[]{:S(2)}) collective-permute-start(bf16[160,128]{1,0:T(8,128)(2,1)S(1)} %get-tuple-element.40), channel_id=1, source_target_pairs={{0,8},{1,9},{2,10},{3,11},{4,12},{5,13},{6,14},{7,15},{8,0},{9,1},... | collective-permute-start | bytes 122888 | tf_op jit(solution)/shard_map/ppermute | solution.py:52
  53.1 2.4 %collective-permute-start.14 = (bf16[160,128]{1,0:T(8,128)(2,1)S(1)}, bf16[160,128]{1,0:T(8,128)(2,1)S(1)}, u32[]{:S(2)}, u32[]{:S(2)}) collective-permute-start(bf16[160,128]{1,0:T(8,128)(2,1)S(1)} %get-tuple-element.39), channel_id=1, source_target_pairs={{0,10},{1,11},{2,12},{3,13},{4,14},{5,15},{6,0},{7,1},{8,2},{9,3},... | collective-permute-start | bytes 122888 | tf_op jit(solution)/shard_map/ppermute | solution.py:52
  55.4 1.5 %collective-permute-start.15 = (bf16[160,128]{1,0:T(8,128)(2,1)S(1)}, bf16[160,128]{1,0:T(8,128)(2,1)S(1)}, u32[]{:S(2)}, u32[]{:S(2)}) collective-permute-start(bf16[160,128]{1,0:T(8,128)(2,1)S(1)} %get-tuple-element.38), channel_id=1, source_target_pairs={{0,12},{1,13},{2,14},{3,15},{4,0},{5,1},{6,2},{7,3},{8,4},{9,5},{1... | collective-permute-start | bytes 122888 | tf_op jit(solution)/shard_map/ppermute | solution.py:52
  56.9 1.5 %collective-permute-start.16 = (bf16[160,128]{1,0:T(8,128)(2,1)S(1)}, bf16[160,128]{1,0:T(8,128)(2,1)S(1)}, u32[]{:S(2)}, u32[]{:S(2)}) collective-permute-start(bf16[160,128]{1,0:T(8,128)(2,1)S(1)} %get-tuple-element.37), channel_id=1, source_target_pairs={{0,14},{1,15},{2,0},{3,1},{4,2},{5,3},{6,4},{7,5},{8,6},{9,7},{10,... | collective-permute-start | bytes 122888 | tf_op jit(solution)/shard_map/ppermute | solution.py:52
  58.5 1.0 %collective-permute-done.15.refs_5_ = bf16[160,128]{1,0:T(8,128)(2,1)S(1)} collective-permute-done((bf16[160,128]{1,0:T(8,128)(2,1)S(1)}, bf16[160,128]{1,0:T(8,128)(2,1)S(1)}, u32[]{:S(2)}, u32[]{:S(2)}) %collective-permute-start.15) | collective-permute-done | bytes 40992 | tf_op jit(solution)/shard_map/ppermute | solution.py:52
  59.4 1.5 %collective-permute-done.16.refs_6_ = bf16[160,128]{1,0:T(8,128)(2,1)S(1)} collective-permute-done((bf16[160,128]{1,0:T(8,128)(2,1)S(1)}, bf16[160,128]{1,0:T(8,128)(2,1)S(1)}, u32[]{:S(2)}, u32[]{:S(2)}) %collective-permute-start.16) | collective-permute-done | bytes 40992 | tf_op jit(solution)/shard_map/ppermute | solution.py:52
  60.9 0.7 %total.1 = bf16[64,320]{1,0:T(8,128)(2,1)} custom-call(f32[160,128]{1,0:T(8,128)S(1)} %slice_bitcast_fusion.own_ref, bf16[160,128]{1,0:T(8,128)(2,1)S(1)} %collective-permute-done.10.refs_0_, bf16[160,128]{1,0:T(8,128)(2,1)S(1)} %collective-permute-done.11.refs_1_, bf16[160,128]{1,0:T(8,128)(2,1)S(1)} %collective-permute-done.12.refs_2_, ...), custom_call_target="tpu_custom_call" | custom-call | tf_op jit(solution)/shard_map/total/pallas_call | solution.py:570
  (28 shorter events, 2.6 us)
Async XLA Ops:
  2.2 11.0 %collective-permute-start.6 = (bf16[240,128]{1,0:T(8,128)(2,1)S(1)}, bf16[240,128]{1,0:T(8,128)(2,1)S(1)}, u32[]{:S(2)}, u32[]{:S(2)}) collective-permute-start(bf16[240,128]{1,0:T(8,128)(2,1)S(1)} %get-tuple-element.30), channel_id=1, source_target_pairs={{0,2},{1,3},{2,4},{3,5},{4,6},{5,7},{6,8},{7,9},{8,10},{9,11},{10,... | collective-permute-start | bytes 184328 | tf_op jit(solution)/shard_map/ppermute | solution.py:52
  5.2 9.4 %collective-permute-start.5 = (bf16[240,128]{1,0:T(8,128)(2,1)S(1)}, bf16[240,128]{1,0:T(8,128)(2,1)S(1)}, u32[]{:S(2)}, u32[]{:S(2)}) collective-permute-start(bf16[240,128]{1,0:T(8,128)(2,1)S(1)} %get-tuple-element.31), channel_id=1, source_target_pairs={{0,4},{1,5},{2,6},{3,7},{4,8},{5,9},{6,10},{7,11},{8,12},{9,13},{1... | collective-permute-start | bytes 184328 | tf_op jit(solution)/shard_map/ppermute | solution.py:52
  6.8 9.4 %collective-permute-start.4 = (bf16[240,128]{1,0:T(8,128)(2,1)S(1)}, bf16[240,128]{1,0:T(8,128)(2,1)S(1)}, u32[]{:S(2)}, u32[]{:S(2)}) collective-permute-start(bf16[240,128]{1,0:T(8,128)(2,1)S(1)} %get-tuple-element.32), channel_id=1, source_target_pairs={{0,6},{1,7},{2,8},{3,9},{4,10},{5,11},{6,12},{7,13},{8,14},{9,15},... | collective-permute-start | bytes 184328 | tf_op jit(solution)/shard_map/ppermute | solution.py:52
  9.3 7.4 %collective-permute-start.3 = (bf16[240,128]{1,0:T(8,128)(2,1)S(1)}, bf16[240,128]{1,0:T(8,128)(2,1)S(1)}, u32[]{:S(2)}, u32[]{:S(2)}) collective-permute-start(bf16[240,128]{1,0:T(8,128)(2,1)S(1)} %get-tuple-element.33), channel_id=1, source_target_pairs={{0,8},{1,9},{2,10},{3,11},{4,12},{5,13},{6,14},{7,15},{8,0},{9,1},... | collective-permute-start | bytes 184328 | tf_op jit(solution)/shard_map/ppermute | solution.py:52
  10.6 8.7 %collective-permute-start.2 = (bf16[240,128]{1,0:T(8,128)(2,1)S(1)}, bf16[240,128]{1,0:T(8,128)(2,1)S(1)}, u32[]{:S(2)}, u32[]{:S(2)}) collective-permute-start(bf16[240,128]{1,0:T(8,128)(2,1)S(1)} %get-tuple-element.34), channel_id=1, source_target_pairs={{0,10},{1,11},{2,12},{3,13},{4,14},{5,15},{6,0},{7,1},{8,2},{9,3},... | collective-permute-start | bytes 184328 | tf_op jit(solution)/shard_map/ppermute | solution.py:52
  13.2 6.0 %collective-permute-start.1 = (bf16[240,128]{1,0:T(8,128)(2,1)S(1)}, bf16[240,128]{1,0:T(8,128)(2,1)S(1)}, u32[]{:S(2)}, u32[]{:S(2)}) collective-permute-start(bf16[240,128]{1,0:T(8,128)(2,1)S(1)} %get-tuple-element.35), channel_id=1, source_target_pairs={{0,12},{1,13},{2,14},{3,15},{4,0},{5,1},{6,2},{7,3},{8,4},{9,5},{1... | collective-permute-start | bytes 184328 | tf_op jit(solution)/shard_map/ppermute | solution.py:52
  14.6 4.7 %collective-permute-start = (bf16[240,128]{1,0:T(8,128)(2,1)S(1)}, bf16[240,128]{1,0:T(8,128)(2,1)S(1)}, u32[]{:S(2)}, u32[]{:S(2)}) collective-permute-start(bf16[240,128]{1,0:T(8,128)(2,1)S(1)} %get-tuple-element.36), channel_id=1, source_target_pairs={{0,14},{1,15},{2,0},{3,1},{4,2},{5,3},{6,4},{7,5},{8,6},{9,7},{10,... | collective-permute-start | bytes 184328 | tf_op jit(solution)/shard_map/ppermute | solution.py:52
  16.8 4.2 %collective-permute-start.8 = (bf16[5,240,128]{2,1,0:T(8,128)(2,1)S(1)}, bf16[5,240,128]{2,1,0:T(8,128)(2,1)S(1)}, u32[]{:S(2)}, u32[]{:S(2)}) collective-permute-start(bf16[5,240,128]{2,1,0:T(8,128)(2,1)S(1)} %bitcast_dynamic-update-slice_fusion), channel_id=1, source_target_pairs={{0,1},{1,0},{2,3},{3,2},{4,5},{5,4},{6,7},{7,6},{8,9},{9,8},{10,11... | collective-permute-start | bytes 921608 | tf_op jit(solution)/shard_map/ppermute | solution.py:47
  19.3 1.6 %collective-permute-start.7 = (bf16[3,240,128]{2,1,0:T(8,128)(2,1)S(1)}, bf16[3,240,128]{2,1,0:T(8,128)(2,1)S(1)}, u32[]{:S(2)}, u32[]{:S(2)}) collective-permute-start(bf16[3,240,128]{2,1,0:T(8,128)(2,1)S(1)} %pad_maximum_fusion), channel_id=1, source_target_pairs={{0,1},{1,0},{2,3},{3,2},{4,5},{5,4},{6,7},{7,6},{8,9},{9,8},{10,11... | collective-permute-start | bytes 552968 | tf_op jit(solution)/shard_map/ppermute | solution.py:47
  28.6 13.6 %all-to-all-start = ((f32[16,8,128]{2,1,0:T(8,128)}), f32[16,8,128]{2,1,0:T(8,128)S(1)}, u32[]{:S(2)}, u32[]{:S(2)}) async-start(f32[16,8,128]{2,1,0:T(8,128)} %get-tuple-element.19.own_ref), calls=%async_computation | async-start | bytes 131072 | tf_op jit(solution)/shard_map/all_to_all | solution.py:525
  44.0 1.6 %collective-permute-start.9 = (bf16[8,160,128]{2,1,0:T(8,128)(2,1)S(1)}, bf16[8,160,128]{2,1,0:T(8,128)(2,1)S(1)}, u32[]{:S(2)}, u32[]{:S(2)}) collective-permute-start(bf16[8,160,128]{2,1,0:T(8,128)(2,1)S(1)} %get-tuple-element.24), channel_id=1, source_target_pairs={{0,1},{1,0},{2,3},{3,2},{4,5},{5,4},{6,7},{7,6},{8,9},{9,8},{10,11... | collective-permute-start | bytes 983048 | tf_op jit(solution)/shard_map/ppermute | solution.py:47
  45.8 9.6 %collective-permute-start.10 = (bf16[160,128]{1,0:T(8,128)(2,1)S(1)}, bf16[160,128]{1,0:T(8,128)(2,1)S(1)}, u32[]{:S(2)}, u32[]{:S(2)}) collective-permute-start(bf16[160,128]{1,0:T(8,128)(2,1)S(1)} %get-tuple-element.43), channel_id=1, source_target_pairs={{0,2},{1,3},{2,4},{3,5},{4,6},{5,7},{6,8},{7,9},{8,10},{9,11},{10,... | collective-permute-start | bytes 122888 | tf_op jit(solution)/shard_map/ppermute | solution.py:52
  47.8 9.1 %collective-permute-start.11 = (bf16[160,128]{1,0:T(8,128)(2,1)S(1)}, bf16[160,128]{1,0:T(8,128)(2,1)S(1)}, u32[]{:S(2)}, u32[]{:S(2)}) collective-permute-start(bf16[160,128]{1,0:T(8,128)(2,1)S(1)} %get-tuple-element.42), channel_id=1, source_target_pairs={{0,4},{1,5},{2,6},{3,7},{4,8},{5,9},{6,10},{7,11},{8,12},{9,13},{1... | collective-permute-start | bytes 122888 | tf_op jit(solution)/shard_map/ppermute | solution.py:52
  49.2 9.1 %collective-permute-start.12 = (bf16[160,128]{1,0:T(8,128)(2,1)S(1)}, bf16[160,128]{1,0:T(8,128)(2,1)S(1)}, u32[]{:S(2)}, u32[]{:S(2)}) collective-permute-start(bf16[160,128]{1,0:T(8,128)(2,1)S(1)} %get-tuple-element.41), channel_id=1, source_target_pairs={{0,6},{1,7},{2,8},{3,9},{4,10},{5,11},{6,12},{7,13},{8,14},{9,15},... | collective-permute-start | bytes 122888 | tf_op jit(solution)/shard_map/ppermute | solution.py:52
  51.6 6.8 %collective-permute-start.13 = (bf16[160,128]{1,0:T(8,128)(2,1)S(1)}, bf16[160,128]{1,0:T(8,128)(2,1)S(1)}, u32[]{:S(2)}, u32[]{:S(2)}) collective-permute-start(bf16[160,128]{1,0:T(8,128)(2,1)S(1)} %get-tuple-element.40), channel_id=1, source_target_pairs={{0,8},{1,9},{2,10},{3,11},{4,12},{5,13},{6,14},{7,15},{8,0},{9,1},... | collective-permute-start | bytes 122888 | tf_op jit(solution)/shard_map/ppermute | solution.py:52
  53.1 5.4 %collective-permute-start.14 = (bf16[160,128]{1,0:T(8,128)(2,1)S(1)}, bf16[160,128]{1,0:T(8,128)(2,1)S(1)}, u32[]{:S(2)}, u32[]{:S(2)}) collective-permute-start(bf16[160,128]{1,0:T(8,128)(2,1)S(1)} %get-tuple-element.39), channel_id=1, source_target_pairs={{0,10},{1,11},{2,12},{3,13},{4,14},{5,15},{6,0},{7,1},{8,2},{9,3},... | collective-permute-start | bytes 122888 | tf_op jit(solution)/shard_map/ppermute | solution.py:52
  55.4 4.0 %collective-permute-start.15 = (bf16[160,128]{1,0:T(8,128)(2,1)S(1)}, bf16[160,128]{1,0:T(8,128)(2,1)S(1)}, u32[]{:S(2)}, u32[]{:S(2)}) collective-permute-start(bf16[160,128]{1,0:T(8,128)(2,1)S(1)} %get-tuple-element.38), channel_id=1, source_target_pairs={{0,12},{1,13},{2,14},{3,15},{4,0},{5,1},{6,2},{7,3},{8,4},{9,5},{1... | collective-permute-start | bytes 122888 | tf_op jit(solution)/shard_map/ppermute | solution.py:52
  56.9 4.0 %collective-permute-start.16 = (bf16[160,128]{1,0:T(8,128)(2,1)S(1)}, bf16[160,128]{1,0:T(8,128)(2,1)S(1)}, u32[]{:S(2)}, u32[]{:S(2)}) collective-permute-start(bf16[160,128]{1,0:T(8,128)(2,1)S(1)} %get-tuple-element.37), channel_id=1, source_target_pairs={{0,14},{1,15},{2,0},{3,1},{4,2},{5,3},{6,4},{7,5},{8,6},{9,7},{10,... | collective-permute-start | bytes 122888 | tf_op jit(solution)/shard_map/ppermute | solution.py:52

commit v14 on v13

--- a/solution.py
+++ b/solution.py
@@ -217,22 +217,42 @@
 
 
 def head_copies(head_ref, held_ref, sems, chips):
-    width = held_ref.shape[2]
+    width = held_ref.shape[1] // len(chips)
     copies = []
     for step, chip in enumerate(chips):
         columns = pl.ds(pl.multiple_of(chip * width, LANES), width)
         copies.append(
-            pltpu.make_async_copy(head_ref.at[:, columns], held_ref.at[step], sems.at[step])
+            pltpu.make_async_copy(
+                head_ref.at[:, columns],
+                held_ref.at[:, width * step : width * (step + 1)],
+                sems.at[step],
+            )
         )
     return copies
 
 
+def take(copies, steps):
+    for step in steps:
+        copies[step].wait()
+        if step + AHEAD < len(copies):
+            copies[step + AHEAD].start()
+
+
+def grouped(count, sizes):
+    groups, start = [], 0
+    while start < count:
+        size = min(sizes[min(len(groups), len(sizes) - 1)], count - start)
+        groups.append(range(start, start + size))
+        start += size
+    return groups
+
+
 def source_chips(place_ref, chips):
     return [lax.rem(place_ref[0] // 2 - step + chips, chips) for step in range(chips)]
 
 
 def preload_kernel(place_ref, head_ref, _, early_ref, sems, *, chips):
-    sources = source_chips(place_ref, chips)[: early_ref.shape[0]]
+    sources = source_chips(place_ref, chips)[:EARLY]
     copies = head_copies(head_ref, early_ref, sems, sources)
     for copy in copies:
         copy.start()
@@ -242,15 +262,14 @@
 
 def logits_kernel(place_ref, *refs, chips):
     near, far, refs = refs[:chips][::-1], refs[chips : chips + 2], refs[chips + 2 :]
-    owner_ref, tokens_ref, early_ref, head_ref, rows_ref, stats_ref = refs[:6]
-    held_ref, made_ref, hidden_ref, arrived_ref, teacher_ref, sems, made_sem = refs[6:]
+    owner_ref, tokens_ref, early_ref, head_ref, rows_ref, stats_ref, own_ref = refs[:7]
+    held_ref, made_ref, hidden_ref, arrived_ref, teacher_ref, sems, made_sem = refs[7:]
     core = place_ref[0] % 2
     sources = source_chips(place_ref, chips)
-    early = early_ref.shape[0]
-    copies = head_copies(head_ref, held_ref, sems, sources[early:])
+    copies = head_copies(head_ref, held_ref, sems, sources[EARLY:])
     for copy in copies[:AHEAD]:
         copy.start()
-    _, tokens, width = hidden_ref.shape
+    tokens, width = hidden_ref.shape[0], hidden_ref.shape[1] // chips
     shard_rows = head_ref.shape[0]
     hidden_rows = tokens * width // 2 // LANES
     slots = tokens // (2 * chips)
@@ -266,7 +285,8 @@
     def unpack_hidden(step):
         first, second = both(step, slice(0, hidden_rows))
         tiles = joined(unpacked_half(first, tokens), unpacked_half(second, tokens))
-        hidden_ref[step] = jnp.concatenate(tiles, axis=1).astype(jnp.bfloat16)
+        tiles = jnp.concatenate(tiles, axis=1).astype(jnp.bfloat16)
+        hidden_ref[:, width * step : width * (step + 1)] = tiles
 
     def unpack_teacher(step):
         first, second = both(step, slice(hidden_rows, near[0].shape[0]))
@@ -281,34 +301,31 @@
         rows = pl.ds(pl.multiple_of(2 * slots * sources[step], 2 * slots), 2 * slots)
         arrived_ref[rows] = jnp.concatenate(tiles, axis=1)
 
-    unpack_hidden(0)
-    logits = jnp.zeros((tokens, shard_rows), jnp.float32)
-    for chip in range(chips):
-        if chip >= early:
-            copies[chip - early].wait()
-        if 0 < chip + 1 - early and chip + AHEAD - early < len(copies):
-            copies[chip + AHEAD - early].start()
-        if chip + 1 < chips:
-            unpack_hidden(chip + 1)
-        if chip < chips // 2:
-            unpack_teacher(2 * chip)
-            unpack_teacher(2 * chip + 1)
-        if chip == chips // 2:
-            teacher = jnp.dot(
-                owner_ref[...],
-                arrived_ref[:, :shard_rows].astype(jnp.bfloat16),
-                preferred_element_type=jnp.float32,
-            )
-            teacher_top = jnp.max(teacher, axis=1, keepdims=True)
-            teacher_off = teacher - teacher_top
-            teacher_total = jnp.sum(jnp.exp(teacher_off), axis=1, keepdims=True)
-            teacher_ref[...] = teacher_off
-        logits += lax.dot_general(
-            hidden_ref[chip],
-            early_ref[chip] if chip < early else held_ref[chip - early],
+    def product(step, count, columns):
+        return lax.dot_general(
+            hidden_ref[:, width * step : width * (step + count)],
+            columns,
             (((1,), (1,)), ((), ())),
             preferred_element_type=jnp.float32,
         )
+
+    for step in range(chips):
+        unpack_hidden(step)
+        unpack_teacher(step)
+    logits = product(0, EARLY, early_ref[...])
+    teacher = jnp.dot(
+        owner_ref[...],
+        arrived_ref[:, :shard_rows].astype(jnp.bfloat16),
+        preferred_element_type=jnp.float32,
+    )
+    teacher_top = jnp.max(teacher, axis=1, keepdims=True)
+    teacher_off = teacher - teacher_top
+    teacher_total = jnp.sum(jnp.exp(teacher_off), axis=1, keepdims=True)
+    teacher_ref[...] = teacher_off
+    for group in grouped(len(copies), (3, 2)):
+        take(copies, group)
+        columns = held_ref[:, width * group.start : width * group.stop]
+        logits += product(EARLY + group.start, len(group), columns)
 
     top = jnp.max(logits, axis=1, keepdims=True)
     off = logits - top
@@ -333,7 +350,9 @@
     ):
         table = jnp.where(lane == place, column, table)
     stats = jnp.concatenate([table, jnp.zeros((stats_ref.shape[2] - tokens, LANES), jnp.float32)])
-    stats_ref[...] = jnp.broadcast_to(stats.T[None, :STATS], stats_ref.shape)
+    stats = stats.T[:STATS]
+    own_ref[...] = stats
+    stats_ref[...] = jnp.broadcast_to(stats[None], stats_ref.shape)
     out.wait()
 
 
@@ -342,28 +361,32 @@
 ):
     into = pltpu.make_async_copy(rows_ref, made_ref, made_sem)
     into.start()
-    chips = held_ref.shape[0]
+    chips = terms_ref.shape[0]
     targets = [lax.rem(place_ref[0] // 2 + step, chips) for step in range(chips)]
     copies = head_copies(head_ref, held_ref, sems, targets)
     for copy in copies[:AHEAD]:
         copy.start()
     into.wait()
     tokens = made_ref.shape[0] // 3
-    width = held_ref.shape[2]
-    for step, copy in enumerate(copies):
-        copy.wait()
-        if step + AHEAD < len(copies):
-            copies[step + AHEAD].start()
-        products = jnp.dot(made_ref[...], held_ref[step], preferred_element_type=jnp.float32)
-        for part in range(3):
-            rows = products[tokens * part : tokens * (part + 1)]
-            halves = parted([rows[:, i : i + LANES] for i in range(0, width, LANES)])
-            for parity, tiles in enumerate(halves):
-                packed = packed_half(tiles)
-                if part < 2:
-                    terms_ref[step, parity, part] = packed
-                else:
-                    picks_ref[step, parity] = packed.astype(jnp.bfloat16)
+    width = held_ref.shape[1] // chips
+    for group in grouped(chips, (2, 2, 2, 1)):
+        take(copies, group)
+        products = jnp.dot(
+            made_ref[...],
+            held_ref[:, width * group.start : width * group.stop],
+            preferred_element_type=jnp.float32,
+        )
+        for place, step in enumerate(group):
+            for part in range(3):
+                rows = products[tokens * part : tokens * (part + 1)]
+                columns = range(width * place, width * (place + 1), LANES)
+                halves = parted([rows[:, i : i + LANES] for i in columns])
+                for parity, tiles in enumerate(halves):
+                    packed = packed_half(tiles)
+                    if part < 2:
+                        terms_ref[step, parity, part] = packed
+                    else:
+                        picks_ref[step, parity] = packed.astype(jnp.bfloat16)
 
 
 def gradient_share(step, parity, factors_ref, terms_ref, picks_ref):
@@ -396,11 +419,11 @@
     divergence = cross / total - (student_log - teacher_log)
     student_lse = top + student_log
     per_token = divergence + sample_weight * (student_lse - target)
-    student_shift = own_ref[0, 0:1, :tokens] - top - student_log
-    teacher_shift = own_ref[0, 2:3, :tokens] - teacher_top - teacher_log
+    student_shift = own_ref[0:1, :tokens] - top - student_log
+    teacher_shift = own_ref[2:3, :tokens] - teacher_top - teacher_log
     factor = jnp.exp(student_shift)
     level = (
-        own_ref[0, 6:7, :tokens] + student_shift - teacher_shift - divergence + sample_weight
+        own_ref[6:7, :tokens] + student_shift - teacher_shift - divergence + sample_weight
     )
     zeros = jnp.zeros((LANES - 3, tokens), jnp.float32)
     columns = jnp.concatenate([factor, level, per_token, zeros], axis=0).T
@@ -417,7 +440,8 @@
         give_ref[step] = share.astype(jnp.bfloat16)
 
 
-def keep_kernel(place_ref, factors_ref, terms_ref, picks_ref, keep_ref):
+def keep_kernel(place_ref, factors_ref, found_ref, terms_ref, picks_ref, keep_ref, loss_ref):
+    loss_ref[...] = found_ref[...]
     parity = place_ref[0] % 2
     for step in range(terms_ref.shape[0]):
         keep_ref[step] = gradient_share(step, parity, factors_ref, terms_ref, picks_ref)
@@ -447,7 +471,7 @@
     hbm = pl.BlockSpec(memory_space=pl.ANY)
     params = pltpu.CompilerParams(vmem_limit_bytes=VMEM_LIMIT)
     head = in_hbm(head)
-    head_scratch = pltpu.VMEM((chips, shard_rows, width), head.dtype)
+    head_scratch = pltpu.VMEM((shard_rows, chips * width), head.dtype)
     head_sems = pltpu.SemaphoreType.DMA((chips,))
     rows_scratch = pltpu.VMEM((3 * tokens, shard_rows), jnp.bfloat16)
     rows_sem = pltpu.SemaphoreType.DMA
@@ -485,7 +509,7 @@
     first, last = jnp.stack(near[: chips // 2 + 1]), jnp.stack(near[chips // 2 + 1 :])
     early = pl.pallas_call(
         functools.partial(preload_kernel, chips=chips),
-        out_shape=vmem_array((EARLY, shard_rows, width), head.dtype),
+        out_shape=vmem_array((shard_rows, EARLY * width), head.dtype),
         in_specs=[smem] + [hbm] * 2,
         out_specs=vmem,
         scratch_shapes=[pltpu.SemaphoreType.DMA((EARLY,))],
@@ -498,18 +522,19 @@
     last, early = lax.optimization_barrier((last, early))
     far = [swap_cores(last), swap_cores(first)]
 
-    rows, stats = pl.pallas_call(
+    rows, stats, own_stats = pl.pallas_call(
         functools.partial(logits_kernel, chips=chips),
         out_shape=(
             hbm_array((3 * tokens, shard_rows), jnp.bfloat16),
             jax.ShapeDtypeStruct((count, STATS, pl.cdiv(tokens, LANES) * LANES), jnp.float32),
+            vmem_array((STATS, pl.cdiv(tokens, LANES) * LANES), jnp.float32),
         ),
         in_specs=[smem] + [vmem] * (chips + 5) + [hbm],
-        out_specs=[hbm, vmem],
+        out_specs=[hbm, vmem, vmem],
         scratch_shapes=[
-            pltpu.VMEM((chips - EARLY, shard_rows, width), head.dtype),
+            pltpu.VMEM((shard_rows, (chips - EARLY) * width), head.dtype),
             rows_scratch,
-            pltpu.VMEM((chips, tokens, width), jnp.bfloat16),
+            pltpu.VMEM((tokens, chips * width), jnp.bfloat16),
             pltpu.VMEM((tokens, shard_rows + LANES // 2), jnp.float32),
             pltpu.VMEM((tokens, shard_rows), jnp.float32),
             pltpu.SemaphoreType.DMA((chips - EARLY,)),
@@ -546,25 +571,28 @@
         out_shape=(
             vmem_array((chips, hidden_rows, LANES), jnp.bfloat16),
             vmem_array((3, hidden_rows, LANES), jnp.float32),
-            jax.ShapeDtypeStruct((1, 1), jnp.float32),
+            vmem_array((1, 1), jnp.float32),
         ),
         in_specs=[smem] * 2 + [vmem] * 5,
         out_specs=[vmem] * 3,
         compiler_params=params,
         name="give",
-    )(place, loss_scale, all_stats, stats, in_vmem(table), terms, picks)
+    )(place, loss_scale, all_stats, in_vmem(own_stats), in_vmem(table), terms, picks)
     taken = swap_cores(give)
-    keep = pl.pallas_call(
+    keep, loss = pl.pallas_call(
         keep_kernel,
-        out_shape=vmem_array((chips, hidden_rows, LANES), jnp.float32),
-        in_specs=[smem] + [vmem] * 3,
-        out_specs=vmem,
+        out_shape=(
+            vmem_array((chips, hidden_rows, LANES), jnp.float32),
+            jax.ShapeDtypeStruct((1, 1), jnp.float32),
+        ),
+        in_specs=[smem] + [vmem] * 4,
+        out_specs=[vmem] * 2,
         compiler_params=params,
         cost_estimate=pl.CostEstimate(
             flops=4 * terms.size, bytes_accessed=4 * terms.size, transcendentals=0
         ),
         name="keep",
-    )(place, in_vmem(factors), terms, picks)
+    )(place, in_vmem(factors), in_vmem(loss), terms, picks)
     sums = keep + taken.astype(jnp.float32)
     shares = [along_chips(sums[step].astype(jnp.bfloat16), step) for step in steps]
     total = pl.pallas_call(

time: 61.9 us -> 62.1 us (level)
  Pallas kernels: 21.7 us -> 23 us
  waiting for transfers between devices: 4.67 us -> 3.68 us
    pallas_call x1, Pallas kernels: 7.7 us -> 8.78 us  [paired_shards(): pl.pallas_call(functools.partial(logits_kernel, chips=chips), out_shape=(...]
    pallas_call x1, Pallas kernels: 0.18 us -> 1.21 us  [paired_shards(): pl.pallas_call(keep_kernel, out_shape=(vmem_array((chips, hidden_rows, LA...]
    ppermute x3, waiting for transfers between devices: 1.48 us -> 0.47 us  [swap_cores(): return lax.ppermute(array, 'vocab', [(i, i ^ 1) for i in range(count)])]
    pallas_call x1, Pallas kernels: 1.79 us -> 0.95 us  [paired_shards(): pl.pallas_call(give_kernel, out_shape=(vmem_array((chips, hidden_rows, LA...]
  transfers between devices with their start and end apart: 18 -> 18, of which waited for: 7 -> 7; matrix products, arithmetic and copies ran while one was open for 0% -> 0% of each run, Pallas kernels for 16% -> 18%
where the time goes in v14:
time: 62.1 us; the launch traced here: 61.9 us
  starting transfers between devices  33.5 us (54%)
  Pallas kernels  23 us (37%)
  waiting for transfers between devices  3.68 us (6%)
  between operations  1.43 us (2%)
    ppermute x14, starting transfers between devices, along_chips(): lax.ppermute(array, 'vocab', [(i, (i + 2 * step) % count) for i in range(...  26.3 us
    pallas_call x1, Pallas kernels, paired_shards(): pl.pallas_call(functools.partial(logits_kernel, chips=chips), out_shape=(...  8.78 us
    pallas_call x1, Pallas kernels, paired_shards(): pl.pallas_call(products_kernel, out_shape=(vmem_array((chips, 2, 2, hidde...  7.41 us
    all_to_all x1, starting transfers between devices, paired_shards(): lax.all_to_all(stats, 'vocab', split_axis=0, concat_axis=0, tiled=True)  6.21 us
    ppermute x14, waiting for transfers between devices, along_chips(): lax.ppermute(array, 'vocab', [(i, (i + 2 * step) % count) for i in range(...  3.2 us
    pallas_call x1, Pallas kernels, paired_shards(): pl.pallas_call(functools.partial(preload_kernel, chips=chips), out_shape=...  2.4 us
    pallas_call x1, Pallas kernels, paired_shards(): pl.pallas_call(functools.partial(pack_kernel, shard_rows=shard_rows), out...  1.52 us
  transfers between devices with their start and end apart: 18, of which 7 were waited for; matrix products, arithmetic and copies ran while one was open for 0% of the time, Pallas kernels for 18%

profile of v14, /device:TPU:0, one launch (start us, length us, event | category | flops | bytes accessed | tf_op | source)
XLA Modules:
  0.0 61.9 jit_solution(12082011261897448878)
XLA Ops:
  0.6 1.5 %pack.1 = (bf16[8,240,128]{2,1,0:T(8,128)(2,1)S(1)}, bf16[64,64]{1,0:T(8,128)(2,1)S(1)}, f32[64,128]{1,0:T(8,128)S(1)}) custom-call(s32[1]{0:T(128)} %bitcast.place_ref, bf16[64,320]{1,0:T(8,128)(2,1)} %refs_0_.1, bf16[4,19456]{1,0:T(4,128)(2,1)} %refs_1_.1, f32[4,608]{1,0:T(4,128)} %refs_2_.1, s32[1,64]{1,0:T(1,128)} %bitcast.51, s32[1,64]{1,0:T(1,128)} %bitcast.52, ...), custom_call_target="tpu_custom_call" | custom-call | tf_op jit(solution)/shard_map/pack/pallas_call | solution.py:490
  2.2 3.0 %collective-permute-start.6 = (bf16[240,128]{1,0:T(8,128)(2,1)S(1)}, bf16[240,128]{1,0:T(8,128)(2,1)S(1)}, u32[]{:S(2)}, u32[]{:S(2)}) collective-permute-start(bf16[240,128]{1,0:T(8,128)(2,1)S(1)} %get-tuple-element.36), channel_id=1, source_target_pairs={{0,2},{1,3},{2,4},{3,5},{4,6},{5,7},{6,8},{7,9},{8,10},{9,11},{10,... | collective-permute-start | bytes 184328 | tf_op jit(solution)/shard_map/ppermute | solution.py:52
  5.2 1.6 %collective-permute-start.5 = (bf16[240,128]{1,0:T(8,128)(2,1)S(1)}, bf16[240,128]{1,0:T(8,128)(2,1)S(1)}, u32[]{:S(2)}, u32[]{:S(2)}) collective-permute-start(bf16[240,128]{1,0:T(8,128)(2,1)S(1)} %get-tuple-element.37), channel_id=1, source_target_pairs={{0,4},{1,5},{2,6},{3,7},{4,8},{5,9},{6,10},{7,11},{8,12},{9,13},{1... | collective-permute-start | bytes 184328 | tf_op jit(solution)/shard_map/ppermute | solution.py:52
  6.8 2.5 %collective-permute-start.4 = (bf16[240,128]{1,0:T(8,128)(2,1)S(1)}, bf16[240,128]{1,0:T(8,128)(2,1)S(1)}, u32[]{:S(2)}, u32[]{:S(2)}) collective-permute-start(bf16[240,128]{1,0:T(8,128)(2,1)S(1)} %get-tuple-element.38), channel_id=1, source_target_pairs={{0,6},{1,7},{2,8},{3,9},{4,10},{5,11},{6,12},{7,13},{8,14},{9,15},... | collective-permute-start | bytes 184328 | tf_op jit(solution)/shard_map/ppermute | solution.py:52
  9.3 1.2 %collective-permute-start.3 = (bf16[240,128]{1,0:T(8,128)(2,1)S(1)}, bf16[240,128]{1,0:T(8,128)(2,1)S(1)}, u32[]{:S(2)}, u32[]{:S(2)}) collective-permute-start(bf16[240,128]{1,0:T(8,128)(2,1)S(1)} %get-tuple-element.39), channel_id=1, source_target_pairs={{0,8},{1,9},{2,10},{3,11},{4,12},{5,13},{6,14},{7,15},{8,0},{9,1},... | collective-permute-start | bytes 184328 | tf_op jit(solution)/shard_map/ppermute | solution.py:52
  10.6 2.6 %collective-permute-start.2 = (bf16[240,128]{1,0:T(8,128)(2,1)S(1)}, bf16[240,128]{1,0:T(8,128)(2,1)S(1)}, u32[]{:S(2)}, u32[]{:S(2)}) collective-permute-start(bf16[240,128]{1,0:T(8,128)(2,1)S(1)} %get-tuple-element.40), channel_id=1, source_target_pairs={{0,10},{1,11},{2,12},{3,13},{4,14},{5,15},{6,0},{7,1},{8,2},{9,3},... | collective-permute-start | bytes 184328 | tf_op jit(solution)/shard_map/ppermute | solution.py:52
  13.2 1.3 %collective-permute-start.1 = (bf16[240,128]{1,0:T(8,128)(2,1)S(1)}, bf16[240,128]{1,0:T(8,128)(2,1)S(1)}, u32[]{:S(2)}, u32[]{:S(2)}) collective-permute-start(bf16[240,128]{1,0:T(8,128)(2,1)S(1)} %get-tuple-element.41), channel_id=1, source_target_pairs={{0,12},{1,13},{2,14},{3,15},{4,0},{5,1},{6,2},{7,3},{8,4},{9,5},{1... | collective-permute-start | bytes 184328 | tf_op jit(solution)/shard_map/ppermute | solution.py:52
  14.6 1.5 %collective-permute-start = (bf16[240,128]{1,0:T(8,128)(2,1)S(1)}, bf16[240,128]{1,0:T(8,128)(2,1)S(1)}, u32[]{:S(2)}, u32[]{:S(2)}) collective-permute-start(bf16[240,128]{1,0:T(8,128)(2,1)S(1)} %get-tuple-element.42), channel_id=1, source_target_pairs={{0,14},{1,15},{2,0},{3,1},{4,2},{5,3},{6,4},{7,5},{8,6},{9,7},{10,... | collective-permute-start | bytes 184328 | tf_op jit(solution)/shard_map/ppermute | solution.py:52
  16.8 2.4 %preload.1.refs_12_ = bf16[1216,1920]{1,0:T(8,128)(2,1)S(1)} custom-call(s32[1]{0:T(128)} %bitcast.place_ref, bf16[1216,5120]{1,0:T(8,128)(2,1)} %head_ref.3, bf16[240,128]{1,0:T(8,128)(2,1)S(1)} %collective-permute-done.4._.refs_4_), custom_call_target="tpu_custom_call" | custom-call | bytes 9338880 | tf_op jit(solution)/shard_map/preload/pallas_call | solution.py:510
  20.9 8.8 %logits.1 = (bf16[192,1216]{1,0:T(8,128)(2,1)}, f32[16,8,128]{2,1,0:T(8,128)}, f32[8,128]{1,0:T(8,128)S(1)}) custom-call(s32[1]{0:T(128)} %bitcast.place_ref, bf16[240,128]{1,0:T(8,128)(2,1)S(1)} %collective-permute-done.refs_0_, bf16[240,128]{1,0:T(8,128)(2,1)S(1)} %collective-permute-done.1.refs_1_, bf16[240,128]{1,0:T(8,128)(2,1)S(1)} %collective-permute-done.2.refs_2_, ...), custom_call_target="tpu_custom_call" | custom-call | flops 796917760 | bytes 12451840 | tf_op jit(solution)/shard_map/logits/pallas_call | solution.py:525
  29.7 6.2 %all-to-all-start = ((f32[16,8,128]{2,1,0:T(8,128)}), f32[16,8,128]{2,1,0:T(8,128)S(1)}, u32[]{:S(2)}, u32[]{:S(2)}) async-start(f32[16,8,128]{2,1,0:T(8,128)} %get-tuple-element.22), calls=%async_computation | async-start | bytes 131072 | tf_op jit(solution)/shard_map/all_to_all | solution.py:550
  35.9 7.4 %products.1 = (f32[8,2,2,160,128]{4,3,2,1,0:T(8,128)S(1)}, bf16[8,2,160,128]{3,2,1,0:T(8,128)(2,1)S(1)}) custom-call(s32[1]{0:T(128)} %bitcast.place_ref, bf16[192,1216]{1,0:T(8,128)(2,1)} %get-tuple-element.24.rows_ref, bf16[1216,5120]{1,0:T(8,128)(2,1)} %head_ref.3), custom_call_target="tpu_custom_call" | custom-call | flops 2390753280 | bytes 12451840 | tf_op jit(solution)/shard_map/products/pallas_call | solution.py:552
  43.3 1.0 %give.1 = (bf16[8,160,128]{2,1,0:T(8,128)(2,1)S(1)}, f32[3,160,128]{2,1,0:T(8,128)S(1)}, f32[1,1]{1,0:T(1,128)}) custom-call(s32[1]{0:T(128)} %bitcast.place_ref, f32[1]{0:T(128)S(6)} %copy.14.scale_ref, f32[16,8,128]{2,1,0:T(8,128)S(1)} %all-to-all-done.stats_ref, f32[8,128]{1,0:T(8,128)S(1)} %get-tuple-element.23.own_ref, ...), custom_call_target="tpu_custom_call" | custom-call | tf_op jit(solution)/shard_map/give/pallas_call | solution.py:569
  44.7 1.2 %keep.1 = (f32[8,160,128]{2,1,0:T(8,128)S(1)}, f32[1,1]{1,0:T(1,128)}) custom-call(s32[1]{0:T(128)} %bitcast.place_ref, f32[3,160,128]{2,1,0:T(8,128)S(1)} %get-tuple-element.27.factors_ref, f32[1,1]{1,0:T(1,128)} %get-tuple-element.28.found_ref, f32[8,2,2,160,128]{4,3,2,1,0:T(8,128)S(1)} %get-tuple-element.25.terms_ref, ...), custom_call_target="tpu_custom_call" | custom-call | flops 2621440 | bytes 2621440 | tf_op jit(solution)/shard_map/keep/pallas_call | solution.py:582
  46.1 1.9 %collective-permute-start.10 = (bf16[160,128]{1,0:T(8,128)(2,1)S(1)}, bf16[160,128]{1,0:T(8,128)(2,1)S(1)}, u32[]{:S(2)}, u32[]{:S(2)}) collective-permute-start(bf16[160,128]{1,0:T(8,128)(2,1)S(1)} %get-tuple-element.49), channel_id=1, source_target_pairs={{0,2},{1,3},{2,4},{3,5},{4,6},{5,7},{6,8},{7,9},{8,10},{9,11},{10,... | collective-permute-start | bytes 122888 | tf_op jit(solution)/shard_map/ppermute | solution.py:52
  48.0 1.5 %collective-permute-start.11 = (bf16[160,128]{1,0:T(8,128)(2,1)S(1)}, bf16[160,128]{1,0:T(8,128)(2,1)S(1)}, u32[]{:S(2)}, u32[]{:S(2)}) collective-permute-start(bf16[160,128]{1,0:T(8,128)(2,1)S(1)} %get-tuple-element.48), channel_id=1, source_target_pairs={{0,4},{1,5},{2,6},{3,7},{4,8},{5,9},{6,10},{7,11},{8,12},{9,13},{1... | collective-permute-start | bytes 122888 | tf_op jit(solution)/shard_map/ppermute | solution.py:52
  49.5 2.4 %collective-permute-start.12 = (bf16[160,128]{1,0:T(8,128)(2,1)S(1)}, bf16[160,128]{1,0:T(8,128)(2,1)S(1)}, u32[]{:S(2)}, u32[]{:S(2)}) collective-permute-start(bf16[160,128]{1,0:T(8,128)(2,1)S(1)} %get-tuple-element.47), channel_id=1, source_target_pairs={{0,6},{1,7},{2,8},{3,9},{4,10},{5,11},{6,12},{7,13},{8,14},{9,15},... | collective-permute-start | bytes 122888 | tf_op jit(solution)/shard_map/ppermute | solution.py:52
  51.9 1.5 %collective-permute-start.13 = (bf16[160,128]{1,0:T(8,128)(2,1)S(1)}, bf16[160,128]{1,0:T(8,128)(2,1)S(1)}, u32[]{:S(2)}, u32[]{:S(2)}) collective-permute-start(bf16[160,128]{1,0:T(8,128)(2,1)S(1)} %get-tuple-element.46), channel_id=1, source_target_pairs={{0,8},{1,9},{2,10},{3,11},{4,12},{5,13},{6,14},{7,15},{8,0},{9,1},... | collective-permute-start | bytes 122888 | tf_op jit(solution)/shard_map/ppermute | solution.py:52
  53.3 2.4 %collective-permute-start.14 = (bf16[160,128]{1,0:T(8,128)(2,1)S(1)}, bf16[160,128]{1,0:T(8,128)(2,1)S(1)}, u32[]{:S(2)}, u32[]{:S(2)}) collective-permute-start(bf16[160,128]{1,0:T(8,128)(2,1)S(1)} %get-tuple-element.45), channel_id=1, source_target_pairs={{0,10},{1,11},{2,12},{3,13},{4,14},{5,15},{6,0},{7,1},{8,2},{9,3},... | collective-permute-start | bytes 122888 | tf_op jit(solution)/shard_map/ppermute | solution.py:52
  55.7 1.5 %collective-permute-start.15 = (bf16[160,128]{1,0:T(8,128)(2,1)S(1)}, bf16[160,128]{1,0:T(8,128)(2,1)S(1)}, u32[]{:S(2)}, u32[]{:S(2)}) collective-permute-start(bf16[160,128]{1,0:T(8,128)(2,1)S(1)} %get-tuple-element.44), channel_id=1, source_target_pairs={{0,12},{1,13},{2,14},{3,15},{4,0},{5,1},{6,2},{7,3},{8,4},{9,5},{1... | collective-permute-start | bytes 122888 | tf_op jit(solution)/shard_map/ppermute | solution.py:52
  57.1 1.4 %collective-permute-start.16 = (bf16[160,128]{1,0:T(8,128)(2,1)S(1)}, bf16[160,128]{1,0:T(8,128)(2,1)S(1)}, u32[]{:S(2)}, u32[]{:S(2)}) collective-permute-start(bf16[160,128]{1,0:T(8,128)(2,1)S(1)} %get-tuple-element.43), channel_id=1, source_target_pairs={{0,14},{1,15},{2,0},{3,1},{4,2},{5,3},{6,4},{7,5},{8,6},{9,7},{10,... | collective-permute-start | bytes 122888 | tf_op jit(solution)/shard_map/ppermute | solution.py:52
  58.7 1.0 %collective-permute-done.15.refs_5_ = bf16[160,128]{1,0:T(8,128)(2,1)S(1)} collective-permute-done((bf16[160,128]{1,0:T(8,128)(2,1)S(1)}, bf16[160,128]{1,0:T(8,128)(2,1)S(1)}, u32[]{:S(2)}, u32[]{:S(2)}) %collective-permute-start.15) | collective-permute-done | bytes 40992 | tf_op jit(solution)/shard_map/ppermute | solution.py:52
  59.7 1.4 %collective-permute-done.16.refs_6_ = bf16[160,128]{1,0:T(8,128)(2,1)S(1)} collective-permute-done((bf16[160,128]{1,0:T(8,128)(2,1)S(1)}, bf16[160,128]{1,0:T(8,128)(2,1)S(1)}, u32[]{:S(2)}, u32[]{:S(2)}) %collective-permute-start.16) | collective-permute-done | bytes 40992 | tf_op jit(solution)/shard_map/ppermute | solution.py:52
  61.1 0.7 %total.1 = bf16[64,320]{1,0:T(8,128)(2,1)} custom-call(f32[160,128]{1,0:T(8,128)S(1)} %slice_bitcast_fusion.own_ref, bf16[160,128]{1,0:T(8,128)(2,1)S(1)} %collective-permute-done.10.refs_0_, bf16[160,128]{1,0:T(8,128)(2,1)S(1)} %collective-permute-done.11.refs_1_, bf16[160,128]{1,0:T(8,128)(2,1)S(1)} %collective-permute-done.12.refs_2_, ...), custom_call_target="tpu_custom_call" | custom-call | tf_op jit(solution)/shard_map/total/pallas_call | solution.py:598
  (28 shorter events, 2.5 us)
Async XLA Ops:
  2.2 11.0 %collective-permute-start.6 = (bf16[240,128]{1,0:T(8,128)(2,1)S(1)}, bf16[240,128]{1,0:T(8,128)(2,1)S(1)}, u32[]{:S(2)}, u32[]{:S(2)}) collective-permute-start(bf16[240,128]{1,0:T(8,128)(2,1)S(1)} %get-tuple-element.36), channel_id=1, source_target_pairs={{0,2},{1,3},{2,4},{3,5},{4,6},{5,7},{6,8},{7,9},{8,10},{9,11},{10,... | collective-permute-start | bytes 184328 | tf_op jit(solution)/shard_map/ppermute | solution.py:52
  5.2 9.4 %collective-permute-start.5 = (bf16[240,128]{1,0:T(8,128)(2,1)S(1)}, bf16[240,128]{1,0:T(8,128)(2,1)S(1)}, u32[]{:S(2)}, u32[]{:S(2)}) collective-permute-start(bf16[240,128]{1,0:T(8,128)(2,1)S(1)} %get-tuple-element.37), channel_id=1, source_target_pairs={{0,4},{1,5},{2,6},{3,7},{4,8},{5,9},{6,10},{7,11},{8,12},{9,13},{1... | collective-permute-start | bytes 184328 | tf_op jit(solution)/shard_map/ppermute | solution.py:52
  6.8 9.4 %collective-permute-start.4 = (bf16[240,128]{1,0:T(8,128)(2,1)S(1)}, bf16[240,128]{1,0:T(8,128)(2,1)S(1)}, u32[]{:S(2)}, u32[]{:S(2)}) collective-permute-start(bf16[240,128]{1,0:T(8,128)(2,1)S(1)} %get-tuple-element.38), channel_id=1, source_target_pairs={{0,6},{1,7},{2,8},{3,9},{4,10},{5,11},{6,12},{7,13},{8,14},{9,15},... | collective-permute-start | bytes 184328 | tf_op jit(solution)/shard_map/ppermute | solution.py:52
  9.3 7.4 %collective-permute-start.3 = (bf16[240,128]{1,0:T(8,128)(2,1)S(1)}, bf16[240,128]{1,0:T(8,128)(2,1)S(1)}, u32[]{:S(2)}, u32[]{:S(2)}) collective-permute-start(bf16[240,128]{1,0:T(8,128)(2,1)S(1)} %get-tuple-element.39), channel_id=1, source_target_pairs={{0,8},{1,9},{2,10},{3,11},{4,12},{5,13},{6,14},{7,15},{8,0},{9,1},... | collective-permute-start | bytes 184328 | tf_op jit(solution)/shard_map/ppermute | solution.py:52
  10.6 8.7 %collective-permute-start.2 = (bf16[240,128]{1,0:T(8,128)(2,1)S(1)}, bf16[240,128]{1,0:T(8,128)(2,1)S(1)}, u32[]{:S(2)}, u32[]{:S(2)}) collective-permute-start(bf16[240,128]{1,0:T(8,128)(2,1)S(1)} %get-tuple-element.40), channel_id=1, source_target_pairs={{0,10},{1,11},{2,12},{3,13},{4,14},{5,15},{6,0},{7,1},{8,2},{9,3},... | collective-permute-start | bytes 184328 | tf_op jit(solution)/shard_map/ppermute | solution.py:52
  13.2 6.0 %collective-permute-start.1 = (bf16[240,128]{1,0:T(8,128)(2,1)S(1)}, bf16[240,128]{1,0:T(8,128)(2,1)S(1)}, u32[]{:S(2)}, u32[]{:S(2)}) collective-permute-start(bf16[240,128]{1,0:T(8,128)(2,1)S(1)} %get-tuple-element.41), channel_id=1, source_target_pairs={{0,12},{1,13},{2,14},{3,15},{4,0},{5,1},{6,2},{7,3},{8,4},{9,5},{1... | collective-permute-start | bytes 184328 | tf_op jit(solution)/shard_map/ppermute | solution.py:52
  14.6 4.7 %collective-permute-start = (bf16[240,128]{1,0:T(8,128)(2,1)S(1)}, bf16[240,128]{1,0:T(8,128)(2,1)S(1)}, u32[]{:S(2)}, u32[]{:S(2)}) collective-permute-start(bf16[240,128]{1,0:T(8,128)(2,1)S(1)} %get-tuple-element.42), channel_id=1, source_target_pairs={{0,14},{1,15},{2,0},{3,1},{4,2},{5,3},{6,4},{7,5},{8,6},{9,7},{10,... | collective-permute-start | bytes 184328 | tf_op jit(solution)/shard_map/ppermute | solution.py:52
  16.8 4.2 %collective-permute-start.8 = (bf16[5,240,128]{2,1,0:T(8,128)(2,1)S(1)}, bf16[5,240,128]{2,1,0:T(8,128)(2,1)S(1)}, u32[]{:S(2)}, u32[]{:S(2)}) collective-permute-start(bf16[5,240,128]{2,1,0:T(8,128)(2,1)S(1)} %bitcast_dynamic-update-slice_fusion), channel_id=1, source_target_pairs={{0,1},{1,0},{2,3},{3,2},{4,5},{5,4},{6,7},{7,6},{8,9},{9,8},{10,11... | collective-permute-start | bytes 921608 | tf_op jit(solution)/shard_map/ppermute | solution.py:47
  19.3 1.6 %collective-permute-start.7 = (bf16[3,240,128]{2,1,0:T(8,128)(2,1)S(1)}, bf16[3,240,128]{2,1,0:T(8,128)(2,1)S(1)}, u32[]{:S(2)}, u32[]{:S(2)}) collective-permute-start(bf16[3,240,128]{2,1,0:T(8,128)(2,1)S(1)} %pad_maximum_fusion), channel_id=1, source_target_pairs={{0,1},{1,0},{2,3},{3,2},{4,5},{5,4},{6,7},{7,6},{8,9},{9,8},{10,11... | collective-permute-start | bytes 552968 | tf_op jit(solution)/shard_map/ppermute | solution.py:47
  29.7 13.6 %all-to-all-start = ((f32[16,8,128]{2,1,0:T(8,128)}), f32[16,8,128]{2,1,0:T(8,128)S(1)}, u32[]{:S(2)}, u32[]{:S(2)}) async-start(f32[16,8,128]{2,1,0:T(8,128)} %get-tuple-element.22), calls=%async_computation | async-start | bytes 131072 | tf_op jit(solution)/shard_map/all_to_all | solution.py:550
  44.3 1.6 %collective-permute-start.9 = (bf16[8,160,128]{2,1,0:T(8,128)(2,1)S(1)}, bf16[8,160,128]{2,1,0:T(8,128)(2,1)S(1)}, u32[]{:S(2)}, u32[]{:S(2)}) collective-permute-start(bf16[8,160,128]{2,1,0:T(8,128)(2,1)S(1)} %get-tuple-element.30), channel_id=1, source_target_pairs={{0,1},{1,0},{2,3},{3,2},{4,5},{5,4},{6,7},{7,6},{8,9},{9,8},{10,11... | collective-permute-start | bytes 983048 | tf_op jit(solution)/shard_map/ppermute | solution.py:47
  46.1 9.6 %collective-permute-start.10 = (bf16[160,128]{1,0:T(8,128)(2,1)S(1)}, bf16[160,128]{1,0:T(8,128)(2,1)S(1)}, u32[]{:S(2)}, u32[]{:S(2)}) collective-permute-start(bf16[160,128]{1,0:T(8,128)(2,1)S(1)} %get-tuple-element.49), channel_id=1, source_target_pairs={{0,2},{1,3},{2,4},{3,5},{4,6},{5,7},{6,8},{7,9},{8,10},{9,11},{10,... | collective-permute-start | bytes 122888 | tf_op jit(solution)/shard_map/ppermute | solution.py:52
  48.0 9.1 %collective-permute-start.11 = (bf16[160,128]{1,0:T(8,128)(2,1)S(1)}, bf16[160,128]{1,0:T(8,128)(2,1)S(1)}, u32[]{:S(2)}, u32[]{:S(2)}) collective-permute-start(bf16[160,128]{1,0:T(8,128)(2,1)S(1)} %get-tuple-element.48), channel_id=1, source_target_pairs={{0,4},{1,5},{2,6},{3,7},{4,8},{5,9},{6,10},{7,11},{8,12},{9,13},{1... | collective-permute-start | bytes 122888 | tf_op jit(solution)/shard_map/ppermute | solution.py:52
  49.5 9.1 %collective-permute-start.12 = (bf16[160,128]{1,0:T(8,128)(2,1)S(1)}, bf16[160,128]{1,0:T(8,128)(2,1)S(1)}, u32[]{:S(2)}, u32[]{:S(2)}) collective-permute-start(bf16[160,128]{1,0:T(8,128)(2,1)S(1)} %get-tuple-element.47), channel_id=1, source_target_pairs={{0,6},{1,7},{2,8},{3,9},{4,10},{5,11},{6,12},{7,13},{8,14},{9,15},... | collective-permute-start | bytes 122888 | tf_op jit(solution)/shard_map/ppermute | solution.py:52
  51.9 6.8 %collective-permute-start.13 = (bf16[160,128]{1,0:T(8,128)(2,1)S(1)}, bf16[160,128]{1,0:T(8,128)(2,1)S(1)}, u32[]{:S(2)}, u32[]{:S(2)}) collective-permute-start(bf16[160,128]{1,0:T(8,128)(2,1)S(1)} %get-tuple-element.46), channel_id=1, source_target_pairs={{0,8},{1,9},{2,10},{3,11},{4,12},{5,13},{6,14},{7,15},{8,0},{9,1},... | collective-permute-start | bytes 122888 | tf_op jit(solution)/shard_map/ppermute | solution.py:52
  53.3 5.4 %collective-permute-start.14 = (bf16[160,128]{1,0:T(8,128)(2,1)S(1)}, bf16[160,128]{1,0:T(8,128)(2,1)S(1)}, u32[]{:S(2)}, u32[]{:S(2)}) collective-permute-start(bf16[160,128]{1,0:T(8,128)(2,1)S(1)} %get-tuple-element.45), channel_id=1, source_target_pairs={{0,10},{1,11},{2,12},{3,13},{4,14},{5,15},{6,0},{7,1},{8,2},{9,3},... | collective-permute-start | bytes 122888 | tf_op jit(solution)/shard_map/ppermute | solution.py:52
  55.7 4.0 %collective-permute-start.15 = (bf16[160,128]{1,0:T(8,128)(2,1)S(1)}, bf16[160,128]{1,0:T(8,128)(2,1)S(1)}, u32[]{:S(2)}, u32[]{:S(2)}) collective-permute-start(bf16[160,128]{1,0:T(8,128)(2,1)S(1)} %get-tuple-element.44), channel_id=1, source_target_pairs={{0,12},{1,13},{2,14},{3,15},{4,0},{5,1},{6,2},{7,3},{8,4},{9,5},{1... | collective-permute-start | bytes 122888 | tf_op jit(solution)/shard_map/ppermute | solution.py:52
  57.1 4.0 %collective-permute-start.16 = (bf16[160,128]{1,0:T(8,128)(2,1)S(1)}, bf16[160,128]{1,0:T(8,128)(2,1)S(1)}, u32[]{:S(2)}, u32[]{:S(2)}) collective-permute-start(bf16[160,128]{1,0:T(8,128)(2,1)S(1)} %get-tuple-element.43), channel_id=1, source_target_pairs={{0,14},{1,15},{2,0},{3,1},{4,2},{5,3},{6,4},{7,5},{8,6},{9,7},{10,... | collective-permute-start | bytes 122888 | tf_op jit(solution)/shard_map/ppermute | solution.py:52

commit v15 on v14

--- a/solution.py
+++ b/solution.py
@@ -80,38 +80,8 @@
     return pltpu.roll(array, LANES // 2, 1)
 
 
-def packed_half(tiles):
-    rows = tiles[2].shape[0] // 2
-    upper, lower = tiles[2][:rows], tiles[2][rows:]
-    rest = jnp.where(low_lanes(upper.shape), upper, turned(lower))
-    return jnp.concatenate([tiles[0], tiles[1], rest], axis=0)
-
-
-def unpacked_half(packed, tokens):
-    rest = packed[2 * tokens :]
-    return [packed[:tokens], packed[tokens : 2 * tokens], jnp.concatenate([rest, turned(rest)])]
-
-
-def joined(first, second):
-    low = low_lanes(first[0].shape)
-    turns = [turned(tile) for tile in second]
-    return [
-        first[0],
-        first[1],
-        jnp.where(low, first[2], turns[0]),
-        jnp.where(low, turns[0], turns[1]),
-        jnp.where(low, turns[1], turns[2]),
-    ]
-
-
-def parted(tiles):
-    low = low_lanes(tiles[0].shape)
-    turns = [turned(tile) for tile in tiles[2:]]
-    return tiles[:3], [
-        jnp.where(low, turns[0], turns[1]),
-        jnp.where(low, turns[1], turns[2]),
-        turns[2],
-    ]
+def tiles_of(array, count):
+    return [array[:, LANES * i : LANES * (i + 1)] for i in range(count)]
 
 
 def column_of(row):
@@ -121,13 +91,21 @@
     return jnp.sum(jnp.where(down == along, row, jnp.zeros_like(row)), axis=1, keepdims=True)
 
 
-def token_facts(ids, row_map, lengths, first_entry):
+def token_facts(ids, row_map, lengths, first_entry, slots):
     tokens = row_map.shape[1]
     token = lax.broadcasted_iota(jnp.int32, (tokens, tokens), 0)
     slot = lax.broadcasted_iota(jnp.int32, (tokens, tokens), 1)
     owner = (row_map == token).astype(jnp.float32)
     named = jnp.max(owner, axis=1, keepdims=True)
     owner = jnp.where((slot == 0) & (named == 0.0), 1.0, owner)
+    rows = 2 * tokens
+    slot = lax.broadcasted_iota(jnp.int32, (tokens, rows), 0)
+    row = lax.broadcasted_iota(jnp.int32, (tokens, rows), 1)
+    source, within = row // (2 * slots), row % (2 * slots)
+    chosen = (slot == source * slots + within % slots).astype(jnp.bfloat16)
+    owner = jnp.dot(owner.astype(jnp.bfloat16), chosen, preferred_element_type=jnp.float32)
+    odd = within >= slots
+    owner = jnp.concatenate([jnp.where(odd, 0.0, owner), jnp.where(odd, owner, 0.0)], axis=0)
 
     seqs = lengths.shape[1]
     seq_length = tokens // seqs
@@ -158,7 +136,7 @@
         copy.wait()
     hidden_ref, values_ref, scales_ref, ids_ref, map_ref, lengths_ref = inside
     owner_ref[...], table_ref[...] = token_facts(
-        ids_ref[...], map_ref[...], lengths_ref[...], place_ref[0] * shard_rows
+        ids_ref[...], map_ref[...], lengths_ref[...], place_ref[0] * shard_rows, values_ref.shape[0]
     )
     chips = packed_ref.shape[0]
     tokens, half = hidden_ref.shape
@@ -188,9 +166,19 @@
     wide_ref[:, entries:] = jnp.zeros((2 * slots, LANES), jnp.float32)
 
     hidden = hidden_ref[...].astype(jnp.float32)
-    hidden = jnp.concatenate([hidden, jnp.zeros((tokens, LANES // 2), jnp.float32)], axis=1)
-    hidden = packed_half([hidden[:, LANES * i : LANES * (i + 1)] for i in range(3)])
-    hidden = hidden.astype(jnp.bfloat16)
+    zeros = jnp.zeros((tokens, LANES // 2), jnp.float32)
+    tiles = tiles_of(jnp.concatenate([hidden, zeros], axis=1), 3)
+    turns = [turned(tile) for tile in tiles]
+    low = low_lanes(tiles[0].shape)
+    first = place_ref[0] % 2 == 0
+    hidden = jnp.concatenate(
+        [
+            jnp.where(first, tiles[0], jnp.where(low, turns[0], turns[1])),
+            jnp.where(first, tiles[1], jnp.where(low, turns[1], turns[2])),
+            jnp.where(first, tiles[2], jnp.where(low, 0.0, turns[0])),
+        ],
+        axis=0,
+    ).astype(jnp.bfloat16)
     hidden_rows = hidden.shape[0]
     upper = low_rows((2 * slots, LANES), slots)
     low = low_lanes((2 * slots, LANES))
@@ -231,20 +219,10 @@
     return copies
 
 
-def take(copies, steps):
-    for step in steps:
-        copies[step].wait()
-        if step + AHEAD < len(copies):
-            copies[step + AHEAD].start()
-
-
-def grouped(count, sizes):
-    groups, start = [], 0
-    while start < count:
-        size = min(sizes[min(len(groups), len(sizes) - 1)], count - start)
-        groups.append(range(start, start + size))
-        start += size
-    return groups
+def take(copies, step):
+    copies[step].wait()
+    if step + AHEAD < len(copies):
+        copies[step + AHEAD].start()
 
 
 def source_chips(place_ref, chips):
@@ -271,35 +249,31 @@
         copy.start()
     tokens, width = hidden_ref.shape[0], hidden_ref.shape[1] // chips
     shard_rows = head_ref.shape[0]
-    hidden_rows = tokens * width // 2 // LANES
+    hidden_rows = 3 * tokens
     slots = tokens // (2 * chips)
-    upper = low_rows((2 * slots, LANES), slots)
-
-    def both(step, rows):
-        own = near[step][rows].astype(jnp.float32)
+
+    for step in range(chips):
         late = step > chips // 2
         group = far[0] if late else far[1]
-        other = group[step - chips // 2 - 1 if late else step, rows].astype(jnp.float32)
-        return jnp.where(core == 0, own, other), jnp.where(core == 0, other, own)
-
-    def unpack_hidden(step):
-        first, second = both(step, slice(0, hidden_rows))
-        tiles = joined(unpacked_half(first, tokens), unpacked_half(second, tokens))
-        tiles = jnp.concatenate(tiles, axis=1).astype(jnp.bfloat16)
-        hidden_ref[:, width * step : width * (step + 1)] = tiles
-
-    def unpack_teacher(step):
-        first, second = both(step, slice(hidden_rows, near[0].shape[0]))
-        share = first.shape[0] // 2
-        first = jnp.where(core == 0, first[:share], first[share:])
-        second = jnp.where(core == 0, second[:share], second[share:])
-        tiles = []
-        for row in range(0, share, 2 * slots):
-            one, two = first[row : row + 2 * slots], second[row : row + 2 * slots]
-            tiles.append(jnp.where(upper, one, pltpu.roll(two, slots, 0)))
-            tiles.append(jnp.where(upper, pltpu.roll(one, slots, 0), two))
-        rows = pl.ds(pl.multiple_of(2 * slots * sources[step], 2 * slots), 2 * slots)
-        arrived_ref[rows] = jnp.concatenate(tiles, axis=1)
+        place = step - chips // 2 - 1 if late else step
+        blocks = near[step], group.at[place]
+        base = width * step
+        for block, parity in zip(blocks, (core, 1 - core)):
+            for i in range(2):
+                column = base + LANES * i + (width - 2 * LANES) * parity
+                lanes = pl.ds(pl.multiple_of(column, LANES), LANES)
+                hidden_ref[:, lanes] = block[tokens * i : tokens * (i + 1)]
+            teacher = block[hidden_rows:].astype(jnp.float32)
+            share = teacher.shape[0] // 2
+            teacher = jnp.where(core == 0, teacher[:share], teacher[share:])
+            row = 2 * slots * (2 * sources[step] + parity)
+            rows = pl.ds(pl.multiple_of(row, 2 * slots), 2 * slots)
+            for i in range(share // (2 * slots)):
+                arrived_ref[rows, LANES * i : LANES * (i + 1)] = teacher[
+                    2 * slots * i : 2 * slots * (i + 1)
+                ]
+        both = [block[2 * tokens : hidden_rows] for block in blocks]
+        hidden_ref[:, base + 2 * LANES : base + 3 * LANES] = both[0] + both[1]
 
     def product(step, count, columns):
         return lax.dot_general(
@@ -309,23 +283,22 @@
             preferred_element_type=jnp.float32,
         )
 
-    for step in range(chips):
-        unpack_hidden(step)
-        unpack_teacher(step)
     logits = product(0, EARLY, early_ref[...])
-    teacher = jnp.dot(
-        owner_ref[...],
-        arrived_ref[:, :shard_rows].astype(jnp.bfloat16),
-        preferred_element_type=jnp.float32,
-    )
+    placed = jnp.dot(
+        owner_ref[...], arrived_ref[...].astype(jnp.bfloat16), preferred_element_type=jnp.float32
+    )
+    pairs = arrived_ref.shape[1] // LANES
+    even, odd = tiles_of(placed[:tokens], pairs), tiles_of(placed[tokens:], pairs)
+    teacher = jnp.concatenate([tile for pair in zip(even, odd) for tile in pair], axis=1)
+    teacher = teacher[:, :shard_rows]
     teacher_top = jnp.max(teacher, axis=1, keepdims=True)
     teacher_off = teacher - teacher_top
     teacher_total = jnp.sum(jnp.exp(teacher_off), axis=1, keepdims=True)
     teacher_ref[...] = teacher_off
-    for group in grouped(len(copies), (3, 2)):
-        take(copies, group)
-        columns = held_ref[:, width * group.start : width * group.stop]
-        logits += product(EARLY + group.start, len(group), columns)
+    for step in range(len(copies)):
+        take(copies, step)
+        columns = held_ref[:, width * step : width * (step + 1)]
+        logits += product(EARLY + step, 1, columns)
 
     top = jnp.max(logits, axis=1, keepdims=True)
     off = logits - top
@@ -369,29 +342,28 @@
     into.wait()
     tokens = made_ref.shape[0] // 3
     width = held_ref.shape[1] // chips
-    for group in grouped(chips, (2, 2, 2, 1)):
-        take(copies, group)
+    for step in range(chips):
+        take(copies, step)
         products = jnp.dot(
             made_ref[...],
-            held_ref[:, width * group.start : width * group.stop],
+            held_ref[:, width * step : width * (step + 1)],
             preferred_element_type=jnp.float32,
         )
-        for place, step in enumerate(group):
-            for part in range(3):
-                rows = products[tokens * part : tokens * (part + 1)]
-                columns = range(width * place, width * (place + 1), LANES)
-                halves = parted([rows[:, i : i + LANES] for i in columns])
-                for parity, tiles in enumerate(halves):
-                    packed = packed_half(tiles)
-                    if part < 2:
-                        terms_ref[step, parity, part] = packed
-                    else:
-                        picks_ref[step, parity] = packed.astype(jnp.bfloat16)
-
-
-def gradient_share(step, parity, factors_ref, terms_ref, picks_ref):
-    sums = terms_ref[step, parity, 0] + factors_ref[1] * terms_ref[step, parity, 1]
-    return factors_ref[0] * sums - factors_ref[2] * picks_ref[step, parity].astype(jnp.float32)
+        for i, tile in enumerate(tiles_of(products, width // LANES)):
+            terms_ref[step, i, 0] = tile[:tokens]
+            terms_ref[step, i, 1] = tile[tokens : 2 * tokens]
+            picks_ref[step, i] = tile[2 * tokens :].astype(jnp.bfloat16)
+
+
+def put_shares(parity, factors_ref, terms_ref, picks_ref, out_ref):
+    tokens = terms_ref.shape[3]
+    factor, level, weight = [factors_ref[i] for i in range(3)]
+    for step in range(terms_ref.shape[0]):
+        for i in range(3):
+            tile = 2 * parity + i
+            sums = terms_ref[step, tile, 0] + level * terms_ref[step, tile, 1]
+            share = factor * sums - weight * picks_ref[step, tile].astype(jnp.float32)
+            out_ref[step, tokens * i : tokens * (i + 1)] = share.astype(out_ref.dtype)
 
 
 def give_kernel(
@@ -433,27 +405,31 @@
     for i, column in enumerate(
         (weight * columns[:, 0:1], columns[:, 1:2], sample_weight * weight)
     ):
-        factors_ref[i] = packed_half([jnp.broadcast_to(column, (tokens, LANES))] * 3)
-    parity = 1 - place_ref[0] % 2
-    for step in range(terms_ref.shape[0]):
-        share = gradient_share(step, parity, factors_ref, terms_ref, picks_ref)
-        give_ref[step] = share.astype(jnp.bfloat16)
+        factors_ref[i] = jnp.broadcast_to(column, (tokens, LANES))
+    put_shares(1 - place_ref[0] % 2, factors_ref, terms_ref, picks_ref, give_ref)
 
 
 def keep_kernel(place_ref, factors_ref, found_ref, terms_ref, picks_ref, keep_ref, loss_ref):
     loss_ref[...] = found_ref[...]
-    parity = place_ref[0] % 2
-    for step in range(terms_ref.shape[0]):
-        keep_ref[step] = gradient_share(step, parity, factors_ref, terms_ref, picks_ref)
-
-
-def sum_kernel(own_ref, *refs):
+    put_shares(place_ref[0] % 2, factors_ref, terms_ref, picks_ref, keep_ref)
+
+
+def sum_kernel(place_ref, own_ref, *refs):
     tokens, half = refs[-1].shape
     total = own_ref[...]
     for share_ref in refs[:-1]:
         total += share_ref[...].astype(jnp.float32)
-    tiles = jnp.concatenate(unpacked_half(total, tokens), axis=1)
-    refs[-1][...] = tiles[:, :half].astype(refs[-1].dtype)
+    tiles = [total[tokens * i : tokens * (i + 1)] for i in range(3)]
+    turns = [turned(tile) for tile in tiles]
+    low = low_lanes(tiles[0].shape)
+    first = place_ref[0] % 2 == 0
+    tiles = [
+        jnp.where(first, tiles[0], jnp.where(low, turns[0], turns[1])),
+        jnp.where(first, tiles[1], jnp.where(low, turns[1], turns[2])),
+        jnp.where(first, tiles[2], turns[2]),
+    ]
+    total = jnp.concatenate(tiles, axis=1)[:, :half]
+    refs[-1][...] = total.astype(refs[-1].dtype)
 
 
 def paired_shards(
@@ -476,7 +452,7 @@
     rows_scratch = pltpu.VMEM((3 * tokens, shard_rows), jnp.bfloat16)
     rows_sem = pltpu.SemaphoreType.DMA
     slots, entries = teacher_values.shape
-    hidden_rows = tokens * half // LANES
+    hidden_rows = 3 * tokens
     teacher_rows = 2 * slots * (shard_rows + LANES // 2) // LANES
 
     operands = (
@@ -491,7 +467,7 @@
         functools.partial(pack_kernel, shard_rows=shard_rows),
         out_shape=(
             jax.ShapeDtypeStruct((chips, hidden_rows + teacher_rows, LANES), jnp.bfloat16),
-            vmem_array((tokens, tokens), jnp.bfloat16),
+            vmem_array((2 * tokens, 2 * tokens), jnp.bfloat16),
             vmem_array((tokens, LANES), jnp.float32),
         ),
         in_specs=[smem] + [hbm] * len(operands),
@@ -535,7 +511,7 @@
             pltpu.VMEM((shard_rows, (chips - EARLY) * width), head.dtype),
             rows_scratch,
             pltpu.VMEM((tokens, chips * width), jnp.bfloat16),
-            pltpu.VMEM((tokens, shard_rows + LANES // 2), jnp.float32),
+            pltpu.VMEM((2 * tokens, (shard_rows + LANES // 2) // 2), jnp.float32),
             pltpu.VMEM((tokens, shard_rows), jnp.float32),
             pltpu.SemaphoreType.DMA((chips - EARLY,)),
             rows_sem,
@@ -552,8 +528,8 @@
     terms, picks = pl.pallas_call(
         products_kernel,
         out_shape=(
-            vmem_array((chips, 2, 2, hidden_rows, LANES), jnp.float32),
-            vmem_array((chips, 2, hidden_rows, LANES), jnp.bfloat16),
+            vmem_array((chips, width // LANES, 2, tokens, LANES), jnp.float32),
+            vmem_array((chips, width // LANES, tokens, LANES), jnp.bfloat16),
         ),
         in_specs=[smem, hbm, hbm],
         out_specs=[vmem] * 2,
@@ -570,7 +546,7 @@
         give_kernel,
         out_shape=(
             vmem_array((chips, hidden_rows, LANES), jnp.bfloat16),
-            vmem_array((3, hidden_rows, LANES), jnp.float32),
+            vmem_array((3, tokens, LANES), jnp.float32),
             vmem_array((1, 1), jnp.float32),
         ),
         in_specs=[smem] * 2 + [vmem] * 5,
@@ -598,11 +574,11 @@
     total = pl.pallas_call(
         sum_kernel,
         out_shape=jax.ShapeDtypeStruct((tokens, half), jnp.bfloat16),
-        in_specs=[vmem] * chips,
+        in_specs=[smem] + [vmem] * chips,
         out_specs=vmem,
         compiler_params=params,
         name="total",
-    )(sums[0], *shares)
+    )(place, sums[0], *shares)
     return total, jnp.reshape(loss, (1,))
 
 

time: 62.1 us -> 61.9 us (level)
  waiting for transfers between devices: 3.68 us -> 5.65 us
  Pallas kernels: 23 us -> 21.1 us
    pallas_call x1, Pallas kernels: 7.41 us -> 6.31 us  [paired_shards(): pl.pallas_call(products_kernel, out_shape=(vmem_array((chips, width // LA...]
    ppermute x14, waiting for transfers between devices: 3.2 us -> 4.08 us  [along_chips(): lax.ppermute(array, 'vocab', [(i, (i + 2 * step) % count) for i in range(...]
    pallas_call x1, Pallas kernels: 8.78 us -> 8.04 us  [paired_shards(): pl.pallas_call(functools.partial(logits_kernel, chips=chips), out_shape=(...]
  transfers between devices with their start and end apart: 18 -> 18, of which waited for: 7 -> 8; matrix products, arithmetic and copies ran while one was open for 0% -> 0% of each run, Pallas kernels for 18% -> 16%
where the time goes in v15:
time: 61.9 us; the launch traced here: 61.6 us
  starting transfers between devices  33.1 us (53%)
  Pallas kernels  21.1 us (34%)
  waiting for transfers between devices  5.65 us (9%)
  between operations  1.43 us (2%)
    ppermute x14, starting transfers between devices, along_chips(): lax.ppermute(array, 'vocab', [(i, (i + 2 * step) % count) for i in range(...  25.8 us
    pallas_call x1, Pallas kernels, paired_shards(): pl.pallas_call(functools.partial(logits_kernel, chips=chips), out_shape=(...  8.04 us
    all_to_all x1, starting transfers between devices, paired_shards(): lax.all_to_all(stats, 'vocab', split_axis=0, concat_axis=0, tiled=True)  6.73 us
    pallas_call x1, Pallas kernels, paired_shards(): pl.pallas_call(products_kernel, out_shape=(vmem_array((chips, width // LA...  6.31 us
    ppermute x14, waiting for transfers between devices, along_chips(): lax.ppermute(array, 'vocab', [(i, (i + 2 * step) % count) for i in range(...  4.08 us
    pallas_call x1, Pallas kernels, paired_shards(): pl.pallas_call(functools.partial(preload_kernel, chips=chips), out_shape=...  2.4 us
    pallas_call x1, Pallas kernels, paired_shards(): pl.pallas_call(functools.partial(pack_kernel, shard_rows=shard_rows), out...  1.52 us
  transfers between devices with their start and end apart: 18, of which 8 were waited for; matrix products, arithmetic and copies ran while one was open for 0% of the time, Pallas kernels for 16%

profile of v15, /device:TPU:0, one launch (start us, length us, event | category | flops | bytes accessed | tf_op | source)
XLA Modules:
  0.0 61.6 jit_solution(6569396313234019239)
XLA Ops:
  0.6 1.5 %pack.1 = (bf16[8,272,128]{2,1,0:T(8,128)(2,1)S(1)}, bf16[128,128]{1,0:T(8,128)(2,1)S(1)}, f32[64,128]{1,0:T(8,128)S(1)}) custom-call(s32[1]{0:T(128)} %bitcast.place_ref, bf16[64,320]{1,0:T(8,128)(2,1)} %refs_0_.1, bf16[4,19456]{1,0:T(4,128)(2,1)} %refs_1_.1, f32[4,608]{1,0:T(4,128)} %refs_2_.1, s32[1,64]{1,0:T(1,128)} %bitcast.51, s32[1,64]{1,0:T(1,128)} %bitcast.52, ...), custom_call_target="tpu_custom_call" | custom-call | tf_op jit(solution)/shard_map/pack/pallas_call | solution.py:466
  2.2 3.0 %collective-permute-start.6 = (bf16[272,128]{1,0:T(8,128)(2,1)S(1)}, bf16[272,128]{1,0:T(8,128)(2,1)S(1)}, u32[]{:S(2)}, u32[]{:S(2)}) collective-permute-start(bf16[272,128]{1,0:T(8,128)(2,1)S(1)} %get-tuple-element.36), channel_id=1, source_target_pairs={{0,2},{1,3},{2,4},{3,5},{4,6},{5,7},{6,8},{7,9},{8,10},{9,11},{10,... | collective-permute-start | bytes 208904 | tf_op jit(solution)/shard_map/ppermute | solution.py:52
  5.2 1.6 %collective-permute-start.5 = (bf16[272,128]{1,0:T(8,128)(2,1)S(1)}, bf16[272,128]{1,0:T(8,128)(2,1)S(1)}, u32[]{:S(2)}, u32[]{:S(2)}) collective-permute-start(bf16[272,128]{1,0:T(8,128)(2,1)S(1)} %get-tuple-element.37), channel_id=1, source_target_pairs={{0,4},{1,5},{2,6},{3,7},{4,8},{5,9},{6,10},{7,11},{8,12},{9,13},{1... | collective-permute-start | bytes 208904 | tf_op jit(solution)/shard_map/ppermute | solution.py:52
  6.8 2.5 %collective-permute-start.4 = (bf16[272,128]{1,0:T(8,128)(2,1)S(1)}, bf16[272,128]{1,0:T(8,128)(2,1)S(1)}, u32[]{:S(2)}, u32[]{:S(2)}) collective-permute-start(bf16[272,128]{1,0:T(8,128)(2,1)S(1)} %get-tuple-element.38), channel_id=1, source_target_pairs={{0,6},{1,7},{2,8},{3,9},{4,10},{5,11},{6,12},{7,13},{8,14},{9,15},... | collective-permute-start | bytes 208904 | tf_op jit(solution)/shard_map/ppermute | solution.py:52
  9.4 1.2 %collective-permute-start.3 = (bf16[272,128]{1,0:T(8,128)(2,1)S(1)}, bf16[272,128]{1,0:T(8,128)(2,1)S(1)}, u32[]{:S(2)}, u32[]{:S(2)}) collective-permute-start(bf16[272,128]{1,0:T(8,128)(2,1)S(1)} %get-tuple-element.39), channel_id=1, source_target_pairs={{0,8},{1,9},{2,10},{3,11},{4,12},{5,13},{6,14},{7,15},{8,0},{9,1},... | collective-permute-start | bytes 208904 | tf_op jit(solution)/shard_map/ppermute | solution.py:52
  10.6 2.6 %collective-permute-start.2 = (bf16[272,128]{1,0:T(8,128)(2,1)S(1)}, bf16[272,128]{1,0:T(8,128)(2,1)S(1)}, u32[]{:S(2)}, u32[]{:S(2)}) collective-permute-start(bf16[272,128]{1,0:T(8,128)(2,1)S(1)} %get-tuple-element.40), channel_id=1, source_target_pairs={{0,10},{1,11},{2,12},{3,13},{4,14},{5,15},{6,0},{7,1},{8,2},{9,3},... | collective-permute-start | bytes 208904 | tf_op jit(solution)/shard_map/ppermute | solution.py:52
  13.2 1.3 %collective-permute-start.1 = (bf16[272,128]{1,0:T(8,128)(2,1)S(1)}, bf16[272,128]{1,0:T(8,128)(2,1)S(1)}, u32[]{:S(2)}, u32[]{:S(2)}) collective-permute-start(bf16[272,128]{1,0:T(8,128)(2,1)S(1)} %get-tuple-element.41), channel_id=1, source_target_pairs={{0,12},{1,13},{2,14},{3,15},{4,0},{5,1},{6,2},{7,3},{8,4},{9,5},{1... | collective-permute-start | bytes 208904 | tf_op jit(solution)/shard_map/ppermute | solution.py:52
  14.6 1.5 %collective-permute-start = (bf16[272,128]{1,0:T(8,128)(2,1)S(1)}, bf16[272,128]{1,0:T(8,128)(2,1)S(1)}, u32[]{:S(2)}, u32[]{:S(2)}) collective-permute-start(bf16[272,128]{1,0:T(8,128)(2,1)S(1)} %get-tuple-element.42), channel_id=1, source_target_pairs={{0,14},{1,15},{2,0},{3,1},{4,2},{5,3},{6,4},{7,5},{8,6},{9,7},{10,... | collective-permute-start | bytes 208904 | tf_op jit(solution)/shard_map/ppermute | solution.py:52
  16.1 0.7 %collective-permute-done.4._.refs_4_ = bf16[272,128]{1,0:T(8,128)(2,1)S(1)} collective-permute-done((bf16[272,128]{1,0:T(8,128)(2,1)S(1)}, bf16[272,128]{1,0:T(8,128)(2,1)S(1)}, u32[]{:S(2)}, u32[]{:S(2)}) %collective-permute-start.4) | collective-permute-done | bytes 69664 | tf_op jit(solution)/shard_map/ppermute | solution.py:52
  17.6 2.4 %preload.1.refs_12_ = bf16[1216,1920]{1,0:T(8,128)(2,1)S(1)} custom-call(s32[1]{0:T(128)} %bitcast.place_ref, bf16[1216,5120]{1,0:T(8,128)(2,1)} %head_ref.3, bf16[272,128]{1,0:T(8,128)(2,1)S(1)} %collective-permute-done.4._.refs_4_), custom_call_target="tpu_custom_call" | custom-call | bytes 9338880 | tf_op jit(solution)/shard_map/preload/pallas_call | solution.py:486
  21.7 8.0 %logits.1 = (bf16[192,1216]{1,0:T(8,128)(2,1)}, f32[16,8,128]{2,1,0:T(8,128)}, f32[8,128]{1,0:T(8,128)S(1)}) custom-call(s32[1]{0:T(128)} %bitcast.place_ref, bf16[272,128]{1,0:T(8,128)(2,1)S(1)} %collective-permute-done.refs_0_, bf16[272,128]{1,0:T(8,128)(2,1)S(1)} %collective-permute-done.1.refs_1_, bf16[272,128]{1,0:T(8,128)(2,1)S(1)} %collective-permute-done.2.refs_2_, ...), custom_call_target="tpu_custom_call" | custom-call | flops 796917760 | bytes 12451840 | tf_op jit(solution)/shard_map/logits/pallas_call | solution.py:501
  29.8 6.7 %all-to-all-start = ((f32[16,8,128]{2,1,0:T(8,128)}), f32[16,8,128]{2,1,0:T(8,128)S(1)}, u32[]{:S(2)}, u32[]{:S(2)}) async-start(f32[16,8,128]{2,1,0:T(8,128)} %get-tuple-element.22), calls=%async_computation | async-start | bytes 131072 | tf_op jit(solution)/shard_map/all_to_all | solution.py:526
  36.5 6.3 %products.1 = (f32[8,5,2,64,128]{4,3,2,1,0:T(8,128)S(1)}, bf16[8,5,64,128]{3,2,1,0:T(8,128)(2,1)S(1)}) custom-call(s32[1]{0:T(128)} %bitcast.place_ref, bf16[192,1216]{1,0:T(8,128)(2,1)} %get-tuple-element.24.rows_ref, bf16[1216,5120]{1,0:T(8,128)(2,1)} %head_ref.3), custom_call_target="tpu_custom_call" | custom-call | flops 2390753280 | bytes 12451840 | tf_op jit(solution)/shard_map/products/pallas_call | solution.py:528
  43.4 1.0 %give.1 = (bf16[8,192,128]{2,1,0:T(8,128)(2,1)S(1)}, f32[3,64,128]{2,1,0:T(8,128)S(1)}, f32[1,1]{1,0:T(1,128)}) custom-call(s32[1]{0:T(128)} %bitcast.place_ref, f32[1]{0:T(128)S(6)} %copy.14.scale_ref, f32[16,8,128]{2,1,0:T(8,128)S(1)} %all-to-all-done.stats_ref, f32[8,128]{1,0:T(8,128)S(1)} %get-tuple-element.23.own_ref, ...), custom_call_target="tpu_custom_call" | custom-call | tf_op jit(solution)/shard_map/give/pallas_call | solution.py:545
  44.4 1.2 %keep.1 = (f32[8,192,128]{2,1,0:T(8,128)S(1)}, f32[1,1]{1,0:T(1,128)}) custom-call(s32[1]{0:T(128)} %bitcast.place_ref, f32[3,64,128]{2,1,0:T(8,128)S(1)} %get-tuple-element.27.factors_ref, f32[1,1]{1,0:T(1,128)} %get-tuple-element.28.found_ref, f32[8,5,2,64,128]{4,3,2,1,0:T(8,128)S(1)} %get-tuple-element.25.terms_ref, ...), custom_call_target="tpu_custom_call" | custom-call | flops 2621440 | bytes 2621440 | tf_op jit(solution)/shard_map/keep/pallas_call | solution.py:558
  46.3 1.4 %collective-permute-start.10 = (bf16[192,128]{1,0:T(8,128)(2,1)S(1)}, bf16[192,128]{1,0:T(8,128)(2,1)S(1)}, u32[]{:S(2)}, u32[]{:S(2)}) collective-permute-start(bf16[192,128]{1,0:T(8,128)(2,1)S(1)} %get-tuple-element.49), channel_id=1, source_target_pairs={{0,2},{1,3},{2,4},{3,5},{4,6},{5,7},{6,8},{7,9},{8,10},{9,11},{10,... | collective-permute-start | bytes 147464 | tf_op jit(solution)/shard_map/ppermute | solution.py:52
  47.7 1.5 %collective-permute-start.11 = (bf16[192,128]{1,0:T(8,128)(2,1)S(1)}, bf16[192,128]{1,0:T(8,128)(2,1)S(1)}, u32[]{:S(2)}, u32[]{:S(2)}) collective-permute-start(bf16[192,128]{1,0:T(8,128)(2,1)S(1)} %get-tuple-element.48), channel_id=1, source_target_pairs={{0,4},{1,5},{2,6},{3,7},{4,8},{5,9},{6,10},{7,11},{8,12},{9,13},{1... | collective-permute-start | bytes 147464 | tf_op jit(solution)/shard_map/ppermute | solution.py:52
  49.1 2.4 %collective-permute-start.12 = (bf16[192,128]{1,0:T(8,128)(2,1)S(1)}, bf16[192,128]{1,0:T(8,128)(2,1)S(1)}, u32[]{:S(2)}, u32[]{:S(2)}) collective-permute-start(bf16[192,128]{1,0:T(8,128)(2,1)S(1)} %get-tuple-element.47), channel_id=1, source_target_pairs={{0,6},{1,7},{2,8},{3,9},{4,10},{5,11},{6,12},{7,13},{8,14},{9,15},... | collective-permute-start | bytes 147464 | tf_op jit(solution)/shard_map/ppermute | solution.py:52
  51.5 1.5 %collective-permute-start.13 = (bf16[192,128]{1,0:T(8,128)(2,1)S(1)}, bf16[192,128]{1,0:T(8,128)(2,1)S(1)}, u32[]{:S(2)}, u32[]{:S(2)}) collective-permute-start(bf16[192,128]{1,0:T(8,128)(2,1)S(1)} %get-tuple-element.46), channel_id=1, source_target_pairs={{0,8},{1,9},{2,10},{3,11},{4,12},{5,13},{6,14},{7,15},{8,0},{9,1},... | collective-permute-start | bytes 147464 | tf_op jit(solution)/shard_map/ppermute | solution.py:52
  53.0 2.4 %collective-permute-start.14 = (bf16[192,128]{1,0:T(8,128)(2,1)S(1)}, bf16[192,128]{1,0:T(8,128)(2,1)S(1)}, u32[]{:S(2)}, u32[]{:S(2)}) collective-permute-start(bf16[192,128]{1,0:T(8,128)(2,1)S(1)} %get-tuple-element.45), channel_id=1, source_target_pairs={{0,10},{1,11},{2,12},{3,13},{4,14},{5,15},{6,0},{7,1},{8,2},{9,3},... | collective-permute-start | bytes 147464 | tf_op jit(solution)/shard_map/ppermute | solution.py:52
  55.3 1.5 %collective-permute-start.15 = (bf16[192,128]{1,0:T(8,128)(2,1)S(1)}, bf16[192,128]{1,0:T(8,128)(2,1)S(1)}, u32[]{:S(2)}, u32[]{:S(2)}) collective-permute-start(bf16[192,128]{1,0:T(8,128)(2,1)S(1)} %get-tuple-element.44), channel_id=1, source_target_pairs={{0,12},{1,13},{2,14},{3,15},{4,0},{5,1},{6,2},{7,3},{8,4},{9,5},{1... | collective-permute-start | bytes 147464 | tf_op jit(solution)/shard_map/ppermute | solution.py:52
  56.8 1.5 %collective-permute-start.16 = (bf16[192,128]{1,0:T(8,128)(2,1)S(1)}, bf16[192,128]{1,0:T(8,128)(2,1)S(1)}, u32[]{:S(2)}, u32[]{:S(2)}) collective-permute-start(bf16[192,128]{1,0:T(8,128)(2,1)S(1)} %get-tuple-element.43), channel_id=1, source_target_pairs={{0,14},{1,15},{2,0},{3,1},{4,2},{5,3},{6,4},{7,5},{8,6},{9,7},{10,... | collective-permute-start | bytes 147464 | tf_op jit(solution)/shard_map/ppermute | solution.py:52
  58.9 0.9 %collective-permute-done.15.refs_5_ = bf16[192,128]{1,0:T(8,128)(2,1)S(1)} collective-permute-done((bf16[192,128]{1,0:T(8,128)(2,1)S(1)}, bf16[192,128]{1,0:T(8,128)(2,1)S(1)}, u32[]{:S(2)}, u32[]{:S(2)}) %collective-permute-start.15) | collective-permute-done | bytes 49184 | tf_op jit(solution)/shard_map/ppermute | solution.py:52
  59.9 1.0 %collective-permute-done.16.refs_6_ = bf16[192,128]{1,0:T(8,128)(2,1)S(1)} collective-permute-done((bf16[192,128]{1,0:T(8,128)(2,1)S(1)}, bf16[192,128]{1,0:T(8,128)(2,1)S(1)}, u32[]{:S(2)}, u32[]{:S(2)}) %collective-permute-start.16) | collective-permute-done | bytes 49184 | tf_op jit(solution)/shard_map/ppermute | solution.py:52
  (28 shorter events, 4.6 us)
Async XLA Ops:
  2.2 11.0 %collective-permute-start.6 = (bf16[272,128]{1,0:T(8,128)(2,1)S(1)}, bf16[272,128]{1,0:T(8,128)(2,1)S(1)}, u32[]{:S(2)}, u32[]{:S(2)}) collective-permute-start(bf16[272,128]{1,0:T(8,128)(2,1)S(1)} %get-tuple-element.36), channel_id=1, source_target_pairs={{0,2},{1,3},{2,4},{3,5},{4,6},{5,7},{6,8},{7,9},{8,10},{9,11},{10,... | collective-permute-start | bytes 208904 | tf_op jit(solution)/shard_map/ppermute | solution.py:52
  5.2 9.4 %collective-permute-start.5 = (bf16[272,128]{1,0:T(8,128)(2,1)S(1)}, bf16[272,128]{1,0:T(8,128)(2,1)S(1)}, u32[]{:S(2)}, u32[]{:S(2)}) collective-permute-start(bf16[272,128]{1,0:T(8,128)(2,1)S(1)} %get-tuple-element.37), channel_id=1, source_target_pairs={{0,4},{1,5},{2,6},{3,7},{4,8},{5,9},{6,10},{7,11},{8,12},{9,13},{1... | collective-permute-start | bytes 208904 | tf_op jit(solution)/shard_map/ppermute | solution.py:52
  6.8 10.0 %collective-permute-start.4 = (bf16[272,128]{1,0:T(8,128)(2,1)S(1)}, bf16[272,128]{1,0:T(8,128)(2,1)S(1)}, u32[]{:S(2)}, u32[]{:S(2)}) collective-permute-start(bf16[272,128]{1,0:T(8,128)(2,1)S(1)} %get-tuple-element.38), channel_id=1, source_target_pairs={{0,6},{1,7},{2,8},{3,9},{4,10},{5,11},{6,12},{7,13},{8,14},{9,15},... | collective-permute-start | bytes 208904 | tf_op jit(solution)/shard_map/ppermute | solution.py:52
  9.4 8.2 %collective-permute-start.3 = (bf16[272,128]{1,0:T(8,128)(2,1)S(1)}, bf16[272,128]{1,0:T(8,128)(2,1)S(1)}, u32[]{:S(2)}, u32[]{:S(2)}) collective-permute-start(bf16[272,128]{1,0:T(8,128)(2,1)S(1)} %get-tuple-element.39), channel_id=1, source_target_pairs={{0,8},{1,9},{2,10},{3,11},{4,12},{5,13},{6,14},{7,15},{8,0},{9,1},... | collective-permute-start | bytes 208904 | tf_op jit(solution)/shard_map/ppermute | solution.py:52
  10.6 9.5 %collective-permute-start.2 = (bf16[272,128]{1,0:T(8,128)(2,1)S(1)}, bf16[272,128]{1,0:T(8,128)(2,1)S(1)}, u32[]{:S(2)}, u32[]{:S(2)}) collective-permute-start(bf16[272,128]{1,0:T(8,128)(2,1)S(1)} %get-tuple-element.40), channel_id=1, source_target_pairs={{0,10},{1,11},{2,12},{3,13},{4,14},{5,15},{6,0},{7,1},{8,2},{9,3},... | collective-permute-start | bytes 208904 | tf_op jit(solution)/shard_map/ppermute | solution.py:52
  13.2 6.8 %collective-permute-start.1 = (bf16[272,128]{1,0:T(8,128)(2,1)S(1)}, bf16[272,128]{1,0:T(8,128)(2,1)S(1)}, u32[]{:S(2)}, u32[]{:S(2)}) collective-permute-start(bf16[272,128]{1,0:T(8,128)(2,1)S(1)} %get-tuple-element.41), channel_id=1, source_target_pairs={{0,12},{1,13},{2,14},{3,15},{4,0},{5,1},{6,2},{7,3},{8,4},{9,5},{1... | collective-permute-start | bytes 208904 | tf_op jit(solution)/shard_map/ppermute | solution.py:52
  14.6 5.5 %collective-permute-start = (bf16[272,128]{1,0:T(8,128)(2,1)S(1)}, bf16[272,128]{1,0:T(8,128)(2,1)S(1)}, u32[]{:S(2)}, u32[]{:S(2)}) collective-permute-start(bf16[272,128]{1,0:T(8,128)(2,1)S(1)} %get-tuple-element.42), channel_id=1, source_target_pairs={{0,14},{1,15},{2,0},{3,1},{4,2},{5,3},{6,4},{7,5},{8,6},{9,7},{10,... | collective-permute-start | bytes 208904 | tf_op jit(solution)/shard_map/ppermute | solution.py:52
  17.6 4.2 %collective-permute-start.8 = (bf16[5,272,128]{2,1,0:T(8,128)(2,1)S(1)}, bf16[5,272,128]{2,1,0:T(8,128)(2,1)S(1)}, u32[]{:S(2)}, u32[]{:S(2)}) collective-permute-start(bf16[5,272,128]{2,1,0:T(8,128)(2,1)S(1)} %bitcast_dynamic-update-slice_fusion), channel_id=1, source_target_pairs={{0,1},{1,0},{2,3},{3,2},{4,5},{5,4},{6,7},{7,6},{8,9},{9,8},{10,11... | collective-permute-start | bytes 1044488 | tf_op jit(solution)/shard_map/ppermute | solution.py:47
  20.1 1.6 %collective-permute-start.7 = (bf16[3,272,128]{2,1,0:T(8,128)(2,1)S(1)}, bf16[3,272,128]{2,1,0:T(8,128)(2,1)S(1)}, u32[]{:S(2)}, u32[]{:S(2)}) collective-permute-start(bf16[3,272,128]{2,1,0:T(8,128)(2,1)S(1)} %pad_maximum_fusion), channel_id=1, source_target_pairs={{0,1},{1,0},{2,3},{3,2},{4,5},{5,4},{6,7},{7,6},{8,9},{9,8},{10,11... | collective-permute-start | bytes 626696 | tf_op jit(solution)/shard_map/ppermute | solution.py:47
  29.8 13.6 %all-to-all-start = ((f32[16,8,128]{2,1,0:T(8,128)}), f32[16,8,128]{2,1,0:T(8,128)S(1)}, u32[]{:S(2)}, u32[]{:S(2)}) async-start(f32[16,8,128]{2,1,0:T(8,128)} %get-tuple-element.22), calls=%async_computation | async-start | bytes 131072 | tf_op jit(solution)/shard_map/all_to_all | solution.py:526
  44.4 1.7 %collective-permute-start.9 = (bf16[8,192,128]{2,1,0:T(8,128)(2,1)S(1)}, bf16[8,192,128]{2,1,0:T(8,128)(2,1)S(1)}, u32[]{:S(2)}, u32[]{:S(2)}) collective-permute-start(bf16[8,192,128]{2,1,0:T(8,128)(2,1)S(1)} %get-tuple-element.30), channel_id=1, source_target_pairs={{0,1},{1,0},{2,3},{3,2},{4,5},{5,4},{6,7},{7,6},{8,9},{9,8},{10,11... | collective-permute-start | bytes 1179656 | tf_op jit(solution)/shard_map/ppermute | solution.py:47
  46.3 9.0 %collective-permute-start.10 = (bf16[192,128]{1,0:T(8,128)(2,1)S(1)}, bf16[192,128]{1,0:T(8,128)(2,1)S(1)}, u32[]{:S(2)}, u32[]{:S(2)}) collective-permute-start(bf16[192,128]{1,0:T(8,128)(2,1)S(1)} %get-tuple-element.49), channel_id=1, source_target_pairs={{0,2},{1,3},{2,4},{3,5},{4,6},{5,7},{6,8},{7,9},{8,10},{9,11},{10,... | collective-permute-start | bytes 147464 | tf_op jit(solution)/shard_map/ppermute | solution.py:52
  47.7 9.1 %collective-permute-start.11 = (bf16[192,128]{1,0:T(8,128)(2,1)S(1)}, bf16[192,128]{1,0:T(8,128)(2,1)S(1)}, u32[]{:S(2)}, u32[]{:S(2)}) collective-permute-start(bf16[192,128]{1,0:T(8,128)(2,1)S(1)} %get-tuple-element.48), channel_id=1, source_target_pairs={{0,4},{1,5},{2,6},{3,7},{4,8},{5,9},{6,10},{7,11},{8,12},{9,13},{1... | collective-permute-start | bytes 147464 | tf_op jit(solution)/shard_map/ppermute | solution.py:52
  49.1 9.1 %collective-permute-start.12 = (bf16[192,128]{1,0:T(8,128)(2,1)S(1)}, bf16[192,128]{1,0:T(8,128)(2,1)S(1)}, u32[]{:S(2)}, u32[]{:S(2)}) collective-permute-start(bf16[192,128]{1,0:T(8,128)(2,1)S(1)} %get-tuple-element.47), channel_id=1, source_target_pairs={{0,6},{1,7},{2,8},{3,9},{4,10},{5,11},{6,12},{7,13},{8,14},{9,15},... | collective-permute-start | bytes 147464 | tf_op jit(solution)/shard_map/ppermute | solution.py:52
  51.5 6.8 %collective-permute-start.13 = (bf16[192,128]{1,0:T(8,128)(2,1)S(1)}, bf16[192,128]{1,0:T(8,128)(2,1)S(1)}, u32[]{:S(2)}, u32[]{:S(2)}) collective-permute-start(bf16[192,128]{1,0:T(8,128)(2,1)S(1)} %get-tuple-element.46), channel_id=1, source_target_pairs={{0,8},{1,9},{2,10},{3,11},{4,12},{5,13},{6,14},{7,15},{8,0},{9,1},... | collective-permute-start | bytes 147464 | tf_op jit(solution)/shard_map/ppermute | solution.py:52
  53.0 6.0 %collective-permute-start.14 = (bf16[192,128]{1,0:T(8,128)(2,1)S(1)}, bf16[192,128]{1,0:T(8,128)(2,1)S(1)}, u32[]{:S(2)}, u32[]{:S(2)}) collective-permute-start(bf16[192,128]{1,0:T(8,128)(2,1)S(1)} %get-tuple-element.45), channel_id=1, source_target_pairs={{0,10},{1,11},{2,12},{3,13},{4,14},{5,15},{6,0},{7,1},{8,2},{9,3},... | collective-permute-start | bytes 147464 | tf_op jit(solution)/shard_map/ppermute | solution.py:52
  55.3 4.5 %collective-permute-start.15 = (bf16[192,128]{1,0:T(8,128)(2,1)S(1)}, bf16[192,128]{1,0:T(8,128)(2,1)S(1)}, u32[]{:S(2)}, u32[]{:S(2)}) collective-permute-start(bf16[192,128]{1,0:T(8,128)(2,1)S(1)} %get-tuple-element.44), channel_id=1, source_target_pairs={{0,12},{1,13},{2,14},{3,15},{4,0},{5,1},{6,2},{7,3},{8,4},{9,5},{1... | collective-permute-start | bytes 147464 | tf_op jit(solution)/shard_map/ppermute | solution.py:52
  56.8 4.1 %collective-permute-start.16 = (bf16[192,128]{1,0:T(8,128)(2,1)S(1)}, bf16[192,128]{1,0:T(8,128)(2,1)S(1)}, u32[]{:S(2)}, u32[]{:S(2)}) collective-permute-start(bf16[192,128]{1,0:T(8,128)(2,1)S(1)} %get-tuple-element.43), channel_id=1, source_target_pairs={{0,14},{1,15},{2,0},{3,1},{4,2},{5,3},{6,4},{7,5},{8,6},{9,7},{10,... | collective-permute-start | bytes 147464 | tf_op jit(solution)/shard_map/ppermute | solution.py:52

commit v16 on v15

--- a/solution.py
+++ b/solution.py
@@ -78,6 +78,13 @@
 
 def turned(array):
     return pltpu.roll(array, LANES // 2, 1)
+
+
+def folded(first, tile):
+    rows = tile.shape[0] // 2
+    upper, lower = tile[:rows], turned(tile[rows:])
+    low = low_lanes(upper.shape)
+    return jnp.where(first, jnp.where(low, upper, lower), jnp.where(low, lower, upper))
 
 
 def tiles_of(array, count):
@@ -175,7 +182,7 @@
         [
             jnp.where(first, tiles[0], jnp.where(low, turns[0], turns[1])),
             jnp.where(first, tiles[1], jnp.where(low, turns[1], turns[2])),
-            jnp.where(first, tiles[2], jnp.where(low, 0.0, turns[0])),
+            folded(first, jnp.where(first, tiles[2], turns[0])),
         ],
         axis=0,
     ).astype(jnp.bfloat16)
@@ -249,8 +256,9 @@
         copy.start()
     tokens, width = hidden_ref.shape[0], hidden_ref.shape[1] // chips
     shard_rows = head_ref.shape[0]
-    hidden_rows = 3 * tokens
+    hidden_rows = 5 * tokens // 2
     slots = tokens // (2 * chips)
+    low = low_lanes((tokens // 2, LANES))
 
     for step in range(chips):
         late = step > chips // 2
@@ -272,8 +280,11 @@
                 arrived_ref[rows, LANES * i : LANES * (i + 1)] = teacher[
                     2 * slots * i : 2 * slots * (i + 1)
                 ]
-        both = [block[2 * tokens : hidden_rows] for block in blocks]
-        hidden_ref[:, base + 2 * LANES : base + 3 * LANES] = both[0] + both[1]
+        own, other = [block[2 * tokens : hidden_rows].astype(jnp.float32) for block in blocks]
+        one, two = jnp.where(core == 0, own, other), jnp.where(core == 0, other, own)
+        tile = [jnp.where(low, one, two), turned(jnp.where(low, two, one))]
+        tile = jnp.concatenate(tile, axis=0).astype(jnp.bfloat16)
+        hidden_ref[:, base + 2 * LANES : base + 3 * LANES] = tile
 
     def product(step, count, columns):
         return lax.dot_general(
@@ -359,11 +370,12 @@
     tokens = terms_ref.shape[3]
     factor, level, weight = [factors_ref[i] for i in range(3)]
     for step in range(terms_ref.shape[0]):
-        for i in range(3):
-            tile = 2 * parity + i
+        for i, tile in enumerate((3 * parity, 3 * parity + 1, 2)):
             sums = terms_ref[step, tile, 0] + level * terms_ref[step, tile, 1]
             share = factor * sums - weight * picks_ref[step, tile].astype(jnp.float32)
-            out_ref[step, tokens * i : tokens * (i + 1)] = share.astype(out_ref.dtype)
+            if i == 2:
+                share = folded(parity == 0, share)
+            out_ref[step, tokens * i : tokens * i + share.shape[0]] = share.astype(out_ref.dtype)
 
 
 def give_kernel(
@@ -419,14 +431,15 @@
     total = own_ref[...]
     for share_ref in refs[:-1]:
         total += share_ref[...].astype(jnp.float32)
-    tiles = [total[tokens * i : tokens * (i + 1)] for i in range(3)]
-    turns = [turned(tile) for tile in tiles]
-    low = low_lanes(tiles[0].shape)
+    one, two, rest = total[:tokens], total[tokens : 2 * tokens], total[2 * tokens :]
+    rest = jnp.concatenate([rest, turned(rest)], axis=0)
+    turns = [turned(tile) for tile in (rest, one, two)]
+    low = low_lanes(one.shape)
     first = place_ref[0] % 2 == 0
     tiles = [
-        jnp.where(first, tiles[0], jnp.where(low, turns[0], turns[1])),
-        jnp.where(first, tiles[1], jnp.where(low, turns[1], turns[2])),
-        jnp.where(first, tiles[2], turns[2]),
+        jnp.where(first, one, jnp.where(low, turns[0], turns[1])),
+        jnp.where(first, two, jnp.where(low, turns[1], turns[2])),
+        jnp.where(first, rest, turns[2]),
     ]
     total = jnp.concatenate(tiles, axis=1)[:, :half]
     refs[-1][...] = total.astype(refs[-1].dtype)
@@ -452,7 +465,7 @@
     rows_scratch = pltpu.VMEM((3 * tokens, shard_rows), jnp.bfloat16)
     rows_sem = pltpu.SemaphoreType.DMA
     slots, entries = teacher_values.shape
-    hidden_rows = 3 * tokens
+    hidden_rows = 5 * tokens // 2
     teacher_rows = 2 * slots * (shard_rows + LANES // 2) // LANES
 
     operands = (
@@ -466,7 +479,7 @@
     packed, owner, table = pl.pallas_call(
         functools.partial(pack_kernel, shard_rows=shard_rows),
         out_shape=(
-            jax.ShapeDtypeStruct((chips, hidden_rows + teacher_rows, LANES), jnp.bfloat16),
+            vmem_array((chips, hidden_rows + teacher_rows, LANES), jnp.bfloat16),
             vmem_array((2 * tokens, 2 * tokens), jnp.bfloat16),
             vmem_array((tokens, LANES), jnp.float32),
         ),
@@ -521,7 +534,7 @@
             flops=2 * tokens * head.size, bytes_accessed=2 * head.size, transcendentals=0
         ),
         name="logits",
-    )(place, *near[::-1], *far, in_vmem(owner), in_vmem(table), in_vmem(early), head)
+    )(place, *[in_vmem(block) for block in near[::-1] + far], in_vmem(owner), in_vmem(table), in_vmem(early), head)
 
     all_stats = lax.all_to_all(stats, "vocab", split_axis=0, concat_axis=0, tiled=True)
 
@@ -553,7 +566,7 @@
         out_specs=[vmem] * 3,
         compiler_params=params,
         name="give",
-    )(place, loss_scale, all_stats, in_vmem(own_stats), in_vmem(table), terms, picks)
+    )(place, loss_scale, in_vmem(all_stats), in_vmem(own_stats), in_vmem(table), terms, picks)
     taken = swap_cores(give)
     keep, loss = pl.pallas_call(
         keep_kernel,
@@ -578,7 +591,7 @@
         out_specs=vmem,
         compiler_params=params,
         name="total",
-    )(place, sums[0], *shares)
+    )(place, *[in_vmem(share) for share in [sums[0]] + shares])
     return total, jnp.reshape(loss, (1,))
 
 

time: 61.9 us -> 60.5 us (0.977)
  waiting for transfers between devices: 5.65 us -> 4.47 us
    ppermute x14, waiting for transfers between devices: 4.08 us -> 3.19 us  [along_chips(): lax.ppermute(array, 'vocab', [(i, (i + 2 * step) % count) for i in range(...]
  transfers between devices with their start and end apart: 18 -> 18, of which waited for: 8 -> 8; matrix products, arithmetic and copies ran while one was open for 0% -> 0% of each run, Pallas kernels for 16% -> 17%
where the time goes in v16:
time: 60.5 us; the launch traced here: 60.3 us
  starting transfers between devices  32.6 us (54%)
  Pallas kernels  21.6 us (36%)
  waiting for transfers between devices  4.47 us (7%)
  between operations  1.43 us (2%)
    ppermute x14, starting transfers between devices, along_chips(): lax.ppermute(array, 'vocab', [(i, (i + 2 * step) % count) for i in range(...  25.8 us
    pallas_call x1, Pallas kernels, paired_shards(): pl.pallas_call(functools.partial(logits_kernel, chips=chips), out_shape=(...  8.29 us
    pallas_call x1, Pallas kernels, paired_shards(): pl.pallas_call(products_kernel, out_shape=(vmem_array((chips, width // LA...  6.31 us
    all_to_all x1, starting transfers between devices, paired_shards(): lax.all_to_all(stats, 'vocab', split_axis=0, concat_axis=0, tiled=True)  6.21 us
    ppermute x14, waiting for transfers between devices, along_chips(): lax.ppermute(array, 'vocab', [(i, (i + 2 * step) % count) for i in range(...  3.19 us
    pallas_call x1, Pallas kernels, paired_shards(): pl.pallas_call(functools.partial(preload_kernel, chips=chips), out_shape=...  2.4 us
    pallas_call x1, Pallas kernels, paired_shards(): pl.pallas_call(functools.partial(pack_kernel, shard_rows=shard_rows), out...  1.52 us
    pallas_call x1, Pallas kernels, paired_shards(): pl.pallas_call(keep_kernel, out_shape=(vmem_array((chips, hidden_rows, LA...  1.34 us
  transfers between devices with their start and end apart: 18, of which 8 were waited for; matrix products, arithmetic and copies ran while one was open for 0% of the time, Pallas kernels for 17%

profile of v16, /device:TPU:0, one launch (start us, length us, event | category | flops | bytes accessed | tf_op | source)
XLA Modules:
  0.0 60.3 jit_solution(2347165936474048806)
XLA Ops:
  0.6 1.5 %pack.1 = (bf16[8,240,128]{2,1,0:T(8,128)(2,1)S(1)}, bf16[128,128]{1,0:T(8,128)(2,1)S(1)}, f32[64,128]{1,0:T(8,128)S(1)}) custom-call(s32[1]{0:T(128)} %bitcast.place_ref, bf16[64,320]{1,0:T(8,128)(2,1)} %refs_0_.1, bf16[4,19456]{1,0:T(4,128)(2,1)} %refs_1_.1, f32[4,608]{1,0:T(4,128)} %refs_2_.1, s32[1,64]{1,0:T(1,128)} %bitcast.51, s32[1,64]{1,0:T(1,128)} %bitcast.52, ...), custom_call_target="tpu_custom_call" | custom-call | tf_op jit(solution)/shard_map/pack/pallas_call | solution.py:479
  2.2 3.0 %collective-permute-start.6 = (bf16[240,128]{1,0:T(8,128)(2,1)S(1)}, bf16[240,128]{1,0:T(8,128)(2,1)S(1)}, u32[]{:S(2)}, u32[]{:S(2)}) collective-permute-start(bf16[240,128]{1,0:T(8,128)(2,1)S(1)} %get-tuple-element.36), channel_id=1, source_target_pairs={{0,2},{1,3},{2,4},{3,5},{4,6},{5,7},{6,8},{7,9},{8,10},{9,11},{10,... | collective-permute-start | bytes 184328 | tf_op jit(solution)/shard_map/ppermute | solution.py:52
  5.2 1.6 %collective-permute-start.5 = (bf16[240,128]{1,0:T(8,128)(2,1)S(1)}, bf16[240,128]{1,0:T(8,128)(2,1)S(1)}, u32[]{:S(2)}, u32[]{:S(2)}) collective-permute-start(bf16[240,128]{1,0:T(8,128)(2,1)S(1)} %get-tuple-element.37), channel_id=1, source_target_pairs={{0,4},{1,5},{2,6},{3,7},{4,8},{5,9},{6,10},{7,11},{8,12},{9,13},{1... | collective-permute-start | bytes 184328 | tf_op jit(solution)/shard_map/ppermute | solution.py:52
  6.8 2.5 %collective-permute-start.4 = (bf16[240,128]{1,0:T(8,128)(2,1)S(1)}, bf16[240,128]{1,0:T(8,128)(2,1)S(1)}, u32[]{:S(2)}, u32[]{:S(2)}) collective-permute-start(bf16[240,128]{1,0:T(8,128)(2,1)S(1)} %get-tuple-element.38), channel_id=1, source_target_pairs={{0,6},{1,7},{2,8},{3,9},{4,10},{5,11},{6,12},{7,13},{8,14},{9,15},... | collective-permute-start | bytes 184328 | tf_op jit(solution)/shard_map/ppermute | solution.py:52
  9.3 1.2 %collective-permute-start.3 = (bf16[240,128]{1,0:T(8,128)(2,1)S(1)}, bf16[240,128]{1,0:T(8,128)(2,1)S(1)}, u32[]{:S(2)}, u32[]{:S(2)}) collective-permute-start(bf16[240,128]{1,0:T(8,128)(2,1)S(1)} %get-tuple-element.39), channel_id=1, source_target_pairs={{0,8},{1,9},{2,10},{3,11},{4,12},{5,13},{6,14},{7,15},{8,0},{9,1},... | collective-permute-start | bytes 184328 | tf_op jit(solution)/shard_map/ppermute | solution.py:52
  10.6 2.6 %collective-permute-start.2 = (bf16[240,128]{1,0:T(8,128)(2,1)S(1)}, bf16[240,128]{1,0:T(8,128)(2,1)S(1)}, u32[]{:S(2)}, u32[]{:S(2)}) collective-permute-start(bf16[240,128]{1,0:T(8,128)(2,1)S(1)} %get-tuple-element.40), channel_id=1, source_target_pairs={{0,10},{1,11},{2,12},{3,13},{4,14},{5,15},{6,0},{7,1},{8,2},{9,3},... | collective-permute-start | bytes 184328 | tf_op jit(solution)/shard_map/ppermute | solution.py:52
  13.2 1.3 %collective-permute-start.1 = (bf16[240,128]{1,0:T(8,128)(2,1)S(1)}, bf16[240,128]{1,0:T(8,128)(2,1)S(1)}, u32[]{:S(2)}, u32[]{:S(2)}) collective-permute-start(bf16[240,128]{1,0:T(8,128)(2,1)S(1)} %get-tuple-element.41), channel_id=1, source_target_pairs={{0,12},{1,13},{2,14},{3,15},{4,0},{5,1},{6,2},{7,3},{8,4},{9,5},{1... | collective-permute-start | bytes 184328 | tf_op jit(solution)/shard_map/ppermute | solution.py:52
  14.6 1.5 %collective-permute-start = (bf16[240,128]{1,0:T(8,128)(2,1)S(1)}, bf16[240,128]{1,0:T(8,128)(2,1)S(1)}, u32[]{:S(2)}, u32[]{:S(2)}) collective-permute-start(bf16[240,128]{1,0:T(8,128)(2,1)S(1)} %get-tuple-element.42), channel_id=1, source_target_pairs={{0,14},{1,15},{2,0},{3,1},{4,2},{5,3},{6,4},{7,5},{8,6},{9,7},{10,... | collective-permute-start | bytes 184328 | tf_op jit(solution)/shard_map/ppermute | solution.py:52
  16.8 2.4 %preload.1.refs_12_ = bf16[1216,1920]{1,0:T(8,128)(2,1)S(1)} custom-call(s32[1]{0:T(128)} %bitcast.place_ref, bf16[1216,5120]{1,0:T(8,128)(2,1)} %head_ref.3, bf16[240,128]{1,0:T(8,128)(2,1)S(1)} %collective-permute-done.4._.refs_4_), custom_call_target="tpu_custom_call" | custom-call | bytes 9338880 | tf_op jit(solution)/shard_map/preload/pallas_call | solution.py:499
  20.9 8.3 %logits.1 = (bf16[192,1216]{1,0:T(8,128)(2,1)}, f32[16,8,128]{2,1,0:T(8,128)}, f32[8,128]{1,0:T(8,128)S(1)}) custom-call(s32[1]{0:T(128)} %bitcast.place_ref, bf16[240,128]{1,0:T(8,128)(2,1)S(1)} %collective-permute-done.refs_0_, bf16[240,128]{1,0:T(8,128)(2,1)S(1)} %collective-permute-done.1.refs_1_, bf16[240,128]{1,0:T(8,128)(2,1)S(1)} %collective-permute-done.2.refs_2_, ...), custom_call_target="tpu_custom_call" | custom-call | flops 796917760 | bytes 12451840 | tf_op jit(solution)/shard_map/logits/pallas_call | solution.py:514
  29.2 6.2 %all-to-all-start = ((f32[16,8,128]{2,1,0:T(8,128)}), f32[16,8,128]{2,1,0:T(8,128)S(1)}, u32[]{:S(2)}, u32[]{:S(2)}) async-start(f32[16,8,128]{2,1,0:T(8,128)} %get-tuple-element.22), calls=%async_computation | async-start | bytes 131072 | tf_op jit(solution)/shard_map/all_to_all | solution.py:539
  35.4 6.3 %products.1 = (f32[8,5,2,64,128]{4,3,2,1,0:T(8,128)S(1)}, bf16[8,5,64,128]{3,2,1,0:T(8,128)(2,1)S(1)}) custom-call(s32[1]{0:T(128)} %bitcast.place_ref, bf16[192,1216]{1,0:T(8,128)(2,1)} %get-tuple-element.24.rows_ref, bf16[1216,5120]{1,0:T(8,128)(2,1)} %head_ref.3), custom_call_target="tpu_custom_call" | custom-call | flops 2390753280 | bytes 12451840 | tf_op jit(solution)/shard_map/products/pallas_call | solution.py:541
  42.3 0.9 %give.1 = (bf16[8,160,128]{2,1,0:T(8,128)(2,1)S(1)}, f32[3,64,128]{2,1,0:T(8,128)S(1)}, f32[1,1]{1,0:T(1,128)}) custom-call(s32[1]{0:T(128)} %bitcast.place_ref, f32[1]{0:T(128)S(6)} %copy.14.scale_ref, f32[16,8,128]{2,1,0:T(8,128)S(1)} %all-to-all-done.stats_ref, f32[8,128]{1,0:T(8,128)S(1)} %get-tuple-element.23.own_ref, ...), custom_call_target="tpu_custom_call" | custom-call | tf_op jit(solution)/shard_map/give/pallas_call | solution.py:558
  43.3 1.3 %keep.1 = (f32[8,160,128]{2,1,0:T(8,128)S(1)}, f32[1,1]{1,0:T(1,128)}) custom-call(s32[1]{0:T(128)} %bitcast.place_ref, f32[3,64,128]{2,1,0:T(8,128)S(1)} %get-tuple-element.27.factors_ref, f32[1,1]{1,0:T(1,128)} %get-tuple-element.28.found_ref, f32[8,5,2,64,128]{4,3,2,1,0:T(8,128)S(1)} %get-tuple-element.25.terms_ref, ...), custom_call_target="tpu_custom_call" | custom-call | flops 2621440 | bytes 2621440 | tf_op jit(solution)/shard_map/keep/pallas_call | solution.py:571
  45.0 1.4 %collective-permute-start.10 = (bf16[160,128]{1,0:T(8,128)(2,1)S(1)}, bf16[160,128]{1,0:T(8,128)(2,1)S(1)}, u32[]{:S(2)}, u32[]{:S(2)}) collective-permute-start(bf16[160,128]{1,0:T(8,128)(2,1)S(1)} %get-tuple-element.49), channel_id=1, source_target_pairs={{0,2},{1,3},{2,4},{3,5},{4,6},{5,7},{6,8},{7,9},{8,10},{9,11},{10,... | collective-permute-start | bytes 122888 | tf_op jit(solution)/shard_map/ppermute | solution.py:52
  46.4 1.5 %collective-permute-start.11 = (bf16[160,128]{1,0:T(8,128)(2,1)S(1)}, bf16[160,128]{1,0:T(8,128)(2,1)S(1)}, u32[]{:S(2)}, u32[]{:S(2)}) collective-permute-start(bf16[160,128]{1,0:T(8,128)(2,1)S(1)} %get-tuple-element.48), channel_id=1, source_target_pairs={{0,4},{1,5},{2,6},{3,7},{4,8},{5,9},{6,10},{7,11},{8,12},{9,13},{1... | collective-permute-start | bytes 122888 | tf_op jit(solution)/shard_map/ppermute | solution.py:52
  47.9 2.4 %collective-permute-start.12 = (bf16[160,128]{1,0:T(8,128)(2,1)S(1)}, bf16[160,128]{1,0:T(8,128)(2,1)S(1)}, u32[]{:S(2)}, u32[]{:S(2)}) collective-permute-start(bf16[160,128]{1,0:T(8,128)(2,1)S(1)} %get-tuple-element.47), channel_id=1, source_target_pairs={{0,6},{1,7},{2,8},{3,9},{4,10},{5,11},{6,12},{7,13},{8,14},{9,15},... | collective-permute-start | bytes 122888 | tf_op jit(solution)/shard_map/ppermute | solution.py:52
  50.2 1.5 %collective-permute-start.13 = (bf16[160,128]{1,0:T(8,128)(2,1)S(1)}, bf16[160,128]{1,0:T(8,128)(2,1)S(1)}, u32[]{:S(2)}, u32[]{:S(2)}) collective-permute-start(bf16[160,128]{1,0:T(8,128)(2,1)S(1)} %get-tuple-element.46), channel_id=1, source_target_pairs={{0,8},{1,9},{2,10},{3,11},{4,12},{5,13},{6,14},{7,15},{8,0},{9,1},... | collective-permute-start | bytes 122888 | tf_op jit(solution)/shard_map/ppermute | solution.py:52
  51.7 2.4 %collective-permute-start.14 = (bf16[160,128]{1,0:T(8,128)(2,1)S(1)}, bf16[160,128]{1,0:T(8,128)(2,1)S(1)}, u32[]{:S(2)}, u32[]{:S(2)}) collective-permute-start(bf16[160,128]{1,0:T(8,128)(2,1)S(1)} %get-tuple-element.45), channel_id=1, source_target_pairs={{0,10},{1,11},{2,12},{3,13},{4,14},{5,15},{6,0},{7,1},{8,2},{9,3},... | collective-permute-start | bytes 122888 | tf_op jit(solution)/shard_map/ppermute | solution.py:52
  54.1 1.5 %collective-permute-start.15 = (bf16[160,128]{1,0:T(8,128)(2,1)S(1)}, bf16[160,128]{1,0:T(8,128)(2,1)S(1)}, u32[]{:S(2)}, u32[]{:S(2)}) collective-permute-start(bf16[160,128]{1,0:T(8,128)(2,1)S(1)} %get-tuple-element.44), channel_id=1, source_target_pairs={{0,12},{1,13},{2,14},{3,15},{4,0},{5,1},{6,2},{7,3},{8,4},{9,5},{1... | collective-permute-start | bytes 122888 | tf_op jit(solution)/shard_map/ppermute | solution.py:52
  55.5 1.5 %collective-permute-start.16 = (bf16[160,128]{1,0:T(8,128)(2,1)S(1)}, bf16[160,128]{1,0:T(8,128)(2,1)S(1)}, u32[]{:S(2)}, u32[]{:S(2)}) collective-permute-start(bf16[160,128]{1,0:T(8,128)(2,1)S(1)} %get-tuple-element.43), channel_id=1, source_target_pairs={{0,14},{1,15},{2,0},{3,1},{4,2},{5,3},{6,4},{7,5},{8,6},{9,7},{10,... | collective-permute-start | bytes 122888 | tf_op jit(solution)/shard_map/ppermute | solution.py:52
  57.1 1.1 %collective-permute-done.15.refs_5_ = bf16[160,128]{1,0:T(8,128)(2,1)S(1)} collective-permute-done((bf16[160,128]{1,0:T(8,128)(2,1)S(1)}, bf16[160,128]{1,0:T(8,128)(2,1)S(1)}, u32[]{:S(2)}, u32[]{:S(2)}) %collective-permute-start.15) | collective-permute-done | bytes 40992 | tf_op jit(solution)/shard_map/ppermute | solution.py:52
  58.2 1.4 %collective-permute-done.16.refs_6_ = bf16[160,128]{1,0:T(8,128)(2,1)S(1)} collective-permute-done((bf16[160,128]{1,0:T(8,128)(2,1)S(1)}, bf16[160,128]{1,0:T(8,128)(2,1)S(1)}, u32[]{:S(2)}, u32[]{:S(2)}) %collective-permute-start.16) | collective-permute-done | bytes 40992 | tf_op jit(solution)/shard_map/ppermute | solution.py:52
  59.5 0.8 %total.1 = bf16[64,320]{1,0:T(8,128)(2,1)} custom-call(s32[1]{0:T(128)} %bitcast.place_ref, f32[160,128]{1,0:T(8,128)S(1)} %slice_bitcast_fusion.own_ref, bf16[160,128]{1,0:T(8,128)(2,1)S(1)} %collective-permute-done.10.refs_0_, bf16[160,128]{1,0:T(8,128)(2,1)S(1)} %collective-permute-done.11.refs_1_, bf16[160,128]{1,0:T(8,128)(2,1)S(1)} %collective-permute-done.12.refs_2_, ...), custom_call_target="tpu_custom_call" | custom-call | tf_op jit(solution)/shard_map/total/pallas_call | solution.py:587
  (28 shorter events, 2.9 us)
Async XLA Ops:
  2.2 11.0 %collective-permute-start.6 = (bf16[240,128]{1,0:T(8,128)(2,1)S(1)}, bf16[240,128]{1,0:T(8,128)(2,1)S(1)}, u32[]{:S(2)}, u32[]{:S(2)}) collective-permute-start(bf16[240,128]{1,0:T(8,128)(2,1)S(1)} %get-tuple-element.36), channel_id=1, source_target_pairs={{0,2},{1,3},{2,4},{3,5},{4,6},{5,7},{6,8},{7,9},{8,10},{9,11},{10,... | collective-permute-start | bytes 184328 | tf_op jit(solution)/shard_map/ppermute | solution.py:52
  5.2 9.4 %collective-permute-start.5 = (bf16[240,128]{1,0:T(8,128)(2,1)S(1)}, bf16[240,128]{1,0:T(8,128)(2,1)S(1)}, u32[]{:S(2)}, u32[]{:S(2)}) collective-permute-start(bf16[240,128]{1,0:T(8,128)(2,1)S(1)} %get-tuple-element.37), channel_id=1, source_target_pairs={{0,4},{1,5},{2,6},{3,7},{4,8},{5,9},{6,10},{7,11},{8,12},{9,13},{1... | collective-permute-start | bytes 184328 | tf_op jit(solution)/shard_map/ppermute | solution.py:52
  6.8 9.4 %collective-permute-start.4 = (bf16[240,128]{1,0:T(8,128)(2,1)S(1)}, bf16[240,128]{1,0:T(8,128)(2,1)S(1)}, u32[]{:S(2)}, u32[]{:S(2)}) collective-permute-start(bf16[240,128]{1,0:T(8,128)(2,1)S(1)} %get-tuple-element.38), channel_id=1, source_target_pairs={{0,6},{1,7},{2,8},{3,9},{4,10},{5,11},{6,12},{7,13},{8,14},{9,15},... | collective-permute-start | bytes 184328 | tf_op jit(solution)/shard_map/ppermute | solution.py:52
  9.3 7.4 %collective-permute-start.3 = (bf16[240,128]{1,0:T(8,128)(2,1)S(1)}, bf16[240,128]{1,0:T(8,128)(2,1)S(1)}, u32[]{:S(2)}, u32[]{:S(2)}) collective-permute-start(bf16[240,128]{1,0:T(8,128)(2,1)S(1)} %get-tuple-element.39), channel_id=1, source_target_pairs={{0,8},{1,9},{2,10},{3,11},{4,12},{5,13},{6,14},{7,15},{8,0},{9,1},... | collective-permute-start | bytes 184328 | tf_op jit(solution)/shard_map/ppermute | solution.py:52
  10.6 8.7 %collective-permute-start.2 = (bf16[240,128]{1,0:T(8,128)(2,1)S(1)}, bf16[240,128]{1,0:T(8,128)(2,1)S(1)}, u32[]{:S(2)}, u32[]{:S(2)}) collective-permute-start(bf16[240,128]{1,0:T(8,128)(2,1)S(1)} %get-tuple-element.40), channel_id=1, source_target_pairs={{0,10},{1,11},{2,12},{3,13},{4,14},{5,15},{6,0},{7,1},{8,2},{9,3},... | collective-permute-start | bytes 184328 | tf_op jit(solution)/shard_map/ppermute | solution.py:52
  13.2 6.0 %collective-permute-start.1 = (bf16[240,128]{1,0:T(8,128)(2,1)S(1)}, bf16[240,128]{1,0:T(8,128)(2,1)S(1)}, u32[]{:S(2)}, u32[]{:S(2)}) collective-permute-start(bf16[240,128]{1,0:T(8,128)(2,1)S(1)} %get-tuple-element.41), channel_id=1, source_target_pairs={{0,12},{1,13},{2,14},{3,15},{4,0},{5,1},{6,2},{7,3},{8,4},{9,5},{1... | collective-permute-start | bytes 184328 | tf_op jit(solution)/shard_map/ppermute | solution.py:52
  14.6 4.7 %collective-permute-start = (bf16[240,128]{1,0:T(8,128)(2,1)S(1)}, bf16[240,128]{1,0:T(8,128)(2,1)S(1)}, u32[]{:S(2)}, u32[]{:S(2)}) collective-permute-start(bf16[240,128]{1,0:T(8,128)(2,1)S(1)} %get-tuple-element.42), channel_id=1, source_target_pairs={{0,14},{1,15},{2,0},{3,1},{4,2},{5,3},{6,4},{7,5},{8,6},{9,7},{10,... | collective-permute-start | bytes 184328 | tf_op jit(solution)/shard_map/ppermute | solution.py:52
  16.8 4.2 %collective-permute-start.8 = (bf16[5,240,128]{2,1,0:T(8,128)(2,1)S(1)}, bf16[5,240,128]{2,1,0:T(8,128)(2,1)S(1)}, u32[]{:S(2)}, u32[]{:S(2)}) collective-permute-start(bf16[5,240,128]{2,1,0:T(8,128)(2,1)S(1)} %bitcast_dynamic-update-slice_fusion), channel_id=1, source_target_pairs={{0,1},{1,0},{2,3},{3,2},{4,5},{5,4},{6,7},{7,6},{8,9},{9,8},{10,11... | collective-permute-start | bytes 921608 | tf_op jit(solution)/shard_map/ppermute | solution.py:47
  19.3 1.6 %collective-permute-start.7 = (bf16[3,240,128]{2,1,0:T(8,128)(2,1)S(1)}, bf16[3,240,128]{2,1,0:T(8,128)(2,1)S(1)}, u32[]{:S(2)}, u32[]{:S(2)}) collective-permute-start(bf16[3,240,128]{2,1,0:T(8,128)(2,1)S(1)} %pad_maximum_fusion), channel_id=1, source_target_pairs={{0,1},{1,0},{2,3},{3,2},{4,5},{5,4},{6,7},{7,6},{8,9},{9,8},{10,11... | collective-permute-start | bytes 552968 | tf_op jit(solution)/shard_map/ppermute | solution.py:47
  29.2 13.1 %all-to-all-start = ((f32[16,8,128]{2,1,0:T(8,128)}), f32[16,8,128]{2,1,0:T(8,128)S(1)}, u32[]{:S(2)}, u32[]{:S(2)}) async-start(f32[16,8,128]{2,1,0:T(8,128)} %get-tuple-element.22), calls=%async_computation | async-start | bytes 131072 | tf_op jit(solution)/shard_map/all_to_all | solution.py:539
  43.3 1.6 %collective-permute-start.9 = (bf16[8,160,128]{2,1,0:T(8,128)(2,1)S(1)}, bf16[8,160,128]{2,1,0:T(8,128)(2,1)S(1)}, u32[]{:S(2)}, u32[]{:S(2)}) collective-permute-start(bf16[8,160,128]{2,1,0:T(8,128)(2,1)S(1)} %get-tuple-element.30), channel_id=1, source_target_pairs={{0,1},{1,0},{2,3},{3,2},{4,5},{5,4},{6,7},{7,6},{8,9},{9,8},{10,11... | collective-permute-start | bytes 983048 | tf_op jit(solution)/shard_map/ppermute | solution.py:47
  45.0 9.0 %collective-permute-start.10 = (bf16[160,128]{1,0:T(8,128)(2,1)S(1)}, bf16[160,128]{1,0:T(8,128)(2,1)S(1)}, u32[]{:S(2)}, u32[]{:S(2)}) collective-permute-start(bf16[160,128]{1,0:T(8,128)(2,1)S(1)} %get-tuple-element.49), channel_id=1, source_target_pairs={{0,2},{1,3},{2,4},{3,5},{4,6},{5,7},{6,8},{7,9},{8,10},{9,11},{10,... | collective-permute-start | bytes 122888 | tf_op jit(solution)/shard_map/ppermute | solution.py:52
  46.4 9.1 %collective-permute-start.11 = (bf16[160,128]{1,0:T(8,128)(2,1)S(1)}, bf16[160,128]{1,0:T(8,128)(2,1)S(1)}, u32[]{:S(2)}, u32[]{:S(2)}) collective-permute-start(bf16[160,128]{1,0:T(8,128)(2,1)S(1)} %get-tuple-element.48), channel_id=1, source_target_pairs={{0,4},{1,5},{2,6},{3,7},{4,8},{5,9},{6,10},{7,11},{8,12},{9,13},{1... | collective-permute-start | bytes 122888 | tf_op jit(solution)/shard_map/ppermute | solution.py:52
  47.9 9.1 %collective-permute-start.12 = (bf16[160,128]{1,0:T(8,128)(2,1)S(1)}, bf16[160,128]{1,0:T(8,128)(2,1)S(1)}, u32[]{:S(2)}, u32[]{:S(2)}) collective-permute-start(bf16[160,128]{1,0:T(8,128)(2,1)S(1)} %get-tuple-element.47), channel_id=1, source_target_pairs={{0,6},{1,7},{2,8},{3,9},{4,10},{5,11},{6,12},{7,13},{8,14},{9,15},... | collective-permute-start | bytes 122888 | tf_op jit(solution)/shard_map/ppermute | solution.py:52
  50.2 6.8 %collective-permute-start.13 = (bf16[160,128]{1,0:T(8,128)(2,1)S(1)}, bf16[160,128]{1,0:T(8,128)(2,1)S(1)}, u32[]{:S(2)}, u32[]{:S(2)}) collective-permute-start(bf16[160,128]{1,0:T(8,128)(2,1)S(1)} %get-tuple-element.46), channel_id=1, source_target_pairs={{0,8},{1,9},{2,10},{3,11},{4,12},{5,13},{6,14},{7,15},{8,0},{9,1},... | collective-permute-start | bytes 122888 | tf_op jit(solution)/shard_map/ppermute | solution.py:52
  51.7 5.4 %collective-permute-start.14 = (bf16[160,128]{1,0:T(8,128)(2,1)S(1)}, bf16[160,128]{1,0:T(8,128)(2,1)S(1)}, u32[]{:S(2)}, u32[]{:S(2)}) collective-permute-start(bf16[160,128]{1,0:T(8,128)(2,1)S(1)} %get-tuple-element.45), channel_id=1, source_target_pairs={{0,10},{1,11},{2,12},{3,13},{4,14},{5,15},{6,0},{7,1},{8,2},{9,3},... | collective-permute-start | bytes 122888 | tf_op jit(solution)/shard_map/ppermute | solution.py:52
  54.1 4.1 %collective-permute-start.15 = (bf16[160,128]{1,0:T(8,128)(2,1)S(1)}, bf16[160,128]{1,0:T(8,128)(2,1)S(1)}, u32[]{:S(2)}, u32[]{:S(2)}) collective-permute-start(bf16[160,128]{1,0:T(8,128)(2,1)S(1)} %get-tuple-element.44), channel_id=1, source_target_pairs={{0,12},{1,13},{2,14},{3,15},{4,0},{5,1},{6,2},{7,3},{8,4},{9,5},{1... | collective-permute-start | bytes 122888 | tf_op jit(solution)/shard_map/ppermute | solution.py:52
  55.5 4.0 %collective-permute-start.16 = (bf16[160,128]{1,0:T(8,128)(2,1)S(1)}, bf16[160,128]{1,0:T(8,128)(2,1)S(1)}, u32[]{:S(2)}, u32[]{:S(2)}) collective-permute-start(bf16[160,128]{1,0:T(8,128)(2,1)S(1)} %get-tuple-element.43), channel_id=1, source_target_pairs={{0,14},{1,15},{2,0},{3,1},{4,2},{5,3},{6,4},{7,5},{8,6},{9,7},{10,... | collective-permute-start | bytes 122888 | tf_op jit(solution)/shard_map/ppermute | solution.py:52

commit v17 on v16

--- a/solution.py
+++ b/solution.py
@@ -286,15 +286,17 @@
         tile = jnp.concatenate(tile, axis=0).astype(jnp.bfloat16)
         hidden_ref[:, base + 2 * LANES : base + 3 * LANES] = tile
 
-    def product(step, count, columns):
+    def product(step, columns):
         return lax.dot_general(
-            hidden_ref[:, width * step : width * (step + count)],
+            hidden_ref[:, width * step : width * (step + 1)],
             columns,
             (((1,), (1,)), ((), ())),
             preferred_element_type=jnp.float32,
         )
 
-    logits = product(0, EARLY, early_ref[...])
+    logits = product(0, early_ref[:, :width])
+    for step in range(1, EARLY):
+        logits += product(step, early_ref[:, width * step : width * (step + 1)])
     placed = jnp.dot(
         owner_ref[...], arrived_ref[...].astype(jnp.bfloat16), preferred_element_type=jnp.float32
     )
@@ -309,7 +311,7 @@
     for step in range(len(copies)):
         take(copies, step)
         columns = held_ref[:, width * step : width * (step + 1)]
-        logits += product(EARLY + step, 1, columns)
+        logits += product(EARLY + step, columns)
 
     top = jnp.max(logits, axis=1, keepdims=True)
     off = logits - top

time: 60.5 us -> 60.4 us (level)
  no operation moved by 1% of the time
where the time goes in v17:
time: 60.4 us; the launch traced here: 60.2 us
  starting transfers between devices  32.6 us (54%)
  Pallas kernels  21.4 us (35%)
  waiting for transfers between devices  4.47 us (7%)
  between operations  1.43 us (2%)
    ppermute x14, starting transfers between devices, along_chips(): lax.ppermute(array, 'vocab', [(i, (i + 2 * step) % count) for i in range(...  25.8 us
    pallas_call x1, Pallas kernels, paired_shards(): pl.pallas_call(functools.partial(logits_kernel, chips=chips), out_shape=(...  8.15 us
    pallas_call x1, Pallas kernels, paired_shards(): pl.pallas_call(products_kernel, out_shape=(vmem_array((chips, width // LA...  6.31 us
    all_to_all x1, starting transfers between devices, paired_shards(): lax.all_to_all(stats, 'vocab', split_axis=0, concat_axis=0, tiled=True)  6.2 us
    ppermute x14, waiting for transfers between devices, along_chips(): lax.ppermute(array, 'vocab', [(i, (i + 2 * step) % count) for i in range(...  3.2 us
    pallas_call x1, Pallas kernels, paired_shards(): pl.pallas_call(functools.partial(preload_kernel, chips=chips), out_shape=...  2.4 us
    pallas_call x1, Pallas kernels, paired_shards(): pl.pallas_call(functools.partial(pack_kernel, shard_rows=shard_rows), out...  1.52 us
    pallas_call x1, Pallas kernels, paired_shards(): pl.pallas_call(keep_kernel, out_shape=(vmem_array((chips, hidden_rows, LA...  1.34 us
  transfers between devices with their start and end apart: 18, of which 8 were waited for; matrix products, arithmetic and copies ran while one was open for 0% of the time, Pallas kernels for 17%

profile of v17, /device:TPU:0, one launch (start us, length us, event | category | flops | bytes accessed | tf_op | source)
XLA Modules:
  0.0 60.2 jit_solution(7042178506779952877)
XLA Ops:
  0.6 1.5 %pack.1 = (bf16[8,240,128]{2,1,0:T(8,128)(2,1)S(1)}, bf16[128,128]{1,0:T(8,128)(2,1)S(1)}, f32[64,128]{1,0:T(8,128)S(1)}) custom-call(s32[1]{0:T(128)} %bitcast.place_ref, bf16[64,320]{1,0:T(8,128)(2,1)} %refs_0_.1, bf16[4,19456]{1,0:T(4,128)(2,1)} %refs_1_.1, f32[4,608]{1,0:T(4,128)} %refs_2_.1, s32[1,64]{1,0:T(1,128)} %bitcast.51, s32[1,64]{1,0:T(1,128)} %bitcast.52, ...), custom_call_target="tpu_custom_call" | custom-call | tf_op jit(solution)/shard_map/pack/pallas_call | solution.py:481
  2.2 3.0 %collective-permute-start.6 = (bf16[240,128]{1,0:T(8,128)(2,1)S(1)}, bf16[240,128]{1,0:T(8,128)(2,1)S(1)}, u32[]{:S(2)}, u32[]{:S(2)}) collective-permute-start(bf16[240,128]{1,0:T(8,128)(2,1)S(1)} %get-tuple-element.36), channel_id=1, source_target_pairs={{0,2},{1,3},{2,4},{3,5},{4,6},{5,7},{6,8},{7,9},{8,10},{9,11},{10,... | collective-permute-start | bytes 184328 | tf_op jit(solution)/shard_map/ppermute | solution.py:52
  5.2 1.6 %collective-permute-start.5 = (bf16[240,128]{1,0:T(8,128)(2,1)S(1)}, bf16[240,128]{1,0:T(8,128)(2,1)S(1)}, u32[]{:S(2)}, u32[]{:S(2)}) collective-permute-start(bf16[240,128]{1,0:T(8,128)(2,1)S(1)} %get-tuple-element.37), channel_id=1, source_target_pairs={{0,4},{1,5},{2,6},{3,7},{4,8},{5,9},{6,10},{7,11},{8,12},{9,13},{1... | collective-permute-start | bytes 184328 | tf_op jit(solution)/shard_map/ppermute | solution.py:52
  6.8 2.5 %collective-permute-start.4 = (bf16[240,128]{1,0:T(8,128)(2,1)S(1)}, bf16[240,128]{1,0:T(8,128)(2,1)S(1)}, u32[]{:S(2)}, u32[]{:S(2)}) collective-permute-start(bf16[240,128]{1,0:T(8,128)(2,1)S(1)} %get-tuple-element.38), channel_id=1, source_target_pairs={{0,6},{1,7},{2,8},{3,9},{4,10},{5,11},{6,12},{7,13},{8,14},{9,15},... | collective-permute-start | bytes 184328 | tf_op jit(solution)/shard_map/ppermute | solution.py:52
  9.3 1.2 %collective-permute-start.3 = (bf16[240,128]{1,0:T(8,128)(2,1)S(1)}, bf16[240,128]{1,0:T(8,128)(2,1)S(1)}, u32[]{:S(2)}, u32[]{:S(2)}) collective-permute-start(bf16[240,128]{1,0:T(8,128)(2,1)S(1)} %get-tuple-element.39), channel_id=1, source_target_pairs={{0,8},{1,9},{2,10},{3,11},{4,12},{5,13},{6,14},{7,15},{8,0},{9,1},... | collective-permute-start | bytes 184328 | tf_op jit(solution)/shard_map/ppermute | solution.py:52
  10.6 2.6 %collective-permute-start.2 = (bf16[240,128]{1,0:T(8,128)(2,1)S(1)}, bf16[240,128]{1,0:T(8,128)(2,1)S(1)}, u32[]{:S(2)}, u32[]{:S(2)}) collective-permute-start(bf16[240,128]{1,0:T(8,128)(2,1)S(1)} %get-tuple-element.40), channel_id=1, source_target_pairs={{0,10},{1,11},{2,12},{3,13},{4,14},{5,15},{6,0},{7,1},{8,2},{9,3},... | collective-permute-start | bytes 184328 | tf_op jit(solution)/shard_map/ppermute | solution.py:52
  13.2 1.3 %collective-permute-start.1 = (bf16[240,128]{1,0:T(8,128)(2,1)S(1)}, bf16[240,128]{1,0:T(8,128)(2,1)S(1)}, u32[]{:S(2)}, u32[]{:S(2)}) collective-permute-start(bf16[240,128]{1,0:T(8,128)(2,1)S(1)} %get-tuple-element.41), channel_id=1, source_target_pairs={{0,12},{1,13},{2,14},{3,15},{4,0},{5,1},{6,2},{7,3},{8,4},{9,5},{1... | collective-permute-start | bytes 184328 | tf_op jit(solution)/shard_map/ppermute | solution.py:52
  14.6 1.5 %collective-permute-start = (bf16[240,128]{1,0:T(8,128)(2,1)S(1)}, bf16[240,128]{1,0:T(8,128)(2,1)S(1)}, u32[]{:S(2)}, u32[]{:S(2)}) collective-permute-start(bf16[240,128]{1,0:T(8,128)(2,1)S(1)} %get-tuple-element.42), channel_id=1, source_target_pairs={{0,14},{1,15},{2,0},{3,1},{4,2},{5,3},{6,4},{7,5},{8,6},{9,7},{10,... | collective-permute-start | bytes 184328 | tf_op jit(solution)/shard_map/ppermute | solution.py:52
  16.8 2.4 %preload.1.refs_12_ = bf16[1216,1920]{1,0:T(8,128)(2,1)S(1)} custom-call(s32[1]{0:T(128)} %bitcast.place_ref, bf16[1216,5120]{1,0:T(8,128)(2,1)} %head_ref.3, bf16[240,128]{1,0:T(8,128)(2,1)S(1)} %collective-permute-done.4._.refs_4_), custom_call_target="tpu_custom_call" | custom-call | bytes 9338880 | tf_op jit(solution)/shard_map/preload/pallas_call | solution.py:501
  20.9 8.2 %logits.1 = (bf16[192,1216]{1,0:T(8,128)(2,1)}, f32[16,8,128]{2,1,0:T(8,128)}, f32[8,128]{1,0:T(8,128)S(1)}) custom-call(s32[1]{0:T(128)} %bitcast.place_ref, bf16[240,128]{1,0:T(8,128)(2,1)S(1)} %collective-permute-done.refs_0_, bf16[240,128]{1,0:T(8,128)(2,1)S(1)} %collective-permute-done.1.refs_1_, bf16[240,128]{1,0:T(8,128)(2,1)S(1)} %collective-permute-done.2.refs_2_, ...), custom_call_target="tpu_custom_call" | custom-call | flops 796917760 | bytes 12451840 | tf_op jit(solution)/shard_map/logits/pallas_call | solution.py:516
  29.1 6.2 %all-to-all-start = ((f32[16,8,128]{2,1,0:T(8,128)}), f32[16,8,128]{2,1,0:T(8,128)S(1)}, u32[]{:S(2)}, u32[]{:S(2)}) async-start(f32[16,8,128]{2,1,0:T(8,128)} %get-tuple-element.22), calls=%async_computation | async-start | bytes 131072 | tf_op jit(solution)/shard_map/all_to_all | solution.py:541
  35.3 6.3 %products.1 = (f32[8,5,2,64,128]{4,3,2,1,0:T(8,128)S(1)}, bf16[8,5,64,128]{3,2,1,0:T(8,128)(2,1)S(1)}) custom-call(s32[1]{0:T(128)} %bitcast.place_ref, bf16[192,1216]{1,0:T(8,128)(2,1)} %get-tuple-element.24.rows_ref, bf16[1216,5120]{1,0:T(8,128)(2,1)} %head_ref.3), custom_call_target="tpu_custom_call" | custom-call | flops 2390753280 | bytes 12451840 | tf_op jit(solution)/shard_map/products/pallas_call | solution.py:543
  42.2 0.9 %give.1 = (bf16[8,160,128]{2,1,0:T(8,128)(2,1)S(1)}, f32[3,64,128]{2,1,0:T(8,128)S(1)}, f32[1,1]{1,0:T(1,128)}) custom-call(s32[1]{0:T(128)} %bitcast.place_ref, f32[1]{0:T(128)S(6)} %copy.14.scale_ref, f32[16,8,128]{2,1,0:T(8,128)S(1)} %all-to-all-done.stats_ref, f32[8,128]{1,0:T(8,128)S(1)} %get-tuple-element.23.own_ref, ...), custom_call_target="tpu_custom_call" | custom-call | tf_op jit(solution)/shard_map/give/pallas_call | solution.py:560
  43.1 1.3 %keep.1 = (f32[8,160,128]{2,1,0:T(8,128)S(1)}, f32[1,1]{1,0:T(1,128)}) custom-call(s32[1]{0:T(128)} %bitcast.place_ref, f32[3,64,128]{2,1,0:T(8,128)S(1)} %get-tuple-element.27.factors_ref, f32[1,1]{1,0:T(1,128)} %get-tuple-element.28.found_ref, f32[8,5,2,64,128]{4,3,2,1,0:T(8,128)S(1)} %get-tuple-element.25.terms_ref, ...), custom_call_target="tpu_custom_call" | custom-call | flops 2621440 | bytes 2621440 | tf_op jit(solution)/shard_map/keep/pallas_call | solution.py:573
  44.9 1.4 %collective-permute-start.10 = (bf16[160,128]{1,0:T(8,128)(2,1)S(1)}, bf16[160,128]{1,0:T(8,128)(2,1)S(1)}, u32[]{:S(2)}, u32[]{:S(2)}) collective-permute-start(bf16[160,128]{1,0:T(8,128)(2,1)S(1)} %get-tuple-element.49), channel_id=1, source_target_pairs={{0,2},{1,3},{2,4},{3,5},{4,6},{5,7},{6,8},{7,9},{8,10},{9,11},{10,... | collective-permute-start | bytes 122888 | tf_op jit(solution)/shard_map/ppermute | solution.py:52
  46.3 1.5 %collective-permute-start.11 = (bf16[160,128]{1,0:T(8,128)(2,1)S(1)}, bf16[160,128]{1,0:T(8,128)(2,1)S(1)}, u32[]{:S(2)}, u32[]{:S(2)}) collective-permute-start(bf16[160,128]{1,0:T(8,128)(2,1)S(1)} %get-tuple-element.48), channel_id=1, source_target_pairs={{0,4},{1,5},{2,6},{3,7},{4,8},{5,9},{6,10},{7,11},{8,12},{9,13},{1... | collective-permute-start | bytes 122888 | tf_op jit(solution)/shard_map/ppermute | solution.py:52
  47.7 2.4 %collective-permute-start.12 = (bf16[160,128]{1,0:T(8,128)(2,1)S(1)}, bf16[160,128]{1,0:T(8,128)(2,1)S(1)}, u32[]{:S(2)}, u32[]{:S(2)}) collective-permute-start(bf16[160,128]{1,0:T(8,128)(2,1)S(1)} %get-tuple-element.47), channel_id=1, source_target_pairs={{0,6},{1,7},{2,8},{3,9},{4,10},{5,11},{6,12},{7,13},{8,14},{9,15},... | collective-permute-start | bytes 122888 | tf_op jit(solution)/shard_map/ppermute | solution.py:52
  50.1 1.5 %collective-permute-start.13 = (bf16[160,128]{1,0:T(8,128)(2,1)S(1)}, bf16[160,128]{1,0:T(8,128)(2,1)S(1)}, u32[]{:S(2)}, u32[]{:S(2)}) collective-permute-start(bf16[160,128]{1,0:T(8,128)(2,1)S(1)} %get-tuple-element.46), channel_id=1, source_target_pairs={{0,8},{1,9},{2,10},{3,11},{4,12},{5,13},{6,14},{7,15},{8,0},{9,1},... | collective-permute-start | bytes 122888 | tf_op jit(solution)/shard_map/ppermute | solution.py:52
  51.5 2.4 %collective-permute-start.14 = (bf16[160,128]{1,0:T(8,128)(2,1)S(1)}, bf16[160,128]{1,0:T(8,128)(2,1)S(1)}, u32[]{:S(2)}, u32[]{:S(2)}) collective-permute-start(bf16[160,128]{1,0:T(8,128)(2,1)S(1)} %get-tuple-element.45), channel_id=1, source_target_pairs={{0,10},{1,11},{2,12},{3,13},{4,14},{5,15},{6,0},{7,1},{8,2},{9,3},... | collective-permute-start | bytes 122888 | tf_op jit(solution)/shard_map/ppermute | solution.py:52
  53.9 1.5 %collective-permute-start.15 = (bf16[160,128]{1,0:T(8,128)(2,1)S(1)}, bf16[160,128]{1,0:T(8,128)(2,1)S(1)}, u32[]{:S(2)}, u32[]{:S(2)}) collective-permute-start(bf16[160,128]{1,0:T(8,128)(2,1)S(1)} %get-tuple-element.44), channel_id=1, source_target_pairs={{0,12},{1,13},{2,14},{3,15},{4,0},{5,1},{6,2},{7,3},{8,4},{9,5},{1... | collective-permute-start | bytes 122888 | tf_op jit(solution)/shard_map/ppermute | solution.py:52
  55.4 1.5 %collective-permute-start.16 = (bf16[160,128]{1,0:T(8,128)(2,1)S(1)}, bf16[160,128]{1,0:T(8,128)(2,1)S(1)}, u32[]{:S(2)}, u32[]{:S(2)}) collective-permute-start(bf16[160,128]{1,0:T(8,128)(2,1)S(1)} %get-tuple-element.43), channel_id=1, source_target_pairs={{0,14},{1,15},{2,0},{3,1},{4,2},{5,3},{6,4},{7,5},{8,6},{9,7},{10,... | collective-permute-start | bytes 122888 | tf_op jit(solution)/shard_map/ppermute | solution.py:52
  57.0 1.1 %collective-permute-done.15.refs_5_ = bf16[160,128]{1,0:T(8,128)(2,1)S(1)} collective-permute-done((bf16[160,128]{1,0:T(8,128)(2,1)S(1)}, bf16[160,128]{1,0:T(8,128)(2,1)S(1)}, u32[]{:S(2)}, u32[]{:S(2)}) %collective-permute-start.15) | collective-permute-done | bytes 40992 | tf_op jit(solution)/shard_map/ppermute | solution.py:52
  58.0 1.4 %collective-permute-done.16.refs_6_ = bf16[160,128]{1,0:T(8,128)(2,1)S(1)} collective-permute-done((bf16[160,128]{1,0:T(8,128)(2,1)S(1)}, bf16[160,128]{1,0:T(8,128)(2,1)S(1)}, u32[]{:S(2)}, u32[]{:S(2)}) %collective-permute-start.16) | collective-permute-done | bytes 40992 | tf_op jit(solution)/shard_map/ppermute | solution.py:52
  59.4 0.8 %total.1 = bf16[64,320]{1,0:T(8,128)(2,1)} custom-call(s32[1]{0:T(128)} %bitcast.place_ref, f32[160,128]{1,0:T(8,128)S(1)} %slice_bitcast_fusion.own_ref, bf16[160,128]{1,0:T(8,128)(2,1)S(1)} %collective-permute-done.10.refs_0_, bf16[160,128]{1,0:T(8,128)(2,1)S(1)} %collective-permute-done.11.refs_1_, bf16[160,128]{1,0:T(8,128)(2,1)S(1)} %collective-permute-done.12.refs_2_, ...), custom_call_target="tpu_custom_call" | custom-call | tf_op jit(solution)/shard_map/total/pallas_call | solution.py:589
  (28 shorter events, 2.9 us)
Async XLA Ops:
  2.2 11.0 %collective-permute-start.6 = (bf16[240,128]{1,0:T(8,128)(2,1)S(1)}, bf16[240,128]{1,0:T(8,128)(2,1)S(1)}, u32[]{:S(2)}, u32[]{:S(2)}) collective-permute-start(bf16[240,128]{1,0:T(8,128)(2,1)S(1)} %get-tuple-element.36), channel_id=1, source_target_pairs={{0,2},{1,3},{2,4},{3,5},{4,6},{5,7},{6,8},{7,9},{8,10},{9,11},{10,... | collective-permute-start | bytes 184328 | tf_op jit(solution)/shard_map/ppermute | solution.py:52
  5.2 9.4 %collective-permute-start.5 = (bf16[240,128]{1,0:T(8,128)(2,1)S(1)}, bf16[240,128]{1,0:T(8,128)(2,1)S(1)}, u32[]{:S(2)}, u32[]{:S(2)}) collective-permute-start(bf16[240,128]{1,0:T(8,128)(2,1)S(1)} %get-tuple-element.37), channel_id=1, source_target_pairs={{0,4},{1,5},{2,6},{3,7},{4,8},{5,9},{6,10},{7,11},{8,12},{9,13},{1... | collective-permute-start | bytes 184328 | tf_op jit(solution)/shard_map/ppermute | solution.py:52
  6.8 9.4 %collective-permute-start.4 = (bf16[240,128]{1,0:T(8,128)(2,1)S(1)}, bf16[240,128]{1,0:T(8,128)(2,1)S(1)}, u32[]{:S(2)}, u32[]{:S(2)}) collective-permute-start(bf16[240,128]{1,0:T(8,128)(2,1)S(1)} %get-tuple-element.38), channel_id=1, source_target_pairs={{0,6},{1,7},{2,8},{3,9},{4,10},{5,11},{6,12},{7,13},{8,14},{9,15},... | collective-permute-start | bytes 184328 | tf_op jit(solution)/shard_map/ppermute | solution.py:52
  9.3 7.4 %collective-permute-start.3 = (bf16[240,128]{1,0:T(8,128)(2,1)S(1)}, bf16[240,128]{1,0:T(8,128)(2,1)S(1)}, u32[]{:S(2)}, u32[]{:S(2)}) collective-permute-start(bf16[240,128]{1,0:T(8,128)(2,1)S(1)} %get-tuple-element.39), channel_id=1, source_target_pairs={{0,8},{1,9},{2,10},{3,11},{4,12},{5,13},{6,14},{7,15},{8,0},{9,1},... | collective-permute-start | bytes 184328 | tf_op jit(solution)/shard_map/ppermute | solution.py:52
  10.6 8.7 %collective-permute-start.2 = (bf16[240,128]{1,0:T(8,128)(2,1)S(1)}, bf16[240,128]{1,0:T(8,128)(2,1)S(1)}, u32[]{:S(2)}, u32[]{:S(2)}) collective-permute-start(bf16[240,128]{1,0:T(8,128)(2,1)S(1)} %get-tuple-element.40), channel_id=1, source_target_pairs={{0,10},{1,11},{2,12},{3,13},{4,14},{5,15},{6,0},{7,1},{8,2},{9,3},... | collective-permute-start | bytes 184328 | tf_op jit(solution)/shard_map/ppermute | solution.py:52
  13.2 6.0 %collective-permute-start.1 = (bf16[240,128]{1,0:T(8,128)(2,1)S(1)}, bf16[240,128]{1,0:T(8,128)(2,1)S(1)}, u32[]{:S(2)}, u32[]{:S(2)}) collective-permute-start(bf16[240,128]{1,0:T(8,128)(2,1)S(1)} %get-tuple-element.41), channel_id=1, source_target_pairs={{0,12},{1,13},{2,14},{3,15},{4,0},{5,1},{6,2},{7,3},{8,4},{9,5},{1... | collective-permute-start | bytes 184328 | tf_op jit(solution)/shard_map/ppermute | solution.py:52
  14.6 4.7 %collective-permute-start = (bf16[240,128]{1,0:T(8,128)(2,1)S(1)}, bf16[240,128]{1,0:T(8,128)(2,1)S(1)}, u32[]{:S(2)}, u32[]{:S(2)}) collective-permute-start(bf16[240,128]{1,0:T(8,128)(2,1)S(1)} %get-tuple-element.42), channel_id=1, source_target_pairs={{0,14},{1,15},{2,0},{3,1},{4,2},{5,3},{6,4},{7,5},{8,6},{9,7},{10,... | collective-permute-start | bytes 184328 | tf_op jit(solution)/shard_map/ppermute | solution.py:52
  16.8 4.2 %collective-permute-start.8 = (bf16[5,240,128]{2,1,0:T(8,128)(2,1)S(1)}, bf16[5,240,128]{2,1,0:T(8,128)(2,1)S(1)}, u32[]{:S(2)}, u32[]{:S(2)}) collective-permute-start(bf16[5,240,128]{2,1,0:T(8,128)(2,1)S(1)} %bitcast_dynamic-update-slice_fusion), channel_id=1, source_target_pairs={{0,1},{1,0},{2,3},{3,2},{4,5},{5,4},{6,7},{7,6},{8,9},{9,8},{10,11... | collective-permute-start | bytes 921608 | tf_op jit(solution)/shard_map/ppermute | solution.py:47
  19.3 1.6 %collective-permute-start.7 = (bf16[3,240,128]{2,1,0:T(8,128)(2,1)S(1)}, bf16[3,240,128]{2,1,0:T(8,128)(2,1)S(1)}, u32[]{:S(2)}, u32[]{:S(2)}) collective-permute-start(bf16[3,240,128]{2,1,0:T(8,128)(2,1)S(1)} %pad_maximum_fusion), channel_id=1, source_target_pairs={{0,1},{1,0},{2,3},{3,2},{4,5},{5,4},{6,7},{7,6},{8,9},{9,8},{10,11... | collective-permute-start | bytes 552968 | tf_op jit(solution)/shard_map/ppermute | solution.py:47
  29.1 13.1 %all-to-all-start = ((f32[16,8,128]{2,1,0:T(8,128)}), f32[16,8,128]{2,1,0:T(8,128)S(1)}, u32[]{:S(2)}, u32[]{:S(2)}) async-start(f32[16,8,128]{2,1,0:T(8,128)} %get-tuple-element.22), calls=%async_computation | async-start | bytes 131072 | tf_op jit(solution)/shard_map/all_to_all | solution.py:541
  43.1 1.6 %collective-permute-start.9 = (bf16[8,160,128]{2,1,0:T(8,128)(2,1)S(1)}, bf16[8,160,128]{2,1,0:T(8,128)(2,1)S(1)}, u32[]{:S(2)}, u32[]{:S(2)}) collective-permute-start(bf16[8,160,128]{2,1,0:T(8,128)(2,1)S(1)} %get-tuple-element.30), channel_id=1, source_target_pairs={{0,1},{1,0},{2,3},{3,2},{4,5},{5,4},{6,7},{7,6},{8,9},{9,8},{10,11... | collective-permute-start | bytes 983048 | tf_op jit(solution)/shard_map/ppermute | solution.py:47
  44.9 9.0 %collective-permute-start.10 = (bf16[160,128]{1,0:T(8,128)(2,1)S(1)}, bf16[160,128]{1,0:T(8,128)(2,1)S(1)}, u32[]{:S(2)}, u32[]{:S(2)}) collective-permute-start(bf16[160,128]{1,0:T(8,128)(2,1)S(1)} %get-tuple-element.49), channel_id=1, source_target_pairs={{0,2},{1,3},{2,4},{3,5},{4,6},{5,7},{6,8},{7,9},{8,10},{9,11},{10,... | collective-permute-start | bytes 122888 | tf_op jit(solution)/shard_map/ppermute | solution.py:52
  46.3 9.1 %collective-permute-start.11 = (bf16[160,128]{1,0:T(8,128)(2,1)S(1)}, bf16[160,128]{1,0:T(8,128)(2,1)S(1)}, u32[]{:S(2)}, u32[]{:S(2)}) collective-permute-start(bf16[160,128]{1,0:T(8,128)(2,1)S(1)} %get-tuple-element.48), channel_id=1, source_target_pairs={{0,4},{1,5},{2,6},{3,7},{4,8},{5,9},{6,10},{7,11},{8,12},{9,13},{1... | collective-permute-start | bytes 122888 | tf_op jit(solution)/shard_map/ppermute | solution.py:52
  47.7 9.1 %collective-permute-start.12 = (bf16[160,128]{1,0:T(8,128)(2,1)S(1)}, bf16[160,128]{1,0:T(8,128)(2,1)S(1)}, u32[]{:S(2)}, u32[]{:S(2)}) collective-permute-start(bf16[160,128]{1,0:T(8,128)(2,1)S(1)} %get-tuple-element.47), channel_id=1, source_target_pairs={{0,6},{1,7},{2,8},{3,9},{4,10},{5,11},{6,12},{7,13},{8,14},{9,15},... | collective-permute-start | bytes 122888 | tf_op jit(solution)/shard_map/ppermute | solution.py:52
  50.1 6.8 %collective-permute-start.13 = (bf16[160,128]{1,0:T(8,128)(2,1)S(1)}, bf16[160,128]{1,0:T(8,128)(2,1)S(1)}, u32[]{:S(2)}, u32[]{:S(2)}) collective-permute-start(bf16[160,128]{1,0:T(8,128)(2,1)S(1)} %get-tuple-element.46), channel_id=1, source_target_pairs={{0,8},{1,9},{2,10},{3,11},{4,12},{5,13},{6,14},{7,15},{8,0},{9,1},... | collective-permute-start | bytes 122888 | tf_op jit(solution)/shard_map/ppermute | solution.py:52
  51.5 5.4 %collective-permute-start.14 = (bf16[160,128]{1,0:T(8,128)(2,1)S(1)}, bf16[160,128]{1,0:T(8,128)(2,1)S(1)}, u32[]{:S(2)}, u32[]{:S(2)}) collective-permute-start(bf16[160,128]{1,0:T(8,128)(2,1)S(1)} %get-tuple-element.45), channel_id=1, source_target_pairs={{0,10},{1,11},{2,12},{3,13},{4,14},{5,15},{6,0},{7,1},{8,2},{9,3},... | collective-permute-start | bytes 122888 | tf_op jit(solution)/shard_map/ppermute | solution.py:52
  53.9 4.1 %collective-permute-start.15 = (bf16[160,128]{1,0:T(8,128)(2,1)S(1)}, bf16[160,128]{1,0:T(8,128)(2,1)S(1)}, u32[]{:S(2)}, u32[]{:S(2)}) collective-permute-start(bf16[160,128]{1,0:T(8,128)(2,1)S(1)} %get-tuple-element.44), channel_id=1, source_target_pairs={{0,12},{1,13},{2,14},{3,15},{4,0},{5,1},{6,2},{7,3},{8,4},{9,5},{1... | collective-permute-start | bytes 122888 | tf_op jit(solution)/shard_map/ppermute | solution.py:52
  55.4 4.0 %collective-permute-start.16 = (bf16[160,128]{1,0:T(8,128)(2,1)S(1)}, bf16[160,128]{1,0:T(8,128)(2,1)S(1)}, u32[]{:S(2)}, u32[]{:S(2)}) collective-permute-start(bf16[160,128]{1,0:T(8,128)(2,1)S(1)} %get-tuple-element.43), channel_id=1, source_target_pairs={{0,14},{1,15},{2,0},{3,1},{4,2},{5,3},{6,4},{7,5},{8,6},{9,7},{10,... | collective-permute-start | bytes 122888 | tf_op jit(solution)/shard_map/ppermute | solution.py:52

commit v18 on v17

--- a/solution.py
+++ b/solution.py
@@ -308,10 +308,12 @@
     teacher_off = teacher - teacher_top
     teacher_total = jnp.sum(jnp.exp(teacher_off), axis=1, keepdims=True)
     teacher_ref[...] = teacher_off
-    for step in range(len(copies)):
-        take(copies, step)
-        columns = held_ref[:, width * step : width * (step + 1)]
-        logits += product(EARLY + step, columns)
+    for group in (range(AHEAD), range(AHEAD, len(copies))):
+        for step in group:
+            take(copies, step)
+        for step in group:
+            columns = held_ref[:, width * step : width * (step + 1)]
+            logits += product(EARLY + step, columns)
 
     top = jnp.max(logits, axis=1, keepdims=True)
     off = logits - top

time: 60.4 us -> 61.2 us (1.013)
  Pallas kernels: 21.4 us -> 22.3 us
    pallas_call x1, Pallas kernels: 8.15 us -> 8.99 us  [paired_shards(): pl.pallas_call(functools.partial(logits_kernel, chips=chips), out_shape=(...]
  transfers between devices with their start and end apart: 18 -> 18, of which waited for: 8 -> 8; matrix products, arithmetic and copies ran while one was open for 0% -> 0% of each run, Pallas kernels for 17% -> 16%
where the time goes in v18:
time: 61.2 us; the launch traced here: 61 us
  starting transfers between devices  32.6 us (53%)
  Pallas kernels  22.3 us (36%)
  waiting for transfers between devices  4.46 us (7%)
  between operations  1.43 us (2%)
    ppermute x14, starting transfers between devices, along_chips(): lax.ppermute(array, 'vocab', [(i, (i + 2 * step) % count) for i in range(...  25.8 us
    pallas_call x1, Pallas kernels, paired_shards(): pl.pallas_call(functools.partial(logits_kernel, chips=chips), out_shape=(...  8.99 us
    pallas_call x1, Pallas kernels, paired_shards(): pl.pallas_call(products_kernel, out_shape=(vmem_array((chips, width // LA...  6.31 us
    all_to_all x1, starting transfers between devices, paired_shards(): lax.all_to_all(stats, 'vocab', split_axis=0, concat_axis=0, tiled=True)  6.2 us
    ppermute x14, waiting for transfers between devices, along_chips(): lax.ppermute(array, 'vocab', [(i, (i + 2 * step) % count) for i in range(...  3.19 us
    pallas_call x1, Pallas kernels, paired_shards(): pl.pallas_call(functools.partial(preload_kernel, chips=chips), out_shape=...  2.4 us
    pallas_call x1, Pallas kernels, paired_shards(): pl.pallas_call(functools.partial(pack_kernel, shard_rows=shard_rows), out...  1.52 us
    pallas_call x1, Pallas kernels, paired_shards(): pl.pallas_call(keep_kernel, out_shape=(vmem_array((chips, hidden_rows, LA...  1.34 us
  transfers between devices with their start and end apart: 18, of which 8 were waited for; matrix products, arithmetic and copies ran while one was open for 0% of the time, Pallas kernels for 16%

profile of v18, /device:TPU:0, one launch (start us, length us, event | category | flops | bytes accessed | tf_op | source)
XLA Modules:
  0.0 61.0 jit_solution(18406671589234423708)
XLA Ops:
  0.6 1.5 %pack.1 = (bf16[8,240,128]{2,1,0:T(8,128)(2,1)S(1)}, bf16[128,128]{1,0:T(8,128)(2,1)S(1)}, f32[64,128]{1,0:T(8,128)S(1)}) custom-call(s32[1]{0:T(128)} %bitcast.place_ref, bf16[64,320]{1,0:T(8,128)(2,1)} %refs_0_.1, bf16[4,19456]{1,0:T(4,128)(2,1)} %refs_1_.1, f32[4,608]{1,0:T(4,128)} %refs_2_.1, s32[1,64]{1,0:T(1,128)} %bitcast.51, s32[1,64]{1,0:T(1,128)} %bitcast.52, ...), custom_call_target="tpu_custom_call" | custom-call | tf_op jit(solution)/shard_map/pack/pallas_call | solution.py:483
  2.2 3.0 %collective-permute-start.6 = (bf16[240,128]{1,0:T(8,128)(2,1)S(1)}, bf16[240,128]{1,0:T(8,128)(2,1)S(1)}, u32[]{:S(2)}, u32[]{:S(2)}) collective-permute-start(bf16[240,128]{1,0:T(8,128)(2,1)S(1)} %get-tuple-element.36), channel_id=1, source_target_pairs={{0,2},{1,3},{2,4},{3,5},{4,6},{5,7},{6,8},{7,9},{8,10},{9,11},{10,... | collective-permute-start | bytes 184328 | tf_op jit(solution)/shard_map/ppermute | solution.py:52
  5.2 1.6 %collective-permute-start.5 = (bf16[240,128]{1,0:T(8,128)(2,1)S(1)}, bf16[240,128]{1,0:T(8,128)(2,1)S(1)}, u32[]{:S(2)}, u32[]{:S(2)}) collective-permute-start(bf16[240,128]{1,0:T(8,128)(2,1)S(1)} %get-tuple-element.37), channel_id=1, source_target_pairs={{0,4},{1,5},{2,6},{3,7},{4,8},{5,9},{6,10},{7,11},{8,12},{9,13},{1... | collective-permute-start | bytes 184328 | tf_op jit(solution)/shard_map/ppermute | solution.py:52
  6.8 2.5 %collective-permute-start.4 = (bf16[240,128]{1,0:T(8,128)(2,1)S(1)}, bf16[240,128]{1,0:T(8,128)(2,1)S(1)}, u32[]{:S(2)}, u32[]{:S(2)}) collective-permute-start(bf16[240,128]{1,0:T(8,128)(2,1)S(1)} %get-tuple-element.38), channel_id=1, source_target_pairs={{0,6},{1,7},{2,8},{3,9},{4,10},{5,11},{6,12},{7,13},{8,14},{9,15},... | collective-permute-start | bytes 184328 | tf_op jit(solution)/shard_map/ppermute | solution.py:52
  9.3 1.2 %collective-permute-start.3 = (bf16[240,128]{1,0:T(8,128)(2,1)S(1)}, bf16[240,128]{1,0:T(8,128)(2,1)S(1)}, u32[]{:S(2)}, u32[]{:S(2)}) collective-permute-start(bf16[240,128]{1,0:T(8,128)(2,1)S(1)} %get-tuple-element.39), channel_id=1, source_target_pairs={{0,8},{1,9},{2,10},{3,11},{4,12},{5,13},{6,14},{7,15},{8,0},{9,1},... | collective-permute-start | bytes 184328 | tf_op jit(solution)/shard_map/ppermute | solution.py:52
  10.6 2.6 %collective-permute-start.2 = (bf16[240,128]{1,0:T(8,128)(2,1)S(1)}, bf16[240,128]{1,0:T(8,128)(2,1)S(1)}, u32[]{:S(2)}, u32[]{:S(2)}) collective-permute-start(bf16[240,128]{1,0:T(8,128)(2,1)S(1)} %get-tuple-element.40), channel_id=1, source_target_pairs={{0,10},{1,11},{2,12},{3,13},{4,14},{5,15},{6,0},{7,1},{8,2},{9,3},... | collective-permute-start | bytes 184328 | tf_op jit(solution)/shard_map/ppermute | solution.py:52
  13.2 1.3 %collective-permute-start.1 = (bf16[240,128]{1,0:T(8,128)(2,1)S(1)}, bf16[240,128]{1,0:T(8,128)(2,1)S(1)}, u32[]{:S(2)}, u32[]{:S(2)}) collective-permute-start(bf16[240,128]{1,0:T(8,128)(2,1)S(1)} %get-tuple-element.41), channel_id=1, source_target_pairs={{0,12},{1,13},{2,14},{3,15},{4,0},{5,1},{6,2},{7,3},{8,4},{9,5},{1... | collective-permute-start | bytes 184328 | tf_op jit(solution)/shard_map/ppermute | solution.py:52
  14.6 1.5 %collective-permute-start = (bf16[240,128]{1,0:T(8,128)(2,1)S(1)}, bf16[240,128]{1,0:T(8,128)(2,1)S(1)}, u32[]{:S(2)}, u32[]{:S(2)}) collective-permute-start(bf16[240,128]{1,0:T(8,128)(2,1)S(1)} %get-tuple-element.42), channel_id=1, source_target_pairs={{0,14},{1,15},{2,0},{3,1},{4,2},{5,3},{6,4},{7,5},{8,6},{9,7},{10,... | collective-permute-start | bytes 184328 | tf_op jit(solution)/shard_map/ppermute | solution.py:52
  16.8 2.4 %preload.1.refs_12_ = bf16[1216,1920]{1,0:T(8,128)(2,1)S(1)} custom-call(s32[1]{0:T(128)} %bitcast.place_ref, bf16[1216,5120]{1,0:T(8,128)(2,1)} %head_ref.3, bf16[240,128]{1,0:T(8,128)(2,1)S(1)} %collective-permute-done.4._.refs_4_), custom_call_target="tpu_custom_call" | custom-call | bytes 9338880 | tf_op jit(solution)/shard_map/preload/pallas_call | solution.py:503
  20.9 9.0 %logits.1 = (bf16[192,1216]{1,0:T(8,128)(2,1)}, f32[16,8,128]{2,1,0:T(8,128)}, f32[8,128]{1,0:T(8,128)S(1)}) custom-call(s32[1]{0:T(128)} %bitcast.place_ref, bf16[240,128]{1,0:T(8,128)(2,1)S(1)} %collective-permute-done.refs_0_, bf16[240,128]{1,0:T(8,128)(2,1)S(1)} %collective-permute-done.1.refs_1_, bf16[240,128]{1,0:T(8,128)(2,1)S(1)} %collective-permute-done.2.refs_2_, ...), custom_call_target="tpu_custom_call" | custom-call | flops 796917760 | bytes 12451840 | tf_op jit(solution)/shard_map/logits/pallas_call | solution.py:518
  29.9 6.2 %all-to-all-start = ((f32[16,8,128]{2,1,0:T(8,128)}), f32[16,8,128]{2,1,0:T(8,128)S(1)}, u32[]{:S(2)}, u32[]{:S(2)}) async-start(f32[16,8,128]{2,1,0:T(8,128)} %get-tuple-element.22), calls=%async_computation | async-start | bytes 131072 | tf_op jit(solution)/shard_map/all_to_all | solution.py:543
  36.1 6.3 %products.1 = (f32[8,5,2,64,128]{4,3,2,1,0:T(8,128)S(1)}, bf16[8,5,64,128]{3,2,1,0:T(8,128)(2,1)S(1)}) custom-call(s32[1]{0:T(128)} %bitcast.place_ref, bf16[192,1216]{1,0:T(8,128)(2,1)} %get-tuple-element.24.rows_ref, bf16[1216,5120]{1,0:T(8,128)(2,1)} %head_ref.3), custom_call_target="tpu_custom_call" | custom-call | flops 2390753280 | bytes 12451840 | tf_op jit(solution)/shard_map/products/pallas_call | solution.py:545
  43.0 0.9 %give.1 = (bf16[8,160,128]{2,1,0:T(8,128)(2,1)S(1)}, f32[3,64,128]{2,1,0:T(8,128)S(1)}, f32[1,1]{1,0:T(1,128)}) custom-call(s32[1]{0:T(128)} %bitcast.place_ref, f32[1]{0:T(128)S(6)} %copy.14.scale_ref, f32[16,8,128]{2,1,0:T(8,128)S(1)} %all-to-all-done.stats_ref, f32[8,128]{1,0:T(8,128)S(1)} %get-tuple-element.23.own_ref, ...), custom_call_target="tpu_custom_call" | custom-call | tf_op jit(solution)/shard_map/give/pallas_call | solution.py:562
  43.9 1.3 %keep.1 = (f32[8,160,128]{2,1,0:T(8,128)S(1)}, f32[1,1]{1,0:T(1,128)}) custom-call(s32[1]{0:T(128)} %bitcast.place_ref, f32[3,64,128]{2,1,0:T(8,128)S(1)} %get-tuple-element.27.factors_ref, f32[1,1]{1,0:T(1,128)} %get-tuple-element.28.found_ref, f32[8,5,2,64,128]{4,3,2,1,0:T(8,128)S(1)} %get-tuple-element.25.terms_ref, ...), custom_call_target="tpu_custom_call" | custom-call | flops 2621440 | bytes 2621440 | tf_op jit(solution)/shard_map/keep/pallas_call | solution.py:575
  45.7 1.4 %collective-permute-start.10 = (bf16[160,128]{1,0:T(8,128)(2,1)S(1)}, bf16[160,128]{1,0:T(8,128)(2,1)S(1)}, u32[]{:S(2)}, u32[]{:S(2)}) collective-permute-start(bf16[160,128]{1,0:T(8,128)(2,1)S(1)} %get-tuple-element.49), channel_id=1, source_target_pairs={{0,2},{1,3},{2,4},{3,5},{4,6},{5,7},{6,8},{7,9},{8,10},{9,11},{10,... | collective-permute-start | bytes 122888 | tf_op jit(solution)/shard_map/ppermute | solution.py:52
  47.1 1.5 %collective-permute-start.11 = (bf16[160,128]{1,0:T(8,128)(2,1)S(1)}, bf16[160,128]{1,0:T(8,128)(2,1)S(1)}, u32[]{:S(2)}, u32[]{:S(2)}) collective-permute-start(bf16[160,128]{1,0:T(8,128)(2,1)S(1)} %get-tuple-element.48), channel_id=1, source_target_pairs={{0,4},{1,5},{2,6},{3,7},{4,8},{5,9},{6,10},{7,11},{8,12},{9,13},{1... | collective-permute-start | bytes 122888 | tf_op jit(solution)/shard_map/ppermute | solution.py:52
  48.6 2.4 %collective-permute-start.12 = (bf16[160,128]{1,0:T(8,128)(2,1)S(1)}, bf16[160,128]{1,0:T(8,128)(2,1)S(1)}, u32[]{:S(2)}, u32[]{:S(2)}) collective-permute-start(bf16[160,128]{1,0:T(8,128)(2,1)S(1)} %get-tuple-element.47), channel_id=1, source_target_pairs={{0,6},{1,7},{2,8},{3,9},{4,10},{5,11},{6,12},{7,13},{8,14},{9,15},... | collective-permute-start | bytes 122888 | tf_op jit(solution)/shard_map/ppermute | solution.py:52
  50.9 1.5 %collective-permute-start.13 = (bf16[160,128]{1,0:T(8,128)(2,1)S(1)}, bf16[160,128]{1,0:T(8,128)(2,1)S(1)}, u32[]{:S(2)}, u32[]{:S(2)}) collective-permute-start(bf16[160,128]{1,0:T(8,128)(2,1)S(1)} %get-tuple-element.46), channel_id=1, source_target_pairs={{0,8},{1,9},{2,10},{3,11},{4,12},{5,13},{6,14},{7,15},{8,0},{9,1},... | collective-permute-start | bytes 122888 | tf_op jit(solution)/shard_map/ppermute | solution.py:52
  52.4 2.4 %collective-permute-start.14 = (bf16[160,128]{1,0:T(8,128)(2,1)S(1)}, bf16[160,128]{1,0:T(8,128)(2,1)S(1)}, u32[]{:S(2)}, u32[]{:S(2)}) collective-permute-start(bf16[160,128]{1,0:T(8,128)(2,1)S(1)} %get-tuple-element.45), channel_id=1, source_target_pairs={{0,10},{1,11},{2,12},{3,13},{4,14},{5,15},{6,0},{7,1},{8,2},{9,3},... | collective-permute-start | bytes 122888 | tf_op jit(solution)/shard_map/ppermute | solution.py:52
  54.7 1.5 %collective-permute-start.15 = (bf16[160,128]{1,0:T(8,128)(2,1)S(1)}, bf16[160,128]{1,0:T(8,128)(2,1)S(1)}, u32[]{:S(2)}, u32[]{:S(2)}) collective-permute-start(bf16[160,128]{1,0:T(8,128)(2,1)S(1)} %get-tuple-element.44), channel_id=1, source_target_pairs={{0,12},{1,13},{2,14},{3,15},{4,0},{5,1},{6,2},{7,3},{8,4},{9,5},{1... | collective-permute-start | bytes 122888 | tf_op jit(solution)/shard_map/ppermute | solution.py:52
  56.2 1.5 %collective-permute-start.16 = (bf16[160,128]{1,0:T(8,128)(2,1)S(1)}, bf16[160,128]{1,0:T(8,128)(2,1)S(1)}, u32[]{:S(2)}, u32[]{:S(2)}) collective-permute-start(bf16[160,128]{1,0:T(8,128)(2,1)S(1)} %get-tuple-element.43), channel_id=1, source_target_pairs={{0,14},{1,15},{2,0},{3,1},{4,2},{5,3},{6,4},{7,5},{8,6},{9,7},{10,... | collective-permute-start | bytes 122888 | tf_op jit(solution)/shard_map/ppermute | solution.py:52
  57.8 1.1 %collective-permute-done.15.refs_5_ = bf16[160,128]{1,0:T(8,128)(2,1)S(1)} collective-permute-done((bf16[160,128]{1,0:T(8,128)(2,1)S(1)}, bf16[160,128]{1,0:T(8,128)(2,1)S(1)}, u32[]{:S(2)}, u32[]{:S(2)}) %collective-permute-start.15) | collective-permute-done | bytes 40992 | tf_op jit(solution)/shard_map/ppermute | solution.py:52
  58.9 1.4 %collective-permute-done.16.refs_6_ = bf16[160,128]{1,0:T(8,128)(2,1)S(1)} collective-permute-done((bf16[160,128]{1,0:T(8,128)(2,1)S(1)}, bf16[160,128]{1,0:T(8,128)(2,1)S(1)}, u32[]{:S(2)}, u32[]{:S(2)}) %collective-permute-start.16) | collective-permute-done | bytes 40992 | tf_op jit(solution)/shard_map/ppermute | solution.py:52
  60.2 0.8 %total.1 = bf16[64,320]{1,0:T(8,128)(2,1)} custom-call(s32[1]{0:T(128)} %bitcast.place_ref, f32[160,128]{1,0:T(8,128)S(1)} %slice_bitcast_fusion.own_ref, bf16[160,128]{1,0:T(8,128)(2,1)S(1)} %collective-permute-done.10.refs_0_, bf16[160,128]{1,0:T(8,128)(2,1)S(1)} %collective-permute-done.11.refs_1_, bf16[160,128]{1,0:T(8,128)(2,1)S(1)} %collective-permute-done.12.refs_2_, ...), custom_call_target="tpu_custom_call" | custom-call | tf_op jit(solution)/shard_map/total/pallas_call | solution.py:591
  (28 shorter events, 2.9 us)
Async XLA Ops:
  2.2 11.0 %collective-permute-start.6 = (bf16[240,128]{1,0:T(8,128)(2,1)S(1)}, bf16[240,128]{1,0:T(8,128)(2,1)S(1)}, u32[]{:S(2)}, u32[]{:S(2)}) collective-permute-start(bf16[240,128]{1,0:T(8,128)(2,1)S(1)} %get-tuple-element.36), channel_id=1, source_target_pairs={{0,2},{1,3},{2,4},{3,5},{4,6},{5,7},{6,8},{7,9},{8,10},{9,11},{10,... | collective-permute-start | bytes 184328 | tf_op jit(solution)/shard_map/ppermute | solution.py:52
  5.2 9.4 %collective-permute-start.5 = (bf16[240,128]{1,0:T(8,128)(2,1)S(1)}, bf16[240,128]{1,0:T(8,128)(2,1)S(1)}, u32[]{:S(2)}, u32[]{:S(2)}) collective-permute-start(bf16[240,128]{1,0:T(8,128)(2,1)S(1)} %get-tuple-element.37), channel_id=1, source_target_pairs={{0,4},{1,5},{2,6},{3,7},{4,8},{5,9},{6,10},{7,11},{8,12},{9,13},{1... | collective-permute-start | bytes 184328 | tf_op jit(solution)/shard_map/ppermute | solution.py:52
  6.8 9.4 %collective-permute-start.4 = (bf16[240,128]{1,0:T(8,128)(2,1)S(1)}, bf16[240,128]{1,0:T(8,128)(2,1)S(1)}, u32[]{:S(2)}, u32[]{:S(2)}) collective-permute-start(bf16[240,128]{1,0:T(8,128)(2,1)S(1)} %get-tuple-element.38), channel_id=1, source_target_pairs={{0,6},{1,7},{2,8},{3,9},{4,10},{5,11},{6,12},{7,13},{8,14},{9,15},... | collective-permute-start | bytes 184328 | tf_op jit(solution)/shard_map/ppermute | solution.py:52
  9.3 7.4 %collective-permute-start.3 = (bf16[240,128]{1,0:T(8,128)(2,1)S(1)}, bf16[240,128]{1,0:T(8,128)(2,1)S(1)}, u32[]{:S(2)}, u32[]{:S(2)}) collective-permute-start(bf16[240,128]{1,0:T(8,128)(2,1)S(1)} %get-tuple-element.39), channel_id=1, source_target_pairs={{0,8},{1,9},{2,10},{3,11},{4,12},{5,13},{6,14},{7,15},{8,0},{9,1},... | collective-permute-start | bytes 184328 | tf_op jit(solution)/shard_map/ppermute | solution.py:52
  10.6 8.7 %collective-permute-start.2 = (bf16[240,128]{1,0:T(8,128)(2,1)S(1)}, bf16[240,128]{1,0:T(8,128)(2,1)S(1)}, u32[]{:S(2)}, u32[]{:S(2)}) collective-permute-start(bf16[240,128]{1,0:T(8,128)(2,1)S(1)} %get-tuple-element.40), channel_id=1, source_target_pairs={{0,10},{1,11},{2,12},{3,13},{4,14},{5,15},{6,0},{7,1},{8,2},{9,3},... | collective-permute-start | bytes 184328 | tf_op jit(solution)/shard_map/ppermute | solution.py:52
  13.2 6.0 %collective-permute-start.1 = (bf16[240,128]{1,0:T(8,128)(2,1)S(1)}, bf16[240,128]{1,0:T(8,128)(2,1)S(1)}, u32[]{:S(2)}, u32[]{:S(2)}) collective-permute-start(bf16[240,128]{1,0:T(8,128)(2,1)S(1)} %get-tuple-element.41), channel_id=1, source_target_pairs={{0,12},{1,13},{2,14},{3,15},{4,0},{5,1},{6,2},{7,3},{8,4},{9,5},{1... | collective-permute-start | bytes 184328 | tf_op jit(solution)/shard_map/ppermute | solution.py:52
  14.6 4.7 %collective-permute-start = (bf16[240,128]{1,0:T(8,128)(2,1)S(1)}, bf16[240,128]{1,0:T(8,128)(2,1)S(1)}, u32[]{:S(2)}, u32[]{:S(2)}) collective-permute-start(bf16[240,128]{1,0:T(8,128)(2,1)S(1)} %get-tuple-element.42), channel_id=1, source_target_pairs={{0,14},{1,15},{2,0},{3,1},{4,2},{5,3},{6,4},{7,5},{8,6},{9,7},{10,... | collective-permute-start | bytes 184328 | tf_op jit(solution)/shard_map/ppermute | solution.py:52
  16.8 4.2 %collective-permute-start.8 = (bf16[5,240,128]{2,1,0:T(8,128)(2,1)S(1)}, bf16[5,240,128]{2,1,0:T(8,128)(2,1)S(1)}, u32[]{:S(2)}, u32[]{:S(2)}) collective-permute-start(bf16[5,240,128]{2,1,0:T(8,128)(2,1)S(1)} %bitcast_dynamic-update-slice_fusion), channel_id=1, source_target_pairs={{0,1},{1,0},{2,3},{3,2},{4,5},{5,4},{6,7},{7,6},{8,9},{9,8},{10,11... | collective-permute-start | bytes 921608 | tf_op jit(solution)/shard_map/ppermute | solution.py:47
  19.3 1.6 %collective-permute-start.7 = (bf16[3,240,128]{2,1,0:T(8,128)(2,1)S(1)}, bf16[3,240,128]{2,1,0:T(8,128)(2,1)S(1)}, u32[]{:S(2)}, u32[]{:S(2)}) collective-permute-start(bf16[3,240,128]{2,1,0:T(8,128)(2,1)S(1)} %pad_maximum_fusion), channel_id=1, source_target_pairs={{0,1},{1,0},{2,3},{3,2},{4,5},{5,4},{6,7},{7,6},{8,9},{9,8},{10,11... | collective-permute-start | bytes 552968 | tf_op jit(solution)/shard_map/ppermute | solution.py:47
  29.9 13.1 %all-to-all-start = ((f32[16,8,128]{2,1,0:T(8,128)}), f32[16,8,128]{2,1,0:T(8,128)S(1)}, u32[]{:S(2)}, u32[]{:S(2)}) async-start(f32[16,8,128]{2,1,0:T(8,128)} %get-tuple-element.22), calls=%async_computation | async-start | bytes 131072 | tf_op jit(solution)/shard_map/all_to_all | solution.py:543
  43.9 1.6 %collective-permute-start.9 = (bf16[8,160,128]{2,1,0:T(8,128)(2,1)S(1)}, bf16[8,160,128]{2,1,0:T(8,128)(2,1)S(1)}, u32[]{:S(2)}, u32[]{:S(2)}) collective-permute-start(bf16[8,160,128]{2,1,0:T(8,128)(2,1)S(1)} %get-tuple-element.30), channel_id=1, source_target_pairs={{0,1},{1,0},{2,3},{3,2},{4,5},{5,4},{6,7},{7,6},{8,9},{9,8},{10,11... | collective-permute-start | bytes 983048 | tf_op jit(solution)/shard_map/ppermute | solution.py:47
  45.7 9.0 %collective-permute-start.10 = (bf16[160,128]{1,0:T(8,128)(2,1)S(1)}, bf16[160,128]{1,0:T(8,128)(2,1)S(1)}, u32[]{:S(2)}, u32[]{:S(2)}) collective-permute-start(bf16[160,128]{1,0:T(8,128)(2,1)S(1)} %get-tuple-element.49), channel_id=1, source_target_pairs={{0,2},{1,3},{2,4},{3,5},{4,6},{5,7},{6,8},{7,9},{8,10},{9,11},{10,... | collective-permute-start | bytes 122888 | tf_op jit(solution)/shard_map/ppermute | solution.py:52
  47.1 9.1 %collective-permute-start.11 = (bf16[160,128]{1,0:T(8,128)(2,1)S(1)}, bf16[160,128]{1,0:T(8,128)(2,1)S(1)}, u32[]{:S(2)}, u32[]{:S(2)}) collective-permute-start(bf16[160,128]{1,0:T(8,128)(2,1)S(1)} %get-tuple-element.48), channel_id=1, source_target_pairs={{0,4},{1,5},{2,6},{3,7},{4,8},{5,9},{6,10},{7,11},{8,12},{9,13},{1... | collective-permute-start | bytes 122888 | tf_op jit(solution)/shard_map/ppermute | solution.py:52
  48.6 9.1 %collective-permute-start.12 = (bf16[160,128]{1,0:T(8,128)(2,1)S(1)}, bf16[160,128]{1,0:T(8,128)(2,1)S(1)}, u32[]{:S(2)}, u32[]{:S(2)}) collective-permute-start(bf16[160,128]{1,0:T(8,128)(2,1)S(1)} %get-tuple-element.47), channel_id=1, source_target_pairs={{0,6},{1,7},{2,8},{3,9},{4,10},{5,11},{6,12},{7,13},{8,14},{9,15},... | collective-permute-start | bytes 122888 | tf_op jit(solution)/shard_map/ppermute | solution.py:52
  50.9 6.8 %collective-permute-start.13 = (bf16[160,128]{1,0:T(8,128)(2,1)S(1)}, bf16[160,128]{1,0:T(8,128)(2,1)S(1)}, u32[]{:S(2)}, u32[]{:S(2)}) collective-permute-start(bf16[160,128]{1,0:T(8,128)(2,1)S(1)} %get-tuple-element.46), channel_id=1, source_target_pairs={{0,8},{1,9},{2,10},{3,11},{4,12},{5,13},{6,14},{7,15},{8,0},{9,1},... | collective-permute-start | bytes 122888 | tf_op jit(solution)/shard_map/ppermute | solution.py:52
  52.4 5.4 %collective-permute-start.14 = (bf16[160,128]{1,0:T(8,128)(2,1)S(1)}, bf16[160,128]{1,0:T(8,128)(2,1)S(1)}, u32[]{:S(2)}, u32[]{:S(2)}) collective-permute-start(bf16[160,128]{1,0:T(8,128)(2,1)S(1)} %get-tuple-element.45), channel_id=1, source_target_pairs={{0,10},{1,11},{2,12},{3,13},{4,14},{5,15},{6,0},{7,1},{8,2},{9,3},... | collective-permute-start | bytes 122888 | tf_op jit(solution)/shard_map/ppermute | solution.py:52
  54.7 4.1 %collective-permute-start.15 = (bf16[160,128]{1,0:T(8,128)(2,1)S(1)}, bf16[160,128]{1,0:T(8,128)(2,1)S(1)}, u32[]{:S(2)}, u32[]{:S(2)}) collective-permute-start(bf16[160,128]{1,0:T(8,128)(2,1)S(1)} %get-tuple-element.44), channel_id=1, source_target_pairs={{0,12},{1,13},{2,14},{3,15},{4,0},{5,1},{6,2},{7,3},{8,4},{9,5},{1... | collective-permute-start | bytes 122888 | tf_op jit(solution)/shard_map/ppermute | solution.py:52
  56.2 4.0 %collective-permute-start.16 = (bf16[160,128]{1,0:T(8,128)(2,1)S(1)}, bf16[160,128]{1,0:T(8,128)(2,1)S(1)}, u32[]{:S(2)}, u32[]{:S(2)}) collective-permute-start(bf16[160,128]{1,0:T(8,128)(2,1)S(1)} %get-tuple-element.43), channel_id=1, source_target_pairs={{0,14},{1,15},{2,0},{3,1},{4,2},{5,3},{6,4},{7,5},{8,6},{9,7},{10,... | collective-permute-start | bytes 122888 | tf_op jit(solution)/shard_map/ppermute | solution.py:52

commit v19 on v17

--- a/solution.py
+++ b/solution.py
@@ -252,7 +252,7 @@
     core = place_ref[0] % 2
     sources = source_chips(place_ref, chips)
     copies = head_copies(head_ref, held_ref, sems, sources[EARLY:])
-    for copy in copies[:AHEAD]:
+    for copy in copies:
         copy.start()
     tokens, width = hidden_ref.shape[0], hidden_ref.shape[1] // chips
     shard_rows = head_ref.shape[0]
@@ -308,8 +308,9 @@
     teacher_off = teacher - teacher_top
     teacher_total = jnp.sum(jnp.exp(teacher_off), axis=1, keepdims=True)
     teacher_ref[...] = teacher_off
+    for copy in copies:
+        copy.wait()
     for step in range(len(copies)):
-        take(copies, step)
         columns = held_ref[:, width * step : width * (step + 1)]
         logits += product(EARLY + step, columns)
 

time: 60.4 us -> 62.1 us (1.028)
  Pallas kernels: 21.4 us -> 23.2 us
    pallas_call x1, Pallas kernels: 8.15 us -> 9.9 us  [paired_shards(): pl.pallas_call(functools.partial(logits_kernel, chips=chips), out_shape=(...]
  transfers between devices with their start and end apart: 18 -> 18, of which waited for: 8 -> 8; matrix products, arithmetic and copies ran while one was open for 0% -> 0% of each run, Pallas kernels for 17% -> 16%
where the time goes in v19:
time: 62.1 us; the launch traced here: 61.9 us
  starting transfers between devices  32.6 us (52%)
  Pallas kernels  23.2 us (37%)
  waiting for transfers between devices  4.47 us (7%)
  between operations  1.43 us (2%)
    ppermute x14, starting transfers between devices, along_chips(): lax.ppermute(array, 'vocab', [(i, (i + 2 * step) % count) for i in range(...  25.8 us
    pallas_call x1, Pallas kernels, paired_shards(): pl.pallas_call(functools.partial(logits_kernel, chips=chips), out_shape=(...  9.9 us
    pallas_call x1, Pallas kernels, paired_shards(): pl.pallas_call(products_kernel, out_shape=(vmem_array((chips, width // LA...  6.3 us
    all_to_all x1, starting transfers between devices, paired_shards(): lax.all_to_all(stats, 'vocab', split_axis=0, concat_axis=0, tiled=True)  6.2 us
    ppermute x14, waiting for transfers between devices, along_chips(): lax.ppermute(array, 'vocab', [(i, (i + 2 * step) % count) for i in range(...  3.19 us
    pallas_call x1, Pallas kernels, paired_shards(): pl.pallas_call(functools.partial(preload_kernel, chips=chips), out_shape=...  2.4 us
    pallas_call x1, Pallas kernels, paired_shards(): pl.pallas_call(functools.partial(pack_kernel, shard_rows=shard_rows), out...  1.52 us
    pallas_call x1, Pallas kernels, paired_shards(): pl.pallas_call(keep_kernel, out_shape=(vmem_array((chips, hidden_rows, LA...  1.34 us
  transfers between devices with their start and end apart: 18, of which 8 were waited for; matrix products, arithmetic and copies ran while one was open for 0% of the time, Pallas kernels for 16%

profile of v19, /device:TPU:0, one launch (start us, length us, event | category | flops | bytes accessed | tf_op | source)
XLA Modules:
  0.0 61.9 jit_solution(11303649608810231142)
XLA Ops:
  0.6 1.5 %pack.1 = (bf16[8,240,128]{2,1,0:T(8,128)(2,1)S(1)}, bf16[128,128]{1,0:T(8,128)(2,1)S(1)}, f32[64,128]{1,0:T(8,128)S(1)}) custom-call(s32[1]{0:T(128)} %bitcast.place_ref, bf16[64,320]{1,0:T(8,128)(2,1)} %refs_0_.1, bf16[4,19456]{1,0:T(4,128)(2,1)} %refs_1_.1, f32[4,608]{1,0:T(4,128)} %refs_2_.1, s32[1,64]{1,0:T(1,128)} %bitcast.51, s32[1,64]{1,0:T(1,128)} %bitcast.52, ...), custom_call_target="tpu_custom_call" | custom-call | tf_op jit(solution)/shard_map/pack/pallas_call | solution.py:482
  2.2 3.0 %collective-permute-start.6 = (bf16[240,128]{1,0:T(8,128)(2,1)S(1)}, bf16[240,128]{1,0:T(8,128)(2,1)S(1)}, u32[]{:S(2)}, u32[]{:S(2)}) collective-permute-start(bf16[240,128]{1,0:T(8,128)(2,1)S(1)} %get-tuple-element.36), channel_id=1, source_target_pairs={{0,2},{1,3},{2,4},{3,5},{4,6},{5,7},{6,8},{7,9},{8,10},{9,11},{10,... | collective-permute-start | bytes 184328 | tf_op jit(solution)/shard_map/ppermute | solution.py:52
  5.2 1.6 %collective-permute-start.5 = (bf16[240,128]{1,0:T(8,128)(2,1)S(1)}, bf16[240,128]{1,0:T(8,128)(2,1)S(1)}, u32[]{:S(2)}, u32[]{:S(2)}) collective-permute-start(bf16[240,128]{1,0:T(8,128)(2,1)S(1)} %get-tuple-element.37), channel_id=1, source_target_pairs={{0,4},{1,5},{2,6},{3,7},{4,8},{5,9},{6,10},{7,11},{8,12},{9,13},{1... | collective-permute-start | bytes 184328 | tf_op jit(solution)/shard_map/ppermute | solution.py:52
  6.8 2.5 %collective-permute-start.4 = (bf16[240,128]{1,0:T(8,128)(2,1)S(1)}, bf16[240,128]{1,0:T(8,128)(2,1)S(1)}, u32[]{:S(2)}, u32[]{:S(2)}) collective-permute-start(bf16[240,128]{1,0:T(8,128)(2,1)S(1)} %get-tuple-element.38), channel_id=1, source_target_pairs={{0,6},{1,7},{2,8},{3,9},{4,10},{5,11},{6,12},{7,13},{8,14},{9,15},... | collective-permute-start | bytes 184328 | tf_op jit(solution)/shard_map/ppermute | solution.py:52
  9.3 1.2 %collective-permute-start.3 = (bf16[240,128]{1,0:T(8,128)(2,1)S(1)}, bf16[240,128]{1,0:T(8,128)(2,1)S(1)}, u32[]{:S(2)}, u32[]{:S(2)}) collective-permute-start(bf16[240,128]{1,0:T(8,128)(2,1)S(1)} %get-tuple-element.39), channel_id=1, source_target_pairs={{0,8},{1,9},{2,10},{3,11},{4,12},{5,13},{6,14},{7,15},{8,0},{9,1},... | collective-permute-start | bytes 184328 | tf_op jit(solution)/shard_map/ppermute | solution.py:52
  10.6 2.6 %collective-permute-start.2 = (bf16[240,128]{1,0:T(8,128)(2,1)S(1)}, bf16[240,128]{1,0:T(8,128)(2,1)S(1)}, u32[]{:S(2)}, u32[]{:S(2)}) collective-permute-start(bf16[240,128]{1,0:T(8,128)(2,1)S(1)} %get-tuple-element.40), channel_id=1, source_target_pairs={{0,10},{1,11},{2,12},{3,13},{4,14},{5,15},{6,0},{7,1},{8,2},{9,3},... | collective-permute-start | bytes 184328 | tf_op jit(solution)/shard_map/ppermute | solution.py:52
  13.2 1.3 %collective-permute-start.1 = (bf16[240,128]{1,0:T(8,128)(2,1)S(1)}, bf16[240,128]{1,0:T(8,128)(2,1)S(1)}, u32[]{:S(2)}, u32[]{:S(2)}) collective-permute-start(bf16[240,128]{1,0:T(8,128)(2,1)S(1)} %get-tuple-element.41), channel_id=1, source_target_pairs={{0,12},{1,13},{2,14},{3,15},{4,0},{5,1},{6,2},{7,3},{8,4},{9,5},{1... | collective-permute-start | bytes 184328 | tf_op jit(solution)/shard_map/ppermute | solution.py:52
  14.6 1.5 %collective-permute-start = (bf16[240,128]{1,0:T(8,128)(2,1)S(1)}, bf16[240,128]{1,0:T(8,128)(2,1)S(1)}, u32[]{:S(2)}, u32[]{:S(2)}) collective-permute-start(bf16[240,128]{1,0:T(8,128)(2,1)S(1)} %get-tuple-element.42), channel_id=1, source_target_pairs={{0,14},{1,15},{2,0},{3,1},{4,2},{5,3},{6,4},{7,5},{8,6},{9,7},{10,... | collective-permute-start | bytes 184328 | tf_op jit(solution)/shard_map/ppermute | solution.py:52
  16.8 2.4 %preload.1.refs_12_ = bf16[1216,1920]{1,0:T(8,128)(2,1)S(1)} custom-call(s32[1]{0:T(128)} %bitcast.place_ref, bf16[1216,5120]{1,0:T(8,128)(2,1)} %head_ref.3, bf16[240,128]{1,0:T(8,128)(2,1)S(1)} %collective-permute-done.4._.refs_4_), custom_call_target="tpu_custom_call" | custom-call | bytes 9338880 | tf_op jit(solution)/shard_map/preload/pallas_call | solution.py:502
  20.9 9.9 %logits.1 = (bf16[192,1216]{1,0:T(8,128)(2,1)}, f32[16,8,128]{2,1,0:T(8,128)}, f32[8,128]{1,0:T(8,128)S(1)}) custom-call(s32[1]{0:T(128)} %bitcast.place_ref, bf16[240,128]{1,0:T(8,128)(2,1)S(1)} %collective-permute-done.refs_0_, bf16[240,128]{1,0:T(8,128)(2,1)S(1)} %collective-permute-done.1.refs_1_, bf16[240,128]{1,0:T(8,128)(2,1)S(1)} %collective-permute-done.2.refs_2_, ...), custom_call_target="tpu_custom_call" | custom-call | flops 796917760 | bytes 12451840 | tf_op jit(solution)/shard_map/logits/pallas_call | solution.py:517
  30.8 6.2 %all-to-all-start = ((f32[16,8,128]{2,1,0:T(8,128)}), f32[16,8,128]{2,1,0:T(8,128)S(1)}, u32[]{:S(2)}, u32[]{:S(2)}) async-start(f32[16,8,128]{2,1,0:T(8,128)} %get-tuple-element.22), calls=%async_computation | async-start | bytes 131072 | tf_op jit(solution)/shard_map/all_to_all | solution.py:542
  37.0 6.3 %products.1 = (f32[8,5,2,64,128]{4,3,2,1,0:T(8,128)S(1)}, bf16[8,5,64,128]{3,2,1,0:T(8,128)(2,1)S(1)}) custom-call(s32[1]{0:T(128)} %bitcast.place_ref, bf16[192,1216]{1,0:T(8,128)(2,1)} %get-tuple-element.24.rows_ref, bf16[1216,5120]{1,0:T(8,128)(2,1)} %head_ref.3), custom_call_target="tpu_custom_call" | custom-call | flops 2390753280 | bytes 12451840 | tf_op jit(solution)/shard_map/products/pallas_call | solution.py:544
  43.9 0.9 %give.1 = (bf16[8,160,128]{2,1,0:T(8,128)(2,1)S(1)}, f32[3,64,128]{2,1,0:T(8,128)S(1)}, f32[1,1]{1,0:T(1,128)}) custom-call(s32[1]{0:T(128)} %bitcast.place_ref, f32[1]{0:T(128)S(6)} %copy.14.scale_ref, f32[16,8,128]{2,1,0:T(8,128)S(1)} %all-to-all-done.stats_ref, f32[8,128]{1,0:T(8,128)S(1)} %get-tuple-element.23.own_ref, ...), custom_call_target="tpu_custom_call" | custom-call | tf_op jit(solution)/shard_map/give/pallas_call | solution.py:561
  44.9 1.3 %keep.1 = (f32[8,160,128]{2,1,0:T(8,128)S(1)}, f32[1,1]{1,0:T(1,128)}) custom-call(s32[1]{0:T(128)} %bitcast.place_ref, f32[3,64,128]{2,1,0:T(8,128)S(1)} %get-tuple-element.27.factors_ref, f32[1,1]{1,0:T(1,128)} %get-tuple-element.28.found_ref, f32[8,5,2,64,128]{4,3,2,1,0:T(8,128)S(1)} %get-tuple-element.25.terms_ref, ...), custom_call_target="tpu_custom_call" | custom-call | flops 2621440 | bytes 2621440 | tf_op jit(solution)/shard_map/keep/pallas_call | solution.py:574
  46.6 1.4 %collective-permute-start.10 = (bf16[160,128]{1,0:T(8,128)(2,1)S(1)}, bf16[160,128]{1,0:T(8,128)(2,1)S(1)}, u32[]{:S(2)}, u32[]{:S(2)}) collective-permute-start(bf16[160,128]{1,0:T(8,128)(2,1)S(1)} %get-tuple-element.49), channel_id=1, source_target_pairs={{0,2},{1,3},{2,4},{3,5},{4,6},{5,7},{6,8},{7,9},{8,10},{9,11},{10,... | collective-permute-start | bytes 122888 | tf_op jit(solution)/shard_map/ppermute | solution.py:52
  48.0 1.5 %collective-permute-start.11 = (bf16[160,128]{1,0:T(8,128)(2,1)S(1)}, bf16[160,128]{1,0:T(8,128)(2,1)S(1)}, u32[]{:S(2)}, u32[]{:S(2)}) collective-permute-start(bf16[160,128]{1,0:T(8,128)(2,1)S(1)} %get-tuple-element.48), channel_id=1, source_target_pairs={{0,4},{1,5},{2,6},{3,7},{4,8},{5,9},{6,10},{7,11},{8,12},{9,13},{1... | collective-permute-start | bytes 122888 | tf_op jit(solution)/shard_map/ppermute | solution.py:52
  49.5 2.4 %collective-permute-start.12 = (bf16[160,128]{1,0:T(8,128)(2,1)S(1)}, bf16[160,128]{1,0:T(8,128)(2,1)S(1)}, u32[]{:S(2)}, u32[]{:S(2)}) collective-permute-start(bf16[160,128]{1,0:T(8,128)(2,1)S(1)} %get-tuple-element.47), channel_id=1, source_target_pairs={{0,6},{1,7},{2,8},{3,9},{4,10},{5,11},{6,12},{7,13},{8,14},{9,15},... | collective-permute-start | bytes 122888 | tf_op jit(solution)/shard_map/ppermute | solution.py:52
  51.8 1.5 %collective-permute-start.13 = (bf16[160,128]{1,0:T(8,128)(2,1)S(1)}, bf16[160,128]{1,0:T(8,128)(2,1)S(1)}, u32[]{:S(2)}, u32[]{:S(2)}) collective-permute-start(bf16[160,128]{1,0:T(8,128)(2,1)S(1)} %get-tuple-element.46), channel_id=1, source_target_pairs={{0,8},{1,9},{2,10},{3,11},{4,12},{5,13},{6,14},{7,15},{8,0},{9,1},... | collective-permute-start | bytes 122888 | tf_op jit(solution)/shard_map/ppermute | solution.py:52
  53.3 2.4 %collective-permute-start.14 = (bf16[160,128]{1,0:T(8,128)(2,1)S(1)}, bf16[160,128]{1,0:T(8,128)(2,1)S(1)}, u32[]{:S(2)}, u32[]{:S(2)}) collective-permute-start(bf16[160,128]{1,0:T(8,128)(2,1)S(1)} %get-tuple-element.45), channel_id=1, source_target_pairs={{0,10},{1,11},{2,12},{3,13},{4,14},{5,15},{6,0},{7,1},{8,2},{9,3},... | collective-permute-start | bytes 122888 | tf_op jit(solution)/shard_map/ppermute | solution.py:52
  55.7 1.5 %collective-permute-start.15 = (bf16[160,128]{1,0:T(8,128)(2,1)S(1)}, bf16[160,128]{1,0:T(8,128)(2,1)S(1)}, u32[]{:S(2)}, u32[]{:S(2)}) collective-permute-start(bf16[160,128]{1,0:T(8,128)(2,1)S(1)} %get-tuple-element.44), channel_id=1, source_target_pairs={{0,12},{1,13},{2,14},{3,15},{4,0},{5,1},{6,2},{7,3},{8,4},{9,5},{1... | collective-permute-start | bytes 122888 | tf_op jit(solution)/shard_map/ppermute | solution.py:52
  57.1 1.5 %collective-permute-start.16 = (bf16[160,128]{1,0:T(8,128)(2,1)S(1)}, bf16[160,128]{1,0:T(8,128)(2,1)S(1)}, u32[]{:S(2)}, u32[]{:S(2)}) collective-permute-start(bf16[160,128]{1,0:T(8,128)(2,1)S(1)} %get-tuple-element.43), channel_id=1, source_target_pairs={{0,14},{1,15},{2,0},{3,1},{4,2},{5,3},{6,4},{7,5},{8,6},{9,7},{10,... | collective-permute-start | bytes 122888 | tf_op jit(solution)/shard_map/ppermute | solution.py:52
  58.7 1.1 %collective-permute-done.15.refs_5_ = bf16[160,128]{1,0:T(8,128)(2,1)S(1)} collective-permute-done((bf16[160,128]{1,0:T(8,128)(2,1)S(1)}, bf16[160,128]{1,0:T(8,128)(2,1)S(1)}, u32[]{:S(2)}, u32[]{:S(2)}) %collective-permute-start.15) | collective-permute-done | bytes 40992 | tf_op jit(solution)/shard_map/ppermute | solution.py:52
  59.8 1.4 %collective-permute-done.16.refs_6_ = bf16[160,128]{1,0:T(8,128)(2,1)S(1)} collective-permute-done((bf16[160,128]{1,0:T(8,128)(2,1)S(1)}, bf16[160,128]{1,0:T(8,128)(2,1)S(1)}, u32[]{:S(2)}, u32[]{:S(2)}) %collective-permute-start.16) | collective-permute-done | bytes 40992 | tf_op jit(solution)/shard_map/ppermute | solution.py:52
  61.1 0.8 %total.1 = bf16[64,320]{1,0:T(8,128)(2,1)} custom-call(s32[1]{0:T(128)} %bitcast.place_ref, f32[160,128]{1,0:T(8,128)S(1)} %slice_bitcast_fusion.own_ref, bf16[160,128]{1,0:T(8,128)(2,1)S(1)} %collective-permute-done.10.refs_0_, bf16[160,128]{1,0:T(8,128)(2,1)S(1)} %collective-permute-done.11.refs_1_, bf16[160,128]{1,0:T(8,128)(2,1)S(1)} %collective-permute-done.12.refs_2_, ...), custom_call_target="tpu_custom_call" | custom-call | tf_op jit(solution)/shard_map/total/pallas_call | solution.py:590
  (28 shorter events, 2.9 us)
Async XLA Ops:
  2.2 11.0 %collective-permute-start.6 = (bf16[240,128]{1,0:T(8,128)(2,1)S(1)}, bf16[240,128]{1,0:T(8,128)(2,1)S(1)}, u32[]{:S(2)}, u32[]{:S(2)}) collective-permute-start(bf16[240,128]{1,0:T(8,128)(2,1)S(1)} %get-tuple-element.36), channel_id=1, source_target_pairs={{0,2},{1,3},{2,4},{3,5},{4,6},{5,7},{6,8},{7,9},{8,10},{9,11},{10,... | collective-permute-start | bytes 184328 | tf_op jit(solution)/shard_map/ppermute | solution.py:52
  5.2 9.4 %collective-permute-start.5 = (bf16[240,128]{1,0:T(8,128)(2,1)S(1)}, bf16[240,128]{1,0:T(8,128)(2,1)S(1)}, u32[]{:S(2)}, u32[]{:S(2)}) collective-permute-start(bf16[240,128]{1,0:T(8,128)(2,1)S(1)} %get-tuple-element.37), channel_id=1, source_target_pairs={{0,4},{1,5},{2,6},{3,7},{4,8},{5,9},{6,10},{7,11},{8,12},{9,13},{1... | collective-permute-start | bytes 184328 | tf_op jit(solution)/shard_map/ppermute | solution.py:52
  6.8 9.4 %collective-permute-start.4 = (bf16[240,128]{1,0:T(8,128)(2,1)S(1)}, bf16[240,128]{1,0:T(8,128)(2,1)S(1)}, u32[]{:S(2)}, u32[]{:S(2)}) collective-permute-start(bf16[240,128]{1,0:T(8,128)(2,1)S(1)} %get-tuple-element.38), channel_id=1, source_target_pairs={{0,6},{1,7},{2,8},{3,9},{4,10},{5,11},{6,12},{7,13},{8,14},{9,15},... | collective-permute-start | bytes 184328 | tf_op jit(solution)/shard_map/ppermute | solution.py:52
  9.3 7.4 %collective-permute-start.3 = (bf16[240,128]{1,0:T(8,128)(2,1)S(1)}, bf16[240,128]{1,0:T(8,128)(2,1)S(1)}, u32[]{:S(2)}, u32[]{:S(2)}) collective-permute-start(bf16[240,128]{1,0:T(8,128)(2,1)S(1)} %get-tuple-element.39), channel_id=1, source_target_pairs={{0,8},{1,9},{2,10},{3,11},{4,12},{5,13},{6,14},{7,15},{8,0},{9,1},... | collective-permute-start | bytes 184328 | tf_op jit(solution)/shard_map/ppermute | solution.py:52
  10.6 8.7 %collective-permute-start.2 = (bf16[240,128]{1,0:T(8,128)(2,1)S(1)}, bf16[240,128]{1,0:T(8,128)(2,1)S(1)}, u32[]{:S(2)}, u32[]{:S(2)}) collective-permute-start(bf16[240,128]{1,0:T(8,128)(2,1)S(1)} %get-tuple-element.40), channel_id=1, source_target_pairs={{0,10},{1,11},{2,12},{3,13},{4,14},{5,15},{6,0},{7,1},{8,2},{9,3},... | collective-permute-start | bytes 184328 | tf_op jit(solution)/shard_map/ppermute | solution.py:52
  13.2 6.0 %collective-permute-start.1 = (bf16[240,128]{1,0:T(8,128)(2,1)S(1)}, bf16[240,128]{1,0:T(8,128)(2,1)S(1)}, u32[]{:S(2)}, u32[]{:S(2)}) collective-permute-start(bf16[240,128]{1,0:T(8,128)(2,1)S(1)} %get-tuple-element.41), channel_id=1, source_target_pairs={{0,12},{1,13},{2,14},{3,15},{4,0},{5,1},{6,2},{7,3},{8,4},{9,5},{1... | collective-permute-start | bytes 184328 | tf_op jit(solution)/shard_map/ppermute | solution.py:52
  14.6 4.7 %collective-permute-start = (bf16[240,128]{1,0:T(8,128)(2,1)S(1)}, bf16[240,128]{1,0:T(8,128)(2,1)S(1)}, u32[]{:S(2)}, u32[]{:S(2)}) collective-permute-start(bf16[240,128]{1,0:T(8,128)(2,1)S(1)} %get-tuple-element.42), channel_id=1, source_target_pairs={{0,14},{1,15},{2,0},{3,1},{4,2},{5,3},{6,4},{7,5},{8,6},{9,7},{10,... | collective-permute-start | bytes 184328 | tf_op jit(solution)/shard_map/ppermute | solution.py:52
  16.8 4.2 %collective-permute-start.8 = (bf16[5,240,128]{2,1,0:T(8,128)(2,1)S(1)}, bf16[5,240,128]{2,1,0:T(8,128)(2,1)S(1)}, u32[]{:S(2)}, u32[]{:S(2)}) collective-permute-start(bf16[5,240,128]{2,1,0:T(8,128)(2,1)S(1)} %bitcast_dynamic-update-slice_fusion), channel_id=1, source_target_pairs={{0,1},{1,0},{2,3},{3,2},{4,5},{5,4},{6,7},{7,6},{8,9},{9,8},{10,11... | collective-permute-start | bytes 921608 | tf_op jit(solution)/shard_map/ppermute | solution.py:47
  19.3 1.6 %collective-permute-start.7 = (bf16[3,240,128]{2,1,0:T(8,128)(2,1)S(1)}, bf16[3,240,128]{2,1,0:T(8,128)(2,1)S(1)}, u32[]{:S(2)}, u32[]{:S(2)}) collective-permute-start(bf16[3,240,128]{2,1,0:T(8,128)(2,1)S(1)} %pad_maximum_fusion), channel_id=1, source_target_pairs={{0,1},{1,0},{2,3},{3,2},{4,5},{5,4},{6,7},{7,6},{8,9},{9,8},{10,11... | collective-permute-start | bytes 552968 | tf_op jit(solution)/shard_map/ppermute | solution.py:47
  30.8 13.1 %all-to-all-start = ((f32[16,8,128]{2,1,0:T(8,128)}), f32[16,8,128]{2,1,0:T(8,128)S(1)}, u32[]{:S(2)}, u32[]{:S(2)}) async-start(f32[16,8,128]{2,1,0:T(8,128)} %get-tuple-element.22), calls=%async_computation | async-start | bytes 131072 | tf_op jit(solution)/shard_map/all_to_all | solution.py:542
  44.9 1.6 %collective-permute-start.9 = (bf16[8,160,128]{2,1,0:T(8,128)(2,1)S(1)}, bf16[8,160,128]{2,1,0:T(8,128)(2,1)S(1)}, u32[]{:S(2)}, u32[]{:S(2)}) collective-permute-start(bf16[8,160,128]{2,1,0:T(8,128)(2,1)S(1)} %get-tuple-element.30), channel_id=1, source_target_pairs={{0,1},{1,0},{2,3},{3,2},{4,5},{5,4},{6,7},{7,6},{8,9},{9,8},{10,11... | collective-permute-start | bytes 983048 | tf_op jit(solution)/shard_map/ppermute | solution.py:47
  46.6 9.0 %collective-permute-start.10 = (bf16[160,128]{1,0:T(8,128)(2,1)S(1)}, bf16[160,128]{1,0:T(8,128)(2,1)S(1)}, u32[]{:S(2)}, u32[]{:S(2)}) collective-permute-start(bf16[160,128]{1,0:T(8,128)(2,1)S(1)} %get-tuple-element.49), channel_id=1, source_target_pairs={{0,2},{1,3},{2,4},{3,5},{4,6},{5,7},{6,8},{7,9},{8,10},{9,11},{10,... | collective-permute-start | bytes 122888 | tf_op jit(solution)/shard_map/ppermute | solution.py:52
  48.0 9.1 %collective-permute-start.11 = (bf16[160,128]{1,0:T(8,128)(2,1)S(1)}, bf16[160,128]{1,0:T(8,128)(2,1)S(1)}, u32[]{:S(2)}, u32[]{:S(2)}) collective-permute-start(bf16[160,128]{1,0:T(8,128)(2,1)S(1)} %get-tuple-element.48), channel_id=1, source_target_pairs={{0,4},{1,5},{2,6},{3,7},{4,8},{5,9},{6,10},{7,11},{8,12},{9,13},{1... | collective-permute-start | bytes 122888 | tf_op jit(solution)/shard_map/ppermute | solution.py:52
  49.5 9.1 %collective-permute-start.12 = (bf16[160,128]{1,0:T(8,128)(2,1)S(1)}, bf16[160,128]{1,0:T(8,128)(2,1)S(1)}, u32[]{:S(2)}, u32[]{:S(2)}) collective-permute-start(bf16[160,128]{1,0:T(8,128)(2,1)S(1)} %get-tuple-element.47), channel_id=1, source_target_pairs={{0,6},{1,7},{2,8},{3,9},{4,10},{5,11},{6,12},{7,13},{8,14},{9,15},... | collective-permute-start | bytes 122888 | tf_op jit(solution)/shard_map/ppermute | solution.py:52
  51.8 6.8 %collective-permute-start.13 = (bf16[160,128]{1,0:T(8,128)(2,1)S(1)}, bf16[160,128]{1,0:T(8,128)(2,1)S(1)}, u32[]{:S(2)}, u32[]{:S(2)}) collective-permute-start(bf16[160,128]{1,0:T(8,128)(2,1)S(1)} %get-tuple-element.46), channel_id=1, source_target_pairs={{0,8},{1,9},{2,10},{3,11},{4,12},{5,13},{6,14},{7,15},{8,0},{9,1},... | collective-permute-start | bytes 122888 | tf_op jit(solution)/shard_map/ppermute | solution.py:52
  53.3 5.4 %collective-permute-start.14 = (bf16[160,128]{1,0:T(8,128)(2,1)S(1)}, bf16[160,128]{1,0:T(8,128)(2,1)S(1)}, u32[]{:S(2)}, u32[]{:S(2)}) collective-permute-start(bf16[160,128]{1,0:T(8,128)(2,1)S(1)} %get-tuple-element.45), channel_id=1, source_target_pairs={{0,10},{1,11},{2,12},{3,13},{4,14},{5,15},{6,0},{7,1},{8,2},{9,3},... | collective-permute-start | bytes 122888 | tf_op jit(solution)/shard_map/ppermute | solution.py:52
  55.7 4.1 %collective-permute-start.15 = (bf16[160,128]{1,0:T(8,128)(2,1)S(1)}, bf16[160,128]{1,0:T(8,128)(2,1)S(1)}, u32[]{:S(2)}, u32[]{:S(2)}) collective-permute-start(bf16[160,128]{1,0:T(8,128)(2,1)S(1)} %get-tuple-element.44), channel_id=1, source_target_pairs={{0,12},{1,13},{2,14},{3,15},{4,0},{5,1},{6,2},{7,3},{8,4},{9,5},{1... | collective-permute-start | bytes 122888 | tf_op jit(solution)/shard_map/ppermute | solution.py:52
  57.1 4.0 %collective-permute-start.16 = (bf16[160,128]{1,0:T(8,128)(2,1)S(1)}, bf16[160,128]{1,0:T(8,128)(2,1)S(1)}, u32[]{:S(2)}, u32[]{:S(2)}) collective-permute-start(bf16[160,128]{1,0:T(8,128)(2,1)S(1)} %get-tuple-element.43), channel_id=1, source_target_pairs={{0,14},{1,15},{2,0},{3,1},{4,2},{5,3},{6,4},{7,5},{8,6},{9,7},{10,... | collective-permute-start | bytes 122888 | tf_op jit(solution)/shard_map/ppermute | solution.py:52

commit v20 on v16

--- a/solution.py
+++ b/solution.py
@@ -211,90 +211,118 @@
         packed_ref[step, hidden_rows:] = jnp.concatenate(rows, axis=0).astype(jnp.bfloat16)
 
 
-def head_copies(head_ref, held_ref, sems, chips):
-    width = held_ref.shape[1] // len(chips)
-    copies = []
-    for step, chip in enumerate(chips):
-        columns = pl.ds(pl.multiple_of(chip * width, LANES), width)
-        copies.append(
-            pltpu.make_async_copy(
-                head_ref.at[:, columns],
-                held_ref.at[:, width * step : width * (step + 1)],
-                sems.at[step],
-            )
-        )
-    return copies
-
-
-def take(copies, step):
-    copies[step].wait()
-    if step + AHEAD < len(copies):
-        copies[step + AHEAD].start()
-
-
-def source_chips(place_ref, chips):
-    return [lax.rem(place_ref[0] // 2 - step + chips, chips) for step in range(chips)]
+def head_copy(head_ref, held_ref, sems, chip, step):
+    width = held_ref.shape[2]
+    columns = pl.ds(pl.multiple_of(chip * width, LANES), width)
+    return pltpu.make_async_copy(head_ref.at[:, columns], held_ref.at[step], sems.at[step])
+
+
+def stream(chip_at, count, head_ref, held_ref, sems, use):
+    def copy(step):
+        return head_copy(head_ref, held_ref, sems, chip_at(step), step)
+
+    def body(step, _):
+        copy(step).wait()
+
+        @pl.when(step + AHEAD < count)
+        def _():
+            copy(step + AHEAD).start()
+
+        use(step)
+
+    for step in range(min(AHEAD, count)):
+        copy(step).start()
+    return lambda: lax.fori_loop(0, count, body, None)
+
+
+def source_chip(place_ref, chips, step):
+    return lax.rem(place_ref[0] // 2 - step + chips, chips)
 
 
 def preload_kernel(place_ref, head_ref, _, early_ref, sems, *, chips):
-    sources = source_chips(place_ref, chips)[:EARLY]
-    copies = head_copies(head_ref, early_ref, sems, sources)
+    copies = [
+        head_copy(head_ref, early_ref, sems, source_chip(place_ref, chips, step), step)
+        for step in range(EARLY)
+    ]
     for copy in copies:
         copy.start()
     for copy in copies:
         copy.wait()
 
 
-def logits_kernel(place_ref, *refs, chips):
-    near, far, refs = refs[:chips][::-1], refs[chips : chips + 2], refs[chips + 2 :]
-    owner_ref, tokens_ref, early_ref, head_ref, rows_ref, stats_ref, own_ref = refs[:7]
-    held_ref, made_ref, hidden_ref, arrived_ref, teacher_ref, sems, made_sem = refs[7:]
+def logits_kernel(
+    place_ref,
+    first_ref,
+    last_ref,
+    first_far_ref,
+    last_far_ref,
+    owner_ref,
+    tokens_ref,
+    early_ref,
+    head_ref,
+    rows_ref,
+    stats_ref,
+    own_ref,
+    held_ref,
+    made_ref,
+    hidden_ref,
+    arrived_ref,
+    teacher_ref,
+    logits_ref,
+    sems,
+    made_sem,
+):
     core = place_ref[0] % 2
-    sources = source_chips(place_ref, chips)
-    copies = head_copies(head_ref, held_ref, sems, sources[EARLY:])
-    for copy in copies[:AHEAD]:
-        copy.start()
-    tokens, width = hidden_ref.shape[0], hidden_ref.shape[1] // chips
+    chips, tokens, width = hidden_ref.shape
     shard_rows = head_ref.shape[0]
     hidden_rows = 5 * tokens // 2
     slots = tokens // (2 * chips)
     low = low_lanes((tokens // 2, LANES))
 
-    for step in range(chips):
-        late = step > chips // 2
-        group = far[0] if late else far[1]
-        place = step - chips // 2 - 1 if late else step
-        blocks = near[step], group.at[place]
-        base = width * step
-        for block, parity in zip(blocks, (core, 1 - core)):
-            for i in range(2):
-                column = base + LANES * i + (width - 2 * LANES) * parity
-                lanes = pl.ds(pl.multiple_of(column, LANES), LANES)
-                hidden_ref[:, lanes] = block[tokens * i : tokens * (i + 1)]
-            teacher = block[hidden_rows:].astype(jnp.float32)
-            share = teacher.shape[0] // 2
-            teacher = jnp.where(core == 0, teacher[:share], teacher[share:])
-            row = 2 * slots * (2 * sources[step] + parity)
-            rows = pl.ds(pl.multiple_of(row, 2 * slots), 2 * slots)
-            for i in range(share // (2 * slots)):
-                arrived_ref[rows, LANES * i : LANES * (i + 1)] = teacher[
-                    2 * slots * i : 2 * slots * (i + 1)
-                ]
-        own, other = [block[2 * tokens : hidden_rows].astype(jnp.float32) for block in blocks]
-        one, two = jnp.where(core == 0, own, other), jnp.where(core == 0, other, own)
-        tile = [jnp.where(low, one, two), turned(jnp.where(low, two, one))]
-        tile = jnp.concatenate(tile, axis=0).astype(jnp.bfloat16)
-        hidden_ref[:, base + 2 * LANES : base + 3 * LANES] = tile
-
-    def product(step, count, columns):
-        return lax.dot_general(
-            hidden_ref[:, width * step : width * (step + count)],
-            columns,
-            (((1,), (1,)), ((), ())),
-            preferred_element_type=jnp.float32,
+    def add(step, columns):
+        logits_ref[...] += lax.dot_general(
+            hidden_ref[step], columns, (((1,), (1,)), ((), ())), preferred_element_type=jnp.float32
         )
 
-    logits = product(0, EARLY, early_ref[...])
+    run = stream(
+        lambda step: source_chip(place_ref, chips, step + EARLY),
+        chips - EARLY,
+        head_ref,
+        held_ref,
+        sems,
+        lambda step: add(step + EARLY, held_ref[step]),
+    )
+
+    def unpack(near_ref, far_ref, base):
+        def body(place, _):
+            step = place + base
+            blocks = near_ref.at[place], far_ref.at[place]
+            for block, parity in zip(blocks, (core, 1 - core)):
+                for i in range(2):
+                    column = LANES * i + (width - 2 * LANES) * parity
+                    lanes = pl.ds(pl.multiple_of(column, LANES), LANES)
+                    hidden_ref[step, :, lanes] = block[tokens * i : tokens * (i + 1)]
+                teacher = block[hidden_rows:].astype(jnp.float32)
+                share = teacher.shape[0] // 2
+                teacher = jnp.where(core == 0, teacher[:share], teacher[share:])
+                row = 2 * slots * (2 * source_chip(place_ref, chips, step) + parity)
+                rows = pl.ds(pl.multiple_of(row, 2 * slots), 2 * slots)
+                for i in range(share // (2 * slots)):
+                    arrived_ref[rows, LANES * i : LANES * (i + 1)] = teacher[
+                        2 * slots * i : 2 * slots * (i + 1)
+                    ]
+            own, other = [block[2 * tokens : hidden_rows].astype(jnp.float32) for block in blocks]
+            one, two = jnp.where(core == 0, own, other), jnp.where(core == 0, other, own)
+            tile = [jnp.where(low, one, two), turned(jnp.where(low, two, one))]
+            tile = jnp.concatenate(tile, axis=0).astype(jnp.bfloat16)
+            hidden_ref[step, :, 2 * LANES : 3 * LANES] = tile
+
+        lax.fori_loop(0, near_ref.shape[0], body, None)
+
+    unpack(first_ref, first_far_ref, 0)
+    unpack(last_ref, last_far_ref, first_ref.shape[0])
+    logits_ref[...] = jnp.zeros_like(logits_ref)
+    lax.fori_loop(0, EARLY, lambda step, _: add(step, early_ref[step]), None)
     placed = jnp.dot(
         owner_ref[...], arrived_ref[...].astype(jnp.bfloat16), preferred_element_type=jnp.float32
     )
@@ -306,10 +334,8 @@
     teacher_off = teacher - teacher_top
     teacher_total = jnp.sum(jnp.exp(teacher_off), axis=1, keepdims=True)
     teacher_ref[...] = teacher_off
-    for step in range(len(copies)):
-        take(copies, step)
-        columns = held_ref[:, width * step : width * (step + 1)]
-        logits += product(EARLY + step, 1, columns)
+    run()
+    logits = logits_ref[...]
 
     top = jnp.max(logits, axis=1, keepdims=True)
     off = logits - top
@@ -346,36 +372,41 @@
     into = pltpu.make_async_copy(rows_ref, made_ref, made_sem)
     into.start()
     chips = terms_ref.shape[0]
-    targets = [lax.rem(place_ref[0] // 2 + step, chips) for step in range(chips)]
-    copies = head_copies(head_ref, held_ref, sems, targets)
-    for copy in copies[:AHEAD]:
-        copy.start()
-    into.wait()
     tokens = made_ref.shape[0] // 3
-    width = held_ref.shape[1] // chips
-    for step in range(chips):
-        take(copies, step)
-        products = jnp.dot(
-            made_ref[...],
-            held_ref[:, width * step : width * (step + 1)],
-            preferred_element_type=jnp.float32,
-        )
+    width = held_ref.shape[2]
+
+    def multiply(step):
+        products = jnp.dot(made_ref[...], held_ref[step], preferred_element_type=jnp.float32)
         for i, tile in enumerate(tiles_of(products, width // LANES)):
             terms_ref[step, i, 0] = tile[:tokens]
             terms_ref[step, i, 1] = tile[tokens : 2 * tokens]
             picks_ref[step, i] = tile[2 * tokens :].astype(jnp.bfloat16)
 
+    run = stream(
+        lambda step: lax.rem(place_ref[0] // 2 + step, chips),
+        chips,
+        head_ref,
+        held_ref,
+        sems,
+        multiply,
+    )
+    into.wait()
+    run()
+
 
 def put_shares(parity, factors_ref, terms_ref, picks_ref, out_ref):
     tokens = terms_ref.shape[3]
     factor, level, weight = [factors_ref[i] for i in range(3)]
-    for step in range(terms_ref.shape[0]):
+
+    def put(step, _):
         for i, tile in enumerate((3 * parity, 3 * parity + 1, 2)):
             sums = terms_ref[step, tile, 0] + level * terms_ref[step, tile, 1]
             share = factor * sums - weight * picks_ref[step, tile].astype(jnp.float32)
             if i == 2:
                 share = folded(parity == 0, share)
             out_ref[step, tokens * i : tokens * i + share.shape[0]] = share.astype(out_ref.dtype)
+
+    lax.fori_loop(0, terms_ref.shape[0], put, None)
 
 
 def give_kernel(
@@ -460,7 +491,7 @@
     hbm = pl.BlockSpec(memory_space=pl.ANY)
     params = pltpu.CompilerParams(vmem_limit_bytes=VMEM_LIMIT)
     head = in_hbm(head)
-    head_scratch = pltpu.VMEM((shard_rows, chips * width), head.dtype)
+    head_scratch = pltpu.VMEM((chips, shard_rows, width), head.dtype)
     head_sems = pltpu.SemaphoreType.DMA((chips,))
     rows_scratch = pltpu.VMEM((3 * tokens, shard_rows), jnp.bfloat16)
     rows_sem = pltpu.SemaphoreType.DMA
@@ -498,7 +529,7 @@
     first, last = jnp.stack(near[: chips // 2 + 1]), jnp.stack(near[chips // 2 + 1 :])
     early = pl.pallas_call(
         functools.partial(preload_kernel, chips=chips),
-        out_shape=vmem_array((shard_rows, EARLY * width), head.dtype),
+        out_shape=vmem_array((EARLY, shard_rows, width), head.dtype),
         in_specs=[smem] + [hbm] * 2,
         out_specs=vmem,
         scratch_shapes=[pltpu.SemaphoreType.DMA((EARLY,))],
@@ -512,19 +543,20 @@
     far = [swap_cores(last), swap_cores(first)]
 
     rows, stats, own_stats = pl.pallas_call(
-        functools.partial(logits_kernel, chips=chips),
+        logits_kernel,
         out_shape=(
             hbm_array((3 * tokens, shard_rows), jnp.bfloat16),
             jax.ShapeDtypeStruct((count, STATS, pl.cdiv(tokens, LANES) * LANES), jnp.float32),
             vmem_array((STATS, pl.cdiv(tokens, LANES) * LANES), jnp.float32),
         ),
-        in_specs=[smem] + [vmem] * (chips + 5) + [hbm],
+        in_specs=[smem] + [vmem] * 7 + [hbm],
         out_specs=[hbm, vmem, vmem],
         scratch_shapes=[
-            pltpu.VMEM((shard_rows, (chips - EARLY) * width), head.dtype),
+            pltpu.VMEM((chips - EARLY, shard_rows, width), head.dtype),
             rows_scratch,
-            pltpu.VMEM((tokens, chips * width), jnp.bfloat16),
+            pltpu.VMEM((chips, tokens, width), jnp.bfloat16),
             pltpu.VMEM((2 * tokens, (shard_rows + LANES // 2) // 2), jnp.float32),
+            pltpu.VMEM((tokens, shard_rows), jnp.float32),
             pltpu.VMEM((tokens, shard_rows), jnp.float32),
             pltpu.SemaphoreType.DMA((chips - EARLY,)),
             rows_sem,
@@ -534,7 +566,14 @@
             flops=2 * tokens * head.size, bytes_accessed=2 * head.size, transcendentals=0
         ),
         name="logits",
-    )(place, *[in_vmem(block) for block in near[::-1] + far], in_vmem(owner), in_vmem(table), in_vmem(early), head)
+    )(
+        place,
+        *[in_vmem(blocks) for blocks in (first, last, far[1], far[0])],
+        in_vmem(owner),
+        in_vmem(table),
+        in_vmem(early),
+        head,
+    )
 
     all_stats = lax.all_to_all(stats, "vocab", split_axis=0, concat_axis=0, tiled=True)
 

time: 60.5 us -> 60.6 us (level)
  transfers between devices with their start and end apart: 18 -> 18, of which waited for: 8 -> 7; matrix products, arithmetic and copies ran while one was open for 0% -> 0% of each run, Pallas kernels for 17% -> 17%
where the time goes in v20:
time: 60.6 us; the launch traced here: 60.4 us
  starting transfers between devices  32.6 us (54%)
  Pallas kernels  21.8 us (36%)
  waiting for transfers between devices  4.33 us (7%)
  between operations  1.43 us (2%)
    ppermute x14, starting transfers between devices, along_chips(): lax.ppermute(array, 'vocab', [(i, (i + 2 * step) % count) for i in range(...  25.8 us
    pallas_call x1, Pallas kernels, paired_shards(): pl.pallas_call(logits_kernel, out_shape=(hbm_array((3 * tokens, shard_row...  7.69 us
    all_to_all x1, starting transfers between devices, paired_shards(): lax.all_to_all(stats, 'vocab', split_axis=0, concat_axis=0, tiled=True)  6.21 us
    pallas_call x1, Pallas kernels, paired_shards(): pl.pallas_call(products_kernel, out_shape=(vmem_array((chips, width // LA...  6.17 us
    ppermute x14, waiting for transfers between devices, along_chips(): lax.ppermute(array, 'vocab', [(i, (i + 2 * step) % count) for i in range(...  3.2 us
    pallas_call x1, Pallas kernels, paired_shards(): pl.pallas_call(functools.partial(preload_kernel, chips=chips), out_shape=...  2.4 us
    pallas_call x1, Pallas kernels, paired_shards(): pl.pallas_call(keep_kernel, out_shape=(vmem_array((chips, hidden_rows, LA...  1.81 us
    pallas_call x1, Pallas kernels, paired_shards(): pl.pallas_call(functools.partial(pack_kernel, shard_rows=shard_rows), out...  1.52 us
  transfers between devices with their start and end apart: 18, of which 7 were waited for; matrix products, arithmetic and copies ran while one was open for 0% of the time, Pallas kernels for 17%

profile of v20, /device:TPU:0, one launch (start us, length us, event | category | flops | bytes accessed | tf_op | source)
XLA Modules:
  0.0 60.4 jit_solution(17745703627007321058)
XLA Ops:
  0.6 1.5 %pack.1 = (bf16[8,240,128]{2,1,0:T(8,128)(2,1)S(1)}, bf16[128,128]{1,0:T(8,128)(2,1)S(1)}, f32[64,128]{1,0:T(8,128)S(1)}) custom-call(s32[1]{0:T(128)} %bitcast.place_ref, bf16[64,320]{1,0:T(8,128)(2,1)} %refs_0_.1, bf16[4,19456]{1,0:T(4,128)(2,1)} %refs_1_.1, f32[4,608]{1,0:T(4,128)} %refs_2_.1, s32[1,64]{1,0:T(1,128)} %bitcast.49, s32[1,64]{1,0:T(1,128)} %bitcast.50, ...), custom_call_target="tpu_custom_call" | custom-call | tf_op jit(solution)/shard_map/pack/pallas_call | solution.py:510
  2.2 3.0 %collective-permute-start = (bf16[240,128]{1,0:T(8,128)(2,1)S(1)}, bf16[240,128]{1,0:T(8,128)(2,1)S(1)}, u32[]{:S(2)}, u32[]{:S(2)}) collective-permute-start(bf16[240,128]{1,0:T(8,128)(2,1)S(1)} %get-tuple-element.40), channel_id=1, source_target_pairs={{0,2},{1,3},{2,4},{3,5},{4,6},{5,7},{6,8},{7,9},{8,10},{9,11},{10,... | collective-permute-start | bytes 184328 | tf_op jit(solution)/shard_map/ppermute | solution.py:52
  5.2 1.6 %collective-permute-start.1 = (bf16[240,128]{1,0:T(8,128)(2,1)S(1)}, bf16[240,128]{1,0:T(8,128)(2,1)S(1)}, u32[]{:S(2)}, u32[]{:S(2)}) collective-permute-start(bf16[240,128]{1,0:T(8,128)(2,1)S(1)} %get-tuple-element.39), channel_id=1, source_target_pairs={{0,4},{1,5},{2,6},{3,7},{4,8},{5,9},{6,10},{7,11},{8,12},{9,13},{1... | collective-permute-start | bytes 184328 | tf_op jit(solution)/shard_map/ppermute | solution.py:52
  6.8 2.5 %collective-permute-start.2 = (bf16[240,128]{1,0:T(8,128)(2,1)S(1)}, bf16[240,128]{1,0:T(8,128)(2,1)S(1)}, u32[]{:S(2)}, u32[]{:S(2)}) collective-permute-start(bf16[240,128]{1,0:T(8,128)(2,1)S(1)} %get-tuple-element.38), channel_id=1, source_target_pairs={{0,6},{1,7},{2,8},{3,9},{4,10},{5,11},{6,12},{7,13},{8,14},{9,15},... | collective-permute-start | bytes 184328 | tf_op jit(solution)/shard_map/ppermute | solution.py:52
  9.3 1.2 %collective-permute-start.3 = (bf16[240,128]{1,0:T(8,128)(2,1)S(1)}, bf16[240,128]{1,0:T(8,128)(2,1)S(1)}, u32[]{:S(2)}, u32[]{:S(2)}) collective-permute-start(bf16[240,128]{1,0:T(8,128)(2,1)S(1)} %get-tuple-element.37), channel_id=1, source_target_pairs={{0,8},{1,9},{2,10},{3,11},{4,12},{5,13},{6,14},{7,15},{8,0},{9,1},... | collective-permute-start | bytes 184328 | tf_op jit(solution)/shard_map/ppermute | solution.py:52
  10.6 2.6 %collective-permute-start.4 = (bf16[240,128]{1,0:T(8,128)(2,1)S(1)}, bf16[240,128]{1,0:T(8,128)(2,1)S(1)}, u32[]{:S(2)}, u32[]{:S(2)}) collective-permute-start(bf16[240,128]{1,0:T(8,128)(2,1)S(1)} %get-tuple-element.34), channel_id=1, source_target_pairs={{0,10},{1,11},{2,12},{3,13},{4,14},{5,15},{6,0},{7,1},{8,2},{9,3},... | collective-permute-start | bytes 184328 | tf_op jit(solution)/shard_map/ppermute | solution.py:52
  13.2 1.3 %collective-permute-start.5 = (bf16[240,128]{1,0:T(8,128)(2,1)S(1)}, bf16[240,128]{1,0:T(8,128)(2,1)S(1)}, u32[]{:S(2)}, u32[]{:S(2)}) collective-permute-start(bf16[240,128]{1,0:T(8,128)(2,1)S(1)} %get-tuple-element.36), channel_id=1, source_target_pairs={{0,12},{1,13},{2,14},{3,15},{4,0},{5,1},{6,2},{7,3},{8,4},{9,5},{1... | collective-permute-start | bytes 184328 | tf_op jit(solution)/shard_map/ppermute | solution.py:52
  14.6 1.5 %collective-permute-start.6 = (bf16[240,128]{1,0:T(8,128)(2,1)S(1)}, bf16[240,128]{1,0:T(8,128)(2,1)S(1)}, u32[]{:S(2)}, u32[]{:S(2)}) collective-permute-start(bf16[240,128]{1,0:T(8,128)(2,1)S(1)} %get-tuple-element.35), channel_id=1, source_target_pairs={{0,14},{1,15},{2,0},{3,1},{4,2},{5,3},{6,4},{7,5},{8,6},{9,7},{10,... | collective-permute-start | bytes 184328 | tf_op jit(solution)/shard_map/ppermute | solution.py:52
  16.8 2.4 %preload.1.early_ref = bf16[3,1216,640]{2,1,0:T(8,128)(2,1)S(1)} custom-call(s32[1]{0:T(128)} %bitcast.place_ref, bf16[1216,5120]{1,0:T(8,128)(2,1)} %head_ref.5, bf16[240,128]{1,0:T(8,128)(2,1)S(1)} %collective-permute-done.2._), custom_call_target="tpu_custom_call" | custom-call | bytes 9338880 | tf_op jit(solution)/shard_map/preload/pallas_call | solution.py:530
  20.9 7.7 %logits.1 = (bf16[192,1216]{1,0:T(8,128)(2,1)}, f32[16,8,128]{2,1,0:T(8,128)}, f32[8,128]{1,0:T(8,128)S(1)}) custom-call(s32[1]{0:T(128)} %bitcast.place_ref, bf16[5,240,128]{2,1,0:T(8,128)(2,1)S(1)} %bitcast_dynamic-update-slice_fusion.first_ref, bf16[3,240,128]{2,1,0:T(8,128)(2,1)S(1)} %pad_maximum_fusion.last_ref, ...), custom_call_target="tpu_custom_call" | custom-call | flops 796917760 | bytes 12451840 | tf_op jit(solution)/shard_map/logits/pallas_call | solution.py:545
  28.6 6.2 %all-to-all-start = ((f32[16,8,128]{2,1,0:T(8,128)}), f32[16,8,128]{2,1,0:T(8,128)S(1)}, u32[]{:S(2)}, u32[]{:S(2)}) async-start(f32[16,8,128]{2,1,0:T(8,128)} %get-tuple-element.22), calls=%async_computation | async-start | bytes 131072 | tf_op jit(solution)/shard_map/all_to_all | solution.py:578
  34.8 6.2 %products.1 = (f32[8,5,2,64,128]{4,3,2,1,0:T(8,128)S(1)}, bf16[8,5,64,128]{3,2,1,0:T(8,128)(2,1)S(1)}) custom-call(s32[1]{0:T(128)} %bitcast.place_ref, bf16[192,1216]{1,0:T(8,128)(2,1)} %get-tuple-element.24.rows_ref, bf16[1216,5120]{1,0:T(8,128)(2,1)} %head_ref.5), custom_call_target="tpu_custom_call" | custom-call | flops 2390753280 | bytes 12451840 | tf_op jit(solution)/shard_map/products/pallas_call | solution.py:580
  41.7 1.4 %give.1 = (bf16[8,160,128]{2,1,0:T(8,128)(2,1)S(1)}, f32[3,64,128]{2,1,0:T(8,128)S(1)}, f32[1,1]{1,0:T(1,128)}) custom-call(s32[1]{0:T(128)} %bitcast.place_ref, f32[1]{0:T(128)S(6)} %copy.14.scale_ref, f32[16,8,128]{2,1,0:T(8,128)S(1)} %all-to-all-done.stats_ref, f32[8,128]{1,0:T(8,128)S(1)} %get-tuple-element.23.own_ref, ...), custom_call_target="tpu_custom_call" | custom-call | tf_op jit(solution)/shard_map/give/pallas_call | solution.py:597
  43.1 1.8 %keep.1 = (f32[8,160,128]{2,1,0:T(8,128)S(1)}, f32[1,1]{1,0:T(1,128)}) custom-call(s32[1]{0:T(128)} %bitcast.place_ref, f32[3,64,128]{2,1,0:T(8,128)S(1)} %get-tuple-element.27.factors_ref, f32[1,1]{1,0:T(1,128)} %get-tuple-element.28.found_ref, f32[8,5,2,64,128]{4,3,2,1,0:T(8,128)S(1)} %get-tuple-element.25.terms_ref, ...), custom_call_target="tpu_custom_call" | custom-call | flops 2621440 | bytes 2621440 | tf_op jit(solution)/shard_map/keep/pallas_call | solution.py:610
  45.1 1.4 %collective-permute-start.10 = (bf16[160,128]{1,0:T(8,128)(2,1)S(1)}, bf16[160,128]{1,0:T(8,128)(2,1)S(1)}, u32[]{:S(2)}, u32[]{:S(2)}) collective-permute-start(bf16[160,128]{1,0:T(8,128)(2,1)S(1)} %get-tuple-element.48), channel_id=1, source_target_pairs={{0,2},{1,3},{2,4},{3,5},{4,6},{5,7},{6,8},{7,9},{8,10},{9,11},{10,... | collective-permute-start | bytes 122888 | tf_op jit(solution)/shard_map/ppermute | solution.py:52
  46.5 1.5 %collective-permute-start.11 = (bf16[160,128]{1,0:T(8,128)(2,1)S(1)}, bf16[160,128]{1,0:T(8,128)(2,1)S(1)}, u32[]{:S(2)}, u32[]{:S(2)}) collective-permute-start(bf16[160,128]{1,0:T(8,128)(2,1)S(1)} %get-tuple-element.47), channel_id=1, source_target_pairs={{0,4},{1,5},{2,6},{3,7},{4,8},{5,9},{6,10},{7,11},{8,12},{9,13},{1... | collective-permute-start | bytes 122888 | tf_op jit(solution)/shard_map/ppermute | solution.py:52
  47.9 2.4 %collective-permute-start.12 = (bf16[160,128]{1,0:T(8,128)(2,1)S(1)}, bf16[160,128]{1,0:T(8,128)(2,1)S(1)}, u32[]{:S(2)}, u32[]{:S(2)}) collective-permute-start(bf16[160,128]{1,0:T(8,128)(2,1)S(1)} %get-tuple-element.46), channel_id=1, source_target_pairs={{0,6},{1,7},{2,8},{3,9},{4,10},{5,11},{6,12},{7,13},{8,14},{9,15},... | collective-permute-start | bytes 122888 | tf_op jit(solution)/shard_map/ppermute | solution.py:52
  50.3 1.5 %collective-permute-start.13 = (bf16[160,128]{1,0:T(8,128)(2,1)S(1)}, bf16[160,128]{1,0:T(8,128)(2,1)S(1)}, u32[]{:S(2)}, u32[]{:S(2)}) collective-permute-start(bf16[160,128]{1,0:T(8,128)(2,1)S(1)} %get-tuple-element.45), channel_id=1, source_target_pairs={{0,8},{1,9},{2,10},{3,11},{4,12},{5,13},{6,14},{7,15},{8,0},{9,1},... | collective-permute-start | bytes 122888 | tf_op jit(solution)/shard_map/ppermute | solution.py:52
  51.8 2.4 %collective-permute-start.14 = (bf16[160,128]{1,0:T(8,128)(2,1)S(1)}, bf16[160,128]{1,0:T(8,128)(2,1)S(1)}, u32[]{:S(2)}, u32[]{:S(2)}) collective-permute-start(bf16[160,128]{1,0:T(8,128)(2,1)S(1)} %get-tuple-element.44), channel_id=1, source_target_pairs={{0,10},{1,11},{2,12},{3,13},{4,14},{5,15},{6,0},{7,1},{8,2},{9,3},... | collective-permute-start | bytes 122888 | tf_op jit(solution)/shard_map/ppermute | solution.py:52
  54.1 1.5 %collective-permute-start.15 = (bf16[160,128]{1,0:T(8,128)(2,1)S(1)}, bf16[160,128]{1,0:T(8,128)(2,1)S(1)}, u32[]{:S(2)}, u32[]{:S(2)}) collective-permute-start(bf16[160,128]{1,0:T(8,128)(2,1)S(1)} %get-tuple-element.43), channel_id=1, source_target_pairs={{0,12},{1,13},{2,14},{3,15},{4,0},{5,1},{6,2},{7,3},{8,4},{9,5},{1... | collective-permute-start | bytes 122888 | tf_op jit(solution)/shard_map/ppermute | solution.py:52
  55.6 1.5 %collective-permute-start.16 = (bf16[160,128]{1,0:T(8,128)(2,1)S(1)}, bf16[160,128]{1,0:T(8,128)(2,1)S(1)}, u32[]{:S(2)}, u32[]{:S(2)}) collective-permute-start(bf16[160,128]{1,0:T(8,128)(2,1)S(1)} %get-tuple-element.42), channel_id=1, source_target_pairs={{0,14},{1,15},{2,0},{3,1},{4,2},{5,3},{6,4},{7,5},{8,6},{9,7},{10,... | collective-permute-start | bytes 122888 | tf_op jit(solution)/shard_map/ppermute | solution.py:52
  57.3 0.9 %collective-permute-done.15.refs_5_ = bf16[160,128]{1,0:T(8,128)(2,1)S(1)} collective-permute-done((bf16[160,128]{1,0:T(8,128)(2,1)S(1)}, bf16[160,128]{1,0:T(8,128)(2,1)S(1)}, u32[]{:S(2)}, u32[]{:S(2)}) %collective-permute-start.15) | collective-permute-done | bytes 40992 | tf_op jit(solution)/shard_map/ppermute | solution.py:52
  58.2 1.4 %collective-permute-done.16.refs_6_ = bf16[160,128]{1,0:T(8,128)(2,1)S(1)} collective-permute-done((bf16[160,128]{1,0:T(8,128)(2,1)S(1)}, bf16[160,128]{1,0:T(8,128)(2,1)S(1)}, u32[]{:S(2)}, u32[]{:S(2)}) %collective-permute-start.16) | collective-permute-done | bytes 40992 | tf_op jit(solution)/shard_map/ppermute | solution.py:52
  59.6 0.8 %total.1 = bf16[64,320]{1,0:T(8,128)(2,1)} custom-call(s32[1]{0:T(128)} %bitcast.place_ref, f32[160,128]{1,0:T(8,128)S(1)} %slice_bitcast_fusion.own_ref, bf16[160,128]{1,0:T(8,128)(2,1)S(1)} %collective-permute-done.10.refs_0_, bf16[160,128]{1,0:T(8,128)(2,1)S(1)} %collective-permute-done.11.refs_1_, bf16[160,128]{1,0:T(8,128)(2,1)S(1)} %collective-permute-done.12.refs_2_, ...), custom_call_target="tpu_custom_call" | custom-call | tf_op jit(solution)/shard_map/total/pallas_call | solution.py:626
  (28 shorter events, 2.9 us)
Async XLA Ops:
  2.2 11.0 %collective-permute-start = (bf16[240,128]{1,0:T(8,128)(2,1)S(1)}, bf16[240,128]{1,0:T(8,128)(2,1)S(1)}, u32[]{:S(2)}, u32[]{:S(2)}) collective-permute-start(bf16[240,128]{1,0:T(8,128)(2,1)S(1)} %get-tuple-element.40), channel_id=1, source_target_pairs={{0,2},{1,3},{2,4},{3,5},{4,6},{5,7},{6,8},{7,9},{8,10},{9,11},{10,... | collective-permute-start | bytes 184328 | tf_op jit(solution)/shard_map/ppermute | solution.py:52
  5.2 9.4 %collective-permute-start.1 = (bf16[240,128]{1,0:T(8,128)(2,1)S(1)}, bf16[240,128]{1,0:T(8,128)(2,1)S(1)}, u32[]{:S(2)}, u32[]{:S(2)}) collective-permute-start(bf16[240,128]{1,0:T(8,128)(2,1)S(1)} %get-tuple-element.39), channel_id=1, source_target_pairs={{0,4},{1,5},{2,6},{3,7},{4,8},{5,9},{6,10},{7,11},{8,12},{9,13},{1... | collective-permute-start | bytes 184328 | tf_op jit(solution)/shard_map/ppermute | solution.py:52
  6.8 9.4 %collective-permute-start.2 = (bf16[240,128]{1,0:T(8,128)(2,1)S(1)}, bf16[240,128]{1,0:T(8,128)(2,1)S(1)}, u32[]{:S(2)}, u32[]{:S(2)}) collective-permute-start(bf16[240,128]{1,0:T(8,128)(2,1)S(1)} %get-tuple-element.38), channel_id=1, source_target_pairs={{0,6},{1,7},{2,8},{3,9},{4,10},{5,11},{6,12},{7,13},{8,14},{9,15},... | collective-permute-start | bytes 184328 | tf_op jit(solution)/shard_map/ppermute | solution.py:52
  9.3 7.4 %collective-permute-start.3 = (bf16[240,128]{1,0:T(8,128)(2,1)S(1)}, bf16[240,128]{1,0:T(8,128)(2,1)S(1)}, u32[]{:S(2)}, u32[]{:S(2)}) collective-permute-start(bf16[240,128]{1,0:T(8,128)(2,1)S(1)} %get-tuple-element.37), channel_id=1, source_target_pairs={{0,8},{1,9},{2,10},{3,11},{4,12},{5,13},{6,14},{7,15},{8,0},{9,1},... | collective-permute-start | bytes 184328 | tf_op jit(solution)/shard_map/ppermute | solution.py:52
  10.6 8.7 %collective-permute-start.4 = (bf16[240,128]{1,0:T(8,128)(2,1)S(1)}, bf16[240,128]{1,0:T(8,128)(2,1)S(1)}, u32[]{:S(2)}, u32[]{:S(2)}) collective-permute-start(bf16[240,128]{1,0:T(8,128)(2,1)S(1)} %get-tuple-element.34), channel_id=1, source_target_pairs={{0,10},{1,11},{2,12},{3,13},{4,14},{5,15},{6,0},{7,1},{8,2},{9,3},... | collective-permute-start | bytes 184328 | tf_op jit(solution)/shard_map/ppermute | solution.py:52
  13.2 6.0 %collective-permute-start.5 = (bf16[240,128]{1,0:T(8,128)(2,1)S(1)}, bf16[240,128]{1,0:T(8,128)(2,1)S(1)}, u32[]{:S(2)}, u32[]{:S(2)}) collective-permute-start(bf16[240,128]{1,0:T(8,128)(2,1)S(1)} %get-tuple-element.36), channel_id=1, source_target_pairs={{0,12},{1,13},{2,14},{3,15},{4,0},{5,1},{6,2},{7,3},{8,4},{9,5},{1... | collective-permute-start | bytes 184328 | tf_op jit(solution)/shard_map/ppermute | solution.py:52
  14.6 4.7 %collective-permute-start.6 = (bf16[240,128]{1,0:T(8,128)(2,1)S(1)}, bf16[240,128]{1,0:T(8,128)(2,1)S(1)}, u32[]{:S(2)}, u32[]{:S(2)}) collective-permute-start(bf16[240,128]{1,0:T(8,128)(2,1)S(1)} %get-tuple-element.35), channel_id=1, source_target_pairs={{0,14},{1,15},{2,0},{3,1},{4,2},{5,3},{6,4},{7,5},{8,6},{9,7},{10,... | collective-permute-start | bytes 184328 | tf_op jit(solution)/shard_map/ppermute | solution.py:52
  16.7 4.2 %collective-permute-start.7 = (bf16[5,240,128]{2,1,0:T(8,128)(2,1)S(1)}, bf16[5,240,128]{2,1,0:T(8,128)(2,1)S(1)}, u32[]{:S(2)}, u32[]{:S(2)}) collective-permute-start(bf16[5,240,128]{2,1,0:T(8,128)(2,1)S(1)} %bitcast_dynamic-update-slice_fusion.first_ref), channel_id=1, source_target_pairs={{0,1},{1,0},{2,3},{3,2},{4,5},{5,4},{6,7},{7,6},{8,9},{9,8},{10,11... | collective-permute-start | bytes 921608 | tf_op jit(solution)/shard_map/ppermute | solution.py:47
  19.3 1.6 %collective-permute-start.8 = (bf16[3,240,128]{2,1,0:T(8,128)(2,1)S(1)}, bf16[3,240,128]{2,1,0:T(8,128)(2,1)S(1)}, u32[]{:S(2)}, u32[]{:S(2)}) collective-permute-start(bf16[3,240,128]{2,1,0:T(8,128)(2,1)S(1)} %pad_maximum_fusion.last_ref), channel_id=1, source_target_pairs={{0,1},{1,0},{2,3},{3,2},{4,5},{5,4},{6,7},{7,6},{8,9},{9,8},{10,11... | collective-permute-start | bytes 552968 | tf_op jit(solution)/shard_map/ppermute | solution.py:47
  28.6 13.1 %all-to-all-start = ((f32[16,8,128]{2,1,0:T(8,128)}), f32[16,8,128]{2,1,0:T(8,128)S(1)}, u32[]{:S(2)}, u32[]{:S(2)}) async-start(f32[16,8,128]{2,1,0:T(8,128)} %get-tuple-element.22), calls=%async_computation | async-start | bytes 131072 | tf_op jit(solution)/shard_map/all_to_all | solution.py:578
  43.1 1.8 %collective-permute-start.9 = (bf16[8,160,128]{2,1,0:T(8,128)(2,1)S(1)}, bf16[8,160,128]{2,1,0:T(8,128)(2,1)S(1)}, u32[]{:S(2)}, u32[]{:S(2)}) collective-permute-start(bf16[8,160,128]{2,1,0:T(8,128)(2,1)S(1)} %get-tuple-element.30), channel_id=1, source_target_pairs={{0,1},{1,0},{2,3},{3,2},{4,5},{5,4},{6,7},{7,6},{8,9},{9,8},{10,11... | collective-permute-start | bytes 983048 | tf_op jit(solution)/shard_map/ppermute | solution.py:47
  45.1 9.1 %collective-permute-start.10 = (bf16[160,128]{1,0:T(8,128)(2,1)S(1)}, bf16[160,128]{1,0:T(8,128)(2,1)S(1)}, u32[]{:S(2)}, u32[]{:S(2)}) collective-permute-start(bf16[160,128]{1,0:T(8,128)(2,1)S(1)} %get-tuple-element.48), channel_id=1, source_target_pairs={{0,2},{1,3},{2,4},{3,5},{4,6},{5,7},{6,8},{7,9},{8,10},{9,11},{10,... | collective-permute-start | bytes 122888 | tf_op jit(solution)/shard_map/ppermute | solution.py:52
  46.5 9.1 %collective-permute-start.11 = (bf16[160,128]{1,0:T(8,128)(2,1)S(1)}, bf16[160,128]{1,0:T(8,128)(2,1)S(1)}, u32[]{:S(2)}, u32[]{:S(2)}) collective-permute-start(bf16[160,128]{1,0:T(8,128)(2,1)S(1)} %get-tuple-element.47), channel_id=1, source_target_pairs={{0,4},{1,5},{2,6},{3,7},{4,8},{5,9},{6,10},{7,11},{8,12},{9,13},{1... | collective-permute-start | bytes 122888 | tf_op jit(solution)/shard_map/ppermute | solution.py:52
  47.9 9.1 %collective-permute-start.12 = (bf16[160,128]{1,0:T(8,128)(2,1)S(1)}, bf16[160,128]{1,0:T(8,128)(2,1)S(1)}, u32[]{:S(2)}, u32[]{:S(2)}) collective-permute-start(bf16[160,128]{1,0:T(8,128)(2,1)S(1)} %get-tuple-element.46), channel_id=1, source_target_pairs={{0,6},{1,7},{2,8},{3,9},{4,10},{5,11},{6,12},{7,13},{8,14},{9,15},... | collective-permute-start | bytes 122888 | tf_op jit(solution)/shard_map/ppermute | solution.py:52
  50.3 6.8 %collective-permute-start.13 = (bf16[160,128]{1,0:T(8,128)(2,1)S(1)}, bf16[160,128]{1,0:T(8,128)(2,1)S(1)}, u32[]{:S(2)}, u32[]{:S(2)}) collective-permute-start(bf16[160,128]{1,0:T(8,128)(2,1)S(1)} %get-tuple-element.45), channel_id=1, source_target_pairs={{0,8},{1,9},{2,10},{3,11},{4,12},{5,13},{6,14},{7,15},{8,0},{9,1},... | collective-permute-start | bytes 122888 | tf_op jit(solution)/shard_map/ppermute | solution.py:52
  51.8 5.6 %collective-permute-start.14 = (bf16[160,128]{1,0:T(8,128)(2,1)S(1)}, bf16[160,128]{1,0:T(8,128)(2,1)S(1)}, u32[]{:S(2)}, u32[]{:S(2)}) collective-permute-start(bf16[160,128]{1,0:T(8,128)(2,1)S(1)} %get-tuple-element.44), channel_id=1, source_target_pairs={{0,10},{1,11},{2,12},{3,13},{4,14},{5,15},{6,0},{7,1},{8,2},{9,3},... | collective-permute-start | bytes 122888 | tf_op jit(solution)/shard_map/ppermute | solution.py:52
  54.1 4.0 %collective-permute-start.15 = (bf16[160,128]{1,0:T(8,128)(2,1)S(1)}, bf16[160,128]{1,0:T(8,128)(2,1)S(1)}, u32[]{:S(2)}, u32[]{:S(2)}) collective-permute-start(bf16[160,128]{1,0:T(8,128)(2,1)S(1)} %get-tuple-element.43), channel_id=1, source_target_pairs={{0,12},{1,13},{2,14},{3,15},{4,0},{5,1},{6,2},{7,3},{8,4},{9,5},{1... | collective-permute-start | bytes 122888 | tf_op jit(solution)/shard_map/ppermute | solution.py:52
  55.6 4.0 %collective-permute-start.16 = (bf16[160,128]{1,0:T(8,128)(2,1)S(1)}, bf16[160,128]{1,0:T(8,128)(2,1)S(1)}, u32[]{:S(2)}, u32[]{:S(2)}) collective-permute-start(bf16[160,128]{1,0:T(8,128)(2,1)S(1)} %get-tuple-element.42), channel_id=1, source_target_pairs={{0,14},{1,15},{2,0},{3,1},{4,2},{5,3},{6,4},{7,5},{8,6},{9,7},{10,... | collective-permute-start | bytes 122888 | tf_op jit(solution)/shard_map/ppermute | solution.py:52

commit v21 on v20

--- a/solution.py
+++ b/solution.py
@@ -269,8 +269,10 @@
     arrived_ref,
     teacher_ref,
     logits_ref,
+    copies_ref,
     sems,
     made_sem,
+    stats_sem,
 ):
     core = place_ref[0] % 2
     chips, tokens, width = hidden_ref.shape
@@ -359,11 +361,14 @@
         (top, total, teacher_top, teacher_total, cross, target, centre)
     ):
         table = jnp.where(lane == place, column, table)
-    stats = jnp.concatenate([table, jnp.zeros((stats_ref.shape[2] - tokens, LANES), jnp.float32)])
+    stats = jnp.concatenate([table, jnp.zeros((own_ref.shape[1] - tokens, LANES), jnp.float32)])
     stats = stats.T[:STATS]
     own_ref[...] = stats
-    stats_ref[...] = jnp.broadcast_to(stats[None], stats_ref.shape)
+    copies_ref[...] = jnp.broadcast_to(stats[None], copies_ref.shape)
+    out_stats = pltpu.make_async_copy(copies_ref, stats_ref, stats_sem)
+    out_stats.start()
     out.wait()
+    out_stats.wait()
 
 
 def products_kernel(
@@ -397,16 +402,13 @@
 def put_shares(parity, factors_ref, terms_ref, picks_ref, out_ref):
     tokens = terms_ref.shape[3]
     factor, level, weight = [factors_ref[i] for i in range(3)]
-
-    def put(step, _):
+    for step in range(terms_ref.shape[0]):
         for i, tile in enumerate((3 * parity, 3 * parity + 1, 2)):
             sums = terms_ref[step, tile, 0] + level * terms_ref[step, tile, 1]
             share = factor * sums - weight * picks_ref[step, tile].astype(jnp.float32)
             if i == 2:
                 share = folded(parity == 0, share)
             out_ref[step, tokens * i : tokens * i + share.shape[0]] = share.astype(out_ref.dtype)
-
-    lax.fori_loop(0, terms_ref.shape[0], put, None)
 
 
 def give_kernel(
@@ -542,15 +544,16 @@
     last, early = lax.optimization_barrier((last, early))
     far = [swap_cores(last), swap_cores(first)]
 
+    stats_shape = (count, STATS, pl.cdiv(tokens, LANES) * LANES)
     rows, stats, own_stats = pl.pallas_call(
         logits_kernel,
         out_shape=(
             hbm_array((3 * tokens, shard_rows), jnp.bfloat16),
-            jax.ShapeDtypeStruct((count, STATS, pl.cdiv(tokens, LANES) * LANES), jnp.float32),
-            vmem_array((STATS, pl.cdiv(tokens, LANES) * LANES), jnp.float32),
+            hbm_array(stats_shape, jnp.float32),
+            vmem_array(stats_shape[1:], jnp.float32),
         ),
         in_specs=[smem] + [vmem] * 7 + [hbm],
-        out_specs=[hbm, vmem, vmem],
+        out_specs=[hbm, hbm, vmem],
         scratch_shapes=[
             pltpu.VMEM((chips - EARLY, shard_rows, width), head.dtype),
             rows_scratch,
@@ -558,7 +561,9 @@
             pltpu.VMEM((2 * tokens, (shard_rows + LANES // 2) // 2), jnp.float32),
             pltpu.VMEM((tokens, shard_rows), jnp.float32),
             pltpu.VMEM((tokens, shard_rows), jnp.float32),
+            pltpu.VMEM(stats_shape, jnp.float32),
             pltpu.SemaphoreType.DMA((chips - EARLY,)),
+            rows_sem,
             rows_sem,
         ],
         compiler_params=params,

time: 60.6 us -> 59.2 us (0.977)
  Pallas kernels: 21.8 us -> 20.2 us
  transfers between devices with their start and end apart: 18 -> 18, of which waited for: 7 -> 8; matrix products, arithmetic and copies ran while one was open for 0% -> 0% of each run, Pallas kernels for 17% -> 17%
where the time goes in v21:
time: 59.2 us; the launch traced here: 59 us
  starting transfers between devices  32.5 us (55%)
  Pallas kernels  20.2 us (34%)
  waiting for transfers between devices  4.59 us (8%)
  between operations  1.43 us (2%)
    ppermute x14, starting transfers between devices, along_chips(): lax.ppermute(array, 'vocab', [(i, (i + 2 * step) % count) for i in range(...  25.7 us
    pallas_call x1, Pallas kernels, paired_shards(): pl.pallas_call(logits_kernel, out_shape=(hbm_array((3 * tokens, shard_row...  7.09 us
    all_to_all x1, starting transfers between devices, paired_shards(): lax.all_to_all(stats, 'vocab', split_axis=0, concat_axis=0, tiled=True)  6.21 us
    pallas_call x1, Pallas kernels, paired_shards(): pl.pallas_call(products_kernel, out_shape=(vmem_array((chips, width // LA...  6.18 us
    ppermute x14, waiting for transfers between devices, along_chips(): lax.ppermute(array, 'vocab', [(i, (i + 2 * step) % count) for i in range(...  3.19 us
    pallas_call x1, Pallas kernels, paired_shards(): pl.pallas_call(functools.partial(preload_kernel, chips=chips), out_shape=...  2.4 us
    pallas_call x1, Pallas kernels, paired_shards(): pl.pallas_call(functools.partial(pack_kernel, shard_rows=shard_rows), out...  1.52 us
    pallas_call x1, Pallas kernels, paired_shards(): pl.pallas_call(keep_kernel, out_shape=(vmem_array((chips, hidden_rows, LA...  1.34 us
  transfers between devices with their start and end apart: 18, of which 8 were waited for; matrix products, arithmetic and copies ran while one was open for 0% of the time, Pallas kernels for 17%

profile of v21, /device:TPU:0, one launch (start us, length us, event | category | flops | bytes accessed | tf_op | source)
XLA Modules:
  0.0 59.0 jit_solution(14616939134450574093)
XLA Ops:
  0.6 1.5 %pack.1 = (bf16[8,240,128]{2,1,0:T(8,128)(2,1)S(1)}, bf16[128,128]{1,0:T(8,128)(2,1)S(1)}, f32[64,128]{1,0:T(8,128)S(1)}) custom-call(s32[1]{0:T(128)} %bitcast.place_ref, bf16[64,320]{1,0:T(8,128)(2,1)} %refs_0_.1, bf16[4,19456]{1,0:T(4,128)(2,1)} %refs_1_.1, f32[4,608]{1,0:T(4,128)} %refs_2_.1, s32[1,64]{1,0:T(1,128)} %bitcast.49, s32[1,64]{1,0:T(1,128)} %bitcast.50, ...), custom_call_target="tpu_custom_call" | custom-call | tf_op jit(solution)/shard_map/pack/pallas_call | solution.py:512
  2.2 3.0 %collective-permute-start = (bf16[240,128]{1,0:T(8,128)(2,1)S(1)}, bf16[240,128]{1,0:T(8,128)(2,1)S(1)}, u32[]{:S(2)}, u32[]{:S(2)}) collective-permute-start(bf16[240,128]{1,0:T(8,128)(2,1)S(1)} %get-tuple-element.40), channel_id=1, source_target_pairs={{0,2},{1,3},{2,4},{3,5},{4,6},{5,7},{6,8},{7,9},{8,10},{9,11},{10,... | collective-permute-start | bytes 184328 | tf_op jit(solution)/shard_map/ppermute | solution.py:52
  5.2 1.6 %collective-permute-start.1 = (bf16[240,128]{1,0:T(8,128)(2,1)S(1)}, bf16[240,128]{1,0:T(8,128)(2,1)S(1)}, u32[]{:S(2)}, u32[]{:S(2)}) collective-permute-start(bf16[240,128]{1,0:T(8,128)(2,1)S(1)} %get-tuple-element.39), channel_id=1, source_target_pairs={{0,4},{1,5},{2,6},{3,7},{4,8},{5,9},{6,10},{7,11},{8,12},{9,13},{1... | collective-permute-start | bytes 184328 | tf_op jit(solution)/shard_map/ppermute | solution.py:52
  6.8 2.5 %collective-permute-start.2 = (bf16[240,128]{1,0:T(8,128)(2,1)S(1)}, bf16[240,128]{1,0:T(8,128)(2,1)S(1)}, u32[]{:S(2)}, u32[]{:S(2)}) collective-permute-start(bf16[240,128]{1,0:T(8,128)(2,1)S(1)} %get-tuple-element.38), channel_id=1, source_target_pairs={{0,6},{1,7},{2,8},{3,9},{4,10},{5,11},{6,12},{7,13},{8,14},{9,15},... | collective-permute-start | bytes 184328 | tf_op jit(solution)/shard_map/ppermute | solution.py:52
  9.3 1.2 %collective-permute-start.3 = (bf16[240,128]{1,0:T(8,128)(2,1)S(1)}, bf16[240,128]{1,0:T(8,128)(2,1)S(1)}, u32[]{:S(2)}, u32[]{:S(2)}) collective-permute-start(bf16[240,128]{1,0:T(8,128)(2,1)S(1)} %get-tuple-element.37), channel_id=1, source_target_pairs={{0,8},{1,9},{2,10},{3,11},{4,12},{5,13},{6,14},{7,15},{8,0},{9,1},... | collective-permute-start | bytes 184328 | tf_op jit(solution)/shard_map/ppermute | solution.py:52
  10.6 2.6 %collective-permute-start.4 = (bf16[240,128]{1,0:T(8,128)(2,1)S(1)}, bf16[240,128]{1,0:T(8,128)(2,1)S(1)}, u32[]{:S(2)}, u32[]{:S(2)}) collective-permute-start(bf16[240,128]{1,0:T(8,128)(2,1)S(1)} %get-tuple-element.34), channel_id=1, source_target_pairs={{0,10},{1,11},{2,12},{3,13},{4,14},{5,15},{6,0},{7,1},{8,2},{9,3},... | collective-permute-start | bytes 184328 | tf_op jit(solution)/shard_map/ppermute | solution.py:52
  13.2 1.3 %collective-permute-start.5 = (bf16[240,128]{1,0:T(8,128)(2,1)S(1)}, bf16[240,128]{1,0:T(8,128)(2,1)S(1)}, u32[]{:S(2)}, u32[]{:S(2)}) collective-permute-start(bf16[240,128]{1,0:T(8,128)(2,1)S(1)} %get-tuple-element.36), channel_id=1, source_target_pairs={{0,12},{1,13},{2,14},{3,15},{4,0},{5,1},{6,2},{7,3},{8,4},{9,5},{1... | collective-permute-start | bytes 184328 | tf_op jit(solution)/shard_map/ppermute | solution.py:52
  14.6 1.5 %collective-permute-start.6 = (bf16[240,128]{1,0:T(8,128)(2,1)S(1)}, bf16[240,128]{1,0:T(8,128)(2,1)S(1)}, u32[]{:S(2)}, u32[]{:S(2)}) collective-permute-start(bf16[240,128]{1,0:T(8,128)(2,1)S(1)} %get-tuple-element.35), channel_id=1, source_target_pairs={{0,14},{1,15},{2,0},{3,1},{4,2},{5,3},{6,4},{7,5},{8,6},{9,7},{10,... | collective-permute-start | bytes 184328 | tf_op jit(solution)/shard_map/ppermute | solution.py:52
  16.8 2.4 %preload.1.early_ref = bf16[3,1216,640]{2,1,0:T(8,128)(2,1)S(1)} custom-call(s32[1]{0:T(128)} %bitcast.place_ref, bf16[1216,5120]{1,0:T(8,128)(2,1)} %head_ref.5, bf16[240,128]{1,0:T(8,128)(2,1)S(1)} %collective-permute-done.2._), custom_call_target="tpu_custom_call" | custom-call | bytes 9338880 | tf_op jit(solution)/shard_map/preload/pallas_call | solution.py:532
  20.9 7.1 %logits.1 = (bf16[192,1216]{1,0:T(8,128)(2,1)}, f32[16,8,128]{2,1,0:T(8,128)}, f32[8,128]{1,0:T(8,128)S(1)}) custom-call(s32[1]{0:T(128)} %bitcast.place_ref, bf16[5,240,128]{2,1,0:T(8,128)(2,1)S(1)} %bitcast_dynamic-update-slice_fusion.first_ref, bf16[3,240,128]{2,1,0:T(8,128)(2,1)S(1)} %pad_maximum_fusion.last_ref, ...), custom_call_target="tpu_custom_call" | custom-call | flops 796917760 | bytes 12451840 | tf_op jit(solution)/shard_map/logits/pallas_call | solution.py:548
  28.0 6.2 %all-to-all-start = ((f32[16,8,128]{2,1,0:T(8,128)}), f32[16,8,128]{2,1,0:T(8,128)S(1)}, u32[]{:S(2)}, u32[]{:S(2)}) async-start(f32[16,8,128]{2,1,0:T(8,128)} %get-tuple-element.22), calls=%async_computation | async-start | bytes 131072 | tf_op jit(solution)/shard_map/all_to_all | solution.py:583
  34.2 6.2 %products.1 = (f32[8,5,2,64,128]{4,3,2,1,0:T(8,128)S(1)}, bf16[8,5,64,128]{3,2,1,0:T(8,128)(2,1)S(1)}) custom-call(s32[1]{0:T(128)} %bitcast.place_ref, bf16[192,1216]{1,0:T(8,128)(2,1)} %get-tuple-element.24.rows_ref, bf16[1216,5120]{1,0:T(8,128)(2,1)} %head_ref.5), custom_call_target="tpu_custom_call" | custom-call | flops 2390753280 | bytes 12451840 | tf_op jit(solution)/shard_map/products/pallas_call | solution.py:585
  41.1 0.9 %give.1 = (bf16[8,160,128]{2,1,0:T(8,128)(2,1)S(1)}, f32[3,64,128]{2,1,0:T(8,128)S(1)}, f32[1,1]{1,0:T(1,128)}) custom-call(s32[1]{0:T(128)} %bitcast.place_ref, f32[1]{0:T(128)S(6)} %copy.14.scale_ref, f32[16,8,128]{2,1,0:T(8,128)S(1)} %all-to-all-done.stats_ref, f32[8,128]{1,0:T(8,128)S(1)} %get-tuple-element.23.own_ref, ...), custom_call_target="tpu_custom_call" | custom-call | tf_op jit(solution)/shard_map/give/pallas_call | solution.py:602
  42.1 1.3 %keep.1 = (f32[8,160,128]{2,1,0:T(8,128)S(1)}, f32[1,1]{1,0:T(1,128)}) custom-call(s32[1]{0:T(128)} %bitcast.place_ref, f32[3,64,128]{2,1,0:T(8,128)S(1)} %get-tuple-element.27.factors_ref, f32[1,1]{1,0:T(1,128)} %get-tuple-element.28.found_ref, f32[8,5,2,64,128]{4,3,2,1,0:T(8,128)S(1)} %get-tuple-element.25.terms_ref, ...), custom_call_target="tpu_custom_call" | custom-call | flops 2621440 | bytes 2621440 | tf_op jit(solution)/shard_map/keep/pallas_call | solution.py:615
  43.8 1.3 %collective-permute-start.10 = (bf16[160,128]{1,0:T(8,128)(2,1)S(1)}, bf16[160,128]{1,0:T(8,128)(2,1)S(1)}, u32[]{:S(2)}, u32[]{:S(2)}) collective-permute-start(bf16[160,128]{1,0:T(8,128)(2,1)S(1)} %get-tuple-element.48), channel_id=1, source_target_pairs={{0,2},{1,3},{2,4},{3,5},{4,6},{5,7},{6,8},{7,9},{8,10},{9,11},{10,... | collective-permute-start | bytes 122888 | tf_op jit(solution)/shard_map/ppermute | solution.py:52
  45.1 1.5 %collective-permute-start.11 = (bf16[160,128]{1,0:T(8,128)(2,1)S(1)}, bf16[160,128]{1,0:T(8,128)(2,1)S(1)}, u32[]{:S(2)}, u32[]{:S(2)}) collective-permute-start(bf16[160,128]{1,0:T(8,128)(2,1)S(1)} %get-tuple-element.47), channel_id=1, source_target_pairs={{0,4},{1,5},{2,6},{3,7},{4,8},{5,9},{6,10},{7,11},{8,12},{9,13},{1... | collective-permute-start | bytes 122888 | tf_op jit(solution)/shard_map/ppermute | solution.py:52
  46.5 2.4 %collective-permute-start.12 = (bf16[160,128]{1,0:T(8,128)(2,1)S(1)}, bf16[160,128]{1,0:T(8,128)(2,1)S(1)}, u32[]{:S(2)}, u32[]{:S(2)}) collective-permute-start(bf16[160,128]{1,0:T(8,128)(2,1)S(1)} %get-tuple-element.46), channel_id=1, source_target_pairs={{0,6},{1,7},{2,8},{3,9},{4,10},{5,11},{6,12},{7,13},{8,14},{9,15},... | collective-permute-start | bytes 122888 | tf_op jit(solution)/shard_map/ppermute | solution.py:52
  48.9 1.5 %collective-permute-start.13 = (bf16[160,128]{1,0:T(8,128)(2,1)S(1)}, bf16[160,128]{1,0:T(8,128)(2,1)S(1)}, u32[]{:S(2)}, u32[]{:S(2)}) collective-permute-start(bf16[160,128]{1,0:T(8,128)(2,1)S(1)} %get-tuple-element.45), channel_id=1, source_target_pairs={{0,8},{1,9},{2,10},{3,11},{4,12},{5,13},{6,14},{7,15},{8,0},{9,1},... | collective-permute-start | bytes 122888 | tf_op jit(solution)/shard_map/ppermute | solution.py:52
  50.4 2.4 %collective-permute-start.14 = (bf16[160,128]{1,0:T(8,128)(2,1)S(1)}, bf16[160,128]{1,0:T(8,128)(2,1)S(1)}, u32[]{:S(2)}, u32[]{:S(2)}) collective-permute-start(bf16[160,128]{1,0:T(8,128)(2,1)S(1)} %get-tuple-element.44), channel_id=1, source_target_pairs={{0,10},{1,11},{2,12},{3,13},{4,14},{5,15},{6,0},{7,1},{8,2},{9,3},... | collective-permute-start | bytes 122888 | tf_op jit(solution)/shard_map/ppermute | solution.py:52
  52.7 1.5 %collective-permute-start.15 = (bf16[160,128]{1,0:T(8,128)(2,1)S(1)}, bf16[160,128]{1,0:T(8,128)(2,1)S(1)}, u32[]{:S(2)}, u32[]{:S(2)}) collective-permute-start(bf16[160,128]{1,0:T(8,128)(2,1)S(1)} %get-tuple-element.43), channel_id=1, source_target_pairs={{0,12},{1,13},{2,14},{3,15},{4,0},{5,1},{6,2},{7,3},{8,4},{9,5},{1... | collective-permute-start | bytes 122888 | tf_op jit(solution)/shard_map/ppermute | solution.py:52
  54.2 1.5 %collective-permute-start.16 = (bf16[160,128]{1,0:T(8,128)(2,1)S(1)}, bf16[160,128]{1,0:T(8,128)(2,1)S(1)}, u32[]{:S(2)}, u32[]{:S(2)}) collective-permute-start(bf16[160,128]{1,0:T(8,128)(2,1)S(1)} %get-tuple-element.42), channel_id=1, source_target_pairs={{0,14},{1,15},{2,0},{3,1},{4,2},{5,3},{6,4},{7,5},{8,6},{9,7},{10,... | collective-permute-start | bytes 122888 | tf_op jit(solution)/shard_map/ppermute | solution.py:52
  55.8 1.0 %collective-permute-done.15.refs_5_ = bf16[160,128]{1,0:T(8,128)(2,1)S(1)} collective-permute-done((bf16[160,128]{1,0:T(8,128)(2,1)S(1)}, bf16[160,128]{1,0:T(8,128)(2,1)S(1)}, u32[]{:S(2)}, u32[]{:S(2)}) %collective-permute-start.15) | collective-permute-done | bytes 40992 | tf_op jit(solution)/shard_map/ppermute | solution.py:52
  56.8 1.4 %collective-permute-done.16.refs_6_ = bf16[160,128]{1,0:T(8,128)(2,1)S(1)} collective-permute-done((bf16[160,128]{1,0:T(8,128)(2,1)S(1)}, bf16[160,128]{1,0:T(8,128)(2,1)S(1)}, u32[]{:S(2)}, u32[]{:S(2)}) %collective-permute-start.16) | collective-permute-done | bytes 40992 | tf_op jit(solution)/shard_map/ppermute | solution.py:52
  58.2 0.8 %total.1 = bf16[64,320]{1,0:T(8,128)(2,1)} custom-call(s32[1]{0:T(128)} %bitcast.place_ref, f32[160,128]{1,0:T(8,128)S(1)} %slice_bitcast_fusion.own_ref, bf16[160,128]{1,0:T(8,128)(2,1)S(1)} %collective-permute-done.10.refs_0_, bf16[160,128]{1,0:T(8,128)(2,1)S(1)} %collective-permute-done.11.refs_1_, bf16[160,128]{1,0:T(8,128)(2,1)S(1)} %collective-permute-done.12.refs_2_, ...), custom_call_target="tpu_custom_call" | custom-call | tf_op jit(solution)/shard_map/total/pallas_call | solution.py:631
  (28 shorter events, 3.0 us)
Async XLA Ops:
  2.2 11.0 %collective-permute-start = (bf16[240,128]{1,0:T(8,128)(2,1)S(1)}, bf16[240,128]{1,0:T(8,128)(2,1)S(1)}, u32[]{:S(2)}, u32[]{:S(2)}) collective-permute-start(bf16[240,128]{1,0:T(8,128)(2,1)S(1)} %get-tuple-element.40), channel_id=1, source_target_pairs={{0,2},{1,3},{2,4},{3,5},{4,6},{5,7},{6,8},{7,9},{8,10},{9,11},{10,... | collective-permute-start | bytes 184328 | tf_op jit(solution)/shard_map/ppermute | solution.py:52
  5.2 9.4 %collective-permute-start.1 = (bf16[240,128]{1,0:T(8,128)(2,1)S(1)}, bf16[240,128]{1,0:T(8,128)(2,1)S(1)}, u32[]{:S(2)}, u32[]{:S(2)}) collective-permute-start(bf16[240,128]{1,0:T(8,128)(2,1)S(1)} %get-tuple-element.39), channel_id=1, source_target_pairs={{0,4},{1,5},{2,6},{3,7},{4,8},{5,9},{6,10},{7,11},{8,12},{9,13},{1... | collective-permute-start | bytes 184328 | tf_op jit(solution)/shard_map/ppermute | solution.py:52
  6.8 9.4 %collective-permute-start.2 = (bf16[240,128]{1,0:T(8,128)(2,1)S(1)}, bf16[240,128]{1,0:T(8,128)(2,1)S(1)}, u32[]{:S(2)}, u32[]{:S(2)}) collective-permute-start(bf16[240,128]{1,0:T(8,128)(2,1)S(1)} %get-tuple-element.38), channel_id=1, source_target_pairs={{0,6},{1,7},{2,8},{3,9},{4,10},{5,11},{6,12},{7,13},{8,14},{9,15},... | collective-permute-start | bytes 184328 | tf_op jit(solution)/shard_map/ppermute | solution.py:52
  9.3 7.4 %collective-permute-start.3 = (bf16[240,128]{1,0:T(8,128)(2,1)S(1)}, bf16[240,128]{1,0:T(8,128)(2,1)S(1)}, u32[]{:S(2)}, u32[]{:S(2)}) collective-permute-start(bf16[240,128]{1,0:T(8,128)(2,1)S(1)} %get-tuple-element.37), channel_id=1, source_target_pairs={{0,8},{1,9},{2,10},{3,11},{4,12},{5,13},{6,14},{7,15},{8,0},{9,1},... | collective-permute-start | bytes 184328 | tf_op jit(solution)/shard_map/ppermute | solution.py:52
  10.6 8.7 %collective-permute-start.4 = (bf16[240,128]{1,0:T(8,128)(2,1)S(1)}, bf16[240,128]{1,0:T(8,128)(2,1)S(1)}, u32[]{:S(2)}, u32[]{:S(2)}) collective-permute-start(bf16[240,128]{1,0:T(8,128)(2,1)S(1)} %get-tuple-element.34), channel_id=1, source_target_pairs={{0,10},{1,11},{2,12},{3,13},{4,14},{5,15},{6,0},{7,1},{8,2},{9,3},... | collective-permute-start | bytes 184328 | tf_op jit(solution)/shard_map/ppermute | solution.py:52
  13.2 6.0 %collective-permute-start.5 = (bf16[240,128]{1,0:T(8,128)(2,1)S(1)}, bf16[240,128]{1,0:T(8,128)(2,1)S(1)}, u32[]{:S(2)}, u32[]{:S(2)}) collective-permute-start(bf16[240,128]{1,0:T(8,128)(2,1)S(1)} %get-tuple-element.36), channel_id=1, source_target_pairs={{0,12},{1,13},{2,14},{3,15},{4,0},{5,1},{6,2},{7,3},{8,4},{9,5},{1... | collective-permute-start | bytes 184328 | tf_op jit(solution)/shard_map/ppermute | solution.py:52
  14.6 4.7 %collective-permute-start.6 = (bf16[240,128]{1,0:T(8,128)(2,1)S(1)}, bf16[240,128]{1,0:T(8,128)(2,1)S(1)}, u32[]{:S(2)}, u32[]{:S(2)}) collective-permute-start(bf16[240,128]{1,0:T(8,128)(2,1)S(1)} %get-tuple-element.35), channel_id=1, source_target_pairs={{0,14},{1,15},{2,0},{3,1},{4,2},{5,3},{6,4},{7,5},{8,6},{9,7},{10,... | collective-permute-start | bytes 184328 | tf_op jit(solution)/shard_map/ppermute | solution.py:52
  16.7 4.2 %collective-permute-start.7 = (bf16[5,240,128]{2,1,0:T(8,128)(2,1)S(1)}, bf16[5,240,128]{2,1,0:T(8,128)(2,1)S(1)}, u32[]{:S(2)}, u32[]{:S(2)}) collective-permute-start(bf16[5,240,128]{2,1,0:T(8,128)(2,1)S(1)} %bitcast_dynamic-update-slice_fusion.first_ref), channel_id=1, source_target_pairs={{0,1},{1,0},{2,3},{3,2},{4,5},{5,4},{6,7},{7,6},{8,9},{9,8},{10,11... | collective-permute-start | bytes 921608 | tf_op jit(solution)/shard_map/ppermute | solution.py:47
  19.3 1.6 %collective-permute-start.8 = (bf16[3,240,128]{2,1,0:T(8,128)(2,1)S(1)}, bf16[3,240,128]{2,1,0:T(8,128)(2,1)S(1)}, u32[]{:S(2)}, u32[]{:S(2)}) collective-permute-start(bf16[3,240,128]{2,1,0:T(8,128)(2,1)S(1)} %pad_maximum_fusion.last_ref), channel_id=1, source_target_pairs={{0,1},{1,0},{2,3},{3,2},{4,5},{5,4},{6,7},{7,6},{8,9},{9,8},{10,11... | collective-permute-start | bytes 552968 | tf_op jit(solution)/shard_map/ppermute | solution.py:47
  28.0 13.1 %all-to-all-start = ((f32[16,8,128]{2,1,0:T(8,128)}), f32[16,8,128]{2,1,0:T(8,128)S(1)}, u32[]{:S(2)}, u32[]{:S(2)}) async-start(f32[16,8,128]{2,1,0:T(8,128)} %get-tuple-element.22), calls=%async_computation | async-start | bytes 131072 | tf_op jit(solution)/shard_map/all_to_all | solution.py:583
  42.1 1.6 %collective-permute-start.9 = (bf16[8,160,128]{2,1,0:T(8,128)(2,1)S(1)}, bf16[8,160,128]{2,1,0:T(8,128)(2,1)S(1)}, u32[]{:S(2)}, u32[]{:S(2)}) collective-permute-start(bf16[8,160,128]{2,1,0:T(8,128)(2,1)S(1)} %get-tuple-element.30), channel_id=1, source_target_pairs={{0,1},{1,0},{2,3},{3,2},{4,5},{5,4},{6,7},{7,6},{8,9},{9,8},{10,11... | collective-permute-start | bytes 983048 | tf_op jit(solution)/shard_map/ppermute | solution.py:47
  43.8 8.9 %collective-permute-start.10 = (bf16[160,128]{1,0:T(8,128)(2,1)S(1)}, bf16[160,128]{1,0:T(8,128)(2,1)S(1)}, u32[]{:S(2)}, u32[]{:S(2)}) collective-permute-start(bf16[160,128]{1,0:T(8,128)(2,1)S(1)} %get-tuple-element.48), channel_id=1, source_target_pairs={{0,2},{1,3},{2,4},{3,5},{4,6},{5,7},{6,8},{7,9},{8,10},{9,11},{10,... | collective-permute-start | bytes 122888 | tf_op jit(solution)/shard_map/ppermute | solution.py:52
  45.1 9.1 %collective-permute-start.11 = (bf16[160,128]{1,0:T(8,128)(2,1)S(1)}, bf16[160,128]{1,0:T(8,128)(2,1)S(1)}, u32[]{:S(2)}, u32[]{:S(2)}) collective-permute-start(bf16[160,128]{1,0:T(8,128)(2,1)S(1)} %get-tuple-element.47), channel_id=1, source_target_pairs={{0,4},{1,5},{2,6},{3,7},{4,8},{5,9},{6,10},{7,11},{8,12},{9,13},{1... | collective-permute-start | bytes 122888 | tf_op jit(solution)/shard_map/ppermute | solution.py:52
  46.5 9.1 %collective-permute-start.12 = (bf16[160,128]{1,0:T(8,128)(2,1)S(1)}, bf16[160,128]{1,0:T(8,128)(2,1)S(1)}, u32[]{:S(2)}, u32[]{:S(2)}) collective-permute-start(bf16[160,128]{1,0:T(8,128)(2,1)S(1)} %get-tuple-element.46), channel_id=1, source_target_pairs={{0,6},{1,7},{2,8},{3,9},{4,10},{5,11},{6,12},{7,13},{8,14},{9,15},... | collective-permute-start | bytes 122888 | tf_op jit(solution)/shard_map/ppermute | solution.py:52
  48.9 6.8 %collective-permute-start.13 = (bf16[160,128]{1,0:T(8,128)(2,1)S(1)}, bf16[160,128]{1,0:T(8,128)(2,1)S(1)}, u32[]{:S(2)}, u32[]{:S(2)}) collective-permute-start(bf16[160,128]{1,0:T(8,128)(2,1)S(1)} %get-tuple-element.45), channel_id=1, source_target_pairs={{0,8},{1,9},{2,10},{3,11},{4,12},{5,13},{6,14},{7,15},{8,0},{9,1},... | collective-permute-start | bytes 122888 | tf_op jit(solution)/shard_map/ppermute | solution.py:52
  50.4 5.4 %collective-permute-start.14 = (bf16[160,128]{1,0:T(8,128)(2,1)S(1)}, bf16[160,128]{1,0:T(8,128)(2,1)S(1)}, u32[]{:S(2)}, u32[]{:S(2)}) collective-permute-start(bf16[160,128]{1,0:T(8,128)(2,1)S(1)} %get-tuple-element.44), channel_id=1, source_target_pairs={{0,10},{1,11},{2,12},{3,13},{4,14},{5,15},{6,0},{7,1},{8,2},{9,3},... | collective-permute-start | bytes 122888 | tf_op jit(solution)/shard_map/ppermute | solution.py:52
  52.7 4.1 %collective-permute-start.15 = (bf16[160,128]{1,0:T(8,128)(2,1)S(1)}, bf16[160,128]{1,0:T(8,128)(2,1)S(1)}, u32[]{:S(2)}, u32[]{:S(2)}) collective-permute-start(bf16[160,128]{1,0:T(8,128)(2,1)S(1)} %get-tuple-element.43), channel_id=1, source_target_pairs={{0,12},{1,13},{2,14},{3,15},{4,0},{5,1},{6,2},{7,3},{8,4},{9,5},{1... | collective-permute-start | bytes 122888 | tf_op jit(solution)/shard_map/ppermute | solution.py:52
  54.2 4.0 %collective-permute-start.16 = (bf16[160,128]{1,0:T(8,128)(2,1)S(1)}, bf16[160,128]{1,0:T(8,128)(2,1)S(1)}, u32[]{:S(2)}, u32[]{:S(2)}) collective-permute-start(bf16[160,128]{1,0:T(8,128)(2,1)S(1)} %get-tuple-element.42), channel_id=1, source_target_pairs={{0,14},{1,15},{2,0},{3,1},{4,2},{5,3},{6,4},{7,5},{8,6},{9,7},{10,... | collective-permute-start | bytes 122888 | tf_op jit(solution)/shard_map/ppermute | solution.py:52

commit v22 on v21

--- a/solution.py
+++ b/solution.py
@@ -283,7 +283,7 @@
 
     def add(step, columns):
         logits_ref[...] += lax.dot_general(
-            hidden_ref[step], columns, (((1,), (1,)), ((), ())), preferred_element_type=jnp.float32
+            columns, hidden_ref[step], (((1,), (1,)), ((), ())), preferred_element_type=jnp.float32
         )
 
     run = stream(
@@ -337,7 +337,7 @@
     teacher_total = jnp.sum(jnp.exp(teacher_off), axis=1, keepdims=True)
     teacher_ref[...] = teacher_off
     run()
-    logits = logits_ref[...]
+    logits = logits_ref[...].T
 
     top = jnp.max(logits, axis=1, keepdims=True)
     off = logits - top
@@ -560,7 +560,7 @@
             pltpu.VMEM((chips, tokens, width), jnp.bfloat16),
             pltpu.VMEM((2 * tokens, (shard_rows + LANES // 2) // 2), jnp.float32),
             pltpu.VMEM((tokens, shard_rows), jnp.float32),
-            pltpu.VMEM((tokens, shard_rows), jnp.float32),
+            pltpu.VMEM((shard_rows, tokens), jnp.float32),
             pltpu.VMEM(stats_shape, jnp.float32),
             pltpu.SemaphoreType.DMA((chips - EARLY,)),
             rows_sem,

time: 59.2 us -> 59 us (level)
  no operation moved by 1% of the time
where the time goes in v22:
time: 59 us; the launch traced here: 58.7 us
  starting transfers between devices  32.5 us (55%)
  Pallas kernels  20 us (34%)
  waiting for transfers between devices  4.59 us (8%)
  between operations  1.43 us (2%)
    ppermute x14, starting transfers between devices, along_chips(): lax.ppermute(array, 'vocab', [(i, (i + 2 * step) % count) for i in range(...  25.7 us
    pallas_call x1, Pallas kernels, paired_shards(): pl.pallas_call(logits_kernel, out_shape=(hbm_array((3 * tokens, shard_row...  6.87 us
    all_to_all x1, starting transfers between devices, paired_shards(): lax.all_to_all(stats, 'vocab', split_axis=0, concat_axis=0, tiled=True)  6.2 us
    pallas_call x1, Pallas kernels, paired_shards(): pl.pallas_call(products_kernel, out_shape=(vmem_array((chips, width // LA...  6.18 us
    ppermute x14, waiting for transfers between devices, along_chips(): lax.ppermute(array, 'vocab', [(i, (i + 2 * step) % count) for i in range(...  3.19 us
    pallas_call x1, Pallas kernels, paired_shards(): pl.pallas_call(functools.partial(preload_kernel, chips=chips), out_shape=...  2.4 us
    pallas_call x1, Pallas kernels, paired_shards(): pl.pallas_call(functools.partial(pack_kernel, shard_rows=shard_rows), out...  1.52 us
    pallas_call x1, Pallas kernels, paired_shards(): pl.pallas_call(keep_kernel, out_shape=(vmem_array((chips, hidden_rows, LA...  1.34 us
  transfers between devices with their start and end apart: 18, of which 8 were waited for; matrix products, arithmetic and copies ran while one was open for 0% of the time, Pallas kernels for 17%

profile of v22, /device:TPU:0, one launch (start us, length us, event | category | flops | bytes accessed | tf_op | source)
XLA Modules:
  0.0 58.7 jit_solution(17405933191027262499)
XLA Ops:
  0.6 1.5 %pack.1 = (bf16[8,240,128]{2,1,0:T(8,128)(2,1)S(1)}, bf16[128,128]{1,0:T(8,128)(2,1)S(1)}, f32[64,128]{1,0:T(8,128)S(1)}) custom-call(s32[1]{0:T(128)} %bitcast.place_ref, bf16[64,320]{1,0:T(8,128)(2,1)} %refs_0_.1, bf16[4,19456]{1,0:T(4,128)(2,1)} %refs_1_.1, f32[4,608]{1,0:T(4,128)} %refs_2_.1, s32[1,64]{1,0:T(1,128)} %bitcast.49, s32[1,64]{1,0:T(1,128)} %bitcast.50, ...), custom_call_target="tpu_custom_call" | custom-call | tf_op jit(solution)/shard_map/pack/pallas_call | solution.py:512
  2.2 3.0 %collective-permute-start = (bf16[240,128]{1,0:T(8,128)(2,1)S(1)}, bf16[240,128]{1,0:T(8,128)(2,1)S(1)}, u32[]{:S(2)}, u32[]{:S(2)}) collective-permute-start(bf16[240,128]{1,0:T(8,128)(2,1)S(1)} %get-tuple-element.40), channel_id=1, source_target_pairs={{0,2},{1,3},{2,4},{3,5},{4,6},{5,7},{6,8},{7,9},{8,10},{9,11},{10,... | collective-permute-start | bytes 184328 | tf_op jit(solution)/shard_map/ppermute | solution.py:52
  5.2 1.6 %collective-permute-start.1 = (bf16[240,128]{1,0:T(8,128)(2,1)S(1)}, bf16[240,128]{1,0:T(8,128)(2,1)S(1)}, u32[]{:S(2)}, u32[]{:S(2)}) collective-permute-start(bf16[240,128]{1,0:T(8,128)(2,1)S(1)} %get-tuple-element.39), channel_id=1, source_target_pairs={{0,4},{1,5},{2,6},{3,7},{4,8},{5,9},{6,10},{7,11},{8,12},{9,13},{1... | collective-permute-start | bytes 184328 | tf_op jit(solution)/shard_map/ppermute | solution.py:52
  6.8 2.5 %collective-permute-start.2 = (bf16[240,128]{1,0:T(8,128)(2,1)S(1)}, bf16[240,128]{1,0:T(8,128)(2,1)S(1)}, u32[]{:S(2)}, u32[]{:S(2)}) collective-permute-start(bf16[240,128]{1,0:T(8,128)(2,1)S(1)} %get-tuple-element.38), channel_id=1, source_target_pairs={{0,6},{1,7},{2,8},{3,9},{4,10},{5,11},{6,12},{7,13},{8,14},{9,15},... | collective-permute-start | bytes 184328 | tf_op jit(solution)/shard_map/ppermute | solution.py:52
  9.3 1.2 %collective-permute-start.3 = (bf16[240,128]{1,0:T(8,128)(2,1)S(1)}, bf16[240,128]{1,0:T(8,128)(2,1)S(1)}, u32[]{:S(2)}, u32[]{:S(2)}) collective-permute-start(bf16[240,128]{1,0:T(8,128)(2,1)S(1)} %get-tuple-element.37), channel_id=1, source_target_pairs={{0,8},{1,9},{2,10},{3,11},{4,12},{5,13},{6,14},{7,15},{8,0},{9,1},... | collective-permute-start | bytes 184328 | tf_op jit(solution)/shard_map/ppermute | solution.py:52
  10.6 2.6 %collective-permute-start.4 = (bf16[240,128]{1,0:T(8,128)(2,1)S(1)}, bf16[240,128]{1,0:T(8,128)(2,1)S(1)}, u32[]{:S(2)}, u32[]{:S(2)}) collective-permute-start(bf16[240,128]{1,0:T(8,128)(2,1)S(1)} %get-tuple-element.34), channel_id=1, source_target_pairs={{0,10},{1,11},{2,12},{3,13},{4,14},{5,15},{6,0},{7,1},{8,2},{9,3},... | collective-permute-start | bytes 184328 | tf_op jit(solution)/shard_map/ppermute | solution.py:52
  13.2 1.3 %collective-permute-start.5 = (bf16[240,128]{1,0:T(8,128)(2,1)S(1)}, bf16[240,128]{1,0:T(8,128)(2,1)S(1)}, u32[]{:S(2)}, u32[]{:S(2)}) collective-permute-start(bf16[240,128]{1,0:T(8,128)(2,1)S(1)} %get-tuple-element.36), channel_id=1, source_target_pairs={{0,12},{1,13},{2,14},{3,15},{4,0},{5,1},{6,2},{7,3},{8,4},{9,5},{1... | collective-permute-start | bytes 184328 | tf_op jit(solution)/shard_map/ppermute | solution.py:52
  14.6 1.5 %collective-permute-start.6 = (bf16[240,128]{1,0:T(8,128)(2,1)S(1)}, bf16[240,128]{1,0:T(8,128)(2,1)S(1)}, u32[]{:S(2)}, u32[]{:S(2)}) collective-permute-start(bf16[240,128]{1,0:T(8,128)(2,1)S(1)} %get-tuple-element.35), channel_id=1, source_target_pairs={{0,14},{1,15},{2,0},{3,1},{4,2},{5,3},{6,4},{7,5},{8,6},{9,7},{10,... | collective-permute-start | bytes 184328 | tf_op jit(solution)/shard_map/ppermute | solution.py:52
  16.8 2.4 %preload.1.early_ref = bf16[3,1216,640]{2,1,0:T(8,128)(2,1)S(1)} custom-call(s32[1]{0:T(128)} %bitcast.place_ref, bf16[1216,5120]{1,0:T(8,128)(2,1)} %head_ref.5, bf16[240,128]{1,0:T(8,128)(2,1)S(1)} %collective-permute-done.2._), custom_call_target="tpu_custom_call" | custom-call | bytes 9338880 | tf_op jit(solution)/shard_map/preload/pallas_call | solution.py:532
  20.9 6.9 %logits.1 = (bf16[192,1216]{1,0:T(8,128)(2,1)}, f32[16,8,128]{2,1,0:T(8,128)}, f32[8,128]{1,0:T(8,128)S(1)}) custom-call(s32[1]{0:T(128)} %bitcast.place_ref, bf16[5,240,128]{2,1,0:T(8,128)(2,1)S(1)} %bitcast_dynamic-update-slice_fusion.first_ref, bf16[3,240,128]{2,1,0:T(8,128)(2,1)S(1)} %pad_maximum_fusion.last_ref, ...), custom_call_target="tpu_custom_call" | custom-call | flops 796917760 | bytes 12451840 | tf_op jit(solution)/shard_map/logits/pallas_call | solution.py:548
  27.8 6.2 %all-to-all-start = ((f32[16,8,128]{2,1,0:T(8,128)}), f32[16,8,128]{2,1,0:T(8,128)S(1)}, u32[]{:S(2)}, u32[]{:S(2)}) async-start(f32[16,8,128]{2,1,0:T(8,128)} %get-tuple-element.22), calls=%async_computation | async-start | bytes 131072 | tf_op jit(solution)/shard_map/all_to_all | solution.py:583
  34.0 6.2 %products.1 = (f32[8,5,2,64,128]{4,3,2,1,0:T(8,128)S(1)}, bf16[8,5,64,128]{3,2,1,0:T(8,128)(2,1)S(1)}) custom-call(s32[1]{0:T(128)} %bitcast.place_ref, bf16[192,1216]{1,0:T(8,128)(2,1)} %get-tuple-element.24.rows_ref, bf16[1216,5120]{1,0:T(8,128)(2,1)} %head_ref.5), custom_call_target="tpu_custom_call" | custom-call | flops 2390753280 | bytes 12451840 | tf_op jit(solution)/shard_map/products/pallas_call | solution.py:585
  40.9 0.9 %give.1 = (bf16[8,160,128]{2,1,0:T(8,128)(2,1)S(1)}, f32[3,64,128]{2,1,0:T(8,128)S(1)}, f32[1,1]{1,0:T(1,128)}) custom-call(s32[1]{0:T(128)} %bitcast.place_ref, f32[1]{0:T(128)S(6)} %copy.14.scale_ref, f32[16,8,128]{2,1,0:T(8,128)S(1)} %all-to-all-done.stats_ref, f32[8,128]{1,0:T(8,128)S(1)} %get-tuple-element.23.own_ref, ...), custom_call_target="tpu_custom_call" | custom-call | tf_op jit(solution)/shard_map/give/pallas_call | solution.py:602
  41.8 1.3 %keep.1 = (f32[8,160,128]{2,1,0:T(8,128)S(1)}, f32[1,1]{1,0:T(1,128)}) custom-call(s32[1]{0:T(128)} %bitcast.place_ref, f32[3,64,128]{2,1,0:T(8,128)S(1)} %get-tuple-element.27.factors_ref, f32[1,1]{1,0:T(1,128)} %get-tuple-element.28.found_ref, f32[8,5,2,64,128]{4,3,2,1,0:T(8,128)S(1)} %get-tuple-element.25.terms_ref, ...), custom_call_target="tpu_custom_call" | custom-call | flops 2621440 | bytes 2621440 | tf_op jit(solution)/shard_map/keep/pallas_call | solution.py:615
  43.6 1.3 %collective-permute-start.10 = (bf16[160,128]{1,0:T(8,128)(2,1)S(1)}, bf16[160,128]{1,0:T(8,128)(2,1)S(1)}, u32[]{:S(2)}, u32[]{:S(2)}) collective-permute-start(bf16[160,128]{1,0:T(8,128)(2,1)S(1)} %get-tuple-element.48), channel_id=1, source_target_pairs={{0,2},{1,3},{2,4},{3,5},{4,6},{5,7},{6,8},{7,9},{8,10},{9,11},{10,... | collective-permute-start | bytes 122888 | tf_op jit(solution)/shard_map/ppermute | solution.py:52
  44.8 1.5 %collective-permute-start.11 = (bf16[160,128]{1,0:T(8,128)(2,1)S(1)}, bf16[160,128]{1,0:T(8,128)(2,1)S(1)}, u32[]{:S(2)}, u32[]{:S(2)}) collective-permute-start(bf16[160,128]{1,0:T(8,128)(2,1)S(1)} %get-tuple-element.47), channel_id=1, source_target_pairs={{0,4},{1,5},{2,6},{3,7},{4,8},{5,9},{6,10},{7,11},{8,12},{9,13},{1... | collective-permute-start | bytes 122888 | tf_op jit(solution)/shard_map/ppermute | solution.py:52
  46.3 2.4 %collective-permute-start.12 = (bf16[160,128]{1,0:T(8,128)(2,1)S(1)}, bf16[160,128]{1,0:T(8,128)(2,1)S(1)}, u32[]{:S(2)}, u32[]{:S(2)}) collective-permute-start(bf16[160,128]{1,0:T(8,128)(2,1)S(1)} %get-tuple-element.46), channel_id=1, source_target_pairs={{0,6},{1,7},{2,8},{3,9},{4,10},{5,11},{6,12},{7,13},{8,14},{9,15},... | collective-permute-start | bytes 122888 | tf_op jit(solution)/shard_map/ppermute | solution.py:52
  48.7 1.5 %collective-permute-start.13 = (bf16[160,128]{1,0:T(8,128)(2,1)S(1)}, bf16[160,128]{1,0:T(8,128)(2,1)S(1)}, u32[]{:S(2)}, u32[]{:S(2)}) collective-permute-start(bf16[160,128]{1,0:T(8,128)(2,1)S(1)} %get-tuple-element.45), channel_id=1, source_target_pairs={{0,8},{1,9},{2,10},{3,11},{4,12},{5,13},{6,14},{7,15},{8,0},{9,1},... | collective-permute-start | bytes 122888 | tf_op jit(solution)/shard_map/ppermute | solution.py:52
  50.1 2.4 %collective-permute-start.14 = (bf16[160,128]{1,0:T(8,128)(2,1)S(1)}, bf16[160,128]{1,0:T(8,128)(2,1)S(1)}, u32[]{:S(2)}, u32[]{:S(2)}) collective-permute-start(bf16[160,128]{1,0:T(8,128)(2,1)S(1)} %get-tuple-element.44), channel_id=1, source_target_pairs={{0,10},{1,11},{2,12},{3,13},{4,14},{5,15},{6,0},{7,1},{8,2},{9,3},... | collective-permute-start | bytes 122888 | tf_op jit(solution)/shard_map/ppermute | solution.py:52
  52.5 1.5 %collective-permute-start.15 = (bf16[160,128]{1,0:T(8,128)(2,1)S(1)}, bf16[160,128]{1,0:T(8,128)(2,1)S(1)}, u32[]{:S(2)}, u32[]{:S(2)}) collective-permute-start(bf16[160,128]{1,0:T(8,128)(2,1)S(1)} %get-tuple-element.43), channel_id=1, source_target_pairs={{0,12},{1,13},{2,14},{3,15},{4,0},{5,1},{6,2},{7,3},{8,4},{9,5},{1... | collective-permute-start | bytes 122888 | tf_op jit(solution)/shard_map/ppermute | solution.py:52
  54.0 1.5 %collective-permute-start.16 = (bf16[160,128]{1,0:T(8,128)(2,1)S(1)}, bf16[160,128]{1,0:T(8,128)(2,1)S(1)}, u32[]{:S(2)}, u32[]{:S(2)}) collective-permute-start(bf16[160,128]{1,0:T(8,128)(2,1)S(1)} %get-tuple-element.42), channel_id=1, source_target_pairs={{0,14},{1,15},{2,0},{3,1},{4,2},{5,3},{6,4},{7,5},{8,6},{9,7},{10,... | collective-permute-start | bytes 122888 | tf_op jit(solution)/shard_map/ppermute | solution.py:52
  55.6 1.0 %collective-permute-done.15.refs_5_ = bf16[160,128]{1,0:T(8,128)(2,1)S(1)} collective-permute-done((bf16[160,128]{1,0:T(8,128)(2,1)S(1)}, bf16[160,128]{1,0:T(8,128)(2,1)S(1)}, u32[]{:S(2)}, u32[]{:S(2)}) %collective-permute-start.15) | collective-permute-done | bytes 40992 | tf_op jit(solution)/shard_map/ppermute | solution.py:52
  56.6 1.4 %collective-permute-done.16.refs_6_ = bf16[160,128]{1,0:T(8,128)(2,1)S(1)} collective-permute-done((bf16[160,128]{1,0:T(8,128)(2,1)S(1)}, bf16[160,128]{1,0:T(8,128)(2,1)S(1)}, u32[]{:S(2)}, u32[]{:S(2)}) %collective-permute-start.16) | collective-permute-done | bytes 40992 | tf_op jit(solution)/shard_map/ppermute | solution.py:52
  58.0 0.8 %total.1 = bf16[64,320]{1,0:T(8,128)(2,1)} custom-call(s32[1]{0:T(128)} %bitcast.place_ref, f32[160,128]{1,0:T(8,128)S(1)} %slice_bitcast_fusion.own_ref, bf16[160,128]{1,0:T(8,128)(2,1)S(1)} %collective-permute-done.10.refs_0_, bf16[160,128]{1,0:T(8,128)(2,1)S(1)} %collective-permute-done.11.refs_1_, bf16[160,128]{1,0:T(8,128)(2,1)S(1)} %collective-permute-done.12.refs_2_, ...), custom_call_target="tpu_custom_call" | custom-call | tf_op jit(solution)/shard_map/total/pallas_call | solution.py:631
  (28 shorter events, 3.0 us)
Async XLA Ops:
  2.2 11.0 %collective-permute-start = (bf16[240,128]{1,0:T(8,128)(2,1)S(1)}, bf16[240,128]{1,0:T(8,128)(2,1)S(1)}, u32[]{:S(2)}, u32[]{:S(2)}) collective-permute-start(bf16[240,128]{1,0:T(8,128)(2,1)S(1)} %get-tuple-element.40), channel_id=1, source_target_pairs={{0,2},{1,3},{2,4},{3,5},{4,6},{5,7},{6,8},{7,9},{8,10},{9,11},{10,... | collective-permute-start | bytes 184328 | tf_op jit(solution)/shard_map/ppermute | solution.py:52
  5.2 9.4 %collective-permute-start.1 = (bf16[240,128]{1,0:T(8,128)(2,1)S(1)}, bf16[240,128]{1,0:T(8,128)(2,1)S(1)}, u32[]{:S(2)}, u32[]{:S(2)}) collective-permute-start(bf16[240,128]{1,0:T(8,128)(2,1)S(1)} %get-tuple-element.39), channel_id=1, source_target_pairs={{0,4},{1,5},{2,6},{3,7},{4,8},{5,9},{6,10},{7,11},{8,12},{9,13},{1... | collective-permute-start | bytes 184328 | tf_op jit(solution)/shard_map/ppermute | solution.py:52
  6.8 9.4 %collective-permute-start.2 = (bf16[240,128]{1,0:T(8,128)(2,1)S(1)}, bf16[240,128]{1,0:T(8,128)(2,1)S(1)}, u32[]{:S(2)}, u32[]{:S(2)}) collective-permute-start(bf16[240,128]{1,0:T(8,128)(2,1)S(1)} %get-tuple-element.38), channel_id=1, source_target_pairs={{0,6},{1,7},{2,8},{3,9},{4,10},{5,11},{6,12},{7,13},{8,14},{9,15},... | collective-permute-start | bytes 184328 | tf_op jit(solution)/shard_map/ppermute | solution.py:52
  9.3 7.4 %collective-permute-start.3 = (bf16[240,128]{1,0:T(8,128)(2,1)S(1)}, bf16[240,128]{1,0:T(8,128)(2,1)S(1)}, u32[]{:S(2)}, u32[]{:S(2)}) collective-permute-start(bf16[240,128]{1,0:T(8,128)(2,1)S(1)} %get-tuple-element.37), channel_id=1, source_target_pairs={{0,8},{1,9},{2,10},{3,11},{4,12},{5,13},{6,14},{7,15},{8,0},{9,1},... | collective-permute-start | bytes 184328 | tf_op jit(solution)/shard_map/ppermute | solution.py:52
  10.6 8.7 %collective-permute-start.4 = (bf16[240,128]{1,0:T(8,128)(2,1)S(1)}, bf16[240,128]{1,0:T(8,128)(2,1)S(1)}, u32[]{:S(2)}, u32[]{:S(2)}) collective-permute-start(bf16[240,128]{1,0:T(8,128)(2,1)S(1)} %get-tuple-element.34), channel_id=1, source_target_pairs={{0,10},{1,11},{2,12},{3,13},{4,14},{5,15},{6,0},{7,1},{8,2},{9,3},... | collective-permute-start | bytes 184328 | tf_op jit(solution)/shard_map/ppermute | solution.py:52
  13.2 6.0 %collective-permute-start.5 = (bf16[240,128]{1,0:T(8,128)(2,1)S(1)}, bf16[240,128]{1,0:T(8,128)(2,1)S(1)}, u32[]{:S(2)}, u32[]{:S(2)}) collective-permute-start(bf16[240,128]{1,0:T(8,128)(2,1)S(1)} %get-tuple-element.36), channel_id=1, source_target_pairs={{0,12},{1,13},{2,14},{3,15},{4,0},{5,1},{6,2},{7,3},{8,4},{9,5},{1... | collective-permute-start | bytes 184328 | tf_op jit(solution)/shard_map/ppermute | solution.py:52
  14.6 4.7 %collective-permute-start.6 = (bf16[240,128]{1,0:T(8,128)(2,1)S(1)}, bf16[240,128]{1,0:T(8,128)(2,1)S(1)}, u32[]{:S(2)}, u32[]{:S(2)}) collective-permute-start(bf16[240,128]{1,0:T(8,128)(2,1)S(1)} %get-tuple-element.35), channel_id=1, source_target_pairs={{0,14},{1,15},{2,0},{3,1},{4,2},{5,3},{6,4},{7,5},{8,6},{9,7},{10,... | collective-permute-start | bytes 184328 | tf_op jit(solution)/shard_map/ppermute | solution.py:52
  16.7 4.2 %collective-permute-start.7 = (bf16[5,240,128]{2,1,0:T(8,128)(2,1)S(1)}, bf16[5,240,128]{2,1,0:T(8,128)(2,1)S(1)}, u32[]{:S(2)}, u32[]{:S(2)}) collective-permute-start(bf16[5,240,128]{2,1,0:T(8,128)(2,1)S(1)} %bitcast_dynamic-update-slice_fusion.first_ref), channel_id=1, source_target_pairs={{0,1},{1,0},{2,3},{3,2},{4,5},{5,4},{6,7},{7,6},{8,9},{9,8},{10,11... | collective-permute-start | bytes 921608 | tf_op jit(solution)/shard_map/ppermute | solution.py:47
  19.3 1.6 %collective-permute-start.8 = (bf16[3,240,128]{2,1,0:T(8,128)(2,1)S(1)}, bf16[3,240,128]{2,1,0:T(8,128)(2,1)S(1)}, u32[]{:S(2)}, u32[]{:S(2)}) collective-permute-start(bf16[3,240,128]{2,1,0:T(8,128)(2,1)S(1)} %pad_maximum_fusion.last_ref), channel_id=1, source_target_pairs={{0,1},{1,0},{2,3},{3,2},{4,5},{5,4},{6,7},{7,6},{8,9},{9,8},{10,11... | collective-permute-start | bytes 552968 | tf_op jit(solution)/shard_map/ppermute | solution.py:47
  27.8 13.1 %all-to-all-start = ((f32[16,8,128]{2,1,0:T(8,128)}), f32[16,8,128]{2,1,0:T(8,128)S(1)}, u32[]{:S(2)}, u32[]{:S(2)}) async-start(f32[16,8,128]{2,1,0:T(8,128)} %get-tuple-element.22), calls=%async_computation | async-start | bytes 131072 | tf_op jit(solution)/shard_map/all_to_all | solution.py:583
  41.8 1.6 %collective-permute-start.9 = (bf16[8,160,128]{2,1,0:T(8,128)(2,1)S(1)}, bf16[8,160,128]{2,1,0:T(8,128)(2,1)S(1)}, u32[]{:S(2)}, u32[]{:S(2)}) collective-permute-start(bf16[8,160,128]{2,1,0:T(8,128)(2,1)S(1)} %get-tuple-element.30), channel_id=1, source_target_pairs={{0,1},{1,0},{2,3},{3,2},{4,5},{5,4},{6,7},{7,6},{8,9},{9,8},{10,11... | collective-permute-start | bytes 983048 | tf_op jit(solution)/shard_map/ppermute | solution.py:47
  43.6 8.9 %collective-permute-start.10 = (bf16[160,128]{1,0:T(8,128)(2,1)S(1)}, bf16[160,128]{1,0:T(8,128)(2,1)S(1)}, u32[]{:S(2)}, u32[]{:S(2)}) collective-permute-start(bf16[160,128]{1,0:T(8,128)(2,1)S(1)} %get-tuple-element.48), channel_id=1, source_target_pairs={{0,2},{1,3},{2,4},{3,5},{4,6},{5,7},{6,8},{7,9},{8,10},{9,11},{10,... | collective-permute-start | bytes 122888 | tf_op jit(solution)/shard_map/ppermute | solution.py:52
  44.8 9.1 %collective-permute-start.11 = (bf16[160,128]{1,0:T(8,128)(2,1)S(1)}, bf16[160,128]{1,0:T(8,128)(2,1)S(1)}, u32[]{:S(2)}, u32[]{:S(2)}) collective-permute-start(bf16[160,128]{1,0:T(8,128)(2,1)S(1)} %get-tuple-element.47), channel_id=1, source_target_pairs={{0,4},{1,5},{2,6},{3,7},{4,8},{5,9},{6,10},{7,11},{8,12},{9,13},{1... | collective-permute-start | bytes 122888 | tf_op jit(solution)/shard_map/ppermute | solution.py:52
  46.3 9.1 %collective-permute-start.12 = (bf16[160,128]{1,0:T(8,128)(2,1)S(1)}, bf16[160,128]{1,0:T(8,128)(2,1)S(1)}, u32[]{:S(2)}, u32[]{:S(2)}) collective-permute-start(bf16[160,128]{1,0:T(8,128)(2,1)S(1)} %get-tuple-element.46), channel_id=1, source_target_pairs={{0,6},{1,7},{2,8},{3,9},{4,10},{5,11},{6,12},{7,13},{8,14},{9,15},... | collective-permute-start | bytes 122888 | tf_op jit(solution)/shard_map/ppermute | solution.py:52
  48.7 6.8 %collective-permute-start.13 = (bf16[160,128]{1,0:T(8,128)(2,1)S(1)}, bf16[160,128]{1,0:T(8,128)(2,1)S(1)}, u32[]{:S(2)}, u32[]{:S(2)}) collective-permute-start(bf16[160,128]{1,0:T(8,128)(2,1)S(1)} %get-tuple-element.45), channel_id=1, source_target_pairs={{0,8},{1,9},{2,10},{3,11},{4,12},{5,13},{6,14},{7,15},{8,0},{9,1},... | collective-permute-start | bytes 122888 | tf_op jit(solution)/shard_map/ppermute | solution.py:52
  50.1 5.4 %collective-permute-start.14 = (bf16[160,128]{1,0:T(8,128)(2,1)S(1)}, bf16[160,128]{1,0:T(8,128)(2,1)S(1)}, u32[]{:S(2)}, u32[]{:S(2)}) collective-permute-start(bf16[160,128]{1,0:T(8,128)(2,1)S(1)} %get-tuple-element.44), channel_id=1, source_target_pairs={{0,10},{1,11},{2,12},{3,13},{4,14},{5,15},{6,0},{7,1},{8,2},{9,3},... | collective-permute-start | bytes 122888 | tf_op jit(solution)/shard_map/ppermute | solution.py:52
  52.5 4.1 %collective-permute-start.15 = (bf16[160,128]{1,0:T(8,128)(2,1)S(1)}, bf16[160,128]{1,0:T(8,128)(2,1)S(1)}, u32[]{:S(2)}, u32[]{:S(2)}) collective-permute-start(bf16[160,128]{1,0:T(8,128)(2,1)S(1)} %get-tuple-element.43), channel_id=1, source_target_pairs={{0,12},{1,13},{2,14},{3,15},{4,0},{5,1},{6,2},{7,3},{8,4},{9,5},{1... | collective-permute-start | bytes 122888 | tf_op jit(solution)/shard_map/ppermute | solution.py:52
  54.0 4.0 %collective-permute-start.16 = (bf16[160,128]{1,0:T(8,128)(2,1)S(1)}, bf16[160,128]{1,0:T(8,128)(2,1)S(1)}, u32[]{:S(2)}, u32[]{:S(2)}) collective-permute-start(bf16[160,128]{1,0:T(8,128)(2,1)S(1)} %get-tuple-element.42), channel_id=1, source_target_pairs={{0,14},{1,15},{2,0},{3,1},{4,2},{5,3},{6,4},{7,5},{8,6},{9,7},{10,... | collective-permute-start | bytes 122888 | tf_op jit(solution)/shard_map/ppermute | solution.py:52

commit v23 on v22

--- a/solution.py
+++ b/solution.py
@@ -296,7 +296,7 @@
     )
 
     def unpack(near_ref, far_ref, base):
-        def body(place, _):
+        for place in range(near_ref.shape[0]):
             step = place + base
             blocks = near_ref.at[place], far_ref.at[place]
             for block, parity in zip(blocks, (core, 1 - core)):
@@ -318,8 +318,6 @@
             tile = [jnp.where(low, one, two), turned(jnp.where(low, two, one))]
             tile = jnp.concatenate(tile, axis=0).astype(jnp.bfloat16)
             hidden_ref[step, :, 2 * LANES : 3 * LANES] = tile
-
-        lax.fori_loop(0, near_ref.shape[0], body, None)
 
     unpack(first_ref, first_far_ref, 0)
     unpack(last_ref, last_far_ref, first_ref.shape[0])

time: 59 us -> 58.5 us (level)
  no operation moved by 1% of the time
where the time goes in v23:
time: 58.5 us; the launch traced here: 58.3 us
  starting transfers between devices  32.5 us (56%)
  Pallas kernels  19.6 us (34%)
  waiting for transfers between devices  4.59 us (8%)
  between operations  1.43 us (2%)
    ppermute x14, starting transfers between devices, along_chips(): lax.ppermute(array, 'vocab', [(i, (i + 2 * step) % count) for i in range(...  25.7 us
    pallas_call x1, Pallas kernels, paired_shards(): pl.pallas_call(logits_kernel, out_shape=(hbm_array((3 * tokens, shard_row...  6.43 us
    all_to_all x1, starting transfers between devices, paired_shards(): lax.all_to_all(stats, 'vocab', split_axis=0, concat_axis=0, tiled=True)  6.2 us
    pallas_call x1, Pallas kernels, paired_shards(): pl.pallas_call(products_kernel, out_shape=(vmem_array((chips, width // LA...  6.18 us
    ppermute x14, waiting for transfers between devices, along_chips(): lax.ppermute(array, 'vocab', [(i, (i + 2 * step) % count) for i in range(...  3.19 us
    pallas_call x1, Pallas kernels, paired_shards(): pl.pallas_call(functools.partial(preload_kernel, chips=chips), out_shape=...  2.4 us
    pallas_call x1, Pallas kernels, paired_shards(): pl.pallas_call(functools.partial(pack_kernel, shard_rows=shard_rows), out...  1.52 us
    pallas_call x1, Pallas kernels, paired_shards(): pl.pallas_call(keep_kernel, out_shape=(vmem_array((chips, hidden_rows, LA...  1.34 us
  transfers between devices with their start and end apart: 18, of which 8 were waited for; matrix products, arithmetic and copies ran while one was open for 0% of the time, Pallas kernels for 17%

profile of v23, /device:TPU:0, one launch (start us, length us, event | category | flops | bytes accessed | tf_op | source)
XLA Modules:
  0.0 58.3 jit_solution(6695637493933626595)
XLA Ops:
  0.6 1.5 %pack.1 = (bf16[8,240,128]{2,1,0:T(8,128)(2,1)S(1)}, bf16[128,128]{1,0:T(8,128)(2,1)S(1)}, f32[64,128]{1,0:T(8,128)S(1)}) custom-call(s32[1]{0:T(128)} %bitcast.place_ref, bf16[64,320]{1,0:T(8,128)(2,1)} %refs_0_.1, bf16[4,19456]{1,0:T(4,128)(2,1)} %refs_1_.1, f32[4,608]{1,0:T(4,128)} %refs_2_.1, s32[1,64]{1,0:T(1,128)} %bitcast.49, s32[1,64]{1,0:T(1,128)} %bitcast.50, ...), custom_call_target="tpu_custom_call" | custom-call | tf_op jit(solution)/shard_map/pack/pallas_call | solution.py:510
  2.2 3.0 %collective-permute-start = (bf16[240,128]{1,0:T(8,128)(2,1)S(1)}, bf16[240,128]{1,0:T(8,128)(2,1)S(1)}, u32[]{:S(2)}, u32[]{:S(2)}) collective-permute-start(bf16[240,128]{1,0:T(8,128)(2,1)S(1)} %get-tuple-element.40), channel_id=1, source_target_pairs={{0,2},{1,3},{2,4},{3,5},{4,6},{5,7},{6,8},{7,9},{8,10},{9,11},{10,... | collective-permute-start | bytes 184328 | tf_op jit(solution)/shard_map/ppermute | solution.py:52
  5.2 1.6 %collective-permute-start.1 = (bf16[240,128]{1,0:T(8,128)(2,1)S(1)}, bf16[240,128]{1,0:T(8,128)(2,1)S(1)}, u32[]{:S(2)}, u32[]{:S(2)}) collective-permute-start(bf16[240,128]{1,0:T(8,128)(2,1)S(1)} %get-tuple-element.39), channel_id=1, source_target_pairs={{0,4},{1,5},{2,6},{3,7},{4,8},{5,9},{6,10},{7,11},{8,12},{9,13},{1... | collective-permute-start | bytes 184328 | tf_op jit(solution)/shard_map/ppermute | solution.py:52
  6.8 2.5 %collective-permute-start.2 = (bf16[240,128]{1,0:T(8,128)(2,1)S(1)}, bf16[240,128]{1,0:T(8,128)(2,1)S(1)}, u32[]{:S(2)}, u32[]{:S(2)}) collective-permute-start(bf16[240,128]{1,0:T(8,128)(2,1)S(1)} %get-tuple-element.38), channel_id=1, source_target_pairs={{0,6},{1,7},{2,8},{3,9},{4,10},{5,11},{6,12},{7,13},{8,14},{9,15},... | collective-permute-start | bytes 184328 | tf_op jit(solution)/shard_map/ppermute | solution.py:52
  9.3 1.2 %collective-permute-start.3 = (bf16[240,128]{1,0:T(8,128)(2,1)S(1)}, bf16[240,128]{1,0:T(8,128)(2,1)S(1)}, u32[]{:S(2)}, u32[]{:S(2)}) collective-permute-start(bf16[240,128]{1,0:T(8,128)(2,1)S(1)} %get-tuple-element.37), channel_id=1, source_target_pairs={{0,8},{1,9},{2,10},{3,11},{4,12},{5,13},{6,14},{7,15},{8,0},{9,1},... | collective-permute-start | bytes 184328 | tf_op jit(solution)/shard_map/ppermute | solution.py:52
  10.6 2.6 %collective-permute-start.4 = (bf16[240,128]{1,0:T(8,128)(2,1)S(1)}, bf16[240,128]{1,0:T(8,128)(2,1)S(1)}, u32[]{:S(2)}, u32[]{:S(2)}) collective-permute-start(bf16[240,128]{1,0:T(8,128)(2,1)S(1)} %get-tuple-element.34), channel_id=1, source_target_pairs={{0,10},{1,11},{2,12},{3,13},{4,14},{5,15},{6,0},{7,1},{8,2},{9,3},... | collective-permute-start | bytes 184328 | tf_op jit(solution)/shard_map/ppermute | solution.py:52
  13.2 1.3 %collective-permute-start.5 = (bf16[240,128]{1,0:T(8,128)(2,1)S(1)}, bf16[240,128]{1,0:T(8,128)(2,1)S(1)}, u32[]{:S(2)}, u32[]{:S(2)}) collective-permute-start(bf16[240,128]{1,0:T(8,128)(2,1)S(1)} %get-tuple-element.36), channel_id=1, source_target_pairs={{0,12},{1,13},{2,14},{3,15},{4,0},{5,1},{6,2},{7,3},{8,4},{9,5},{1... | collective-permute-start | bytes 184328 | tf_op jit(solution)/shard_map/ppermute | solution.py:52
  14.6 1.5 %collective-permute-start.6 = (bf16[240,128]{1,0:T(8,128)(2,1)S(1)}, bf16[240,128]{1,0:T(8,128)(2,1)S(1)}, u32[]{:S(2)}, u32[]{:S(2)}) collective-permute-start(bf16[240,128]{1,0:T(8,128)(2,1)S(1)} %get-tuple-element.35), channel_id=1, source_target_pairs={{0,14},{1,15},{2,0},{3,1},{4,2},{5,3},{6,4},{7,5},{8,6},{9,7},{10,... | collective-permute-start | bytes 184328 | tf_op jit(solution)/shard_map/ppermute | solution.py:52
  16.8 2.4 %preload.1.early_ref = bf16[3,1216,640]{2,1,0:T(8,128)(2,1)S(1)} custom-call(s32[1]{0:T(128)} %bitcast.place_ref, bf16[1216,5120]{1,0:T(8,128)(2,1)} %head_ref.5, bf16[240,128]{1,0:T(8,128)(2,1)S(1)} %collective-permute-done.2._), custom_call_target="tpu_custom_call" | custom-call | bytes 9338880 | tf_op jit(solution)/shard_map/preload/pallas_call | solution.py:530
  20.9 6.4 %logits.1 = (bf16[192,1216]{1,0:T(8,128)(2,1)}, f32[16,8,128]{2,1,0:T(8,128)}, f32[8,128]{1,0:T(8,128)S(1)}) custom-call(s32[1]{0:T(128)} %bitcast.place_ref, bf16[5,240,128]{2,1,0:T(8,128)(2,1)S(1)} %bitcast_dynamic-update-slice_fusion.first_ref, bf16[3,240,128]{2,1,0:T(8,128)(2,1)S(1)} %pad_maximum_fusion.last_ref, ...), custom_call_target="tpu_custom_call" | custom-call | flops 796917760 | bytes 12451840 | tf_op jit(solution)/shard_map/logits/pallas_call | solution.py:546
  27.3 6.2 %all-to-all-start = ((f32[16,8,128]{2,1,0:T(8,128)}), f32[16,8,128]{2,1,0:T(8,128)S(1)}, u32[]{:S(2)}, u32[]{:S(2)}) async-start(f32[16,8,128]{2,1,0:T(8,128)} %get-tuple-element.22), calls=%async_computation | async-start | bytes 131072 | tf_op jit(solution)/shard_map/all_to_all | solution.py:581
  33.5 6.2 %products.1 = (f32[8,5,2,64,128]{4,3,2,1,0:T(8,128)S(1)}, bf16[8,5,64,128]{3,2,1,0:T(8,128)(2,1)S(1)}) custom-call(s32[1]{0:T(128)} %bitcast.place_ref, bf16[192,1216]{1,0:T(8,128)(2,1)} %get-tuple-element.24.rows_ref, bf16[1216,5120]{1,0:T(8,128)(2,1)} %head_ref.5), custom_call_target="tpu_custom_call" | custom-call | flops 2390753280 | bytes 12451840 | tf_op jit(solution)/shard_map/products/pallas_call | solution.py:583
  40.4 0.9 %give.1 = (bf16[8,160,128]{2,1,0:T(8,128)(2,1)S(1)}, f32[3,64,128]{2,1,0:T(8,128)S(1)}, f32[1,1]{1,0:T(1,128)}) custom-call(s32[1]{0:T(128)} %bitcast.place_ref, f32[1]{0:T(128)S(6)} %copy.14.scale_ref, f32[16,8,128]{2,1,0:T(8,128)S(1)} %all-to-all-done.stats_ref, f32[8,128]{1,0:T(8,128)S(1)} %get-tuple-element.23.own_ref, ...), custom_call_target="tpu_custom_call" | custom-call | tf_op jit(solution)/shard_map/give/pallas_call | solution.py:600
  41.4 1.3 %keep.1 = (f32[8,160,128]{2,1,0:T(8,128)S(1)}, f32[1,1]{1,0:T(1,128)}) custom-call(s32[1]{0:T(128)} %bitcast.place_ref, f32[3,64,128]{2,1,0:T(8,128)S(1)} %get-tuple-element.27.factors_ref, f32[1,1]{1,0:T(1,128)} %get-tuple-element.28.found_ref, f32[8,5,2,64,128]{4,3,2,1,0:T(8,128)S(1)} %get-tuple-element.25.terms_ref, ...), custom_call_target="tpu_custom_call" | custom-call | flops 2621440 | bytes 2621440 | tf_op jit(solution)/shard_map/keep/pallas_call | solution.py:613
  43.1 1.3 %collective-permute-start.10 = (bf16[160,128]{1,0:T(8,128)(2,1)S(1)}, bf16[160,128]{1,0:T(8,128)(2,1)S(1)}, u32[]{:S(2)}, u32[]{:S(2)}) collective-permute-start(bf16[160,128]{1,0:T(8,128)(2,1)S(1)} %get-tuple-element.48), channel_id=1, source_target_pairs={{0,2},{1,3},{2,4},{3,5},{4,6},{5,7},{6,8},{7,9},{8,10},{9,11},{10,... | collective-permute-start | bytes 122888 | tf_op jit(solution)/shard_map/ppermute | solution.py:52
  44.4 1.5 %collective-permute-start.11 = (bf16[160,128]{1,0:T(8,128)(2,1)S(1)}, bf16[160,128]{1,0:T(8,128)(2,1)S(1)}, u32[]{:S(2)}, u32[]{:S(2)}) collective-permute-start(bf16[160,128]{1,0:T(8,128)(2,1)S(1)} %get-tuple-element.47), channel_id=1, source_target_pairs={{0,4},{1,5},{2,6},{3,7},{4,8},{5,9},{6,10},{7,11},{8,12},{9,13},{1... | collective-permute-start | bytes 122888 | tf_op jit(solution)/shard_map/ppermute | solution.py:52
  45.9 2.4 %collective-permute-start.12 = (bf16[160,128]{1,0:T(8,128)(2,1)S(1)}, bf16[160,128]{1,0:T(8,128)(2,1)S(1)}, u32[]{:S(2)}, u32[]{:S(2)}) collective-permute-start(bf16[160,128]{1,0:T(8,128)(2,1)S(1)} %get-tuple-element.46), channel_id=1, source_target_pairs={{0,6},{1,7},{2,8},{3,9},{4,10},{5,11},{6,12},{7,13},{8,14},{9,15},... | collective-permute-start | bytes 122888 | tf_op jit(solution)/shard_map/ppermute | solution.py:52
  48.2 1.5 %collective-permute-start.13 = (bf16[160,128]{1,0:T(8,128)(2,1)S(1)}, bf16[160,128]{1,0:T(8,128)(2,1)S(1)}, u32[]{:S(2)}, u32[]{:S(2)}) collective-permute-start(bf16[160,128]{1,0:T(8,128)(2,1)S(1)} %get-tuple-element.45), channel_id=1, source_target_pairs={{0,8},{1,9},{2,10},{3,11},{4,12},{5,13},{6,14},{7,15},{8,0},{9,1},... | collective-permute-start | bytes 122888 | tf_op jit(solution)/shard_map/ppermute | solution.py:52
  49.7 2.4 %collective-permute-start.14 = (bf16[160,128]{1,0:T(8,128)(2,1)S(1)}, bf16[160,128]{1,0:T(8,128)(2,1)S(1)}, u32[]{:S(2)}, u32[]{:S(2)}) collective-permute-start(bf16[160,128]{1,0:T(8,128)(2,1)S(1)} %get-tuple-element.44), channel_id=1, source_target_pairs={{0,10},{1,11},{2,12},{3,13},{4,14},{5,15},{6,0},{7,1},{8,2},{9,3},... | collective-permute-start | bytes 122888 | tf_op jit(solution)/shard_map/ppermute | solution.py:52
  52.1 1.5 %collective-permute-start.15 = (bf16[160,128]{1,0:T(8,128)(2,1)S(1)}, bf16[160,128]{1,0:T(8,128)(2,1)S(1)}, u32[]{:S(2)}, u32[]{:S(2)}) collective-permute-start(bf16[160,128]{1,0:T(8,128)(2,1)S(1)} %get-tuple-element.43), channel_id=1, source_target_pairs={{0,12},{1,13},{2,14},{3,15},{4,0},{5,1},{6,2},{7,3},{8,4},{9,5},{1... | collective-permute-start | bytes 122888 | tf_op jit(solution)/shard_map/ppermute | solution.py:52
  53.5 1.5 %collective-permute-start.16 = (bf16[160,128]{1,0:T(8,128)(2,1)S(1)}, bf16[160,128]{1,0:T(8,128)(2,1)S(1)}, u32[]{:S(2)}, u32[]{:S(2)}) collective-permute-start(bf16[160,128]{1,0:T(8,128)(2,1)S(1)} %get-tuple-element.42), channel_id=1, source_target_pairs={{0,14},{1,15},{2,0},{3,1},{4,2},{5,3},{6,4},{7,5},{8,6},{9,7},{10,... | collective-permute-start | bytes 122888 | tf_op jit(solution)/shard_map/ppermute | solution.py:52
  55.1 1.0 %collective-permute-done.15.refs_5_ = bf16[160,128]{1,0:T(8,128)(2,1)S(1)} collective-permute-done((bf16[160,128]{1,0:T(8,128)(2,1)S(1)}, bf16[160,128]{1,0:T(8,128)(2,1)S(1)}, u32[]{:S(2)}, u32[]{:S(2)}) %collective-permute-start.15) | collective-permute-done | bytes 40992 | tf_op jit(solution)/shard_map/ppermute | solution.py:52
  56.2 1.4 %collective-permute-done.16.refs_6_ = bf16[160,128]{1,0:T(8,128)(2,1)S(1)} collective-permute-done((bf16[160,128]{1,0:T(8,128)(2,1)S(1)}, bf16[160,128]{1,0:T(8,128)(2,1)S(1)}, u32[]{:S(2)}, u32[]{:S(2)}) %collective-permute-start.16) | collective-permute-done | bytes 40992 | tf_op jit(solution)/shard_map/ppermute | solution.py:52
  57.5 0.8 %total.1 = bf16[64,320]{1,0:T(8,128)(2,1)} custom-call(s32[1]{0:T(128)} %bitcast.place_ref, f32[160,128]{1,0:T(8,128)S(1)} %slice_bitcast_fusion.own_ref, bf16[160,128]{1,0:T(8,128)(2,1)S(1)} %collective-permute-done.10.refs_0_, bf16[160,128]{1,0:T(8,128)(2,1)S(1)} %collective-permute-done.11.refs_1_, bf16[160,128]{1,0:T(8,128)(2,1)S(1)} %collective-permute-done.12.refs_2_, ...), custom_call_target="tpu_custom_call" | custom-call | tf_op jit(solution)/shard_map/total/pallas_call | solution.py:629
  (28 shorter events, 3.1 us)
Async XLA Ops:
  2.2 11.0 %collective-permute-start = (bf16[240,128]{1,0:T(8,128)(2,1)S(1)}, bf16[240,128]{1,0:T(8,128)(2,1)S(1)}, u32[]{:S(2)}, u32[]{:S(2)}) collective-permute-start(bf16[240,128]{1,0:T(8,128)(2,1)S(1)} %get-tuple-element.40), channel_id=1, source_target_pairs={{0,2},{1,3},{2,4},{3,5},{4,6},{5,7},{6,8},{7,9},{8,10},{9,11},{10,... | collective-permute-start | bytes 184328 | tf_op jit(solution)/shard_map/ppermute | solution.py:52
  5.2 9.4 %collective-permute-start.1 = (bf16[240,128]{1,0:T(8,128)(2,1)S(1)}, bf16[240,128]{1,0:T(8,128)(2,1)S(1)}, u32[]{:S(2)}, u32[]{:S(2)}) collective-permute-start(bf16[240,128]{1,0:T(8,128)(2,1)S(1)} %get-tuple-element.39), channel_id=1, source_target_pairs={{0,4},{1,5},{2,6},{3,7},{4,8},{5,9},{6,10},{7,11},{8,12},{9,13},{1... | collective-permute-start | bytes 184328 | tf_op jit(solution)/shard_map/ppermute | solution.py:52
  6.8 9.4 %collective-permute-start.2 = (bf16[240,128]{1,0:T(8,128)(2,1)S(1)}, bf16[240,128]{1,0:T(8,128)(2,1)S(1)}, u32[]{:S(2)}, u32[]{:S(2)}) collective-permute-start(bf16[240,128]{1,0:T(8,128)(2,1)S(1)} %get-tuple-element.38), channel_id=1, source_target_pairs={{0,6},{1,7},{2,8},{3,9},{4,10},{5,11},{6,12},{7,13},{8,14},{9,15},... | collective-permute-start | bytes 184328 | tf_op jit(solution)/shard_map/ppermute | solution.py:52
  9.3 7.4 %collective-permute-start.3 = (bf16[240,128]{1,0:T(8,128)(2,1)S(1)}, bf16[240,128]{1,0:T(8,128)(2,1)S(1)}, u32[]{:S(2)}, u32[]{:S(2)}) collective-permute-start(bf16[240,128]{1,0:T(8,128)(2,1)S(1)} %get-tuple-element.37), channel_id=1, source_target_pairs={{0,8},{1,9},{2,10},{3,11},{4,12},{5,13},{6,14},{7,15},{8,0},{9,1},... | collective-permute-start | bytes 184328 | tf_op jit(solution)/shard_map/ppermute | solution.py:52
  10.6 8.7 %collective-permute-start.4 = (bf16[240,128]{1,0:T(8,128)(2,1)S(1)}, bf16[240,128]{1,0:T(8,128)(2,1)S(1)}, u32[]{:S(2)}, u32[]{:S(2)}) collective-permute-start(bf16[240,128]{1,0:T(8,128)(2,1)S(1)} %get-tuple-element.34), channel_id=1, source_target_pairs={{0,10},{1,11},{2,12},{3,13},{4,14},{5,15},{6,0},{7,1},{8,2},{9,3},... | collective-permute-start | bytes 184328 | tf_op jit(solution)/shard_map/ppermute | solution.py:52
  13.2 6.0 %collective-permute-start.5 = (bf16[240,128]{1,0:T(8,128)(2,1)S(1)}, bf16[240,128]{1,0:T(8,128)(2,1)S(1)}, u32[]{:S(2)}, u32[]{:S(2)}) collective-permute-start(bf16[240,128]{1,0:T(8,128)(2,1)S(1)} %get-tuple-element.36), channel_id=1, source_target_pairs={{0,12},{1,13},{2,14},{3,15},{4,0},{5,1},{6,2},{7,3},{8,4},{9,5},{1... | collective-permute-start | bytes 184328 | tf_op jit(solution)/shard_map/ppermute | solution.py:52
  14.6 4.7 %collective-permute-start.6 = (bf16[240,128]{1,0:T(8,128)(2,1)S(1)}, bf16[240,128]{1,0:T(8,128)(2,1)S(1)}, u32[]{:S(2)}, u32[]{:S(2)}) collective-permute-start(bf16[240,128]{1,0:T(8,128)(2,1)S(1)} %get-tuple-element.35), channel_id=1, source_target_pairs={{0,14},{1,15},{2,0},{3,1},{4,2},{5,3},{6,4},{7,5},{8,6},{9,7},{10,... | collective-permute-start | bytes 184328 | tf_op jit(solution)/shard_map/ppermute | solution.py:52
  16.7 4.2 %collective-permute-start.7 = (bf16[5,240,128]{2,1,0:T(8,128)(2,1)S(1)}, bf16[5,240,128]{2,1,0:T(8,128)(2,1)S(1)}, u32[]{:S(2)}, u32[]{:S(2)}) collective-permute-start(bf16[5,240,128]{2,1,0:T(8,128)(2,1)S(1)} %bitcast_dynamic-update-slice_fusion.first_ref), channel_id=1, source_target_pairs={{0,1},{1,0},{2,3},{3,2},{4,5},{5,4},{6,7},{7,6},{8,9},{9,8},{10,11... | collective-permute-start | bytes 921608 | tf_op jit(solution)/shard_map/ppermute | solution.py:47
  19.3 1.6 %collective-permute-start.8 = (bf16[3,240,128]{2,1,0:T(8,128)(2,1)S(1)}, bf16[3,240,128]{2,1,0:T(8,128)(2,1)S(1)}, u32[]{:S(2)}, u32[]{:S(2)}) collective-permute-start(bf16[3,240,128]{2,1,0:T(8,128)(2,1)S(1)} %pad_maximum_fusion.last_ref), channel_id=1, source_target_pairs={{0,1},{1,0},{2,3},{3,2},{4,5},{5,4},{6,7},{7,6},{8,9},{9,8},{10,11... | collective-permute-start | bytes 552968 | tf_op jit(solution)/shard_map/ppermute | solution.py:47
  27.3 13.1 %all-to-all-start = ((f32[16,8,128]{2,1,0:T(8,128)}), f32[16,8,128]{2,1,0:T(8,128)S(1)}, u32[]{:S(2)}, u32[]{:S(2)}) async-start(f32[16,8,128]{2,1,0:T(8,128)} %get-tuple-element.22), calls=%async_computation | async-start | bytes 131072 | tf_op jit(solution)/shard_map/all_to_all | solution.py:581
  41.4 1.6 %collective-permute-start.9 = (bf16[8,160,128]{2,1,0:T(8,128)(2,1)S(1)}, bf16[8,160,128]{2,1,0:T(8,128)(2,1)S(1)}, u32[]{:S(2)}, u32[]{:S(2)}) collective-permute-start(bf16[8,160,128]{2,1,0:T(8,128)(2,1)S(1)} %get-tuple-element.30), channel_id=1, source_target_pairs={{0,1},{1,0},{2,3},{3,2},{4,5},{5,4},{6,7},{7,6},{8,9},{9,8},{10,11... | collective-permute-start | bytes 983048 | tf_op jit(solution)/shard_map/ppermute | solution.py:47
  43.1 8.9 %collective-permute-start.10 = (bf16[160,128]{1,0:T(8,128)(2,1)S(1)}, bf16[160,128]{1,0:T(8,128)(2,1)S(1)}, u32[]{:S(2)}, u32[]{:S(2)}) collective-permute-start(bf16[160,128]{1,0:T(8,128)(2,1)S(1)} %get-tuple-element.48), channel_id=1, source_target_pairs={{0,2},{1,3},{2,4},{3,5},{4,6},{5,7},{6,8},{7,9},{8,10},{9,11},{10,... | collective-permute-start | bytes 122888 | tf_op jit(solution)/shard_map/ppermute | solution.py:52
  44.4 9.1 %collective-permute-start.11 = (bf16[160,128]{1,0:T(8,128)(2,1)S(1)}, bf16[160,128]{1,0:T(8,128)(2,1)S(1)}, u32[]{:S(2)}, u32[]{:S(2)}) collective-permute-start(bf16[160,128]{1,0:T(8,128)(2,1)S(1)} %get-tuple-element.47), channel_id=1, source_target_pairs={{0,4},{1,5},{2,6},{3,7},{4,8},{5,9},{6,10},{7,11},{8,12},{9,13},{1... | collective-permute-start | bytes 122888 | tf_op jit(solution)/shard_map/ppermute | solution.py:52
  45.9 9.1 %collective-permute-start.12 = (bf16[160,128]{1,0:T(8,128)(2,1)S(1)}, bf16[160,128]{1,0:T(8,128)(2,1)S(1)}, u32[]{:S(2)}, u32[]{:S(2)}) collective-permute-start(bf16[160,128]{1,0:T(8,128)(2,1)S(1)} %get-tuple-element.46), channel_id=1, source_target_pairs={{0,6},{1,7},{2,8},{3,9},{4,10},{5,11},{6,12},{7,13},{8,14},{9,15},... | collective-permute-start | bytes 122888 | tf_op jit(solution)/shard_map/ppermute | solution.py:52
  48.2 6.8 %collective-permute-start.13 = (bf16[160,128]{1,0:T(8,128)(2,1)S(1)}, bf16[160,128]{1,0:T(8,128)(2,1)S(1)}, u32[]{:S(2)}, u32[]{:S(2)}) collective-permute-start(bf16[160,128]{1,0:T(8,128)(2,1)S(1)} %get-tuple-element.45), channel_id=1, source_target_pairs={{0,8},{1,9},{2,10},{3,11},{4,12},{5,13},{6,14},{7,15},{8,0},{9,1},... | collective-permute-start | bytes 122888 | tf_op jit(solution)/shard_map/ppermute | solution.py:52
  49.7 5.4 %collective-permute-start.14 = (bf16[160,128]{1,0:T(8,128)(2,1)S(1)}, bf16[160,128]{1,0:T(8,128)(2,1)S(1)}, u32[]{:S(2)}, u32[]{:S(2)}) collective-permute-start(bf16[160,128]{1,0:T(8,128)(2,1)S(1)} %get-tuple-element.44), channel_id=1, source_target_pairs={{0,10},{1,11},{2,12},{3,13},{4,14},{5,15},{6,0},{7,1},{8,2},{9,3},... | collective-permute-start | bytes 122888 | tf_op jit(solution)/shard_map/ppermute | solution.py:52
  52.1 4.1 %collective-permute-start.15 = (bf16[160,128]{1,0:T(8,128)(2,1)S(1)}, bf16[160,128]{1,0:T(8,128)(2,1)S(1)}, u32[]{:S(2)}, u32[]{:S(2)}) collective-permute-start(bf16[160,128]{1,0:T(8,128)(2,1)S(1)} %get-tuple-element.43), channel_id=1, source_target_pairs={{0,12},{1,13},{2,14},{3,15},{4,0},{5,1},{6,2},{7,3},{8,4},{9,5},{1... | collective-permute-start | bytes 122888 | tf_op jit(solution)/shard_map/ppermute | solution.py:52
  53.5 4.0 %collective-permute-start.16 = (bf16[160,128]{1,0:T(8,128)(2,1)S(1)}, bf16[160,128]{1,0:T(8,128)(2,1)S(1)}, u32[]{:S(2)}, u32[]{:S(2)}) collective-permute-start(bf16[160,128]{1,0:T(8,128)(2,1)S(1)} %get-tuple-element.42), channel_id=1, source_target_pairs={{0,14},{1,15},{2,0},{3,1},{4,2},{5,3},{6,4},{7,5},{8,6},{9,7},{10,... | collective-permute-start | bytes 122888 | tf_op jit(solution)/shard_map/ppermute | solution.py:52

commit v24 on v23

--- a/solution.py
+++ b/solution.py
@@ -217,20 +217,21 @@
     return pltpu.make_async_copy(head_ref.at[:, columns], held_ref.at[step], sems.at[step])
 
 
-def stream(chip_at, count, head_ref, held_ref, sems, use):
+def stream(chip_at, count, ahead, head_ref, held_ref, sems, use):
     def copy(step):
         return head_copy(head_ref, held_ref, sems, chip_at(step), step)
 
     def body(step, _):
         copy(step).wait()
-
-        @pl.when(step + AHEAD < count)
-        def _():
-            copy(step + AHEAD).start()
+        if ahead < count:
+
+            @pl.when(step + ahead < count)
+            def _():
+                copy(step + ahead).start()
 
         use(step)
 
-    for step in range(min(AHEAD, count)):
+    for step in range(min(ahead, count)):
         copy(step).start()
     return lambda: lax.fori_loop(0, count, body, None)
 
@@ -289,6 +290,7 @@
     run = stream(
         lambda step: source_chip(place_ref, chips, step + EARLY),
         chips - EARLY,
+        chips - EARLY,
         head_ref,
         held_ref,
         sems,
@@ -388,6 +390,7 @@
     run = stream(
         lambda step: lax.rem(place_ref[0] // 2 + step, chips),
         chips,
+        AHEAD,
         head_ref,
         held_ref,
         sems,

time: 58.5 us -> 58.5 us (level)
  no operation moved by 1% of the time
where the time goes in v24:
time: 58.5 us; the launch traced here: 58.3 us
  starting transfers between devices  32.5 us (56%)
  Pallas kernels  19.6 us (34%)
  waiting for transfers between devices  4.61 us (8%)
  between operations  1.43 us (2%)
    ppermute x14, starting transfers between devices, along_chips(): lax.ppermute(array, 'vocab', [(i, (i + 2 * step) % count) for i in range(...  25.6 us
    pallas_call x1, Pallas kernels, paired_shards(): pl.pallas_call(logits_kernel, out_shape=(hbm_array((3 * tokens, shard_row...  6.4 us
    all_to_all x1, starting transfers between devices, paired_shards(): lax.all_to_all(stats, 'vocab', split_axis=0, concat_axis=0, tiled=True)  6.21 us
    pallas_call x1, Pallas kernels, paired_shards(): pl.pallas_call(products_kernel, out_shape=(vmem_array((chips, width // LA...  6.17 us
    ppermute x14, waiting for transfers between devices, along_chips(): lax.ppermute(array, 'vocab', [(i, (i + 2 * step) % count) for i in range(...  3.2 us
    pallas_call x1, Pallas kernels, paired_shards(): pl.pallas_call(functools.partial(preload_kernel, chips=chips), out_shape=...  2.4 us
    pallas_call x1, Pallas kernels, paired_shards(): pl.pallas_call(functools.partial(pack_kernel, shard_rows=shard_rows), out...  1.52 us
    pallas_call x1, Pallas kernels, paired_shards(): pl.pallas_call(keep_kernel, out_shape=(vmem_array((chips, hidden_rows, LA...  1.34 us
  transfers between devices with their start and end apart: 18, of which 8 were waited for; matrix products, arithmetic and copies ran while one was open for 0% of the time, Pallas kernels for 17%

profile of v24, /device:TPU:0, one launch (start us, length us, event | category | flops | bytes accessed | tf_op | source)
XLA Modules:
  0.0 58.3 jit_solution(8823854948908503691)
XLA Ops:
  0.6 1.5 %pack.1 = (bf16[8,240,128]{2,1,0:T(8,128)(2,1)S(1)}, bf16[128,128]{1,0:T(8,128)(2,1)S(1)}, f32[64,128]{1,0:T(8,128)S(1)}) custom-call(s32[1]{0:T(128)} %bitcast.place_ref, bf16[64,320]{1,0:T(8,128)(2,1)} %refs_0_.1, bf16[4,19456]{1,0:T(4,128)(2,1)} %refs_1_.1, f32[4,608]{1,0:T(4,128)} %refs_2_.1, s32[1,64]{1,0:T(1,128)} %bitcast.49, s32[1,64]{1,0:T(1,128)} %bitcast.50, ...), custom_call_target="tpu_custom_call" | custom-call | tf_op jit(solution)/shard_map/pack/pallas_call | solution.py:513
  2.2 3.0 %collective-permute-start = (bf16[240,128]{1,0:T(8,128)(2,1)S(1)}, bf16[240,128]{1,0:T(8,128)(2,1)S(1)}, u32[]{:S(2)}, u32[]{:S(2)}) collective-permute-start(bf16[240,128]{1,0:T(8,128)(2,1)S(1)} %get-tuple-element.40), channel_id=1, source_target_pairs={{0,2},{1,3},{2,4},{3,5},{4,6},{5,7},{6,8},{7,9},{8,10},{9,11},{10,... | collective-permute-start | bytes 184328 | tf_op jit(solution)/shard_map/ppermute | solution.py:52
  5.2 1.6 %collective-permute-start.1 = (bf16[240,128]{1,0:T(8,128)(2,1)S(1)}, bf16[240,128]{1,0:T(8,128)(2,1)S(1)}, u32[]{:S(2)}, u32[]{:S(2)}) collective-permute-start(bf16[240,128]{1,0:T(8,128)(2,1)S(1)} %get-tuple-element.39), channel_id=1, source_target_pairs={{0,4},{1,5},{2,6},{3,7},{4,8},{5,9},{6,10},{7,11},{8,12},{9,13},{1... | collective-permute-start | bytes 184328 | tf_op jit(solution)/shard_map/ppermute | solution.py:52
  6.8 2.5 %collective-permute-start.2 = (bf16[240,128]{1,0:T(8,128)(2,1)S(1)}, bf16[240,128]{1,0:T(8,128)(2,1)S(1)}, u32[]{:S(2)}, u32[]{:S(2)}) collective-permute-start(bf16[240,128]{1,0:T(8,128)(2,1)S(1)} %get-tuple-element.38), channel_id=1, source_target_pairs={{0,6},{1,7},{2,8},{3,9},{4,10},{5,11},{6,12},{7,13},{8,14},{9,15},... | collective-permute-start | bytes 184328 | tf_op jit(solution)/shard_map/ppermute | solution.py:52
  9.3 1.2 %collective-permute-start.3 = (bf16[240,128]{1,0:T(8,128)(2,1)S(1)}, bf16[240,128]{1,0:T(8,128)(2,1)S(1)}, u32[]{:S(2)}, u32[]{:S(2)}) collective-permute-start(bf16[240,128]{1,0:T(8,128)(2,1)S(1)} %get-tuple-element.37), channel_id=1, source_target_pairs={{0,8},{1,9},{2,10},{3,11},{4,12},{5,13},{6,14},{7,15},{8,0},{9,1},... | collective-permute-start | bytes 184328 | tf_op jit(solution)/shard_map/ppermute | solution.py:52
  10.6 2.6 %collective-permute-start.4 = (bf16[240,128]{1,0:T(8,128)(2,1)S(1)}, bf16[240,128]{1,0:T(8,128)(2,1)S(1)}, u32[]{:S(2)}, u32[]{:S(2)}) collective-permute-start(bf16[240,128]{1,0:T(8,128)(2,1)S(1)} %get-tuple-element.34), channel_id=1, source_target_pairs={{0,10},{1,11},{2,12},{3,13},{4,14},{5,15},{6,0},{7,1},{8,2},{9,3},... | collective-permute-start | bytes 184328 | tf_op jit(solution)/shard_map/ppermute | solution.py:52
  13.2 1.3 %collective-permute-start.5 = (bf16[240,128]{1,0:T(8,128)(2,1)S(1)}, bf16[240,128]{1,0:T(8,128)(2,1)S(1)}, u32[]{:S(2)}, u32[]{:S(2)}) collective-permute-start(bf16[240,128]{1,0:T(8,128)(2,1)S(1)} %get-tuple-element.36), channel_id=1, source_target_pairs={{0,12},{1,13},{2,14},{3,15},{4,0},{5,1},{6,2},{7,3},{8,4},{9,5},{1... | collective-permute-start | bytes 184328 | tf_op jit(solution)/shard_map/ppermute | solution.py:52
  14.6 1.5 %collective-permute-start.6 = (bf16[240,128]{1,0:T(8,128)(2,1)S(1)}, bf16[240,128]{1,0:T(8,128)(2,1)S(1)}, u32[]{:S(2)}, u32[]{:S(2)}) collective-permute-start(bf16[240,128]{1,0:T(8,128)(2,1)S(1)} %get-tuple-element.35), channel_id=1, source_target_pairs={{0,14},{1,15},{2,0},{3,1},{4,2},{5,3},{6,4},{7,5},{8,6},{9,7},{10,... | collective-permute-start | bytes 184328 | tf_op jit(solution)/shard_map/ppermute | solution.py:52
  16.8 2.4 %preload.1.early_ref = bf16[3,1216,640]{2,1,0:T(8,128)(2,1)S(1)} custom-call(s32[1]{0:T(128)} %bitcast.place_ref, bf16[1216,5120]{1,0:T(8,128)(2,1)} %head_ref.5, bf16[240,128]{1,0:T(8,128)(2,1)S(1)} %collective-permute-done.2._), custom_call_target="tpu_custom_call" | custom-call | bytes 9338880 | tf_op jit(solution)/shard_map/preload/pallas_call | solution.py:533
  20.9 6.4 %logits.1 = (bf16[192,1216]{1,0:T(8,128)(2,1)}, f32[16,8,128]{2,1,0:T(8,128)}, f32[8,128]{1,0:T(8,128)S(1)}) custom-call(s32[1]{0:T(128)} %bitcast.place_ref, bf16[5,240,128]{2,1,0:T(8,128)(2,1)S(1)} %bitcast_dynamic-update-slice_fusion.first_ref, bf16[3,240,128]{2,1,0:T(8,128)(2,1)S(1)} %pad_maximum_fusion.last_ref, ...), custom_call_target="tpu_custom_call" | custom-call | flops 796917760 | bytes 12451840 | tf_op jit(solution)/shard_map/logits/pallas_call | solution.py:549
  27.3 6.2 %all-to-all-start = ((f32[16,8,128]{2,1,0:T(8,128)}), f32[16,8,128]{2,1,0:T(8,128)S(1)}, u32[]{:S(2)}, u32[]{:S(2)}) async-start(f32[16,8,128]{2,1,0:T(8,128)} %get-tuple-element.22), calls=%async_computation | async-start | bytes 131072 | tf_op jit(solution)/shard_map/all_to_all | solution.py:584
  33.5 6.2 %products.1 = (f32[8,5,2,64,128]{4,3,2,1,0:T(8,128)S(1)}, bf16[8,5,64,128]{3,2,1,0:T(8,128)(2,1)S(1)}) custom-call(s32[1]{0:T(128)} %bitcast.place_ref, bf16[192,1216]{1,0:T(8,128)(2,1)} %get-tuple-element.24.rows_ref, bf16[1216,5120]{1,0:T(8,128)(2,1)} %head_ref.5), custom_call_target="tpu_custom_call" | custom-call | flops 2390753280 | bytes 12451840 | tf_op jit(solution)/shard_map/products/pallas_call | solution.py:586
  40.4 0.9 %give.1 = (bf16[8,160,128]{2,1,0:T(8,128)(2,1)S(1)}, f32[3,64,128]{2,1,0:T(8,128)S(1)}, f32[1,1]{1,0:T(1,128)}) custom-call(s32[1]{0:T(128)} %bitcast.place_ref, f32[1]{0:T(128)S(6)} %copy.14.scale_ref, f32[16,8,128]{2,1,0:T(8,128)S(1)} %all-to-all-done.stats_ref, f32[8,128]{1,0:T(8,128)S(1)} %get-tuple-element.23.own_ref, ...), custom_call_target="tpu_custom_call" | custom-call | tf_op jit(solution)/shard_map/give/pallas_call | solution.py:603
  41.4 1.3 %keep.1 = (f32[8,160,128]{2,1,0:T(8,128)S(1)}, f32[1,1]{1,0:T(1,128)}) custom-call(s32[1]{0:T(128)} %bitcast.place_ref, f32[3,64,128]{2,1,0:T(8,128)S(1)} %get-tuple-element.27.factors_ref, f32[1,1]{1,0:T(1,128)} %get-tuple-element.28.found_ref, f32[8,5,2,64,128]{4,3,2,1,0:T(8,128)S(1)} %get-tuple-element.25.terms_ref, ...), custom_call_target="tpu_custom_call" | custom-call | flops 2621440 | bytes 2621440 | tf_op jit(solution)/shard_map/keep/pallas_call | solution.py:616
  43.1 1.3 %collective-permute-start.10 = (bf16[160,128]{1,0:T(8,128)(2,1)S(1)}, bf16[160,128]{1,0:T(8,128)(2,1)S(1)}, u32[]{:S(2)}, u32[]{:S(2)}) collective-permute-start(bf16[160,128]{1,0:T(8,128)(2,1)S(1)} %get-tuple-element.48), channel_id=1, source_target_pairs={{0,2},{1,3},{2,4},{3,5},{4,6},{5,7},{6,8},{7,9},{8,10},{9,11},{10,... | collective-permute-start | bytes 122888 | tf_op jit(solution)/shard_map/ppermute | solution.py:52
  44.4 1.5 %collective-permute-start.11 = (bf16[160,128]{1,0:T(8,128)(2,1)S(1)}, bf16[160,128]{1,0:T(8,128)(2,1)S(1)}, u32[]{:S(2)}, u32[]{:S(2)}) collective-permute-start(bf16[160,128]{1,0:T(8,128)(2,1)S(1)} %get-tuple-element.47), channel_id=1, source_target_pairs={{0,4},{1,5},{2,6},{3,7},{4,8},{5,9},{6,10},{7,11},{8,12},{9,13},{1... | collective-permute-start | bytes 122888 | tf_op jit(solution)/shard_map/ppermute | solution.py:52
  45.9 2.4 %collective-permute-start.12 = (bf16[160,128]{1,0:T(8,128)(2,1)S(1)}, bf16[160,128]{1,0:T(8,128)(2,1)S(1)}, u32[]{:S(2)}, u32[]{:S(2)}) collective-permute-start(bf16[160,128]{1,0:T(8,128)(2,1)S(1)} %get-tuple-element.46), channel_id=1, source_target_pairs={{0,6},{1,7},{2,8},{3,9},{4,10},{5,11},{6,12},{7,13},{8,14},{9,15},... | collective-permute-start | bytes 122888 | tf_op jit(solution)/shard_map/ppermute | solution.py:52
  48.2 1.5 %collective-permute-start.13 = (bf16[160,128]{1,0:T(8,128)(2,1)S(1)}, bf16[160,128]{1,0:T(8,128)(2,1)S(1)}, u32[]{:S(2)}, u32[]{:S(2)}) collective-permute-start(bf16[160,128]{1,0:T(8,128)(2,1)S(1)} %get-tuple-element.45), channel_id=1, source_target_pairs={{0,8},{1,9},{2,10},{3,11},{4,12},{5,13},{6,14},{7,15},{8,0},{9,1},... | collective-permute-start | bytes 122888 | tf_op jit(solution)/shard_map/ppermute | solution.py:52
  49.7 2.4 %collective-permute-start.14 = (bf16[160,128]{1,0:T(8,128)(2,1)S(1)}, bf16[160,128]{1,0:T(8,128)(2,1)S(1)}, u32[]{:S(2)}, u32[]{:S(2)}) collective-permute-start(bf16[160,128]{1,0:T(8,128)(2,1)S(1)} %get-tuple-element.44), channel_id=1, source_target_pairs={{0,10},{1,11},{2,12},{3,13},{4,14},{5,15},{6,0},{7,1},{8,2},{9,3},... | collective-permute-start | bytes 122888 | tf_op jit(solution)/shard_map/ppermute | solution.py:52
  52.0 1.5 %collective-permute-start.15 = (bf16[160,128]{1,0:T(8,128)(2,1)S(1)}, bf16[160,128]{1,0:T(8,128)(2,1)S(1)}, u32[]{:S(2)}, u32[]{:S(2)}) collective-permute-start(bf16[160,128]{1,0:T(8,128)(2,1)S(1)} %get-tuple-element.43), channel_id=1, source_target_pairs={{0,12},{1,13},{2,14},{3,15},{4,0},{5,1},{6,2},{7,3},{8,4},{9,5},{1... | collective-permute-start | bytes 122888 | tf_op jit(solution)/shard_map/ppermute | solution.py:52
  53.5 1.5 %collective-permute-start.16 = (bf16[160,128]{1,0:T(8,128)(2,1)S(1)}, bf16[160,128]{1,0:T(8,128)(2,1)S(1)}, u32[]{:S(2)}, u32[]{:S(2)}) collective-permute-start(bf16[160,128]{1,0:T(8,128)(2,1)S(1)} %get-tuple-element.42), channel_id=1, source_target_pairs={{0,14},{1,15},{2,0},{3,1},{4,2},{5,3},{6,4},{7,5},{8,6},{9,7},{10,... | collective-permute-start | bytes 122888 | tf_op jit(solution)/shard_map/ppermute | solution.py:52
  55.1 1.0 %collective-permute-done.15.refs_5_ = bf16[160,128]{1,0:T(8,128)(2,1)S(1)} collective-permute-done((bf16[160,128]{1,0:T(8,128)(2,1)S(1)}, bf16[160,128]{1,0:T(8,128)(2,1)S(1)}, u32[]{:S(2)}, u32[]{:S(2)}) %collective-permute-start.15) | collective-permute-done | bytes 40992 | tf_op jit(solution)/shard_map/ppermute | solution.py:52
  56.2 1.4 %collective-permute-done.16.refs_6_ = bf16[160,128]{1,0:T(8,128)(2,1)S(1)} collective-permute-done((bf16[160,128]{1,0:T(8,128)(2,1)S(1)}, bf16[160,128]{1,0:T(8,128)(2,1)S(1)}, u32[]{:S(2)}, u32[]{:S(2)}) %collective-permute-start.16) | collective-permute-done | bytes 40992 | tf_op jit(solution)/shard_map/ppermute | solution.py:52
  57.5 0.8 %total.1 = bf16[64,320]{1,0:T(8,128)(2,1)} custom-call(s32[1]{0:T(128)} %bitcast.place_ref, f32[160,128]{1,0:T(8,128)S(1)} %slice_bitcast_fusion.own_ref, bf16[160,128]{1,0:T(8,128)(2,1)S(1)} %collective-permute-done.10.refs_0_, bf16[160,128]{1,0:T(8,128)(2,1)S(1)} %collective-permute-done.11.refs_1_, bf16[160,128]{1,0:T(8,128)(2,1)S(1)} %collective-permute-done.12.refs_2_, ...), custom_call_target="tpu_custom_call" | custom-call | tf_op jit(solution)/shard_map/total/pallas_call | solution.py:632
  (28 shorter events, 3.1 us)
Async XLA Ops:
  2.2 11.0 %collective-permute-start = (bf16[240,128]{1,0:T(8,128)(2,1)S(1)}, bf16[240,128]{1,0:T(8,128)(2,1)S(1)}, u32[]{:S(2)}, u32[]{:S(2)}) collective-permute-start(bf16[240,128]{1,0:T(8,128)(2,1)S(1)} %get-tuple-element.40), channel_id=1, source_target_pairs={{0,2},{1,3},{2,4},{3,5},{4,6},{5,7},{6,8},{7,9},{8,10},{9,11},{10,... | collective-permute-start | bytes 184328 | tf_op jit(solution)/shard_map/ppermute | solution.py:52
  5.2 9.4 %collective-permute-start.1 = (bf16[240,128]{1,0:T(8,128)(2,1)S(1)}, bf16[240,128]{1,0:T(8,128)(2,1)S(1)}, u32[]{:S(2)}, u32[]{:S(2)}) collective-permute-start(bf16[240,128]{1,0:T(8,128)(2,1)S(1)} %get-tuple-element.39), channel_id=1, source_target_pairs={{0,4},{1,5},{2,6},{3,7},{4,8},{5,9},{6,10},{7,11},{8,12},{9,13},{1... | collective-permute-start | bytes 184328 | tf_op jit(solution)/shard_map/ppermute | solution.py:52
  6.8 9.4 %collective-permute-start.2 = (bf16[240,128]{1,0:T(8,128)(2,1)S(1)}, bf16[240,128]{1,0:T(8,128)(2,1)S(1)}, u32[]{:S(2)}, u32[]{:S(2)}) collective-permute-start(bf16[240,128]{1,0:T(8,128)(2,1)S(1)} %get-tuple-element.38), channel_id=1, source_target_pairs={{0,6},{1,7},{2,8},{3,9},{4,10},{5,11},{6,12},{7,13},{8,14},{9,15},... | collective-permute-start | bytes 184328 | tf_op jit(solution)/shard_map/ppermute | solution.py:52
  9.3 7.4 %collective-permute-start.3 = (bf16[240,128]{1,0:T(8,128)(2,1)S(1)}, bf16[240,128]{1,0:T(8,128)(2,1)S(1)}, u32[]{:S(2)}, u32[]{:S(2)}) collective-permute-start(bf16[240,128]{1,0:T(8,128)(2,1)S(1)} %get-tuple-element.37), channel_id=1, source_target_pairs={{0,8},{1,9},{2,10},{3,11},{4,12},{5,13},{6,14},{7,15},{8,0},{9,1},... | collective-permute-start | bytes 184328 | tf_op jit(solution)/shard_map/ppermute | solution.py:52
  10.6 8.7 %collective-permute-start.4 = (bf16[240,128]{1,0:T(8,128)(2,1)S(1)}, bf16[240,128]{1,0:T(8,128)(2,1)S(1)}, u32[]{:S(2)}, u32[]{:S(2)}) collective-permute-start(bf16[240,128]{1,0:T(8,128)(2,1)S(1)} %get-tuple-element.34), channel_id=1, source_target_pairs={{0,10},{1,11},{2,12},{3,13},{4,14},{5,15},{6,0},{7,1},{8,2},{9,3},... | collective-permute-start | bytes 184328 | tf_op jit(solution)/shard_map/ppermute | solution.py:52
  13.2 6.0 %collective-permute-start.5 = (bf16[240,128]{1,0:T(8,128)(2,1)S(1)}, bf16[240,128]{1,0:T(8,128)(2,1)S(1)}, u32[]{:S(2)}, u32[]{:S(2)}) collective-permute-start(bf16[240,128]{1,0:T(8,128)(2,1)S(1)} %get-tuple-element.36), channel_id=1, source_target_pairs={{0,12},{1,13},{2,14},{3,15},{4,0},{5,1},{6,2},{7,3},{8,4},{9,5},{1... | collective-permute-start | bytes 184328 | tf_op jit(solution)/shard_map/ppermute | solution.py:52
  14.6 4.7 %collective-permute-start.6 = (bf16[240,128]{1,0:T(8,128)(2,1)S(1)}, bf16[240,128]{1,0:T(8,128)(2,1)S(1)}, u32[]{:S(2)}, u32[]{:S(2)}) collective-permute-start(bf16[240,128]{1,0:T(8,128)(2,1)S(1)} %get-tuple-element.35), channel_id=1, source_target_pairs={{0,14},{1,15},{2,0},{3,1},{4,2},{5,3},{6,4},{7,5},{8,6},{9,7},{10,... | collective-permute-start | bytes 184328 | tf_op jit(solution)/shard_map/ppermute | solution.py:52
  16.7 4.2 %collective-permute-start.7 = (bf16[5,240,128]{2,1,0:T(8,128)(2,1)S(1)}, bf16[5,240,128]{2,1,0:T(8,128)(2,1)S(1)}, u32[]{:S(2)}, u32[]{:S(2)}) collective-permute-start(bf16[5,240,128]{2,1,0:T(8,128)(2,1)S(1)} %bitcast_dynamic-update-slice_fusion.first_ref), channel_id=1, source_target_pairs={{0,1},{1,0},{2,3},{3,2},{4,5},{5,4},{6,7},{7,6},{8,9},{9,8},{10,11... | collective-permute-start | bytes 921608 | tf_op jit(solution)/shard_map/ppermute | solution.py:47
  19.3 1.6 %collective-permute-start.8 = (bf16[3,240,128]{2,1,0:T(8,128)(2,1)S(1)}, bf16[3,240,128]{2,1,0:T(8,128)(2,1)S(1)}, u32[]{:S(2)}, u32[]{:S(2)}) collective-permute-start(bf16[3,240,128]{2,1,0:T(8,128)(2,1)S(1)} %pad_maximum_fusion.last_ref), channel_id=1, source_target_pairs={{0,1},{1,0},{2,3},{3,2},{4,5},{5,4},{6,7},{7,6},{8,9},{9,8},{10,11... | collective-permute-start | bytes 552968 | tf_op jit(solution)/shard_map/ppermute | solution.py:47
  27.3 13.1 %all-to-all-start = ((f32[16,8,128]{2,1,0:T(8,128)}), f32[16,8,128]{2,1,0:T(8,128)S(1)}, u32[]{:S(2)}, u32[]{:S(2)}) async-start(f32[16,8,128]{2,1,0:T(8,128)} %get-tuple-element.22), calls=%async_computation | async-start | bytes 131072 | tf_op jit(solution)/shard_map/all_to_all | solution.py:584
  41.4 1.6 %collective-permute-start.9 = (bf16[8,160,128]{2,1,0:T(8,128)(2,1)S(1)}, bf16[8,160,128]{2,1,0:T(8,128)(2,1)S(1)}, u32[]{:S(2)}, u32[]{:S(2)}) collective-permute-start(bf16[8,160,128]{2,1,0:T(8,128)(2,1)S(1)} %get-tuple-element.30), channel_id=1, source_target_pairs={{0,1},{1,0},{2,3},{3,2},{4,5},{5,4},{6,7},{7,6},{8,9},{9,8},{10,11... | collective-permute-start | bytes 983048 | tf_op jit(solution)/shard_map/ppermute | solution.py:47
  43.1 8.9 %collective-permute-start.10 = (bf16[160,128]{1,0:T(8,128)(2,1)S(1)}, bf16[160,128]{1,0:T(8,128)(2,1)S(1)}, u32[]{:S(2)}, u32[]{:S(2)}) collective-permute-start(bf16[160,128]{1,0:T(8,128)(2,1)S(1)} %get-tuple-element.48), channel_id=1, source_target_pairs={{0,2},{1,3},{2,4},{3,5},{4,6},{5,7},{6,8},{7,9},{8,10},{9,11},{10,... | collective-permute-start | bytes 122888 | tf_op jit(solution)/shard_map/ppermute | solution.py:52
  44.4 9.1 %collective-permute-start.11 = (bf16[160,128]{1,0:T(8,128)(2,1)S(1)}, bf16[160,128]{1,0:T(8,128)(2,1)S(1)}, u32[]{:S(2)}, u32[]{:S(2)}) collective-permute-start(bf16[160,128]{1,0:T(8,128)(2,1)S(1)} %get-tuple-element.47), channel_id=1, source_target_pairs={{0,4},{1,5},{2,6},{3,7},{4,8},{5,9},{6,10},{7,11},{8,12},{9,13},{1... | collective-permute-start | bytes 122888 | tf_op jit(solution)/shard_map/ppermute | solution.py:52
  45.9 9.1 %collective-permute-start.12 = (bf16[160,128]{1,0:T(8,128)(2,1)S(1)}, bf16[160,128]{1,0:T(8,128)(2,1)S(1)}, u32[]{:S(2)}, u32[]{:S(2)}) collective-permute-start(bf16[160,128]{1,0:T(8,128)(2,1)S(1)} %get-tuple-element.46), channel_id=1, source_target_pairs={{0,6},{1,7},{2,8},{3,9},{4,10},{5,11},{6,12},{7,13},{8,14},{9,15},... | collective-permute-start | bytes 122888 | tf_op jit(solution)/shard_map/ppermute | solution.py:52
  48.2 6.8 %collective-permute-start.13 = (bf16[160,128]{1,0:T(8,128)(2,1)S(1)}, bf16[160,128]{1,0:T(8,128)(2,1)S(1)}, u32[]{:S(2)}, u32[]{:S(2)}) collective-permute-start(bf16[160,128]{1,0:T(8,128)(2,1)S(1)} %get-tuple-element.45), channel_id=1, source_target_pairs={{0,8},{1,9},{2,10},{3,11},{4,12},{5,13},{6,14},{7,15},{8,0},{9,1},... | collective-permute-start | bytes 122888 | tf_op jit(solution)/shard_map/ppermute | solution.py:52
  49.7 5.4 %collective-permute-start.14 = (bf16[160,128]{1,0:T(8,128)(2,1)S(1)}, bf16[160,128]{1,0:T(8,128)(2,1)S(1)}, u32[]{:S(2)}, u32[]{:S(2)}) collective-permute-start(bf16[160,128]{1,0:T(8,128)(2,1)S(1)} %get-tuple-element.44), channel_id=1, source_target_pairs={{0,10},{1,11},{2,12},{3,13},{4,14},{5,15},{6,0},{7,1},{8,2},{9,3},... | collective-permute-start | bytes 122888 | tf_op jit(solution)/shard_map/ppermute | solution.py:52
  52.0 4.1 %collective-permute-start.15 = (bf16[160,128]{1,0:T(8,128)(2,1)S(1)}, bf16[160,128]{1,0:T(8,128)(2,1)S(1)}, u32[]{:S(2)}, u32[]{:S(2)}) collective-permute-start(bf16[160,128]{1,0:T(8,128)(2,1)S(1)} %get-tuple-element.43), channel_id=1, source_target_pairs={{0,12},{1,13},{2,14},{3,15},{4,0},{5,1},{6,2},{7,3},{8,4},{9,5},{1... | collective-permute-start | bytes 122888 | tf_op jit(solution)/shard_map/ppermute | solution.py:52
  53.5 4.0 %collective-permute-start.16 = (bf16[160,128]{1,0:T(8,128)(2,1)S(1)}, bf16[160,128]{1,0:T(8,128)(2,1)S(1)}, u32[]{:S(2)}, u32[]{:S(2)}) collective-permute-start(bf16[160,128]{1,0:T(8,128)(2,1)S(1)} %get-tuple-element.42), channel_id=1, source_target_pairs={{0,14},{1,15},{2,0},{3,1},{4,2},{5,3},{6,4},{7,5},{8,6},{9,7},{10,... | collective-permute-start | bytes 122888 | tf_op jit(solution)/shard_map/ppermute | solution.py:52

commit v25 on v24

--- a/solution.py
+++ b/solution.py
@@ -282,10 +282,13 @@
     slots = tokens // (2 * chips)
     low = low_lanes((tokens // 2, LANES))
 
-    def add(step, columns):
-        logits_ref[...] += lax.dot_general(
+    def product(step, columns):
+        return lax.dot_general(
             columns, hidden_ref[step], (((1,), (1,)), ((), ())), preferred_element_type=jnp.float32
         )
+
+    def add(step, columns):
+        logits_ref[...] += product(step, columns)
 
     run = stream(
         lambda step: source_chip(place_ref, chips, step + EARLY),
@@ -322,9 +325,10 @@
             hidden_ref[step, :, 2 * LANES : 3 * LANES] = tile
 
     unpack(first_ref, first_far_ref, 0)
+    logits_ref[...] = product(0, early_ref[0])
+    for step in range(1, EARLY):
+        add(step, early_ref[step])
     unpack(last_ref, last_far_ref, first_ref.shape[0])
-    logits_ref[...] = jnp.zeros_like(logits_ref)
-    lax.fori_loop(0, EARLY, lambda step, _: add(step, early_ref[step]), None)
     placed = jnp.dot(
         owner_ref[...], arrived_ref[...].astype(jnp.bfloat16), preferred_element_type=jnp.float32
     )

time: 58.5 us -> 59.3 us (1.014)
  Pallas kernels: 19.6 us -> 20.4 us
    pallas_call x1, Pallas kernels: 6.4 us -> 7.21 us  [paired_shards(): pl.pallas_call(logits_kernel, out_shape=(hbm_array((3 * tokens, shard_row...]
where the time goes in v25:
time: 59.3 us; the launch traced here: 59.1 us
  starting transfers between devices  32.5 us (55%)
  Pallas kernels  20.4 us (34%)
  waiting for transfers between devices  4.6 us (8%)
  between operations  1.43 us (2%)
    ppermute x14, starting transfers between devices, along_chips(): lax.ppermute(array, 'vocab', [(i, (i + 2 * step) % count) for i in range(...  25.7 us
    pallas_call x1, Pallas kernels, paired_shards(): pl.pallas_call(logits_kernel, out_shape=(hbm_array((3 * tokens, shard_row...  7.21 us
    all_to_all x1, starting transfers between devices, paired_shards(): lax.all_to_all(stats, 'vocab', split_axis=0, concat_axis=0, tiled=True)  6.19 us
    pallas_call x1, Pallas kernels, paired_shards(): pl.pallas_call(products_kernel, out_shape=(vmem_array((chips, width // LA...  6.17 us
    ppermute x14, waiting for transfers between devices, along_chips(): lax.ppermute(array, 'vocab', [(i, (i + 2 * step) % count) for i in range(...  3.19 us
    pallas_call x1, Pallas kernels, paired_shards(): pl.pallas_call(functools.partial(preload_kernel, chips=chips), out_shape=...  2.4 us
    pallas_call x1, Pallas kernels, paired_shards(): pl.pallas_call(functools.partial(pack_kernel, shard_rows=shard_rows), out...  1.52 us
    pallas_call x1, Pallas kernels, paired_shards(): pl.pallas_call(keep_kernel, out_shape=(vmem_array((chips, hidden_rows, LA...  1.34 us
  transfers between devices with their start and end apart: 18, of which 8 were waited for; matrix products, arithmetic and copies ran while one was open for 0% of the time, Pallas kernels for 17%

profile of v25, /device:TPU:0, one launch (start us, length us, event | category | flops | bytes accessed | tf_op | source)
XLA Modules:
  0.0 59.1 jit_solution(11206401840275381003)
XLA Ops:
  0.6 1.5 %pack.1 = (bf16[8,240,128]{2,1,0:T(8,128)(2,1)S(1)}, bf16[128,128]{1,0:T(8,128)(2,1)S(1)}, f32[64,128]{1,0:T(8,128)S(1)}) custom-call(s32[1]{0:T(128)} %bitcast.place_ref, bf16[64,320]{1,0:T(8,128)(2,1)} %refs_0_.1, bf16[4,19456]{1,0:T(4,128)(2,1)} %refs_1_.1, f32[4,608]{1,0:T(4,128)} %refs_2_.1, s32[1,64]{1,0:T(1,128)} %bitcast.49, s32[1,64]{1,0:T(1,128)} %bitcast.50, ...), custom_call_target="tpu_custom_call" | custom-call | tf_op jit(solution)/shard_map/pack/pallas_call | solution.py:517
  2.2 3.0 %collective-permute-start = (bf16[240,128]{1,0:T(8,128)(2,1)S(1)}, bf16[240,128]{1,0:T(8,128)(2,1)S(1)}, u32[]{:S(2)}, u32[]{:S(2)}) collective-permute-start(bf16[240,128]{1,0:T(8,128)(2,1)S(1)} %get-tuple-element.40), channel_id=1, source_target_pairs={{0,2},{1,3},{2,4},{3,5},{4,6},{5,7},{6,8},{7,9},{8,10},{9,11},{10,... | collective-permute-start | bytes 184328 | tf_op jit(solution)/shard_map/ppermute | solution.py:52
  5.2 1.6 %collective-permute-start.1 = (bf16[240,128]{1,0:T(8,128)(2,1)S(1)}, bf16[240,128]{1,0:T(8,128)(2,1)S(1)}, u32[]{:S(2)}, u32[]{:S(2)}) collective-permute-start(bf16[240,128]{1,0:T(8,128)(2,1)S(1)} %get-tuple-element.39), channel_id=1, source_target_pairs={{0,4},{1,5},{2,6},{3,7},{4,8},{5,9},{6,10},{7,11},{8,12},{9,13},{1... | collective-permute-start | bytes 184328 | tf_op jit(solution)/shard_map/ppermute | solution.py:52
  6.8 2.5 %collective-permute-start.2 = (bf16[240,128]{1,0:T(8,128)(2,1)S(1)}, bf16[240,128]{1,0:T(8,128)(2,1)S(1)}, u32[]{:S(2)}, u32[]{:S(2)}) collective-permute-start(bf16[240,128]{1,0:T(8,128)(2,1)S(1)} %get-tuple-element.38), channel_id=1, source_target_pairs={{0,6},{1,7},{2,8},{3,9},{4,10},{5,11},{6,12},{7,13},{8,14},{9,15},... | collective-permute-start | bytes 184328 | tf_op jit(solution)/shard_map/ppermute | solution.py:52
  9.3 1.2 %collective-permute-start.3 = (bf16[240,128]{1,0:T(8,128)(2,1)S(1)}, bf16[240,128]{1,0:T(8,128)(2,1)S(1)}, u32[]{:S(2)}, u32[]{:S(2)}) collective-permute-start(bf16[240,128]{1,0:T(8,128)(2,1)S(1)} %get-tuple-element.37), channel_id=1, source_target_pairs={{0,8},{1,9},{2,10},{3,11},{4,12},{5,13},{6,14},{7,15},{8,0},{9,1},... | collective-permute-start | bytes 184328 | tf_op jit(solution)/shard_map/ppermute | solution.py:52
  10.6 2.6 %collective-permute-start.4 = (bf16[240,128]{1,0:T(8,128)(2,1)S(1)}, bf16[240,128]{1,0:T(8,128)(2,1)S(1)}, u32[]{:S(2)}, u32[]{:S(2)}) collective-permute-start(bf16[240,128]{1,0:T(8,128)(2,1)S(1)} %get-tuple-element.34), channel_id=1, source_target_pairs={{0,10},{1,11},{2,12},{3,13},{4,14},{5,15},{6,0},{7,1},{8,2},{9,3},... | collective-permute-start | bytes 184328 | tf_op jit(solution)/shard_map/ppermute | solution.py:52
  13.2 1.3 %collective-permute-start.5 = (bf16[240,128]{1,0:T(8,128)(2,1)S(1)}, bf16[240,128]{1,0:T(8,128)(2,1)S(1)}, u32[]{:S(2)}, u32[]{:S(2)}) collective-permute-start(bf16[240,128]{1,0:T(8,128)(2,1)S(1)} %get-tuple-element.36), channel_id=1, source_target_pairs={{0,12},{1,13},{2,14},{3,15},{4,0},{5,1},{6,2},{7,3},{8,4},{9,5},{1... | collective-permute-start | bytes 184328 | tf_op jit(solution)/shard_map/ppermute | solution.py:52
  14.6 1.5 %collective-permute-start.6 = (bf16[240,128]{1,0:T(8,128)(2,1)S(1)}, bf16[240,128]{1,0:T(8,128)(2,1)S(1)}, u32[]{:S(2)}, u32[]{:S(2)}) collective-permute-start(bf16[240,128]{1,0:T(8,128)(2,1)S(1)} %get-tuple-element.35), channel_id=1, source_target_pairs={{0,14},{1,15},{2,0},{3,1},{4,2},{5,3},{6,4},{7,5},{8,6},{9,7},{10,... | collective-permute-start | bytes 184328 | tf_op jit(solution)/shard_map/ppermute | solution.py:52
  16.8 2.4 %preload.1.early_ref = bf16[3,1216,640]{2,1,0:T(8,128)(2,1)S(1)} custom-call(s32[1]{0:T(128)} %bitcast.place_ref, bf16[1216,5120]{1,0:T(8,128)(2,1)} %head_ref.5, bf16[240,128]{1,0:T(8,128)(2,1)S(1)} %collective-permute-done.2._), custom_call_target="tpu_custom_call" | custom-call | bytes 9338880 | tf_op jit(solution)/shard_map/preload/pallas_call | solution.py:537
  20.9 7.2 %logits.1 = (bf16[192,1216]{1,0:T(8,128)(2,1)}, f32[16,8,128]{2,1,0:T(8,128)}, f32[8,128]{1,0:T(8,128)S(1)}) custom-call(s32[1]{0:T(128)} %bitcast.place_ref, bf16[5,240,128]{2,1,0:T(8,128)(2,1)S(1)} %bitcast_dynamic-update-slice_fusion.first_ref, bf16[3,240,128]{2,1,0:T(8,128)(2,1)S(1)} %pad_maximum_fusion.last_ref, ...), custom_call_target="tpu_custom_call" | custom-call | flops 796917760 | bytes 12451840 | tf_op jit(solution)/shard_map/logits/pallas_call | solution.py:553
  28.1 6.2 %all-to-all-start = ((f32[16,8,128]{2,1,0:T(8,128)}), f32[16,8,128]{2,1,0:T(8,128)S(1)}, u32[]{:S(2)}, u32[]{:S(2)}) async-start(f32[16,8,128]{2,1,0:T(8,128)} %get-tuple-element.22), calls=%async_computation | async-start | bytes 131072 | tf_op jit(solution)/shard_map/all_to_all | solution.py:588
  34.3 6.2 %products.1 = (f32[8,5,2,64,128]{4,3,2,1,0:T(8,128)S(1)}, bf16[8,5,64,128]{3,2,1,0:T(8,128)(2,1)S(1)}) custom-call(s32[1]{0:T(128)} %bitcast.place_ref, bf16[192,1216]{1,0:T(8,128)(2,1)} %get-tuple-element.24.rows_ref, bf16[1216,5120]{1,0:T(8,128)(2,1)} %head_ref.5), custom_call_target="tpu_custom_call" | custom-call | flops 2390753280 | bytes 12451840 | tf_op jit(solution)/shard_map/products/pallas_call | solution.py:590
  41.2 0.9 %give.1 = (bf16[8,160,128]{2,1,0:T(8,128)(2,1)S(1)}, f32[3,64,128]{2,1,0:T(8,128)S(1)}, f32[1,1]{1,0:T(1,128)}) custom-call(s32[1]{0:T(128)} %bitcast.place_ref, f32[1]{0:T(128)S(6)} %copy.14.scale_ref, f32[16,8,128]{2,1,0:T(8,128)S(1)} %all-to-all-done.stats_ref, f32[8,128]{1,0:T(8,128)S(1)} %get-tuple-element.23.own_ref, ...), custom_call_target="tpu_custom_call" | custom-call | tf_op jit(solution)/shard_map/give/pallas_call | solution.py:607
  42.1 1.3 %keep.1 = (f32[8,160,128]{2,1,0:T(8,128)S(1)}, f32[1,1]{1,0:T(1,128)}) custom-call(s32[1]{0:T(128)} %bitcast.place_ref, f32[3,64,128]{2,1,0:T(8,128)S(1)} %get-tuple-element.27.factors_ref, f32[1,1]{1,0:T(1,128)} %get-tuple-element.28.found_ref, f32[8,5,2,64,128]{4,3,2,1,0:T(8,128)S(1)} %get-tuple-element.25.terms_ref, ...), custom_call_target="tpu_custom_call" | custom-call | flops 2621440 | bytes 2621440 | tf_op jit(solution)/shard_map/keep/pallas_call | solution.py:620
  43.9 1.3 %collective-permute-start.10 = (bf16[160,128]{1,0:T(8,128)(2,1)S(1)}, bf16[160,128]{1,0:T(8,128)(2,1)S(1)}, u32[]{:S(2)}, u32[]{:S(2)}) collective-permute-start(bf16[160,128]{1,0:T(8,128)(2,1)S(1)} %get-tuple-element.48), channel_id=1, source_target_pairs={{0,2},{1,3},{2,4},{3,5},{4,6},{5,7},{6,8},{7,9},{8,10},{9,11},{10,... | collective-permute-start | bytes 122888 | tf_op jit(solution)/shard_map/ppermute | solution.py:52
  45.2 1.5 %collective-permute-start.11 = (bf16[160,128]{1,0:T(8,128)(2,1)S(1)}, bf16[160,128]{1,0:T(8,128)(2,1)S(1)}, u32[]{:S(2)}, u32[]{:S(2)}) collective-permute-start(bf16[160,128]{1,0:T(8,128)(2,1)S(1)} %get-tuple-element.47), channel_id=1, source_target_pairs={{0,4},{1,5},{2,6},{3,7},{4,8},{5,9},{6,10},{7,11},{8,12},{9,13},{1... | collective-permute-start | bytes 122888 | tf_op jit(solution)/shard_map/ppermute | solution.py:52
  46.6 2.4 %collective-permute-start.12 = (bf16[160,128]{1,0:T(8,128)(2,1)S(1)}, bf16[160,128]{1,0:T(8,128)(2,1)S(1)}, u32[]{:S(2)}, u32[]{:S(2)}) collective-permute-start(bf16[160,128]{1,0:T(8,128)(2,1)S(1)} %get-tuple-element.46), channel_id=1, source_target_pairs={{0,6},{1,7},{2,8},{3,9},{4,10},{5,11},{6,12},{7,13},{8,14},{9,15},... | collective-permute-start | bytes 122888 | tf_op jit(solution)/shard_map/ppermute | solution.py:52
  49.0 1.5 %collective-permute-start.13 = (bf16[160,128]{1,0:T(8,128)(2,1)S(1)}, bf16[160,128]{1,0:T(8,128)(2,1)S(1)}, u32[]{:S(2)}, u32[]{:S(2)}) collective-permute-start(bf16[160,128]{1,0:T(8,128)(2,1)S(1)} %get-tuple-element.45), channel_id=1, source_target_pairs={{0,8},{1,9},{2,10},{3,11},{4,12},{5,13},{6,14},{7,15},{8,0},{9,1},... | collective-permute-start | bytes 122888 | tf_op jit(solution)/shard_map/ppermute | solution.py:52
  50.5 2.4 %collective-permute-start.14 = (bf16[160,128]{1,0:T(8,128)(2,1)S(1)}, bf16[160,128]{1,0:T(8,128)(2,1)S(1)}, u32[]{:S(2)}, u32[]{:S(2)}) collective-permute-start(bf16[160,128]{1,0:T(8,128)(2,1)S(1)} %get-tuple-element.44), channel_id=1, source_target_pairs={{0,10},{1,11},{2,12},{3,13},{4,14},{5,15},{6,0},{7,1},{8,2},{9,3},... | collective-permute-start | bytes 122888 | tf_op jit(solution)/shard_map/ppermute | solution.py:52
  52.8 1.5 %collective-permute-start.15 = (bf16[160,128]{1,0:T(8,128)(2,1)S(1)}, bf16[160,128]{1,0:T(8,128)(2,1)S(1)}, u32[]{:S(2)}, u32[]{:S(2)}) collective-permute-start(bf16[160,128]{1,0:T(8,128)(2,1)S(1)} %get-tuple-element.43), channel_id=1, source_target_pairs={{0,12},{1,13},{2,14},{3,15},{4,0},{5,1},{6,2},{7,3},{8,4},{9,5},{1... | collective-permute-start | bytes 122888 | tf_op jit(solution)/shard_map/ppermute | solution.py:52
  54.3 1.5 %collective-permute-start.16 = (bf16[160,128]{1,0:T(8,128)(2,1)S(1)}, bf16[160,128]{1,0:T(8,128)(2,1)S(1)}, u32[]{:S(2)}, u32[]{:S(2)}) collective-permute-start(bf16[160,128]{1,0:T(8,128)(2,1)S(1)} %get-tuple-element.42), channel_id=1, source_target_pairs={{0,14},{1,15},{2,0},{3,1},{4,2},{5,3},{6,4},{7,5},{8,6},{9,7},{10,... | collective-permute-start | bytes 122888 | tf_op jit(solution)/shard_map/ppermute | solution.py:52
  55.9 1.0 %collective-permute-done.15.refs_5_ = bf16[160,128]{1,0:T(8,128)(2,1)S(1)} collective-permute-done((bf16[160,128]{1,0:T(8,128)(2,1)S(1)}, bf16[160,128]{1,0:T(8,128)(2,1)S(1)}, u32[]{:S(2)}, u32[]{:S(2)}) %collective-permute-start.15) | collective-permute-done | bytes 40992 | tf_op jit(solution)/shard_map/ppermute | solution.py:52
  56.9 1.4 %collective-permute-done.16.refs_6_ = bf16[160,128]{1,0:T(8,128)(2,1)S(1)} collective-permute-done((bf16[160,128]{1,0:T(8,128)(2,1)S(1)}, bf16[160,128]{1,0:T(8,128)(2,1)S(1)}, u32[]{:S(2)}, u32[]{:S(2)}) %collective-permute-start.16) | collective-permute-done | bytes 40992 | tf_op jit(solution)/shard_map/ppermute | solution.py:52
  58.3 0.8 %total.1 = bf16[64,320]{1,0:T(8,128)(2,1)} custom-call(s32[1]{0:T(128)} %bitcast.place_ref, f32[160,128]{1,0:T(8,128)S(1)} %slice_bitcast_fusion.own_ref, bf16[160,128]{1,0:T(8,128)(2,1)S(1)} %collective-permute-done.10.refs_0_, bf16[160,128]{1,0:T(8,128)(2,1)S(1)} %collective-permute-done.11.refs_1_, bf16[160,128]{1,0:T(8,128)(2,1)S(1)} %collective-permute-done.12.refs_2_, ...), custom_call_target="tpu_custom_call" | custom-call | tf_op jit(solution)/shard_map/total/pallas_call | solution.py:636
  (28 shorter events, 3.1 us)
Async XLA Ops:
  2.2 11.0 %collective-permute-start = (bf16[240,128]{1,0:T(8,128)(2,1)S(1)}, bf16[240,128]{1,0:T(8,128)(2,1)S(1)}, u32[]{:S(2)}, u32[]{:S(2)}) collective-permute-start(bf16[240,128]{1,0:T(8,128)(2,1)S(1)} %get-tuple-element.40), channel_id=1, source_target_pairs={{0,2},{1,3},{2,4},{3,5},{4,6},{5,7},{6,8},{7,9},{8,10},{9,11},{10,... | collective-permute-start | bytes 184328 | tf_op jit(solution)/shard_map/ppermute | solution.py:52
  5.2 9.4 %collective-permute-start.1 = (bf16[240,128]{1,0:T(8,128)(2,1)S(1)}, bf16[240,128]{1,0:T(8,128)(2,1)S(1)}, u32[]{:S(2)}, u32[]{:S(2)}) collective-permute-start(bf16[240,128]{1,0:T(8,128)(2,1)S(1)} %get-tuple-element.39), channel_id=1, source_target_pairs={{0,4},{1,5},{2,6},{3,7},{4,8},{5,9},{6,10},{7,11},{8,12},{9,13},{1... | collective-permute-start | bytes 184328 | tf_op jit(solution)/shard_map/ppermute | solution.py:52
  6.8 9.4 %collective-permute-start.2 = (bf16[240,128]{1,0:T(8,128)(2,1)S(1)}, bf16[240,128]{1,0:T(8,128)(2,1)S(1)}, u32[]{:S(2)}, u32[]{:S(2)}) collective-permute-start(bf16[240,128]{1,0:T(8,128)(2,1)S(1)} %get-tuple-element.38), channel_id=1, source_target_pairs={{0,6},{1,7},{2,8},{3,9},{4,10},{5,11},{6,12},{7,13},{8,14},{9,15},... | collective-permute-start | bytes 184328 | tf_op jit(solution)/shard_map/ppermute | solution.py:52
  9.3 7.4 %collective-permute-start.3 = (bf16[240,128]{1,0:T(8,128)(2,1)S(1)}, bf16[240,128]{1,0:T(8,128)(2,1)S(1)}, u32[]{:S(2)}, u32[]{:S(2)}) collective-permute-start(bf16[240,128]{1,0:T(8,128)(2,1)S(1)} %get-tuple-element.37), channel_id=1, source_target_pairs={{0,8},{1,9},{2,10},{3,11},{4,12},{5,13},{6,14},{7,15},{8,0},{9,1},... | collective-permute-start | bytes 184328 | tf_op jit(solution)/shard_map/ppermute | solution.py:52
  10.6 8.7 %collective-permute-start.4 = (bf16[240,128]{1,0:T(8,128)(2,1)S(1)}, bf16[240,128]{1,0:T(8,128)(2,1)S(1)}, u32[]{:S(2)}, u32[]{:S(2)}) collective-permute-start(bf16[240,128]{1,0:T(8,128)(2,1)S(1)} %get-tuple-element.34), channel_id=1, source_target_pairs={{0,10},{1,11},{2,12},{3,13},{4,14},{5,15},{6,0},{7,1},{8,2},{9,3},... | collective-permute-start | bytes 184328 | tf_op jit(solution)/shard_map/ppermute | solution.py:52
  13.2 6.0 %collective-permute-start.5 = (bf16[240,128]{1,0:T(8,128)(2,1)S(1)}, bf16[240,128]{1,0:T(8,128)(2,1)S(1)}, u32[]{:S(2)}, u32[]{:S(2)}) collective-permute-start(bf16[240,128]{1,0:T(8,128)(2,1)S(1)} %get-tuple-element.36), channel_id=1, source_target_pairs={{0,12},{1,13},{2,14},{3,15},{4,0},{5,1},{6,2},{7,3},{8,4},{9,5},{1... | collective-permute-start | bytes 184328 | tf_op jit(solution)/shard_map/ppermute | solution.py:52
  14.6 4.7 %collective-permute-start.6 = (bf16[240,128]{1,0:T(8,128)(2,1)S(1)}, bf16[240,128]{1,0:T(8,128)(2,1)S(1)}, u32[]{:S(2)}, u32[]{:S(2)}) collective-permute-start(bf16[240,128]{1,0:T(8,128)(2,1)S(1)} %get-tuple-element.35), channel_id=1, source_target_pairs={{0,14},{1,15},{2,0},{3,1},{4,2},{5,3},{6,4},{7,5},{8,6},{9,7},{10,... | collective-permute-start | bytes 184328 | tf_op jit(solution)/shard_map/ppermute | solution.py:52
  16.7 4.2 %collective-permute-start.7 = (bf16[5,240,128]{2,1,0:T(8,128)(2,1)S(1)}, bf16[5,240,128]{2,1,0:T(8,128)(2,1)S(1)}, u32[]{:S(2)}, u32[]{:S(2)}) collective-permute-start(bf16[5,240,128]{2,1,0:T(8,128)(2,1)S(1)} %bitcast_dynamic-update-slice_fusion.first_ref), channel_id=1, source_target_pairs={{0,1},{1,0},{2,3},{3,2},{4,5},{5,4},{6,7},{7,6},{8,9},{9,8},{10,11... | collective-permute-start | bytes 921608 | tf_op jit(solution)/shard_map/ppermute | solution.py:47
  19.3 1.6 %collective-permute-start.8 = (bf16[3,240,128]{2,1,0:T(8,128)(2,1)S(1)}, bf16[3,240,128]{2,1,0:T(8,128)(2,1)S(1)}, u32[]{:S(2)}, u32[]{:S(2)}) collective-permute-start(bf16[3,240,128]{2,1,0:T(8,128)(2,1)S(1)} %pad_maximum_fusion.last_ref), channel_id=1, source_target_pairs={{0,1},{1,0},{2,3},{3,2},{4,5},{5,4},{6,7},{7,6},{8,9},{9,8},{10,11... | collective-permute-start | bytes 552968 | tf_op jit(solution)/shard_map/ppermute | solution.py:47
  28.1 13.1 %all-to-all-start = ((f32[16,8,128]{2,1,0:T(8,128)}), f32[16,8,128]{2,1,0:T(8,128)S(1)}, u32[]{:S(2)}, u32[]{:S(2)}) async-start(f32[16,8,128]{2,1,0:T(8,128)} %get-tuple-element.22), calls=%async_computation | async-start | bytes 131072 | tf_op jit(solution)/shard_map/all_to_all | solution.py:588
  42.1 1.6 %collective-permute-start.9 = (bf16[8,160,128]{2,1,0:T(8,128)(2,1)S(1)}, bf16[8,160,128]{2,1,0:T(8,128)(2,1)S(1)}, u32[]{:S(2)}, u32[]{:S(2)}) collective-permute-start(bf16[8,160,128]{2,1,0:T(8,128)(2,1)S(1)} %get-tuple-element.30), channel_id=1, source_target_pairs={{0,1},{1,0},{2,3},{3,2},{4,5},{5,4},{6,7},{7,6},{8,9},{9,8},{10,11... | collective-permute-start | bytes 983048 | tf_op jit(solution)/shard_map/ppermute | solution.py:47
  43.9 8.9 %collective-permute-start.10 = (bf16[160,128]{1,0:T(8,128)(2,1)S(1)}, bf16[160,128]{1,0:T(8,128)(2,1)S(1)}, u32[]{:S(2)}, u32[]{:S(2)}) collective-permute-start(bf16[160,128]{1,0:T(8,128)(2,1)S(1)} %get-tuple-element.48), channel_id=1, source_target_pairs={{0,2},{1,3},{2,4},{3,5},{4,6},{5,7},{6,8},{7,9},{8,10},{9,11},{10,... | collective-permute-start | bytes 122888 | tf_op jit(solution)/shard_map/ppermute | solution.py:52
  45.2 9.1 %collective-permute-start.11 = (bf16[160,128]{1,0:T(8,128)(2,1)S(1)}, bf16[160,128]{1,0:T(8,128)(2,1)S(1)}, u32[]{:S(2)}, u32[]{:S(2)}) collective-permute-start(bf16[160,128]{1,0:T(8,128)(2,1)S(1)} %get-tuple-element.47), channel_id=1, source_target_pairs={{0,4},{1,5},{2,6},{3,7},{4,8},{5,9},{6,10},{7,11},{8,12},{9,13},{1... | collective-permute-start | bytes 122888 | tf_op jit(solution)/shard_map/ppermute | solution.py:52
  46.6 9.1 %collective-permute-start.12 = (bf16[160,128]{1,0:T(8,128)(2,1)S(1)}, bf16[160,128]{1,0:T(8,128)(2,1)S(1)}, u32[]{:S(2)}, u32[]{:S(2)}) collective-permute-start(bf16[160,128]{1,0:T(8,128)(2,1)S(1)} %get-tuple-element.46), channel_id=1, source_target_pairs={{0,6},{1,7},{2,8},{3,9},{4,10},{5,11},{6,12},{7,13},{8,14},{9,15},... | collective-permute-start | bytes 122888 | tf_op jit(solution)/shard_map/ppermute | solution.py:52
  49.0 6.8 %collective-permute-start.13 = (bf16[160,128]{1,0:T(8,128)(2,1)S(1)}, bf16[160,128]{1,0:T(8,128)(2,1)S(1)}, u32[]{:S(2)}, u32[]{:S(2)}) collective-permute-start(bf16[160,128]{1,0:T(8,128)(2,1)S(1)} %get-tuple-element.45), channel_id=1, source_target_pairs={{0,8},{1,9},{2,10},{3,11},{4,12},{5,13},{6,14},{7,15},{8,0},{9,1},... | collective-permute-start | bytes 122888 | tf_op jit(solution)/shard_map/ppermute | solution.py:52
  50.5 5.4 %collective-permute-start.14 = (bf16[160,128]{1,0:T(8,128)(2,1)S(1)}, bf16[160,128]{1,0:T(8,128)(2,1)S(1)}, u32[]{:S(2)}, u32[]{:S(2)}) collective-permute-start(bf16[160,128]{1,0:T(8,128)(2,1)S(1)} %get-tuple-element.44), channel_id=1, source_target_pairs={{0,10},{1,11},{2,12},{3,13},{4,14},{5,15},{6,0},{7,1},{8,2},{9,3},... | collective-permute-start | bytes 122888 | tf_op jit(solution)/shard_map/ppermute | solution.py:52
  52.8 4.1 %collective-permute-start.15 = (bf16[160,128]{1,0:T(8,128)(2,1)S(1)}, bf16[160,128]{1,0:T(8,128)(2,1)S(1)}, u32[]{:S(2)}, u32[]{:S(2)}) collective-permute-start(bf16[160,128]{1,0:T(8,128)(2,1)S(1)} %get-tuple-element.43), channel_id=1, source_target_pairs={{0,12},{1,13},{2,14},{3,15},{4,0},{5,1},{6,2},{7,3},{8,4},{9,5},{1... | collective-permute-start | bytes 122888 | tf_op jit(solution)/shard_map/ppermute | solution.py:52
  54.3 4.0 %collective-permute-start.16 = (bf16[160,128]{1,0:T(8,128)(2,1)S(1)}, bf16[160,128]{1,0:T(8,128)(2,1)S(1)}, u32[]{:S(2)}, u32[]{:S(2)}) collective-permute-start(bf16[160,128]{1,0:T(8,128)(2,1)S(1)} %get-tuple-element.42), channel_id=1, source_target_pairs={{0,14},{1,15},{2,0},{3,1},{4,2},{5,3},{6,4},{7,5},{8,6},{9,7},{10,... | collective-permute-start | bytes 122888 | tf_op jit(solution)/shard_map/ppermute | solution.py:52

commit v26 on v24

--- a/solution.py
+++ b/solution.py
@@ -11,7 +11,7 @@
 LANES = 128
 STATS = 8
 AHEAD = 3
-EARLY = 3
+EARLY = 2
 
 
 sample_weight = 0.5

time: 58.5 us -> 58.1 us (level)
  transfers between devices with their start and end apart: 18 -> 18, of which waited for: 8 -> 9; matrix products, arithmetic and copies ran while one was open for 0% -> 0% of each run, Pallas kernels for 17% -> 16%
where the time goes in v26:
time: 58.1 us; the launch traced here: 57.8 us
  starting transfers between devices  32.4 us (56%)
  Pallas kernels  19.1 us (33%)
  waiting for transfers between devices  4.69 us (8%)
  between operations  1.42 us (2%)
    ppermute x14, starting transfers between devices, along_chips(): lax.ppermute(array, 'vocab', [(i, (i + 2 * step) % count) for i in range(...  25.7 us
    pallas_call x1, Pallas kernels, paired_shards(): pl.pallas_call(logits_kernel, out_shape=(hbm_array((3 * tokens, shard_row...  6.4 us
    all_to_all x1, starting transfers between devices, paired_shards(): lax.all_to_all(stats, 'vocab', split_axis=0, concat_axis=0, tiled=True)  6.22 us
    pallas_call x1, Pallas kernels, paired_shards(): pl.pallas_call(products_kernel, out_shape=(vmem_array((chips, width // LA...  6.18 us
    ppermute x14, waiting for transfers between devices, along_chips(): lax.ppermute(array, 'vocab', [(i, (i + 2 * step) % count) for i in range(...  3.29 us
    pallas_call x1, Pallas kernels, paired_shards(): pl.pallas_call(functools.partial(preload_kernel, chips=chips), out_shape=...  1.91 us
    pallas_call x1, Pallas kernels, paired_shards(): pl.pallas_call(functools.partial(pack_kernel, shard_rows=shard_rows), out...  1.52 us
    pallas_call x1, Pallas kernels, paired_shards(): pl.pallas_call(keep_kernel, out_shape=(vmem_array((chips, hidden_rows, LA...  1.34 us
  transfers between devices with their start and end apart: 18, of which 9 were waited for; matrix products, arithmetic and copies ran while one was open for 0% of the time, Pallas kernels for 16%

profile of v26, /device:TPU:0, one launch (start us, length us, event | category | flops | bytes accessed | tf_op | source)
XLA Modules:
  0.0 57.8 jit_solution(17076757640587701994)
XLA Ops:
  0.6 1.5 %pack.1 = (bf16[8,240,128]{2,1,0:T(8,128)(2,1)S(1)}, bf16[128,128]{1,0:T(8,128)(2,1)S(1)}, f32[64,128]{1,0:T(8,128)S(1)}) custom-call(s32[1]{0:T(128)} %bitcast.place_ref, bf16[64,320]{1,0:T(8,128)(2,1)} %refs_0_.1, bf16[4,19456]{1,0:T(4,128)(2,1)} %refs_1_.1, f32[4,608]{1,0:T(4,128)} %refs_2_.1, s32[1,64]{1,0:T(1,128)} %bitcast.49, s32[1,64]{1,0:T(1,128)} %bitcast.50, ...), custom_call_target="tpu_custom_call" | custom-call | tf_op jit(solution)/shard_map/pack/pallas_call | solution.py:513
  2.2 3.0 %collective-permute-start = (bf16[240,128]{1,0:T(8,128)(2,1)S(1)}, bf16[240,128]{1,0:T(8,128)(2,1)S(1)}, u32[]{:S(2)}, u32[]{:S(2)}) collective-permute-start(bf16[240,128]{1,0:T(8,128)(2,1)S(1)} %get-tuple-element.40), channel_id=1, source_target_pairs={{0,2},{1,3},{2,4},{3,5},{4,6},{5,7},{6,8},{7,9},{8,10},{9,11},{10,... | collective-permute-start | bytes 184328 | tf_op jit(solution)/shard_map/ppermute | solution.py:52
  5.2 1.6 %collective-permute-start.1 = (bf16[240,128]{1,0:T(8,128)(2,1)S(1)}, bf16[240,128]{1,0:T(8,128)(2,1)S(1)}, u32[]{:S(2)}, u32[]{:S(2)}) collective-permute-start(bf16[240,128]{1,0:T(8,128)(2,1)S(1)} %get-tuple-element.39), channel_id=1, source_target_pairs={{0,4},{1,5},{2,6},{3,7},{4,8},{5,9},{6,10},{7,11},{8,12},{9,13},{1... | collective-permute-start | bytes 184328 | tf_op jit(solution)/shard_map/ppermute | solution.py:52
  6.8 2.5 %collective-permute-start.2 = (bf16[240,128]{1,0:T(8,128)(2,1)S(1)}, bf16[240,128]{1,0:T(8,128)(2,1)S(1)}, u32[]{:S(2)}, u32[]{:S(2)}) collective-permute-start(bf16[240,128]{1,0:T(8,128)(2,1)S(1)} %get-tuple-element.38), channel_id=1, source_target_pairs={{0,6},{1,7},{2,8},{3,9},{4,10},{5,11},{6,12},{7,13},{8,14},{9,15},... | collective-permute-start | bytes 184328 | tf_op jit(solution)/shard_map/ppermute | solution.py:52
  9.3 1.2 %collective-permute-start.3 = (bf16[240,128]{1,0:T(8,128)(2,1)S(1)}, bf16[240,128]{1,0:T(8,128)(2,1)S(1)}, u32[]{:S(2)}, u32[]{:S(2)}) collective-permute-start(bf16[240,128]{1,0:T(8,128)(2,1)S(1)} %get-tuple-element.37), channel_id=1, source_target_pairs={{0,8},{1,9},{2,10},{3,11},{4,12},{5,13},{6,14},{7,15},{8,0},{9,1},... | collective-permute-start | bytes 184328 | tf_op jit(solution)/shard_map/ppermute | solution.py:52
  10.6 2.6 %collective-permute-start.4 = (bf16[240,128]{1,0:T(8,128)(2,1)S(1)}, bf16[240,128]{1,0:T(8,128)(2,1)S(1)}, u32[]{:S(2)}, u32[]{:S(2)}) collective-permute-start(bf16[240,128]{1,0:T(8,128)(2,1)S(1)} %get-tuple-element.34), channel_id=1, source_target_pairs={{0,10},{1,11},{2,12},{3,13},{4,14},{5,15},{6,0},{7,1},{8,2},{9,3},... | collective-permute-start | bytes 184328 | tf_op jit(solution)/shard_map/ppermute | solution.py:52
  13.2 1.3 %collective-permute-start.5 = (bf16[240,128]{1,0:T(8,128)(2,1)S(1)}, bf16[240,128]{1,0:T(8,128)(2,1)S(1)}, u32[]{:S(2)}, u32[]{:S(2)}) collective-permute-start(bf16[240,128]{1,0:T(8,128)(2,1)S(1)} %get-tuple-element.36), channel_id=1, source_target_pairs={{0,12},{1,13},{2,14},{3,15},{4,0},{5,1},{6,2},{7,3},{8,4},{9,5},{1... | collective-permute-start | bytes 184328 | tf_op jit(solution)/shard_map/ppermute | solution.py:52
  14.6 1.5 %collective-permute-start.6 = (bf16[240,128]{1,0:T(8,128)(2,1)S(1)}, bf16[240,128]{1,0:T(8,128)(2,1)S(1)}, u32[]{:S(2)}, u32[]{:S(2)}) collective-permute-start(bf16[240,128]{1,0:T(8,128)(2,1)S(1)} %get-tuple-element.35), channel_id=1, source_target_pairs={{0,14},{1,15},{2,0},{3,1},{4,2},{5,3},{6,4},{7,5},{8,6},{9,7},{10,... | collective-permute-start | bytes 184328 | tf_op jit(solution)/shard_map/ppermute | solution.py:52
  16.8 1.9 %preload.1.early_ref = bf16[2,1216,640]{2,1,0:T(8,128)(2,1)S(1)} custom-call(s32[1]{0:T(128)} %bitcast.place_ref, bf16[1216,5120]{1,0:T(8,128)(2,1)} %head_ref.5, bf16[240,128]{1,0:T(8,128)(2,1)S(1)} %collective-permute-done.2._), custom_call_target="tpu_custom_call" | custom-call | bytes 6225920 | tf_op jit(solution)/shard_map/preload/pallas_call | solution.py:533
  20.4 6.4 %logits.1 = (bf16[192,1216]{1,0:T(8,128)(2,1)}, f32[16,8,128]{2,1,0:T(8,128)}, f32[8,128]{1,0:T(8,128)S(1)}) custom-call(s32[1]{0:T(128)} %bitcast.place_ref, bf16[5,240,128]{2,1,0:T(8,128)(2,1)S(1)} %bitcast_dynamic-update-slice_fusion.first_ref, bf16[3,240,128]{2,1,0:T(8,128)(2,1)S(1)} %pad_maximum_fusion.last_ref, ...), custom_call_target="tpu_custom_call" | custom-call | flops 796917760 | bytes 12451840 | tf_op jit(solution)/shard_map/logits/pallas_call | solution.py:549
  26.8 6.2 %all-to-all-start = ((f32[16,8,128]{2,1,0:T(8,128)}), f32[16,8,128]{2,1,0:T(8,128)S(1)}, u32[]{:S(2)}, u32[]{:S(2)}) async-start(f32[16,8,128]{2,1,0:T(8,128)} %get-tuple-element.22), calls=%async_computation | async-start | bytes 131072 | tf_op jit(solution)/shard_map/all_to_all | solution.py:584
  33.0 6.2 %products.1 = (f32[8,5,2,64,128]{4,3,2,1,0:T(8,128)S(1)}, bf16[8,5,64,128]{3,2,1,0:T(8,128)(2,1)S(1)}) custom-call(s32[1]{0:T(128)} %bitcast.place_ref, bf16[192,1216]{1,0:T(8,128)(2,1)} %get-tuple-element.24.rows_ref, bf16[1216,5120]{1,0:T(8,128)(2,1)} %head_ref.5), custom_call_target="tpu_custom_call" | custom-call | flops 2390753280 | bytes 12451840 | tf_op jit(solution)/shard_map/products/pallas_call | solution.py:586
  39.9 0.9 %give.1 = (bf16[8,160,128]{2,1,0:T(8,128)(2,1)S(1)}, f32[3,64,128]{2,1,0:T(8,128)S(1)}, f32[1,1]{1,0:T(1,128)}) custom-call(s32[1]{0:T(128)} %bitcast.place_ref, f32[1]{0:T(128)S(6)} %copy.14.scale_ref, f32[16,8,128]{2,1,0:T(8,128)S(1)} %all-to-all-done.stats_ref, f32[8,128]{1,0:T(8,128)S(1)} %get-tuple-element.23.own_ref, ...), custom_call_target="tpu_custom_call" | custom-call | tf_op jit(solution)/shard_map/give/pallas_call | solution.py:603
  40.9 1.3 %keep.1 = (f32[8,160,128]{2,1,0:T(8,128)S(1)}, f32[1,1]{1,0:T(1,128)}) custom-call(s32[1]{0:T(128)} %bitcast.place_ref, f32[3,64,128]{2,1,0:T(8,128)S(1)} %get-tuple-element.27.factors_ref, f32[1,1]{1,0:T(1,128)} %get-tuple-element.28.found_ref, f32[8,5,2,64,128]{4,3,2,1,0:T(8,128)S(1)} %get-tuple-element.25.terms_ref, ...), custom_call_target="tpu_custom_call" | custom-call | flops 2621440 | bytes 2621440 | tf_op jit(solution)/shard_map/keep/pallas_call | solution.py:616
  42.6 1.3 %collective-permute-start.10 = (bf16[160,128]{1,0:T(8,128)(2,1)S(1)}, bf16[160,128]{1,0:T(8,128)(2,1)S(1)}, u32[]{:S(2)}, u32[]{:S(2)}) collective-permute-start(bf16[160,128]{1,0:T(8,128)(2,1)S(1)} %get-tuple-element.48), channel_id=1, source_target_pairs={{0,2},{1,3},{2,4},{3,5},{4,6},{5,7},{6,8},{7,9},{8,10},{9,11},{10,... | collective-permute-start | bytes 122888 | tf_op jit(solution)/shard_map/ppermute | solution.py:52
  43.9 1.5 %collective-permute-start.11 = (bf16[160,128]{1,0:T(8,128)(2,1)S(1)}, bf16[160,128]{1,0:T(8,128)(2,1)S(1)}, u32[]{:S(2)}, u32[]{:S(2)}) collective-permute-start(bf16[160,128]{1,0:T(8,128)(2,1)S(1)} %get-tuple-element.47), channel_id=1, source_target_pairs={{0,4},{1,5},{2,6},{3,7},{4,8},{5,9},{6,10},{7,11},{8,12},{9,13},{1... | collective-permute-start | bytes 122888 | tf_op jit(solution)/shard_map/ppermute | solution.py:52
  45.4 2.4 %collective-permute-start.12 = (bf16[160,128]{1,0:T(8,128)(2,1)S(1)}, bf16[160,128]{1,0:T(8,128)(2,1)S(1)}, u32[]{:S(2)}, u32[]{:S(2)}) collective-permute-start(bf16[160,128]{1,0:T(8,128)(2,1)S(1)} %get-tuple-element.46), channel_id=1, source_target_pairs={{0,6},{1,7},{2,8},{3,9},{4,10},{5,11},{6,12},{7,13},{8,14},{9,15},... | collective-permute-start | bytes 122888 | tf_op jit(solution)/shard_map/ppermute | solution.py:52
  47.7 1.5 %collective-permute-start.13 = (bf16[160,128]{1,0:T(8,128)(2,1)S(1)}, bf16[160,128]{1,0:T(8,128)(2,1)S(1)}, u32[]{:S(2)}, u32[]{:S(2)}) collective-permute-start(bf16[160,128]{1,0:T(8,128)(2,1)S(1)} %get-tuple-element.45), channel_id=1, source_target_pairs={{0,8},{1,9},{2,10},{3,11},{4,12},{5,13},{6,14},{7,15},{8,0},{9,1},... | collective-permute-start | bytes 122888 | tf_op jit(solution)/shard_map/ppermute | solution.py:52
  49.2 2.4 %collective-permute-start.14 = (bf16[160,128]{1,0:T(8,128)(2,1)S(1)}, bf16[160,128]{1,0:T(8,128)(2,1)S(1)}, u32[]{:S(2)}, u32[]{:S(2)}) collective-permute-start(bf16[160,128]{1,0:T(8,128)(2,1)S(1)} %get-tuple-element.44), channel_id=1, source_target_pairs={{0,10},{1,11},{2,12},{3,13},{4,14},{5,15},{6,0},{7,1},{8,2},{9,3},... | collective-permute-start | bytes 122888 | tf_op jit(solution)/shard_map/ppermute | solution.py:52
  51.6 1.5 %collective-permute-start.15 = (bf16[160,128]{1,0:T(8,128)(2,1)S(1)}, bf16[160,128]{1,0:T(8,128)(2,1)S(1)}, u32[]{:S(2)}, u32[]{:S(2)}) collective-permute-start(bf16[160,128]{1,0:T(8,128)(2,1)S(1)} %get-tuple-element.43), channel_id=1, source_target_pairs={{0,12},{1,13},{2,14},{3,15},{4,0},{5,1},{6,2},{7,3},{8,4},{9,5},{1... | collective-permute-start | bytes 122888 | tf_op jit(solution)/shard_map/ppermute | solution.py:52
  53.0 1.5 %collective-permute-start.16 = (bf16[160,128]{1,0:T(8,128)(2,1)S(1)}, bf16[160,128]{1,0:T(8,128)(2,1)S(1)}, u32[]{:S(2)}, u32[]{:S(2)}) collective-permute-start(bf16[160,128]{1,0:T(8,128)(2,1)S(1)} %get-tuple-element.42), channel_id=1, source_target_pairs={{0,14},{1,15},{2,0},{3,1},{4,2},{5,3},{6,4},{7,5},{8,6},{9,7},{10,... | collective-permute-start | bytes 122888 | tf_op jit(solution)/shard_map/ppermute | solution.py:52
  54.6 1.0 %collective-permute-done.15.refs_5_ = bf16[160,128]{1,0:T(8,128)(2,1)S(1)} collective-permute-done((bf16[160,128]{1,0:T(8,128)(2,1)S(1)}, bf16[160,128]{1,0:T(8,128)(2,1)S(1)}, u32[]{:S(2)}, u32[]{:S(2)}) %collective-permute-start.15) | collective-permute-done | bytes 40992 | tf_op jit(solution)/shard_map/ppermute | solution.py:52
  55.7 1.4 %collective-permute-done.16.refs_6_ = bf16[160,128]{1,0:T(8,128)(2,1)S(1)} collective-permute-done((bf16[160,128]{1,0:T(8,128)(2,1)S(1)}, bf16[160,128]{1,0:T(8,128)(2,1)S(1)}, u32[]{:S(2)}, u32[]{:S(2)}) %collective-permute-start.16) | collective-permute-done | bytes 40992 | tf_op jit(solution)/shard_map/ppermute | solution.py:52
  57.0 0.8 %total.1 = bf16[64,320]{1,0:T(8,128)(2,1)} custom-call(s32[1]{0:T(128)} %bitcast.place_ref, f32[160,128]{1,0:T(8,128)S(1)} %slice_bitcast_fusion.own_ref, bf16[160,128]{1,0:T(8,128)(2,1)S(1)} %collective-permute-done.10.refs_0_, bf16[160,128]{1,0:T(8,128)(2,1)S(1)} %collective-permute-done.11.refs_1_, bf16[160,128]{1,0:T(8,128)(2,1)S(1)} %collective-permute-done.12.refs_2_, ...), custom_call_target="tpu_custom_call" | custom-call | tf_op jit(solution)/shard_map/total/pallas_call | solution.py:632
  (28 shorter events, 3.1 us)
Async XLA Ops:
  2.2 11.0 %collective-permute-start = (bf16[240,128]{1,0:T(8,128)(2,1)S(1)}, bf16[240,128]{1,0:T(8,128)(2,1)S(1)}, u32[]{:S(2)}, u32[]{:S(2)}) collective-permute-start(bf16[240,128]{1,0:T(8,128)(2,1)S(1)} %get-tuple-element.40), channel_id=1, source_target_pairs={{0,2},{1,3},{2,4},{3,5},{4,6},{5,7},{6,8},{7,9},{8,10},{9,11},{10,... | collective-permute-start | bytes 184328 | tf_op jit(solution)/shard_map/ppermute | solution.py:52
  5.2 9.4 %collective-permute-start.1 = (bf16[240,128]{1,0:T(8,128)(2,1)S(1)}, bf16[240,128]{1,0:T(8,128)(2,1)S(1)}, u32[]{:S(2)}, u32[]{:S(2)}) collective-permute-start(bf16[240,128]{1,0:T(8,128)(2,1)S(1)} %get-tuple-element.39), channel_id=1, source_target_pairs={{0,4},{1,5},{2,6},{3,7},{4,8},{5,9},{6,10},{7,11},{8,12},{9,13},{1... | collective-permute-start | bytes 184328 | tf_op jit(solution)/shard_map/ppermute | solution.py:52
  6.8 9.4 %collective-permute-start.2 = (bf16[240,128]{1,0:T(8,128)(2,1)S(1)}, bf16[240,128]{1,0:T(8,128)(2,1)S(1)}, u32[]{:S(2)}, u32[]{:S(2)}) collective-permute-start(bf16[240,128]{1,0:T(8,128)(2,1)S(1)} %get-tuple-element.38), channel_id=1, source_target_pairs={{0,6},{1,7},{2,8},{3,9},{4,10},{5,11},{6,12},{7,13},{8,14},{9,15},... | collective-permute-start | bytes 184328 | tf_op jit(solution)/shard_map/ppermute | solution.py:52
  9.3 7.4 %collective-permute-start.3 = (bf16[240,128]{1,0:T(8,128)(2,1)S(1)}, bf16[240,128]{1,0:T(8,128)(2,1)S(1)}, u32[]{:S(2)}, u32[]{:S(2)}) collective-permute-start(bf16[240,128]{1,0:T(8,128)(2,1)S(1)} %get-tuple-element.37), channel_id=1, source_target_pairs={{0,8},{1,9},{2,10},{3,11},{4,12},{5,13},{6,14},{7,15},{8,0},{9,1},... | collective-permute-start | bytes 184328 | tf_op jit(solution)/shard_map/ppermute | solution.py:52
  10.6 8.2 %collective-permute-start.4 = (bf16[240,128]{1,0:T(8,128)(2,1)S(1)}, bf16[240,128]{1,0:T(8,128)(2,1)S(1)}, u32[]{:S(2)}, u32[]{:S(2)}) collective-permute-start(bf16[240,128]{1,0:T(8,128)(2,1)S(1)} %get-tuple-element.34), channel_id=1, source_target_pairs={{0,10},{1,11},{2,12},{3,13},{4,14},{5,15},{6,0},{7,1},{8,2},{9,3},... | collective-permute-start | bytes 184328 | tf_op jit(solution)/shard_map/ppermute | solution.py:52
  13.2 5.5 %collective-permute-start.5 = (bf16[240,128]{1,0:T(8,128)(2,1)S(1)}, bf16[240,128]{1,0:T(8,128)(2,1)S(1)}, u32[]{:S(2)}, u32[]{:S(2)}) collective-permute-start(bf16[240,128]{1,0:T(8,128)(2,1)S(1)} %get-tuple-element.36), channel_id=1, source_target_pairs={{0,12},{1,13},{2,14},{3,15},{4,0},{5,1},{6,2},{7,3},{8,4},{9,5},{1... | collective-permute-start | bytes 184328 | tf_op jit(solution)/shard_map/ppermute | solution.py:52
  14.6 4.3 %collective-permute-start.6 = (bf16[240,128]{1,0:T(8,128)(2,1)S(1)}, bf16[240,128]{1,0:T(8,128)(2,1)S(1)}, u32[]{:S(2)}, u32[]{:S(2)}) collective-permute-start(bf16[240,128]{1,0:T(8,128)(2,1)S(1)} %get-tuple-element.35), channel_id=1, source_target_pairs={{0,14},{1,15},{2,0},{3,1},{4,2},{5,3},{6,4},{7,5},{8,6},{9,7},{10,... | collective-permute-start | bytes 184328 | tf_op jit(solution)/shard_map/ppermute | solution.py:52
  16.7 3.7 %collective-permute-start.7 = (bf16[5,240,128]{2,1,0:T(8,128)(2,1)S(1)}, bf16[5,240,128]{2,1,0:T(8,128)(2,1)S(1)}, u32[]{:S(2)}, u32[]{:S(2)}) collective-permute-start(bf16[5,240,128]{2,1,0:T(8,128)(2,1)S(1)} %bitcast_dynamic-update-slice_fusion.first_ref), channel_id=1, source_target_pairs={{0,1},{1,0},{2,3},{3,2},{4,5},{5,4},{6,7},{7,6},{8,9},{9,8},{10,11... | collective-permute-start | bytes 921608 | tf_op jit(solution)/shard_map/ppermute | solution.py:47
  18.9 1.5 %collective-permute-start.8 = (bf16[3,240,128]{2,1,0:T(8,128)(2,1)S(1)}, bf16[3,240,128]{2,1,0:T(8,128)(2,1)S(1)}, u32[]{:S(2)}, u32[]{:S(2)}) collective-permute-start(bf16[3,240,128]{2,1,0:T(8,128)(2,1)S(1)} %pad_maximum_fusion.last_ref), channel_id=1, source_target_pairs={{0,1},{1,0},{2,3},{3,2},{4,5},{5,4},{6,7},{7,6},{8,9},{9,8},{10,11... | collective-permute-start | bytes 552968 | tf_op jit(solution)/shard_map/ppermute | solution.py:47
  26.8 13.1 %all-to-all-start = ((f32[16,8,128]{2,1,0:T(8,128)}), f32[16,8,128]{2,1,0:T(8,128)S(1)}, u32[]{:S(2)}, u32[]{:S(2)}) async-start(f32[16,8,128]{2,1,0:T(8,128)} %get-tuple-element.22), calls=%async_computation | async-start | bytes 131072 | tf_op jit(solution)/shard_map/all_to_all | solution.py:584
  40.9 1.6 %collective-permute-start.9 = (bf16[8,160,128]{2,1,0:T(8,128)(2,1)S(1)}, bf16[8,160,128]{2,1,0:T(8,128)(2,1)S(1)}, u32[]{:S(2)}, u32[]{:S(2)}) collective-permute-start(bf16[8,160,128]{2,1,0:T(8,128)(2,1)S(1)} %get-tuple-element.30), channel_id=1, source_target_pairs={{0,1},{1,0},{2,3},{3,2},{4,5},{5,4},{6,7},{7,6},{8,9},{9,8},{10,11... | collective-permute-start | bytes 983048 | tf_op jit(solution)/shard_map/ppermute | solution.py:47
  42.6 8.9 %collective-permute-start.10 = (bf16[160,128]{1,0:T(8,128)(2,1)S(1)}, bf16[160,128]{1,0:T(8,128)(2,1)S(1)}, u32[]{:S(2)}, u32[]{:S(2)}) collective-permute-start(bf16[160,128]{1,0:T(8,128)(2,1)S(1)} %get-tuple-element.48), channel_id=1, source_target_pairs={{0,2},{1,3},{2,4},{3,5},{4,6},{5,7},{6,8},{7,9},{8,10},{9,11},{10,... | collective-permute-start | bytes 122888 | tf_op jit(solution)/shard_map/ppermute | solution.py:52
  43.9 9.1 %collective-permute-start.11 = (bf16[160,128]{1,0:T(8,128)(2,1)S(1)}, bf16[160,128]{1,0:T(8,128)(2,1)S(1)}, u32[]{:S(2)}, u32[]{:S(2)}) collective-permute-start(bf16[160,128]{1,0:T(8,128)(2,1)S(1)} %get-tuple-element.47), channel_id=1, source_target_pairs={{0,4},{1,5},{2,6},{3,7},{4,8},{5,9},{6,10},{7,11},{8,12},{9,13},{1... | collective-permute-start | bytes 122888 | tf_op jit(solution)/shard_map/ppermute | solution.py:52
  45.4 9.1 %collective-permute-start.12 = (bf16[160,128]{1,0:T(8,128)(2,1)S(1)}, bf16[160,128]{1,0:T(8,128)(2,1)S(1)}, u32[]{:S(2)}, u32[]{:S(2)}) collective-permute-start(bf16[160,128]{1,0:T(8,128)(2,1)S(1)} %get-tuple-element.46), channel_id=1, source_target_pairs={{0,6},{1,7},{2,8},{3,9},{4,10},{5,11},{6,12},{7,13},{8,14},{9,15},... | collective-permute-start | bytes 122888 | tf_op jit(solution)/shard_map/ppermute | solution.py:52
  47.7 6.8 %collective-permute-start.13 = (bf16[160,128]{1,0:T(8,128)(2,1)S(1)}, bf16[160,128]{1,0:T(8,128)(2,1)S(1)}, u32[]{:S(2)}, u32[]{:S(2)}) collective-permute-start(bf16[160,128]{1,0:T(8,128)(2,1)S(1)} %get-tuple-element.45), channel_id=1, source_target_pairs={{0,8},{1,9},{2,10},{3,11},{4,12},{5,13},{6,14},{7,15},{8,0},{9,1},... | collective-permute-start | bytes 122888 | tf_op jit(solution)/shard_map/ppermute | solution.py:52
  49.2 5.4 %collective-permute-start.14 = (bf16[160,128]{1,0:T(8,128)(2,1)S(1)}, bf16[160,128]{1,0:T(8,128)(2,1)S(1)}, u32[]{:S(2)}, u32[]{:S(2)}) collective-permute-start(bf16[160,128]{1,0:T(8,128)(2,1)S(1)} %get-tuple-element.44), channel_id=1, source_target_pairs={{0,10},{1,11},{2,12},{3,13},{4,14},{5,15},{6,0},{7,1},{8,2},{9,3},... | collective-permute-start | bytes 122888 | tf_op jit(solution)/shard_map/ppermute | solution.py:52
  51.6 4.1 %collective-permute-start.15 = (bf16[160,128]{1,0:T(8,128)(2,1)S(1)}, bf16[160,128]{1,0:T(8,128)(2,1)S(1)}, u32[]{:S(2)}, u32[]{:S(2)}) collective-permute-start(bf16[160,128]{1,0:T(8,128)(2,1)S(1)} %get-tuple-element.43), channel_id=1, source_target_pairs={{0,12},{1,13},{2,14},{3,15},{4,0},{5,1},{6,2},{7,3},{8,4},{9,5},{1... | collective-permute-start | bytes 122888 | tf_op jit(solution)/shard_map/ppermute | solution.py:52
  53.0 4.0 %collective-permute-start.16 = (bf16[160,128]{1,0:T(8,128)(2,1)S(1)}, bf16[160,128]{1,0:T(8,128)(2,1)S(1)}, u32[]{:S(2)}, u32[]{:S(2)}) collective-permute-start(bf16[160,128]{1,0:T(8,128)(2,1)S(1)} %get-tuple-element.42), channel_id=1, source_target_pairs={{0,14},{1,15},{2,0},{3,1},{4,2},{5,3},{6,4},{7,5},{8,6},{9,7},{10,... | collective-permute-start | bytes 122888 | tf_op jit(solution)/shard_map/ppermute | solution.py:52
